TPU v7x, 32 devices: a whole 2x2x4 slice. The times are simulated.
32 devices in a mesh: members: 2 (over y), window: 4 (over z), space: 4 (over x, core).
Axes of the slice: x: 2, y: 2, z: 4, core: 2. Of those that a mesh axis runs over, the one named last changes fastest.
Arguments:
- trajectory: bfloat16 [8, 4, 5, 4, 32, 384], P('members', None, None, None, 'space', 'window'), parts along dimension 0, may hold values from -4 to 4
- dual_model: float32 [8, 5, 4, 32, 384], P(('members', 'window'), None, None, 'space'), parts along dimension 0, may hold values from -6 to 6
- increment: float32 [8, 5, 4, 32, 384], P(('members', 'window'), None, None, 'space'), parts along dimension 0, may hold values from -6 to 6
- model_rhs: float32 [8, 5, 4, 32, 384], P(('members', 'window'), None, None, 'space'), parts along dimension 0, may hold values from -6 to 6
- dual_obs: float32 [8, 4, 4, 32, 384], P(('members', 'window'), None, None, 'space'), parts along dimension 0, may hold values from -6 to 6
- innovation: float32 [8, 4, 4, 32, 384], P(('members', 'window'), None, None, 'space'), parts along dimension 0, may hold values from -6 to 6
- coupling: float32 [5, 5], replicated, may hold values from -2.5 to 2.5
- error_var: float32 [8, 5, 4], P(('members', 'window')), parts along dimension 0, may hold values from 0.25 to 4
- obs_var: float32 [8, 4, 4], P(('members', 'window')), parts along dimension 0, may hold values from 0.5 to 2
- obs_count: int32 [8], P(('members', 'window')), parts along dimension 0, may hold values from 1 to 4
Outputs:
- new_dual_model: float32 [8, 5, 4, 32, 384], P(('members', 'window'), None, None, 'space'), parts along dimension 0
- new_dual_obs: float32 [8, 4, 4, 32, 384], P(('members', 'window'), None, None, 'space'), parts along dimension 0
- new_increment: float32 [8, 5, 4, 32, 384], P(('members', 'window'), None, None, 'space'), parts along dimension 0
There are 2 independent parts, one for each index of `members`. A program takes and returns all parts, laid end to end along the dimension named above; an argument that names none is the same for every part. Nothing has to cross between parts.
Inputs may be any that keep to these rules, and one draw needn't show every extreme that they name: `obs_count`: observed steps of a subwindow are its first ones.
All inputs are finite; a program needn't handle non-finite values.
Results may differ from a plain program's by a relative error of at most 0.00085.
Values may be sent and summed in bfloat16 or wider, within the bound.
No kernel may reach another device: no remote copies, remote signals or barrier semaphores. Data moves between devices by JAX's collectives and lax.ppermute only.
A program may use at most 64 MiB of HBM per device.

v0:
```python
import jax
import jax.numpy as jnp
from jax import lax
from jax.sharding import PartitionSpec as P

STEPS = 4


diffusion = 0.2
advection = 0.2
coupling_gain = 0.5


def shifted(block, axis, distance):
    devices = range(lax.axis_size(axis))
    route = [(i - distance, i) for i in devices if i - distance in devices]
    return lax.ppermute(block, axis, route)


def padded(block, sides, width):
    for axis, dim in sides:
        count = lax.axis_size(axis)
        forward = [(i, i + 1) for i in range(count - 1)]
        backward = [(target, source) for source, target in forward]
        low = lax.ppermute(
            lax.slice_in_dim(block, block.shape[dim] - width, None, axis=dim), axis, forward
        )
        high = lax.ppermute(lax.slice_in_dim(block, 0, width, axis=dim), axis, backward)
        block = jnp.concatenate([low, block, high], axis=dim)
    return block


def entering(value, axis, join, neutral, backward):
    count, mine = (lax.axis_size(axis), lax.axis_index(axis))
    pieces = lax.all_gather(value, axis)
    if backward:
        pieces = pieces[::-1]
        mine = count - 1 - mine
    so_far = jnp.full_like(value, 0) + jnp.asarray(neutral, value.dtype)

    def step(position, so_far):
        longer = join(so_far, pieces[position])
        return jnp.where(position < mine, longer, so_far)

    return lax.fori_loop(0, count - 1, step, so_far)


def along_y(field):
    edge = jnp.zeros_like(field[..., :1])
    north = jnp.concatenate([field[..., 1:], edge], -1)
    south = jnp.concatenate([edge, field[..., :-1]], -1)
    return (north, south)


def tangent_core(state, east, west, traj, coupling):
    north, south = along_y(state)
    laplace = east + west + north + south - 4.0 * state
    slope_x = 0.5 * (east - west)
    slope_y = 0.5 * (north - south)
    mixed = jnp.sum(coupling[:, :, None, None, None] * (traj * state)[None], axis=1)
    return (
        state
        + diffusion * laplace
        - advection * (traj[0] * slope_x + traj[1] * slope_y)
        + coupling_gain * mixed
    )


def adjoint_core(state, east, west, east_x, west_x, traj, coupling):
    north, south = along_y(state)
    north_y, south_y = along_y(traj[1] * state)
    laplace = east + west + north + south - 4.0 * state
    mixed = traj * jnp.sum(coupling[:, :, None, None, None] * state[:, None], axis=0)
    return (
        state
        + diffusion * laplace
        + advection * (0.5 * (east_x - west_x) + 0.5 * (north_y - south_y))
        + coupling_gain * mixed
    )


def valid_rows(first, length, tile):
    rows = lax.axis_index("space") * tile + first + jnp.arange(length, dtype=jnp.int32)
    inside = (rows >= 0) & (rows < tile * lax.axis_size("space"))
    return inside.astype(jnp.float32)[None, None, :, None]


def add_sums(earlier, later):
    return earlier + later


def body(
    trajectory,
    dual_model,
    increment,
    model_rhs,
    dual_obs,
    innovation,
    coupling,
    error_var,
    obs_var,
    obs_count,
):
    owned = lax.all_to_all(trajectory, "window", split_axis=0, concat_axis=5, tiled=True)[0]
    tile = owned.shape[3]
    margin = STEPS
    state = increment[0]
    observed = (jnp.arange(STEPS, dtype=jnp.int32) < obs_count[0]).astype(jnp.float32)
    weights = observed[:, None, None, None]
    forcing = weights * dual_obs[0]
    after = shifted(dual_model[0], "window", -1)
    seen = []
    widened = padded(owned, (("space", 3),), margin).astype(jnp.float32)
    current = padded(state, (("space", 2),), margin)
    for index in range(STEPS):
        length = current.shape[2]
        seen.append(current[0, :, margin - index : margin - index + tile])
        traj = widened[index][:, :, index + 1 : index + length - 1]
        fresh = tangent_core(
            current[:, :, 1:-1], current[:, :, 2:], current[:, :, :-2], traj, coupling
        )
        current = fresh * valid_rows(index + 1 - margin, length - 2, tile)
    ending = current
    count = after.shape[0]
    joined = padded(jnp.concatenate([-after, forcing], 0), (("space", 2),), margin)
    current = joined[:count]
    pushes = joined[count:]
    for turn, index in enumerate(reversed(range(STEPS))):
        length = current.shape[2]
        traj = widened[index][:, :, turn : turn + length]
        carried_x = traj[0] * current
        fresh = adjoint_core(
            current[:, :, 1:-1],
            current[:, :, 2:],
            current[:, :, :-2],
            carried_x[:, :, 2:],
            carried_x[:, :, :-2],
            traj[:, :, 1:-1],
            coupling,
        )
        fresh = fresh * valid_rows(turn + 1 - margin, length - 2, tile)
        current = fresh.at[0].add(pushes[index][:, turn + 1 : turn + length - 1])
    before = shifted(ending.astype(jnp.bfloat16), "window", 1).astype(ending.dtype)
    variance = error_var[0][:, :, None, None]
    model_res = model_rhs[0] - variance * dual_model[0] - (increment[0] - before)
    noise = obs_var[0][:, :, None, None]
    new_dual_obs = weights * (innovation[0] - noise * dual_obs[0] - jnp.stack(seen)) / noise
    state_res = -(dual_model[0] + current)
    later = entering(state_res, "window", add_sums, jnp.zeros_like(state_res), True)
    new_dual_model = later + state_res
    pushed = model_res - variance * new_dual_model
    earlier = entering(pushed, "window", add_sums, jnp.zeros_like(pushed), False)
    new_increment = earlier + pushed
    return (new_dual_model[None], new_dual_obs[None], new_increment[None])


def solution(mesh):
    placed = (
        P("members", None, None, None, "space", "window"),
        P(("members", "window"), None, None, "space", None),
        P(("members", "window"), None, None, "space", None),
        P(("members", "window"), None, None, "space", None),
        P(("members", "window"), None, None, "space", None),
        P(("members", "window"), None, None, "space", None),
        P(),
        P(("members", "window"), None, None),
        P(("members", "window"), None, None),
        P(("members", "window")),
    )
    return jax.shard_map(
        body,
        mesh=mesh,
        in_specs=placed,
        out_specs=(
            P(("members", "window"), None, None, "space", None),
            P(("members", "window"), None, None, "space", None),
            P(("members", "window"), None, None, "space", None),
        ),
        check_vma=False,
    )
```

profile of v0, /device:TPU:0, one launch (start us, length us, event | category | flops | bytes accessed | tf_op | source)
XLA Modules:
  0.0 112.6 jit_solution(7487561723157025695)
XLA Ops:
  0.7 6.5 %all-to-all-start = ((bf16[4,4,5,4,8,96]{5,4,3,2,1,0:T(8,128)(2,1)}), bf16[4,4,5,4,8,96]{5,4,3,2,1,0:T(8,128)(2,1)S(1)}, u32[]{:S(2)}, u32[]{:S(2)}) async-start(bf16[4,4,5,4,8,96]{5,4,3,2,1,0:T(8,128)(2,1)} %param.22), calls=%async_computation | async-start | bytes 1310720 | tf_op jit(solution)/shard_map/all_to_all | solution.py:104
  7.1 1.0 copy.67
  8.1 1.3 %collective-permute-start = (f32[5,4,8,384]{3,1,2,0:T(4,128)S(1)}, f32[5,4,8,384]{3,1,2,0:T(4,128)S(1)}, u32[]{:S(2)}, u32[]{:S(2)}) collective-permute-start(f32[5,4,8,384]{3,1,2,0:T(4,128)S(1)} %bitcast.142), channel_id=1, source_target_pairs={{4,0},{8,4},{12,8},{5,1},{9,5},{13,9},{6,2},{10,6},{14,10},{7,3},{... | collective-permute-start | bytes 737288 | tf_op jit(solution)/shard_map/ppermute | solution.py:17
  9.6 1.5 %collective-permute-start.5 = (f32[5,4,4,384]{3,1,2,0:T(4,128)S(1)}, f32[5,4,4,384]{3,1,2,0:T(4,128)S(1)}, u32[]{:S(2)}, u32[]{:S(2)}) collective-permute-start(f32[5,4,4,384]{3,1,2,0:T(4,128)S(1)} %get-tuple-element.322), channel_id=1, source_target_pairs={{0,1},{1,2},{2,3},{4,5},{5,6},{6,7},{8,9},{9,10},{10,11},{12,13},{... | collective-permute-start | bytes 368648 | tf_op jit(solution)/shard_map/ppermute | solution.py:25
  11.0 1.3 %collective-permute-start.6 = (f32[5,4,4,384]{3,1,2,0:T(4,128)S(1)}, f32[5,4,4,384]{3,1,2,0:T(4,128)S(1)}, u32[]{:S(2)}, u32[]{:S(2)}) collective-permute-start(f32[5,4,4,384]{3,1,2,0:T(4,128)S(1)} %get-tuple-element.323), channel_id=1, source_target_pairs={{1,0},{2,1},{3,2},{5,4},{6,5},{7,6},{9,8},{10,9},{11,10},{13,12},{... | collective-permute-start | bytes 368648 | tf_op jit(solution)/shard_map/ppermute | solution.py:28
  13.3 2.5 %collective-permute-done.6 = f32[5,4,4,384]{3,1,2,0:T(4,128)S(1)} collective-permute-done((f32[5,4,4,384]{3,1,2,0:T(4,128)S(1)}, f32[5,4,4,384]{3,1,2,0:T(4,128)S(1)}, u32[]{:S(2)}, u32[]{:S(2)}) %collective-permute-start.6) | collective-permute-done | bytes 122912 | tf_op jit(solution)/shard_map/ppermute | solution.py:28
  15.9 9.2 %collective-permute-done = f32[5,4,8,384]{3,1,2,0:T(4,128)S(1)} collective-permute-done((f32[5,4,8,384]{3,1,2,0:T(4,128)S(1)}, f32[5,4,8,384]{3,1,2,0:T(4,128)S(1)}, u32[]{:S(2)}, u32[]{:S(2)}) %collective-permute-start) | collective-permute-done | bytes 245792 | tf_op jit(solution)/shard_map/ppermute | solution.py:17
  25.3 1.3 %collective-permute-start.1 = (f32[9,4,4,384]{3,1,2,0:T(4,128)S(1)}, f32[9,4,4,384]{3,1,2,0:T(4,128)S(1)}, u32[]{:S(2)}, u32[]{:S(2)}) collective-permute-start(f32[9,4,4,384]{3,1,2,0:T(4,128)S(1)} %get-tuple-element.294), channel_id=1, source_target_pairs={{0,1},{1,2},{2,3},{4,5},{5,6},{6,7},{8,9},{9,10},{10,11},{12,13},{... | collective-permute-start | bytes 663560 | tf_op jit(solution)/shard_map/ppermute | solution.py:25
  26.6 1.3 %collective-permute-start.2 = (f32[9,4,4,384]{3,1,2,0:T(4,128)S(1)}, f32[9,4,4,384]{3,1,2,0:T(4,128)S(1)}, u32[]{:S(2)}, u32[]{:S(2)}) collective-permute-start(f32[9,4,4,384]{3,1,2,0:T(4,128)S(1)} %get-tuple-element.295), channel_id=1, source_target_pairs={{1,0},{2,1},{3,2},{5,4},{6,5},{7,6},{9,8},{10,9},{11,10},{13,12},{... | collective-permute-start | bytes 663560 | tf_op jit(solution)/shard_map/ppermute | solution.py:28
  27.9 1.2 %fusion.70 = (f32[5,4,14,383]{3,1,2,0:T(4,128)}, f32[5,4,14,383]{3,1,2,0:T(4,128)}) fusion(f32[5,4,16,384]{3,1,2,0:T(4,128)S(1)} %pad_maximum_fusion.1), kind=kLoop, calls=%fused_computation.159 | loop fusion | bytes 1715840 | tf_op jit(solution)/shard_map/slice | solution.py:50
  29.1 2.6 %collective-permute-done.2 = f32[9,4,4,384]{3,1,2,0:T(4,128)S(1)} collective-permute-done((f32[9,4,4,384]{3,1,2,0:T(4,128)S(1)}, f32[9,4,4,384]{3,1,2,0:T(4,128)S(1)}, u32[]{:S(2)}, u32[]{:S(2)}) %collective-permute-start.2) | collective-permute-done | bytes 221216 | tf_op jit(solution)/shard_map/ppermute | solution.py:28
  33.2 6.3 %collective-permute-start.3 = (bf16[4,5,4,4,384]{4,2,3,1,0:T(4,128)(2,1)S(1)}, bf16[4,5,4,4,384]{4,2,3,1,0:T(4,128)(2,1)S(1)}, u32[]{:S(2)}, u32[]{:S(2)}) collective-permute-start(bf16[4,5,4,4,384]{4,2,3,1,0:T(4,128)(2,1)S(1)} %get-tuple-element.292), channel_id=1, source_target_pairs={{0,1},{1,2},{2,3},{4,5},{5,6},{6,7},{8,9},{9,10},{10,11},{12,13},{... | collective-permute-start | bytes 737288 | tf_op jit(solution)/shard_map/ppermute | solution.py:25
  39.5 1.5 %collective-permute-start.4 = (bf16[4,5,4,4,384]{4,2,3,1,0:T(4,128)(2,1)S(1)}, bf16[4,5,4,4,384]{4,2,3,1,0:T(4,128)(2,1)S(1)}, u32[]{:S(2)}, u32[]{:S(2)}) collective-permute-start(bf16[4,5,4,4,384]{4,2,3,1,0:T(4,128)(2,1)S(1)} %get-tuple-element.293), channel_id=1, source_target_pairs={{1,0},{2,1},{3,2},{5,4},{6,5},{7,6},{9,8},{10,9},{11,10},{13,12},{... | collective-permute-start | bytes 737288 | tf_op jit(solution)/shard_map/ppermute | solution.py:28
  41.4 1.6 %collective-permute-done.4 = bf16[4,5,4,4,384]{4,2,3,1,0:T(4,128)(2,1)S(1)} collective-permute-done((bf16[4,5,4,4,384]{4,2,3,1,0:T(4,128)(2,1)S(1)}, bf16[4,5,4,4,384]{4,2,3,1,0:T(4,128)(2,1)S(1)}, u32[]{:S(2)}, u32[]{:S(2)}) %collective-permute-start.4) | collective-permute-done | bytes 245792 | tf_op jit(solution)/shard_map/ppermute | solution.py:28
  45.2 1.1 multiply_reduce_fusion
  46.3 0.9 fusion.2
  47.6 0.7 copy-done.1
  48.4 0.6 add_multiply_fusion
  49.5 0.9 multiply_reduce_fusion.2
  51.6 0.8 fusion.13
  52.8 0.8 multiply_reduce_fusion.4
  54.2 0.9 fusion.78
  55.1 0.6 slice_bitcast_fusion.19
  56.0 0.7 fusion.24
  57.3 0.9 multiply_reduce_fusion.6
  58.9 21.7 %all-gather = f32[20,4,8,384]{3,2,1,0:T(8,128)S(1)} all-gather(f32[5,4,8,384]{3,2,1,0:T(8,128)S(1)} %copy.22), channel_id=2, replica_groups=mesh['members'=2,'window'=4,'space'=4] {'window'}, dimensions={0}, use_global_device_ids=true | all-gather | bytes 1228800 | tf_op jit(solution)/shard_map/all_gather | solution.py:35
  82.3 2.4 %collective-permute-start.7 = (bf16[5,4,8,384]{3,1,2,0:T(4,128)(2,1)S(1)}, bf16[5,4,8,384]{3,1,2,0:T(4,128)(2,1)S(1)}, u32[]{:S(2)}, u32[]{:S(2)}) collective-permute-start(bf16[5,4,8,384]{3,1,2,0:T(4,128)(2,1)S(1)} %fusion.49), channel_id=1, source_target_pairs={{0,4},{4,8},{8,12},{1,5},{5,9},{9,13},{2,6},{6,10},{10,14},{3,7},{... | collective-permute-start | bytes 368648 | tf_op jit(solution)/shard_map/ppermute | solution.py:17
  84.7 1.1 fusion.52
  85.8 0.7 copy.35
  87.4 23.4 %all-gather.1 = f32[20,4,8,384]{3,2,1,0:T(8,128)S(1)} all-gather(f32[5,4,8,384]{3,2,1,0:T(8,128)S(1)} %copy.32), channel_id=3, replica_groups=mesh['members'=2,'window'=4,'space'=4] {'window'}, dimensions={0}, use_global_device_ids=true | all-gather | bytes 1228800 | tf_op jit(solution)/shard_map/all_gather | solution.py:35
  111.2 0.7 copy.36
  111.9 0.7 copy.34
  (115 shorter events, 12.5 us)
Async XLA Ops:
  0.6 8.8 %copy-start.3 = (f32[1,5,4,8,384]{4,3,2,1,0:T(8,128)S(1)}, f32[1,5,4,8,384]{4,3,2,1,0:T(8,128)}, u32[]{:S(2)}) copy-start(f32[1,5,4,8,384]{4,3,2,1,0:T(8,128)} %param.24) | copy-start | bytes 737284
  0.6 12.7 %slice-start = ((f32[1,5,4,8,384]{4,3,2,1,0:T(8,128)}), f32[1,1,4,8,384]{4,3,2,1,0:T(8,128)S(1)}, s32[]{:S(2)}) async-start(f32[1,5,4,8,384]{4,3,2,1,0:T(8,128)} %param.24), calls=%async_computation.1 | async-start | bytes 98304 | tf_op jit(solution)/shard_map/slice | solution.py:117
  0.7 12.4 %copy-start.8 = (f32[1,4,4,8,384]{4,3,2,1,0:T(8,128)S(1)}, f32[1,4,4,8,384]{4,3,2,1,0:T(8,128)}, u32[]{:S(2)}) copy-start(f32[1,4,4,8,384]{4,3,2,1,0:T(8,128)} %param.26) | copy-start | bytes 589828
  0.7 12.5 %copy-start.14 = (f32[1,5,4]{1,2,0:T(4,128)S(1)}, f32[1,5,4]{1,2,0:T(4,128)}, u32[]{:S(2)}) copy-start(f32[1,5,4]{1,2,0:T(4,128)} %param.29) | copy-start | bytes 244
  0.7 31.2 %all-to-all-start = ((bf16[4,4,5,4,8,96]{5,4,3,2,1,0:T(8,128)(2,1)}), bf16[4,4,5,4,8,96]{5,4,3,2,1,0:T(8,128)(2,1)S(1)}, u32[]{:S(2)}, u32[]{:S(2)}) async-start(bf16[4,4,5,4,8,96]{5,4,3,2,1,0:T(8,128)(2,1)} %param.22), calls=%async_computation | async-start | bytes 1310720 | tf_op jit(solution)/shard_map/all_to_all | solution.py:104
  8.1 16.9 %collective-permute-start = (f32[5,4,8,384]{3,1,2,0:T(4,128)S(1)}, f32[5,4,8,384]{3,1,2,0:T(4,128)S(1)}, u32[]{:S(2)}, u32[]{:S(2)}) collective-permute-start(f32[5,4,8,384]{3,1,2,0:T(4,128)S(1)} %bitcast.142), channel_id=1, source_target_pairs={{4,0},{8,4},{12,8},{5,1},{9,5},{13,9},{6,2},{10,6},{14,10},{7,3},{... | collective-permute-start | bytes 737288 | tf_op jit(solution)/shard_map/ppermute | solution.py:17
  9.6 3.8 %collective-permute-start.5 = (f32[5,4,4,384]{3,1,2,0:T(4,128)S(1)}, f32[5,4,4,384]{3,1,2,0:T(4,128)S(1)}, u32[]{:S(2)}, u32[]{:S(2)}) collective-permute-start(f32[5,4,4,384]{3,1,2,0:T(4,128)S(1)} %get-tuple-element.322), channel_id=1, source_target_pairs={{0,1},{1,2},{2,3},{4,5},{5,6},{6,7},{8,9},{9,10},{10,11},{12,13},{... | collective-permute-start | bytes 368648 | tf_op jit(solution)/shard_map/ppermute | solution.py:25
  11.0 4.8 %collective-permute-start.6 = (f32[5,4,4,384]{3,1,2,0:T(4,128)S(1)}, f32[5,4,4,384]{3,1,2,0:T(4,128)S(1)}, u32[]{:S(2)}, u32[]{:S(2)}) collective-permute-start(f32[5,4,4,384]{3,1,2,0:T(4,128)S(1)} %get-tuple-element.323), channel_id=1, source_target_pairs={{1,0},{2,1},{3,2},{5,4},{6,5},{7,6},{9,8},{10,9},{11,10},{13,12},{... | collective-permute-start | bytes 368648 | tf_op jit(solution)/shard_map/ppermute | solution.py:28
  25.3 3.8 %collective-permute-start.1 = (f32[9,4,4,384]{3,1,2,0:T(4,128)S(1)}, f32[9,4,4,384]{3,1,2,0:T(4,128)S(1)}, u32[]{:S(2)}, u32[]{:S(2)}) collective-permute-start(f32[9,4,4,384]{3,1,2,0:T(4,128)S(1)} %get-tuple-element.294), channel_id=1, source_target_pairs={{0,1},{1,2},{2,3},{4,5},{5,6},{6,7},{8,9},{9,10},{10,11},{12,13},{... | collective-permute-start | bytes 663560 | tf_op jit(solution)/shard_map/ppermute | solution.py:25
  26.6 5.1 %collective-permute-start.2 = (f32[9,4,4,384]{3,1,2,0:T(4,128)S(1)}, f32[9,4,4,384]{3,1,2,0:T(4,128)S(1)}, u32[]{:S(2)}, u32[]{:S(2)}) collective-permute-start(f32[9,4,4,384]{3,1,2,0:T(4,128)S(1)} %get-tuple-element.295), channel_id=1, source_target_pairs={{1,0},{2,1},{3,2},{5,4},{6,5},{7,6},{9,8},{10,9},{11,10},{13,12},{... | collective-permute-start | bytes 663560 | tf_op jit(solution)/shard_map/ppermute | solution.py:28
  33.2 8.1 %collective-permute-start.3 = (bf16[4,5,4,4,384]{4,2,3,1,0:T(4,128)(2,1)S(1)}, bf16[4,5,4,4,384]{4,2,3,1,0:T(4,128)(2,1)S(1)}, u32[]{:S(2)}, u32[]{:S(2)}) collective-permute-start(bf16[4,5,4,4,384]{4,2,3,1,0:T(4,128)(2,1)S(1)} %get-tuple-element.292), channel_id=1, source_target_pairs={{0,1},{1,2},{2,3},{4,5},{5,6},{6,7},{8,9},{9,10},{10,11},{12,13},{... | collective-permute-start | bytes 737288 | tf_op jit(solution)/shard_map/ppermute | solution.py:25
  39.5 3.4 %collective-permute-start.4 = (bf16[4,5,4,4,384]{4,2,3,1,0:T(4,128)(2,1)S(1)}, bf16[4,5,4,4,384]{4,2,3,1,0:T(4,128)(2,1)S(1)}, u32[]{:S(2)}, u32[]{:S(2)}) collective-permute-start(bf16[4,5,4,4,384]{4,2,3,1,0:T(4,128)(2,1)S(1)} %get-tuple-element.293), channel_id=1, source_target_pairs={{1,0},{2,1},{3,2},{5,4},{6,5},{7,6},{9,8},{10,9},{11,10},{13,12},{... | collective-permute-start | bytes 737288 | tf_op jit(solution)/shard_map/ppermute | solution.py:28
  44.5 0.7 copy-start.12
  47.2 1.0 copy-start.1
  47.2 1.1 %copy-start.2 = (f32[5,4,14,383]{3,1,2,0:T(4,128)S(1)}, f32[5,4,14,383]{3,1,2,0:T(4,128)}, u32[]{:S(2)}) copy-start(f32[5,4,14,383]{3,1,2,0:T(4,128)} %get-tuple-element.291) | copy-start | bytes 1286884
  57.3 1.5 %copy-start = (f32[1,5,4,8,384]{4,3,2,1,0:T(8,128)S(1)}, f32[1,5,4,8,384]{4,3,2,1,0:T(8,128)}, u32[]{:S(2)}) copy-start(f32[1,5,4,8,384]{4,3,2,1,0:T(8,128)} %param.23) | copy-start | bytes 737284
  80.7 0.9 copy-start.5
  80.7 1.1 copy-start.6
  80.7 1.2 %copy-start.7 = (f32[5,4,8,384]{3,2,1,0:T(8,128)S(1)}, f32[5,4,8,384]{3,2,1,0:T(8,128)}, u32[]{:S(2)}) copy-start(f32[5,4,8,384]{3,2,1,0:T(8,128)} %get-tuple-element.244) | copy-start | bytes 737284
  80.7 4.0 %copy-start.9 = (f32[1,4,4,8,384]{4,3,2,1,0:T(8,128)S(1)}, f32[1,4,4,8,384]{4,3,2,1,0:T(8,128)}, u32[]{:S(2)}) copy-start(f32[1,4,4,8,384]{4,3,2,1,0:T(8,128)} %param.26) | copy-start | bytes 589828
  80.7 4.0 %copy-start.11 = (f32[1,1,4,8,384]{4,2,3,1,0:T(4,128)S(1)}, f32[1,1,4,8,384]{4,2,3,1,0:T(4,128)}, u32[]{:S(2)}) copy-start(f32[1,1,4,8,384]{4,2,3,1,0:T(4,128)} %slice_bitcast_fusion.19) | copy-start | bytes 147460
  80.8 4.0 %copy-start.13 = (f32[1,4,4]{2,1,0:T(4,128)S(1)}, f32[1,4,4]{2,1,0:T(4,128)}, u32[]{:S(2)}) copy-start(f32[1,4,4]{2,1,0:T(4,128)} %param.30) | copy-start | bytes 196
  81.1 6.0 %copy-start.4 = (f32[1,5,4,8,384]{4,3,2,1,0:T(8,128)S(1)}, f32[1,5,4,8,384]{4,3,2,1,0:T(8,128)}, u32[]{:S(2)}) copy-start(f32[1,5,4,8,384]{4,3,2,1,0:T(8,128)} %param.24) | copy-start | bytes 737284
  81.1 6.0 %copy-start.10 = (f32[1,5,4,8,384]{4,3,2,1,0:T(8,128)S(1)}, f32[1,5,4,8,384]{4,3,2,1,0:T(8,128)}, u32[]{:S(2)}) copy-start(f32[1,5,4,8,384]{4,3,2,1,0:T(8,128)} %param.25) | copy-start | bytes 737284
  82.3 4.8 %collective-permute-start.7 = (bf16[5,4,8,384]{3,1,2,0:T(4,128)(2,1)S(1)}, bf16[5,4,8,384]{3,1,2,0:T(4,128)(2,1)S(1)}, u32[]{:S(2)}, u32[]{:S(2)}) collective-permute-start(bf16[5,4,8,384]{3,1,2,0:T(4,128)(2,1)S(1)} %fusion.49), channel_id=1, source_target_pairs={{0,4},{4,8},{8,12},{1,5},{5,9},{9,13},{2,6},{6,10},{10,14},{3,7},{... | collective-permute-start | bytes 368648 | tf_op jit(solution)/shard_map/ppermute | solution.py:17
where the time goes:
time: 113 us
  blocking collectives  45.1 us (40%)
  starting transfers between devices  23.3 us (21%)
  waiting for transfers between devices  16.4 us (15%)
  other arithmetic  13.3 us (12%)
  local copies, waits for them, and re-layouts  12.4 us (11%)
  between operations  2.02 us (2%)
    all_gather x2, blocking collectives, entering(): pieces = lax.all_gather(value, axis)  45.1 us
    ppermute x2, waiting for transfers between devices, shifted(): return lax.ppermute(block, axis, route)  9.77 us
    ppermute x3, starting transfers between devices, padded(): lax.ppermute(lax.slice_in_dim(block, block.shape[dim] - width, None, axis...  9.07 us
    ppermute x3, waiting for transfers between devices, padded(): lax.ppermute(lax.slice_in_dim(block, 0, width, axis=dim), axis, backward)  6.66 us
    all_to_all x1, starting transfers between devices, body(): lax.all_to_all(trajectory, 'window', split_axis=0, concat_axis=5, tiled=T...  6.46 us
    unnamed x36, local copies, waits for them, and re-layouts  5.11 us
    slice x12, local copies, waits for them, and re-layouts, along_y(): north = jnp.concatenate([field[..., 1:], edge], -1)  4.48 us
    ppermute x3, starting transfers between devices, padded(): lax.ppermute(lax.slice_in_dim(block, 0, width, axis=dim), axis, backward)  4.06 us
  transfers between devices with their start and end apart: 9, of which 5 were waited for; matrix products, arithmetic and copies ran while one was open for 5% of the time, Pallas kernels for 0%

commit v1 on v0

v1 whole, which is shorter than its diff:
```python
import jax
import jax.numpy as jnp
from jax import lax
from jax.experimental import pallas as pl
from jax.experimental.pallas import tpu as pltpu
from jax.sharding import PartitionSpec as P

LANES = 128
SUB = 8
CODE_MAX = 32766.0
ROUNDER = 12582912.0

diffusion = 0.2
advection = 0.2
coupling_gain = 0.5
keep = 1.0 - 4.0 * diffusion
half_adv = 0.5 * advection

VMEM = pl.BlockSpec(memory_space=pltpu.VMEM)
SMEM = pl.BlockSpec(memory_space=pltpu.SMEM)


def lane_pieces(src, first, width, target):
    out = []
    done = 0
    while done < width:
        a, b = first + done, target + done
        n = min(width - done, LANES - a % LANES, LANES - b % LANES)
        shift = (b - a) % LANES
        out.append((b // LANES, b % LANES, b % LANES + n, a // LANES, shift))
        done += n
    return out


def model_kernel(
    steps, nvar, windows, spaces, tiles, part,
    coupling_ref, var_ref, count_ref, traj_ref, fields_ref, after_ref,
    payload_ref, images_ref,
    x_ref, s_ref, a_ref, ends_ref, q_ref,
):
    rows = spaces * SUB
    me = lax.axis_index("window")
    level = lax.axis_index("space")
    lane = lax.broadcasted_iota(jnp.int32, (SUB, LANES), 1)
    zero = jnp.zeros((SUB, LANES), jnp.float32)
    cells = [(b, t) for b in range(spaces) for t in range(tiles)]

    for t in range(tiles):
        for edge in (0, SUB + rows):
            for v in range(nvar):
                for p in range(2):
                    s_ref[p, v, t, edge : edge + SUB, :] = zero
                    a_ref[p, v, t, edge : edge + SUB, :] = zero
            for j in range(steps):
                x_ref[j, 0, t, edge : edge + SUB, :] = zero

    def gather(b, carry):
        here = pl.ds(pl.multiple_of(SUB + b * SUB, SUB), SUB)
        for v in range(nvar):
            rolled = {}
            built = {}
            for w in range(windows):
                wide = traj_ref[w * spaces + b, v].astype(jnp.float32)
                total = wide.shape[1]
                short = -total % LANES
                if short:
                    wide = jnp.concatenate([wide, jnp.zeros((SUB, short), jnp.float32)], 1)
                for j in range(steps):
                    for tile, low, high, source, shift in lane_pieces(
                        None, j * part, part, w * part
                    ):
                        key = (w, source, shift)
                        if key not in rolled:
                            value = wide[:, source * LANES : (source + 1) * LANES]
                            rolled[key] = pltpu.roll(value, shift, 1) if shift else value
                        if low == 0:
                            old = built.get((j, tile), None)
                            built[j, tile] = (
                                rolled[key]
                                if old is None
                                else jnp.where(lane < high, rolled[key], old)
                            )
                        else:
                            old = built.get((j, tile), zero)
                            built[j, tile] = jnp.where(lane >= low, rolled[key], old)
            for (j, tile), value in built.items():
                x_ref[j, v, tile, here, :] = value
        for v in range(nvar):
            for t in range(tiles):
                cut = slice(t * LANES, (t + 1) * LANES)
                s_ref[0, v, t, here, :] = fields_ref[b, v, :, cut]
                a_ref[0, v, t, here, :] = -after_ref[b, v, :, cut]
        return carry

    lax.fori_loop(0, spaces, gather, 0)

    mix = [[coupling_gain * coupling_ref[v, u] for u in range(nvar)] for v in range(nvar)]

    def from_north(row):
        turned = [pltpu.roll(value, LANES - 1, 1) for value in row]
        return [
            jnp.where(lane < LANES - 1, turned[t], turned[(t + 1) % tiles]) for t in range(tiles)
        ]

    def from_south(row):
        turned = [pltpu.roll(value, 1, 1) for value in row]
        return [jnp.where(lane > 0, turned[t], turned[t - 1]) for t in range(tiles)]

    def masked_last(row):
        return row[:-1] + [jnp.where(lane < LANES - 1, row[-1], 0.0)]

    def masked_first(row):
        return [jnp.where(lane > 0, row[0], 0.0)] + row[1:]

    def tangent(j, carry):
        now = lax.rem(j, 2)

        def block(b, inner):
            first = pl.multiple_of(SUB + b * SUB, SUB)
            here = pl.ds(first, SUB)
            up, down = pl.ds(first + 1, SUB), pl.ds(first - 1, SUB)
            x = [[x_ref[j, u, t, here, :] for t in range(tiles)] for u in range(nvar)]
            ce = [diffusion - half_adv * value for value in x[0]]
            cw = [diffusion + half_adv * value for value in x[0]]
            cn = masked_last([diffusion - half_adv * value for value in x[1]])
            cs = masked_first([diffusion + half_adv * value for value in x[1]])
            s = [[s_ref[now, u, t, here, :] for t in range(tiles)] for u in range(nvar)]
            xs = [[x[u][t] * s[u][t] for t in range(tiles)] for u in range(nvar)]
            for v in range(nvar):
                north, south = from_north(s[v]), from_south(s[v])
                for t in range(tiles):
                    fresh = keep * s[v][t] + ce[t] * s_ref[now, v, t, up, :]
                    fresh = fresh + cw[t] * s_ref[now, v, t, down, :]
                    fresh = fresh + cn[t] * north[t] + cs[t] * south[t]
                    for u in range(nvar):
                        fresh = fresh + mix[v][u] * xs[u][t]
                    s_ref[1 - now, v, t, here, :] = fresh
            for t in range(tiles):
                images_ref[b, j, :, t * LANES : (t + 1) * LANES] = s[0][t]
            return inner

        return lax.fori_loop(0, spaces, block, carry)

    lax.fori_loop(0, steps, tangent, 0)

    def adjoint(turn, carry):
        now = lax.rem(turn, 2)
        j = steps - 1 - turn
        seen = jnp.where(j < count_ref[0], 1.0, 0.0)

        def block(b, inner):
            first = pl.multiple_of(SUB + b * SUB, SUB)
            here = pl.ds(first, SUB)
            up, down = pl.ds(first + 1, SUB), pl.ds(first - 1, SUB)
            x = [[x_ref[j, u, t, here, :] for t in range(tiles)] for u in range(nvar)]
            ce = [diffusion + half_adv * x_ref[j, 0, t, up, :] for t in range(tiles)]
            cw = [diffusion - half_adv * x_ref[j, 0, t, down, :] for t in range(tiles)]
            cn = masked_first([diffusion + half_adv * value for value in x[1]])
            cs = masked_last([diffusion - half_adv * value for value in x[1]])
            a = [[a_ref[now, u, t, here, :] for t in range(tiles)] for u in range(nvar)]
            for u in range(nvar):
                north = from_north([cn[t] * a[u][t] for t in range(tiles)])
                south = from_south([cs[t] * a[u][t] for t in range(tiles)])
                for t in range(tiles):
                    fresh = keep * a[u][t] + ce[t] * a_ref[now, u, t, up, :]
                    fresh = fresh + cw[t] * a_ref[now, u, t, down, :]
                    fresh = fresh + north[t] + south[t]
                    pull = mix[0][u] * a[0][t]
                    for v in range(1, nvar):
                        pull = pull + mix[v][u] * a[v][t]
                    fresh = fresh + x[u][t] * pull
                    if u == 0:
                        fresh = fresh + seen * fields_ref[
                            b, nvar + j, :, t * LANES : (t + 1) * LANES
                        ]
                    a_ref[1 - now, u, t, here, :] = fresh
            return inner

        return lax.fori_loop(0, spaces, block, carry)

    lax.fori_loop(0, steps, adjoint, 0)

    end = steps % 2
    total_var = []
    for v in range(nvar):
        total_var.append(
            lax.fori_loop(
                0, windows,
                lambda w, acc: acc + jnp.where(w <= me, var_ref[w, v, level], 0.0),
                jnp.float32(0.0),
            )
        )

    def coded(planes):
        scales = zero
        out = []
        for v in range(nvar):
            big = jnp.abs(planes[v][0])
            for t in range(1, tiles):
                big = jnp.maximum(big, jnp.abs(planes[v][t]))
            big = jnp.max(big, axis=1, keepdims=True)
            power = jnp.clip(jnp.ceil(jnp.log2(jnp.maximum(big, 1e-30))), -90.0, 126.0)
            scales = jnp.where(lane == v, power, scales)
            gain = CODE_MAX * jnp.exp2(-power)
            for t in range(tiles):
                scaled = jnp.clip(planes[v][t] * gain, -CODE_MAX, CODE_MAX)
                out.append((scaled + ROUNDER) - ROUNDER)
        out.append(scales)
        while len(out) % 2:
            out.append(zero)
        pairs = [jnp.concatenate(out[i : i + 2], 0) for i in range(0, len(out), 2)]
        return [pair.astype(jnp.int32).astype(jnp.int16) for pair in pairs]

    def finish(b, carry):
        first = pl.multiple_of(SUB + b * SUB, SUB)
        here = pl.ds(first, SUB)
        back, ahead = [], []
        for v in range(nvar):
            tv, gv = [], []
            for t in range(tiles):
                cut = slice(t * LANES, (t + 1) * LANES)
                term = a_ref[end, v, t, here, :] + after_ref[b, v, :, cut]
                given = fields_ref[b, nvar + steps + v, :, cut] - fields_ref[b, v, :, cut]
                tv.append(term)
                gv.append(given + s_ref[end, v, t, here, :] + total_var[v] * term)
            back.append(tv)
            ahead.append(gv)
        for kind, planes in ((0, back), (1, ahead)):
            for i, pair in enumerate(coded(planes)):
                q_ref[kind, b, i * 2 * SUB : (i + 1) * 2 * SUB, :] = pair
        return carry

    lax.fori_loop(0, spaces, finish, 0)

    def send(w, carry):
        kind = jnp.where(w <= me, 0, 1)
        for b in range(spaces):
            payload_ref[w * spaces + b] = q_ref[kind, b]
        return carry

    lax.fori_loop(0, windows, send, 0)


def final_kernel(
    steps, nvar, windows, spaces, tiles,
    var_ref, noise_ref, count_ref, codes_ref, images_ref, dual_ref, inc_ref, rhs_ref, dobs_ref, innov_ref,
    ndm_ref, ndo_ref, ninc_ref,
):
    me = lax.axis_index("window")
    for lev in range(spaces):
        empty = [jnp.zeros((SUB, LANES), jnp.float32)] * (2 * nvar * tiles)

        def add(w, sums):
            source = w * spaces + lev
            later = jnp.where(w >= me, 1.0 / CODE_MAX, 0.0)
            earlier = jnp.where(w < me, 1.0 / CODE_MAX, 0.0)
            parts = []
            for i in range(codes_ref.shape[1] // (2 * SUB)):
                pair = codes_ref[source, i * 2 * SUB : (i + 1) * 2 * SUB, :]
                pair = pair.astype(jnp.int32).astype(jnp.float32)
                parts += [pair[:SUB], pair[SUB:]]
            scales = jnp.exp2(parts[nvar * tiles])
            out = list(sums)
            for v in range(nvar):
                column = scales[:, v : v + 1]
                up, down = column * later, column * earlier
                for t in range(tiles):
                    i = v * tiles + t
                    out[i] = out[i] + up * parts[i]
                    out[nvar * tiles + i] = out[nvar * tiles + i] + down * parts[i]
            return tuple(out)

        sums = lax.fori_loop(0, windows, add, tuple(empty), unroll=windows <= 4)
        for v in range(nvar):
            total = lax.fori_loop(
                0, windows,
                lambda w, acc: acc + jnp.where(w <= me, var_ref[w, v, lev], 0.0),
                jnp.float32(0.0),
            )
            for t in range(tiles):
                cut = slice(t * LANES, (t + 1) * LANES)
                tail = sums[v * tiles + t]
                head = sums[(nvar + v) * tiles + t]
                ndm_ref[0, v, lev, :, cut] = -(dual_ref[0, v, lev, :, cut] + tail)
                given = rhs_ref[0, v, lev, :, cut] - inc_ref[0, v, lev, :, cut]
                ninc_ref[0, v, lev, :, cut] = head + given + total * tail
        for j in range(steps):
            seen = jnp.where(j < count_ref[0], 1.0, 0.0)
            noise = jnp.full((SUB, LANES), noise_ref[0, j, lev])
            inverse = seen / noise
            for t in range(tiles):
                cut = slice(t * LANES, (t + 1) * LANES)
                gap = innov_ref[0, j, lev, :, cut] - noise * dobs_ref[0, j, lev, :, cut]
                gap = gap - images_ref[lev, j, :, cut]
                ndo_ref[0, j, lev, :, cut] = gap * inverse


def shifted(block, axis, distance):
    devices = range(lax.axis_size(axis))
    route = [(i - distance, i) for i in devices if i - distance in devices]
    return lax.ppermute(block, axis, route)


def body(
    trajectory,
    dual_model,
    increment,
    model_rhs,
    dual_obs,
    innovation,
    coupling,
    error_var,
    obs_var,
    obs_count,
):
    windows, spaces = lax.axis_size("window"), lax.axis_size("space")
    _, steps, nvar, levels, rows, part = trajectory.shape
    columns = dual_model.shape[-1]
    tiles = columns // LANES
    assert trajectory.shape[0] == windows and levels == spaces and rows == SUB
    assert columns == tiles * LANES == windows * part

    after = shifted(dual_model[0], "window", -1)
    sending = trajectory.transpose(0, 3, 2, 4, 1, 5)
    sending = sending.reshape(windows * levels, nvar, rows, steps * part)
    traj = lax.all_to_all(sending, ("window", "space"), 0, 0, tiled=True)
    fields = jnp.concatenate([increment[0], dual_obs[0], model_rhs[0]], 0)
    fields = lax.all_to_all(fields.transpose(1, 0, 2, 3), "space", 0, 0, tiled=True)
    after = lax.all_to_all(after.transpose(1, 0, 2, 3), "space", 0, 0, tiled=True)
    variances = lax.all_gather(error_var[0], "window")

    code_rows = -(-(nvar * tiles + 1) // 2) * 2 * SUB
    padded = SUB + spaces * rows + SUB
    payload, images = pl.pallas_call(
        lambda *refs: model_kernel(steps, nvar, windows, spaces, tiles, part, *refs),
        out_shape=(
            jax.ShapeDtypeStruct((windows * spaces, code_rows, LANES), jnp.int16),
            jax.ShapeDtypeStruct((spaces, steps, rows, columns), jnp.float32),
        ),
        in_specs=[SMEM, SMEM, SMEM, VMEM, VMEM, VMEM],
        out_specs=(VMEM, VMEM),
        scratch_shapes=[
            pltpu.VMEM((steps, nvar, tiles, padded, LANES), jnp.float32),
            pltpu.VMEM((2, nvar, tiles, padded, LANES), jnp.float32),
            pltpu.VMEM((2, nvar, tiles, padded, LANES), jnp.float32),
            pltpu.VMEM((SUB, LANES), jnp.float32),
            pltpu.VMEM((2, spaces, code_rows, LANES), jnp.int16),
        ],
        compiler_params=pltpu.CompilerParams(vmem_limit_bytes=24 * 1024 * 1024),
    )(coupling, variances, obs_count, traj, fields, after)

    codes = lax.all_to_all(payload, ("window", "space"), 0, 0, tiled=True)
    images = lax.all_to_all(images, "space", 0, 0, tiled=True)

    shapes = [jax.ShapeDtypeStruct(a.shape, jnp.float32) for a in (dual_model, dual_obs, increment)]
    return pl.pallas_call(
        lambda *refs: final_kernel(steps, nvar, windows, spaces, tiles, *refs),
        out_shape=tuple(shapes),
        in_specs=[SMEM, SMEM, SMEM] + [VMEM] * 7,
        out_specs=(VMEM, VMEM, VMEM),
        compiler_params=pltpu.CompilerParams(vmem_limit_bytes=24 * 1024 * 1024),
    )(
        variances, obs_var, obs_count, codes, images,
        dual_model, increment, model_rhs, dual_obs, innovation,
    )


def solution(mesh):
    placed = (
        P("members", None, None, None, "space", "window"),
        P(("members", "window"), None, None, "space", None),
        P(("members", "window"), None, None, "space", None),
        P(("members", "window"), None, None, "space", None),
        P(("members", "window"), None, None, "space", None),
        P(("members", "window"), None, None, "space", None),
        P(),
        P(("members", "window"), None, None),
        P(("members", "window"), None, None),
        P(("members", "window")),
    )
    return jax.shard_map(
        body,
        mesh=mesh,
        in_specs=placed,
        out_specs=(
            P(("members", "window"), None, None, "space", None),
            P(("members", "window"), None, None, "space", None),
            P(("members", "window"), None, None, "space", None),
        ),
        check_vma=False,
    )
```

time: 113 us -> 98.7 us (0.87)
  other arithmetic: 13.3 us -> 0.91 us
  Pallas kernels: 0 us -> 12.2 us
  starting transfers between devices: 23.3 us -> 12.6 us
  local copies, waits for them, and re-layouts: 12.4 us -> 4.18 us
  waiting for transfers between devices: 16.4 us -> 22.6 us
    all_gather x2 -> x1, blocking collectives: 45.1 us -> 19.3 us  [body(): variances = lax.all_gather(error_var[0], 'window')]
    all_to_all x0 -> x2, blocking collectives: none -> 25 us  [the longest x1 17.2 us: body(): codes = lax.all_to_all(payload, ('window', 'space'), 0, 0, tiled=True)]
    ppermute x6 -> x0, starting transfers between devices: 13.1 us -> none  [the longest x3 9.07 us: padded(): lax.ppermute(lax.slice_in_dim(block, block.shape[dim] - width, None, axis...]
    all_to_all x1 -> x3, waiting for transfers between devices: 0.01 us -> 12.9 us  [the longest x1 8.97 us: body(): lax.all_to_all(fields.transpose(1, 0, 2, 3), 'space', 0, 0, tiled=True)]
    pallas_call x0 -> x2, Pallas kernels: none -> 12.2 us  [the longest x1 9.37 us: body(): pl.pallas_call(lambda *refs: model_kernel(steps, nvar, windows, spaces, t...]
    ppermute x6 -> x0, waiting for transfers between devices: 6.67 us -> none  [the longest x3 6.66 us: padded(): lax.ppermute(lax.slice_in_dim(block, 0, width, axis=dim), axis, backward)]
    mul x25 -> x0, other arithmetic: 5.91 us -> none  [the longest x4 2.98 us: body(): fresh = fresh * valid_rows(turn + 1 - margin, length - 2, tile)]
    all_to_all x1 -> x3, starting transfers between devices: 6.46 us -> 11.3 us  [the longest x1 4.26 us: body(): traj = lax.all_to_all(sending, ('window', 'space'), 0, 0, tiled=True)]
  transfers between devices with their start and end apart: 9 -> 4, of which waited for: 5 -> 3; matrix products, arithmetic and copies ran while one was open for 5% -> 3% of each run, Pallas kernels for 0% -> 0%
where the time goes in v1:
time: 98.7 us; the launch traced here: 98.1 us
  blocking collectives  44.3 us (45%)
  waiting for transfers between devices  22.6 us (23%)
  starting transfers between devices  12.6 us (13%)
  Pallas kernels  12.2 us (12%)
  local copies, waits for them, and re-layouts  4.18 us (4%)
  between operations  1.39 us (1%)
    all_gather x1, blocking collectives, body(): variances = lax.all_gather(error_var[0], 'window')  19.3 us
    all_to_all x1, blocking collectives, body(): codes = lax.all_to_all(payload, ('window', 'space'), 0, 0, tiled=True)  17.2 us
    ppermute x1, waiting for transfers between devices, shifted(): return lax.ppermute(block, axis, route)  9.68 us
    pallas_call x1, Pallas kernels, body(): pl.pallas_call(lambda *refs: model_kernel(steps, nvar, windows, spaces, t...  9.37 us
    all_to_all x1, waiting for transfers between devices, body(): lax.all_to_all(fields.transpose(1, 0, 2, 3), 'space', 0, 0, tiled=True)  8.97 us
    all_to_all x1, blocking collectives, body(): images = lax.all_to_all(images, 'space', 0, 0, tiled=True)  7.83 us
    all_to_all x1, starting transfers between devices, body(): traj = lax.all_to_all(sending, ('window', 'space'), 0, 0, tiled=True)  4.26 us
    all_to_all x1, waiting for transfers between devices, body(): lax.all_to_all(after.transpose(1, 0, 2, 3), 'space', 0, 0, tiled=True)  3.95 us
  transfers between devices with their start and end apart: 4, of which 3 were waited for; matrix products, arithmetic and copies ran while one was open for 3% of the time, Pallas kernels for 0%

profile of v1, /device:TPU:0, one launch (start us, length us, event | category | flops | bytes accessed | tf_op | source)
XLA Modules:
  0.0 98.1 jit_solution(10821066799216910456)
XLA Ops:
  0.6 1.0 copy.30
  1.6 1.3 %collective-permute-start = (f32[5,4,8,384]{3,2,0,1:T(8,128)S(1)}, f32[5,4,8,384]{3,2,0,1:T(8,128)}, u32[]{:S(2)}, u32[]{:S(2)}) collective-permute-start(f32[5,4,8,384]{3,2,0,1:T(8,128)S(1)} %bitcast.16), channel_id=1, source_target_pairs={{4,0},{8,4},{12,8},{5,1},{9,5},{13,9},{6,2},{10,6},{14,10},{7,3},{... | collective-permute-start | bytes 737288 | tf_op jit(solution)/shard_map/ppermute | solution.py:301
  2.9 9.7 %collective-permute-done = f32[5,4,8,384]{3,2,0,1:T(8,128)} collective-permute-done((f32[5,4,8,384]{3,2,0,1:T(8,128)S(1)}, f32[5,4,8,384]{3,2,0,1:T(8,128)}, u32[]{:S(2)}, u32[]{:S(2)}) %collective-permute-start) | collective-permute-done | bytes 245792 | tf_op jit(solution)/shard_map/ppermute | solution.py:301
  12.6 0.0 copy-start.1
  12.6 0.0 copy-start.2
  12.6 3.5 %all-to-all-start.2 = ((f32[4,5,8,384]{3,2,1,0:T(8,128)}), f32[4,5,8,384]{3,2,1,0:T(8,128)S(1)}, u32[]{:S(2)}, u32[]{:S(2)}) async-start(f32[4,5,8,384]{3,2,1,0:T(8,128)} %bitcast.6), calls=%async_computation.2 | async-start | bytes 491520 | tf_op jit(solution)/shard_map/all_to_all | solution.py:329
  16.1 0.0 copy-done.1
  16.1 0.0 copy-done.2
  16.1 0.0 copy-start.3
  16.2 0.9 copy-done.3
  17.1 0.9 maximum_bitcast_fusion
  18.0 0.0 copy-start.7
  18.0 4.0 %all-to-all-done.2.refs_5_ = f32[4,5,8,384]{3,2,1,0:T(8,128)S(1)} async-done(((f32[4,5,8,384]{3,2,1,0:T(8,128)}), f32[4,5,8,384]{3,2,1,0:T(8,128)S(1)}, u32[]{:S(2)}, u32[]{:S(2)}) %all-to-all-start.2) | async-done | bytes 245792 | tf_op jit(solution)/shard_map/all_to_all | solution.py:329
  21.9 3.5 %all-to-all-start.1 = ((f32[4,14,8,384]{3,2,1,0:T(8,128)}), f32[4,14,8,384]{3,2,1,0:T(8,128)S(1)}, u32[]{:S(2)}, u32[]{:S(2)}) async-start(f32[4,14,8,384]{3,2,1,0:T(8,128)} %maximum_bitcast_fusion), calls=%async_computation.1 | async-start | bytes 1376256 | tf_op jit(solution)/shard_map/all_to_all | solution.py:328
  25.4 0.0 copy-done.7
  25.4 0.3 copy.19
  25.8 1.2 %reshape.9 = bf16[16,5,8,384]{3,2,1,0:T(8,128)(2,1)} reshape(bf16[4,4,5,8,4,96]{5,4,3,2,1,0:T(4,128)(2,1)S(1)} %copy.19) | data formatting | bytes 983040 | tf_op jit(solution)/shard_map/reshape | solution.py:325
  27.0 9.0 %all-to-all-done.1.refs_4_ = f32[4,14,8,384]{3,2,1,0:T(8,128)S(1)} async-done(((f32[4,14,8,384]{3,2,1,0:T(8,128)}), f32[4,14,8,384]{3,2,1,0:T(8,128)S(1)}, u32[]{:S(2)}, u32[]{:S(2)}) %all-to-all-start.1) | async-done | bytes 688160 | tf_op jit(solution)/shard_map/all_to_all | solution.py:328
  36.0 0.0 copy-start.8
  36.0 4.3 %all-to-all-start = ((bf16[16,5,8,384]{3,2,1,0:T(8,128)(2,1)}), bf16[16,5,8,384]{3,2,1,0:T(8,128)(2,1)S(1)}, u32[]{:S(2)}, u32[]{:S(2)}) async-start(bf16[16,5,8,384]{3,2,1,0:T(8,128)(2,1)} %reshape.9), calls=%async_computation | async-start | bytes 983040 | tf_op jit(solution)/shard_map/all_to_all | solution.py:326
  40.9 0.0 copy-done.8
  40.9 19.3 %all_gather.3 = f32[4,5,4]{1,2,0:T(4,128)S(1)} all-gather(f32[1,5,4]{1,2,0:T(4,128)S(1)} %copy-done.8), channel_id=1, replica_groups=mesh['members'=2,'window'=4,'space'=4] {'window'}, dimensions={0}, use_global_device_ids=true | all-gather | bytes 400 | tf_op jit(solution)/shard_map/all_gather | solution.py:330
  60.2 0.1 copy.25.refs_1_.refs_0_
  60.3 0.0 all-to-all-done.refs_3_
  60.3 0.6 copy-done.5
  60.9 9.4 %shard_map.121 = (s16[16,128,128]{2,1,0:T(8,128)(2,1)S(1)}, f32[4,4,8,384]{3,2,1,0:T(8,128)S(1)}) custom-call(f32[5,5]{1,0:T(8,128)S(1)} %copy-done.5, f32[4,5,4]{2,1,0:T(8,128)S(1)} %copy.25.refs_1_.refs_0_, s32[1]{0:T(128)S(6)} %copy.32.refs_2_, bf16[16,5,8,384]{3,2,1,0:T(8,128)(2,1)S(1)} %all-to-all-done.refs_3_, ...), custom_call_target="tpu_custom_call" | custom-call | tf_op jit(solution)/shard_map/pallas_call | solution.py:334
  70.3 7.8 %all_to_all.25.refs_4_ = f32[4,4,8,384]{3,2,1,0:T(8,128)S(1)} all-to-all(f32[4,4,8,384]{3,2,1,0:T(8,128)S(1)} %get-tuple-element.6), channel_id=1, replica_groups=mesh['members'=2,'window'=4,'space'=4] {'space'}, dimensions={0} | all-to-all | bytes 393216 | tf_op jit(solution)/shard_map/all_to_all | solution.py:353
  78.1 17.2 %all_to_all.26.refs_3_ = s16[16,128,128]{2,1,0:T(8,128)(2,1)S(1)} all-to-all(s16[16,128,128]{2,1,0:T(8,128)(2,1)S(1)} %get-tuple-element.5), channel_id=1, replica_groups=mesh['members'=2,'window'=4,'space'=4] {'window','space'}, dimensions={0} | all-to-all | bytes 1048576 | tf_op jit(solution)/shard_map/all_to_all | solution.py:352
  95.3 0.0 copy-done
  95.3 0.0 copy-done.4
  95.3 0.0 copy-done.6
  95.3 2.8 %shard_map.122 = (f32[1,5,4,8,384]{4,3,2,1,0:T(8,128)}, f32[1,4,4,8,384]{4,3,2,1,0:T(8,128)}, f32[1,5,4,8,384]{4,3,2,1,0:T(8,128)}) custom-call(f32[4,5,4]{2,1,0:T(8,128)S(1)} %copy.25.refs_1_.refs_0_, f32[1,4,4]{2,1,0:T(4,128)S(1)} %copy-done.6, s32[1]{0:T(128)S(6)} %copy.32.refs_2_, s16[16,128,128]{2,1,0:T(8,128)(2,1)S(1)} %all_to_all.26.refs_3_, ...), custom_call_target="tpu_custom_call" | custom-call | tf_op jit(solution)/shard_map/pallas_call | solution.py:356
  (6 shorter events, 0.1 us)
Async XLA Ops:
  1.6 11.0 %collective-permute-start = (f32[5,4,8,384]{3,2,0,1:T(8,128)S(1)}, f32[5,4,8,384]{3,2,0,1:T(8,128)}, u32[]{:S(2)}, u32[]{:S(2)}) collective-permute-start(f32[5,4,8,384]{3,2,0,1:T(8,128)S(1)} %bitcast.16), channel_id=1, source_target_pairs={{4,0},{8,4},{12,8},{5,1},{9,5},{13,9},{6,2},{10,6},{14,10},{7,3},{... | collective-permute-start | bytes 737288 | tf_op jit(solution)/shard_map/ppermute | solution.py:301
  12.6 3.5 %copy-start.1 = (f32[1,5,4,8,384]{4,3,2,1,0:T(8,128)S(1)}, f32[1,5,4,8,384]{4,3,2,1,0:T(8,128)}, u32[]{:S(2)}) copy-start(f32[1,5,4,8,384]{4,3,2,1,0:T(8,128)} %refs_7_.1) | copy-start | bytes 737284
  12.6 3.5 %copy-start.2 = (f32[1,5,4,8,384]{4,3,2,1,0:T(8,128)S(1)}, f32[1,5,4,8,384]{4,3,2,1,0:T(8,128)}, u32[]{:S(2)}) copy-start(f32[1,5,4,8,384]{4,3,2,1,0:T(8,128)} %refs_6_.1) | copy-start | bytes 737284
  12.6 9.4 %all-to-all-start.2 = ((f32[4,5,8,384]{3,2,1,0:T(8,128)}), f32[4,5,8,384]{3,2,1,0:T(8,128)S(1)}, u32[]{:S(2)}, u32[]{:S(2)}) async-start(f32[4,5,8,384]{3,2,1,0:T(8,128)} %bitcast.6), calls=%async_computation.2 | async-start | bytes 491520 | tf_op jit(solution)/shard_map/all_to_all | solution.py:329
  16.1 0.9 copy-start.3
  18.0 7.4 %copy-start.7 = (bf16[4,4,5,4,8,96]{5,4,3,2,1,0:T(8,128)(2,1)S(1)}, bf16[4,4,5,4,8,96]{5,4,3,2,1,0:T(8,128)(2,1)}, u32[]{:S(2)}) copy-start(bf16[4,4,5,4,8,96]{5,4,3,2,1,0:T(8,128)(2,1)} %param.10) | copy-start | bytes 1474564
  21.9 14.1 %all-to-all-start.1 = ((f32[4,14,8,384]{3,2,1,0:T(8,128)}), f32[4,14,8,384]{3,2,1,0:T(8,128)S(1)}, u32[]{:S(2)}, u32[]{:S(2)}) async-start(f32[4,14,8,384]{3,2,1,0:T(8,128)} %maximum_bitcast_fusion), calls=%async_computation.1 | async-start | bytes 1376256 | tf_op jit(solution)/shard_map/all_to_all | solution.py:328
  36.0 4.9 %copy-start.8 = (f32[1,5,4]{1,2,0:T(4,128)S(1)}, f32[1,5,4]{1,2,0:T(4,128)}, u32[]{:S(2)}) copy-start(f32[1,5,4]{1,2,0:T(4,128)} %param.17) | copy-start | bytes 244
  36.0 24.3 %all-to-all-start = ((bf16[16,5,8,384]{3,2,1,0:T(8,128)(2,1)}), bf16[16,5,8,384]{3,2,1,0:T(8,128)(2,1)S(1)}, u32[]{:S(2)}, u32[]{:S(2)}) async-start(bf16[16,5,8,384]{3,2,1,0:T(8,128)(2,1)} %reshape.9), calls=%async_computation | async-start | bytes 983040 | tf_op jit(solution)/shard_map/all_to_all | solution.py:326
  60.2 0.7 copy-start.5
  78.1 17.2 %copy-start = (f32[1,5,4,8,384]{4,3,2,1,0:T(8,128)S(1)}, f32[1,5,4,8,384]{4,3,2,1,0:T(8,128)}, u32[]{:S(2)}) copy-start(f32[1,5,4,8,384]{4,3,2,1,0:T(8,128)} %refs_5_.1) | copy-start | bytes 737284
  78.1 17.2 %copy-start.4 = (f32[1,4,4,8,384]{4,3,2,1,0:T(8,128)S(1)}, f32[1,4,4,8,384]{4,3,2,1,0:T(8,128)}, u32[]{:S(2)}) copy-start(f32[1,4,4,8,384]{4,3,2,1,0:T(8,128)} %refs_9_.1) | copy-start | bytes 589828
  78.1 17.2 %copy-start.6 = (f32[1,4,4]{2,1,0:T(4,128)S(1)}, f32[1,4,4]{2,1,0:T(4,128)}, u32[]{:S(2)}) copy-start(f32[1,4,4]{2,1,0:T(4,128)} %refs_1_.1) | copy-start | bytes 196

commit v2 on v0

v2 whole, which is shorter than its diff:
```python
import jax
import jax.numpy as jnp
from jax import lax
from jax.experimental import pallas as pl
from jax.experimental.pallas import tpu as pltpu
from jax.sharding import PartitionSpec as P

LANES = 128
SUB = 8
HALF = SUB // 2
CODE_MAX = 32766.0
ROUNDER = 12582912.0

diffusion = 0.2
advection = 0.2
coupling_gain = 0.5
keep = 1.0 - 4.0 * diffusion
half_adv = 0.5 * advection

VMEM = pl.BlockSpec(memory_space=pltpu.VMEM)
SMEM = pl.BlockSpec(memory_space=pltpu.SMEM)


def params(mib=24):
    return pltpu.CompilerParams(vmem_limit_bytes=mib * 1024 * 1024)


def lane_index():
    return lax.broadcasted_iota(jnp.int32, (SUB, LANES), 1)


def row_index():
    return lax.broadcasted_iota(jnp.int32, (SUB, LANES), 0)


def tiled(wide):
    short = -wide.shape[1] % LANES
    if short:
        wide = jnp.concatenate([wide, jnp.zeros((wide.shape[0], short), wide.dtype)], 1)
    return [wide[:, i : i + LANES] for i in range(0, wide.shape[1], LANES)]


def place(parts, rolled, lane):
    built = {}
    for key, tiles, first, width, target in parts:
        done = 0
        while done < width:
            a, b = first + done, target + done
            n = min(width - done, LANES - a % LANES, LANES - b % LANES)
            shift = (b - a) % LANES
            name = (key, a // LANES, shift)
            if name not in rolled:
                value = tiles[a // LANES]
                rolled[name] = pltpu.roll(value, shift, 1) if shift else value
            if b % LANES:
                built[b // LANES] = jnp.where(
                    lane >= b % LANES, rolled[name], built[b // LANES]
                )
            else:
                built[b // LANES] = rolled[name]
            done += n
    return [built[i] for i in range(len(built))]


def joined_halves(first, second):
    top = row_index()[:, :1] < HALF
    last = jnp.where(top, pltpu.roll(first, HALF, 0), second)
    start = jnp.where(top, first, pltpu.roll(second, HALF, 0))
    return last, start


def widened(own, low, high, odd):
    top = row_index() < HALF
    turned = pltpu.roll(own, HALF, 0)
    low = pltpu.roll(low, HALF, 0) if odd else low
    high = high if odd else pltpu.roll(high, HALF, 0)
    return jnp.where(top, low, turned), jnp.where(top, turned, high)


def row_codes(planes):
    lane = lax.broadcasted_iota(jnp.int32, planes[0][0].shape, 1)
    scales = jnp.zeros(planes[0][0].shape, jnp.float32)
    out = []
    for v, row in enumerate(planes):
        big = jnp.abs(row[0])
        for value in row[1:]:
            big = jnp.maximum(big, jnp.abs(value))
        big = jnp.max(big, axis=1, keepdims=True)
        power = jnp.clip(jnp.ceil(jnp.log2(jnp.maximum(big, 1e-30))), -90.0, 126.0)
        scales = jnp.where(lane == v, power, scales)
        gain = CODE_MAX * jnp.exp2(-power)
        for value in row:
            scaled = jnp.clip(value * gain, -CODE_MAX, CODE_MAX)
            out.append((scaled + ROUNDER) - ROUNDER)
    return out, scales


def shorts(value):
    return value.astype(jnp.int32).astype(jnp.int16)


def floats(value):
    return value.astype(jnp.int32).astype(jnp.float32)


def pack_kernel(windows, steps, nvar, levels, part, var_ref, traj_ref, *out_refs):
    me = lax.axis_index("window")
    lane, row = lane_index(), row_index()
    variance = jnp.zeros((SUB, LANES), jnp.float32)
    for v in range(nvar):
        for lev in range(levels):
            variance = jnp.where(lane == v * levels + lev, var_ref[0, v, lev], variance)
    high = variance.astype(jnp.bfloat16).astype(jnp.float32)
    middle = (variance - high).astype(jnp.bfloat16).astype(jnp.float32)
    low = variance - high - middle
    split = jnp.where(row == 0, high, jnp.where(row == 1, middle, jnp.where(row == 2, low, 0.0)))

    for d in range(windows):
        target = lax.rem(me + d, windows)

        def level(lev, carry, d=d, target=target):
            for v in range(nvar):
                pieces = [
                    tiled(traj_ref[target, j, v, lev].astype(jnp.float32)) for j in range(steps)
                ]
                parts = [(j, pieces[j], 0, part, j * part) for j in range(steps)]
                wide = jnp.concatenate(place(parts, {}, lane), 1)
                out_refs[d][v * levels + lev] = wide.astype(jnp.bfloat16)
            return carry

        lax.fori_loop(0, levels, level, 0)
        out_refs[d][nvar * levels, :, :LANES] = split.astype(jnp.bfloat16)


def field_halo_kernel(inc_ref, dobs_ref, dual_ref, low_ref, high_ref):
    base = 0
    tiles = inc_ref.shape[-1] // LANES
    for ref in (inc_ref, dobs_ref, dual_ref):
        count, pairs = ref.shape[1], ref.shape[2] // 2

        def field(f, carry, ref=ref, base=base, pairs=pairs):
            for i in range(pairs):
                for t in range(tiles):
                    cut = slice(t * LANES, (t + 1) * LANES)
                    last, start = joined_halves(
                        ref[0, f, 2 * i, :, cut], ref[0, f, 2 * i + 1, :, cut]
                    )
                    low_ref[base + f * pairs + i, :, cut] = last
                    high_ref[base + f * pairs + i, :, cut] = start
            return carry

        lax.fori_loop(0, count, field, 0)
        base += count * pairs


def dual_code_kernel(base, dual_ref, low_ref, high_ref, codes_ref):
    nvar, levels = dual_ref.shape[1:3]
    tiles = dual_ref.shape[-1] // LANES
    pairs = levels // 2

    def pair(i, carry):
        for odd in range(2):
            lev = 2 * i + odd
            planes = []
            for v in range(nvar):
                row = []
                for t in range(tiles):
                    cut = slice(t * LANES, (t + 1) * LANES)
                    halves = widened(
                        dual_ref[0, v, lev, :, cut],
                        low_ref[base + v * pairs + i, :, cut],
                        high_ref[base + v * pairs + i, :, cut],
                        odd,
                    )
                    row.append(jnp.concatenate(halves, 0))
                planes.append(row)
            values, scales = row_codes(planes)
            for n, value in enumerate(values + [scales]):
                codes_ref[lev, n] = shorts(value)
        return carry

    lax.fori_loop(0, pairs, pair, 0)


def assemble_kernel(windows, steps, nvar, levels, part, *refs):
    pieces = refs[:windows]
    own_ref, low_ref, high_ref, total_ref, stack_ref = refs[windows:]
    me = lax.axis_index("window")
    lane = lane_index()
    total = jnp.zeros((1, LANES), jnp.float32)
    for d in range(windows):
        source = lax.rem(me - d + windows, windows)
        stack_ref[source] = pieces[d][: nvar * levels]
        split = pieces[d][nvar * levels, :, :LANES].astype(jnp.float32)
        here = jnp.sum(split, axis=0, keepdims=True)
        total = total + jnp.where(source <= me, here, 0.0)
    for p in range(nvar * levels):
        total_ref[p] = jnp.broadcast_to(total[:, p : p + 1], (SUB, LANES))

    pairs = levels // 2

    def pair(n, carry):
        both = []
        for odd in range(2):
            plane = 2 * n + odd
            sources = [tiled(stack_ref[w, plane].astype(jnp.float32)) for w in range(windows)]
            rolled = {}
            built = []
            for j in range(steps):
                parts = [(w, sources[w], j * part, part, w * part) for w in range(windows)]
                built.append(place(parts, rolled, lane))
                own_ref[j, plane] = jnp.concatenate(built[j], 1).astype(jnp.bfloat16)
            both.append(built)
        for j in range(steps):
            halves = [joined_halves(a, b) for a, b in zip(both[0][j], both[1][j])]
            low_ref[j, n] = jnp.concatenate([h[0] for h in halves], 1).astype(jnp.bfloat16)
            high_ref[j, n] = jnp.concatenate([h[1] for h in halves], 1).astype(jnp.bfloat16)
        return carry

    lax.fori_loop(0, nvar * pairs, pair, 0)


def model_kernel(
    windows, spaces, steps, nvar, levels, tiles,
    coupling_ref, count_ref, noise_ref, total_ref, own_ref, low_ref, high_ref, after_ref,
    flow_ref, fhigh_ref, inc_ref, dobs_ref, rhs_ref, dual_ref, innov_ref,
    ndo_ref, ndm_ref, ninc_ref, *rest,
):
    payload_refs = rest[: windows - 1]
    x_ref, s_ref, a_ref, f_ref, keep_ref, q_ref = rest[windows - 1 :]
    me = lax.axis_index("window")
    place_x = lax.axis_index("space")
    lane, row = lane_index(), row_index()
    pairs = levels // 2
    zero = jnp.zeros((SUB, LANES), jnp.float32)
    blocks = [slice(SUB, 2 * SUB), slice(2 * SUB, 3 * SUB)]
    ups = [slice(b.start + 1, b.stop + 1) for b in blocks]
    downs = [slice(b.start - 1, b.stop - 1) for b in blocks]
    mine = slice(SUB + HALF, 2 * SUB + HALF)
    cuts = [slice(t * LANES, (t + 1) * LANES) for t in range(tiles)]
    mix = [[coupling_gain * coupling_ref[v, u] for u in range(nvar)] for v in range(nvar)]
    low_wall = jnp.where((row == HALF) & (place_x == 0), 0.0, 1.0)
    high_wall = jnp.where((row == HALF - 1) & (place_x == spaces - 1), 0.0, 1.0)

    def from_north(line):
        turned = [pltpu.roll(value, LANES - 1, 1) for value in line]
        return [
            jnp.where(lane < LANES - 1, turned[t], turned[(t + 1) % tiles]) for t in range(tiles)
        ]

    def from_south(line):
        turned = [pltpu.roll(value, 1, 1) for value in line]
        return [jnp.where(lane > 0, turned[t], turned[t - 1]) for t in range(tiles)]

    def masked_last(line):
        return line[:-1] + [jnp.where(lane < LANES - 1, line[-1], 0.0)]

    def masked_first(line):
        return [jnp.where(lane > 0, line[0], 0.0)] + line[1:]

    def walled(block, east, west):
        if block == 0:
            return east, [low_wall * value for value in west]
        return [high_wall * value for value in east], west

    def pair(i, outer):
        for odd in range(2):
            lev = 2 * i + odd

            def spread(j, carry, odd=odd, lev=lev):
                for v in range(nvar):
                    for t in range(tiles):
                        halves = widened(
                            own_ref[j, v * levels + lev, :, cuts[t]].astype(jnp.float32),
                            low_ref[j, v * pairs + i, :, cuts[t]].astype(jnp.float32),
                            high_ref[j, v * pairs + i, :, cuts[t]].astype(jnp.float32),
                            odd,
                        )
                        for b in range(2):
                            x_ref[odd, j, v, t, blocks[b], :] = halves[b]
                seen = jnp.where(j < count_ref[0], 1.0, 0.0)
                for t in range(tiles):
                    halves = widened(
                        dobs_ref[0, j, lev, :, cuts[t]],
                        flow_ref[(nvar + j) * pairs + i, :, cuts[t]],
                        fhigh_ref[(nvar + j) * pairs + i, :, cuts[t]],
                        odd,
                    )
                    for b in range(2):
                        f_ref[odd, j, t, b * SUB : (b + 1) * SUB, :] = seen * halves[b]
                return carry

            lax.fori_loop(0, steps, spread, 0)
            scales = jnp.exp2(floats(after_ref[lev, nvar * tiles])) * (1.0 / CODE_MAX)
            for v in range(nvar):
                for t in range(tiles):
                    halves = widened(
                        inc_ref[0, v, lev, :, cuts[t]],
                        flow_ref[v * pairs + i, :, cuts[t]],
                        fhigh_ref[v * pairs + i, :, cuts[t]],
                        odd,
                    )
                    for b in range(2):
                        s_ref[odd, 0, v, t, blocks[b], :] = halves[b]
                    later = floats(after_ref[lev, v * tiles + t]) * scales[:, v : v + 1]
                    a_ref[odd, 0, v, t, SUB : 3 * SUB, :] = -later
                    keep_ref[odd, v, t] = a_ref[odd, 0, v, t, mine, :]

        def tangent(j, carry):
            now = lax.rem(j, 2)
            seen = jnp.where(j < count_ref[0], 1.0, 0.0)
            for odd in range(2):
                lev = 2 * i + odd
                noise = jnp.full((SUB, LANES), noise_ref[0, j, lev])
                share = seen / noise
                for t in range(tiles):
                    gap = innov_ref[0, j, lev, :, cuts[t]] - noise * dobs_ref[0, j, lev, :, cuts[t]]
                    gap = gap - s_ref[odd, now, 0, t, mine, :]
                    ndo_ref[0, j, lev, :, cuts[t]] = gap * share
                for b in range(2):
                    here, up, down = blocks[b], ups[b], downs[b]
                    x = [[x_ref[odd, j, u, t, here, :] for t in range(tiles)] for u in range(nvar)]
                    ce = [diffusion - half_adv * value for value in x[0]]
                    cw = [diffusion + half_adv * value for value in x[0]]
                    ce, cw = walled(b, ce, cw)
                    cn = masked_last([diffusion - half_adv * value for value in x[1]])
                    cs = masked_first([diffusion + half_adv * value for value in x[1]])
                    s = [
                        [s_ref[odd, now, u, t, here, :] for t in range(tiles)] for u in range(nvar)
                    ]
                    xs = [[x[u][t] * s[u][t] for t in range(tiles)] for u in range(nvar)]
                    for v in range(nvar):
                        north, south = from_north(s[v]), from_south(s[v])
                        for t in range(tiles):
                            fresh = keep * s[v][t] + ce[t] * s_ref[odd, now, v, t, up, :]
                            fresh = fresh + cw[t] * s_ref[odd, now, v, t, down, :]
                            fresh = fresh + cn[t] * north[t] + cs[t] * south[t]
                            for u in range(nvar):
                                fresh = fresh + mix[v][u] * xs[u][t]
                            s_ref[odd, 1 - now, v, t, here, :] = fresh
            return carry

        lax.fori_loop(0, steps, tangent, 0)

        def adjoint(turn, carry):
            now = lax.rem(turn, 2)
            j = steps - 1 - turn
            for odd in range(2):
                for b in range(2):
                    here, up, down = blocks[b], ups[b], downs[b]
                    x = [[x_ref[odd, j, u, t, here, :] for t in range(tiles)] for u in range(nvar)]
                    ce = [
                        diffusion + half_adv * x_ref[odd, j, 0, t, up, :] for t in range(tiles)
                    ]
                    cw = [
                        diffusion - half_adv * x_ref[odd, j, 0, t, down, :] for t in range(tiles)
                    ]
                    ce, cw = walled(b, ce, cw)
                    cn = masked_first([diffusion + half_adv * value for value in x[1]])
                    cs = masked_last([diffusion - half_adv * value for value in x[1]])
                    a = [
                        [a_ref[odd, now, u, t, here, :] for t in range(tiles)] for u in range(nvar)
                    ]
                    for u in range(nvar):
                        north = from_north([cn[t] * a[u][t] for t in range(tiles)])
                        south = from_south([cs[t] * a[u][t] for t in range(tiles)])
                        for t in range(tiles):
                            fresh = keep * a[u][t] + ce[t] * a_ref[odd, now, u, t, up, :]
                            fresh = fresh + cw[t] * a_ref[odd, now, u, t, down, :]
                            fresh = fresh + north[t] + south[t]
                            pull = mix[0][u] * a[0][t]
                            for v in range(1, nvar):
                                pull = pull + mix[v][u] * a[v][t]
                            fresh = fresh + x[u][t] * pull
                            if u == 0:
                                fresh = fresh + f_ref[odd, j, t, b * SUB : (b + 1) * SUB, :]
                            a_ref[odd, 1 - now, u, t, here, :] = fresh
            return carry

        lax.fori_loop(0, steps, adjoint, 0)

        end = steps % 2
        coded = []
        for odd in range(2):
            lev = 2 * i + odd
            back, ahead = [], []
            for v in range(nvar):
                share = total_ref[v * levels + lev]
                tv, gv = [], []
                for t in range(tiles):
                    term = a_ref[odd, end, v, t, mine, :] - keep_ref[odd, v, t]
                    given = rhs_ref[0, v, lev, :, cuts[t]] - inc_ref[0, v, lev, :, cuts[t]]
                    given = given + share * term
                    ndm_ref[v, lev, :, cuts[t]] = -(dual_ref[0, v, lev, :, cuts[t]] + term)
                    ninc_ref[v, lev, :, cuts[t]] = given
                    tv.append(term)
                    gv.append(given + s_ref[odd, end, v, t, mine, :])
                back.append(tv)
                ahead.append(gv)
            coded.append((row_codes(back), row_codes(ahead)))
        for kind in range(2):
            first, second = coded[0][kind], coded[1][kind]
            for n, (a, b) in enumerate(zip(first[0] + [first[1]], second[0] + [second[1]])):
                q_ref[kind, i, n] = shorts(jnp.concatenate([a, b], 0))
        return outer

    lax.fori_loop(0, pairs, pair, 0)
    for d in range(1, windows):
        payload_refs[d - 1][...] = q_ref[jnp.where(me + d >= windows, 0, 1)]


def final_kernel(windows, nvar, levels, tiles, *refs):
    pieces = refs[: windows - 1]
    total_ref, base_dual_ref, base_inc_ref, ndm_ref, ninc_ref = refs[windows - 1 :]
    me = lax.axis_index("window")
    pairs = levels // 2
    cuts = [slice(t * LANES, (t + 1) * LANES) for t in range(tiles)]

    def pair(i, carry):
        tails = [None] * (nvar * tiles)
        heads = [None] * (nvar * tiles)
        for d in range(1, windows):
            piece = pieces[d - 1]
            scales = jnp.exp2(floats(piece[i, nvar * tiles])) * (1.0 / CODE_MAX)
            later = jnp.where(d > me, scales, 0.0)
            earlier = jnp.where(d > me, 0.0, scales)
            for v in range(nvar):
                for t in range(tiles):
                    n = v * tiles + t
                    value = floats(piece[i, n])
                    tail, head = value * later[:, v : v + 1], value * earlier[:, v : v + 1]
                    tails[n] = tail if d == 1 else tails[n] + tail
                    heads[n] = head if d == 1 else heads[n] + head
        for v in range(nvar):
            for odd in range(2):
                lev = 2 * i + odd
                share = total_ref[v * levels + lev]
                for t in range(tiles):
                    rows = slice(odd * SUB, (odd + 1) * SUB)
                    tail, head = tails[v * tiles + t][rows], heads[v * tiles + t][rows]
                    ndm_ref[0, v, lev, :, cuts[t]] = base_dual_ref[v, lev, :, cuts[t]] - tail
                    ninc_ref[0, v, lev, :, cuts[t]] = (
                        base_inc_ref[v, lev, :, cuts[t]] + head + share * tail
                    )
        return carry

    lax.fori_loop(0, pairs, pair, 0)


def moved(block, axis, distance, around=False):
    count = lax.axis_size(axis)
    route = [(i, (i + distance) % count) for i in range(count) if around or 0 <= i + distance < count]
    return lax.ppermute(block, axis, route)


def body(
    trajectory,
    dual_model,
    increment,
    model_rhs,
    dual_obs,
    innovation,
    coupling,
    error_var,
    obs_var,
    obs_count,
):
    windows, spaces = lax.axis_size("window"), lax.axis_size("space")
    _, steps, nvar, levels, rows, part = trajectory.shape
    columns = dual_model.shape[-1]
    tiles = columns // LANES
    assert trajectory.shape[0] == windows and windows > 1 and rows == SUB and steps == HALF
    assert columns == tiles * LANES == windows * part and levels % 2 == 0
    pairs = levels // 2
    wide = -(-steps * part // LANES) * LANES
    bf16, f32, i16 = jnp.bfloat16, jnp.float32, jnp.int16

    def shape(dims, dtype):
        return jax.ShapeDtypeStruct(dims, dtype)

    blocks = pl.pallas_call(
        lambda *refs: pack_kernel(windows, steps, nvar, levels, part, *refs),
        out_shape=[shape((nvar * levels + 1, rows, wide), bf16)] * windows,
        in_specs=[SMEM, VMEM],
        out_specs=[VMEM] * windows,
        compiler_params=params(),
    )(error_var, trajectory)
    order = sorted(range(1, windows), key=lambda d: -d * (windows - d))
    arrived = {0: blocks[0]}
    for d in order:
        arrived[d] = moved(blocks[d], "window", d, around=True)

    field_tiles = shape(((2 * nvar + steps) * pairs, rows, columns), f32)
    low, high = pl.pallas_call(
        field_halo_kernel,
        out_shape=[field_tiles, field_tiles],
        in_specs=[VMEM] * 3,
        out_specs=[VMEM] * 2,
        compiler_params=params(),
    )(increment, dual_obs, dual_model)
    low, high = moved(low, "space", 1), moved(high, "space", -1)

    after = pl.pallas_call(
        lambda *refs: dual_code_kernel((nvar + steps) * pairs, *refs),
        out_shape=shape((levels, nvar * tiles + 1, 2 * SUB, LANES), i16),
        in_specs=[VMEM] * 3,
        out_specs=VMEM,
        compiler_params=params(),
    )(dual_model, low, high)
    after = moved(after, "window", -1)

    own, traj_low, traj_high, totals = pl.pallas_call(
        lambda *refs: assemble_kernel(windows, steps, nvar, levels, part, *refs),
        out_shape=[
            shape((steps, nvar * levels, rows, columns), bf16),
            shape((steps, nvar * pairs, rows, columns), bf16),
            shape((steps, nvar * pairs, rows, columns), bf16),
            shape((nvar * levels, rows, LANES), f32),
        ],
        in_specs=[VMEM] * windows,
        out_specs=[VMEM] * 4,
        scratch_shapes=[pltpu.VMEM((windows, nvar * levels, rows, wide), bf16)],
        compiler_params=params(),
    )(*[arrived[d] for d in range(windows)])
    traj_low, traj_high = moved(traj_low, "space", 1), moved(traj_high, "space", -1)

    state = shape((nvar, levels, rows, columns), f32)
    payload = shape((pairs, nvar * tiles + 1, 2 * SUB, LANES), i16)
    new_dual_obs, base_dual, base_inc, *payloads = pl.pallas_call(
        lambda *refs: model_kernel(windows, spaces, steps, nvar, levels, tiles, *refs),
        out_shape=[shape(dual_obs.shape, f32), state, state] + [payload] * (windows - 1),
        in_specs=[SMEM] * 3 + [VMEM] * 12,
        out_specs=[VMEM] * (3 + windows - 1),
        scratch_shapes=[
            pltpu.VMEM((2, steps, nvar, tiles, 4 * SUB, LANES), f32),
            pltpu.VMEM((2, 2, nvar, tiles, 4 * SUB, LANES), f32),
            pltpu.VMEM((2, 2, nvar, tiles, 4 * SUB, LANES), f32),
            pltpu.VMEM((2, steps, tiles, 2 * SUB, LANES), f32),
            pltpu.VMEM((2, nvar, tiles, SUB, LANES), f32),
            pltpu.VMEM((2,) + payload.shape, i16),
        ],
        compiler_params=params(32),
    )(
        coupling, obs_count, obs_var, totals, own, traj_low, traj_high, after,
        low, high, increment, dual_obs, model_rhs, dual_model, innovation,
    )
    sent = {d: moved(payloads[d - 1], "window", d, around=True) for d in order}

    new_dual_model, new_increment = pl.pallas_call(
        lambda *refs: final_kernel(windows, nvar, levels, tiles, *refs),
        out_shape=[shape(dual_model.shape, f32), shape(increment.shape, f32)],
        in_specs=[VMEM] * (windows + 2),
        out_specs=[VMEM] * 2,
        compiler_params=params(),
    )(*[sent[d] for d in range(1, windows)], totals, base_dual, base_inc)
    return new_dual_model, new_dual_obs, new_increment


def solution(mesh):
    placed = (
        P("members", None, None, None, "space", "window"),
        P(("members", "window"), None, None, "space", None),
        P(("members", "window"), None, None, "space", None),
        P(("members", "window"), None, None, "space", None),
        P(("members", "window"), None, None, "space", None),
        P(("members", "window"), None, None, "space", None),
        P(),
        P(("members", "window"), None, None),
        P(("members", "window"), None, None),
        P(("members", "window")),
    )
    return jax.shard_map(
        body,
        mesh=mesh,
        in_specs=placed,
        out_specs=(
            P(("members", "window"), None, None, "space", None),
            P(("members", "window"), None, None, "space", None),
            P(("members", "window"), None, None, "space", None),
        ),
        check_vma=False,
    )
```

time: 113 us -> 56.4 us (0.50)
  the two profiles are of different devices: /device:TPU:0 before, /device:TPU:1 now
where the time goes in v2:
time: 56.4 us; the launch traced here: 56.1 us
  starting transfers between devices  23 us (41%)
  waiting for transfers between devices  17.1 us (30%)
  Pallas kernels  11.6 us (21%)
  local copies, waits for them, and re-layouts  2.94 us (5%)
  between operations  1.44 us (3%)
    ppermute x11, starting transfers between devices, moved(): return lax.ppermute(block, axis, route)  23 us
    ppermute x11, waiting for transfers between devices, moved(): return lax.ppermute(block, axis, route)  17.1 us
    pallas_call x1, Pallas kernels, body(): pl.pallas_call(lambda *refs: model_kernel(windows, spaces, steps, nvar, l...  6.99 us
    unnamed x25, local copies, waits for them, and re-layouts  2.94 us
    pallas_call x1, Pallas kernels, body(): pl.pallas_call(lambda *refs: pack_kernel(windows, steps, nvar, levels, pa...  1.93 us
  transfers between devices with their start and end apart: 11, of which 8 were waited for; matrix products, arithmetic and copies ran while one was open for 0% of the time, Pallas kernels for 6%

profile of v2, /device:TPU:1, one launch (start us, length us, event | category | flops | bytes accessed | tf_op | source)
XLA Modules:
  0.0 56.1 jit_solution(11171173605720151661)
XLA Ops:
  0.6 0.0 copy-start
  0.6 0.9 %copy-done = f32[1,5,4,8,384]{4,3,2,1,0:T(8,128)S(1)} copy-done((f32[1,5,4,8,384]{4,3,2,1,0:T(8,128)S(1)}, f32[1,5,4,8,384]{4,3,2,1,0:T(8,128)}, u32[]{:S(2)}) %copy-start) | copy-done | bytes 245784
  1.6 0.9 %copy-done.2 = f32[1,5,4,8,384]{4,3,2,1,0:T(8,128)S(1)} copy-done((f32[1,5,4,8,384]{4,3,2,1,0:T(8,128)S(1)}, f32[1,5,4,8,384]{4,3,2,1,0:T(8,128)}, u32[]{:S(2)}) %copy-start.2) | copy-done | bytes 245784
  2.5 0.9 %copy-done.4 = f32[1,4,4,8,384]{4,3,2,1,0:T(8,128)S(1)} copy-done((f32[1,4,4,8,384]{4,3,2,1,0:T(8,128)S(1)}, f32[1,4,4,8,384]{4,3,2,1,0:T(8,128)}, u32[]{:S(2)}) %copy-start.4) | copy-done | bytes 196632
  3.5 0.1 shard_map.123
  3.6 0.0 copy-start.11
  3.6 4.6 %collective-permute-start.5 = (f32[28,8,384]{2,1,0:T(8,128)S(1)}, f32[28,8,384]{2,1,0:T(8,128)S(1)}, u32[]{:S(2)}, u32[]{:S(2)}) collective-permute-start(f32[28,8,384]{2,1,0:T(8,128)S(1)} %get-tuple-element.29), channel_id=1, source_target_pairs={{0,1},{1,2},{2,3},{4,5},{5,6},{6,7},{8,9},{9,10},{10,11},{12,13},{... | collective-permute-start | bytes 1032200 | tf_op jit(solution)/shard_map/ppermute | solution.py:453
  8.2 1.9 %collective-permute-start.6 = (f32[28,8,384]{2,1,0:T(8,128)S(1)}, f32[28,8,384]{2,1,0:T(8,128)S(1)}, u32[]{:S(2)}, u32[]{:S(2)}) collective-permute-start(f32[28,8,384]{2,1,0:T(8,128)S(1)} %get-tuple-element.30), channel_id=1, source_target_pairs={{1,0},{2,1},{3,2},{5,4},{6,5},{7,6},{9,8},{10,9},{11,10},{13,12},{... | collective-permute-start | bytes 1032200 | tf_op jit(solution)/shard_map/ppermute | solution.py:453
  10.2 0.1 copy.13.refs_0_
  10.2 1.9 %shard_map.121 = (bf16[21,8,384]{2,1,0:T(8,128)(2,1)S(1)}, bf16[21,8,384]{2,1,0:T(8,128)(2,1)S(1)}, bf16[21,8,384]{2,1,0:T(8,128)(2,1)S(1)}, bf16[21,8,384]{2,1,0:T(8,128)(2,1)S(1)}) custom-call(f32[1,5,4]{2,1,0:T(8,128)S(1)} %copy.13.refs_0_, bf16[4,4,5,4,8,96]{5,4,3,2,1,0:T(8,128)(2,1)S(1)} %copy-done.6), custom_call_target="tpu_custom_call" | custom-call | tf_op jit(solution)/shard_map/pallas_call | solution.py:481
  12.2 1.3 %collective-permute-start = (bf16[21,8,384]{2,1,0:T(8,128)(2,1)S(1)}, bf16[21,8,384]{2,1,0:T(8,128)(2,1)S(1)}, u32[]{:S(2)}, u32[]{:S(2)}) collective-permute-start(bf16[21,8,384]{2,1,0:T(8,128)(2,1)S(1)} %get-tuple-element.22), channel_id=1, source_target_pairs={{0,4},{4,8},{8,12},{12,0},{1,5},{5,9},{9,13},{13,1},{2,6},{6,10},{... | collective-permute-start | bytes 387080 | tf_op jit(solution)/shard_map/ppermute | solution.py:453
  13.5 2.3 %collective-permute-start.1 = (bf16[21,8,384]{2,1,0:T(8,128)(2,1)S(1)}, bf16[21,8,384]{2,1,0:T(8,128)(2,1)S(1)}, u32[]{:S(2)}, u32[]{:S(2)}) collective-permute-start(bf16[21,8,384]{2,1,0:T(8,128)(2,1)S(1)} %get-tuple-element.23), channel_id=1, source_target_pairs={{0,8},{4,12},{8,0},{12,4},{1,9},{5,13},{9,1},{13,5},{2,10},{6,14},... | collective-permute-start | bytes 387080 | tf_op jit(solution)/shard_map/ppermute | solution.py:453
  15.8 1.1 %collective-permute-start.2 = (bf16[21,8,384]{2,1,0:T(8,128)(2,1)S(1)}, bf16[21,8,384]{2,1,0:T(8,128)(2,1)S(1)}, u32[]{:S(2)}, u32[]{:S(2)}) collective-permute-start(bf16[21,8,384]{2,1,0:T(8,128)(2,1)S(1)} %get-tuple-element.24), channel_id=1, source_target_pairs={{0,12},{4,0},{8,4},{12,8},{1,13},{5,1},{9,5},{13,9},{2,14},{6,2},{... | collective-permute-start | bytes 387080 | tf_op jit(solution)/shard_map/ppermute | solution.py:453
  16.9 0.2 collective-permute-done.6.refs_2_.refs_9_
  17.1 0.4 shard_map.124
  17.5 1.3 %collective-permute-start.7 = (s16[4,16,16,128]{3,2,1,0:T(8,128)(2,1)S(1)}, s16[4,16,16,128]{3,2,1,0:T(8,128)(2,1)S(1)}, u32[]{:S(2)}, u32[]{:S(2)}) collective-permute-start(s16[4,16,16,128]{3,2,1,0:T(8,128)(2,1)S(1)} %shard_map.124), channel_id=1, source_target_pairs={{4,0},{8,4},{12,8},{5,1},{9,5},{13,9},{6,2},{10,6},{14,10},{7,3},{... | collective-permute-start | bytes 786440 | tf_op jit(solution)/shard_map/ppermute | solution.py:453
  18.8 0.3 collective-permute-done.refs_1_
  19.1 4.4 %collective-permute-done.1.refs_2_ = bf16[21,8,384]{2,1,0:T(8,128)(2,1)S(1)} collective-permute-done((bf16[21,8,384]{2,1,0:T(8,128)(2,1)S(1)}, bf16[21,8,384]{2,1,0:T(8,128)(2,1)S(1)}, u32[]{:S(2)}, u32[]{:S(2)}) %collective-permute-start.1) | collective-permute-done | bytes 129056 | tf_op jit(solution)/shard_map/ppermute | solution.py:453
  23.5 0.7 %collective-permute-done.2.refs_3_ = bf16[21,8,384]{2,1,0:T(8,128)(2,1)S(1)} collective-permute-done((bf16[21,8,384]{2,1,0:T(8,128)(2,1)S(1)}, bf16[21,8,384]{2,1,0:T(8,128)(2,1)S(1)}, u32[]{:S(2)}, u32[]{:S(2)}) %collective-permute-start.2) | collective-permute-done | bytes 129056 | tf_op jit(solution)/shard_map/ppermute | solution.py:453
  24.2 1.1 %shard_map.122 = (bf16[4,20,8,384]{3,2,1,0:T(8,128)(2,1)S(1)}, bf16[4,10,8,384]{3,2,1,0:T(8,128)(2,1)S(1)}, bf16[4,10,8,384]{3,2,1,0:T(8,128)(2,1)S(1)}, f32[20,8,128]{2,1,0:T(8,128)S(1)}) custom-call(bf16[21,8,384]{2,1,0:T(8,128)(2,1)S(1)} %get-tuple-element.21.refs_0_, bf16[21,8,384]{2,1,0:T(8,128)(2,1)S(1)} %collective-permute-done.refs_1_, ...), custom_call_target="tpu_custom_call" | custom-call | tf_op jit(solution)/shard_map/pallas_call | solution.py:512
  25.3 0.0 copy-start.9
  25.3 4.8 %collective-permute-start.3 = (bf16[4,10,8,384]{3,2,1,0:T(8,128)(2,1)S(1)}, bf16[4,10,8,384]{3,2,1,0:T(8,128)(2,1)S(1)}, u32[]{:S(2)}, u32[]{:S(2)}) collective-permute-start(bf16[4,10,8,384]{3,2,1,0:T(8,128)(2,1)S(1)} %get-tuple-element.27), channel_id=1, source_target_pairs={{0,1},{1,2},{2,3},{4,5},{5,6},{6,7},{8,9},{9,10},{10,11},{12,13},{... | collective-permute-start | bytes 737288 | tf_op jit(solution)/shard_map/ppermute | solution.py:453
  30.1 1.9 %collective-permute-start.4 = (bf16[4,10,8,384]{3,2,1,0:T(8,128)(2,1)S(1)}, bf16[4,10,8,384]{3,2,1,0:T(8,128)(2,1)S(1)}, u32[]{:S(2)}, u32[]{:S(2)}) collective-permute-start(bf16[4,10,8,384]{3,2,1,0:T(8,128)(2,1)S(1)} %get-tuple-element.28), channel_id=1, source_target_pairs={{1,0},{2,1},{3,2},{5,4},{6,5},{7,6},{9,8},{10,9},{11,10},{13,12},{... | collective-permute-start | bytes 737288 | tf_op jit(solution)/shard_map/ppermute | solution.py:453
  32.7 0.5 collective-permute-done.3.refs_5_
  33.2 4.4 %collective-permute-done.4.refs_6_ = bf16[4,10,8,384]{3,2,1,0:T(8,128)(2,1)S(1)} collective-permute-done((bf16[4,10,8,384]{3,2,1,0:T(8,128)(2,1)S(1)}, bf16[4,10,8,384]{3,2,1,0:T(8,128)(2,1)S(1)}, u32[]{:S(2)}, u32[]{:S(2)}) %collective-permute-start.4) | collective-permute-done | bytes 245792 | tf_op jit(solution)/shard_map/ppermute | solution.py:453
  37.7 7.0 %shard_map.125 = (f32[1,4,4,8,384]{4,3,2,1,0:T(8,128)}, f32[5,4,8,384]{3,2,1,0:T(8,128)S(1)}, f32[5,4,8,384]{3,2,1,0:T(8,128)S(1)}, s16[2,16,16,128]{3,2,1,0:T(8...) custom-call(f32[5,5]{1,0:T(8,128)S(1)} %copy-done.9, s32[1]{0:T(128)S(6)} %copy.14.refs_1_, ...), custom_call_target="tpu_custom_call" | custom-call | tf_op jit(solution)/shard_map/pallas_call | solution.py:529
  44.7 1.6 %collective-permute-start.8 = (s16[2,16,16,128]{3,2,1,0:T(8,128)(2,1)S(1)}, s16[2,16,16,128]{3,2,1,0:T(8,128)(2,1)S(1)}, u32[]{:S(2)}, u32[]{:S(2)}) collective-permute-start(s16[2,16,16,128]{3,2,1,0:T(8,128)(2,1)S(1)} %get-tuple-element.31), channel_id=1, source_target_pairs={{0,4},{4,8},{8,12},{12,0},{1,5},{5,9},{9,13},{13,1},{2,6},{6,10},{... | collective-permute-start | bytes 393224 | tf_op jit(solution)/shard_map/ppermute | solution.py:453
  46.3 1.2 %collective-permute-start.9 = (s16[2,16,16,128]{3,2,1,0:T(8,128)(2,1)S(1)}, s16[2,16,16,128]{3,2,1,0:T(8,128)(2,1)S(1)}, u32[]{:S(2)}, u32[]{:S(2)}) collective-permute-start(s16[2,16,16,128]{3,2,1,0:T(8,128)(2,1)S(1)} %get-tuple-element.32), channel_id=1, source_target_pairs={{0,8},{4,12},{8,0},{12,4},{1,9},{5,13},{9,1},{13,5},{2,10},{6,14},... | collective-permute-start | bytes 393224 | tf_op jit(solution)/shard_map/ppermute | solution.py:453
  47.5 0.9 %collective-permute-start.10 = (s16[2,16,16,128]{3,2,1,0:T(8,128)(2,1)S(1)}, s16[2,16,16,128]{3,2,1,0:T(8,128)(2,1)S(1)}, u32[]{:S(2)}, u32[]{:S(2)}) collective-permute-start(s16[2,16,16,128]{3,2,1,0:T(8,128)(2,1)S(1)} %get-tuple-element.33), channel_id=1, source_target_pairs={{0,12},{4,0},{8,4},{12,8},{1,13},{5,1},{9,5},{13,9},{2,14},{6,2},{... | collective-permute-start | bytes 393224 | tf_op jit(solution)/shard_map/ppermute | solution.py:453
  48.4 2.6 %collective-permute-done.8.refs_0_ = s16[2,16,16,128]{3,2,1,0:T(8,128)(2,1)S(1)} collective-permute-done((s16[2,16,16,128]{3,2,1,0:T(8,128)(2,1)S(1)}, s16[2,16,16,128]{3,2,1,0:T(8,128)(2,1)S(1)}, u32[]{:S(2)}, u32[]{:S(2)}) %collective-permute-start.8) | collective-permute-done | bytes 131104 | tf_op jit(solution)/shard_map/ppermute | solution.py:453
  51.0 4.0 %collective-permute-done.9.refs_1_ = s16[2,16,16,128]{3,2,1,0:T(8,128)(2,1)S(1)} collective-permute-done((s16[2,16,16,128]{3,2,1,0:T(8,128)(2,1)S(1)}, s16[2,16,16,128]{3,2,1,0:T(8,128)(2,1)S(1)}, u32[]{:S(2)}, u32[]{:S(2)}) %collective-permute-start.9) | collective-permute-done | bytes 131104 | tf_op jit(solution)/shard_map/ppermute | solution.py:453
  55.0 1.1 %shard_map.126 = (f32[1,5,4,8,384]{4,3,2,1,0:T(8,128)}, f32[1,5,4,8,384]{4,3,2,1,0:T(8,128)}) custom-call(s16[2,16,16,128]{3,2,1,0:T(8,128)(2,1)S(1)} %collective-permute-done.8.refs_0_, s16[2,16,16,128]{3,2,1,0:T(8,128)(2,1)S(1)} %collective-permute-done.9.refs_1_, s16[2,16,16,128]{3,2,1,0:T(8,128)(2,1)S(1)} %collective-permute-done.10.refs_2_, ...), custom_call_target="tpu_custom_call" | custom-call | tf_op jit(solution)/shard_map/pallas_call | solution.py:549
  (21 shorter events, 0.0 us)
Async XLA Ops:
  0.6 0.9 %copy-start = (f32[1,5,4,8,384]{4,3,2,1,0:T(8,128)S(1)}, f32[1,5,4,8,384]{4,3,2,1,0:T(8,128)}, u32[]{:S(2)}) copy-start(f32[1,5,4,8,384]{4,3,2,1,0:T(8,128)} %refs_13_.1) | copy-start | bytes 737284
  1.6 0.9 %copy-start.2 = (f32[1,5,4,8,384]{4,3,2,1,0:T(8,128)S(1)}, f32[1,5,4,8,384]{4,3,2,1,0:T(8,128)}, u32[]{:S(2)}) copy-start(f32[1,5,4,8,384]{4,3,2,1,0:T(8,128)} %refs_10_.1) | copy-start | bytes 737284
  2.5 0.9 %copy-start.4 = (f32[1,4,4,8,384]{4,3,2,1,0:T(8,128)S(1)}, f32[1,4,4,8,384]{4,3,2,1,0:T(8,128)}, u32[]{:S(2)}) copy-start(f32[1,4,4,8,384]{4,3,2,1,0:T(8,128)} %refs_11_.1) | copy-start | bytes 589828
  3.4 6.8 %copy-start.6 = (bf16[4,4,5,4,8,96]{5,4,3,2,1,0:T(8,128)(2,1)S(1)}, bf16[4,4,5,4,8,96]{5,4,3,2,1,0:T(8,128)(2,1)}, u32[]{:S(2)}) copy-start(bf16[4,4,5,4,8,96]{5,4,3,2,1,0:T(8,128)(2,1)} %refs_1_.2) | copy-start | bytes 1474564
  3.6 6.6 %copy-start.11 = (f32[1,5,4]{1,2,0:T(4,128)S(1)}, f32[1,5,4]{1,2,0:T(4,128)}, u32[]{:S(2)}) copy-start(f32[1,5,4]{1,2,0:T(4,128)} %param.17) | copy-start | bytes 244
  3.6 13.3 %collective-permute-start.5 = (f32[28,8,384]{2,1,0:T(8,128)S(1)}, f32[28,8,384]{2,1,0:T(8,128)S(1)}, u32[]{:S(2)}, u32[]{:S(2)}) collective-permute-start(f32[28,8,384]{2,1,0:T(8,128)S(1)} %get-tuple-element.29), channel_id=1, source_target_pairs={{0,1},{1,2},{2,3},{4,5},{5,6},{6,7},{8,9},{9,10},{10,11},{12,13},{... | collective-permute-start | bytes 1032200 | tf_op jit(solution)/shard_map/ppermute | solution.py:453
  8.2 8.9 %collective-permute-start.6 = (f32[28,8,384]{2,1,0:T(8,128)S(1)}, f32[28,8,384]{2,1,0:T(8,128)S(1)}, u32[]{:S(2)}, u32[]{:S(2)}) collective-permute-start(f32[28,8,384]{2,1,0:T(8,128)S(1)} %get-tuple-element.30), channel_id=1, source_target_pairs={{1,0},{2,1},{3,2},{5,4},{6,5},{7,6},{9,8},{10,9},{11,10},{13,12},{... | collective-permute-start | bytes 1032200 | tf_op jit(solution)/shard_map/ppermute | solution.py:453
  10.2 6.8 %copy-start.1 = (f32[1,5,4,8,384]{4,3,2,1,0:T(8,128)S(1)}, f32[1,5,4,8,384]{4,3,2,1,0:T(8,128)}, u32[]{:S(2)}) copy-start(f32[1,5,4,8,384]{4,3,2,1,0:T(8,128)} %refs_13_.1) | copy-start | bytes 737284
  12.2 6.9 %collective-permute-start = (bf16[21,8,384]{2,1,0:T(8,128)(2,1)S(1)}, bf16[21,8,384]{2,1,0:T(8,128)(2,1)S(1)}, u32[]{:S(2)}, u32[]{:S(2)}) collective-permute-start(bf16[21,8,384]{2,1,0:T(8,128)(2,1)S(1)} %get-tuple-element.22), channel_id=1, source_target_pairs={{0,4},{4,8},{8,12},{12,0},{1,5},{5,9},{9,13},{13,1},{2,6},{6,10},{... | collective-permute-start | bytes 387080 | tf_op jit(solution)/shard_map/ppermute | solution.py:453
  13.5 9.9 %collective-permute-start.1 = (bf16[21,8,384]{2,1,0:T(8,128)(2,1)S(1)}, bf16[21,8,384]{2,1,0:T(8,128)(2,1)S(1)}, u32[]{:S(2)}, u32[]{:S(2)}) collective-permute-start(bf16[21,8,384]{2,1,0:T(8,128)(2,1)S(1)} %get-tuple-element.23), channel_id=1, source_target_pairs={{0,8},{4,12},{8,0},{12,4},{1,9},{5,13},{9,1},{13,5},{2,10},{6,14},... | collective-permute-start | bytes 387080 | tf_op jit(solution)/shard_map/ppermute | solution.py:453
  15.8 8.3 %collective-permute-start.2 = (bf16[21,8,384]{2,1,0:T(8,128)(2,1)S(1)}, bf16[21,8,384]{2,1,0:T(8,128)(2,1)S(1)}, u32[]{:S(2)}, u32[]{:S(2)}) collective-permute-start(bf16[21,8,384]{2,1,0:T(8,128)(2,1)S(1)} %get-tuple-element.24), channel_id=1, source_target_pairs={{0,12},{4,0},{8,4},{12,8},{1,13},{5,1},{9,5},{13,9},{2,14},{6,2},{... | collective-permute-start | bytes 387080 | tf_op jit(solution)/shard_map/ppermute | solution.py:453
  17.1 20.6 %copy-start.7 = (f32[1,5,4,8,384]{4,3,2,1,0:T(8,128)S(1)}, f32[1,5,4,8,384]{4,3,2,1,0:T(8,128)}, u32[]{:S(2)}) copy-start(f32[1,5,4,8,384]{4,3,2,1,0:T(8,128)} %refs_12_.1) | copy-start | bytes 737284
  17.1 20.6 %copy-start.8 = (f32[1,4,4,8,384]{4,3,2,1,0:T(8,128)S(1)}, f32[1,4,4,8,384]{4,3,2,1,0:T(8,128)}, u32[]{:S(2)}) copy-start(f32[1,4,4,8,384]{4,3,2,1,0:T(8,128)} %refs_14_.1) | copy-start | bytes 589828
  17.5 20.2 %collective-permute-start.7 = (s16[4,16,16,128]{3,2,1,0:T(8,128)(2,1)S(1)}, s16[4,16,16,128]{3,2,1,0:T(8,128)(2,1)S(1)}, u32[]{:S(2)}, u32[]{:S(2)}) collective-permute-start(s16[4,16,16,128]{3,2,1,0:T(8,128)(2,1)S(1)} %shard_map.124), channel_id=1, source_target_pairs={{4,0},{8,4},{12,8},{5,1},{9,5},{13,9},{6,2},{10,6},{14,10},{7,3},{... | collective-permute-start | bytes 786440 | tf_op jit(solution)/shard_map/ppermute | solution.py:453
  24.1 13.5 %copy-start.3 = (f32[1,5,4,8,384]{4,3,2,1,0:T(8,128)S(1)}, f32[1,5,4,8,384]{4,3,2,1,0:T(8,128)}, u32[]{:S(2)}) copy-start(f32[1,5,4,8,384]{4,3,2,1,0:T(8,128)} %refs_10_.1) | copy-start | bytes 737284
  24.1 13.5 %copy-start.5 = (f32[1,4,4,8,384]{4,3,2,1,0:T(8,128)S(1)}, f32[1,4,4,8,384]{4,3,2,1,0:T(8,128)}, u32[]{:S(2)}) copy-start(f32[1,4,4,8,384]{4,3,2,1,0:T(8,128)} %refs_11_.1) | copy-start | bytes 589828
  25.3 12.4 %copy-start.9 = (f32[5,5]{1,0:T(8,128)S(1)}, f32[5,5]{1,0:T(8,128)}, u32[]{:S(2)}) copy-start(f32[5,5]{1,0:T(8,128)} %refs_0_.4) | copy-start | bytes 304
  25.3 7.9 %collective-permute-start.3 = (bf16[4,10,8,384]{3,2,1,0:T(8,128)(2,1)S(1)}, bf16[4,10,8,384]{3,2,1,0:T(8,128)(2,1)S(1)}, u32[]{:S(2)}, u32[]{:S(2)}) collective-permute-start(bf16[4,10,8,384]{3,2,1,0:T(8,128)(2,1)S(1)} %get-tuple-element.27), channel_id=1, source_target_pairs={{0,1},{1,2},{2,3},{4,5},{5,6},{6,7},{8,9},{9,10},{10,11},{12,13},{... | collective-permute-start | bytes 737288 | tf_op jit(solution)/shard_map/ppermute | solution.py:453
  30.1 7.5 %collective-permute-start.4 = (bf16[4,10,8,384]{3,2,1,0:T(8,128)(2,1)S(1)}, bf16[4,10,8,384]{3,2,1,0:T(8,128)(2,1)S(1)}, u32[]{:S(2)}, u32[]{:S(2)}) collective-permute-start(bf16[4,10,8,384]{3,2,1,0:T(8,128)(2,1)S(1)} %get-tuple-element.28), channel_id=1, source_target_pairs={{1,0},{2,1},{3,2},{5,4},{6,5},{7,6},{9,8},{10,9},{11,10},{13,12},{... | collective-permute-start | bytes 737288 | tf_op jit(solution)/shard_map/ppermute | solution.py:453
  32.7 5.0 %copy-start.10 = (f32[1,4,4]{2,1,0:T(4,128)S(1)}, f32[1,4,4]{2,1,0:T(4,128)}, u32[]{:S(2)}) copy-start(f32[1,4,4]{2,1,0:T(4,128)} %refs_2_.1) | copy-start | bytes 196
  44.7 6.3 %collective-permute-start.8 = (s16[2,16,16,128]{3,2,1,0:T(8,128)(2,1)S(1)}, s16[2,16,16,128]{3,2,1,0:T(8,128)(2,1)S(1)}, u32[]{:S(2)}, u32[]{:S(2)}) collective-permute-start(s16[2,16,16,128]{3,2,1,0:T(8,128)(2,1)S(1)} %get-tuple-element.31), channel_id=1, source_target_pairs={{0,4},{4,8},{8,12},{12,0},{1,5},{5,9},{9,13},{13,1},{2,6},{6,10},{... | collective-permute-start | bytes 393224 | tf_op jit(solution)/shard_map/ppermute | solution.py:453
  46.3 8.7 %collective-permute-start.9 = (s16[2,16,16,128]{3,2,1,0:T(8,128)(2,1)S(1)}, s16[2,16,16,128]{3,2,1,0:T(8,128)(2,1)S(1)}, u32[]{:S(2)}, u32[]{:S(2)}) collective-permute-start(s16[2,16,16,128]{3,2,1,0:T(8,128)(2,1)S(1)} %get-tuple-element.32), channel_id=1, source_target_pairs={{0,8},{4,12},{8,0},{12,4},{1,9},{5,13},{9,1},{13,5},{2,10},{6,14},... | collective-permute-start | bytes 393224 | tf_op jit(solution)/shard_map/ppermute | solution.py:453
  47.5 7.4 %collective-permute-start.10 = (s16[2,16,16,128]{3,2,1,0:T(8,128)(2,1)S(1)}, s16[2,16,16,128]{3,2,1,0:T(8,128)(2,1)S(1)}, u32[]{:S(2)}, u32[]{:S(2)}) collective-permute-start(s16[2,16,16,128]{3,2,1,0:T(8,128)(2,1)S(1)} %get-tuple-element.33), channel_id=1, source_target_pairs={{0,12},{4,0},{8,4},{12,8},{1,13},{5,1},{9,5},{13,9},{2,14},{6,2},{... | collective-permute-start | bytes 393224 | tf_op jit(solution)/shard_map/ppermute | solution.py:453

commit v3 on v2

--- a/solution.py
+++ b/solution.py
@@ -19,6 +19,7 @@
 
 VMEM = pl.BlockSpec(memory_space=pltpu.VMEM)
 SMEM = pl.BlockSpec(memory_space=pltpu.SMEM)
+ANY = pl.BlockSpec(memory_space=pl.ANY)
 
 
 def params(mib=24):
@@ -69,8 +70,9 @@
     return last, start
 
 
-def widened(own, low, high, odd):
+def widened(own, near, far, odd, even):
     top = row_index() < HALF
+    low, high = jnp.where(even, far, near), jnp.where(even, near, far)
     turned = pltpu.roll(own, HALF, 0)
     low = pltpu.roll(low, HALF, 0) if odd else low
     high = high if odd else pltpu.roll(high, HALF, 0)
@@ -103,7 +105,7 @@
     return value.astype(jnp.int32).astype(jnp.float32)
 
 
-def pack_kernel(windows, steps, nvar, levels, part, var_ref, traj_ref, *out_refs):
+def pack_kernel(distances, windows, steps, nvar, levels, part, var_ref, traj_ref, *outs):
     me = lax.axis_index("window")
     lane, row = lane_index(), row_index()
     variance = jnp.zeros((SUB, LANES), jnp.float32)
@@ -114,78 +116,79 @@
     middle = (variance - high).astype(jnp.bfloat16).astype(jnp.float32)
     low = variance - high - middle
     split = jnp.where(row == 0, high, jnp.where(row == 1, middle, jnp.where(row == 2, low, 0.0)))
-
-    for d in range(windows):
+    split = split.astype(jnp.bfloat16)
+
+    for n, d in enumerate(distances):
+        outs[n][nvar * levels, :, :LANES] = split
         target = lax.rem(me + d, windows)
 
-        def level(lev, carry, d=d, target=target):
-            for v in range(nvar):
+        def variable(v, carry, n=n, target=target):
+            for lev in range(levels):
                 pieces = [
                     tiled(traj_ref[target, j, v, lev].astype(jnp.float32)) for j in range(steps)
                 ]
                 parts = [(j, pieces[j], 0, part, j * part) for j in range(steps)]
                 wide = jnp.concatenate(place(parts, {}, lane), 1)
-                out_refs[d][v * levels + lev] = wide.astype(jnp.bfloat16)
+                outs[n][v * levels + lev] = wide.astype(jnp.bfloat16)
             return carry
 
-        lax.fori_loop(0, levels, level, 0)
-        out_refs[d][nvar * levels, :, :LANES] = split.astype(jnp.bfloat16)
-
-
-def field_halo_kernel(inc_ref, dobs_ref, dual_ref, low_ref, high_ref):
-    base = 0
-    tiles = inc_ref.shape[-1] // LANES
-    for ref in (inc_ref, dobs_ref, dual_ref):
-        count, pairs = ref.shape[1], ref.shape[2] // 2
-
-        def field(f, carry, ref=ref, base=base, pairs=pairs):
-            for i in range(pairs):
-                for t in range(tiles):
-                    cut = slice(t * LANES, (t + 1) * LANES)
-                    last, start = joined_halves(
-                        ref[0, f, 2 * i, :, cut], ref[0, f, 2 * i + 1, :, cut]
-                    )
-                    low_ref[base + f * pairs + i, :, cut] = last
-                    high_ref[base + f * pairs + i, :, cut] = start
-            return carry
-
-        lax.fori_loop(0, count, field, 0)
-        base += count * pairs
-
-
-def dual_code_kernel(base, dual_ref, low_ref, high_ref, codes_ref):
-    nvar, levels = dual_ref.shape[1:3]
-    tiles = dual_ref.shape[-1] // LANES
-    pairs = levels // 2
+        lax.fori_loop(0, nvar, variable, 0, unroll=len(distances) == 1)
+
+
+def even_place():
+    return lax.rem(lax.axis_index("space"), 2) == 0
+
+
+def code_kernel(count, own_codes, *refs):
+    sources, near_ref, far_ref = refs[:count], refs[count + 1], refs[count + 2]
+    even = even_place()
 
     def pair(i, carry):
-        for odd in range(2):
-            lev = 2 * i + odd
-            planes = []
-            for v in range(nvar):
-                row = []
-                for t in range(tiles):
-                    cut = slice(t * LANES, (t + 1) * LANES)
-                    halves = widened(
-                        dual_ref[0, v, lev, :, cut],
-                        low_ref[base + v * pairs + i, :, cut],
-                        high_ref[base + v * pairs + i, :, cut],
-                        odd,
-                    )
-                    row.append(jnp.concatenate(halves, 0))
-                planes.append(row)
-            values, scales = row_codes(planes)
-            for n, value in enumerate(values + [scales]):
-                codes_ref[lev, n] = shorts(value)
+        near, far = [], []
+        for ref in sources:
+            coded = []
+            for odd in range(2):
+                planes = [
+                    [ref[0, v, 2 * i + odd, :, t : t + LANES] for t in range(0, ref.shape[-1], LANES)]
+                    for v in range(ref.shape[1])
+                ]
+                values, scales = row_codes(planes)
+                coded.append(values + [scales])
+            if own_codes:
+                for n, (first, second) in enumerate(zip(*coded)):
+                    refs[count + 3][i, n] = shorts(jnp.concatenate([first, second], 0))
+            for first, second in zip(*coded):
+                last, start = joined_halves(first, second)
+                near.append(jnp.where(even, last, start))
+                far.append(jnp.where(even, start, last))
+            if len(near) % 2:
+                near.append(jnp.zeros((SUB, LANES), jnp.float32))
+                far.append(jnp.zeros((SUB, LANES), jnp.float32))
+        for tiles, ref in ((near, near_ref), (far, far_ref)):
+            for n in range(0, len(tiles), 2):
+                ref[i, n // 2] = shorts(jnp.concatenate(tiles[n : n + 2], 0))
         return carry
 
-    lax.fori_loop(0, pairs, pair, 0)
+    lax.fori_loop(0, near_ref.shape[0], pair, 0)
+
+
+def decoded(ref, i, first, nvar, tiles):
+    def tile(n):
+        whole = floats(ref[i, n // 2])
+        return whole[SUB:] if n % 2 else whole[:SUB]
+
+    scales = jnp.exp2(tile(first + nvar * tiles)) * (1.0 / CODE_MAX)
+    return [
+        [tile(first + v * tiles + t) * scales[:, v : v + 1] for t in range(tiles)]
+        for v in range(nvar)
+    ]
 
 
 def assemble_kernel(windows, steps, nvar, levels, part, *refs):
     pieces = refs[:windows]
-    own_ref, low_ref, high_ref, total_ref, stack_ref = refs[windows:]
+    own_ref, far_ref, total_ref, stack_ref = refs[windows:]
     me = lax.axis_index("window")
+    even = even_place()
     lane = lane_index()
     total = jnp.zeros((1, LANES), jnp.float32)
     for d in range(windows):
@@ -213,23 +216,81 @@
             both.append(built)
         for j in range(steps):
             halves = [joined_halves(a, b) for a, b in zip(both[0][j], both[1][j])]
-            low_ref[j, n] = jnp.concatenate([h[0] for h in halves], 1).astype(jnp.bfloat16)
-            high_ref[j, n] = jnp.concatenate([h[1] for h in halves], 1).astype(jnp.bfloat16)
+            last, start = (jnp.concatenate([h[k] for h in halves], 1) for k in range(2))
+            far_ref[j, n] = jnp.where(even, start, last).astype(jnp.bfloat16)
         return carry
 
     lax.fori_loop(0, nvar * pairs, pair, 0)
+
+
+def near_kernel(own_ref, order_ref, near_ref):
+    even = even_place()
+
+    def pair(n, carry):
+        for j in range(own_ref.shape[0]):
+            for t in range(0, own_ref.shape[-1], LANES):
+                cut = slice(t, t + LANES)
+                first, second = (
+                    own_ref[j, 2 * n + odd, :, cut].astype(jnp.float32) for odd in range(2)
+                )
+                last, start = joined_halves(first, second)
+                near_ref[j, n, :, cut] = jnp.where(even, last, start).astype(jnp.bfloat16)
+        return carry
+
+    lax.fori_loop(0, near_ref.shape[1], pair, 0)
+
+
+def prepare_kernel(
+    steps, nvar, levels, tiles,
+    count_ref, after_ref, anear_ref, afar_ref, fnear_ref, ffar_ref, inc_ref, dobs_ref,
+    first_ref, last_ref, force_ref,
+):
+    even = even_place()
+    blocks = [slice(0, SUB), slice(SUB, 2 * SUB)]
+    cuts = [slice(t * LANES, (t + 1) * LANES) for t in range(tiles)]
+
+    def pair(i, carry):
+        offset = -(-(nvar * tiles + 1) // 2) * 2
+        fields = [decoded(ref, i, 0, nvar, tiles) for ref in (fnear_ref, ffar_ref)]
+        forces = [decoded(ref, i, offset, steps, tiles) for ref in (fnear_ref, ffar_ref)]
+        afters = [decoded(ref, i, 0, nvar, tiles) for ref in (anear_ref, afar_ref)]
+        scales = jnp.exp2(floats(after_ref[i, nvar * tiles])) * (1.0 / CODE_MAX)
+        for odd in range(2):
+            lev = 2 * i + odd
+            rows = blocks[odd]
+            for t in range(tiles):
+                for v in range(nvar):
+                    near, far = (side[v][t] for side in fields)
+                    halves = widened(inc_ref[0, v, lev, :, cuts[t]], near, far, odd, even)
+                    for b in range(2):
+                        first_ref[lev, v, t, blocks[b], :] = halves[b]
+                    near, far = (side[v][t] for side in afters)
+                    own = floats(after_ref[i, v * tiles + t])[rows] * scales[rows, v : v + 1]
+                    halves = widened(own, near, far, odd, even)
+                    for b in range(2):
+                        last_ref[lev, v, t, blocks[b], :] = -halves[b]
+                for j in range(steps):
+                    seen = jnp.where(j < count_ref[0], 1.0, 0.0)
+                    near, far = (side[j][t] for side in forces)
+                    halves = widened(dobs_ref[0, j, lev, :, cuts[t]], near, far, odd, even)
+                    for b in range(2):
+                        force_ref[lev, j, t, blocks[b], :] = seen * halves[b]
+        return carry
+
+    lax.fori_loop(0, levels // 2, pair, 0)
 
 
 def model_kernel(
     windows, spaces, steps, nvar, levels, tiles,
-    coupling_ref, count_ref, noise_ref, total_ref, own_ref, low_ref, high_ref, after_ref,
-    flow_ref, fhigh_ref, inc_ref, dobs_ref, rhs_ref, dual_ref, innov_ref,
+    coupling_ref, count_ref, noise_ref, total_ref, own_ref, near_ref, far_ref,
+    first_ref, last_ref, force_ref, inc_ref, dobs_ref, rhs_ref, dual_ref, innov_ref,
     ndo_ref, ndm_ref, ninc_ref, *rest,
 ):
     payload_refs = rest[: windows - 1]
-    x_ref, s_ref, a_ref, f_ref, keep_ref, q_ref = rest[windows - 1 :]
+    x_ref, s_ref, a_ref, q_ref = rest[windows - 1 :]
     me = lax.axis_index("window")
     place_x = lax.axis_index("space")
+    even = even_place()
     lane, row = lane_index(), row_index()
     pairs = levels // 2
     zero = jnp.zeros((SUB, LANES), jnp.float32)
@@ -272,39 +333,21 @@
                     for t in range(tiles):
                         halves = widened(
                             own_ref[j, v * levels + lev, :, cuts[t]].astype(jnp.float32),
-                            low_ref[j, v * pairs + i, :, cuts[t]].astype(jnp.float32),
-                            high_ref[j, v * pairs + i, :, cuts[t]].astype(jnp.float32),
+                            near_ref[j, v * pairs + i, :, cuts[t]].astype(jnp.float32),
+                            far_ref[j, v * pairs + i, :, cuts[t]].astype(jnp.float32),
                             odd,
+                            even,
                         )
                         for b in range(2):
                             x_ref[odd, j, v, t, blocks[b], :] = halves[b]
-                seen = jnp.where(j < count_ref[0], 1.0, 0.0)
-                for t in range(tiles):
-                    halves = widened(
-                        dobs_ref[0, j, lev, :, cuts[t]],
-                        flow_ref[(nvar + j) * pairs + i, :, cuts[t]],
-                        fhigh_ref[(nvar + j) * pairs + i, :, cuts[t]],
-                        odd,
-                    )
-                    for b in range(2):
-                        f_ref[odd, j, t, b * SUB : (b + 1) * SUB, :] = seen * halves[b]
                 return carry
 
             lax.fori_loop(0, steps, spread, 0)
-            scales = jnp.exp2(floats(after_ref[lev, nvar * tiles])) * (1.0 / CODE_MAX)
+
             for v in range(nvar):
                 for t in range(tiles):
-                    halves = widened(
-                        inc_ref[0, v, lev, :, cuts[t]],
-                        flow_ref[v * pairs + i, :, cuts[t]],
-                        fhigh_ref[v * pairs + i, :, cuts[t]],
-                        odd,
-                    )
-                    for b in range(2):
-                        s_ref[odd, 0, v, t, blocks[b], :] = halves[b]
-                    later = floats(after_ref[lev, v * tiles + t]) * scales[:, v : v + 1]
-                    a_ref[odd, 0, v, t, SUB : 3 * SUB, :] = -later
-                    keep_ref[odd, v, t] = a_ref[odd, 0, v, t, mine, :]
+                    s_ref[odd, 0, v, t, SUB : 3 * SUB, :] = first_ref[lev, v, t]
+                    a_ref[odd, 0, v, t, SUB : 3 * SUB, :] = last_ref[lev, v, t]
 
         def tangent(j, carry):
             now = lax.rem(j, 2)
@@ -373,7 +416,7 @@
                                 pull = pull + mix[v][u] * a[v][t]
                             fresh = fresh + x[u][t] * pull
                             if u == 0:
-                                fresh = fresh + f_ref[odd, j, t, b * SUB : (b + 1) * SUB, :]
+                                fresh = fresh + force_ref[2 * i + odd, j, t, b * SUB : (b + 1) * SUB, :]
                             a_ref[odd, 1 - now, u, t, here, :] = fresh
             return carry
 
@@ -388,7 +431,7 @@
                 share = total_ref[v * levels + lev]
                 tv, gv = [], []
                 for t in range(tiles):
-                    term = a_ref[odd, end, v, t, mine, :] - keep_ref[odd, v, t]
+                    term = a_ref[odd, end, v, t, mine, :] - last_ref[lev, v, t, HALF : HALF + SUB, :]
                     given = rhs_ref[0, v, lev, :, cuts[t]] - inc_ref[0, v, lev, :, cuts[t]]
                     given = given + share * term
                     ndm_ref[v, lev, :, cuts[t]] = -(dual_ref[0, v, lev, :, cuts[t]] + term)
@@ -453,6 +496,27 @@
     return lax.ppermute(block, axis, route)
 
 
+def swaps(axis, first):
+    route = []
+    for i in range(first, lax.axis_size(axis) - 1, 2):
+        route += [(i, i + 1), (i + 1, i)]
+    return route
+
+
+def swapped(block, axis, first):
+    return lax.ppermute(block, axis, swaps(axis, first))
+
+
+def swapped_back(block, first):
+    windows, spaces = lax.axis_size("window"), lax.axis_size("space")
+    route = [
+        ((w + 1) * spaces + source, w * spaces + target)
+        for w in range(windows - 1)
+        for source, target in swaps("space", first)
+    ]
+    return lax.ppermute(block, ("window", "space"), route)
+
+
 def body(
     trajectory,
     dual_model,
@@ -478,54 +542,80 @@
     def shape(dims, dtype):
         return jax.ShapeDtypeStruct(dims, dtype)
 
-    blocks = pl.pallas_call(
-        lambda *refs: pack_kernel(windows, steps, nvar, levels, part, *refs),
-        out_shape=[shape((nvar * levels + 1, rows, wide), bf16)] * windows,
-        in_specs=[SMEM, VMEM],
-        out_specs=[VMEM] * windows,
-        compiler_params=params(),
-    )(error_var, trajectory)
+    light = pl.CostEstimate(flops=0, bytes_accessed=0, transcendentals=0)
+
+    def packed(distances):
+        return pl.pallas_call(
+            lambda *refs: pack_kernel(distances, windows, steps, nvar, levels, part, *refs),
+            out_shape=[shape((nvar * levels + 1, rows, wide), bf16)] * len(distances),
+            in_specs=[SMEM, VMEM],
+            out_specs=[VMEM] * len(distances),
+            compiler_params=params(),
+            cost_estimate=light,
+        )(error_var, trajectory)
+
     order = sorted(range(1, windows), key=lambda d: -d * (windows - d))
-    arrived = {0: blocks[0]}
-    for d in order:
-        arrived[d] = moved(blocks[d], "window", d, around=True)
-
-    field_tiles = shape(((2 * nvar + steps) * pairs, rows, columns), f32)
-    low, high = pl.pallas_call(
-        field_halo_kernel,
-        out_shape=[field_tiles, field_tiles],
-        in_specs=[VMEM] * 3,
-        out_specs=[VMEM] * 2,
-        compiler_params=params(),
-    )(increment, dual_obs, dual_model)
-    low, high = moved(low, "space", 1), moved(high, "space", -1)
-
-    after = pl.pallas_call(
-        lambda *refs: dual_code_kernel((nvar + steps) * pairs, *refs),
-        out_shape=shape((levels, nvar * tiles + 1, 2 * SUB, LANES), i16),
-        in_specs=[VMEM] * 3,
-        out_specs=VMEM,
-        compiler_params=params(),
-    )(dual_model, low, high)
+    groups = [[d] for d in order] if windows <= 4 else [order]
+    blocks = {}
+    for group in groups:
+        blocks.update(zip(group, packed(group)))
+    arrived = {d: moved(blocks[d], "window", d, around=True) for d in order}
+    arrived[0] = packed([0])[0]
+
+    payload = shape((pairs, nvar * tiles + 1, 2 * SUB, LANES), i16)
+
+    def half_tiles(*counts):
+        total = sum(-(-(count * tiles + 1) // 2) for count in counts)
+        return shape((pairs, total, 2 * SUB, LANES), i16)
+
+    def coded(fields, own_codes):
+        halves = half_tiles(*[field.shape[1] for field in fields])
+        return pl.pallas_call(
+            lambda *refs: code_kernel(len(fields), own_codes, *refs),
+            out_shape=[halves, halves] + [payload] * own_codes,
+            in_specs=[VMEM] * len(fields) + [ANY],
+            out_specs=[VMEM] * (2 + own_codes),
+            compiler_params=params(),
+            cost_estimate=light,
+        )(*fields, arrived[0])
+
+    after_near, after_far, after = coded([dual_model], 1)
     after = moved(after, "window", -1)
-
-    own, traj_low, traj_high, totals = pl.pallas_call(
+    after_near, after_far = swapped_back(after_near, 0), swapped_back(after_far, 1)
+    near, far = coded([increment, dual_obs], 0)
+    far, near = swapped(far, "space", 1), swapped(near, "space", 0)
+
+    own, traj_far, totals = pl.pallas_call(
         lambda *refs: assemble_kernel(windows, steps, nvar, levels, part, *refs),
         out_shape=[
             shape((steps, nvar * levels, rows, columns), bf16),
             shape((steps, nvar * pairs, rows, columns), bf16),
-            shape((steps, nvar * pairs, rows, columns), bf16),
             shape((nvar * levels, rows, LANES), f32),
         ],
         in_specs=[VMEM] * windows,
-        out_specs=[VMEM] * 4,
+        out_specs=[VMEM] * 3,
         scratch_shapes=[pltpu.VMEM((windows, nvar * levels, rows, wide), bf16)],
         compiler_params=params(),
     )(*[arrived[d] for d in range(windows)])
-    traj_low, traj_high = moved(traj_low, "space", 1), moved(traj_high, "space", -1)
+    traj_far = swapped(traj_far, "space", 1)
 
     state = shape((nvar, levels, rows, columns), f32)
-    payload = shape((pairs, nvar * tiles + 1, 2 * SUB, LANES), i16)
+    around = [shape((levels, n, tiles, 2 * SUB, LANES), f32) for n in (nvar, nvar, steps)]
+    first, last, force = pl.pallas_call(
+        lambda *refs: prepare_kernel(steps, nvar, levels, tiles, *refs),
+        out_shape=around,
+        in_specs=[SMEM] + [VMEM] * 7,
+        out_specs=[VMEM] * 3,
+        compiler_params=params(),
+    )(obs_count, after, after_near, after_far, near, far, increment, dual_obs)
+    traj_near = pl.pallas_call(
+        near_kernel,
+        out_shape=shape((steps, nvar * pairs, rows, columns), bf16),
+        in_specs=[VMEM, ANY],
+        out_specs=VMEM,
+        compiler_params=params(),
+    )(own, force)
+    traj_near = swapped(traj_near, "space", 0)
     new_dual_obs, base_dual, base_inc, *payloads = pl.pallas_call(
         lambda *refs: model_kernel(windows, spaces, steps, nvar, levels, tiles, *refs),
         out_shape=[shape(dual_obs.shape, f32), state, state] + [payload] * (windows - 1),
@@ -535,14 +625,12 @@
             pltpu.VMEM((2, steps, nvar, tiles, 4 * SUB, LANES), f32),
             pltpu.VMEM((2, 2, nvar, tiles, 4 * SUB, LANES), f32),
             pltpu.VMEM((2, 2, nvar, tiles, 4 * SUB, LANES), f32),
-            pltpu.VMEM((2, steps, tiles, 2 * SUB, LANES), f32),
-            pltpu.VMEM((2, nvar, tiles, SUB, LANES), f32),
             pltpu.VMEM((2,) + payload.shape, i16),
         ],
         compiler_params=params(32),
     )(
-        coupling, obs_count, obs_var, totals, own, traj_low, traj_high, after,
-        low, high, increment, dual_obs, model_rhs, dual_model, innovation,
+        coupling, obs_count, obs_var, totals, own, traj_near, traj_far,
+        first, last, force, increment, dual_obs, model_rhs, dual_model, innovation,
     )
     sent = {d: moved(payloads[d - 1], "window", d, around=True) for d in order}
 

time: 56.4 us -> 53.3 us (0.945)
  the two profiles are of different devices: /device:TPU:1 before, /device:TPU:0 now
where the time goes in v3:
time: 53.3 us; the launch traced here: 52.7 us
  starting transfers between devices  20.5 us (38%)
  waiting for transfers between devices  15.7 us (29%)
  Pallas kernels  13.1 us (25%)
  local copies, waits for them, and re-layouts  1.9 us (4%)
  between operations  1.51 us (3%)
    ppermute x7, starting transfers between devices, moved(): return lax.ppermute(block, axis, route)  15.7 us
    ppermute x7, waiting for transfers between devices, moved(): return lax.ppermute(block, axis, route)  11.1 us
    pallas_call x1, Pallas kernels, body(): pl.pallas_call(lambda *refs: model_kernel(windows, spaces, steps, nvar, l...  6.67 us
    ppermute x2, waiting for transfers between devices, swapped_back(): return lax.ppermute(block, ('window', 'space'), route)  3.49 us
    pallas_call x4, Pallas kernels, packed(): pl.pallas_call(lambda *refs: pack_kernel(distances, windows, steps, nvar,...  2.87 us
    ppermute x4, starting transfers between devices, swapped(): return lax.ppermute(block, axis, swaps(axis, first))  2.79 us
    ppermute x2, starting transfers between devices, swapped_back(): return lax.ppermute(block, ('window', 'space'), route)  1.95 us
    unnamed x17, local copies, waits for them, and re-layouts  1.9 us
  transfers between devices with their start and end apart: 13, of which 6 were waited for; matrix products, arithmetic and copies ran while one was open for 0% of the time, Pallas kernels for 9%

profile of v3, /device:TPU:0, one launch (start us, length us, event | category | flops | bytes accessed | tf_op | source)
XLA Modules:
  0.0 52.7 jit_solution(11227570528152622374)
XLA Ops:
  0.6 0.8 %copy.13.refs_0_ = f32[1,5,4]{2,1,0:T(8,128)S(1)} copy(f32[1,5,4]{1,2,0:T(4,128)} %param.17) | data formatting | bytes 160 | tf_op args[7]
  1.4 1.1 %copy-done = bf16[4,4,5,4,8,96]{5,4,3,2,1,0:T(8,128)(2,1)S(1)} copy-done((bf16[4,4,5,4,8,96]{5,4,3,2,1,0:T(8,128)(2,1)S(1)}, bf16[4,4,5,4,8,96]{5,4,3,2,1,0:T(8,128)(2,1)}, u32[]{:S(2)}) %copy-start) | copy-done | bytes 491544
  2.5 0.7 %shard_map.122 = bf16[21,8,384]{2,1,0:T(8,128)(2,1)S(1)} custom-call(f32[1,5,4]{2,1,0:T(8,128)S(1)} %copy.13.refs_0_, bf16[4,4,5,4,8,96]{5,4,3,2,1,0:T(8,128)(2,1)S(1)} %copy-done), custom_call_target="tpu_custom_call" | custom-call | tf_op jit(solution)/shard_map/pallas_call | solution.py:548
  3.2 3.1 %collective-permute-start = (bf16[21,8,384]{2,1,0:T(8,128)(2,1)S(1)}, bf16[21,8,384]{2,1,0:T(8,128)(2,1)S(1)}, u32[]{:S(2)}, u32[]{:S(2)}) collective-permute-start(bf16[21,8,384]{2,1,0:T(8,128)(2,1)S(1)} %shard_map.122), channel_id=1, source_target_pairs={{0,4},{4,8},{8,12},{12,0},{1,5},{5,9},{9,13},{13,1},{2,6},{6,10},{... | collective-permute-start | bytes 387080 | tf_op jit(solution)/shard_map/ppermute | solution.py:496
  6.3 0.7 %shard_map.123 = bf16[21,8,384]{2,1,0:T(8,128)(2,1)S(1)} custom-call(f32[1,5,4]{2,1,0:T(8,128)S(1)} %copy.13.refs_0_, bf16[4,4,5,4,8,96]{5,4,3,2,1,0:T(8,128)(2,1)S(1)} %copy-done), custom_call_target="tpu_custom_call" | custom-call | tf_op jit(solution)/shard_map/pallas_call | solution.py:548
  7.0 2.7 %collective-permute-start.1 = (bf16[21,8,384]{2,1,0:T(8,128)(2,1)S(1)}, bf16[21,8,384]{2,1,0:T(8,128)(2,1)S(1)}, u32[]{:S(2)}, u32[]{:S(2)}) collective-permute-start(bf16[21,8,384]{2,1,0:T(8,128)(2,1)S(1)} %shard_map.123), channel_id=1, source_target_pairs={{0,8},{4,12},{8,0},{12,4},{1,9},{5,13},{9,1},{13,5},{2,10},{6,14},... | collective-permute-start | bytes 387080 | tf_op jit(solution)/shard_map/ppermute | solution.py:496
  9.7 0.7 %shard_map.124 = bf16[21,8,384]{2,1,0:T(8,128)(2,1)S(1)} custom-call(f32[1,5,4]{2,1,0:T(8,128)S(1)} %copy.13.refs_0_, bf16[4,4,5,4,8,96]{5,4,3,2,1,0:T(8,128)(2,1)S(1)} %copy-done), custom_call_target="tpu_custom_call" | custom-call | tf_op jit(solution)/shard_map/pallas_call | solution.py:548
  10.4 1.4 %collective-permute-start.2 = (bf16[21,8,384]{2,1,0:T(8,128)(2,1)S(1)}, bf16[21,8,384]{2,1,0:T(8,128)(2,1)S(1)}, u32[]{:S(2)}, u32[]{:S(2)}) collective-permute-start(bf16[21,8,384]{2,1,0:T(8,128)(2,1)S(1)} %shard_map.124), channel_id=1, source_target_pairs={{0,12},{4,0},{8,4},{12,8},{1,13},{5,1},{9,5},{13,9},{2,14},{6,2},{... | collective-permute-start | bytes 387080 | tf_op jit(solution)/shard_map/ppermute | solution.py:496
  11.8 0.7 %shard_map.121.refs_0_.refs_1_.refs_2_ = bf16[21,8,384]{2,1,0:T(8,128)(2,1)S(1)} custom-call(f32[1,5,4]{2,1,0:T(8,128)S(1)} %copy.13.refs_0_, bf16[4,4,5,4,8,96]{5,4,3,2,1,0:T(8,128)(2,1)S(1)} %copy-done), custom_call_target="tpu_custom_call" | custom-call | tf_op jit(solution)/shard_map/pallas_call | solution.py:548
  12.5 0.3 shard_map.126
  12.9 1.3 %collective-permute-start.3 = (s16[2,16,16,128]{3,2,1,0:T(8,128)(2,1)S(1)}, s16[2,16,16,128]{3,2,1,0:T(8,128)(2,1)S(1)}, u32[]{:S(2)}, u32[]{:S(2)}) collective-permute-start(s16[2,16,16,128]{3,2,1,0:T(8,128)(2,1)S(1)} %get-tuple-element.24), channel_id=1, source_target_pairs={{4,0},{8,4},{12,8},{5,1},{9,5},{13,9},{6,2},{10,6},{14,10},{7,3},{... | collective-permute-start | bytes 393224 | tf_op jit(solution)/shard_map/ppermute | solution.py:496
  14.2 0.4 shard_map.127
  14.6 0.1 collective-permute-start.6
  14.7 0.7 %collective-permute-start.7 = (s16[2,15,16,128]{3,2,1,0:T(8,128)(2,1)S(1)}, s16[2,15,16,128]{3,2,1,0:T(8,128)(2,1)S(1)}, u32[]{:S(2)}, u32[]{:S(2)}) collective-permute-start(s16[2,15,16,128]{3,2,1,0:T(8,128)(2,1)S(1)} %get-tuple-element.28), channel_id=1, source_target_pairs={{1,2},{2,1},{5,6},{6,5},{9,10},{10,9},{13,14},{14,13},{17,18},{18,... | collective-permute-start | bytes 368648 | tf_op jit(solution)/shard_map/ppermute | solution.py:507
  15.3 2.1 %collective-permute-done.1.refs_2_ = bf16[21,8,384]{2,1,0:T(8,128)(2,1)S(1)} collective-permute-done((bf16[21,8,384]{2,1,0:T(8,128)(2,1)S(1)}, bf16[21,8,384]{2,1,0:T(8,128)(2,1)S(1)}, u32[]{:S(2)}, u32[]{:S(2)}) %collective-permute-start.1) | collective-permute-done | bytes 129056 | tf_op jit(solution)/shard_map/ppermute | solution.py:496
  17.4 1.3 %collective-permute-start.4 = (s16[2,8,16,128]{3,2,1,0:T(8,128)(2,1)S(1)}, s16[2,8,16,128]{3,2,1,0:T(8,128)(2,1)S(1)}, u32[]{:S(2)}, u32[]{:S(2)}) collective-permute-start(s16[2,8,16,128]{3,2,1,0:T(8,128)(2,1)S(1)} %get-tuple-element.25), channel_id=1, source_target_pairs={{4,1},{5,0},{6,3},{7,2},{8,5},{9,4},{10,7},{11,6},{12,9},{13,8},{1... | collective-permute-start | bytes 196616 | tf_op jit(solution)/shard_map/ppermute | solution.py:517
  18.7 0.7 %collective-permute-start.5 = (s16[2,8,16,128]{3,2,1,0:T(8,128)(2,1)S(1)}, s16[2,8,16,128]{3,2,1,0:T(8,128)(2,1)S(1)}, u32[]{:S(2)}, u32[]{:S(2)}) collective-permute-start(s16[2,8,16,128]{3,2,1,0:T(8,128)(2,1)S(1)} %get-tuple-element.26), channel_id=1, source_target_pairs={{5,2},{6,1},{9,6},{10,5},{13,10},{14,9},{21,18},{22,17},{25,22},{2... | collective-permute-start | bytes 196616 | tf_op jit(solution)/shard_map/ppermute | solution.py:517
  20.0 1.1 %shard_map.125 = (bf16[4,20,8,384]{3,2,1,0:T(8,128)(2,1)S(1)}, bf16[4,10,8,384]{3,2,1,0:T(8,128)(2,1)S(1)}, f32[20,8,128]{2,1,0:T(8,128)S(1)}) custom-call(bf16[21,8,384]{2,1,0:T(8,128)(2,1)S(1)} %shard_map.121.refs_0_.refs_1_.refs_2_, bf16[21,8,384]{2,1,0:T(8,128)(2,1)S(1)} %collective-permute-done.refs_1_, ...), custom_call_target="tpu_custom_call" | custom-call | tf_op jit(solution)/shard_map/pallas_call | solution.py:588
  21.2 3.5 %collective-permute-done.4.refs_2_ = s16[2,8,16,128]{3,2,1,0:T(8,128)(2,1)S(1)} collective-permute-done((s16[2,8,16,128]{3,2,1,0:T(8,128)(2,1)S(1)}, s16[2,8,16,128]{3,2,1,0:T(8,128)(2,1)S(1)}, u32[]{:S(2)}, u32[]{:S(2)}) %collective-permute-start.4) | collective-permute-done | bytes 65568 | tf_op jit(solution)/shard_map/ppermute | solution.py:517
  24.7 0.7 %collective-permute-start.9 = (bf16[4,10,8,384]{3,2,1,0:T(8,128)(2,1)S(1)}, bf16[4,10,8,384]{3,2,1,0:T(8,128)(2,1)S(1)}, u32[]{:S(2)}, u32[]{:S(2)}) collective-permute-start(bf16[4,10,8,384]{3,2,1,0:T(8,128)(2,1)S(1)} %get-tuple-element.30), channel_id=1, source_target_pairs={{1,2},{2,1},{5,6},{6,5},{9,10},{10,9},{13,14},{14,13},{17,18},{18,... | collective-permute-start | bytes 737288 | tf_op jit(solution)/shard_map/ppermute | solution.py:507
  25.4 0.4 shard_map.128
  25.8 0.2 shard_map.129
  26.0 1.4 %collective-permute-start.8 = (bf16[4,10,8,384]{3,2,1,0:T(8,128)(2,1)S(1)}, bf16[4,10,8,384]{3,2,1,0:T(8,128)(2,1)S(1)}, u32[]{:S(2)}, u32[]{:S(2)}) collective-permute-start(bf16[4,10,8,384]{3,2,1,0:T(8,128)(2,1)S(1)} %shard_map.129), channel_id=1, source_target_pairs={{0,1},{1,0},{2,3},{3,2},{4,5},{5,4},{6,7},{7,6},{8,9},{9,8},{10,11... | collective-permute-start | bytes 737288 | tf_op jit(solution)/shard_map/ppermute | solution.py:507
  27.4 1.1 %collective-permute-done.8.refs_5_ = bf16[4,10,8,384]{3,2,1,0:T(8,128)(2,1)S(1)} collective-permute-done((bf16[4,10,8,384]{3,2,1,0:T(8,128)(2,1)S(1)}, bf16[4,10,8,384]{3,2,1,0:T(8,128)(2,1)S(1)}, u32[]{:S(2)}, u32[]{:S(2)}) %collective-permute-start.8) | collective-permute-done | bytes 245792 | tf_op jit(solution)/shard_map/ppermute | solution.py:507
  28.6 6.7 %shard_map.130 = (f32[1,4,4,8,384]{4,3,2,1,0:T(8,128)}, f32[5,4,8,384]{3,2,1,0:T(8,128)S(1)}, f32[5,4,8,384]{3,2,1,0:T(8,128)S(1)}, s16[2,16,16,128]{3,2,1,0:T(8...) custom-call(f32[5,5]{1,0:T(8,128)S(1)} %copy-done.6, ...), custom_call_target="tpu_custom_call" | custom-call | tf_op jit(solution)/shard_map/pallas_call | solution.py:619
  35.2 2.8 %collective-permute-start.10 = (s16[2,16,16,128]{3,2,1,0:T(8,128)(2,1)S(1)}, s16[2,16,16,128]{3,2,1,0:T(8,128)(2,1)S(1)}, u32[]{:S(2)}, u32[]{:S(2)}) collective-permute-start(s16[2,16,16,128]{3,2,1,0:T(8,128)(2,1)S(1)} %get-tuple-element.33), channel_id=1, source_target_pairs={{0,4},{4,8},{8,12},{12,0},{1,5},{5,9},{9,13},{13,1},{2,6},{6,10},{... | collective-permute-start | bytes 393224 | tf_op jit(solution)/shard_map/ppermute | solution.py:496
  38.0 3.9 %collective-permute-start.11 = (s16[2,16,16,128]{3,2,1,0:T(8,128)(2,1)S(1)}, s16[2,16,16,128]{3,2,1,0:T(8,128)(2,1)S(1)}, u32[]{:S(2)}, u32[]{:S(2)}) collective-permute-start(s16[2,16,16,128]{3,2,1,0:T(8,128)(2,1)S(1)} %get-tuple-element.34), channel_id=1, source_target_pairs={{0,8},{4,12},{8,0},{12,4},{1,9},{5,13},{9,1},{13,5},{2,10},{6,14},... | collective-permute-start | bytes 393224 | tf_op jit(solution)/shard_map/ppermute | solution.py:496
  41.9 0.7 %collective-permute-start.12 = (s16[2,16,16,128]{3,2,1,0:T(8,128)(2,1)S(1)}, s16[2,16,16,128]{3,2,1,0:T(8,128)(2,1)S(1)}, u32[]{:S(2)}, u32[]{:S(2)}) collective-permute-start(s16[2,16,16,128]{3,2,1,0:T(8,128)(2,1)S(1)} %get-tuple-element.35), channel_id=1, source_target_pairs={{0,12},{4,0},{8,4},{12,8},{1,13},{5,1},{9,5},{13,9},{2,14},{6,2},{... | collective-permute-start | bytes 393224 | tf_op jit(solution)/shard_map/ppermute | solution.py:496
  42.5 1.8 %collective-permute-done.10.refs_0_ = s16[2,16,16,128]{3,2,1,0:T(8,128)(2,1)S(1)} collective-permute-done((s16[2,16,16,128]{3,2,1,0:T(8,128)(2,1)S(1)}, s16[2,16,16,128]{3,2,1,0:T(8,128)(2,1)S(1)}, u32[]{:S(2)}, u32[]{:S(2)}) %collective-permute-start.10) | collective-permute-done | bytes 131104 | tf_op jit(solution)/shard_map/ppermute | solution.py:496
  44.4 6.9 %collective-permute-done.11.refs_1_ = s16[2,16,16,128]{3,2,1,0:T(8,128)(2,1)S(1)} collective-permute-done((s16[2,16,16,128]{3,2,1,0:T(8,128)(2,1)S(1)}, s16[2,16,16,128]{3,2,1,0:T(8,128)(2,1)S(1)}, u32[]{:S(2)}, u32[]{:S(2)}) %collective-permute-start.11) | collective-permute-done | bytes 131104 | tf_op jit(solution)/shard_map/ppermute | solution.py:496
  51.3 0.3 collective-permute-done.12.refs_2_
  51.5 1.1 %shard_map.131 = (f32[1,5,4,8,384]{4,3,2,1,0:T(8,128)}, f32[1,5,4,8,384]{4,3,2,1,0:T(8,128)}) custom-call(s16[2,16,16,128]{3,2,1,0:T(8,128)(2,1)S(1)} %collective-permute-done.10.refs_0_, s16[2,16,16,128]{3,2,1,0:T(8,128)(2,1)S(1)} %collective-permute-done.11.refs_1_, s16[2,16,16,128]{3,2,1,0:T(8,128)(2,1)S(1)} %collective-permute-done.12.refs_2_, ...), custom_call_target="tpu_custom_call" | custom-call | tf_op jit(solution)/shard_map/pallas_call | solution.py:637
  (22 shorter events, 0.1 us)
Async XLA Ops:
  1.4 1.1 %copy-start = (bf16[4,4,5,4,8,96]{5,4,3,2,1,0:T(8,128)(2,1)S(1)}, bf16[4,4,5,4,8,96]{5,4,3,2,1,0:T(8,128)(2,1)}, u32[]{:S(2)}) copy-start(bf16[4,4,5,4,8,96]{5,4,3,2,1,0:T(8,128)(2,1)} %refs_1_.9) | copy-start | bytes 1474564
  3.2 11.5 %collective-permute-start = (bf16[21,8,384]{2,1,0:T(8,128)(2,1)S(1)}, bf16[21,8,384]{2,1,0:T(8,128)(2,1)S(1)}, u32[]{:S(2)}, u32[]{:S(2)}) collective-permute-start(bf16[21,8,384]{2,1,0:T(8,128)(2,1)S(1)} %shard_map.122), channel_id=1, source_target_pairs={{0,4},{4,8},{8,12},{12,0},{1,5},{5,9},{9,13},{13,1},{2,6},{6,10},{... | collective-permute-start | bytes 387080 | tf_op jit(solution)/shard_map/ppermute | solution.py:496
  7.0 10.4 %collective-permute-start.1 = (bf16[21,8,384]{2,1,0:T(8,128)(2,1)S(1)}, bf16[21,8,384]{2,1,0:T(8,128)(2,1)S(1)}, u32[]{:S(2)}, u32[]{:S(2)}) collective-permute-start(bf16[21,8,384]{2,1,0:T(8,128)(2,1)S(1)} %shard_map.123), channel_id=1, source_target_pairs={{0,8},{4,12},{8,0},{12,4},{1,9},{5,13},{9,1},{13,5},{2,10},{6,14},... | collective-permute-start | bytes 387080 | tf_op jit(solution)/shard_map/ppermute | solution.py:496
  10.4 2.1 %copy-start.3 = (f32[1,5,4,8,384]{4,3,2,1,0:T(8,128)S(1)}, f32[1,5,4,8,384]{4,3,2,1,0:T(8,128)}, u32[]{:S(2)}) copy-start(f32[1,5,4,8,384]{4,3,2,1,0:T(8,128)} %refs_13_.1) | copy-start | bytes 737284
  10.4 8.3 %collective-permute-start.2 = (bf16[21,8,384]{2,1,0:T(8,128)(2,1)S(1)}, bf16[21,8,384]{2,1,0:T(8,128)(2,1)S(1)}, u32[]{:S(2)}, u32[]{:S(2)}) collective-permute-start(bf16[21,8,384]{2,1,0:T(8,128)(2,1)S(1)} %shard_map.124), channel_id=1, source_target_pairs={{0,12},{4,0},{8,4},{12,8},{1,13},{5,1},{9,5},{13,9},{2,14},{6,2},{... | collective-permute-start | bytes 387080 | tf_op jit(solution)/shard_map/ppermute | solution.py:496
  11.8 2.4 %copy-start.2 = (f32[1,4,4,8,384]{4,3,2,1,0:T(8,128)S(1)}, f32[1,4,4,8,384]{4,3,2,1,0:T(8,128)}, u32[]{:S(2)}) copy-start(f32[1,4,4,8,384]{4,3,2,1,0:T(8,128)} %refs_11_.1) | copy-start | bytes 589828
  12.5 1.7 %copy-start.1 = (f32[1,5,4,8,384]{4,3,2,1,0:T(8,128)S(1)}, f32[1,5,4,8,384]{4,3,2,1,0:T(8,128)}, u32[]{:S(2)}) copy-start(f32[1,5,4,8,384]{4,3,2,1,0:T(8,128)} %refs_10_.1) | copy-start | bytes 737284
  12.9 12.5 %collective-permute-start.3 = (s16[2,16,16,128]{3,2,1,0:T(8,128)(2,1)S(1)}, s16[2,16,16,128]{3,2,1,0:T(8,128)(2,1)S(1)}, u32[]{:S(2)}, u32[]{:S(2)}) collective-permute-start(s16[2,16,16,128]{3,2,1,0:T(8,128)(2,1)S(1)} %get-tuple-element.24), channel_id=1, source_target_pairs={{4,0},{8,4},{12,8},{5,1},{9,5},{13,9},{6,2},{10,6},{14,10},{7,3},{... | collective-permute-start | bytes 393224 | tf_op jit(solution)/shard_map/ppermute | solution.py:496
  14.6 10.8 %collective-permute-start.6 = (s16[2,15,16,128]{3,2,1,0:T(8,128)(2,1)S(1)}, s16[2,15,16,128]{3,2,1,0:T(8,128)(2,1)S(1)}, u32[]{:S(2)}, u32[]{:S(2)}) collective-permute-start(s16[2,15,16,128]{3,2,1,0:T(8,128)(2,1)S(1)} %get-tuple-element.27), channel_id=1, source_target_pairs={{0,1},{1,0},{2,3},{3,2},{4,5},{5,4},{6,7},{7,6},{8,9},{9,8},{10,11... | collective-permute-start | bytes 368648 | tf_op jit(solution)/shard_map/ppermute | solution.py:507
  14.7 10.7 %collective-permute-start.7 = (s16[2,15,16,128]{3,2,1,0:T(8,128)(2,1)S(1)}, s16[2,15,16,128]{3,2,1,0:T(8,128)(2,1)S(1)}, u32[]{:S(2)}, u32[]{:S(2)}) collective-permute-start(s16[2,15,16,128]{3,2,1,0:T(8,128)(2,1)S(1)} %get-tuple-element.28), channel_id=1, source_target_pairs={{1,2},{2,1},{5,6},{6,5},{9,10},{10,9},{13,14},{14,13},{17,18},{18,... | collective-permute-start | bytes 368648 | tf_op jit(solution)/shard_map/ppermute | solution.py:507
  17.4 7.2 %collective-permute-start.4 = (s16[2,8,16,128]{3,2,1,0:T(8,128)(2,1)S(1)}, s16[2,8,16,128]{3,2,1,0:T(8,128)(2,1)S(1)}, u32[]{:S(2)}, u32[]{:S(2)}) collective-permute-start(s16[2,8,16,128]{3,2,1,0:T(8,128)(2,1)S(1)} %get-tuple-element.25), channel_id=1, source_target_pairs={{4,1},{5,0},{6,3},{7,2},{8,5},{9,4},{10,7},{11,6},{12,9},{13,8},{1... | collective-permute-start | bytes 196616 | tf_op jit(solution)/shard_map/ppermute | solution.py:517
  18.7 6.6 %collective-permute-start.5 = (s16[2,8,16,128]{3,2,1,0:T(8,128)(2,1)S(1)}, s16[2,8,16,128]{3,2,1,0:T(8,128)(2,1)S(1)}, u32[]{:S(2)}, u32[]{:S(2)}) collective-permute-start(s16[2,8,16,128]{3,2,1,0:T(8,128)(2,1)S(1)} %get-tuple-element.26), channel_id=1, source_target_pairs={{5,2},{6,1},{9,6},{10,5},{13,10},{14,9},{21,18},{22,17},{25,22},{2... | collective-permute-start | bytes 196616 | tf_op jit(solution)/shard_map/ppermute | solution.py:517
  24.7 2.7 %collective-permute-start.9 = (bf16[4,10,8,384]{3,2,1,0:T(8,128)(2,1)S(1)}, bf16[4,10,8,384]{3,2,1,0:T(8,128)(2,1)S(1)}, u32[]{:S(2)}, u32[]{:S(2)}) collective-permute-start(bf16[4,10,8,384]{3,2,1,0:T(8,128)(2,1)S(1)} %get-tuple-element.30), channel_id=1, source_target_pairs={{1,2},{2,1},{5,6},{6,5},{9,10},{10,9},{13,14},{14,13},{17,18},{18,... | collective-permute-start | bytes 737288 | tf_op jit(solution)/shard_map/ppermute | solution.py:507
  25.8 2.8 %copy-start.4 = (f32[1,5,4,8,384]{4,3,2,1,0:T(8,128)S(1)}, f32[1,5,4,8,384]{4,3,2,1,0:T(8,128)}, u32[]{:S(2)}) copy-start(f32[1,5,4,8,384]{4,3,2,1,0:T(8,128)} %refs_12_.1) | copy-start | bytes 737284
  25.8 2.8 %copy-start.5 = (f32[1,4,4,8,384]{4,3,2,1,0:T(8,128)S(1)}, f32[1,4,4,8,384]{4,3,2,1,0:T(8,128)}, u32[]{:S(2)}) copy-start(f32[1,4,4,8,384]{4,3,2,1,0:T(8,128)} %refs_14_.1) | copy-start | bytes 589828
  25.8 2.8 %copy-start.7 = (f32[1,4,4]{2,1,0:T(4,128)S(1)}, f32[1,4,4]{2,1,0:T(4,128)}, u32[]{:S(2)}) copy-start(f32[1,4,4]{2,1,0:T(4,128)} %refs_2_.1) | copy-start | bytes 196
  26.0 2.5 %copy-start.6 = (f32[5,5]{1,0:T(8,128)S(1)}, f32[5,5]{1,0:T(8,128)}, u32[]{:S(2)}) copy-start(f32[5,5]{1,0:T(8,128)} %refs_0_.10) | copy-start | bytes 304
  26.0 2.5 %collective-permute-start.8 = (bf16[4,10,8,384]{3,2,1,0:T(8,128)(2,1)S(1)}, bf16[4,10,8,384]{3,2,1,0:T(8,128)(2,1)S(1)}, u32[]{:S(2)}, u32[]{:S(2)}) collective-permute-start(bf16[4,10,8,384]{3,2,1,0:T(8,128)(2,1)S(1)} %shard_map.129), channel_id=1, source_target_pairs={{0,1},{1,0},{2,3},{3,2},{4,5},{5,4},{6,7},{7,6},{8,9},{9,8},{10,11... | collective-permute-start | bytes 737288 | tf_op jit(solution)/shard_map/ppermute | solution.py:507
  35.2 9.2 %collective-permute-start.10 = (s16[2,16,16,128]{3,2,1,0:T(8,128)(2,1)S(1)}, s16[2,16,16,128]{3,2,1,0:T(8,128)(2,1)S(1)}, u32[]{:S(2)}, u32[]{:S(2)}) collective-permute-start(s16[2,16,16,128]{3,2,1,0:T(8,128)(2,1)S(1)} %get-tuple-element.33), channel_id=1, source_target_pairs={{0,4},{4,8},{8,12},{12,0},{1,5},{5,9},{9,13},{13,1},{2,6},{6,10},{... | collective-permute-start | bytes 393224 | tf_op jit(solution)/shard_map/ppermute | solution.py:496
  38.0 13.3 %collective-permute-start.11 = (s16[2,16,16,128]{3,2,1,0:T(8,128)(2,1)S(1)}, s16[2,16,16,128]{3,2,1,0:T(8,128)(2,1)S(1)}, u32[]{:S(2)}, u32[]{:S(2)}) collective-permute-start(s16[2,16,16,128]{3,2,1,0:T(8,128)(2,1)S(1)} %get-tuple-element.34), channel_id=1, source_target_pairs={{0,8},{4,12},{8,0},{12,4},{1,9},{5,13},{9,1},{13,5},{2,10},{6,14},... | collective-permute-start | bytes 393224 | tf_op jit(solution)/shard_map/ppermute | solution.py:496
  41.9 9.7 %collective-permute-start.12 = (s16[2,16,16,128]{3,2,1,0:T(8,128)(2,1)S(1)}, s16[2,16,16,128]{3,2,1,0:T(8,128)(2,1)S(1)}, u32[]{:S(2)}, u32[]{:S(2)}) collective-permute-start(s16[2,16,16,128]{3,2,1,0:T(8,128)(2,1)S(1)} %get-tuple-element.35), channel_id=1, source_target_pairs={{0,12},{4,0},{8,4},{12,8},{1,13},{5,1},{9,5},{13,9},{2,14},{6,2},{... | collective-permute-start | bytes 393224 | tf_op jit(solution)/shard_map/ppermute | solution.py:496

commit v4 on v3

--- a/solution.py
+++ b/solution.py
@@ -105,17 +105,17 @@
     return value.astype(jnp.int32).astype(jnp.float32)
 
 
-def pack_kernel(distances, windows, steps, nvar, levels, part, var_ref, traj_ref, *outs):
+def pack_kernel(distances, windows, steps, nvar, levels, part, var_ref, traj_ref, *rest):
+    outs, wide_ref = rest[:-1], rest[-1]
     me = lax.axis_index("window")
-    lane, row = lane_index(), row_index()
-    variance = jnp.zeros((SUB, LANES), jnp.float32)
-    for v in range(nvar):
-        for lev in range(levels):
-            variance = jnp.where(lane == v * levels + lev, var_ref[0, v, lev], variance)
+    lane = lane_index()
+    wide_ref[...] = jnp.zeros((SUB, LANES), jnp.float32)
+    wide_ref[:levels, :nvar] = var_ref[0]
+    variance = wide_ref[...]
     high = variance.astype(jnp.bfloat16).astype(jnp.float32)
     middle = (variance - high).astype(jnp.bfloat16).astype(jnp.float32)
     low = variance - high - middle
-    split = jnp.where(row == 0, high, jnp.where(row == 1, middle, jnp.where(row == 2, low, 0.0)))
+    split = high + pltpu.roll(middle, HALF, 0) + pltpu.roll(low, LANES // 2, 1)
     split = split.astype(jnp.bfloat16)
 
     for n, d in enumerate(distances):
@@ -139,24 +139,39 @@
     return lax.rem(lax.axis_index("space"), 2) == 0
 
 
-def code_kernel(count, own_codes, *refs):
-    sources, near_ref, far_ref = refs[:count], refs[count + 1], refs[count + 2]
+def level_codes(ref, lev):
+    planes = [
+        [ref[0, v, lev, :, t : t + LANES] for t in range(0, ref.shape[-1], LANES)]
+        for v in range(ref.shape[1])
+    ]
+    values, scales = row_codes(planes)
+    return values + [scales]
+
+
+def own_code_kernel(field_ref, out_ref):
+    def pair(i, carry):
+        coded = [level_codes(field_ref, 2 * i + odd) for odd in range(2)]
+        for n, (first, second) in enumerate(zip(*coded)):
+            out_ref[i, n] = shorts(jnp.concatenate([first, second], 0))
+        return carry
+
+    lax.fori_loop(0, out_ref.shape[0], pair, 0)
+
+
+def half_code_kernel(*refs):
+    sources, (near_ref, far_ref) = refs[:-2], refs[-2:]
     even = even_place()
 
     def pair(i, carry):
+        groups = []
+        for ref in sources:
+            if ref.dtype == jnp.int16:
+                whole = [floats(ref[i, n]) for n in range(ref.shape[1])]
+                groups.append([[tile[:SUB] for tile in whole], [tile[SUB:] for tile in whole]])
+            else:
+                groups.append([level_codes(ref, 2 * i + odd) for odd in range(2)])
         near, far = [], []
-        for ref in sources:
-            coded = []
-            for odd in range(2):
-                planes = [
-                    [ref[0, v, 2 * i + odd, :, t : t + LANES] for t in range(0, ref.shape[-1], LANES)]
-                    for v in range(ref.shape[1])
-                ]
-                values, scales = row_codes(planes)
-                coded.append(values + [scales])
-            if own_codes:
-                for n, (first, second) in enumerate(zip(*coded)):
-                    refs[count + 3][i, n] = shorts(jnp.concatenate([first, second], 0))
+        for coded in groups:
             for first, second in zip(*coded):
                 last, start = joined_halves(first, second)
                 near.append(jnp.where(even, last, start))
@@ -172,14 +187,15 @@
     lax.fori_loop(0, near_ref.shape[0], pair, 0)
 
 
+def half_tile(ref, i, n):
+    whole = floats(ref[i, n // 2])
+    return whole[SUB:] if n % 2 else whole[:SUB]
+
+
 def decoded(ref, i, first, nvar, tiles):
-    def tile(n):
-        whole = floats(ref[i, n // 2])
-        return whole[SUB:] if n % 2 else whole[:SUB]
-
-    scales = jnp.exp2(tile(first + nvar * tiles)) * (1.0 / CODE_MAX)
+    scales = jnp.exp2(half_tile(ref, i, first + nvar * tiles)) * (1.0 / CODE_MAX)
     return [
-        [tile(first + v * tiles + t) * scales[:, v : v + 1] for t in range(tiles)]
+        [half_tile(ref, i, first + v * tiles + t) * scales[:, v : v + 1] for t in range(tiles)]
         for v in range(nvar)
     ]
 
@@ -190,15 +206,17 @@
     me = lax.axis_index("window")
     even = even_place()
     lane = lane_index()
-    total = jnp.zeros((1, LANES), jnp.float32)
+    total = jnp.zeros((SUB, LANES), jnp.float32)
     for d in range(windows):
         source = lax.rem(me - d + windows, windows)
         stack_ref[source] = pieces[d][: nvar * levels]
         split = pieces[d][nvar * levels, :, :LANES].astype(jnp.float32)
-        here = jnp.sum(split, axis=0, keepdims=True)
+        here = split + pltpu.roll(split, HALF, 0) + pltpu.roll(split, LANES // 2, 1)
         total = total + jnp.where(source <= me, here, 0.0)
-    for p in range(nvar * levels):
-        total_ref[p] = jnp.broadcast_to(total[:, p : p + 1], (SUB, LANES))
+    for v in range(nvar):
+        for lev in range(levels):
+            one = total[lev : lev + 1, v : v + 1]
+            total_ref[v * levels + lev] = jnp.broadcast_to(one, (SUB, LANES))
 
     pairs = levels // 2
 
@@ -223,7 +241,8 @@
     lax.fori_loop(0, nvar * pairs, pair, 0)
 
 
-def near_kernel(own_ref, order_ref, near_ref):
+def near_kernel(own_ref, *refs):
+    near_ref = refs[-1]
     even = even_place()
 
     def pair(n, carry):
@@ -242,7 +261,7 @@
 
 def prepare_kernel(
     steps, nvar, levels, tiles,
-    count_ref, after_ref, anear_ref, afar_ref, fnear_ref, ffar_ref, inc_ref, dobs_ref,
+    count_ref, after_ref, anear_ref, afar_ref, near_ref, far_ref, inc_ref, dobs_ref,
     first_ref, last_ref, force_ref,
 ):
     even = even_place()
@@ -251,8 +270,8 @@
 
     def pair(i, carry):
         offset = -(-(nvar * tiles + 1) // 2) * 2
-        fields = [decoded(ref, i, 0, nvar, tiles) for ref in (fnear_ref, ffar_ref)]
-        forces = [decoded(ref, i, offset, steps, tiles) for ref in (fnear_ref, ffar_ref)]
+        fields = [decoded(ref, i, 0, nvar, tiles) for ref in (near_ref, far_ref)]
+        forces = [decoded(ref, i, offset, steps, tiles) for ref in (near_ref, far_ref)]
         afters = [decoded(ref, i, 0, nvar, tiles) for ref in (anear_ref, afar_ref)]
         scales = jnp.exp2(floats(after_ref[i, nvar * tiles])) * (1.0 / CODE_MAX)
         for odd in range(2):
@@ -507,16 +526,6 @@
     return lax.ppermute(block, axis, swaps(axis, first))
 
 
-def swapped_back(block, first):
-    windows, spaces = lax.axis_size("window"), lax.axis_size("space")
-    route = [
-        ((w + 1) * spaces + source, w * spaces + target)
-        for w in range(windows - 1)
-        for source, target in swaps("space", first)
-    ]
-    return lax.ppermute(block, ("window", "space"), route)
-
-
 def body(
     trajectory,
     dual_model,
@@ -542,17 +551,15 @@
     def shape(dims, dtype):
         return jax.ShapeDtypeStruct(dims, dtype)
 
-    light = pl.CostEstimate(flops=0, bytes_accessed=0, transcendentals=0)
-
     def packed(distances):
         return pl.pallas_call(
             lambda *refs: pack_kernel(distances, windows, steps, nvar, levels, part, *refs),
             out_shape=[shape((nvar * levels + 1, rows, wide), bf16)] * len(distances),
-            in_specs=[SMEM, VMEM],
+            in_specs=[VMEM, VMEM],
             out_specs=[VMEM] * len(distances),
+            scratch_shapes=[pltpu.VMEM((SUB, LANES), f32)],
             compiler_params=params(),
-            cost_estimate=light,
-        )(error_var, trajectory)
+        )(error_var.transpose(0, 2, 1), trajectory)
 
     order = sorted(range(1, windows), key=lambda d: -d * (windows - d))
     groups = [[d] for d in order] if windows <= 4 else [order]
@@ -564,26 +571,30 @@
 
     payload = shape((pairs, nvar * tiles + 1, 2 * SUB, LANES), i16)
 
-    def half_tiles(*counts):
+    after = pl.pallas_call(
+        own_code_kernel,
+        out_shape=payload,
+        in_specs=[VMEM],
+        out_specs=VMEM,
+        compiler_params=params(),
+    )(dual_model)
+    after = moved(after, "window", -1)
+
+    def half_coded(counts, fields):
         total = sum(-(-(count * tiles + 1) // 2) for count in counts)
-        return shape((pairs, total, 2 * SUB, LANES), i16)
-
-    def coded(fields, own_codes):
-        halves = half_tiles(*[field.shape[1] for field in fields])
-        return pl.pallas_call(
-            lambda *refs: code_kernel(len(fields), own_codes, *refs),
-            out_shape=[halves, halves] + [payload] * own_codes,
-            in_specs=[VMEM] * len(fields) + [ANY],
-            out_specs=[VMEM] * (2 + own_codes),
+        halves = shape((pairs, total, 2 * SUB, LANES), i16)
+        near, far = pl.pallas_call(
+            half_code_kernel,
+            out_shape=[halves, halves],
+            in_specs=[VMEM] * len(fields),
+            out_specs=[VMEM] * 2,
             compiler_params=params(),
-            cost_estimate=light,
-        )(*fields, arrived[0])
-
-    after_near, after_far, after = coded([dual_model], 1)
-    after = moved(after, "window", -1)
-    after_near, after_far = swapped_back(after_near, 0), swapped_back(after_far, 1)
-    near, far = coded([increment, dual_obs], 0)
-    far, near = swapped(far, "space", 1), swapped(near, "space", 0)
+        )(*fields)
+        far = swapped(far, "space", 1)
+        return swapped(near, "space", 0), far
+
+    near, far = half_coded([nvar, steps], [increment, dual_obs])
+    after_near, after_far = half_coded([nvar], [after])
 
     own, traj_far, totals = pl.pallas_call(
         lambda *refs: assemble_kernel(windows, steps, nvar, levels, part, *refs),
@@ -598,6 +609,14 @@
         compiler_params=params(),
     )(*[arrived[d] for d in range(windows)])
     traj_far = swapped(traj_far, "space", 1)
+    traj_near = pl.pallas_call(
+        near_kernel,
+        out_shape=shape((steps, nvar * pairs, rows, columns), bf16),
+        in_specs=[VMEM] + [ANY] * 3,
+        out_specs=VMEM,
+        compiler_params=params(),
+    )(own, after, near, far)
+    traj_near = swapped(traj_near, "space", 0)
 
     state = shape((nvar, levels, rows, columns), f32)
     around = [shape((levels, n, tiles, 2 * SUB, LANES), f32) for n in (nvar, nvar, steps)]
@@ -608,14 +627,6 @@
         out_specs=[VMEM] * 3,
         compiler_params=params(),
     )(obs_count, after, after_near, after_far, near, far, increment, dual_obs)
-    traj_near = pl.pallas_call(
-        near_kernel,
-        out_shape=shape((steps, nvar * pairs, rows, columns), bf16),
-        in_specs=[VMEM, ANY],
-        out_specs=VMEM,
-        compiler_params=params(),
-    )(own, force)
-    traj_near = swapped(traj_near, "space", 0)
     new_dual_obs, base_dual, base_inc, *payloads = pl.pallas_call(
         lambda *refs: model_kernel(windows, spaces, steps, nvar, levels, tiles, *refs),
         out_shape=[shape(dual_obs.shape, f32), state, state] + [payload] * (windows - 1),

time: 53.3 us -> 51.9 us (0.974)
  the two profiles are of different devices: /device:TPU:0 before, /device:TPU:1 now
where the time goes in v4:
time: 51.9 us; the launch traced here: 51.5 us
  starting transfers between devices  26.3 us (51%)
  Pallas kernels  10.7 us (21%)
  waiting for transfers between devices  9.55 us (18%)
  local copies, waits for them, and re-layouts  3.39 us (7%)
  between operations  1.57 us (3%)
    ppermute x6, starting transfers between devices, swapped(): return lax.ppermute(block, axis, swaps(axis, first))  14.9 us
    ppermute x7, starting transfers between devices, moved(): return lax.ppermute(block, axis, route)  11.5 us
    pallas_call x1, Pallas kernels, body(): pl.pallas_call(lambda *refs: model_kernel(windows, spaces, steps, nvar, l...  6.65 us
    ppermute x7, waiting for transfers between devices, moved(): return lax.ppermute(block, axis, route)  6.57 us
    unnamed x24, local copies, waits for them, and re-layouts  3.39 us
    ppermute x6, waiting for transfers between devices, swapped(): return lax.ppermute(block, axis, swaps(axis, first))  2.98 us
    pallas_call x1, Pallas kernels, body(): pl.pallas_call(lambda *refs: assemble_kernel(windows, steps, nvar, levels...  1.16 us
    pallas_call x1, Pallas kernels, body(): pl.pallas_call(lambda *refs: final_kernel(windows, nvar, levels, tiles, *...  1.12 us
  transfers between devices with their start and end apart: 13, of which 3 were waited for; matrix products, arithmetic and copies ran while one was open for 0% of the time, Pallas kernels for 5%

profile of v4, /device:TPU:1, one launch (start us, length us, event | category | flops | bytes accessed | tf_op | source)
XLA Modules:
  0.0 51.5 jit_solution(17777701488409062025)
XLA Ops:
  0.6 1.1 %copy-done = bf16[4,4,5,4,8,96]{5,4,3,2,1,0:T(8,128)(2,1)S(1)} copy-done((bf16[4,4,5,4,8,96]{5,4,3,2,1,0:T(8,128)(2,1)S(1)}, bf16[4,4,5,4,8,96]{5,4,3,2,1,0:T(8,128)(2,1)}, u32[]{:S(2)}) %copy-start) | copy-done | bytes 491544
  1.7 0.7 %copy-done.8 = f32[1,5,4]{1,2,0:T(4,128)S(1)} copy-done((f32[1,5,4]{1,2,0:T(4,128)S(1)}, f32[1,5,4]{1,2,0:T(4,128)}, u32[]{:S(2)}) %copy-start.8) | copy-done | bytes 104
  2.4 0.1 shard_map.122
  2.5 2.2 %collective-permute-start = (bf16[21,8,384]{2,1,0:T(8,128)(2,1)S(1)}, bf16[21,8,384]{2,1,0:T(8,128)(2,1)S(1)}, u32[]{:S(2)}, u32[]{:S(2)}) collective-permute-start(bf16[21,8,384]{2,1,0:T(8,128)(2,1)S(1)} %shard_map.122), channel_id=1, source_target_pairs={{0,4},{4,8},{8,12},{12,0},{1,5},{5,9},{9,13},{13,1},{2,6},{6,10},{... | collective-permute-start | bytes 387080 | tf_op jit(solution)/shard_map/ppermute | solution.py:515
  4.7 0.9 %copy-done.4 = f32[1,5,4,8,384]{4,3,2,1,0:T(8,128)S(1)} copy-done((f32[1,5,4,8,384]{4,3,2,1,0:T(8,128)S(1)}, f32[1,5,4,8,384]{4,3,2,1,0:T(8,128)}, u32[]{:S(2)}) %copy-start.4) | copy-done | bytes 245784
  5.6 0.3 shard_map.126
  5.9 1.3 %collective-permute-start.3 = (s16[2,16,16,128]{3,2,1,0:T(8,128)(2,1)S(1)}, s16[2,16,16,128]{3,2,1,0:T(8,128)(2,1)S(1)}, u32[]{:S(2)}, u32[]{:S(2)}) collective-permute-start(s16[2,16,16,128]{3,2,1,0:T(8,128)(2,1)S(1)} %shard_map.126), channel_id=1, source_target_pairs={{4,0},{8,4},{12,8},{5,1},{9,5},{13,9},{6,2},{10,6},{14,10},{7,3},{... | collective-permute-start | bytes 393224 | tf_op jit(solution)/shard_map/ppermute | solution.py:515
  7.2 0.1 shard_map.123
  7.4 3.2 %collective-permute-start.1 = (bf16[21,8,384]{2,1,0:T(8,128)(2,1)S(1)}, bf16[21,8,384]{2,1,0:T(8,128)(2,1)S(1)}, u32[]{:S(2)}, u32[]{:S(2)}) collective-permute-start(bf16[21,8,384]{2,1,0:T(8,128)(2,1)S(1)} %shard_map.123), channel_id=1, source_target_pairs={{0,8},{4,12},{8,0},{12,4},{1,9},{5,13},{9,1},{13,5},{2,10},{6,14},... | collective-permute-start | bytes 387080 | tf_op jit(solution)/shard_map/ppermute | solution.py:515
  10.6 0.1 shard_map.124
  10.7 1.1 %collective-permute-start.2 = (bf16[21,8,384]{2,1,0:T(8,128)(2,1)S(1)}, bf16[21,8,384]{2,1,0:T(8,128)(2,1)S(1)}, u32[]{:S(2)}, u32[]{:S(2)}) collective-permute-start(bf16[21,8,384]{2,1,0:T(8,128)(2,1)S(1)} %shard_map.124), channel_id=1, source_target_pairs={{0,12},{4,0},{8,4},{12,8},{1,13},{5,1},{9,5},{13,9},{2,14},{6,2},{... | collective-permute-start | bytes 387080 | tf_op jit(solution)/shard_map/ppermute | solution.py:515
  11.8 0.4 shard_map.127
  12.2 1.9 %collective-permute-start.4 = (s16[2,15,16,128]{3,2,1,0:T(8,128)(2,1)S(1)}, s16[2,15,16,128]{3,2,1,0:T(8,128)(2,1)S(1)}, u32[]{:S(2)}, u32[]{:S(2)}) collective-permute-start(s16[2,15,16,128]{3,2,1,0:T(8,128)(2,1)S(1)} %get-tuple-element.23), channel_id=1, source_target_pairs={{0,1},{1,0},{2,3},{3,2},{4,5},{5,4},{6,7},{7,6},{8,9},{9,8},{10,11... | collective-permute-start | bytes 368648 | tf_op jit(solution)/shard_map/ppermute | solution.py:526
  14.0 3.0 %collective-permute-start.5 = (s16[2,15,16,128]{3,2,1,0:T(8,128)(2,1)S(1)}, s16[2,15,16,128]{3,2,1,0:T(8,128)(2,1)S(1)}, u32[]{:S(2)}, u32[]{:S(2)}) collective-permute-start(s16[2,15,16,128]{3,2,1,0:T(8,128)(2,1)S(1)} %get-tuple-element.24), channel_id=1, source_target_pairs={{1,2},{2,1},{5,6},{6,5},{9,10},{10,9},{13,14},{14,13},{17,18},{18,... | collective-permute-start | bytes 368648 | tf_op jit(solution)/shard_map/ppermute | solution.py:526
  17.1 0.1 shard_map.121.refs_0_
  17.2 1.2 %shard_map.125 = (bf16[4,20,8,384]{3,2,1,0:T(8,128)(2,1)S(1)}, bf16[4,10,8,384]{3,2,1,0:T(8,128)(2,1)S(1)}, f32[20,8,128]{2,1,0:T(8,128)S(1)}) custom-call(bf16[21,8,384]{2,1,0:T(8,128)(2,1)S(1)} %shard_map.121.refs_0_, bf16[21,8,384]{2,1,0:T(8,128)(2,1)S(1)} %collective-permute-done.refs_1_, bf16[21,8,384]{2,1,0:T(8,128)(2,1)S(1)} %collective-permute-done.1.refs_2_, ...), custom_call_target="tpu_custom_call" | custom-call | tf_op jit(solution)/shard_map/pallas_call | solution.py:599
  18.4 7.4 %collective-permute-start.7 = (bf16[4,10,8,384]{3,2,1,0:T(8,128)(2,1)S(1)}, bf16[4,10,8,384]{3,2,1,0:T(8,128)(2,1)S(1)}, u32[]{:S(2)}, u32[]{:S(2)}) collective-permute-start(bf16[4,10,8,384]{3,2,1,0:T(8,128)(2,1)S(1)} %get-tuple-element.25), channel_id=1, source_target_pairs={{1,2},{2,1},{5,6},{6,5},{9,10},{10,9},{13,14},{14,13},{17,18},{18,... | collective-permute-start | bytes 737288 | tf_op jit(solution)/shard_map/ppermute | solution.py:526
  25.9 0.2 shard_map.128
  26.1 0.1 collective-permute-start.6
  26.2 0.1 shard_map.129
  26.2 0.5 %collective-permute-start.8 = (s16[2,8,16,128]{3,2,1,0:T(8,128)(2,1)S(1)}, s16[2,8,16,128]{3,2,1,0:T(8,128)(2,1)S(1)}, u32[]{:S(2)}, u32[]{:S(2)}) collective-permute-start(s16[2,8,16,128]{3,2,1,0:T(8,128)(2,1)S(1)} %get-tuple-element.26), channel_id=1, source_target_pairs={{0,1},{1,0},{2,3},{3,2},{4,5},{5,4},{6,7},{7,6},{8,9},{9,8},{10,11... | collective-permute-start | bytes 196616 | tf_op jit(solution)/shard_map/ppermute | solution.py:526
  26.8 1.9 %collective-permute-start.9 = (s16[2,8,16,128]{3,2,1,0:T(8,128)(2,1)S(1)}, s16[2,8,16,128]{3,2,1,0:T(8,128)(2,1)S(1)}, u32[]{:S(2)}, u32[]{:S(2)}) collective-permute-start(s16[2,8,16,128]{3,2,1,0:T(8,128)(2,1)S(1)} %get-tuple-element.27), channel_id=1, source_target_pairs={{1,2},{2,1},{5,6},{6,5},{9,10},{10,9},{13,14},{14,13},{17,18},{18,... | collective-permute-start | bytes 196616 | tf_op jit(solution)/shard_map/ppermute | solution.py:526
  29.4 3.0 %collective-permute-done.9.refs_3_ = s16[2,8,16,128]{3,2,1,0:T(8,128)(2,1)S(1)} collective-permute-done((s16[2,8,16,128]{3,2,1,0:T(8,128)(2,1)S(1)}, s16[2,8,16,128]{3,2,1,0:T(8,128)(2,1)S(1)}, u32[]{:S(2)}, u32[]{:S(2)}) %collective-permute-start.9) | collective-permute-done | bytes 65568 | tf_op jit(solution)/shard_map/ppermute | solution.py:526
  32.4 0.4 shard_map.130
  32.8 0.6 %copy-done.10 = f32[5,5]{1,0:T(8,128)S(1)} copy-done((f32[5,5]{1,0:T(8,128)S(1)}, f32[5,5]{1,0:T(8,128)}, u32[]{:S(2)}) %copy-start.10) | copy-done | bytes 124
  33.5 6.7 %shard_map.131 = (f32[1,4,4,8,384]{4,3,2,1,0:T(8,128)}, f32[5,4,8,384]{3,2,1,0:T(8,128)S(1)}, f32[5,4,8,384]{3,2,1,0:T(8,128)S(1)}, s16[2,16,16,128]{3,2,1,0:T(8...) custom-call(f32[5,5]{1,0:T(8,128)S(1)} %copy-done.10, ...), custom_call_target="tpu_custom_call" | custom-call | tf_op jit(solution)/shard_map/pallas_call | solution.py:630
  40.1 1.7 %collective-permute-start.10 = (s16[2,16,16,128]{3,2,1,0:T(8,128)(2,1)S(1)}, s16[2,16,16,128]{3,2,1,0:T(8,128)(2,1)S(1)}, u32[]{:S(2)}, u32[]{:S(2)}) collective-permute-start(s16[2,16,16,128]{3,2,1,0:T(8,128)(2,1)S(1)} %get-tuple-element.31), channel_id=1, source_target_pairs={{0,4},{4,8},{8,12},{12,0},{1,5},{5,9},{9,13},{13,1},{2,6},{6,10},{... | collective-permute-start | bytes 393224 | tf_op jit(solution)/shard_map/ppermute | solution.py:515
  41.8 0.7 %collective-permute-start.11 = (s16[2,16,16,128]{3,2,1,0:T(8,128)(2,1)S(1)}, s16[2,16,16,128]{3,2,1,0:T(8,128)(2,1)S(1)}, u32[]{:S(2)}, u32[]{:S(2)}) collective-permute-start(s16[2,16,16,128]{3,2,1,0:T(8,128)(2,1)S(1)} %get-tuple-element.32), channel_id=1, source_target_pairs={{0,8},{4,12},{8,0},{12,4},{1,9},{5,13},{9,1},{13,5},{2,10},{6,14},... | collective-permute-start | bytes 393224 | tf_op jit(solution)/shard_map/ppermute | solution.py:515
  42.5 1.4 %collective-permute-start.12 = (s16[2,16,16,128]{3,2,1,0:T(8,128)(2,1)S(1)}, s16[2,16,16,128]{3,2,1,0:T(8,128)(2,1)S(1)}, u32[]{:S(2)}, u32[]{:S(2)}) collective-permute-start(s16[2,16,16,128]{3,2,1,0:T(8,128)(2,1)S(1)} %get-tuple-element.33), channel_id=1, source_target_pairs={{0,12},{4,0},{8,4},{12,8},{1,13},{5,1},{9,5},{13,9},{2,14},{6,2},{... | collective-permute-start | bytes 393224 | tf_op jit(solution)/shard_map/ppermute | solution.py:515
  43.9 2.7 %collective-permute-done.10.refs_0_ = s16[2,16,16,128]{3,2,1,0:T(8,128)(2,1)S(1)} collective-permute-done((s16[2,16,16,128]{3,2,1,0:T(8,128)(2,1)S(1)}, s16[2,16,16,128]{3,2,1,0:T(8,128)(2,1)S(1)}, u32[]{:S(2)}, u32[]{:S(2)}) %collective-permute-start.10) | collective-permute-done | bytes 131104 | tf_op jit(solution)/shard_map/ppermute | solution.py:515
  46.5 3.9 %collective-permute-done.11.refs_1_ = s16[2,16,16,128]{3,2,1,0:T(8,128)(2,1)S(1)} collective-permute-done((s16[2,16,16,128]{3,2,1,0:T(8,128)(2,1)S(1)}, s16[2,16,16,128]{3,2,1,0:T(8,128)(2,1)S(1)}, u32[]{:S(2)}, u32[]{:S(2)}) %collective-permute-start.11) | collective-permute-done | bytes 131104 | tf_op jit(solution)/shard_map/ppermute | solution.py:515
  50.4 1.1 %shard_map.132 = (f32[1,5,4,8,384]{4,3,2,1,0:T(8,128)}, f32[1,5,4,8,384]{4,3,2,1,0:T(8,128)}) custom-call(s16[2,16,16,128]{3,2,1,0:T(8,128)(2,1)S(1)} %collective-permute-done.10.refs_0_, s16[2,16,16,128]{3,2,1,0:T(8,128)(2,1)S(1)} %collective-permute-done.11.refs_1_, s16[2,16,16,128]{3,2,1,0:T(8,128)(2,1)S(1)} %collective-permute-done.12.refs_2_, ...), custom_call_target="tpu_custom_call" | custom-call | tf_op jit(solution)/shard_map/pallas_call | solution.py:648
  (30 shorter events, 0.1 us)
Async XLA Ops:
  0.6 1.1 %copy-start = (bf16[4,4,5,4,8,96]{5,4,3,2,1,0:T(8,128)(2,1)S(1)}, bf16[4,4,5,4,8,96]{5,4,3,2,1,0:T(8,128)(2,1)}, u32[]{:S(2)}) copy-start(bf16[4,4,5,4,8,96]{5,4,3,2,1,0:T(8,128)(2,1)} %refs_1_.9) | copy-start | bytes 1474564
  1.7 0.7 %copy-start.8 = (f32[1,5,4]{1,2,0:T(4,128)S(1)}, f32[1,5,4]{1,2,0:T(4,128)}, u32[]{:S(2)}) copy-start(f32[1,5,4]{1,2,0:T(4,128)} %param.17) | copy-start | bytes 244
  2.4 4.8 %copy-start.1 = (bf16[4,4,5,4,8,96]{5,4,3,2,1,0:T(8,128)(2,1)S(1)}, bf16[4,4,5,4,8,96]{5,4,3,2,1,0:T(8,128)(2,1)}, u32[]{:S(2)}) copy-start(bf16[4,4,5,4,8,96]{5,4,3,2,1,0:T(8,128)(2,1)} %refs_1_.9) | copy-start | bytes 1474564
  2.5 11.5 %collective-permute-start = (bf16[21,8,384]{2,1,0:T(8,128)(2,1)S(1)}, bf16[21,8,384]{2,1,0:T(8,128)(2,1)S(1)}, u32[]{:S(2)}, u32[]{:S(2)}) collective-permute-start(bf16[21,8,384]{2,1,0:T(8,128)(2,1)S(1)} %shard_map.122), channel_id=1, source_target_pairs={{0,4},{4,8},{8,12},{12,0},{1,5},{5,9},{9,13},{13,1},{2,6},{6,10},{... | collective-permute-start | bytes 387080 | tf_op jit(solution)/shard_map/ppermute | solution.py:515
  4.7 0.9 %copy-start.4 = (f32[1,5,4,8,384]{4,3,2,1,0:T(8,128)S(1)}, f32[1,5,4,8,384]{4,3,2,1,0:T(8,128)}, u32[]{:S(2)}) copy-start(f32[1,5,4,8,384]{4,3,2,1,0:T(8,128)} %refs_13_.1) | copy-start | bytes 737284
  5.6 1.6 %copy-start.9 = (f32[1,5,4]{1,2,0:T(4,128)S(1)}, f32[1,5,4]{1,2,0:T(4,128)}, u32[]{:S(2)}) copy-start(f32[1,5,4]{1,2,0:T(4,128)} %param.17) | copy-start | bytes 244
  5.9 19.9 %collective-permute-start.3 = (s16[2,16,16,128]{3,2,1,0:T(8,128)(2,1)S(1)}, s16[2,16,16,128]{3,2,1,0:T(8,128)(2,1)S(1)}, u32[]{:S(2)}, u32[]{:S(2)}) collective-permute-start(s16[2,16,16,128]{3,2,1,0:T(8,128)(2,1)S(1)} %shard_map.126), channel_id=1, source_target_pairs={{4,0},{8,4},{12,8},{5,1},{9,5},{13,9},{6,2},{10,6},{14,10},{7,3},{... | collective-permute-start | bytes 393224 | tf_op jit(solution)/shard_map/ppermute | solution.py:515
  7.4 4.4 %copy-start.2 = (f32[1,5,4,8,384]{4,3,2,1,0:T(8,128)S(1)}, f32[1,5,4,8,384]{4,3,2,1,0:T(8,128)}, u32[]{:S(2)}) copy-start(f32[1,5,4,8,384]{4,3,2,1,0:T(8,128)} %refs_10_.1) | copy-start | bytes 737284
  7.4 4.4 %copy-start.3 = (f32[1,4,4,8,384]{4,3,2,1,0:T(8,128)S(1)}, f32[1,4,4,8,384]{4,3,2,1,0:T(8,128)}, u32[]{:S(2)}) copy-start(f32[1,4,4,8,384]{4,3,2,1,0:T(8,128)} %refs_11_.1) | copy-start | bytes 589828
  7.4 9.8 %collective-permute-start.1 = (bf16[21,8,384]{2,1,0:T(8,128)(2,1)S(1)}, bf16[21,8,384]{2,1,0:T(8,128)(2,1)S(1)}, u32[]{:S(2)}, u32[]{:S(2)}) collective-permute-start(bf16[21,8,384]{2,1,0:T(8,128)(2,1)S(1)} %shard_map.123), channel_id=1, source_target_pairs={{0,8},{4,12},{8,0},{12,4},{1,9},{5,13},{9,1},{13,5},{2,10},{6,14},... | collective-permute-start | bytes 387080 | tf_op jit(solution)/shard_map/ppermute | solution.py:515
  10.7 6.5 %collective-permute-start.2 = (bf16[21,8,384]{2,1,0:T(8,128)(2,1)S(1)}, bf16[21,8,384]{2,1,0:T(8,128)(2,1)S(1)}, u32[]{:S(2)}, u32[]{:S(2)}) collective-permute-start(bf16[21,8,384]{2,1,0:T(8,128)(2,1)S(1)} %shard_map.124), channel_id=1, source_target_pairs={{0,12},{4,0},{8,4},{12,8},{1,13},{5,1},{9,5},{13,9},{2,14},{6,2},{... | collective-permute-start | bytes 387080 | tf_op jit(solution)/shard_map/ppermute | solution.py:515
  12.2 13.7 %collective-permute-start.4 = (s16[2,15,16,128]{3,2,1,0:T(8,128)(2,1)S(1)}, s16[2,15,16,128]{3,2,1,0:T(8,128)(2,1)S(1)}, u32[]{:S(2)}, u32[]{:S(2)}) collective-permute-start(s16[2,15,16,128]{3,2,1,0:T(8,128)(2,1)S(1)} %get-tuple-element.23), channel_id=1, source_target_pairs={{0,1},{1,0},{2,3},{3,2},{4,5},{5,4},{6,7},{7,6},{8,9},{9,8},{10,11... | collective-permute-start | bytes 368648 | tf_op jit(solution)/shard_map/ppermute | solution.py:526
  14.0 11.8 %collective-permute-start.5 = (s16[2,15,16,128]{3,2,1,0:T(8,128)(2,1)S(1)}, s16[2,15,16,128]{3,2,1,0:T(8,128)(2,1)S(1)}, u32[]{:S(2)}, u32[]{:S(2)}) collective-permute-start(s16[2,15,16,128]{3,2,1,0:T(8,128)(2,1)S(1)} %get-tuple-element.24), channel_id=1, source_target_pairs={{1,2},{2,1},{5,6},{6,5},{9,10},{10,9},{13,14},{14,13},{17,18},{18,... | collective-permute-start | bytes 368648 | tf_op jit(solution)/shard_map/ppermute | solution.py:526
  18.4 14.4 %collective-permute-start.7 = (bf16[4,10,8,384]{3,2,1,0:T(8,128)(2,1)S(1)}, bf16[4,10,8,384]{3,2,1,0:T(8,128)(2,1)S(1)}, u32[]{:S(2)}, u32[]{:S(2)}) collective-permute-start(bf16[4,10,8,384]{3,2,1,0:T(8,128)(2,1)S(1)} %get-tuple-element.25), channel_id=1, source_target_pairs={{1,2},{2,1},{5,6},{6,5},{9,10},{10,9},{13,14},{14,13},{17,18},{18,... | collective-permute-start | bytes 737288 | tf_op jit(solution)/shard_map/ppermute | solution.py:526
  26.1 6.7 %collective-permute-start.6 = (bf16[4,10,8,384]{3,2,1,0:T(8,128)(2,1)S(1)}, bf16[4,10,8,384]{3,2,1,0:T(8,128)(2,1)S(1)}, u32[]{:S(2)}, u32[]{:S(2)}) collective-permute-start(bf16[4,10,8,384]{3,2,1,0:T(8,128)(2,1)S(1)} %shard_map.128), channel_id=1, source_target_pairs={{0,1},{1,0},{2,3},{3,2},{4,5},{5,4},{6,7},{7,6},{8,9},{9,8},{10,11... | collective-permute-start | bytes 737288 | tf_op jit(solution)/shard_map/ppermute | solution.py:526
  26.2 3.1 %collective-permute-start.8 = (s16[2,8,16,128]{3,2,1,0:T(8,128)(2,1)S(1)}, s16[2,8,16,128]{3,2,1,0:T(8,128)(2,1)S(1)}, u32[]{:S(2)}, u32[]{:S(2)}) collective-permute-start(s16[2,8,16,128]{3,2,1,0:T(8,128)(2,1)S(1)} %get-tuple-element.26), channel_id=1, source_target_pairs={{0,1},{1,0},{2,3},{3,2},{4,5},{5,4},{6,7},{7,6},{8,9},{9,8},{10,11... | collective-permute-start | bytes 196616 | tf_op jit(solution)/shard_map/ppermute | solution.py:526
  26.8 5.6 %collective-permute-start.9 = (s16[2,8,16,128]{3,2,1,0:T(8,128)(2,1)S(1)}, s16[2,8,16,128]{3,2,1,0:T(8,128)(2,1)S(1)}, u32[]{:S(2)}, u32[]{:S(2)}) collective-permute-start(s16[2,8,16,128]{3,2,1,0:T(8,128)(2,1)S(1)} %get-tuple-element.27), channel_id=1, source_target_pairs={{1,2},{2,1},{5,6},{6,5},{9,10},{10,9},{13,14},{14,13},{17,18},{18,... | collective-permute-start | bytes 196616 | tf_op jit(solution)/shard_map/ppermute | solution.py:526
  29.4 3.4 %copy-start.5 = (f32[1,5,4,8,384]{4,3,2,1,0:T(8,128)S(1)}, f32[1,5,4,8,384]{4,3,2,1,0:T(8,128)}, u32[]{:S(2)}) copy-start(f32[1,5,4,8,384]{4,3,2,1,0:T(8,128)} %refs_13_.1) | copy-start | bytes 737284
  29.4 3.4 %copy-start.6 = (f32[1,5,4,8,384]{4,3,2,1,0:T(8,128)S(1)}, f32[1,5,4,8,384]{4,3,2,1,0:T(8,128)}, u32[]{:S(2)}) copy-start(f32[1,5,4,8,384]{4,3,2,1,0:T(8,128)} %refs_12_.1) | copy-start | bytes 737284
  29.4 3.4 %copy-start.7 = (f32[1,4,4,8,384]{4,3,2,1,0:T(8,128)S(1)}, f32[1,4,4,8,384]{4,3,2,1,0:T(8,128)}, u32[]{:S(2)}) copy-start(f32[1,4,4,8,384]{4,3,2,1,0:T(8,128)} %refs_14_.1) | copy-start | bytes 589828
  32.7 0.7 %copy-start.10 = (f32[5,5]{1,0:T(8,128)S(1)}, f32[5,5]{1,0:T(8,128)}, u32[]{:S(2)}) copy-start(f32[5,5]{1,0:T(8,128)} %refs_0_.4) | copy-start | bytes 304
  32.8 0.7 %copy-start.11 = (f32[1,4,4]{2,1,0:T(4,128)S(1)}, f32[1,4,4]{2,1,0:T(4,128)}, u32[]{:S(2)}) copy-start(f32[1,4,4]{2,1,0:T(4,128)} %refs_2_.1) | copy-start | bytes 196
  40.1 6.4 %collective-permute-start.10 = (s16[2,16,16,128]{3,2,1,0:T(8,128)(2,1)S(1)}, s16[2,16,16,128]{3,2,1,0:T(8,128)(2,1)S(1)}, u32[]{:S(2)}, u32[]{:S(2)}) collective-permute-start(s16[2,16,16,128]{3,2,1,0:T(8,128)(2,1)S(1)} %get-tuple-element.31), channel_id=1, source_target_pairs={{0,4},{4,8},{8,12},{12,0},{1,5},{5,9},{9,13},{13,1},{2,6},{6,10},{... | collective-permute-start | bytes 393224 | tf_op jit(solution)/shard_map/ppermute | solution.py:515
  41.8 8.6 %collective-permute-start.11 = (s16[2,16,16,128]{3,2,1,0:T(8,128)(2,1)S(1)}, s16[2,16,16,128]{3,2,1,0:T(8,128)(2,1)S(1)}, u32[]{:S(2)}, u32[]{:S(2)}) collective-permute-start(s16[2,16,16,128]{3,2,1,0:T(8,128)(2,1)S(1)} %get-tuple-element.32), channel_id=1, source_target_pairs={{0,8},{4,12},{8,0},{12,4},{1,9},{5,13},{9,1},{13,5},{2,10},{6,14},... | collective-permute-start | bytes 393224 | tf_op jit(solution)/shard_map/ppermute | solution.py:515
  42.5 7.9 %collective-permute-start.12 = (s16[2,16,16,128]{3,2,1,0:T(8,128)(2,1)S(1)}, s16[2,16,16,128]{3,2,1,0:T(8,128)(2,1)S(1)}, u32[]{:S(2)}, u32[]{:S(2)}) collective-permute-start(s16[2,16,16,128]{3,2,1,0:T(8,128)(2,1)S(1)} %get-tuple-element.33), channel_id=1, source_target_pairs={{0,12},{4,0},{8,4},{12,8},{1,13},{5,1},{9,5},{13,9},{2,14},{6,2},{... | collective-permute-start | bytes 393224 | tf_op jit(solution)/shard_map/ppermute | solution.py:515

commit v5 on v4

--- a/solution.py
+++ b/solution.py
@@ -19,7 +19,6 @@
 
 VMEM = pl.BlockSpec(memory_space=pltpu.VMEM)
 SMEM = pl.BlockSpec(memory_space=pltpu.SMEM)
-ANY = pl.BlockSpec(memory_space=pl.ANY)
 
 
 def params(mib=24):
@@ -148,31 +147,17 @@
     return values + [scales]
 
 
-def own_code_kernel(field_ref, out_ref):
+def half_code_kernel(*refs):
+    sources, (near_ref, far_ref, own_ref) = refs[:-3], refs[-3:]
+    even = even_place()
+
     def pair(i, carry):
-        coded = [level_codes(field_ref, 2 * i + odd) for odd in range(2)]
-        for n, (first, second) in enumerate(zip(*coded)):
-            out_ref[i, n] = shorts(jnp.concatenate([first, second], 0))
-        return carry
-
-    lax.fori_loop(0, out_ref.shape[0], pair, 0)
-
-
-def half_code_kernel(*refs):
-    sources, (near_ref, far_ref) = refs[:-2], refs[-2:]
-    even = even_place()
-
-    def pair(i, carry):
-        groups = []
-        for ref in sources:
-            if ref.dtype == jnp.int16:
-                whole = [floats(ref[i, n]) for n in range(ref.shape[1])]
-                groups.append([[tile[:SUB] for tile in whole], [tile[SUB:] for tile in whole]])
-            else:
-                groups.append([level_codes(ref, 2 * i + odd) for odd in range(2)])
         near, far = [], []
-        for coded in groups:
-            for first, second in zip(*coded):
+        for k, ref in enumerate(sources):
+            coded = [level_codes(ref, 2 * i + odd) for odd in range(2)]
+            for n, (first, second) in enumerate(zip(*coded)):
+                if k == 0:
+                    own_ref[i, n] = shorts(jnp.concatenate([first, second], 0))
                 last, start = joined_halves(first, second)
                 near.append(jnp.where(even, last, start))
                 far.append(jnp.where(even, start, last))
@@ -192,6 +177,29 @@
     return whole[SUB:] if n % 2 else whole[:SUB]
 
 
+def around_kernel(windows, nvar, levels, *refs):
+    pieces, (own_ref, near_ref, far_ref) = refs[:windows], refs[windows : windows + 3]
+    outs, total_ref = refs[windows + 3 : -1], refs[-1]
+    me = lax.axis_index("window")
+    even = even_place()
+    total = jnp.zeros((SUB, LANES), jnp.float32)
+    for d in range(windows):
+        split = pieces[d][nvar * levels, :, :LANES].astype(jnp.float32)
+        here = split + pltpu.roll(split, HALF, 0) + pltpu.roll(split, LANES // 2, 1)
+        total = total + jnp.where(lax.rem(me - d + windows, windows) <= me, here, 0.0)
+    for v in range(nvar):
+        for lev in range(levels):
+            one = total[lev : lev + 1, v : v + 1]
+            total_ref[v * levels + lev] = jnp.broadcast_to(one, (SUB, LANES))
+    for i, out_ref in enumerate(outs):
+        for n in range(own_ref.shape[1]):
+            own = floats(own_ref[i, n])
+            near, far = half_tile(near_ref, i, n), half_tile(far_ref, i, n)
+            for odd in range(2):
+                halves = widened(own[odd * SUB : (odd + 1) * SUB], near, far, odd, even)
+                out_ref[odd, n] = shorts(jnp.concatenate(halves, 0))
+
+
 def decoded(ref, i, first, nvar, tiles):
     scales = jnp.exp2(half_tile(ref, i, first + nvar * tiles)) * (1.0 / CODE_MAX)
     return [
@@ -202,25 +210,17 @@
 
 def assemble_kernel(windows, steps, nvar, levels, part, *refs):
     pieces = refs[:windows]
-    own_ref, far_ref, total_ref, stack_ref = refs[windows:]
+    own_ref, near_ref, early_ref, late_ref, stack_ref = refs[windows:]
     me = lax.axis_index("window")
     even = even_place()
     lane = lane_index()
-    total = jnp.zeros((SUB, LANES), jnp.float32)
     for d in range(windows):
         source = lax.rem(me - d + windows, windows)
         stack_ref[source] = pieces[d][: nvar * levels]
-        split = pieces[d][nvar * levels, :, :LANES].astype(jnp.float32)
-        here = split + pltpu.roll(split, HALF, 0) + pltpu.roll(split, LANES // 2, 1)
-        total = total + jnp.where(source <= me, here, 0.0)
-    for v in range(nvar):
-        for lev in range(levels):
-            one = total[lev : lev + 1, v : v + 1]
-            total_ref[v * levels + lev] = jnp.broadcast_to(one, (SUB, LANES))
 
     pairs = levels // 2
 
-    def pair(n, carry):
+    def pair(n):
         both = []
         for odd in range(2):
             plane = 2 * n + odd
@@ -235,74 +235,68 @@
         for j in range(steps):
             halves = [joined_halves(a, b) for a, b in zip(both[0][j], both[1][j])]
             last, start = (jnp.concatenate([h[k] for h in halves], 1) for k in range(2))
-            far_ref[j, n] = jnp.where(even, start, last).astype(jnp.bfloat16)
+            near_ref[j, n] = jnp.where(even, last, start).astype(jnp.bfloat16)
+            far = jnp.where(even, start, last).astype(jnp.bfloat16)
+            if j < steps // 2:
+                early_ref[j, n] = far
+            else:
+                late_ref[j - steps // 2, n] = far
+
+    def variable(v, carry):
+        for i in range(pairs):
+            pair(v * pairs + i)
         return carry
 
-    lax.fori_loop(0, nvar * pairs, pair, 0)
-
-
-def near_kernel(own_ref, *refs):
-    near_ref = refs[-1]
-    even = even_place()
-
-    def pair(n, carry):
-        for j in range(own_ref.shape[0]):
-            for t in range(0, own_ref.shape[-1], LANES):
-                cut = slice(t, t + LANES)
-                first, second = (
-                    own_ref[j, 2 * n + odd, :, cut].astype(jnp.float32) for odd in range(2)
-                )
-                last, start = joined_halves(first, second)
-                near_ref[j, n, :, cut] = jnp.where(even, last, start).astype(jnp.bfloat16)
-        return carry
-
-    lax.fori_loop(0, near_ref.shape[1], pair, 0)
+    lax.fori_loop(0, nvar, variable, 0)
 
 
 def prepare_kernel(
     steps, nvar, levels, tiles,
-    count_ref, after_ref, anear_ref, afar_ref, near_ref, far_ref, inc_ref, dobs_ref,
-    first_ref, last_ref, force_ref,
+    count_ref, noise_ref, coupling_ref, near_ref, far_ref, inc_ref, dobs_ref, innov_ref, *refs,
 ):
+    after_refs = refs[: levels // 2]
+    first_ref, last_ref, force_ref, obs_ref, share_ref, mix_ref = refs[levels // 2 :]
     even = even_place()
     blocks = [slice(0, SUB), slice(SUB, 2 * SUB)]
     cuts = [slice(t * LANES, (t + 1) * LANES) for t in range(tiles)]
-
-    def pair(i, carry):
-        offset = -(-(nvar * tiles + 1) // 2) * 2
-        fields = [decoded(ref, i, 0, nvar, tiles) for ref in (near_ref, far_ref)]
-        forces = [decoded(ref, i, offset, steps, tiles) for ref in (near_ref, far_ref)]
-        afters = [decoded(ref, i, 0, nvar, tiles) for ref in (anear_ref, afar_ref)]
-        scales = jnp.exp2(floats(after_ref[i, nvar * tiles])) * (1.0 / CODE_MAX)
+    for v in range(nvar):
+        for u in range(nvar):
+            one = coupling_gain * coupling_ref[v : v + 1, u : u + 1]
+            mix_ref[v, u] = jnp.broadcast_to(one, (SUB, LANES))
+    seen = [jnp.where(j < count_ref[0], 1.0, 0.0) for j in range(steps)]
+    offset = -(-(nvar * tiles + 1) // 2) * 2
+    for i, after_ref in enumerate(after_refs):
+        fields = [decoded(ref, i, offset, nvar, tiles) for ref in (near_ref, far_ref)]
+        forces = [decoded(ref, i, 2 * offset, steps, tiles) for ref in (near_ref, far_ref)]
         for odd in range(2):
             lev = 2 * i + odd
-            rows = blocks[odd]
+            scales = jnp.exp2(floats(after_ref[odd, nvar * tiles])) * (-1.0 / CODE_MAX)
             for t in range(tiles):
                 for v in range(nvar):
                     near, far = (side[v][t] for side in fields)
                     halves = widened(inc_ref[0, v, lev, :, cuts[t]], near, far, odd, even)
                     for b in range(2):
                         first_ref[lev, v, t, blocks[b], :] = halves[b]
-                    near, far = (side[v][t] for side in afters)
-                    own = floats(after_ref[i, v * tiles + t])[rows] * scales[rows, v : v + 1]
-                    halves = widened(own, near, far, odd, even)
-                    for b in range(2):
-                        last_ref[lev, v, t, blocks[b], :] = -halves[b]
+                    value = floats(after_ref[odd, v * tiles + t])
+                    last_ref[lev, v, t] = value * scales[:, v : v + 1]
                 for j in range(steps):
-                    seen = jnp.where(j < count_ref[0], 1.0, 0.0)
                     near, far = (side[j][t] for side in forces)
                     halves = widened(dobs_ref[0, j, lev, :, cuts[t]], near, far, odd, even)
                     for b in range(2):
-                        force_ref[lev, j, t, blocks[b], :] = seen * halves[b]
-        return carry
-
-    lax.fori_loop(0, levels // 2, pair, 0)
+                        force_ref[lev, j, t, blocks[b], :] = seen[j] * halves[b]
+            for j in range(steps):
+                noise = jnp.full((SUB, LANES), noise_ref[0, j, lev])
+                share = seen[j] / noise
+                share_ref[lev, j] = share
+                for t in range(tiles):
+                    gap = innov_ref[0, j, lev, :, cuts[t]] - noise * dobs_ref[0, j, lev, :, cuts[t]]
+                    obs_ref[lev, j, t] = gap * share
 
 
 def model_kernel(
     windows, spaces, steps, nvar, levels, tiles,
-    coupling_ref, count_ref, noise_ref, total_ref, own_ref, near_ref, far_ref,
-    first_ref, last_ref, force_ref, inc_ref, dobs_ref, rhs_ref, dual_ref, innov_ref,
+    mix_ref, share_ref, obs_ref, total_ref, own_ref, near_ref, early_ref, late_ref,
+    first_ref, last_ref, force_ref, inc_ref, rhs_ref, dual_ref,
     ndo_ref, ndm_ref, ninc_ref, *rest,
 ):
     payload_refs = rest[: windows - 1]
@@ -318,7 +312,6 @@
     downs = [slice(b.start - 1, b.stop - 1) for b in blocks]
     mine = slice(SUB + HALF, 2 * SUB + HALF)
     cuts = [slice(t * LANES, (t + 1) * LANES) for t in range(tiles)]
-    mix = [[coupling_gain * coupling_ref[v, u] for u in range(nvar)] for v in range(nvar)]
     low_wall = jnp.where((row == HALF) & (place_x == 0), 0.0, 1.0)
     high_wall = jnp.where((row == HALF - 1) & (place_x == spaces - 1), 0.0, 1.0)
 
@@ -347,22 +340,19 @@
         for odd in range(2):
             lev = 2 * i + odd
 
-            def spread(j, carry, odd=odd, lev=lev):
+            for j in range(steps):
+                far_ref = early_ref if j < steps // 2 else late_ref
                 for v in range(nvar):
                     for t in range(tiles):
                         halves = widened(
                             own_ref[j, v * levels + lev, :, cuts[t]].astype(jnp.float32),
                             near_ref[j, v * pairs + i, :, cuts[t]].astype(jnp.float32),
-                            far_ref[j, v * pairs + i, :, cuts[t]].astype(jnp.float32),
+                            far_ref[j % (steps // 2), v * pairs + i, :, cuts[t]].astype(jnp.float32),
                             odd,
                             even,
                         )
                         for b in range(2):
                             x_ref[odd, j, v, t, blocks[b], :] = halves[b]
-                return carry
-
-            lax.fori_loop(0, steps, spread, 0)
-
             for v in range(nvar):
                 for t in range(tiles):
                     s_ref[odd, 0, v, t, SUB : 3 * SUB, :] = first_ref[lev, v, t]
@@ -370,15 +360,11 @@
 
         def tangent(j, carry):
             now = lax.rem(j, 2)
-            seen = jnp.where(j < count_ref[0], 1.0, 0.0)
             for odd in range(2):
                 lev = 2 * i + odd
-                noise = jnp.full((SUB, LANES), noise_ref[0, j, lev])
-                share = seen / noise
                 for t in range(tiles):
-                    gap = innov_ref[0, j, lev, :, cuts[t]] - noise * dobs_ref[0, j, lev, :, cuts[t]]
-                    gap = gap - s_ref[odd, now, 0, t, mine, :]
-                    ndo_ref[0, j, lev, :, cuts[t]] = gap * share
+                    image = share_ref[lev, j] * s_ref[odd, now, 0, t, mine, :]
+                    ndo_ref[0, j, lev, :, cuts[t]] = obs_ref[lev, j, t] - image
                 for b in range(2):
                     here, up, down = blocks[b], ups[b], downs[b]
                     x = [[x_ref[odd, j, u, t, here, :] for t in range(tiles)] for u in range(nvar)]
@@ -398,7 +384,7 @@
                             fresh = fresh + cw[t] * s_ref[odd, now, v, t, down, :]
                             fresh = fresh + cn[t] * north[t] + cs[t] * south[t]
                             for u in range(nvar):
-                                fresh = fresh + mix[v][u] * xs[u][t]
+                                fresh = fresh + mix_ref[v, u] * xs[u][t]
                             s_ref[odd, 1 - now, v, t, here, :] = fresh
             return carry
 
@@ -430,9 +416,9 @@
                             fresh = keep * a[u][t] + ce[t] * a_ref[odd, now, u, t, up, :]
                             fresh = fresh + cw[t] * a_ref[odd, now, u, t, down, :]
                             fresh = fresh + north[t] + south[t]
-                            pull = mix[0][u] * a[0][t]
+                            pull = mix_ref[0, u] * a[0][t]
                             for v in range(1, nvar):
-                                pull = pull + mix[v][u] * a[v][t]
+                                pull = pull + mix_ref[v, u] * a[v][t]
                             fresh = fresh + x[u][t] * pull
                             if u == 0:
                                 fresh = fresh + force_ref[2 * i + odd, j, t, b * SUB : (b + 1) * SUB, :]
@@ -571,66 +557,64 @@
 
     payload = shape((pairs, nvar * tiles + 1, 2 * SUB, LANES), i16)
 
-    after = pl.pallas_call(
-        own_code_kernel,
-        out_shape=payload,
-        in_specs=[VMEM],
-        out_specs=VMEM,
+    counts = [nvar, nvar, steps]
+    half_tiles = sum(-(-(count * tiles + 1) // 2) for count in counts)
+    halves = shape((pairs, half_tiles, 2 * SUB, LANES), i16)
+    near, far, dual = pl.pallas_call(
+        half_code_kernel,
+        out_shape=[halves, halves, payload],
+        in_specs=[VMEM] * 3,
+        out_specs=[VMEM] * 3,
         compiler_params=params(),
-    )(dual_model)
-    after = moved(after, "window", -1)
-
-    def half_coded(counts, fields):
-        total = sum(-(-(count * tiles + 1) // 2) for count in counts)
-        halves = shape((pairs, total, 2 * SUB, LANES), i16)
-        near, far = pl.pallas_call(
-            half_code_kernel,
-            out_shape=[halves, halves],
-            in_specs=[VMEM] * len(fields),
-            out_specs=[VMEM] * 2,
-            compiler_params=params(),
-        )(*fields)
-        far = swapped(far, "space", 1)
-        return swapped(near, "space", 0), far
-
-    near, far = half_coded([nvar, steps], [increment, dual_obs])
-    after_near, after_far = half_coded([nvar], [after])
-
-    own, traj_far, totals = pl.pallas_call(
+    )(dual_model, increment, dual_obs)
+    far, near = swapped(far, "space", 1), swapped(near, "space", 0)
+
+    blocks_here = [arrived[d] for d in range(windows)]
+    around = shape((2,) + payload.shape[1:], i16)
+    *after, totals = pl.pallas_call(
+        lambda *refs: around_kernel(windows, nvar, levels, *refs),
+        out_shape=[around] * pairs + [shape((nvar * levels, rows, LANES), f32)],
+        in_specs=[VMEM] * (windows + 3),
+        out_specs=[VMEM] * (pairs + 1),
+        compiler_params=params(),
+    )(*blocks_here, dual, near, far)
+    after = [moved(piece, "window", -1) for piece in after]
+
+    half_steps = shape((steps // 2, nvar * pairs, rows, columns), bf16)
+    own, traj_near, traj_early, traj_late = pl.pallas_call(
         lambda *refs: assemble_kernel(windows, steps, nvar, levels, part, *refs),
         out_shape=[
             shape((steps, nvar * levels, rows, columns), bf16),
             shape((steps, nvar * pairs, rows, columns), bf16),
-            shape((nvar * levels, rows, LANES), f32),
+            half_steps,
+            half_steps,
         ],
         in_specs=[VMEM] * windows,
-        out_specs=[VMEM] * 3,
+        out_specs=[VMEM] * 4,
         scratch_shapes=[pltpu.VMEM((windows, nvar * levels, rows, wide), bf16)],
         compiler_params=params(),
-    )(*[arrived[d] for d in range(windows)])
-    traj_far = swapped(traj_far, "space", 1)
-    traj_near = pl.pallas_call(
-        near_kernel,
-        out_shape=shape((steps, nvar * pairs, rows, columns), bf16),
-        in_specs=[VMEM] + [ANY] * 3,
-        out_specs=VMEM,
+    )(*blocks_here)
+    traj_early = swapped(traj_early, "space", 1)
+    traj_late = swapped(traj_late, "space", 1)
+    traj_near = swapped(traj_near, "space", 0)
+
+    first, last, force, obs, share, mix = pl.pallas_call(
+        lambda *refs: prepare_kernel(steps, nvar, levels, tiles, *refs),
+        out_shape=[
+            *[shape((levels, n, tiles, 2 * SUB, LANES), f32) for n in (nvar, nvar, steps)],
+            shape((levels, steps, tiles, SUB, LANES), f32),
+            shape((levels, steps, SUB, LANES), f32),
+            shape((nvar, nvar, SUB, LANES), f32),
+        ],
+        in_specs=[SMEM] * 2 + [VMEM] * (6 + pairs),
+        out_specs=[VMEM] * 6,
         compiler_params=params(),
-    )(own, after, near, far)
-    traj_near = swapped(traj_near, "space", 0)
-
+    )(obs_count, obs_var, coupling, near, far, increment, dual_obs, innovation, *after)
     state = shape((nvar, levels, rows, columns), f32)
-    around = [shape((levels, n, tiles, 2 * SUB, LANES), f32) for n in (nvar, nvar, steps)]
-    first, last, force = pl.pallas_call(
-        lambda *refs: prepare_kernel(steps, nvar, levels, tiles, *refs),
-        out_shape=around,
-        in_specs=[SMEM] + [VMEM] * 7,
-        out_specs=[VMEM] * 3,
-        compiler_params=params(),
-    )(obs_count, after, after_near, after_far, near, far, increment, dual_obs)
     new_dual_obs, base_dual, base_inc, *payloads = pl.pallas_call(
         lambda *refs: model_kernel(windows, spaces, steps, nvar, levels, tiles, *refs),
         out_shape=[shape(dual_obs.shape, f32), state, state] + [payload] * (windows - 1),
-        in_specs=[SMEM] * 3 + [VMEM] * 12,
+        in_specs=[VMEM] * 14,
         out_specs=[VMEM] * (3 + windows - 1),
         scratch_shapes=[
             pltpu.VMEM((2, steps, nvar, tiles, 4 * SUB, LANES), f32),
@@ -640,8 +624,8 @@
         ],
         compiler_params=params(32),
     )(
-        coupling, obs_count, obs_var, totals, own, traj_near, traj_far,
-        first, last, force, increment, dual_obs, model_rhs, dual_model, innovation,
+        mix, share, obs, totals, own, traj_near, traj_early, traj_late,
+        first, last, force, increment, model_rhs, dual_model,
     )
     sent = {d: moved(payloads[d - 1], "window", d, around=True) for d in order}
 

time: 51.9 us -> 52.7 us (1.015)
  the two profiles are of different devices: /device:TPU:1 before, /device:TPU:0 now
where the time goes in v5:
time: 52.7 us; the launch traced here: 51.7 us
  waiting for transfers between devices  21.6 us (41%)
  starting transfers between devices  16.8 us (32%)
  Pallas kernels  10 us (19%)
  local copies, waits for them, and re-layouts  1.81 us (3%)
  between operations  1.51 us (3%)
    ppermute x8, waiting for transfers between devices, moved(): return lax.ppermute(block, axis, route)  21.6 us
    ppermute x8, starting transfers between devices, moved(): return lax.ppermute(block, axis, route)  14.7 us
    pallas_call x1, Pallas kernels, body(): pl.pallas_call(lambda *refs: model_kernel(windows, spaces, steps, nvar, l...  6.15 us
    ppermute x5, starting transfers between devices, swapped(): return lax.ppermute(block, axis, swaps(axis, first))  2.15 us
    unnamed x20, local copies, waits for them, and re-layouts  1.81 us
    pallas_call x1, Pallas kernels, body(): pl.pallas_call(lambda *refs: final_kernel(windows, nvar, levels, tiles, *...  1.13 us
  transfers between devices with their start and end apart: 13, of which 6 were waited for; matrix products, arithmetic and copies ran while one was open for 0% of the time, Pallas kernels for 5%

profile of v5, /device:TPU:0, one launch (start us, length us, event | category | flops | bytes accessed | tf_op | source)
XLA Modules:
  0.0 51.7 jit_solution(2088302252961683887)
XLA Ops:
  0.6 1.1 %copy-done = bf16[4,4,5,4,8,96]{5,4,3,2,1,0:T(8,128)(2,1)S(1)} copy-done((bf16[4,4,5,4,8,96]{5,4,3,2,1,0:T(8,128)(2,1)S(1)}, bf16[4,4,5,4,8,96]{5,4,3,2,1,0:T(8,128)(2,1)}, u32[]{:S(2)}) %copy-start) | copy-done | bytes 491544
  1.7 0.7 %copy-done.7 = f32[1,5,4]{1,2,0:T(4,128)S(1)} copy-done((f32[1,5,4]{1,2,0:T(4,128)S(1)}, f32[1,5,4]{1,2,0:T(4,128)}, u32[]{:S(2)}) %copy-start.7) | copy-done | bytes 104
  2.4 0.1 shard_map.123
  2.5 3.1 %collective-permute-start.2 = (bf16[21,8,384]{2,1,0:T(8,128)(2,1)S(1)}, bf16[21,8,384]{2,1,0:T(8,128)(2,1)S(1)}, u32[]{:S(2)}, u32[]{:S(2)}) collective-permute-start(bf16[21,8,384]{2,1,0:T(8,128)(2,1)S(1)} %shard_map.123), channel_id=1, source_target_pairs={{0,4},{4,8},{8,12},{12,0},{1,5},{5,9},{9,13},{13,1},{2,6},{6,10},{... | collective-permute-start | bytes 387080 | tf_op jit(solution)/shard_map/ppermute | solution.py:501
  5.6 0.1 shard_map.124
  5.7 0.0 copy-start.1
  5.7 2.7 %collective-permute-start.3 = (bf16[21,8,384]{2,1,0:T(8,128)(2,1)S(1)}, bf16[21,8,384]{2,1,0:T(8,128)(2,1)S(1)}, u32[]{:S(2)}, u32[]{:S(2)}) collective-permute-start(bf16[21,8,384]{2,1,0:T(8,128)(2,1)S(1)} %shard_map.124), channel_id=1, source_target_pairs={{0,8},{4,12},{8,0},{12,4},{1,9},{5,13},{9,1},{13,5},{2,10},{6,14},... | collective-permute-start | bytes 387080 | tf_op jit(solution)/shard_map/ppermute | solution.py:501
  8.4 0.1 shard_map.125
  8.5 1.4 %collective-permute-start.4 = (bf16[21,8,384]{2,1,0:T(8,128)(2,1)S(1)}, bf16[21,8,384]{2,1,0:T(8,128)(2,1)S(1)}, u32[]{:S(2)}, u32[]{:S(2)}) collective-permute-start(bf16[21,8,384]{2,1,0:T(8,128)(2,1)S(1)} %shard_map.125), channel_id=1, source_target_pairs={{0,12},{4,0},{8,4},{12,8},{1,13},{5,1},{9,5},{13,9},{2,14},{6,2},{... | collective-permute-start | bytes 387080 | tf_op jit(solution)/shard_map/ppermute | solution.py:501
  9.9 0.5 shard_map.121
  10.4 0.1 collective-permute-start
  10.5 0.7 %collective-permute-start.1 = (s16[2,23,16,128]{3,2,1,0:T(8,128)(2,1)S(1)}, s16[2,23,16,128]{3,2,1,0:T(8,128)(2,1)S(1)}, u32[]{:S(2)}, u32[]{:S(2)}) collective-permute-start(s16[2,23,16,128]{3,2,1,0:T(8,128)(2,1)S(1)} %get-tuple-element.28), channel_id=1, source_target_pairs={{1,2},{2,1},{5,6},{6,5},{9,10},{10,9},{13,14},{14,13},{17,18},{18,... | collective-permute-start | bytes 565256 | tf_op jit(solution)/shard_map/ppermute | solution.py:512
  11.2 0.1 shard_map.122.refs_0_
  11.3 0.7 %collective-permute-done.2.refs_1_ = bf16[21,8,384]{2,1,0:T(8,128)(2,1)S(1)} collective-permute-done((bf16[21,8,384]{2,1,0:T(8,128)(2,1)S(1)}, bf16[21,8,384]{2,1,0:T(8,128)(2,1)S(1)}, u32[]{:S(2)}, u32[]{:S(2)}) %collective-permute-start.2) | collective-permute-done | bytes 129056 | tf_op jit(solution)/shard_map/ppermute | solution.py:501
  12.0 4.7 %collective-permute-done.3.refs_2_ = bf16[21,8,384]{2,1,0:T(8,128)(2,1)S(1)} collective-permute-done((bf16[21,8,384]{2,1,0:T(8,128)(2,1)S(1)}, bf16[21,8,384]{2,1,0:T(8,128)(2,1)S(1)}, u32[]{:S(2)}, u32[]{:S(2)}) %collective-permute-start.3) | collective-permute-done | bytes 129056 | tf_op jit(solution)/shard_map/ppermute | solution.py:501
  16.7 0.7 %shard_map.128 = (bf16[4,20,8,384]{3,2,1,0:T(8,128)(2,1)S(1)}, bf16[4,10,8,384]{3,2,1,0:T(8,128)(2,1)S(1)}, bf16[2,10,8,384]{3,2,1,0:T(8,128)(2,1)S(1)}, bf16[2,10,8,384]{3,2,1,0:T(8,128)(2,1)S(1)}) custom-call(bf16[21,8,384]{2,1,0:T(8,128)(2,1)S(1)} %shard_map.122.refs_0_, bf16[21,8,384]{2,1,0:T(8,128)(2,1)S(1)} %collective-permute-done.2.refs_1_, ...), custom_call_target="tpu_custom_call" | custom-call | tf_op jit(solution)/shard_map/pallas_call | solution.py:584
  17.4 0.1 collective-permute-start.7
  17.5 0.3 shard_map.126
  17.8 1.3 %collective-permute-start.5 = (s16[2,16,16,128]{3,2,1,0:T(8,128)(2,1)S(1)}, s16[2,16,16,128]{3,2,1,0:T(8,128)(2,1)S(1)}, u32[]{:S(2)}, u32[]{:S(2)}) collective-permute-start(s16[2,16,16,128]{3,2,1,0:T(8,128)(2,1)S(1)} %get-tuple-element.30), channel_id=1, source_target_pairs={{4,0},{8,4},{12,8},{5,1},{9,5},{13,9},{6,2},{10,6},{14,10},{7,3},{... | collective-permute-start | bytes 393224 | tf_op jit(solution)/shard_map/ppermute | solution.py:501
  19.1 1.3 %collective-permute-start.6 = (s16[2,16,16,128]{3,2,1,0:T(8,128)(2,1)S(1)}, s16[2,16,16,128]{3,2,1,0:T(8,128)(2,1)S(1)}, u32[]{:S(2)}, u32[]{:S(2)}) collective-permute-start(s16[2,16,16,128]{3,2,1,0:T(8,128)(2,1)S(1)} %get-tuple-element.31), channel_id=1, source_target_pairs={{4,0},{8,4},{12,8},{5,1},{9,5},{13,9},{6,2},{10,6},{14,10},{7,3},{... | collective-permute-start | bytes 393224 | tf_op jit(solution)/shard_map/ppermute | solution.py:501
  20.4 0.7 %collective-permute-start.8 = (bf16[2,10,8,384]{3,2,1,0:T(8,128)(2,1)S(1)}, bf16[2,10,8,384]{3,2,1,0:T(8,128)(2,1)S(1)}, u32[]{:S(2)}, u32[]{:S(2)}) collective-permute-start(bf16[2,10,8,384]{3,2,1,0:T(8,128)(2,1)S(1)} %get-tuple-element.38), channel_id=1, source_target_pairs={{1,2},{2,1},{5,6},{6,5},{9,10},{10,9},{13,14},{14,13},{17,18},{18,... | collective-permute-start | bytes 368648 | tf_op jit(solution)/shard_map/ppermute | solution.py:512
  21.1 0.7 %collective-permute-start.9 = (bf16[2,10,8,384]{3,2,1,0:T(8,128)(2,1)S(1)}, bf16[2,10,8,384]{3,2,1,0:T(8,128)(2,1)S(1)}, u32[]{:S(2)}, u32[]{:S(2)}) collective-permute-start(bf16[2,10,8,384]{3,2,1,0:T(8,128)(2,1)S(1)} %get-tuple-element.39), channel_id=1, source_target_pairs={{1,2},{2,1},{5,6},{6,5},{9,10},{10,9},{13,14},{14,13},{17,18},{18,... | collective-permute-start | bytes 368648 | tf_op jit(solution)/shard_map/ppermute | solution.py:512
  22.4 4.9 %collective-permute-done.5.refs_8_ = s16[2,16,16,128]{3,2,1,0:T(8,128)(2,1)S(1)} collective-permute-done((s16[2,16,16,128]{3,2,1,0:T(8,128)(2,1)S(1)}, s16[2,16,16,128]{3,2,1,0:T(8,128)(2,1)S(1)}, u32[]{:S(2)}, u32[]{:S(2)}) %collective-permute-start.5) | collective-permute-done | bytes 131104 | tf_op jit(solution)/shard_map/ppermute | solution.py:501
  27.3 2.6 %collective-permute-done.6.refs_9_ = s16[2,16,16,128]{3,2,1,0:T(8,128)(2,1)S(1)} collective-permute-done((s16[2,16,16,128]{3,2,1,0:T(8,128)(2,1)S(1)}, s16[2,16,16,128]{3,2,1,0:T(8,128)(2,1)S(1)}, u32[]{:S(2)}, u32[]{:S(2)}) %collective-permute-start.6) | collective-permute-done | bytes 131104 | tf_op jit(solution)/shard_map/ppermute | solution.py:501
  29.9 0.9 %shard_map.127 = (f32[4,5,3,16,128]{4,3,2,1,0:T(8,128)S(1)}, f32[4,5,3,16,128]{4,3,2,1,0:T(8,128)S(1)}, f32[4,4,3,16,128]{4,3,2,1,0:T(8,128)S(1)}, f32[4,4,3,8,1...) custom-call(s32[1]{0:T(128)S(6)} %copy.13.refs_0_, f32[1,4,4]{2,1,0:T(4,128)S(1)} %copy-done.9, ...), custom_call_target="tpu_custom_call" | custom-call | tf_op jit(solution)/shard_map/pallas_call | solution.py:601
  30.8 6.2 %shard_map.129 = (f32[1,4,4,8,384]{4,3,2,1,0:T(8,128)}, f32[5,4,8,384]{3,2,1,0:T(8,128)S(1)}, f32[5,4,8,384]{3,2,1,0:T(8,128)S(1)}, s16[2,16,16,128]{3,2,1,0:T(8...) custom-call(f32[5,5,8,128]{3,2,1,0:T(8,128)S(1)} %get-tuple-element.32.refs_0_, ...), custom_call_target="tpu_custom_call" | custom-call | tf_op jit(solution)/shard_map/pallas_call | solution.py:614
  36.9 1.7 %collective-permute-start.10 = (s16[2,16,16,128]{3,2,1,0:T(8,128)(2,1)S(1)}, s16[2,16,16,128]{3,2,1,0:T(8,128)(2,1)S(1)}, u32[]{:S(2)}, u32[]{:S(2)}) collective-permute-start(s16[2,16,16,128]{3,2,1,0:T(8,128)(2,1)S(1)} %get-tuple-element.43), channel_id=1, source_target_pairs={{0,4},{4,8},{8,12},{12,0},{1,5},{5,9},{9,13},{13,1},{2,6},{6,10},{... | collective-permute-start | bytes 393224 | tf_op jit(solution)/shard_map/ppermute | solution.py:501
  38.6 0.3 collective-permute-start.11
  38.9 2.9 %collective-permute-start.12 = (s16[2,16,16,128]{3,2,1,0:T(8,128)(2,1)S(1)}, s16[2,16,16,128]{3,2,1,0:T(8,128)(2,1)S(1)}, u32[]{:S(2)}, u32[]{:S(2)}) collective-permute-start(s16[2,16,16,128]{3,2,1,0:T(8,128)(2,1)S(1)} %get-tuple-element.45), channel_id=1, source_target_pairs={{0,12},{4,0},{8,4},{12,8},{1,13},{5,1},{9,5},{13,9},{2,14},{6,2},{... | collective-permute-start | bytes 393224 | tf_op jit(solution)/shard_map/ppermute | solution.py:501
  41.9 2.0 %collective-permute-done.10.refs_0_ = s16[2,16,16,128]{3,2,1,0:T(8,128)(2,1)S(1)} collective-permute-done((s16[2,16,16,128]{3,2,1,0:T(8,128)(2,1)S(1)}, s16[2,16,16,128]{3,2,1,0:T(8,128)(2,1)S(1)}, u32[]{:S(2)}, u32[]{:S(2)}) %collective-permute-start.10) | collective-permute-done | bytes 131104 | tf_op jit(solution)/shard_map/ppermute | solution.py:501
  43.8 6.8 %collective-permute-done.11.refs_1_ = s16[2,16,16,128]{3,2,1,0:T(8,128)(2,1)S(1)} collective-permute-done((s16[2,16,16,128]{3,2,1,0:T(8,128)(2,1)S(1)}, s16[2,16,16,128]{3,2,1,0:T(8,128)(2,1)S(1)}, u32[]{:S(2)}, u32[]{:S(2)}) %collective-permute-start.11) | collective-permute-done | bytes 131104 | tf_op jit(solution)/shard_map/ppermute | solution.py:501
  50.6 1.1 %shard_map.130 = (f32[1,5,4,8,384]{4,3,2,1,0:T(8,128)}, f32[1,5,4,8,384]{4,3,2,1,0:T(8,128)}) custom-call(s16[2,16,16,128]{3,2,1,0:T(8,128)(2,1)S(1)} %collective-permute-done.10.refs_0_, s16[2,16,16,128]{3,2,1,0:T(8,128)(2,1)S(1)} %collective-permute-done.11.refs_1_, s16[2,16,16,128]{3,2,1,0:T(8,128)(2,1)S(1)} %collective-permute-done.12.refs_2_, ...), custom_call_target="tpu_custom_call" | custom-call | tf_op jit(solution)/shard_map/pallas_call | solution.py:632
  (24 shorter events, 0.1 us)
Async XLA Ops:
  0.6 1.1 %copy-start = (bf16[4,4,5,4,8,96]{5,4,3,2,1,0:T(8,128)(2,1)S(1)}, bf16[4,4,5,4,8,96]{5,4,3,2,1,0:T(8,128)(2,1)}, u32[]{:S(2)}) copy-start(bf16[4,4,5,4,8,96]{5,4,3,2,1,0:T(8,128)(2,1)} %refs_1_.10) | copy-start | bytes 1474564
  1.7 0.7 %copy-start.7 = (f32[1,5,4]{1,2,0:T(4,128)S(1)}, f32[1,5,4]{1,2,0:T(4,128)}, u32[]{:S(2)}) copy-start(f32[1,5,4]{1,2,0:T(4,128)} %param.17) | copy-start | bytes 244
  2.5 9.5 %collective-permute-start.2 = (bf16[21,8,384]{2,1,0:T(8,128)(2,1)S(1)}, bf16[21,8,384]{2,1,0:T(8,128)(2,1)S(1)}, u32[]{:S(2)}, u32[]{:S(2)}) collective-permute-start(bf16[21,8,384]{2,1,0:T(8,128)(2,1)S(1)} %shard_map.123), channel_id=1, source_target_pairs={{0,4},{4,8},{8,12},{12,0},{1,5},{5,9},{9,13},{13,1},{2,6},{6,10},{... | collective-permute-start | bytes 387080 | tf_op jit(solution)/shard_map/ppermute | solution.py:501
  5.6 4.3 %copy-start.2 = (f32[1,5,4,8,384]{4,3,2,1,0:T(8,128)S(1)}, f32[1,5,4,8,384]{4,3,2,1,0:T(8,128)}, u32[]{:S(2)}) copy-start(f32[1,5,4,8,384]{4,3,2,1,0:T(8,128)} %refs_11_.1) | copy-start | bytes 737284
  5.6 4.3 %copy-start.3 = (f32[1,5,4,8,384]{4,3,2,1,0:T(8,128)S(1)}, f32[1,5,4,8,384]{4,3,2,1,0:T(8,128)}, u32[]{:S(2)}) copy-start(f32[1,5,4,8,384]{4,3,2,1,0:T(8,128)} %refs_13_.1) | copy-start | bytes 737284
  5.6 4.3 %copy-start.4 = (f32[1,4,4,8,384]{4,3,2,1,0:T(8,128)S(1)}, f32[1,4,4,8,384]{4,3,2,1,0:T(8,128)}, u32[]{:S(2)}) copy-start(f32[1,4,4,8,384]{4,3,2,1,0:T(8,128)} %refs_6_.1) | copy-start | bytes 589828
  5.7 5.5 %copy-start.1 = (bf16[4,4,5,4,8,96]{5,4,3,2,1,0:T(8,128)(2,1)S(1)}, bf16[4,4,5,4,8,96]{5,4,3,2,1,0:T(8,128)(2,1)}, u32[]{:S(2)}) copy-start(bf16[4,4,5,4,8,96]{5,4,3,2,1,0:T(8,128)(2,1)} %refs_1_.10) | copy-start | bytes 1474564
  5.7 11.0 %collective-permute-start.3 = (bf16[21,8,384]{2,1,0:T(8,128)(2,1)S(1)}, bf16[21,8,384]{2,1,0:T(8,128)(2,1)S(1)}, u32[]{:S(2)}, u32[]{:S(2)}) collective-permute-start(bf16[21,8,384]{2,1,0:T(8,128)(2,1)S(1)} %shard_map.124), channel_id=1, source_target_pairs={{0,8},{4,12},{8,0},{12,4},{1,9},{5,13},{9,1},{13,5},{2,10},{6,14},... | collective-permute-start | bytes 387080 | tf_op jit(solution)/shard_map/ppermute | solution.py:501
  8.5 8.2 %collective-permute-start.4 = (bf16[21,8,384]{2,1,0:T(8,128)(2,1)S(1)}, bf16[21,8,384]{2,1,0:T(8,128)(2,1)S(1)}, u32[]{:S(2)}, u32[]{:S(2)}) collective-permute-start(bf16[21,8,384]{2,1,0:T(8,128)(2,1)S(1)} %shard_map.125), channel_id=1, source_target_pairs={{0,12},{4,0},{8,4},{12,8},{1,13},{5,1},{9,5},{13,9},{2,14},{6,2},{... | collective-permute-start | bytes 387080 | tf_op jit(solution)/shard_map/ppermute | solution.py:501
  10.4 7.0 %collective-permute-start = (s16[2,23,16,128]{3,2,1,0:T(8,128)(2,1)S(1)}, s16[2,23,16,128]{3,2,1,0:T(8,128)(2,1)S(1)}, u32[]{:S(2)}, u32[]{:S(2)}) collective-permute-start(s16[2,23,16,128]{3,2,1,0:T(8,128)(2,1)S(1)} %get-tuple-element.27), channel_id=1, source_target_pairs={{0,1},{1,0},{2,3},{3,2},{4,5},{5,4},{6,7},{7,6},{8,9},{9,8},{10,11... | collective-permute-start | bytes 565256 | tf_op jit(solution)/shard_map/ppermute | solution.py:512
  10.5 7.0 %collective-permute-start.1 = (s16[2,23,16,128]{3,2,1,0:T(8,128)(2,1)S(1)}, s16[2,23,16,128]{3,2,1,0:T(8,128)(2,1)S(1)}, u32[]{:S(2)}, u32[]{:S(2)}) collective-permute-start(s16[2,23,16,128]{3,2,1,0:T(8,128)(2,1)S(1)} %get-tuple-element.28), channel_id=1, source_target_pairs={{1,2},{2,1},{5,6},{6,5},{9,10},{10,9},{13,14},{14,13},{17,18},{18,... | collective-permute-start | bytes 565256 | tf_op jit(solution)/shard_map/ppermute | solution.py:512
  17.4 13.4 %collective-permute-start.7 = (bf16[4,10,8,384]{3,2,1,0:T(8,128)(2,1)S(1)}, bf16[4,10,8,384]{3,2,1,0:T(8,128)(2,1)S(1)}, u32[]{:S(2)}, u32[]{:S(2)}) collective-permute-start(bf16[4,10,8,384]{3,2,1,0:T(8,128)(2,1)S(1)} %get-tuple-element.37), channel_id=1, source_target_pairs={{0,1},{1,0},{2,3},{3,2},{4,5},{5,4},{6,7},{7,6},{8,9},{9,8},{10,11... | collective-permute-start | bytes 737288 | tf_op jit(solution)/shard_map/ppermute | solution.py:512
  17.5 12.4 %copy-start.6 = (f32[1,4,4,8,384]{4,3,2,1,0:T(8,128)S(1)}, f32[1,4,4,8,384]{4,3,2,1,0:T(8,128)}, u32[]{:S(2)}) copy-start(f32[1,4,4,8,384]{4,3,2,1,0:T(8,128)} %refs_7_.1) | copy-start | bytes 589828
  17.8 12.1 %copy-start.8 = (f32[5,5]{1,0:T(8,128)S(1)}, f32[5,5]{1,0:T(8,128)}, u32[]{:S(2)}) copy-start(f32[5,5]{1,0:T(8,128)} %refs_2_.3) | copy-start | bytes 304
  17.8 9.5 %collective-permute-start.5 = (s16[2,16,16,128]{3,2,1,0:T(8,128)(2,1)S(1)}, s16[2,16,16,128]{3,2,1,0:T(8,128)(2,1)S(1)}, u32[]{:S(2)}, u32[]{:S(2)}) collective-permute-start(s16[2,16,16,128]{3,2,1,0:T(8,128)(2,1)S(1)} %get-tuple-element.30), channel_id=1, source_target_pairs={{4,0},{8,4},{12,8},{5,1},{9,5},{13,9},{6,2},{10,6},{14,10},{7,3},{... | collective-permute-start | bytes 393224 | tf_op jit(solution)/shard_map/ppermute | solution.py:501
  19.1 10.8 %collective-permute-start.6 = (s16[2,16,16,128]{3,2,1,0:T(8,128)(2,1)S(1)}, s16[2,16,16,128]{3,2,1,0:T(8,128)(2,1)S(1)}, u32[]{:S(2)}, u32[]{:S(2)}) collective-permute-start(s16[2,16,16,128]{3,2,1,0:T(8,128)(2,1)S(1)} %get-tuple-element.31), channel_id=1, source_target_pairs={{4,0},{8,4},{12,8},{5,1},{9,5},{13,9},{6,2},{10,6},{14,10},{7,3},{... | collective-permute-start | bytes 393224 | tf_op jit(solution)/shard_map/ppermute | solution.py:501
  20.4 9.5 %copy-start.9 = (f32[1,4,4]{2,1,0:T(4,128)S(1)}, f32[1,4,4]{2,1,0:T(4,128)}, u32[]{:S(2)}) copy-start(f32[1,4,4]{2,1,0:T(4,128)} %refs_1_.11) | copy-start | bytes 196
  20.4 10.3 %collective-permute-start.8 = (bf16[2,10,8,384]{3,2,1,0:T(8,128)(2,1)S(1)}, bf16[2,10,8,384]{3,2,1,0:T(8,128)(2,1)S(1)}, u32[]{:S(2)}, u32[]{:S(2)}) collective-permute-start(bf16[2,10,8,384]{3,2,1,0:T(8,128)(2,1)S(1)} %get-tuple-element.38), channel_id=1, source_target_pairs={{1,2},{2,1},{5,6},{6,5},{9,10},{10,9},{13,14},{14,13},{17,18},{18,... | collective-permute-start | bytes 368648 | tf_op jit(solution)/shard_map/ppermute | solution.py:512
  21.1 9.7 %collective-permute-start.9 = (bf16[2,10,8,384]{3,2,1,0:T(8,128)(2,1)S(1)}, bf16[2,10,8,384]{3,2,1,0:T(8,128)(2,1)S(1)}, u32[]{:S(2)}, u32[]{:S(2)}) collective-permute-start(bf16[2,10,8,384]{3,2,1,0:T(8,128)(2,1)S(1)} %get-tuple-element.39), channel_id=1, source_target_pairs={{1,2},{2,1},{5,6},{6,5},{9,10},{10,9},{13,14},{14,13},{17,18},{18,... | collective-permute-start | bytes 368648 | tf_op jit(solution)/shard_map/ppermute | solution.py:512
  22.4 8.4 %copy-start.5 = (f32[1,5,4,8,384]{4,3,2,1,0:T(8,128)S(1)}, f32[1,5,4,8,384]{4,3,2,1,0:T(8,128)}, u32[]{:S(2)}) copy-start(f32[1,5,4,8,384]{4,3,2,1,0:T(8,128)} %refs_12_.1) | copy-start | bytes 737284
  36.9 6.9 %collective-permute-start.10 = (s16[2,16,16,128]{3,2,1,0:T(8,128)(2,1)S(1)}, s16[2,16,16,128]{3,2,1,0:T(8,128)(2,1)S(1)}, u32[]{:S(2)}, u32[]{:S(2)}) collective-permute-start(s16[2,16,16,128]{3,2,1,0:T(8,128)(2,1)S(1)} %get-tuple-element.43), channel_id=1, source_target_pairs={{0,4},{4,8},{8,12},{12,0},{1,5},{5,9},{9,13},{13,1},{2,6},{6,10},{... | collective-permute-start | bytes 393224 | tf_op jit(solution)/shard_map/ppermute | solution.py:501
  38.6 12.0 %collective-permute-start.11 = (s16[2,16,16,128]{3,2,1,0:T(8,128)(2,1)S(1)}, s16[2,16,16,128]{3,2,1,0:T(8,128)(2,1)S(1)}, u32[]{:S(2)}, u32[]{:S(2)}) collective-permute-start(s16[2,16,16,128]{3,2,1,0:T(8,128)(2,1)S(1)} %get-tuple-element.44), channel_id=1, source_target_pairs={{0,8},{4,12},{8,0},{12,4},{1,9},{5,13},{9,1},{13,5},{2,10},{6,14},... | collective-permute-start | bytes 393224 | tf_op jit(solution)/shard_map/ppermute | solution.py:501
  38.9 11.7 %collective-permute-start.12 = (s16[2,16,16,128]{3,2,1,0:T(8,128)(2,1)S(1)}, s16[2,16,16,128]{3,2,1,0:T(8,128)(2,1)S(1)}, u32[]{:S(2)}, u32[]{:S(2)}) collective-permute-start(s16[2,16,16,128]{3,2,1,0:T(8,128)(2,1)S(1)} %get-tuple-element.45), channel_id=1, source_target_pairs={{0,12},{4,0},{8,4},{12,8},{1,13},{5,1},{9,5},{13,9},{2,14},{6,2},{... | collective-permute-start | bytes 393224 | tf_op jit(solution)/shard_map/ppermute | solution.py:501

commit v6 on v5

--- a/solution.py
+++ b/solution.py
@@ -91,8 +91,7 @@
         scales = jnp.where(lane == v, power, scales)
         gain = CODE_MAX * jnp.exp2(-power)
         for value in row:
-            scaled = jnp.clip(value * gain, -CODE_MAX, CODE_MAX)
-            out.append((scaled + ROUNDER) - ROUNDER)
+            out.append((value * gain + ROUNDER) - ROUNDER)
     return out, scales
 
 
@@ -104,13 +103,10 @@
     return value.astype(jnp.int32).astype(jnp.float32)
 
 
-def pack_kernel(distances, windows, steps, nvar, levels, part, var_ref, traj_ref, *rest):
-    outs, wide_ref = rest[:-1], rest[-1]
+def pack_kernel(distances, windows, steps, nvar, levels, part, var_ref, traj_ref, *outs):
     me = lax.axis_index("window")
     lane = lane_index()
-    wide_ref[...] = jnp.zeros((SUB, LANES), jnp.float32)
-    wide_ref[:levels, :nvar] = var_ref[0]
-    variance = wide_ref[...]
+    variance = var_ref[...]
     high = variance.astype(jnp.bfloat16).astype(jnp.float32)
     middle = (variance - high).astype(jnp.bfloat16).astype(jnp.float32)
     low = variance - high - middle
@@ -118,7 +114,7 @@
     split = split.astype(jnp.bfloat16)
 
     for n, d in enumerate(distances):
-        outs[n][nvar * levels, :, :LANES] = split
+        outs[n][outs[n].shape[0] - 1] = split
         target = lax.rem(me + d, windows)
 
         def variable(v, carry, n=n, target=target):
@@ -127,8 +123,9 @@
                     tiled(traj_ref[target, j, v, lev].astype(jnp.float32)) for j in range(steps)
                 ]
                 parts = [(j, pieces[j], 0, part, j * part) for j in range(steps)]
-                wide = jnp.concatenate(place(parts, {}, lane), 1)
-                outs[n][v * levels + lev] = wide.astype(jnp.bfloat16)
+                placed = place(parts, {}, lane)
+                for t, value in enumerate(placed):
+                    outs[n][(v * levels + lev) * len(placed) + t] = value.astype(jnp.bfloat16)
             return carry
 
         lax.fori_loop(0, nvar, variable, 0, unroll=len(distances) == 1)
@@ -138,10 +135,10 @@
     return lax.rem(lax.axis_index("space"), 2) == 0
 
 
-def level_codes(ref, lev):
+def level_codes(ref, lev, first=0):
     planes = [
         [ref[0, v, lev, :, t : t + LANES] for t in range(0, ref.shape[-1], LANES)]
-        for v in range(ref.shape[1])
+        for v in range(first, ref.shape[1])
     ]
     values, scales = row_codes(planes)
     return values + [scales]
@@ -154,7 +151,8 @@
     def pair(i, carry):
         near, far = [], []
         for k, ref in enumerate(sources):
-            coded = [level_codes(ref, 2 * i + odd) for odd in range(2)]
+            skip = int(k == len(sources) - 1)
+            coded = [level_codes(ref, 2 * i + odd, skip) for odd in range(2)]
             for n, (first, second) in enumerate(zip(*coded)):
                 if k == 0:
                     own_ref[i, n] = shorts(jnp.concatenate([first, second], 0))
@@ -184,7 +182,7 @@
     even = even_place()
     total = jnp.zeros((SUB, LANES), jnp.float32)
     for d in range(windows):
-        split = pieces[d][nvar * levels, :, :LANES].astype(jnp.float32)
+        split = pieces[d][pieces[d].shape[0] - 1].astype(jnp.float32)
         here = split + pltpu.roll(split, HALF, 0) + pltpu.roll(split, LANES // 2, 1)
         total = total + jnp.where(lax.rem(me - d + windows, windows) <= me, here, 0.0)
     for v in range(nvar):
@@ -208,54 +206,86 @@
     ]
 
 
+def is_quarter(j, v, steps):
+    return 0 < j < steps - 1 and not (v == 0 and j + 1 > HALF // 2)
+
+
+def far_base(steps, nvar, levels):
+    base, total = {}, 0
+    for j in range(steps):
+        for v in range(nvar):
+            base[j, v] = total
+            total += levels // (4 if is_quarter(j, v, steps) else 2)
+    return base, total
+
+
+def joined_quarters(four):
+    slot = row_index() // 2
+    last, start = pltpu.roll(four[0], 2, 0), four[0]
+    for n in range(1, 4):
+        last = jnp.where(slot == n, pltpu.roll(four[n], (2 * n + 2) % SUB, 0), last)
+        start = jnp.where(slot == n, pltpu.roll(four[n], 2 * n, 0), start)
+    return last, start
+
+
 def assemble_kernel(windows, steps, nvar, levels, part, *refs):
     pieces = refs[:windows]
-    own_ref, near_ref, early_ref, late_ref, stack_ref = refs[windows:]
+    own_ref, early_ref, late_ref, far_ref, stack_ref = refs[windows:]
     me = lax.axis_index("window")
     even = even_place()
     lane = lane_index()
+    count = stack_ref.shape[1]
+    packed_tiles = count // (nvar * levels)
     for d in range(windows):
         source = lax.rem(me - d + windows, windows)
-        stack_ref[source] = pieces[d][: nvar * levels]
+        stack_ref[source] = pieces[d][:count]
 
     pairs = levels // 2
-
-    def pair(n):
-        both = []
-        for odd in range(2):
-            plane = 2 * n + odd
-            sources = [tiled(stack_ref[w, plane].astype(jnp.float32)) for w in range(windows)]
+    base, _ = far_base(steps, nvar, levels)
+
+    def variable(v):
+        built = {}
+        for lev in range(levels):
+            plane = v * levels + lev
+            sources = [
+                [
+                    stack_ref[w, plane * packed_tiles + t].astype(jnp.float32)
+                    for t in range(packed_tiles)
+                ]
+                for w in range(windows)
+            ]
             rolled = {}
-            built = []
             for j in range(steps):
                 parts = [(w, sources[w], j * part, part, w * part) for w in range(windows)]
-                built.append(place(parts, rolled, lane))
-                own_ref[j, plane] = jnp.concatenate(built[j], 1).astype(jnp.bfloat16)
-            both.append(built)
+                built[j, lev] = place(parts, rolled, lane)
+                own_ref[j, plane] = jnp.concatenate(built[j, lev], 1).astype(jnp.bfloat16)
         for j in range(steps):
-            halves = [joined_halves(a, b) for a, b in zip(both[0][j], both[1][j])]
-            last, start = (jnp.concatenate([h[k] for h in halves], 1) for k in range(2))
-            near_ref[j, n] = jnp.where(even, last, start).astype(jnp.bfloat16)
-            far = jnp.where(even, start, last).astype(jnp.bfloat16)
-            if j < steps // 2:
-                early_ref[j, n] = far
-            else:
-                late_ref[j - steps // 2, n] = far
-
-    def variable(v, carry):
-        for i in range(pairs):
-            pair(v * pairs + i)
-        return carry
-
-    lax.fori_loop(0, nvar, variable, 0)
-
-
-def prepare_kernel(
+            for i in range(pairs):
+                halves = [joined_halves(a, b) for a, b in zip(built[j, 2 * i], built[j, 2 * i + 1])]
+                last, start = (jnp.concatenate([h[k] for h in halves], 1) for k in range(2))
+                near = jnp.where(even, last, start).astype(jnp.bfloat16)
+                if j < steps // 2:
+                    early_ref[j, v * pairs + i] = near
+                else:
+                    late_ref[j - steps // 2, v * pairs + i] = near
+                if not is_quarter(j, v, steps):
+                    far_ref[base[j, v] + i] = jnp.where(even, start, last).astype(jnp.bfloat16)
+            if is_quarter(j, v, steps):
+                for q in range(levels // 4):
+                    four = zip(*[built[j, 4 * q + n] for n in range(4)])
+                    ends = [joined_quarters(tiles) for tiles in four]
+                    last, start = (jnp.concatenate([e[k] for e in ends], 1) for k in range(2))
+                    far_ref[base[j, v] + q] = jnp.where(even, start, last).astype(jnp.bfloat16)
+
+    for v in range(nvar):
+        variable(v)
+
+
+def prepare_tangent_kernel(
     steps, nvar, levels, tiles,
-    count_ref, noise_ref, coupling_ref, near_ref, far_ref, inc_ref, dobs_ref, innov_ref, *refs,
+    count_ref, noise_ref, coupling_ref, near_ref, far_ref, inc_ref, dobs_ref, innov_ref,
+    first_ref, obs_ref, share_ref, mix_ref,
 ):
-    after_refs = refs[: levels // 2]
-    first_ref, last_ref, force_ref, obs_ref, share_ref, mix_ref = refs[levels // 2 :]
     even = even_place()
     blocks = [slice(0, SUB), slice(SUB, 2 * SUB)]
     cuts = [slice(t * LANES, (t + 1) * LANES) for t in range(tiles)]
@@ -263,20 +293,45 @@
         for u in range(nvar):
             one = coupling_gain * coupling_ref[v : v + 1, u : u + 1]
             mix_ref[v, u] = jnp.broadcast_to(one, (SUB, LANES))
-    seen = [jnp.where(j < count_ref[0], 1.0, 0.0) for j in range(steps)]
     offset = -(-(nvar * tiles + 1) // 2) * 2
-    for i, after_ref in enumerate(after_refs):
+    for i in range(levels // 2):
         fields = [decoded(ref, i, offset, nvar, tiles) for ref in (near_ref, far_ref)]
-        forces = [decoded(ref, i, 2 * offset, steps, tiles) for ref in (near_ref, far_ref)]
         for odd in range(2):
             lev = 2 * i + odd
-            scales = jnp.exp2(floats(after_ref[odd, nvar * tiles])) * (-1.0 / CODE_MAX)
             for t in range(tiles):
                 for v in range(nvar):
                     near, far = (side[v][t] for side in fields)
                     halves = widened(inc_ref[0, v, lev, :, cuts[t]], near, far, odd, even)
                     for b in range(2):
                         first_ref[lev, v, t, blocks[b], :] = halves[b]
+            for j in range(steps):
+                noise = jnp.full((SUB, LANES), noise_ref[0, j, lev])
+                share = jnp.where(j < count_ref[0], 1.0, 0.0) / noise
+                share_ref[lev, j] = share
+                for t in range(tiles):
+                    gap = innov_ref[0, j, lev, :, cuts[t]] - noise * dobs_ref[0, j, lev, :, cuts[t]]
+                    obs_ref[lev, j, t] = gap * share
+
+
+def prepare_adjoint_kernel(
+    steps, nvar, levels, tiles, count_ref, near_ref, far_ref, dobs_ref, *refs
+):
+    after_refs, (last_ref, force_ref) = refs[: levels // 2], refs[levels // 2 + 1 :]
+    even = even_place()
+    blocks = [slice(0, SUB), slice(SUB, 2 * SUB)]
+    cuts = [slice(t * LANES, (t + 1) * LANES) for t in range(tiles)]
+    seen = [jnp.where(j < count_ref[0], 1.0, 0.0) for j in range(steps)]
+    offset = -(-(nvar * tiles + 1) // 2) * 2
+    none = [[jnp.zeros((SUB, LANES), jnp.float32)] * tiles]
+    for i, after_ref in enumerate(after_refs):
+        forces = [
+            none + decoded(ref, i, 2 * offset, steps - 1, tiles) for ref in (near_ref, far_ref)
+        ]
+        for odd in range(2):
+            lev = 2 * i + odd
+            scales = jnp.exp2(floats(after_ref[odd, nvar * tiles])) * (-1.0 / CODE_MAX)
+            for t in range(tiles):
+                for v in range(nvar):
                     value = floats(after_ref[odd, v * tiles + t])
                     last_ref[lev, v, t] = value * scales[:, v : v + 1]
                 for j in range(steps):
@@ -284,101 +339,112 @@
                     halves = widened(dobs_ref[0, j, lev, :, cuts[t]], near, far, odd, even)
                     for b in range(2):
                         force_ref[lev, j, t, blocks[b], :] = seen[j] * halves[b]
-            for j in range(steps):
-                noise = jnp.full((SUB, LANES), noise_ref[0, j, lev])
-                share = seen[j] / noise
-                share_ref[lev, j] = share
-                for t in range(tiles):
-                    gap = innov_ref[0, j, lev, :, cuts[t]] - noise * dobs_ref[0, j, lev, :, cuts[t]]
-                    obs_ref[lev, j, t] = gap * share
-
-
-def model_kernel(
-    windows, spaces, steps, nvar, levels, tiles,
-    mix_ref, share_ref, obs_ref, total_ref, own_ref, near_ref, early_ref, late_ref,
-    first_ref, last_ref, force_ref, inc_ref, rhs_ref, dual_ref,
-    ndo_ref, ndm_ref, ninc_ref, *rest,
-):
-    payload_refs = rest[: windows - 1]
-    x_ref, s_ref, a_ref, q_ref = rest[windows - 1 :]
-    me = lax.axis_index("window")
-    place_x = lax.axis_index("space")
-    even = even_place()
-    lane, row = lane_index(), row_index()
-    pairs = levels // 2
-    zero = jnp.zeros((SUB, LANES), jnp.float32)
-    blocks = [slice(SUB, 2 * SUB), slice(2 * SUB, 3 * SUB)]
-    ups = [slice(b.start + 1, b.stop + 1) for b in blocks]
-    downs = [slice(b.start - 1, b.stop - 1) for b in blocks]
-    mine = slice(SUB + HALF, 2 * SUB + HALF)
-    cuts = [slice(t * LANES, (t + 1) * LANES) for t in range(tiles)]
-    low_wall = jnp.where((row == HALF) & (place_x == 0), 0.0, 1.0)
-    high_wall = jnp.where((row == HALF - 1) & (place_x == spaces - 1), 0.0, 1.0)
-
-    def from_north(line):
-        turned = [pltpu.roll(value, LANES - 1, 1) for value in line]
-        return [
-            jnp.where(lane < LANES - 1, turned[t], turned[(t + 1) % tiles]) for t in range(tiles)
-        ]
-
-    def from_south(line):
-        turned = [pltpu.roll(value, 1, 1) for value in line]
-        return [jnp.where(lane > 0, turned[t], turned[t - 1]) for t in range(tiles)]
-
-    def masked_last(line):
-        return line[:-1] + [jnp.where(lane < LANES - 1, line[-1], 0.0)]
-
-    def masked_first(line):
-        return [jnp.where(lane > 0, line[0], 0.0)] + line[1:]
+
+
+def from_north(line, lane):
+    turned = [pltpu.roll(value, LANES - 1, 1) for value in line] * 2
+    return [jnp.where(lane < LANES - 1, turned[t], turned[t + 1]) for t in range(len(line))]
+
+
+def from_south(line, lane):
+    turned = [pltpu.roll(value, 1, 1) for value in line]
+    return [jnp.where(lane > 0, turned[t], turned[t - 1]) for t in range(len(line))]
+
+
+def masked_last(line, lane):
+    return line[:-1] + [jnp.where(lane < LANES - 1, line[-1], 0.0)]
+
+
+def masked_first(line, lane):
+    return [jnp.where(lane > 0, line[0], 0.0)] + line[1:]
+
+
+def walls(spaces):
+    row, place_x = row_index(), lax.axis_index("space")
+    low = jnp.where((row == HALF) & (place_x == 0), 0.0, 1.0)
+    high = jnp.where((row == HALF - 1) & (place_x == spaces - 1), 0.0, 1.0)
 
     def walled(block, east, west):
         if block == 0:
-            return east, [low_wall * value for value in west]
-        return [high_wall * value for value in east], west
+            return east, [low * value for value in west]
+        return [high * value for value in east], west
+
+    return walled
+
+
+BLOCKS = [slice(SUB, 2 * SUB), slice(2 * SUB, 3 * SUB)]
+UPS = [slice(b.start + 1, b.stop + 1) for b in BLOCKS]
+DOWNS = [slice(b.start - 1, b.stop - 1) for b in BLOCKS]
+MINE = slice(SUB + HALF, 2 * SUB + HALF)
+
+
+def tangent_kernel(
+    spaces, steps, nvar, levels, tiles,
+    mix_ref, share_ref, obs_ref, own_ref, early_ref, late_ref, far_ref, first_ref,
+    ndo_ref, ends_ref, x_ref, s_ref,
+):
+    lane, row = lane_index(), row_index()
+    even = even_place()
+    top = row < HALF
+    walled = walls(spaces)
+    pairs = levels // 2
+    cuts = [slice(t * LANES, (t + 1) * LANES) for t in range(tiles)]
+    base, _ = far_base(steps, nvar, levels)
+
+    for lev in range(levels):
+        i, odd = lev // 2, lev % 2
+        for j in range(steps):
+            near_ref = early_ref if j < steps // 2 else late_ref
+            for v in range(nvar):
+                for t in range(tiles):
+                    own = own_ref[j, v * levels + lev, :, cuts[t]].astype(jnp.float32)
+                    near = near_ref[j % (steps // 2), v * pairs + i, :, cuts[t]].astype(jnp.float32)
+                    quarter = is_quarter(j, v, steps)
+                    far = far_ref[base[j, v] + lev // (4 if quarter else 2), :, cuts[t]]
+                    far = far.astype(jnp.float32)
+                    if quarter:
+                        slot = 2 * (lev % 4)
+                        low_far = pltpu.roll(far, (HALF - 2 - slot) % SUB, 0)
+                        high_far = pltpu.roll(far, (HALF - slot) % SUB, 0)
+                    else:
+                        low_far = pltpu.roll(far, HALF, 0) if odd else far
+                        high_far = far if odd else pltpu.roll(far, HALF, 0)
+                    low_near = pltpu.roll(near, HALF, 0) if odd else near
+                    high_near = near if odd else pltpu.roll(near, HALF, 0)
+                    turned = pltpu.roll(own, HALF, 0)
+                    low = jnp.where(even, low_far, low_near)
+                    high = jnp.where(even, high_near, high_far)
+                    x_ref[lev, j, v, t, :SUB, :] = jnp.where(top, low, turned)
+                    x_ref[lev, j, v, t, SUB:, :] = jnp.where(top, turned, high)
 
     def pair(i, outer):
         for odd in range(2):
-            lev = 2 * i + odd
-
-            for j in range(steps):
-                far_ref = early_ref if j < steps // 2 else late_ref
-                for v in range(nvar):
-                    for t in range(tiles):
-                        halves = widened(
-                            own_ref[j, v * levels + lev, :, cuts[t]].astype(jnp.float32),
-                            near_ref[j, v * pairs + i, :, cuts[t]].astype(jnp.float32),
-                            far_ref[j % (steps // 2), v * pairs + i, :, cuts[t]].astype(jnp.float32),
-                            odd,
-                            even,
-                        )
-                        for b in range(2):
-                            x_ref[odd, j, v, t, blocks[b], :] = halves[b]
             for v in range(nvar):
                 for t in range(tiles):
-                    s_ref[odd, 0, v, t, SUB : 3 * SUB, :] = first_ref[lev, v, t]
-                    a_ref[odd, 0, v, t, SUB : 3 * SUB, :] = last_ref[lev, v, t]
-
-        def tangent(j, carry):
+                    s_ref[odd, 0, v, t, SUB : 3 * SUB, :] = first_ref[2 * i + odd, v, t]
+
+        def step(j, carry):
             now = lax.rem(j, 2)
             for odd in range(2):
                 lev = 2 * i + odd
                 for t in range(tiles):
-                    image = share_ref[lev, j] * s_ref[odd, now, 0, t, mine, :]
+                    image = share_ref[lev, j] * s_ref[odd, now, 0, t, MINE, :]
                     ndo_ref[0, j, lev, :, cuts[t]] = obs_ref[lev, j, t] - image
                 for b in range(2):
-                    here, up, down = blocks[b], ups[b], downs[b]
-                    x = [[x_ref[odd, j, u, t, here, :] for t in range(tiles)] for u in range(nvar)]
+                    part = slice(b * SUB, (b + 1) * SUB)
+                    here, up, down = BLOCKS[b], UPS[b], DOWNS[b]
+                    x = [[x_ref[lev, j, u, t, part, :] for t in range(tiles)] for u in range(nvar)]
                     ce = [diffusion - half_adv * value for value in x[0]]
                     cw = [diffusion + half_adv * value for value in x[0]]
                     ce, cw = walled(b, ce, cw)
-                    cn = masked_last([diffusion - half_adv * value for value in x[1]])
-                    cs = masked_first([diffusion + half_adv * value for value in x[1]])
+                    cn = masked_last([diffusion - half_adv * value for value in x[1]], lane)
+                    cs = masked_first([diffusion + half_adv * value for value in x[1]], lane)
                     s = [
                         [s_ref[odd, now, u, t, here, :] for t in range(tiles)] for u in range(nvar)
                     ]
                     xs = [[x[u][t] * s[u][t] for t in range(tiles)] for u in range(nvar)]
                     for v in range(nvar):
-                        north, south = from_north(s[v]), from_south(s[v])
+                        north, south = from_north(s[v], lane), from_south(s[v], lane)
                         for t in range(tiles):
                             fresh = keep * s[v][t] + ce[t] * s_ref[odd, now, v, t, up, :]
                             fresh = fresh + cw[t] * s_ref[odd, now, v, t, down, :]
@@ -388,30 +454,58 @@
                             s_ref[odd, 1 - now, v, t, here, :] = fresh
             return carry
 
-        lax.fori_loop(0, steps, tangent, 0)
-
-        def adjoint(turn, carry):
+        lax.fori_loop(0, steps, step, 0)
+        for odd in range(2):
+            for v in range(nvar):
+                for t in range(tiles):
+                    ends_ref[2 * i + odd, v, t] = s_ref[odd, steps % 2, v, t, MINE, :]
+        return outer
+
+    lax.fori_loop(0, pairs, pair, 0)
+
+
+def adjoint_kernel(
+    windows, spaces, steps, nvar, levels, tiles,
+    mix_ref, total_ref, x_ref, last_ref, force_ref, ends_ref, inc_ref, rhs_ref, dual_ref,
+    ndm_ref, ninc_ref, *rest,
+):
+    payload_refs = rest[: windows - 1]
+    x0_ref, a_ref, q_ref = rest[windows - 1 :]
+    me = lax.axis_index("window")
+    lane = lane_index()
+    walled = walls(spaces)
+    pairs = levels // 2
+    cuts = [slice(t * LANES, (t + 1) * LANES) for t in range(tiles)]
+
+    def pair(i, outer):
+        for odd in range(2):
+            lev = 2 * i + odd
+            for t in range(tiles):
+                for j in range(steps):
+                    x0_ref[odd, j, t, SUB : 3 * SUB, :] = x_ref[lev, j, 0, t]
+                for v in range(nvar):
+                    a_ref[odd, 0, v, t, SUB : 3 * SUB, :] = last_ref[lev, v, t]
+
+        def step(turn, carry):
             now = lax.rem(turn, 2)
             j = steps - 1 - turn
             for odd in range(2):
+                lev = 2 * i + odd
                 for b in range(2):
-                    here, up, down = blocks[b], ups[b], downs[b]
-                    x = [[x_ref[odd, j, u, t, here, :] for t in range(tiles)] for u in range(nvar)]
-                    ce = [
-                        diffusion + half_adv * x_ref[odd, j, 0, t, up, :] for t in range(tiles)
-                    ]
-                    cw = [
-                        diffusion - half_adv * x_ref[odd, j, 0, t, down, :] for t in range(tiles)
-                    ]
+                    part = slice(b * SUB, (b + 1) * SUB)
+                    here, up, down = BLOCKS[b], UPS[b], DOWNS[b]
+                    x = [[x_ref[lev, j, u, t, part, :] for t in range(tiles)] for u in range(nvar)]
+                    ce = [diffusion + half_adv * x0_ref[odd, j, t, up, :] for t in range(tiles)]
+                    cw = [diffusion - half_adv * x0_ref[odd, j, t, down, :] for t in range(tiles)]
                     ce, cw = walled(b, ce, cw)
-                    cn = masked_first([diffusion + half_adv * value for value in x[1]])
-                    cs = masked_last([diffusion - half_adv * value for value in x[1]])
+                    cn = masked_first([diffusion + half_adv * value for value in x[1]], lane)
+                    cs = masked_last([diffusion - half_adv * value for value in x[1]], lane)
                     a = [
                         [a_ref[odd, now, u, t, here, :] for t in range(tiles)] for u in range(nvar)
                     ]
                     for u in range(nvar):
-                        north = from_north([cn[t] * a[u][t] for t in range(tiles)])
-                        south = from_south([cs[t] * a[u][t] for t in range(tiles)])
+                        north = from_north([cn[t] * a[u][t] for t in range(tiles)], lane)
+                        south = from_south([cs[t] * a[u][t] for t in range(tiles)], lane)
                         for t in range(tiles):
                             fresh = keep * a[u][t] + ce[t] * a_ref[odd, now, u, t, up, :]
                             fresh = fresh + cw[t] * a_ref[odd, now, u, t, down, :]
@@ -421,11 +515,11 @@
                                 pull = pull + mix_ref[v, u] * a[v][t]
                             fresh = fresh + x[u][t] * pull
                             if u == 0:
-                                fresh = fresh + force_ref[2 * i + odd, j, t, b * SUB : (b + 1) * SUB, :]
+                                fresh = fresh + force_ref[lev, j, t, part, :]
                             a_ref[odd, 1 - now, u, t, here, :] = fresh
             return carry
 
-        lax.fori_loop(0, steps, adjoint, 0)
+        lax.fori_loop(0, steps, step, 0)
 
         end = steps % 2
         coded = []
@@ -436,13 +530,13 @@
                 share = total_ref[v * levels + lev]
                 tv, gv = [], []
                 for t in range(tiles):
-                    term = a_ref[odd, end, v, t, mine, :] - last_ref[lev, v, t, HALF : HALF + SUB, :]
+                    term = a_ref[odd, end, v, t, MINE, :] - last_ref[lev, v, t, HALF : HALF + SUB, :]
                     given = rhs_ref[0, v, lev, :, cuts[t]] - inc_ref[0, v, lev, :, cuts[t]]
                     given = given + share * term
                     ndm_ref[v, lev, :, cuts[t]] = -(dual_ref[0, v, lev, :, cuts[t]] + term)
                     ninc_ref[v, lev, :, cuts[t]] = given
                     tv.append(term)
-                    gv.append(given + s_ref[odd, end, v, t, mine, :])
+                    gv.append(given + ends_ref[lev, v, t])
                 back.append(tv)
                 ahead.append(gv)
             coded.append((row_codes(back), row_codes(ahead)))
@@ -529,7 +623,7 @@
     columns = dual_model.shape[-1]
     tiles = columns // LANES
     assert trajectory.shape[0] == windows and windows > 1 and rows == SUB and steps == HALF
-    assert columns == tiles * LANES == windows * part and levels % 2 == 0
+    assert columns == tiles * LANES == windows * part and levels % 4 == 0
     pairs = levels // 2
     wide = -(-steps * part // LANES) * LANES
     bf16, f32, i16 = jnp.bfloat16, jnp.float32, jnp.int16
@@ -537,15 +631,17 @@
     def shape(dims, dtype):
         return jax.ShapeDtypeStruct(dims, dtype)
 
+    block = shape((nvar * levels * wide // LANES + 1, rows, LANES), bf16)
+    variances = jnp.pad(error_var[0].T, ((0, SUB - levels), (0, LANES - nvar)))
+
     def packed(distances):
         return pl.pallas_call(
             lambda *refs: pack_kernel(distances, windows, steps, nvar, levels, part, *refs),
-            out_shape=[shape((nvar * levels + 1, rows, wide), bf16)] * len(distances),
+            out_shape=[block] * len(distances),
             in_specs=[VMEM, VMEM],
             out_specs=[VMEM] * len(distances),
-            scratch_shapes=[pltpu.VMEM((SUB, LANES), f32)],
             compiler_params=params(),
-        )(error_var.transpose(0, 2, 1), trajectory)
+        )(variances, trajectory)
 
     order = sorted(range(1, windows), key=lambda d: -d * (windows - d))
     groups = [[d] for d in order] if windows <= 4 else [order]
@@ -557,7 +653,7 @@
 
     payload = shape((pairs, nvar * tiles + 1, 2 * SUB, LANES), i16)
 
-    counts = [nvar, nvar, steps]
+    counts = [nvar, nvar, steps - 1]
     half_tiles = sum(-(-(count * tiles + 1) // 2) for count in counts)
     halves = shape((pairs, half_tiles, 2 * SUB, LANES), i16)
     near, far, dual = pl.pallas_call(
@@ -581,52 +677,67 @@
     after = [moved(piece, "window", -1) for piece in after]
 
     half_steps = shape((steps // 2, nvar * pairs, rows, columns), bf16)
-    own, traj_near, traj_early, traj_late = pl.pallas_call(
+    own, traj_early, traj_late, traj_far = pl.pallas_call(
         lambda *refs: assemble_kernel(windows, steps, nvar, levels, part, *refs),
         out_shape=[
             shape((steps, nvar * levels, rows, columns), bf16),
-            shape((steps, nvar * pairs, rows, columns), bf16),
             half_steps,
             half_steps,
+            shape((far_base(steps, nvar, levels)[1], rows, columns), bf16),
         ],
         in_specs=[VMEM] * windows,
         out_specs=[VMEM] * 4,
-        scratch_shapes=[pltpu.VMEM((windows, nvar * levels, rows, wide), bf16)],
+        scratch_shapes=[pltpu.VMEM((windows, block.shape[0] - 1, rows, LANES), bf16)],
         compiler_params=params(),
     )(*blocks_here)
-    traj_early = swapped(traj_early, "space", 1)
-    traj_late = swapped(traj_late, "space", 1)
-    traj_near = swapped(traj_near, "space", 0)
-
-    first, last, force, obs, share, mix = pl.pallas_call(
-        lambda *refs: prepare_kernel(steps, nvar, levels, tiles, *refs),
+    traj_far = swapped(traj_far, "space", 1)
+    traj_early, traj_late = swapped(traj_early, "space", 0), swapped(traj_late, "space", 0)
+
+    first, obs, share, mix = pl.pallas_call(
+        lambda *refs: prepare_tangent_kernel(steps, nvar, levels, tiles, *refs),
         out_shape=[
-            *[shape((levels, n, tiles, 2 * SUB, LANES), f32) for n in (nvar, nvar, steps)],
+            shape((levels, nvar, tiles, 2 * SUB, LANES), f32),
             shape((levels, steps, tiles, SUB, LANES), f32),
             shape((levels, steps, SUB, LANES), f32),
             shape((nvar, nvar, SUB, LANES), f32),
         ],
-        in_specs=[SMEM] * 2 + [VMEM] * (6 + pairs),
-        out_specs=[VMEM] * 6,
+        in_specs=[SMEM] * 2 + [VMEM] * 6,
+        out_specs=[VMEM] * 4,
         compiler_params=params(),
-    )(obs_count, obs_var, coupling, near, far, increment, dual_obs, innovation, *after)
+    )(obs_count, obs_var, coupling, near, far, increment, dual_obs, innovation)
+    new_dual_obs, ends, wide_traj = pl.pallas_call(
+        lambda *refs: tangent_kernel(spaces, steps, nvar, levels, tiles, *refs),
+        out_shape=[
+            shape(dual_obs.shape, f32),
+            shape((levels, nvar, tiles, SUB, LANES), f32),
+            shape((levels, steps, nvar, tiles, 2 * SUB, LANES), f32),
+        ],
+        in_specs=[VMEM] * 8,
+        out_specs=[VMEM] * 3,
+        scratch_shapes=[pltpu.VMEM((2, 2, nvar, tiles, 4 * SUB, LANES), f32)],
+        compiler_params=params(),
+    )(mix, share, obs, own, traj_early, traj_late, traj_far, first)
+
+    last, force = pl.pallas_call(
+        lambda *refs: prepare_adjoint_kernel(steps, nvar, levels, tiles, *refs),
+        out_shape=[shape((levels, n, tiles, 2 * SUB, LANES), f32) for n in (nvar, steps)],
+        in_specs=[SMEM] + [VMEM] * (3 + pairs) + [pl.BlockSpec(memory_space=pl.ANY)],
+        out_specs=[VMEM] * 2,
+        compiler_params=params(),
+    )(obs_count, near, far, dual_obs, *after, ends)
     state = shape((nvar, levels, rows, columns), f32)
-    new_dual_obs, base_dual, base_inc, *payloads = pl.pallas_call(
-        lambda *refs: model_kernel(windows, spaces, steps, nvar, levels, tiles, *refs),
-        out_shape=[shape(dual_obs.shape, f32), state, state] + [payload] * (windows - 1),
-        in_specs=[VMEM] * 14,
-        out_specs=[VMEM] * (3 + windows - 1),
+    base_dual, base_inc, *payloads = pl.pallas_call(
+        lambda *refs: adjoint_kernel(windows, spaces, steps, nvar, levels, tiles, *refs),
+        out_shape=[state, state] + [payload] * (windows - 1),
+        in_specs=[VMEM] * 9,
+        out_specs=[VMEM] * (2 + windows - 1),
         scratch_shapes=[
-            pltpu.VMEM((2, steps, nvar, tiles, 4 * SUB, LANES), f32),
-            pltpu.VMEM((2, 2, nvar, tiles, 4 * SUB, LANES), f32),
+            pltpu.VMEM((2, steps, tiles, 4 * SUB, LANES), f32),
             pltpu.VMEM((2, 2, nvar, tiles, 4 * SUB, LANES), f32),
             pltpu.VMEM((2,) + payload.shape, i16),
         ],
-        compiler_params=params(32),
-    )(
-        mix, share, obs, totals, own, traj_near, traj_early, traj_late,
-        first, last, force, increment, model_rhs, dual_model,
-    )
+        compiler_params=params(),
+    )(mix, totals, wide_traj, last, force, ends, increment, model_rhs, dual_model)
     sent = {d: moved(payloads[d - 1], "window", d, around=True) for d in order}
 
     new_dual_model, new_increment = pl.pallas_call(

time: 52.7 us -> 50.1 us (0.951)
  waiting for transfers between devices: 21.6 us -> 13.7 us
  starting transfers between devices: 16.8 us -> 22.3 us
    ppermute x8, waiting for transfers between devices: 21.6 us -> 13.7 us  [moved(): return lax.ppermute(block, axis, route)]
    ppermute x8, starting transfers between devices: 14.7 us -> 17.8 us  [moved(): return lax.ppermute(block, axis, route)]
    ppermute x5, starting transfers between devices: 2.15 us -> 4.48 us  [swapped(): return lax.ppermute(block, axis, swaps(axis, first))]
    pad x0 -> x1, local copies, waits for them, and re-layouts: none -> 0.69 us  [body(): variances = jnp.pad(error_var[0].T, ((0, SUB - levels), (0, LANES - nvar)))]
    unnamed x20 -> x18, local copies, waits for them, and re-layouts: 1.81 us -> 1.13 us
    pallas_call x2 -> x4, Pallas kernels: 7.01 us -> 7.21 us  [the longest x1 3.48 us: body(): pl.pallas_call(lambda *refs: tangent_kernel(spaces, steps, nvar, levels,...]
  transfers between devices with their start and end apart: 13 -> 13, of which waited for: 6 -> 5; matrix products, arithmetic and copies ran while one was open for 0% -> 0% of each run, Pallas kernels for 5% -> 12%
where the time goes in v6:
time: 50.1 us; the launch traced here: 49.3 us
  starting transfers between devices  22.3 us (45%)
  waiting for transfers between devices  13.7 us (27%)
  Pallas kernels  9.97 us (20%)
  local copies, waits for them, and re-layouts  1.81 us (4%)
  between operations  1.52 us (3%)
    ppermute x8, starting transfers between devices, moved(): return lax.ppermute(block, axis, route)  17.8 us
    ppermute x8, waiting for transfers between devices, moved(): return lax.ppermute(block, axis, route)  13.7 us
    ppermute x5, starting transfers between devices, swapped(): return lax.ppermute(block, axis, swaps(axis, first))  4.48 us
    pallas_call x1, Pallas kernels, body(): pl.pallas_call(lambda *refs: tangent_kernel(spaces, steps, nvar, levels,...  3.48 us
    pallas_call x1, Pallas kernels, body(): pl.pallas_call(lambda *refs: adjoint_kernel(windows, spaces, steps, nvar,...  2.83 us
    pallas_call x1, Pallas kernels, body(): pl.pallas_call(lambda *refs: final_kernel(windows, nvar, levels, tiles, *...  1.13 us
    unnamed x18, local copies, waits for them, and re-layouts  1.13 us
  transfers between devices with their start and end apart: 13, of which 5 were waited for; matrix products, arithmetic and copies ran while one was open for 0% of the time, Pallas kernels for 12%

profile of v6, /device:TPU:0, one launch (start us, length us, event | category | flops | bytes accessed | tf_op | source)
XLA Modules:
  0.0 49.3 jit_solution(6134567678122403362)
XLA Ops:
  0.6 0.7 %pad.4.refs_0_ = f32[8,128]{1,0:T(8,128)S(1)} pad(f32[4,5]{1,0:T(4,128)} %bitcast.3, f32[]{:T(128)} %constant.2.clone.1), padding=0_4x0_123 | pad | bytes 4180 | tf_op jit(solution)/shard_map/jit(_pad)/pad | solution.py:635
  1.3 1.1 %copy-done = bf16[4,4,5,4,8,96]{5,4,3,2,1,0:T(8,128)(2,1)S(1)} copy-done((bf16[4,4,5,4,8,96]{5,4,3,2,1,0:T(8,128)(2,1)S(1)}, bf16[4,4,5,4,8,96]{5,4,3,2,1,0:T(8,128)(2,1)}, u32[]{:S(2)}) %copy-start) | copy-done | bytes 491544
  2.4 0.1 shard_map.124
  2.5 3.1 %collective-permute-start.2 = (bf16[61,8,128]{2,1,0:T(8,128)(2,1)S(1)}, bf16[61,8,128]{2,1,0:T(8,128)(2,1)S(1)}, u32[]{:S(2)}, u32[]{:S(2)}) collective-permute-start(bf16[61,8,128]{2,1,0:T(8,128)(2,1)S(1)} %shard_map.124), channel_id=1, source_target_pairs={{0,4},{4,8},{8,12},{12,0},{1,5},{5,9},{9,13},{13,1},{2,6},{6,10},{... | collective-permute-start | bytes 374792 | tf_op jit(solution)/shard_map/ppermute | solution.py:595
  5.6 0.1 shard_map.125
  5.8 2.7 %collective-permute-start.3 = (bf16[61,8,128]{2,1,0:T(8,128)(2,1)S(1)}, bf16[61,8,128]{2,1,0:T(8,128)(2,1)S(1)}, u32[]{:S(2)}, u32[]{:S(2)}) collective-permute-start(bf16[61,8,128]{2,1,0:T(8,128)(2,1)S(1)} %shard_map.125), channel_id=1, source_target_pairs={{0,8},{4,12},{8,0},{12,4},{1,9},{5,13},{9,1},{13,5},{2,10},{6,14},... | collective-permute-start | bytes 374792 | tf_op jit(solution)/shard_map/ppermute | solution.py:595
  8.4 0.1 shard_map.126
  8.5 1.4 %collective-permute-start.4 = (bf16[61,8,128]{2,1,0:T(8,128)(2,1)S(1)}, bf16[61,8,128]{2,1,0:T(8,128)(2,1)S(1)}, u32[]{:S(2)}, u32[]{:S(2)}) collective-permute-start(bf16[61,8,128]{2,1,0:T(8,128)(2,1)S(1)} %shard_map.126), channel_id=1, source_target_pairs={{0,12},{4,0},{8,4},{12,8},{1,13},{5,1},{9,5},{13,9},{2,14},{6,2},{... | collective-permute-start | bytes 374792 | tf_op jit(solution)/shard_map/ppermute | solution.py:595
  9.9 0.5 shard_map.121
  10.4 0.1 collective-permute-start
  10.5 0.7 %collective-permute-start.1 = (s16[2,21,16,128]{3,2,1,0:T(8,128)(2,1)S(1)}, s16[2,21,16,128]{3,2,1,0:T(8,128)(2,1)S(1)}, u32[]{:S(2)}, u32[]{:S(2)}) collective-permute-start(s16[2,21,16,128]{3,2,1,0:T(8,128)(2,1)S(1)} %get-tuple-element.30), channel_id=1, source_target_pairs={{1,2},{2,1},{5,6},{6,5},{9,10},{10,9},{13,14},{14,13},{17,18},{18,... | collective-permute-start | bytes 516104 | tf_op jit(solution)/shard_map/ppermute | solution.py:606
  11.2 0.1 shard_map.123.refs_0_
  11.3 0.6 %collective-permute-done.2.refs_1_ = bf16[61,8,128]{2,1,0:T(8,128)(2,1)S(1)} collective-permute-done((bf16[61,8,128]{2,1,0:T(8,128)(2,1)S(1)}, bf16[61,8,128]{2,1,0:T(8,128)(2,1)S(1)}, u32[]{:S(2)}, u32[]{:S(2)}) %collective-permute-start.2) | collective-permute-done | bytes 124960 | tf_op jit(solution)/shard_map/ppermute | solution.py:595
  11.9 4.6 %collective-permute-done.3.refs_2_ = bf16[61,8,128]{2,1,0:T(8,128)(2,1)S(1)} collective-permute-done((bf16[61,8,128]{2,1,0:T(8,128)(2,1)S(1)}, bf16[61,8,128]{2,1,0:T(8,128)(2,1)S(1)}, u32[]{:S(2)}, u32[]{:S(2)}) %collective-permute-start.3) | collective-permute-done | bytes 124960 | tf_op jit(solution)/shard_map/ppermute | solution.py:595
  16.5 0.5 shard_map.128
  17.0 0.7 %collective-permute-start.7 = (bf16[31,8,384]{2,1,0:T(8,128)(2,1)S(1)}, bf16[31,8,384]{2,1,0:T(8,128)(2,1)S(1)}, u32[]{:S(2)}, u32[]{:S(2)}) collective-permute-start(bf16[31,8,384]{2,1,0:T(8,128)(2,1)S(1)} %get-tuple-element.39), channel_id=1, source_target_pairs={{1,2},{2,1},{5,6},{6,5},{9,10},{10,9},{13,14},{14,13},{17,18},{18,... | collective-permute-start | bytes 571400 | tf_op jit(solution)/shard_map/ppermute | solution.py:606
  17.7 0.3 shard_map.127
  17.9 1.4 %collective-permute-start.8 = (s16[2,16,16,128]{3,2,1,0:T(8,128)(2,1)S(1)}, s16[2,16,16,128]{3,2,1,0:T(8,128)(2,1)S(1)}, u32[]{:S(2)}, u32[]{:S(2)}) collective-permute-start(s16[2,16,16,128]{3,2,1,0:T(8,128)(2,1)S(1)} %get-tuple-element.42), channel_id=1, source_target_pairs={{4,0},{8,4},{12,8},{5,1},{9,5},{13,9},{6,2},{10,6},{14,10},{7,3},{... | collective-permute-start | bytes 393224 | tf_op jit(solution)/shard_map/ppermute | solution.py:595
  19.4 1.3 %collective-permute-start.9 = (s16[2,16,16,128]{3,2,1,0:T(8,128)(2,1)S(1)}, s16[2,16,16,128]{3,2,1,0:T(8,128)(2,1)S(1)}, u32[]{:S(2)}, u32[]{:S(2)}) collective-permute-start(s16[2,16,16,128]{3,2,1,0:T(8,128)(2,1)S(1)} %get-tuple-element.43), channel_id=1, source_target_pairs={{4,0},{8,4},{12,8},{5,1},{9,5},{13,9},{6,2},{10,6},{14,10},{7,3},{... | collective-permute-start | bytes 393224 | tf_op jit(solution)/shard_map/ppermute | solution.py:595
  20.7 3.0 %collective-permute-start.5 = (bf16[2,10,8,384]{3,2,1,0:T(8,128)(2,1)S(1)}, bf16[2,10,8,384]{3,2,1,0:T(8,128)(2,1)S(1)}, u32[]{:S(2)}, u32[]{:S(2)}) collective-permute-start(bf16[2,10,8,384]{3,2,1,0:T(8,128)(2,1)S(1)} %get-tuple-element.37), channel_id=1, source_target_pairs={{0,1},{1,0},{2,3},{3,2},{4,5},{5,4},{6,7},{7,6},{8,9},{9,8},{10,11... | collective-permute-start | bytes 368648 | tf_op jit(solution)/shard_map/ppermute | solution.py:606
  23.7 0.1 collective-permute-start.6
  24.4 0.7 %shard_map.122 = (f32[4,5,3,16,128]{4,3,2,1,0:T(8,128)S(1)}, f32[4,4,3,8,128]{4,3,2,1,0:T(8,128)S(1)}, f32[4,4,8,128]{3,2,1,0:T(8,128)S(1)}, f32[5,5,8,128]{3,2,1,0:T(8,128)S(1)}) custom-call(s32[1]{0:T(128)S(6)} %copy.13.refs_0_, f32[1,4,4]{2,1,0:T(4,128)S(1)} %copy-done.8, f32[5,5]{1,0:T(8,128)S(1)} %copy-done.7, ...), custom_call_target="tpu_custom_call" | custom-call | tf_op jit(solution)/shard_map/pallas_call | solution.py:696
  25.2 3.5 %shard_map.129 = (f32[1,4,4,8,384]{4,3,2,1,0:T(8,128)}, f32[4,5,3,8,128]{4,3,2,1,0:T(8,128)S(1)}, f32[4,4,5,3,16,128]{5,4,3,2,1,0:T(8,128)S(1)}) custom-call(f32[5,5,8,128]{3,2,1,0:T(8,128)S(1)} %get-tuple-element.31.refs_0_, f32[4,4,8,128]{3,2,1,0:T(8,128)S(1)} %get-tuple-element.34.refs_1_, f32[4,4,3,8,128]{4,3,2,1,0:T(8,128)S(1)} %get-tuple-element.35.refs_2_, ...), custom_call_target="tpu_custom_call" | custom-call | tf_op jit(solution)/shard_map/pallas_call | solution.py:708
  28.7 0.5 collective-permute-done.9.refs_5_
  29.2 0.2 shard_map.130
  29.3 2.8 %shard_map.131 = (f32[5,4,8,384]{3,2,1,0:T(8,128)S(1)}, f32[5,4,8,384]{3,2,1,0:T(8,128)S(1)}, s16[2,16,16,128]{3,2,1,0:T(8,128)(2,1)S(1)}, s16[2,16,16,128]{3,2,...) custom-call(f32[5,5,8,128]{3,2,1,0:T(8,128)S(1)} %get-tuple-element.31.refs_0_, ...), custom_call_target="tpu_custom_call" | custom-call | tf_op jit(solution)/shard_map/pallas_call | solution.py:729
  32.2 3.9 %collective-permute-start.10 = (s16[2,16,16,128]{3,2,1,0:T(8,128)(2,1)S(1)}, s16[2,16,16,128]{3,2,1,0:T(8,128)(2,1)S(1)}, u32[]{:S(2)}, u32[]{:S(2)}) collective-permute-start(s16[2,16,16,128]{3,2,1,0:T(8,128)(2,1)S(1)} %get-tuple-element.47), channel_id=1, source_target_pairs={{0,4},{4,8},{8,12},{12,0},{1,5},{5,9},{9,13},{13,1},{2,6},{6,10},{... | collective-permute-start | bytes 393224 | tf_op jit(solution)/shard_map/ppermute | solution.py:595
  36.1 2.9 %collective-permute-start.11 = (s16[2,16,16,128]{3,2,1,0:T(8,128)(2,1)S(1)}, s16[2,16,16,128]{3,2,1,0:T(8,128)(2,1)S(1)}, u32[]{:S(2)}, u32[]{:S(2)}) collective-permute-start(s16[2,16,16,128]{3,2,1,0:T(8,128)(2,1)S(1)} %get-tuple-element.48), channel_id=1, source_target_pairs={{0,8},{4,12},{8,0},{12,4},{1,9},{5,13},{9,1},{13,5},{2,10},{6,14},... | collective-permute-start | bytes 393224 | tf_op jit(solution)/shard_map/ppermute | solution.py:595
  39.0 1.2 %collective-permute-start.12 = (s16[2,16,16,128]{3,2,1,0:T(8,128)(2,1)S(1)}, s16[2,16,16,128]{3,2,1,0:T(8,128)(2,1)S(1)}, u32[]{:S(2)}, u32[]{:S(2)}) collective-permute-start(s16[2,16,16,128]{3,2,1,0:T(8,128)(2,1)S(1)} %get-tuple-element.49), channel_id=1, source_target_pairs={{0,12},{4,0},{8,4},{12,8},{1,13},{5,1},{9,5},{13,9},{2,14},{6,2},{... | collective-permute-start | bytes 393224 | tf_op jit(solution)/shard_map/ppermute | solution.py:595
  40.2 2.7 %collective-permute-done.10.refs_0_ = s16[2,16,16,128]{3,2,1,0:T(8,128)(2,1)S(1)} collective-permute-done((s16[2,16,16,128]{3,2,1,0:T(8,128)(2,1)S(1)}, s16[2,16,16,128]{3,2,1,0:T(8,128)(2,1)S(1)}, u32[]{:S(2)}, u32[]{:S(2)}) %collective-permute-start.10) | collective-permute-done | bytes 131104 | tf_op jit(solution)/shard_map/ppermute | solution.py:595
  42.9 5.3 %collective-permute-done.11.refs_1_ = s16[2,16,16,128]{3,2,1,0:T(8,128)(2,1)S(1)} collective-permute-done((s16[2,16,16,128]{3,2,1,0:T(8,128)(2,1)S(1)}, s16[2,16,16,128]{3,2,1,0:T(8,128)(2,1)S(1)}, u32[]{:S(2)}, u32[]{:S(2)}) %collective-permute-start.11) | collective-permute-done | bytes 131104 | tf_op jit(solution)/shard_map/ppermute | solution.py:595
  48.2 1.1 %shard_map.132 = (f32[1,5,4,8,384]{4,3,2,1,0:T(8,128)}, f32[1,5,4,8,384]{4,3,2,1,0:T(8,128)}) custom-call(s16[2,16,16,128]{3,2,1,0:T(8,128)(2,1)S(1)} %collective-permute-done.10.refs_0_, s16[2,16,16,128]{3,2,1,0:T(8,128)(2,1)S(1)} %collective-permute-done.11.refs_1_, s16[2,16,16,128]{3,2,1,0:T(8,128)(2,1)S(1)} %collective-permute-done.12.refs_2_, ...), custom_call_target="tpu_custom_call" | custom-call | tf_op jit(solution)/shard_map/pallas_call | solution.py:743
  (25 shorter events, 0.1 us)
Async XLA Ops:
  1.3 1.1 %copy-start = (bf16[4,4,5,4,8,96]{5,4,3,2,1,0:T(8,128)(2,1)S(1)}, bf16[4,4,5,4,8,96]{5,4,3,2,1,0:T(8,128)(2,1)}, u32[]{:S(2)}) copy-start(bf16[4,4,5,4,8,96]{5,4,3,2,1,0:T(8,128)(2,1)} %refs_1_.11) | copy-start | bytes 1474564
  2.4 7.5 %copy-start.2 = (f32[1,5,4,8,384]{4,3,2,1,0:T(8,128)S(1)}, f32[1,5,4,8,384]{4,3,2,1,0:T(8,128)}, u32[]{:S(2)}) copy-start(f32[1,5,4,8,384]{4,3,2,1,0:T(8,128)} %refs_6_.3) | copy-start | bytes 737284
  2.4 7.5 %copy-start.3 = (f32[1,4,4,8,384]{4,3,2,1,0:T(8,128)S(1)}, f32[1,4,4,8,384]{4,3,2,1,0:T(8,128)}, u32[]{:S(2)}) copy-start(f32[1,4,4,8,384]{4,3,2,1,0:T(8,128)} %refs_3_.1) | copy-start | bytes 589828
  2.4 7.5 %copy-start.4 = (f32[1,5,4,8,384]{4,3,2,1,0:T(8,128)S(1)}, f32[1,5,4,8,384]{4,3,2,1,0:T(8,128)}, u32[]{:S(2)}) copy-start(f32[1,5,4,8,384]{4,3,2,1,0:T(8,128)} %refs_8_.1) | copy-start | bytes 737284
  2.4 8.8 %copy-start.1 = (bf16[4,4,5,4,8,96]{5,4,3,2,1,0:T(8,128)(2,1)S(1)}, bf16[4,4,5,4,8,96]{5,4,3,2,1,0:T(8,128)(2,1)}, u32[]{:S(2)}) copy-start(bf16[4,4,5,4,8,96]{5,4,3,2,1,0:T(8,128)(2,1)} %refs_1_.11) | copy-start | bytes 1474564
  2.5 9.4 %collective-permute-start.2 = (bf16[61,8,128]{2,1,0:T(8,128)(2,1)S(1)}, bf16[61,8,128]{2,1,0:T(8,128)(2,1)S(1)}, u32[]{:S(2)}, u32[]{:S(2)}) collective-permute-start(bf16[61,8,128]{2,1,0:T(8,128)(2,1)S(1)} %shard_map.124), channel_id=1, source_target_pairs={{0,4},{4,8},{8,12},{12,0},{1,5},{5,9},{9,13},{13,1},{2,6},{6,10},{... | collective-permute-start | bytes 374792 | tf_op jit(solution)/shard_map/ppermute | solution.py:595
  5.7 18.7 %copy-start.6 = (f32[1,4,4,8,384]{4,3,2,1,0:T(8,128)S(1)}, f32[1,4,4,8,384]{4,3,2,1,0:T(8,128)}, u32[]{:S(2)}) copy-start(f32[1,4,4,8,384]{4,3,2,1,0:T(8,128)} %refs_7_.2) | copy-start | bytes 589828
  5.7 18.7 %copy-start.7 = (f32[5,5]{1,0:T(8,128)S(1)}, f32[5,5]{1,0:T(8,128)}, u32[]{:S(2)}) copy-start(f32[5,5]{1,0:T(8,128)} %refs_2_.3) | copy-start | bytes 304
  5.8 18.7 %copy-start.8 = (f32[1,4,4]{2,1,0:T(4,128)S(1)}, f32[1,4,4]{2,1,0:T(4,128)}, u32[]{:S(2)}) copy-start(f32[1,4,4]{2,1,0:T(4,128)} %refs_1_.7) | copy-start | bytes 196
  5.8 10.7 %collective-permute-start.3 = (bf16[61,8,128]{2,1,0:T(8,128)(2,1)S(1)}, bf16[61,8,128]{2,1,0:T(8,128)(2,1)S(1)}, u32[]{:S(2)}, u32[]{:S(2)}) collective-permute-start(bf16[61,8,128]{2,1,0:T(8,128)(2,1)S(1)} %shard_map.125), channel_id=1, source_target_pairs={{0,8},{4,12},{8,0},{12,4},{1,9},{5,13},{9,1},{13,5},{2,10},{6,14},... | collective-permute-start | bytes 374792 | tf_op jit(solution)/shard_map/ppermute | solution.py:595
  8.5 8.0 %collective-permute-start.4 = (bf16[61,8,128]{2,1,0:T(8,128)(2,1)S(1)}, bf16[61,8,128]{2,1,0:T(8,128)(2,1)S(1)}, u32[]{:S(2)}, u32[]{:S(2)}) collective-permute-start(bf16[61,8,128]{2,1,0:T(8,128)(2,1)S(1)} %shard_map.126), channel_id=1, source_target_pairs={{0,12},{4,0},{8,4},{12,8},{1,13},{5,1},{9,5},{13,9},{2,14},{6,2},{... | collective-permute-start | bytes 374792 | tf_op jit(solution)/shard_map/ppermute | solution.py:595
  10.4 7.2 %collective-permute-start = (s16[2,21,16,128]{3,2,1,0:T(8,128)(2,1)S(1)}, s16[2,21,16,128]{3,2,1,0:T(8,128)(2,1)S(1)}, u32[]{:S(2)}, u32[]{:S(2)}) collective-permute-start(s16[2,21,16,128]{3,2,1,0:T(8,128)(2,1)S(1)} %get-tuple-element.29), channel_id=1, source_target_pairs={{0,1},{1,0},{2,3},{3,2},{4,5},{5,4},{6,7},{7,6},{8,9},{9,8},{10,11... | collective-permute-start | bytes 516104 | tf_op jit(solution)/shard_map/ppermute | solution.py:606
  10.5 7.2 %collective-permute-start.1 = (s16[2,21,16,128]{3,2,1,0:T(8,128)(2,1)S(1)}, s16[2,21,16,128]{3,2,1,0:T(8,128)(2,1)S(1)}, u32[]{:S(2)}, u32[]{:S(2)}) collective-permute-start(s16[2,21,16,128]{3,2,1,0:T(8,128)(2,1)S(1)} %get-tuple-element.30), channel_id=1, source_target_pairs={{1,2},{2,1},{5,6},{6,5},{9,10},{10,9},{13,14},{14,13},{17,18},{18,... | collective-permute-start | bytes 516104 | tf_op jit(solution)/shard_map/ppermute | solution.py:606
  17.0 8.2 %collective-permute-start.7 = (bf16[31,8,384]{2,1,0:T(8,128)(2,1)S(1)}, bf16[31,8,384]{2,1,0:T(8,128)(2,1)S(1)}, u32[]{:S(2)}, u32[]{:S(2)}) collective-permute-start(bf16[31,8,384]{2,1,0:T(8,128)(2,1)S(1)} %get-tuple-element.39), channel_id=1, source_target_pairs={{1,2},{2,1},{5,6},{6,5},{9,10},{10,9},{13,14},{14,13},{17,18},{18,... | collective-permute-start | bytes 571400 | tf_op jit(solution)/shard_map/ppermute | solution.py:606
  17.9 11.4 %copy-start.5 = (f32[1,5,4,8,384]{4,3,2,1,0:T(8,128)S(1)}, f32[1,5,4,8,384]{4,3,2,1,0:T(8,128)}, u32[]{:S(2)}) copy-start(f32[1,5,4,8,384]{4,3,2,1,0:T(8,128)} %refs_7_.3) | copy-start | bytes 737284
  17.9 10.7 %collective-permute-start.8 = (s16[2,16,16,128]{3,2,1,0:T(8,128)(2,1)S(1)}, s16[2,16,16,128]{3,2,1,0:T(8,128)(2,1)S(1)}, u32[]{:S(2)}, u32[]{:S(2)}) collective-permute-start(s16[2,16,16,128]{3,2,1,0:T(8,128)(2,1)S(1)} %get-tuple-element.42), channel_id=1, source_target_pairs={{4,0},{8,4},{12,8},{5,1},{9,5},{13,9},{6,2},{10,6},{14,10},{7,3},{... | collective-permute-start | bytes 393224 | tf_op jit(solution)/shard_map/ppermute | solution.py:595
  19.4 9.8 %collective-permute-start.9 = (s16[2,16,16,128]{3,2,1,0:T(8,128)(2,1)S(1)}, s16[2,16,16,128]{3,2,1,0:T(8,128)(2,1)S(1)}, u32[]{:S(2)}, u32[]{:S(2)}) collective-permute-start(s16[2,16,16,128]{3,2,1,0:T(8,128)(2,1)S(1)} %get-tuple-element.43), channel_id=1, source_target_pairs={{4,0},{8,4},{12,8},{5,1},{9,5},{13,9},{6,2},{10,6},{14,10},{7,3},{... | collective-permute-start | bytes 393224 | tf_op jit(solution)/shard_map/ppermute | solution.py:595
  20.7 4.5 %collective-permute-start.5 = (bf16[2,10,8,384]{3,2,1,0:T(8,128)(2,1)S(1)}, bf16[2,10,8,384]{3,2,1,0:T(8,128)(2,1)S(1)}, u32[]{:S(2)}, u32[]{:S(2)}) collective-permute-start(bf16[2,10,8,384]{3,2,1,0:T(8,128)(2,1)S(1)} %get-tuple-element.37), channel_id=1, source_target_pairs={{0,1},{1,0},{2,3},{3,2},{4,5},{5,4},{6,7},{7,6},{8,9},{9,8},{10,11... | collective-permute-start | bytes 368648 | tf_op jit(solution)/shard_map/ppermute | solution.py:606
  23.7 1.5 %collective-permute-start.6 = (bf16[2,10,8,384]{3,2,1,0:T(8,128)(2,1)S(1)}, bf16[2,10,8,384]{3,2,1,0:T(8,128)(2,1)S(1)}, u32[]{:S(2)}, u32[]{:S(2)}) collective-permute-start(bf16[2,10,8,384]{3,2,1,0:T(8,128)(2,1)S(1)} %get-tuple-element.38), channel_id=1, source_target_pairs={{0,1},{1,0},{2,3},{3,2},{4,5},{5,4},{6,7},{7,6},{8,9},{9,8},{10,11... | collective-permute-start | bytes 368648 | tf_op jit(solution)/shard_map/ppermute | solution.py:606
  32.2 10.7 %collective-permute-start.10 = (s16[2,16,16,128]{3,2,1,0:T(8,128)(2,1)S(1)}, s16[2,16,16,128]{3,2,1,0:T(8,128)(2,1)S(1)}, u32[]{:S(2)}, u32[]{:S(2)}) collective-permute-start(s16[2,16,16,128]{3,2,1,0:T(8,128)(2,1)S(1)} %get-tuple-element.47), channel_id=1, source_target_pairs={{0,4},{4,8},{8,12},{12,0},{1,5},{5,9},{9,13},{13,1},{2,6},{6,10},{... | collective-permute-start | bytes 393224 | tf_op jit(solution)/shard_map/ppermute | solution.py:595
  36.1 12.1 %collective-permute-start.11 = (s16[2,16,16,128]{3,2,1,0:T(8,128)(2,1)S(1)}, s16[2,16,16,128]{3,2,1,0:T(8,128)(2,1)S(1)}, u32[]{:S(2)}, u32[]{:S(2)}) collective-permute-start(s16[2,16,16,128]{3,2,1,0:T(8,128)(2,1)S(1)} %get-tuple-element.48), channel_id=1, source_target_pairs={{0,8},{4,12},{8,0},{12,4},{1,9},{5,13},{9,1},{13,5},{2,10},{6,14},... | collective-permute-start | bytes 393224 | tf_op jit(solution)/shard_map/ppermute | solution.py:595
  39.0 9.2 %collective-permute-start.12 = (s16[2,16,16,128]{3,2,1,0:T(8,128)(2,1)S(1)}, s16[2,16,16,128]{3,2,1,0:T(8,128)(2,1)S(1)}, u32[]{:S(2)}, u32[]{:S(2)}) collective-permute-start(s16[2,16,16,128]{3,2,1,0:T(8,128)(2,1)S(1)} %get-tuple-element.49), channel_id=1, source_target_pairs={{0,12},{4,0},{8,4},{12,8},{1,13},{5,1},{9,5},{13,9},{2,14},{6,2},{... | collective-permute-start | bytes 393224 | tf_op jit(solution)/shard_map/ppermute | solution.py:595

commit v7 on v6

--- a/solution.py
+++ b/solution.py
@@ -19,6 +19,7 @@
 
 VMEM = pl.BlockSpec(memory_space=pltpu.VMEM)
 SMEM = pl.BlockSpec(memory_space=pltpu.SMEM)
+ANY = pl.BlockSpec(memory_space=pl.ANY)
 
 
 def params(mib=24):
@@ -230,7 +231,7 @@
 
 def assemble_kernel(windows, steps, nvar, levels, part, *refs):
     pieces = refs[:windows]
-    own_ref, early_ref, late_ref, far_ref, stack_ref = refs[windows:]
+    own_ref, early_ref, late_ref, far_ref, stack_ref = refs[windows + 1 :]
     me = lax.axis_index("window")
     even = even_place()
     lane = lane_index()
@@ -281,18 +282,29 @@
         variable(v)
 
 
-def prepare_tangent_kernel(
+def prepare_factor_kernel(
     steps, nvar, levels, tiles,
-    count_ref, noise_ref, coupling_ref, near_ref, far_ref, inc_ref, dobs_ref, innov_ref,
-    first_ref, obs_ref, share_ref, mix_ref,
+    count_ref, noise_ref, coupling_ref, dobs_ref, innov_ref, obs_ref, share_ref, mix_ref,
 ):
-    even = even_place()
-    blocks = [slice(0, SUB), slice(SUB, 2 * SUB)]
     cuts = [slice(t * LANES, (t + 1) * LANES) for t in range(tiles)]
     for v in range(nvar):
         for u in range(nvar):
             one = coupling_gain * coupling_ref[v : v + 1, u : u + 1]
             mix_ref[v, u] = jnp.broadcast_to(one, (SUB, LANES))
+    for lev in range(levels):
+        for j in range(steps):
+            noise = jnp.full((SUB, LANES), noise_ref[0, j, lev])
+            share = jnp.where(j < count_ref[0], 1.0, 0.0) / noise
+            share_ref[lev, j] = share
+            for t in range(tiles):
+                gap = innov_ref[0, j, lev, :, cuts[t]] - noise * dobs_ref[0, j, lev, :, cuts[t]]
+                obs_ref[lev, j, t] = gap * share
+
+
+def prepare_tangent_kernel(nvar, levels, tiles, near_ref, far_ref, inc_ref, first_ref):
+    even = even_place()
+    blocks = [slice(0, SUB), slice(SUB, 2 * SUB)]
+    cuts = [slice(t * LANES, (t + 1) * LANES) for t in range(tiles)]
     offset = -(-(nvar * tiles + 1) // 2) * 2
     for i in range(levels // 2):
         fields = [decoded(ref, i, offset, nvar, tiles) for ref in (near_ref, far_ref)]
@@ -304,13 +316,6 @@
                     halves = widened(inc_ref[0, v, lev, :, cuts[t]], near, far, odd, even)
                     for b in range(2):
                         first_ref[lev, v, t, blocks[b], :] = halves[b]
-            for j in range(steps):
-                noise = jnp.full((SUB, LANES), noise_ref[0, j, lev])
-                share = jnp.where(j < count_ref[0], 1.0, 0.0) / noise
-                share_ref[lev, j] = share
-                for t in range(tiles):
-                    gap = innov_ref[0, j, lev, :, cuts[t]] - noise * dobs_ref[0, j, lev, :, cuts[t]]
-                    obs_ref[lev, j, t] = gap * share
 
 
 def prepare_adjoint_kernel(
@@ -547,32 +552,73 @@
         return outer
 
     lax.fori_loop(0, pairs, pair, 0)
-    for d in range(1, windows):
-        payload_refs[d - 1][...] = q_ref[jnp.where(me + d >= windows, 0, 1)]
+    if windows == 4:
+        later_ref, earlier_ref, over_ref = payload_refs
+        later_ref[...] = q_ref[1]
+        earlier_ref[...] = q_ref[0]
+        over_ref[...] = q_ref[jnp.where(me == 0, 1, 0)]
+    else:
+        for d in range(1, windows):
+            payload_refs[d - 1][...] = q_ref[jnp.where(me + d >= windows, 0, 1)]
+
+
+def join_kernel(nvar, tiles, right_ref, left_ref, later_ref, earlier_ref, out_ref):
+    upward = lax.axis_index("window") == 1
+
+    def pair(i, carry):
+        def summed(ref, other_ref):
+            codes = [
+                jnp.where(upward, floats(ref[i, n]), floats(other_ref[i, n]))
+                for n in range(nvar * tiles + 1)
+            ]
+            scales = jnp.exp2(codes[-1]) * (1.0 / CODE_MAX)
+            return [
+                [codes[v * tiles + t] * scales[:, v : v + 1] for t in range(tiles)]
+                for v in range(nvar)
+            ]
+
+        mine, other = summed(later_ref, earlier_ref), summed(right_ref, left_ref)
+        planes = [[a + b for a, b in zip(x, y)] for x, y in zip(mine, other)]
+        values, scales = row_codes(planes)
+        for n, value in enumerate(values + [scales]):
+            out_ref[i, n] = shorts(value)
+        return carry
+
+    lax.fori_loop(0, out_ref.shape[0], pair, 0)
 
 
 def final_kernel(windows, nvar, levels, tiles, *refs):
-    pieces = refs[: windows - 1]
-    total_ref, base_dual_ref, base_inc_ref, ndm_ref, ninc_ref = refs[windows - 1 :]
+    pieces, refs = refs[:-5], refs[-5:]
+    total_ref, base_dual_ref, base_inc_ref, ndm_ref, ninc_ref = refs
     me = lax.axis_index("window")
     pairs = levels // 2
     cuts = [slice(t * LANES, (t + 1) * LANES) for t in range(tiles)]
+    if windows == 4:
+        from_later = [False, True, me < 2, me < 2]
+    else:
+        from_later = [d > me for d in range(1, windows)]
 
     def pair(i, carry):
         tails = [None] * (nvar * tiles)
         heads = [None] * (nvar * tiles)
-        for d in range(1, windows):
-            piece = pieces[d - 1]
+
+        def add(sums, n, value):
+            sums[n] = value if sums[n] is None else sums[n] + value
+
+        for piece, later in zip(pieces, from_later):
             scales = jnp.exp2(floats(piece[i, nvar * tiles])) * (1.0 / CODE_MAX)
-            later = jnp.where(d > me, scales, 0.0)
-            earlier = jnp.where(d > me, 0.0, scales)
             for v in range(nvar):
+                scale = scales[:, v : v + 1]
                 for t in range(tiles):
                     n = v * tiles + t
-                    value = floats(piece[i, n])
-                    tail, head = value * later[:, v : v + 1], value * earlier[:, v : v + 1]
-                    tails[n] = tail if d == 1 else tails[n] + tail
-                    heads[n] = head if d == 1 else heads[n] + head
+                    value = floats(piece[i, n]) * scale
+                    if later is True:
+                        add(tails, n, value)
+                    elif later is False:
+                        add(heads, n, value)
+                    else:
+                        add(tails, n, jnp.where(later, value, 0.0))
+                        add(heads, n, jnp.where(later, 0.0, value))
         for v in range(nvar):
             for odd in range(2):
                 lev = 2 * i + odd
@@ -666,15 +712,27 @@
     far, near = swapped(far, "space", 1), swapped(near, "space", 0)
 
     blocks_here = [arrived[d] for d in range(windows)]
-    around = shape((2,) + payload.shape[1:], i16)
     *after, totals = pl.pallas_call(
         lambda *refs: around_kernel(windows, nvar, levels, *refs),
-        out_shape=[around] * pairs + [shape((nvar * levels, rows, LANES), f32)],
+        out_shape=[shape((2,) + payload.shape[1:], i16)] * pairs
+        + [shape((nvar * levels, rows, LANES), f32)],
         in_specs=[VMEM] * (windows + 3),
         out_specs=[VMEM] * (pairs + 1),
         compiler_params=params(),
     )(*blocks_here, dual, near, far)
     after = [moved(piece, "window", -1) for piece in after]
+
+    obs, share, mix = pl.pallas_call(
+        lambda *refs: prepare_factor_kernel(steps, nvar, levels, tiles, *refs),
+        out_shape=[
+            shape((levels, steps, tiles, SUB, LANES), f32),
+            shape((levels, steps, SUB, LANES), f32),
+            shape((nvar, nvar, SUB, LANES), f32),
+        ],
+        in_specs=[SMEM] * 2 + [VMEM] * 3,
+        out_specs=[VMEM] * 3,
+        compiler_params=params(),
+    )(obs_count, obs_var, coupling, dual_obs, innovation)
 
     half_steps = shape((steps // 2, nvar * pairs, rows, columns), bf16)
     own, traj_early, traj_late, traj_far = pl.pallas_call(
@@ -685,26 +743,21 @@
             half_steps,
             shape((far_base(steps, nvar, levels)[1], rows, columns), bf16),
         ],
-        in_specs=[VMEM] * windows,
+        in_specs=[VMEM] * windows + [ANY],
         out_specs=[VMEM] * 4,
         scratch_shapes=[pltpu.VMEM((windows, block.shape[0] - 1, rows, LANES), bf16)],
         compiler_params=params(),
-    )(*blocks_here)
+    )(*blocks_here, mix)
     traj_far = swapped(traj_far, "space", 1)
     traj_early, traj_late = swapped(traj_early, "space", 0), swapped(traj_late, "space", 0)
 
-    first, obs, share, mix = pl.pallas_call(
-        lambda *refs: prepare_tangent_kernel(steps, nvar, levels, tiles, *refs),
-        out_shape=[
-            shape((levels, nvar, tiles, 2 * SUB, LANES), f32),
-            shape((levels, steps, tiles, SUB, LANES), f32),
-            shape((levels, steps, SUB, LANES), f32),
-            shape((nvar, nvar, SUB, LANES), f32),
-        ],
-        in_specs=[SMEM] * 2 + [VMEM] * 6,
-        out_specs=[VMEM] * 4,
+    first = pl.pallas_call(
+        lambda *refs: prepare_tangent_kernel(nvar, levels, tiles, *refs),
+        out_shape=shape((levels, nvar, tiles, 2 * SUB, LANES), f32),
+        in_specs=[VMEM] * 3,
+        out_specs=VMEM,
         compiler_params=params(),
-    )(obs_count, obs_var, coupling, near, far, increment, dual_obs, innovation)
+    )(near, far, increment)
     new_dual_obs, ends, wide_traj = pl.pallas_call(
         lambda *refs: tangent_kernel(spaces, steps, nvar, levels, tiles, *refs),
         out_shape=[
@@ -721,7 +774,7 @@
     last, force = pl.pallas_call(
         lambda *refs: prepare_adjoint_kernel(steps, nvar, levels, tiles, *refs),
         out_shape=[shape((levels, n, tiles, 2 * SUB, LANES), f32) for n in (nvar, steps)],
-        in_specs=[SMEM] + [VMEM] * (3 + pairs) + [pl.BlockSpec(memory_space=pl.ANY)],
+        in_specs=[SMEM] + [VMEM] * (3 + pairs) + [ANY],
         out_specs=[VMEM] * 2,
         compiler_params=params(),
     )(obs_count, near, far, dual_obs, *after, ends)
@@ -738,15 +791,29 @@
         ],
         compiler_params=params(),
     )(mix, totals, wide_traj, last, force, ends, increment, model_rhs, dual_model)
-    sent = {d: moved(payloads[d - 1], "window", d, around=True) for d in order}
+    if windows == 4:
+        later, earlier, over = payloads
+        right, left = moved(later, "window", 1), moved(earlier, "window", -1)
+        over = lax.ppermute(over, "window", [(0, 2), (3, 1)])
+        both = pl.pallas_call(
+            lambda *refs: join_kernel(nvar, tiles, *refs),
+            out_shape=payload,
+            in_specs=[VMEM] * 4,
+            out_specs=VMEM,
+            compiler_params=params(),
+        )(right, left, later, earlier)
+        both = lax.ppermute(both, "window", [(1, 3), (2, 0)])
+        sent = [right, left, over, both]
+    else:
+        sent = [moved(payloads[d - 1], "window", d, around=True) for d in range(1, windows)]
 
     new_dual_model, new_increment = pl.pallas_call(
         lambda *refs: final_kernel(windows, nvar, levels, tiles, *refs),
         out_shape=[shape(dual_model.shape, f32), shape(increment.shape, f32)],
-        in_specs=[VMEM] * (windows + 2),
+        in_specs=[VMEM] * (len(sent) + 3),
         out_specs=[VMEM] * 2,
         compiler_params=params(),
-    )(*[sent[d] for d in range(1, windows)], totals, base_dual, base_inc)
+    )(*sent, totals, base_dual, base_inc)
     return new_dual_model, new_dual_obs, new_increment
 
 

time: 50.1 us -> 55.1 us (1.100)
  starting transfers between devices: 22.3 us -> 28.2 us
  waiting for transfers between devices: 13.7 us -> 12.5 us
  Pallas kernels: 9.97 us -> 10.6 us
    ppermute x8 -> x7, waiting for transfers between devices: 13.7 us -> 4.53 us  [moved(): return lax.ppermute(block, axis, route)]
    ppermute x0 -> x2, starting transfers between devices: none -> 7.01 us  [the longest x1 5.72 us: body(): over = lax.ppermute(over, 'window', [(0, 2), (3, 1)])]
    ppermute x0 -> x2, waiting for transfers between devices: none -> 6.9 us  [the longest x1 6.29 us: body(): both = lax.ppermute(both, 'window', [(1, 3), (2, 0)])]
    ppermute x8 -> x7, starting transfers between devices: 17.8 us -> 16.7 us  [moved(): return lax.ppermute(block, axis, route)]
    ppermute x5, waiting for transfers between devices: 0.01 us -> 1.12 us  [swapped(): return lax.ppermute(block, axis, swaps(axis, first))]
    pallas_call x1 -> x3, Pallas kernels: 0.73 us -> 1.26 us  [the longest x1 0.69 us: body(): pl.pallas_call(lambda *refs: prepare_factor_kernel(steps, nvar, levels, t...]
  transfers between devices with their start and end apart: 13 -> 14, of which waited for: 5 -> 7; matrix products, arithmetic and copies ran while one was open for 0% -> 0% of each run, Pallas kernels for 12% -> 12%
where the time goes in v7:
time: 55.1 us; the launch traced here: 54.8 us
  starting transfers between devices  28.2 us (51%)
  waiting for transfers between devices  12.5 us (23%)
  Pallas kernels  10.6 us (19%)
  local copies, waits for them, and re-layouts  1.82 us (3%)
  between operations  1.56 us (3%)
    ppermute x7, starting transfers between devices, moved(): return lax.ppermute(block, axis, route)  16.7 us
    ppermute x1, waiting for transfers between devices, body(): both = lax.ppermute(both, 'window', [(1, 3), (2, 0)])  6.29 us
    ppermute x1, starting transfers between devices, body(): over = lax.ppermute(over, 'window', [(0, 2), (3, 1)])  5.72 us
    ppermute x7, waiting for transfers between devices, moved(): return lax.ppermute(block, axis, route)  4.53 us
    ppermute x5, starting transfers between devices, swapped(): return lax.ppermute(block, axis, swaps(axis, first))  4.48 us
    pallas_call x1, Pallas kernels, body(): pl.pallas_call(lambda *refs: tangent_kernel(spaces, steps, nvar, levels,...  3.57 us
    pallas_call x1, Pallas kernels, body(): pl.pallas_call(lambda *refs: adjoint_kernel(windows, spaces, steps, nvar,...  2.9 us
    ppermute x1, starting transfers between devices, body(): both = lax.ppermute(both, 'window', [(1, 3), (2, 0)])  1.29 us
  transfers between devices with their start and end apart: 14, of which 7 were waited for; matrix products, arithmetic and copies ran while one was open for 0% of the time, Pallas kernels for 12%

profile of v7, /device:TPU:0, one launch (start us, length us, event | category | flops | bytes accessed | tf_op | source)
XLA Modules:
  0.0 54.8 jit_solution(2223900169696357208)
XLA Ops:
  0.7 0.7 %pad.4.refs_0_ = f32[8,128]{1,0:T(8,128)S(1)} pad(f32[4,5]{1,0:T(4,128)} %bitcast.3, f32[]{:T(128)} %constant.2.clone.1), padding=0_4x0_123 | pad | bytes 4180 | tf_op jit(solution)/shard_map/jit(_pad)/pad | solution.py:681
  1.4 1.1 %copy-done = bf16[4,4,5,4,8,96]{5,4,3,2,1,0:T(8,128)(2,1)S(1)} copy-done((bf16[4,4,5,4,8,96]{5,4,3,2,1,0:T(8,128)(2,1)S(1)}, bf16[4,4,5,4,8,96]{5,4,3,2,1,0:T(8,128)(2,1)}, u32[]{:S(2)}) %copy-start) | copy-done | bytes 491544
  2.5 0.1 shard_map.123
  2.6 3.1 %collective-permute-start = (bf16[61,8,128]{2,1,0:T(8,128)(2,1)S(1)}, bf16[61,8,128]{2,1,0:T(8,128)(2,1)S(1)}, u32[]{:S(2)}, u32[]{:S(2)}) collective-permute-start(bf16[61,8,128]{2,1,0:T(8,128)(2,1)S(1)} %shard_map.123), channel_id=1, source_target_pairs={{0,4},{4,8},{8,12},{12,0},{1,5},{5,9},{9,13},{13,1},{2,6},{6,10},{... | collective-permute-start | bytes 374792 | tf_op jit(solution)/shard_map/ppermute | solution.py:641
  5.8 2.7 %collective-permute-start.1 = (bf16[61,8,128]{2,1,0:T(8,128)(2,1)S(1)}, bf16[61,8,128]{2,1,0:T(8,128)(2,1)S(1)}, u32[]{:S(2)}, u32[]{:S(2)}) collective-permute-start(bf16[61,8,128]{2,1,0:T(8,128)(2,1)S(1)} %shard_map.124), channel_id=1, source_target_pairs={{0,8},{4,12},{8,0},{12,4},{1,9},{5,13},{9,1},{13,5},{2,10},{6,14},... | collective-permute-start | bytes 374792 | tf_op jit(solution)/shard_map/ppermute | solution.py:641
  8.5 1.4 %collective-permute-start.2 = (bf16[61,8,128]{2,1,0:T(8,128)(2,1)S(1)}, bf16[61,8,128]{2,1,0:T(8,128)(2,1)S(1)}, u32[]{:S(2)}, u32[]{:S(2)}) collective-permute-start(bf16[61,8,128]{2,1,0:T(8,128)(2,1)S(1)} %shard_map.125), channel_id=1, source_target_pairs={{0,12},{4,0},{8,4},{12,8},{1,13},{5,1},{9,5},{13,9},{2,14},{6,2},{... | collective-permute-start | bytes 374792 | tf_op jit(solution)/shard_map/ppermute | solution.py:641
  10.0 0.5 shard_map.126
  10.5 0.7 %collective-permute-start.4 = (s16[2,21,16,128]{3,2,1,0:T(8,128)(2,1)S(1)}, s16[2,21,16,128]{3,2,1,0:T(8,128)(2,1)S(1)}, u32[]{:S(2)}, u32[]{:S(2)}) collective-permute-start(s16[2,21,16,128]{3,2,1,0:T(8,128)(2,1)S(1)} %get-tuple-element.31), channel_id=1, source_target_pairs={{1,2},{2,1},{5,6},{6,5},{9,10},{10,9},{13,14},{14,13},{17,18},{18,... | collective-permute-start | bytes 516104 | tf_op jit(solution)/shard_map/ppermute | solution.py:652
  12.0 0.7 %shard_map.121 = (f32[4,4,3,8,128]{4,3,2,1,0:T(8,128)S(1)}, f32[4,4,8,128]{3,2,1,0:T(8,128)S(1)}, f32[5,5,8,128]{3,2,1,0:T(8,128)S(1)}) custom-call(s32[1]{0:T(128)S(6)} %copy.13.refs_0_, f32[1,4,4]{2,1,0:T(4,128)S(1)} %copy-done.8, f32[5,5]{1,0:T(8,128)S(1)} %copy-done.7, f32[1,4,4,8,384]{4,3,2,1,0:T(8,128)S(1)} %copy-done.3, f32[1,4,4,8,384]{4,3,2,1,0:T(8,128)S(1)} %copy-done.6), custom_call_target="tpu_custom_call" | custom-call | tf_op jit(solution)/shard_map/pallas_call | solution.py:725
  12.7 3.8 %collective-permute-done.1.refs_2_ = bf16[61,8,128]{2,1,0:T(8,128)(2,1)S(1)} collective-permute-done((bf16[61,8,128]{2,1,0:T(8,128)(2,1)S(1)}, bf16[61,8,128]{2,1,0:T(8,128)(2,1)S(1)}, u32[]{:S(2)}, u32[]{:S(2)}) %collective-permute-start.1) | collective-permute-done | bytes 124960 | tf_op jit(solution)/shard_map/ppermute | solution.py:641
  16.5 0.5 shard_map.128
  17.0 0.7 %collective-permute-start.7 = (bf16[31,8,384]{2,1,0:T(8,128)(2,1)S(1)}, bf16[31,8,384]{2,1,0:T(8,128)(2,1)S(1)}, u32[]{:S(2)}, u32[]{:S(2)}) collective-permute-start(bf16[31,8,384]{2,1,0:T(8,128)(2,1)S(1)} %get-tuple-element.38), channel_id=1, source_target_pairs={{1,2},{2,1},{5,6},{6,5},{9,10},{10,9},{13,14},{14,13},{17,18},{18,... | collective-permute-start | bytes 571400 | tf_op jit(solution)/shard_map/ppermute | solution.py:652
  17.7 0.3 shard_map.127
  18.0 1.3 %collective-permute-start.8 = (s16[2,16,16,128]{3,2,1,0:T(8,128)(2,1)S(1)}, s16[2,16,16,128]{3,2,1,0:T(8,128)(2,1)S(1)}, u32[]{:S(2)}, u32[]{:S(2)}) collective-permute-start(s16[2,16,16,128]{3,2,1,0:T(8,128)(2,1)S(1)} %get-tuple-element.40), channel_id=1, source_target_pairs={{4,0},{8,4},{12,8},{5,1},{9,5},{13,9},{6,2},{10,6},{14,10},{7,3},{... | collective-permute-start | bytes 393224 | tf_op jit(solution)/shard_map/ppermute | solution.py:641
  19.3 1.3 %collective-permute-start.9 = (s16[2,16,16,128]{3,2,1,0:T(8,128)(2,1)S(1)}, s16[2,16,16,128]{3,2,1,0:T(8,128)(2,1)S(1)}, u32[]{:S(2)}, u32[]{:S(2)}) collective-permute-start(s16[2,16,16,128]{3,2,1,0:T(8,128)(2,1)S(1)} %get-tuple-element.41), channel_id=1, source_target_pairs={{4,0},{8,4},{12,8},{5,1},{9,5},{13,9},{6,2},{10,6},{14,10},{7,3},{... | collective-permute-start | bytes 393224 | tf_op jit(solution)/shard_map/ppermute | solution.py:641
  20.6 3.0 %collective-permute-start.5 = (bf16[2,10,8,384]{3,2,1,0:T(8,128)(2,1)S(1)}, bf16[2,10,8,384]{3,2,1,0:T(8,128)(2,1)S(1)}, u32[]{:S(2)}, u32[]{:S(2)}) collective-permute-start(bf16[2,10,8,384]{3,2,1,0:T(8,128)(2,1)S(1)} %get-tuple-element.36), channel_id=1, source_target_pairs={{0,1},{1,0},{2,3},{3,2},{4,5},{5,4},{6,7},{7,6},{8,9},{9,8},{10,11... | collective-permute-start | bytes 368648 | tf_op jit(solution)/shard_map/ppermute | solution.py:652
  23.6 0.1 shard_map.129.refs_7_
  23.8 0.8 %collective-permute-done.5.refs_4_ = bf16[2,10,8,384]{3,2,1,0:T(8,128)(2,1)S(1)} collective-permute-done((bf16[2,10,8,384]{3,2,1,0:T(8,128)(2,1)S(1)}, bf16[2,10,8,384]{3,2,1,0:T(8,128)(2,1)S(1)}, u32[]{:S(2)}, u32[]{:S(2)}) %collective-permute-start.5) | collective-permute-done | bytes 122912 | tf_op jit(solution)/shard_map/ppermute | solution.py:652
  24.5 0.4 collective-permute-done.6.refs_5_
  24.9 3.6 %shard_map.130 = (f32[1,4,4,8,384]{4,3,2,1,0:T(8,128)}, f32[4,5,3,8,128]{4,3,2,1,0:T(8,128)S(1)}, f32[4,4,5,3,16,128]{5,4,3,2,1,0:T(8,128)S(1)}) custom-call(f32[5,5,8,128]{3,2,1,0:T(8,128)S(1)} %get-tuple-element.28.refs_4_.refs_0_, f32[4,4,8,128]{3,2,1,0:T(8,128)S(1)} %get-tuple-element.33.refs_1_, f32[4,4,3,8,128]{4,3,2,1,0:T(8,128)S(1)} %get-tuple-element.34.refs_2_, ...), custom_call_target="tpu_custom_call" | custom-call | tf_op jit(solution)/shard_map/pallas_call | solution.py:761
  28.5 0.6 %collective-permute-done.9.refs_5_ = s16[2,16,16,128]{3,2,1,0:T(8,128)(2,1)S(1)} collective-permute-done((s16[2,16,16,128]{3,2,1,0:T(8,128)(2,1)S(1)}, s16[2,16,16,128]{3,2,1,0:T(8,128)(2,1)S(1)}, u32[]{:S(2)}, u32[]{:S(2)}) %collective-permute-start.9) | collective-permute-done | bytes 131104 | tf_op jit(solution)/shard_map/ppermute | solution.py:641
  29.0 0.2 shard_map.131
  29.2 2.9 %shard_map.132 = (f32[5,4,8,384]{3,2,1,0:T(8,128)S(1)}, f32[5,4,8,384]{3,2,1,0:T(8,128)S(1)}, s16[2,16,16,128]{3,2,1,0:T(8,128)(2,1)S(1)}, s16[2,16,16,128]{3,2,...) custom-call(f32[5,5,8,128]{3,2,1,0:T(8,128)S(1)} %get-tuple-element.28.refs_4_.refs_0_, ...), custom_call_target="tpu_custom_call" | custom-call | tf_op jit(solution)/shard_map/pallas_call | solution.py:782
  32.1 5.7 %collective-permute-start.10 = (s16[2,16,16,128]{3,2,1,0:T(8,128)(2,1)S(1)}, s16[2,16,16,128]{3,2,1,0:T(8,128)(2,1)S(1)}, u32[]{:S(2)}, u32[]{:S(2)}) collective-permute-start(s16[2,16,16,128]{3,2,1,0:T(8,128)(2,1)S(1)} %get-tuple-element.45.refs_2_), channel_id=1, source_target_pairs={{0,4},{4,8},{8,12},{1,5},{5,9},{9,13},{2,6},{6,10},{10,14},{3,7},{... | collective-permute-start | bytes 393224 | tf_op jit(solution)/shard_map/ppermute | solution.py:641
  37.8 1.3 %collective-permute-start.11 = (s16[2,16,16,128]{3,2,1,0:T(8,128)(2,1)S(1)}, s16[2,16,16,128]{3,2,1,0:T(8,128)(2,1)S(1)}, u32[]{:S(2)}, u32[]{:S(2)}) collective-permute-start(s16[2,16,16,128]{3,2,1,0:T(8,128)(2,1)S(1)} %get-tuple-element.46.refs_3_), channel_id=1, source_target_pairs={{4,0},{8,4},{12,8},{5,1},{9,5},{13,9},{6,2},{10,6},{14,10},{7,3},{... | collective-permute-start | bytes 393224 | tf_op jit(solution)/shard_map/ppermute | solution.py:641
  39.1 5.7 %collective-permute-start.12 = (s16[2,16,16,128]{3,2,1,0:T(8,128)(2,1)S(1)}, s16[2,16,16,128]{3,2,1,0:T(8,128)(2,1)S(1)}, u32[]{:S(2)}, u32[]{:S(2)}) collective-permute-start(s16[2,16,16,128]{3,2,1,0:T(8,128)(2,1)S(1)} %get-tuple-element.47), channel_id=1, source_target_pairs={{0,8},{12,4},{1,9},{13,5},{2,10},{14,6},{3,11},{15,7},{16,24},{28,... | collective-permute-start | bytes 393224 | tf_op jit(solution)/shard_map/ppermute | solution.py:797
  44.9 0.2 collective-permute-done.11.refs_1_
  45.0 0.4 shard_map.133
  45.4 1.3 %collective-permute-start.13 = (s16[2,16,16,128]{3,2,1,0:T(8,128)(2,1)S(1)}, s16[2,16,16,128]{3,2,1,0:T(8,128)(2,1)S(1)}, u32[]{:S(2)}, u32[]{:S(2)}) collective-permute-start(s16[2,16,16,128]{3,2,1,0:T(8,128)(2,1)S(1)} %shard_map.133), channel_id=1, source_target_pairs={{4,12},{8,0},{5,13},{9,1},{6,14},{10,2},{7,15},{11,3},{20,28},{24,... | collective-permute-start | bytes 393224 | tf_op jit(solution)/shard_map/ppermute | solution.py:805
  46.7 0.6 %collective-permute-done.12.refs_2_ = s16[2,16,16,128]{3,2,1,0:T(8,128)(2,1)S(1)} collective-permute-done((s16[2,16,16,128]{3,2,1,0:T(8,128)(2,1)S(1)}, s16[2,16,16,128]{3,2,1,0:T(8,128)(2,1)S(1)}, u32[]{:S(2)}, u32[]{:S(2)}) %collective-permute-start.12) | collective-permute-done | bytes 131104 | tf_op jit(solution)/shard_map/ppermute | solution.py:797
  47.4 6.3 %collective-permute-done.13.refs_3_ = s16[2,16,16,128]{3,2,1,0:T(8,128)(2,1)S(1)} collective-permute-done((s16[2,16,16,128]{3,2,1,0:T(8,128)(2,1)S(1)}, s16[2,16,16,128]{3,2,1,0:T(8,128)(2,1)S(1)}, u32[]{:S(2)}, u32[]{:S(2)}) %collective-permute-start.13) | collective-permute-done | bytes 131104 | tf_op jit(solution)/shard_map/ppermute | solution.py:805
  53.6 1.1 %shard_map.134 = (f32[1,5,4,8,384]{4,3,2,1,0:T(8,128)}, f32[1,5,4,8,384]{4,3,2,1,0:T(8,128)}) custom-call(s16[2,16,16,128]{3,2,1,0:T(8,128)(2,1)S(1)} %collective-permute-done.10.refs_0_, s16[2,16,16,128]{3,2,1,0:T(8,128)(2,1)S(1)} %collective-permute-done.11.refs_1_, s16[2,16,16,128]{3,2,1,0:T(8,128)(2,1)S(1)} %collective-permute-done.12.refs_2_, ...), custom_call_target="tpu_custom_call" | custom-call | tf_op jit(solution)/shard_map/pallas_call | solution.py:810
  (29 shorter events, 0.5 us)
Async XLA Ops:
  0.6 11.3 %copy-start.8 = (f32[1,4,4]{2,1,0:T(4,128)S(1)}, f32[1,4,4]{2,1,0:T(4,128)}, u32[]{:S(2)}) copy-start(f32[1,4,4]{2,1,0:T(4,128)} %refs_1_.6) | copy-start | bytes 196
  0.6 11.3 %copy-start.7 = (f32[5,5]{1,0:T(8,128)S(1)}, f32[5,5]{1,0:T(8,128)}, u32[]{:S(2)}) copy-start(f32[5,5]{1,0:T(8,128)} %refs_2_.3) | copy-start | bytes 304
  1.3 1.1 %copy-start = (bf16[4,4,5,4,8,96]{5,4,3,2,1,0:T(8,128)(2,1)S(1)}, bf16[4,4,5,4,8,96]{5,4,3,2,1,0:T(8,128)(2,1)}, u32[]{:S(2)}) copy-start(bf16[4,4,5,4,8,96]{5,4,3,2,1,0:T(8,128)(2,1)} %refs_1_.10) | copy-start | bytes 1474564
  2.4 7.5 %copy-start.2 = (f32[1,5,4,8,384]{4,3,2,1,0:T(8,128)S(1)}, f32[1,5,4,8,384]{4,3,2,1,0:T(8,128)}, u32[]{:S(2)}) copy-start(f32[1,5,4,8,384]{4,3,2,1,0:T(8,128)} %refs_6_.1) | copy-start | bytes 737284
  2.4 7.5 %copy-start.3 = (f32[1,4,4,8,384]{4,3,2,1,0:T(8,128)S(1)}, f32[1,4,4,8,384]{4,3,2,1,0:T(8,128)}, u32[]{:S(2)}) copy-start(f32[1,4,4,8,384]{4,3,2,1,0:T(8,128)} %refs_3_.3) | copy-start | bytes 589828
  2.4 7.5 %copy-start.4 = (f32[1,5,4,8,384]{4,3,2,1,0:T(8,128)S(1)}, f32[1,5,4,8,384]{4,3,2,1,0:T(8,128)}, u32[]{:S(2)}) copy-start(f32[1,5,4,8,384]{4,3,2,1,0:T(8,128)} %refs_8_.1) | copy-start | bytes 737284
  2.4 8.7 %copy-start.1 = (bf16[4,4,5,4,8,96]{5,4,3,2,1,0:T(8,128)(2,1)S(1)}, bf16[4,4,5,4,8,96]{5,4,3,2,1,0:T(8,128)(2,1)}, u32[]{:S(2)}) copy-start(bf16[4,4,5,4,8,96]{5,4,3,2,1,0:T(8,128)(2,1)} %refs_1_.10) | copy-start | bytes 1474564
  2.4 9.5 %copy-start.6 = (f32[1,4,4,8,384]{4,3,2,1,0:T(8,128)S(1)}, f32[1,4,4,8,384]{4,3,2,1,0:T(8,128)}, u32[]{:S(2)}) copy-start(f32[1,4,4,8,384]{4,3,2,1,0:T(8,128)} %refs_4_.1) | copy-start | bytes 589828
  2.6 10.1 %collective-permute-start = (bf16[61,8,128]{2,1,0:T(8,128)(2,1)S(1)}, bf16[61,8,128]{2,1,0:T(8,128)(2,1)S(1)}, u32[]{:S(2)}, u32[]{:S(2)}) collective-permute-start(bf16[61,8,128]{2,1,0:T(8,128)(2,1)S(1)} %shard_map.123), channel_id=1, source_target_pairs={{0,4},{4,8},{8,12},{12,0},{1,5},{5,9},{9,13},{13,1},{2,6},{6,10},{... | collective-permute-start | bytes 374792 | tf_op jit(solution)/shard_map/ppermute | solution.py:641
  5.8 10.7 %collective-permute-start.1 = (bf16[61,8,128]{2,1,0:T(8,128)(2,1)S(1)}, bf16[61,8,128]{2,1,0:T(8,128)(2,1)S(1)}, u32[]{:S(2)}, u32[]{:S(2)}) collective-permute-start(bf16[61,8,128]{2,1,0:T(8,128)(2,1)S(1)} %shard_map.124), channel_id=1, source_target_pairs={{0,8},{4,12},{8,0},{12,4},{1,9},{5,13},{9,1},{13,5},{2,10},{6,14},... | collective-permute-start | bytes 374792 | tf_op jit(solution)/shard_map/ppermute | solution.py:641
  8.5 8.0 %collective-permute-start.2 = (bf16[61,8,128]{2,1,0:T(8,128)(2,1)S(1)}, bf16[61,8,128]{2,1,0:T(8,128)(2,1)S(1)}, u32[]{:S(2)}, u32[]{:S(2)}) collective-permute-start(bf16[61,8,128]{2,1,0:T(8,128)(2,1)S(1)} %shard_map.125), channel_id=1, source_target_pairs={{0,12},{4,0},{8,4},{12,8},{1,13},{5,1},{9,5},{13,9},{2,14},{6,2},{... | collective-permute-start | bytes 374792 | tf_op jit(solution)/shard_map/ppermute | solution.py:641
  10.4 7.2 %collective-permute-start.3 = (s16[2,21,16,128]{3,2,1,0:T(8,128)(2,1)S(1)}, s16[2,21,16,128]{3,2,1,0:T(8,128)(2,1)S(1)}, u32[]{:S(2)}, u32[]{:S(2)}) collective-permute-start(s16[2,21,16,128]{3,2,1,0:T(8,128)(2,1)S(1)} %get-tuple-element.30), channel_id=1, source_target_pairs={{0,1},{1,0},{2,3},{3,2},{4,5},{5,4},{6,7},{7,6},{8,9},{9,8},{10,11... | collective-permute-start | bytes 516104 | tf_op jit(solution)/shard_map/ppermute | solution.py:652
  10.5 7.2 %collective-permute-start.4 = (s16[2,21,16,128]{3,2,1,0:T(8,128)(2,1)S(1)}, s16[2,21,16,128]{3,2,1,0:T(8,128)(2,1)S(1)}, u32[]{:S(2)}, u32[]{:S(2)}) collective-permute-start(s16[2,21,16,128]{3,2,1,0:T(8,128)(2,1)S(1)} %get-tuple-element.31), channel_id=1, source_target_pairs={{1,2},{2,1},{5,6},{6,5},{9,10},{10,9},{13,14},{14,13},{17,18},{18,... | collective-permute-start | bytes 516104 | tf_op jit(solution)/shard_map/ppermute | solution.py:652
  17.0 7.9 %collective-permute-start.7 = (bf16[31,8,384]{2,1,0:T(8,128)(2,1)S(1)}, bf16[31,8,384]{2,1,0:T(8,128)(2,1)S(1)}, u32[]{:S(2)}, u32[]{:S(2)}) collective-permute-start(bf16[31,8,384]{2,1,0:T(8,128)(2,1)S(1)} %get-tuple-element.38), channel_id=1, source_target_pairs={{1,2},{2,1},{5,6},{6,5},{9,10},{10,9},{13,14},{14,13},{17,18},{18,... | collective-permute-start | bytes 571400 | tf_op jit(solution)/shard_map/ppermute | solution.py:652
  18.0 10.5 %collective-permute-start.8 = (s16[2,16,16,128]{3,2,1,0:T(8,128)(2,1)S(1)}, s16[2,16,16,128]{3,2,1,0:T(8,128)(2,1)S(1)}, u32[]{:S(2)}, u32[]{:S(2)}) collective-permute-start(s16[2,16,16,128]{3,2,1,0:T(8,128)(2,1)S(1)} %get-tuple-element.40), channel_id=1, source_target_pairs={{4,0},{8,4},{12,8},{5,1},{9,5},{13,9},{6,2},{10,6},{14,10},{7,3},{... | collective-permute-start | bytes 393224 | tf_op jit(solution)/shard_map/ppermute | solution.py:641
  19.3 9.8 %collective-permute-start.9 = (s16[2,16,16,128]{3,2,1,0:T(8,128)(2,1)S(1)}, s16[2,16,16,128]{3,2,1,0:T(8,128)(2,1)S(1)}, u32[]{:S(2)}, u32[]{:S(2)}) collective-permute-start(s16[2,16,16,128]{3,2,1,0:T(8,128)(2,1)S(1)} %get-tuple-element.41), channel_id=1, source_target_pairs={{4,0},{8,4},{12,8},{5,1},{9,5},{13,9},{6,2},{10,6},{14,10},{7,3},{... | collective-permute-start | bytes 393224 | tf_op jit(solution)/shard_map/ppermute | solution.py:641
  20.6 8.6 %copy-start.5 = (f32[1,5,4,8,384]{4,3,2,1,0:T(8,128)S(1)}, f32[1,5,4,8,384]{4,3,2,1,0:T(8,128)}, u32[]{:S(2)}) copy-start(f32[1,5,4,8,384]{4,3,2,1,0:T(8,128)} %refs_7_.1) | copy-start | bytes 737284
  20.6 4.0 %collective-permute-start.5 = (bf16[2,10,8,384]{3,2,1,0:T(8,128)(2,1)S(1)}, bf16[2,10,8,384]{3,2,1,0:T(8,128)(2,1)S(1)}, u32[]{:S(2)}, u32[]{:S(2)}) collective-permute-start(bf16[2,10,8,384]{3,2,1,0:T(8,128)(2,1)S(1)} %get-tuple-element.36), channel_id=1, source_target_pairs={{0,1},{1,0},{2,3},{3,2},{4,5},{5,4},{6,7},{7,6},{8,9},{9,8},{10,11... | collective-permute-start | bytes 368648 | tf_op jit(solution)/shard_map/ppermute | solution.py:652
  23.6 1.3 %collective-permute-start.6 = (bf16[2,10,8,384]{3,2,1,0:T(8,128)(2,1)S(1)}, bf16[2,10,8,384]{3,2,1,0:T(8,128)(2,1)S(1)}, u32[]{:S(2)}, u32[]{:S(2)}) collective-permute-start(bf16[2,10,8,384]{3,2,1,0:T(8,128)(2,1)S(1)} %get-tuple-element.37), channel_id=1, source_target_pairs={{0,1},{1,0},{2,3},{3,2},{4,5},{5,4},{6,7},{7,6},{8,9},{9,8},{10,11... | collective-permute-start | bytes 368648 | tf_op jit(solution)/shard_map/ppermute | solution.py:652
  32.1 12.7 %collective-permute-start.10 = (s16[2,16,16,128]{3,2,1,0:T(8,128)(2,1)S(1)}, s16[2,16,16,128]{3,2,1,0:T(8,128)(2,1)S(1)}, u32[]{:S(2)}, u32[]{:S(2)}) collective-permute-start(s16[2,16,16,128]{3,2,1,0:T(8,128)(2,1)S(1)} %get-tuple-element.45.refs_2_), channel_id=1, source_target_pairs={{0,4},{4,8},{8,12},{1,5},{5,9},{9,13},{2,6},{6,10},{10,14},{3,7},{... | collective-permute-start | bytes 393224 | tf_op jit(solution)/shard_map/ppermute | solution.py:641
  37.8 7.2 %collective-permute-start.11 = (s16[2,16,16,128]{3,2,1,0:T(8,128)(2,1)S(1)}, s16[2,16,16,128]{3,2,1,0:T(8,128)(2,1)S(1)}, u32[]{:S(2)}, u32[]{:S(2)}) collective-permute-start(s16[2,16,16,128]{3,2,1,0:T(8,128)(2,1)S(1)} %get-tuple-element.46.refs_3_), channel_id=1, source_target_pairs={{4,0},{8,4},{12,8},{5,1},{9,5},{13,9},{6,2},{10,6},{14,10},{7,3},{... | collective-permute-start | bytes 393224 | tf_op jit(solution)/shard_map/ppermute | solution.py:641
  39.1 8.2 %collective-permute-start.12 = (s16[2,16,16,128]{3,2,1,0:T(8,128)(2,1)S(1)}, s16[2,16,16,128]{3,2,1,0:T(8,128)(2,1)S(1)}, u32[]{:S(2)}, u32[]{:S(2)}) collective-permute-start(s16[2,16,16,128]{3,2,1,0:T(8,128)(2,1)S(1)} %get-tuple-element.47), channel_id=1, source_target_pairs={{0,8},{12,4},{1,9},{13,5},{2,10},{14,6},{3,11},{15,7},{16,24},{28,... | collective-permute-start | bytes 393224 | tf_op jit(solution)/shard_map/ppermute | solution.py:797
  45.4 8.2 %collective-permute-start.13 = (s16[2,16,16,128]{3,2,1,0:T(8,128)(2,1)S(1)}, s16[2,16,16,128]{3,2,1,0:T(8,128)(2,1)S(1)}, u32[]{:S(2)}, u32[]{:S(2)}) collective-permute-start(s16[2,16,16,128]{3,2,1,0:T(8,128)(2,1)S(1)} %shard_map.133), channel_id=1, source_target_pairs={{4,12},{8,0},{5,13},{9,1},{6,14},{10,2},{7,15},{11,3},{20,28},{24,... | collective-permute-start | bytes 393224 | tf_op jit(solution)/shard_map/ppermute | solution.py:805

commit v8 on v7

--- a/solution.py
+++ b/solution.py
@@ -231,7 +231,7 @@
 
 def assemble_kernel(windows, steps, nvar, levels, part, *refs):
     pieces = refs[:windows]
-    own_ref, early_ref, late_ref, far_ref, stack_ref = refs[windows + 1 :]
+    own_ref, near_ref, far_ref, stack_ref = refs[windows + 1 :]
     me = lax.axis_index("window")
     even = even_place()
     lane = lane_index()
@@ -264,11 +264,7 @@
             for i in range(pairs):
                 halves = [joined_halves(a, b) for a, b in zip(built[j, 2 * i], built[j, 2 * i + 1])]
                 last, start = (jnp.concatenate([h[k] for h in halves], 1) for k in range(2))
-                near = jnp.where(even, last, start).astype(jnp.bfloat16)
-                if j < steps // 2:
-                    early_ref[j, v * pairs + i] = near
-                else:
-                    late_ref[j - steps // 2, v * pairs + i] = near
+                near_ref[j, v * pairs + i] = jnp.where(even, last, start).astype(jnp.bfloat16)
                 if not is_quarter(j, v, steps):
                     far_ref[base[j, v] + i] = jnp.where(even, start, last).astype(jnp.bfloat16)
             if is_quarter(j, v, steps):
@@ -385,7 +381,7 @@
 
 def tangent_kernel(
     spaces, steps, nvar, levels, tiles,
-    mix_ref, share_ref, obs_ref, own_ref, early_ref, late_ref, far_ref, first_ref,
+    mix_ref, share_ref, obs_ref, own_ref, near_ref, far_ref, first_ref,
     ndo_ref, ends_ref, x_ref, s_ref,
 ):
     lane, row = lane_index(), row_index()
@@ -399,11 +395,10 @@
     for lev in range(levels):
         i, odd = lev // 2, lev % 2
         for j in range(steps):
-            near_ref = early_ref if j < steps // 2 else late_ref
             for v in range(nvar):
                 for t in range(tiles):
                     own = own_ref[j, v * levels + lev, :, cuts[t]].astype(jnp.float32)
-                    near = near_ref[j % (steps // 2), v * pairs + i, :, cuts[t]].astype(jnp.float32)
+                    near = near_ref[j, v * pairs + i, :, cuts[t]].astype(jnp.float32)
                     quarter = is_quarter(j, v, steps)
                     far = far_ref[base[j, v] + lev // (4 if quarter else 2), :, cuts[t]]
                     far = far.astype(jnp.float32)
@@ -552,39 +547,8 @@
         return outer
 
     lax.fori_loop(0, pairs, pair, 0)
-    if windows == 4:
-        later_ref, earlier_ref, over_ref = payload_refs
-        later_ref[...] = q_ref[1]
-        earlier_ref[...] = q_ref[0]
-        over_ref[...] = q_ref[jnp.where(me == 0, 1, 0)]
-    else:
-        for d in range(1, windows):
-            payload_refs[d - 1][...] = q_ref[jnp.where(me + d >= windows, 0, 1)]
-
-
-def join_kernel(nvar, tiles, right_ref, left_ref, later_ref, earlier_ref, out_ref):
-    upward = lax.axis_index("window") == 1
-
-    def pair(i, carry):
-        def summed(ref, other_ref):
-            codes = [
-                jnp.where(upward, floats(ref[i, n]), floats(other_ref[i, n]))
-                for n in range(nvar * tiles + 1)
-            ]
-            scales = jnp.exp2(codes[-1]) * (1.0 / CODE_MAX)
-            return [
-                [codes[v * tiles + t] * scales[:, v : v + 1] for t in range(tiles)]
-                for v in range(nvar)
-            ]
-
-        mine, other = summed(later_ref, earlier_ref), summed(right_ref, left_ref)
-        planes = [[a + b for a, b in zip(x, y)] for x, y in zip(mine, other)]
-        values, scales = row_codes(planes)
-        for n, value in enumerate(values + [scales]):
-            out_ref[i, n] = shorts(value)
-        return carry
-
-    lax.fori_loop(0, out_ref.shape[0], pair, 0)
+    for d in range(1, windows):
+        payload_refs[d - 1][...] = q_ref[jnp.where(me + d >= windows, 0, 1)]
 
 
 def final_kernel(windows, nvar, levels, tiles, *refs):
@@ -593,10 +557,7 @@
     me = lax.axis_index("window")
     pairs = levels // 2
     cuts = [slice(t * LANES, (t + 1) * LANES) for t in range(tiles)]
-    if windows == 4:
-        from_later = [False, True, me < 2, me < 2]
-    else:
-        from_later = [d > me for d in range(1, windows)]
+    from_later = [d > me for d in range(1, windows)]
 
     def pair(i, carry):
         tails = [None] * (nvar * tiles)
@@ -612,13 +573,8 @@
                 for t in range(tiles):
                     n = v * tiles + t
                     value = floats(piece[i, n]) * scale
-                    if later is True:
-                        add(tails, n, value)
-                    elif later is False:
-                        add(heads, n, value)
-                    else:
-                        add(tails, n, jnp.where(later, value, 0.0))
-                        add(heads, n, jnp.where(later, 0.0, value))
+                    add(tails, n, jnp.where(later, value, 0.0))
+                    add(heads, n, jnp.where(later, 0.0, value))
         for v in range(nvar):
             for odd in range(2):
                 lev = 2 * i + odd
@@ -734,22 +690,19 @@
         compiler_params=params(),
     )(obs_count, obs_var, coupling, dual_obs, innovation)
 
-    half_steps = shape((steps // 2, nvar * pairs, rows, columns), bf16)
-    own, traj_early, traj_late, traj_far = pl.pallas_call(
+    own, traj_near, traj_far = pl.pallas_call(
         lambda *refs: assemble_kernel(windows, steps, nvar, levels, part, *refs),
         out_shape=[
             shape((steps, nvar * levels, rows, columns), bf16),
-            half_steps,
-            half_steps,
+            shape((steps, nvar * pairs, rows, columns), bf16),
             shape((far_base(steps, nvar, levels)[1], rows, columns), bf16),
         ],
         in_specs=[VMEM] * windows + [ANY],
-        out_specs=[VMEM] * 4,
+        out_specs=[VMEM] * 3,
         scratch_shapes=[pltpu.VMEM((windows, block.shape[0] - 1, rows, LANES), bf16)],
         compiler_params=params(),
     )(*blocks_here, mix)
-    traj_far = swapped(traj_far, "space", 1)
-    traj_early, traj_late = swapped(traj_early, "space", 0), swapped(traj_late, "space", 0)
+    traj_near, traj_far = swapped(traj_near, "space", 0), swapped(traj_far, "space", 1)
 
     first = pl.pallas_call(
         lambda *refs: prepare_tangent_kernel(nvar, levels, tiles, *refs),
@@ -765,11 +718,11 @@
             shape((levels, nvar, tiles, SUB, LANES), f32),
             shape((levels, steps, nvar, tiles, 2 * SUB, LANES), f32),
         ],
-        in_specs=[VMEM] * 8,
+        in_specs=[VMEM] * 7,
         out_specs=[VMEM] * 3,
         scratch_shapes=[pltpu.VMEM((2, 2, nvar, tiles, 4 * SUB, LANES), f32)],
         compiler_params=params(),
-    )(mix, share, obs, own, traj_early, traj_late, traj_far, first)
+    )(mix, share, obs, own, traj_near, traj_far, first)
 
     last, force = pl.pallas_call(
         lambda *refs: prepare_adjoint_kernel(steps, nvar, levels, tiles, *refs),
@@ -791,21 +744,8 @@
         ],
         compiler_params=params(),
     )(mix, totals, wide_traj, last, force, ends, increment, model_rhs, dual_model)
-    if windows == 4:
-        later, earlier, over = payloads
-        right, left = moved(later, "window", 1), moved(earlier, "window", -1)
-        over = lax.ppermute(over, "window", [(0, 2), (3, 1)])
-        both = pl.pallas_call(
-            lambda *refs: join_kernel(nvar, tiles, *refs),
-            out_shape=payload,
-            in_specs=[VMEM] * 4,
-            out_specs=VMEM,
-            compiler_params=params(),
-        )(right, left, later, earlier)
-        both = lax.ppermute(both, "window", [(1, 3), (2, 0)])
-        sent = [right, left, over, both]
-    else:
-        sent = [moved(payloads[d - 1], "window", d, around=True) for d in range(1, windows)]
+    sent = {d: moved(payloads[d - 1], "window", d, around=True) for d in order}
+    sent = [sent[d] for d in range(1, windows)]
 
     new_dual_model, new_increment = pl.pallas_call(
         lambda *refs: final_kernel(windows, nvar, levels, tiles, *refs),

time: 55.1 us -> 48.2 us (0.87); the launches traced: 54.8 us -> 47.3 us
  starting transfers between devices: 28.2 us -> 16.6 us
  waiting for transfers between devices: 12.5 us -> 17.1 us
    ppermute x7 -> x8, waiting for transfers between devices: 4.53 us -> 17.1 us  [moved(): return lax.ppermute(block, axis, route)]
    ppermute x2 -> x0, starting transfers between devices: 7.01 us -> none  [the longest x1 5.72 us: body(): over = lax.ppermute(over, 'window', [(0, 2), (3, 1)])]
    ppermute x2 -> x0, waiting for transfers between devices: 6.9 us -> none  [the longest x1 6.29 us: body(): both = lax.ppermute(both, 'window', [(1, 3), (2, 0)])]
    ppermute x5 -> x4, starting transfers between devices: 4.48 us -> 1.49 us  [swapped(): return lax.ppermute(block, axis, swaps(axis, first))]
    ppermute x7 -> x8, starting transfers between devices: 16.7 us -> 15.1 us  [moved(): return lax.ppermute(block, axis, route)]
    ppermute x5 -> x4, waiting for transfers between devices: 1.12 us -> 0.01 us  [swapped(): return lax.ppermute(block, axis, swaps(axis, first))]
  transfers between devices with their start and end apart: 14 -> 12, of which waited for: 7 -> 5; matrix products, arithmetic and copies ran while one was open for 0% -> 0% of each run, Pallas kernels for 12% -> 13%
where the time goes in v8:
time: 48.2 us; the launch traced here: 47.3 us
  waiting for transfers between devices  17.1 us (35%)
  starting transfers between devices  16.6 us (34%)
  Pallas kernels  10.2 us (21%)
  local copies, waits for them, and re-layouts  1.82 us (4%)
  between operations  1.53 us (3%)
    ppermute x8, waiting for transfers between devices, moved(): return lax.ppermute(block, axis, route)  17.1 us
    ppermute x8, starting transfers between devices, moved(): return lax.ppermute(block, axis, route)  15.1 us
    pallas_call x1, Pallas kernels, body(): pl.pallas_call(lambda *refs: tangent_kernel(spaces, steps, nvar, levels,...  3.57 us
    pallas_call x1, Pallas kernels, body(): pl.pallas_call(lambda *refs: adjoint_kernel(windows, spaces, steps, nvar,...  2.9 us
    ppermute x4, starting transfers between devices, swapped(): return lax.ppermute(block, axis, swaps(axis, first))  1.49 us
    unnamed x18, local copies, waits for them, and re-layouts  1.12 us
    pallas_call x1, Pallas kernels, body(): pl.pallas_call(lambda *refs: final_kernel(windows, nvar, levels, tiles, *...  1.09 us
  transfers between devices with their start and end apart: 12, of which 5 were waited for; matrix products, arithmetic and copies ran while one was open for 0% of the time, Pallas kernels for 13%

profile of v8, /device:TPU:0, one launch (start us, length us, event | category | flops | bytes accessed | tf_op | source)
XLA Modules:
  0.0 47.3 jit_solution(14898352255597433222)
XLA Ops:
  0.7 0.7 %pad.4.refs_0_ = f32[8,128]{1,0:T(8,128)S(1)} pad(f32[4,5]{1,0:T(4,128)} %bitcast.3, f32[]{:T(128)} %constant.2.clone.1), padding=0_4x0_123 | pad | bytes 4180 | tf_op jit(solution)/shard_map/jit(_pad)/pad | solution.py:637
  1.4 1.1 %copy-done = bf16[4,4,5,4,8,96]{5,4,3,2,1,0:T(8,128)(2,1)S(1)} copy-done((bf16[4,4,5,4,8,96]{5,4,3,2,1,0:T(8,128)(2,1)S(1)}, bf16[4,4,5,4,8,96]{5,4,3,2,1,0:T(8,128)(2,1)}, u32[]{:S(2)}) %copy-start) | copy-done | bytes 491544
  2.5 0.1 shard_map.123
  2.6 3.1 %collective-permute-start = (bf16[61,8,128]{2,1,0:T(8,128)(2,1)S(1)}, bf16[61,8,128]{2,1,0:T(8,128)(2,1)S(1)}, u32[]{:S(2)}, u32[]{:S(2)}) collective-permute-start(bf16[61,8,128]{2,1,0:T(8,128)(2,1)S(1)} %shard_map.123), channel_id=1, source_target_pairs={{0,4},{4,8},{8,12},{12,0},{1,5},{5,9},{9,13},{13,1},{2,6},{6,10},{... | collective-permute-start | bytes 374792 | tf_op jit(solution)/shard_map/ppermute | solution.py:597
  5.7 0.1 shard_map.124
  5.8 2.7 %collective-permute-start.1 = (bf16[61,8,128]{2,1,0:T(8,128)(2,1)S(1)}, bf16[61,8,128]{2,1,0:T(8,128)(2,1)S(1)}, u32[]{:S(2)}, u32[]{:S(2)}) collective-permute-start(bf16[61,8,128]{2,1,0:T(8,128)(2,1)S(1)} %shard_map.124), channel_id=1, source_target_pairs={{0,8},{4,12},{8,0},{12,4},{1,9},{5,13},{9,1},{13,5},{2,10},{6,14},... | collective-permute-start | bytes 374792 | tf_op jit(solution)/shard_map/ppermute | solution.py:597
  8.4 0.1 shard_map.125
  8.5 1.4 %collective-permute-start.2 = (bf16[61,8,128]{2,1,0:T(8,128)(2,1)S(1)}, bf16[61,8,128]{2,1,0:T(8,128)(2,1)S(1)}, u32[]{:S(2)}, u32[]{:S(2)}) collective-permute-start(bf16[61,8,128]{2,1,0:T(8,128)(2,1)S(1)} %shard_map.125), channel_id=1, source_target_pairs={{0,12},{4,0},{8,4},{12,8},{1,13},{5,1},{9,5},{13,9},{2,14},{6,2},{... | collective-permute-start | bytes 374792 | tf_op jit(solution)/shard_map/ppermute | solution.py:597
  10.0 0.5 shard_map.126
  10.4 0.1 collective-permute-start.3
  10.5 0.7 %collective-permute-start.4 = (s16[2,21,16,128]{3,2,1,0:T(8,128)(2,1)S(1)}, s16[2,21,16,128]{3,2,1,0:T(8,128)(2,1)S(1)}, u32[]{:S(2)}, u32[]{:S(2)}) collective-permute-start(s16[2,21,16,128]{3,2,1,0:T(8,128)(2,1)S(1)} %get-tuple-element.30), channel_id=1, source_target_pairs={{1,2},{2,1},{5,6},{6,5},{9,10},{10,9},{13,14},{14,13},{17,18},{18,... | collective-permute-start | bytes 516104 | tf_op jit(solution)/shard_map/ppermute | solution.py:608
  11.2 0.1 shard_map.122.refs_0_
  12.0 0.7 %shard_map.121 = (f32[4,4,3,8,128]{4,3,2,1,0:T(8,128)S(1)}, f32[4,4,8,128]{3,2,1,0:T(8,128)S(1)}, f32[5,5,8,128]{3,2,1,0:T(8,128)S(1)}) custom-call(s32[1]{0:T(128)S(6)} %copy.13.refs_0_, f32[1,4,4]{2,1,0:T(4,128)S(1)} %copy-done.8, f32[5,5]{1,0:T(8,128)S(1)} %copy-done.7, f32[1,4,4,8,384]{4,3,2,1,0:T(8,128)S(1)} %copy-done.3, f32[1,4,4,8,384]{4,3,2,1,0:T(8,128)S(1)} %copy-done.6), custom_call_target="tpu_custom_call" | custom-call | tf_op jit(solution)/shard_map/pallas_call | solution.py:681
  12.7 3.8 %collective-permute-done.1.refs_2_ = bf16[61,8,128]{2,1,0:T(8,128)(2,1)S(1)} collective-permute-done((bf16[61,8,128]{2,1,0:T(8,128)(2,1)S(1)}, bf16[61,8,128]{2,1,0:T(8,128)(2,1)S(1)}, u32[]{:S(2)}, u32[]{:S(2)}) %collective-permute-start.1) | collective-permute-done | bytes 124960 | tf_op jit(solution)/shard_map/ppermute | solution.py:597
  16.5 0.5 shard_map.128
  17.0 0.1 collective-permute-start.5
  17.1 0.7 %collective-permute-start.6 = (bf16[31,8,384]{2,1,0:T(8,128)(2,1)S(1)}, bf16[31,8,384]{2,1,0:T(8,128)(2,1)S(1)}, u32[]{:S(2)}, u32[]{:S(2)}) collective-permute-start(bf16[31,8,384]{2,1,0:T(8,128)(2,1)S(1)} %get-tuple-element.36), channel_id=1, source_target_pairs={{1,2},{2,1},{5,6},{6,5},{9,10},{10,9},{13,14},{14,13},{17,18},{18,... | collective-permute-start | bytes 571400 | tf_op jit(solution)/shard_map/ppermute | solution.py:608
  17.8 0.3 shard_map.127
  18.0 1.4 %collective-permute-start.7 = (s16[2,16,16,128]{3,2,1,0:T(8,128)(2,1)S(1)}, s16[2,16,16,128]{3,2,1,0:T(8,128)(2,1)S(1)}, u32[]{:S(2)}, u32[]{:S(2)}) collective-permute-start(s16[2,16,16,128]{3,2,1,0:T(8,128)(2,1)S(1)} %get-tuple-element.38), channel_id=1, source_target_pairs={{4,0},{8,4},{12,8},{5,1},{9,5},{13,9},{6,2},{10,6},{14,10},{7,3},{... | collective-permute-start | bytes 393224 | tf_op jit(solution)/shard_map/ppermute | solution.py:597
  19.5 1.3 %collective-permute-start.8 = (s16[2,16,16,128]{3,2,1,0:T(8,128)(2,1)S(1)}, s16[2,16,16,128]{3,2,1,0:T(8,128)(2,1)S(1)}, u32[]{:S(2)}, u32[]{:S(2)}) collective-permute-start(s16[2,16,16,128]{3,2,1,0:T(8,128)(2,1)S(1)} %get-tuple-element.39), channel_id=1, source_target_pairs={{4,0},{8,4},{12,8},{5,1},{9,5},{13,9},{6,2},{10,6},{14,10},{7,3},{... | collective-permute-start | bytes 393224 | tf_op jit(solution)/shard_map/ppermute | solution.py:597
  20.8 0.1 shard_map.129.refs_6_
  20.9 3.6 %shard_map.130 = (f32[1,4,4,8,384]{4,3,2,1,0:T(8,128)}, f32[4,5,3,8,128]{4,3,2,1,0:T(8,128)S(1)}, f32[4,4,5,3,16,128]{5,4,3,2,1,0:T(8,128)S(1)}) custom-call(f32[5,5,8,128]{3,2,1,0:T(8,128)S(1)} %get-tuple-element.27.refs_4_.refs_0_, f32[4,4,8,128]{3,2,1,0:T(8,128)S(1)} %get-tuple-element.32.refs_1_, f32[4,4,3,8,128]{4,3,2,1,0:T(8,128)S(1)} %get-tuple-element.33.refs_2_, ...), custom_call_target="tpu_custom_call" | custom-call | tf_op jit(solution)/shard_map/pallas_call | solution.py:714
  24.5 1.7 %collective-permute-done.7.refs_4_ = s16[2,16,16,128]{3,2,1,0:T(8,128)(2,1)S(1)} collective-permute-done((s16[2,16,16,128]{3,2,1,0:T(8,128)(2,1)S(1)}, s16[2,16,16,128]{3,2,1,0:T(8,128)(2,1)S(1)}, u32[]{:S(2)}, u32[]{:S(2)}) %collective-permute-start.7) | collective-permute-done | bytes 131104 | tf_op jit(solution)/shard_map/ppermute | solution.py:597
  26.2 3.1 %collective-permute-done.8.refs_5_ = s16[2,16,16,128]{3,2,1,0:T(8,128)(2,1)S(1)} collective-permute-done((s16[2,16,16,128]{3,2,1,0:T(8,128)(2,1)S(1)}, s16[2,16,16,128]{3,2,1,0:T(8,128)(2,1)S(1)}, u32[]{:S(2)}, u32[]{:S(2)}) %collective-permute-start.8) | collective-permute-done | bytes 131104 | tf_op jit(solution)/shard_map/ppermute | solution.py:597
  29.2 0.2 shard_map.131
  29.4 2.9 %shard_map.132 = (f32[5,4,8,384]{3,2,1,0:T(8,128)S(1)}, f32[5,4,8,384]{3,2,1,0:T(8,128)S(1)}, s16[2,16,16,128]{3,2,1,0:T(8,128)(2,1)S(1)}, s16[2,16,16,128]{3,2,...) custom-call(f32[5,5,8,128]{3,2,1,0:T(8,128)S(1)} %get-tuple-element.27.refs_4_.refs_0_, ...), custom_call_target="tpu_custom_call" | custom-call | tf_op jit(solution)/shard_map/pallas_call | solution.py:735
  32.3 2.3 %collective-permute-start.9 = (s16[2,16,16,128]{3,2,1,0:T(8,128)(2,1)S(1)}, s16[2,16,16,128]{3,2,1,0:T(8,128)(2,1)S(1)}, u32[]{:S(2)}, u32[]{:S(2)}) collective-permute-start(s16[2,16,16,128]{3,2,1,0:T(8,128)(2,1)S(1)} %get-tuple-element.43), channel_id=1, source_target_pairs={{0,4},{4,8},{8,12},{12,0},{1,5},{5,9},{9,13},{13,1},{2,6},{6,10},{... | collective-permute-start | bytes 393224 | tf_op jit(solution)/shard_map/ppermute | solution.py:597
  34.6 0.9 %collective-permute-start.10 = (s16[2,16,16,128]{3,2,1,0:T(8,128)(2,1)S(1)}, s16[2,16,16,128]{3,2,1,0:T(8,128)(2,1)S(1)}, u32[]{:S(2)}, u32[]{:S(2)}) collective-permute-start(s16[2,16,16,128]{3,2,1,0:T(8,128)(2,1)S(1)} %get-tuple-element.44), channel_id=1, source_target_pairs={{0,8},{4,12},{8,0},{12,4},{1,9},{5,13},{9,1},{13,5},{2,10},{6,14},... | collective-permute-start | bytes 393224 | tf_op jit(solution)/shard_map/ppermute | solution.py:597
  35.5 2.1 %collective-permute-start.11 = (s16[2,16,16,128]{3,2,1,0:T(8,128)(2,1)S(1)}, s16[2,16,16,128]{3,2,1,0:T(8,128)(2,1)S(1)}, u32[]{:S(2)}, u32[]{:S(2)}) collective-permute-start(s16[2,16,16,128]{3,2,1,0:T(8,128)(2,1)S(1)} %get-tuple-element.45), channel_id=1, source_target_pairs={{0,12},{4,0},{8,4},{12,8},{1,13},{5,1},{9,5},{13,9},{2,14},{6,2},{... | collective-permute-start | bytes 393224 | tf_op jit(solution)/shard_map/ppermute | solution.py:597
  37.6 2.7 %collective-permute-done.9.refs_0_ = s16[2,16,16,128]{3,2,1,0:T(8,128)(2,1)S(1)} collective-permute-done((s16[2,16,16,128]{3,2,1,0:T(8,128)(2,1)S(1)}, s16[2,16,16,128]{3,2,1,0:T(8,128)(2,1)S(1)}, u32[]{:S(2)}, u32[]{:S(2)}) %collective-permute-start.9) | collective-permute-done | bytes 131104 | tf_op jit(solution)/shard_map/ppermute | solution.py:597
  40.3 5.9 %collective-permute-done.10.refs_1_ = s16[2,16,16,128]{3,2,1,0:T(8,128)(2,1)S(1)} collective-permute-done((s16[2,16,16,128]{3,2,1,0:T(8,128)(2,1)S(1)}, s16[2,16,16,128]{3,2,1,0:T(8,128)(2,1)S(1)}, u32[]{:S(2)}, u32[]{:S(2)}) %collective-permute-start.10) | collective-permute-done | bytes 131104 | tf_op jit(solution)/shard_map/ppermute | solution.py:597
  46.2 1.1 %shard_map.133 = (f32[1,5,4,8,384]{4,3,2,1,0:T(8,128)}, f32[1,5,4,8,384]{4,3,2,1,0:T(8,128)}) custom-call(s16[2,16,16,128]{3,2,1,0:T(8,128)(2,1)S(1)} %collective-permute-done.9.refs_0_, s16[2,16,16,128]{3,2,1,0:T(8,128)(2,1)S(1)} %collective-permute-done.10.refs_1_, s16[2,16,16,128]{3,2,1,0:T(8,128)(2,1)S(1)} %collective-permute-done.11.refs_2_, ...), custom_call_target="tpu_custom_call" | custom-call | tf_op jit(solution)/shard_map/pallas_call | solution.py:750
  (24 shorter events, 0.1 us)
Async XLA Ops:
  0.6 11.3 %copy-start.8 = (f32[1,4,4]{2,1,0:T(4,128)S(1)}, f32[1,4,4]{2,1,0:T(4,128)}, u32[]{:S(2)}) copy-start(f32[1,4,4]{2,1,0:T(4,128)} %refs_1_.6) | copy-start | bytes 196
  0.6 11.3 %copy-start.7 = (f32[5,5]{1,0:T(8,128)S(1)}, f32[5,5]{1,0:T(8,128)}, u32[]{:S(2)}) copy-start(f32[5,5]{1,0:T(8,128)} %refs_2_.3) | copy-start | bytes 304
  1.3 1.1 %copy-start = (bf16[4,4,5,4,8,96]{5,4,3,2,1,0:T(8,128)(2,1)S(1)}, bf16[4,4,5,4,8,96]{5,4,3,2,1,0:T(8,128)(2,1)}, u32[]{:S(2)}) copy-start(bf16[4,4,5,4,8,96]{5,4,3,2,1,0:T(8,128)(2,1)} %refs_1_.10) | copy-start | bytes 1474564
  2.4 7.5 %copy-start.2 = (f32[1,5,4,8,384]{4,3,2,1,0:T(8,128)S(1)}, f32[1,5,4,8,384]{4,3,2,1,0:T(8,128)}, u32[]{:S(2)}) copy-start(f32[1,5,4,8,384]{4,3,2,1,0:T(8,128)} %refs_6_.1) | copy-start | bytes 737284
  2.4 7.5 %copy-start.3 = (f32[1,4,4,8,384]{4,3,2,1,0:T(8,128)S(1)}, f32[1,4,4,8,384]{4,3,2,1,0:T(8,128)}, u32[]{:S(2)}) copy-start(f32[1,4,4,8,384]{4,3,2,1,0:T(8,128)} %refs_3_.3) | copy-start | bytes 589828
  2.4 7.5 %copy-start.4 = (f32[1,5,4,8,384]{4,3,2,1,0:T(8,128)S(1)}, f32[1,5,4,8,384]{4,3,2,1,0:T(8,128)}, u32[]{:S(2)}) copy-start(f32[1,5,4,8,384]{4,3,2,1,0:T(8,128)} %refs_8_.1) | copy-start | bytes 737284
  2.4 8.7 %copy-start.1 = (bf16[4,4,5,4,8,96]{5,4,3,2,1,0:T(8,128)(2,1)S(1)}, bf16[4,4,5,4,8,96]{5,4,3,2,1,0:T(8,128)(2,1)}, u32[]{:S(2)}) copy-start(bf16[4,4,5,4,8,96]{5,4,3,2,1,0:T(8,128)(2,1)} %refs_1_.10) | copy-start | bytes 1474564
  2.4 9.5 %copy-start.6 = (f32[1,4,4,8,384]{4,3,2,1,0:T(8,128)S(1)}, f32[1,4,4,8,384]{4,3,2,1,0:T(8,128)}, u32[]{:S(2)}) copy-start(f32[1,4,4,8,384]{4,3,2,1,0:T(8,128)} %refs_4_.1) | copy-start | bytes 589828
  2.6 10.1 %collective-permute-start = (bf16[61,8,128]{2,1,0:T(8,128)(2,1)S(1)}, bf16[61,8,128]{2,1,0:T(8,128)(2,1)S(1)}, u32[]{:S(2)}, u32[]{:S(2)}) collective-permute-start(bf16[61,8,128]{2,1,0:T(8,128)(2,1)S(1)} %shard_map.123), channel_id=1, source_target_pairs={{0,4},{4,8},{8,12},{12,0},{1,5},{5,9},{9,13},{13,1},{2,6},{6,10},{... | collective-permute-start | bytes 374792 | tf_op jit(solution)/shard_map/ppermute | solution.py:597
  5.8 10.7 %collective-permute-start.1 = (bf16[61,8,128]{2,1,0:T(8,128)(2,1)S(1)}, bf16[61,8,128]{2,1,0:T(8,128)(2,1)S(1)}, u32[]{:S(2)}, u32[]{:S(2)}) collective-permute-start(bf16[61,8,128]{2,1,0:T(8,128)(2,1)S(1)} %shard_map.124), channel_id=1, source_target_pairs={{0,8},{4,12},{8,0},{12,4},{1,9},{5,13},{9,1},{13,5},{2,10},{6,14},... | collective-permute-start | bytes 374792 | tf_op jit(solution)/shard_map/ppermute | solution.py:597
  8.5 8.0 %collective-permute-start.2 = (bf16[61,8,128]{2,1,0:T(8,128)(2,1)S(1)}, bf16[61,8,128]{2,1,0:T(8,128)(2,1)S(1)}, u32[]{:S(2)}, u32[]{:S(2)}) collective-permute-start(bf16[61,8,128]{2,1,0:T(8,128)(2,1)S(1)} %shard_map.125), channel_id=1, source_target_pairs={{0,12},{4,0},{8,4},{12,8},{1,13},{5,1},{9,5},{13,9},{2,14},{6,2},{... | collective-permute-start | bytes 374792 | tf_op jit(solution)/shard_map/ppermute | solution.py:597
  10.4 7.3 %collective-permute-start.3 = (s16[2,21,16,128]{3,2,1,0:T(8,128)(2,1)S(1)}, s16[2,21,16,128]{3,2,1,0:T(8,128)(2,1)S(1)}, u32[]{:S(2)}, u32[]{:S(2)}) collective-permute-start(s16[2,21,16,128]{3,2,1,0:T(8,128)(2,1)S(1)} %get-tuple-element.29), channel_id=1, source_target_pairs={{0,1},{1,0},{2,3},{3,2},{4,5},{5,4},{6,7},{7,6},{8,9},{9,8},{10,11... | collective-permute-start | bytes 516104 | tf_op jit(solution)/shard_map/ppermute | solution.py:608
  10.5 7.2 %collective-permute-start.4 = (s16[2,21,16,128]{3,2,1,0:T(8,128)(2,1)S(1)}, s16[2,21,16,128]{3,2,1,0:T(8,128)(2,1)S(1)}, u32[]{:S(2)}, u32[]{:S(2)}) collective-permute-start(s16[2,21,16,128]{3,2,1,0:T(8,128)(2,1)S(1)} %get-tuple-element.30), channel_id=1, source_target_pairs={{1,2},{2,1},{5,6},{6,5},{9,10},{10,9},{13,14},{14,13},{17,18},{18,... | collective-permute-start | bytes 516104 | tf_op jit(solution)/shard_map/ppermute | solution.py:608
  17.0 4.0 %collective-permute-start.5 = (bf16[4,10,8,384]{3,2,1,0:T(8,128)(2,1)S(1)}, bf16[4,10,8,384]{3,2,1,0:T(8,128)(2,1)S(1)}, u32[]{:S(2)}, u32[]{:S(2)}) collective-permute-start(bf16[4,10,8,384]{3,2,1,0:T(8,128)(2,1)S(1)} %get-tuple-element.35), channel_id=1, source_target_pairs={{0,1},{1,0},{2,3},{3,2},{4,5},{5,4},{6,7},{7,6},{8,9},{9,8},{10,11... | collective-permute-start | bytes 737288 | tf_op jit(solution)/shard_map/ppermute | solution.py:608
  17.1 3.9 %collective-permute-start.6 = (bf16[31,8,384]{2,1,0:T(8,128)(2,1)S(1)}, bf16[31,8,384]{2,1,0:T(8,128)(2,1)S(1)}, u32[]{:S(2)}, u32[]{:S(2)}) collective-permute-start(bf16[31,8,384]{2,1,0:T(8,128)(2,1)S(1)} %get-tuple-element.36), channel_id=1, source_target_pairs={{1,2},{2,1},{5,6},{6,5},{9,10},{10,9},{13,14},{14,13},{17,18},{18,... | collective-permute-start | bytes 571400 | tf_op jit(solution)/shard_map/ppermute | solution.py:608
  18.0 11.4 %copy-start.5 = (f32[1,5,4,8,384]{4,3,2,1,0:T(8,128)S(1)}, f32[1,5,4,8,384]{4,3,2,1,0:T(8,128)}, u32[]{:S(2)}) copy-start(f32[1,5,4,8,384]{4,3,2,1,0:T(8,128)} %refs_7_.1) | copy-start | bytes 737284
  18.0 8.1 %collective-permute-start.7 = (s16[2,16,16,128]{3,2,1,0:T(8,128)(2,1)S(1)}, s16[2,16,16,128]{3,2,1,0:T(8,128)(2,1)S(1)}, u32[]{:S(2)}, u32[]{:S(2)}) collective-permute-start(s16[2,16,16,128]{3,2,1,0:T(8,128)(2,1)S(1)} %get-tuple-element.38), channel_id=1, source_target_pairs={{4,0},{8,4},{12,8},{5,1},{9,5},{13,9},{6,2},{10,6},{14,10},{7,3},{... | collective-permute-start | bytes 393224 | tf_op jit(solution)/shard_map/ppermute | solution.py:597
  19.5 9.8 %collective-permute-start.8 = (s16[2,16,16,128]{3,2,1,0:T(8,128)(2,1)S(1)}, s16[2,16,16,128]{3,2,1,0:T(8,128)(2,1)S(1)}, u32[]{:S(2)}, u32[]{:S(2)}) collective-permute-start(s16[2,16,16,128]{3,2,1,0:T(8,128)(2,1)S(1)} %get-tuple-element.39), channel_id=1, source_target_pairs={{4,0},{8,4},{12,8},{5,1},{9,5},{13,9},{6,2},{10,6},{14,10},{7,3},{... | collective-permute-start | bytes 393224 | tf_op jit(solution)/shard_map/ppermute | solution.py:597
  32.3 8.0 %collective-permute-start.9 = (s16[2,16,16,128]{3,2,1,0:T(8,128)(2,1)S(1)}, s16[2,16,16,128]{3,2,1,0:T(8,128)(2,1)S(1)}, u32[]{:S(2)}, u32[]{:S(2)}) collective-permute-start(s16[2,16,16,128]{3,2,1,0:T(8,128)(2,1)S(1)} %get-tuple-element.43), channel_id=1, source_target_pairs={{0,4},{4,8},{8,12},{12,0},{1,5},{5,9},{9,13},{13,1},{2,6},{6,10},{... | collective-permute-start | bytes 393224 | tf_op jit(solution)/shard_map/ppermute | solution.py:597
  34.6 11.5 %collective-permute-start.10 = (s16[2,16,16,128]{3,2,1,0:T(8,128)(2,1)S(1)}, s16[2,16,16,128]{3,2,1,0:T(8,128)(2,1)S(1)}, u32[]{:S(2)}, u32[]{:S(2)}) collective-permute-start(s16[2,16,16,128]{3,2,1,0:T(8,128)(2,1)S(1)} %get-tuple-element.44), channel_id=1, source_target_pairs={{0,8},{4,12},{8,0},{12,4},{1,9},{5,13},{9,1},{13,5},{2,10},{6,14},... | collective-permute-start | bytes 393224 | tf_op jit(solution)/shard_map/ppermute | solution.py:597
  35.5 10.6 %collective-permute-start.11 = (s16[2,16,16,128]{3,2,1,0:T(8,128)(2,1)S(1)}, s16[2,16,16,128]{3,2,1,0:T(8,128)(2,1)S(1)}, u32[]{:S(2)}, u32[]{:S(2)}) collective-permute-start(s16[2,16,16,128]{3,2,1,0:T(8,128)(2,1)S(1)} %get-tuple-element.45), channel_id=1, source_target_pairs={{0,12},{4,0},{8,4},{12,8},{1,13},{5,1},{9,5},{13,9},{2,14},{6,2},{... | collective-permute-start | bytes 393224 | tf_op jit(solution)/shard_map/ppermute | solution.py:597

commit v9 on v8

--- a/solution.py
+++ b/solution.py
@@ -145,42 +145,47 @@
     return values + [scales]
 
 
-def half_code_kernel(*refs):
-    sources, (near_ref, far_ref, own_ref) = refs[:-3], refs[-3:]
+def own_code_kernel(field_ref, out_ref):
+    def pair(i, carry):
+        coded = [level_codes(field_ref, 2 * i + odd) for odd in range(2)]
+        for n, (first, second) in enumerate(zip(*coded)):
+            out_ref[i, n] = shorts(jnp.concatenate([first, second], 0))
+        return carry
+
+    lax.fori_loop(0, out_ref.shape[0], pair, 0)
+
+
+def write_halves(i, groups, near_ref, far_ref):
     even = even_place()
-
+    near, far = [], []
+    for coded in groups:
+        for first, second in zip(*coded):
+            last, start = joined_halves(first, second)
+            near.append(jnp.where(even, last, start))
+            far.append(jnp.where(even, start, last))
+        if len(near) % 2:
+            near.append(jnp.zeros((SUB, LANES), jnp.float32))
+            far.append(jnp.zeros((SUB, LANES), jnp.float32))
+    for tiles, ref in ((near, near_ref), (far, far_ref)):
+        for n in range(0, len(tiles), 2):
+            ref[i, n // 2] = shorts(jnp.concatenate(tiles[n : n + 2], 0))
+
+
+def field_half_kernel(inc_ref, dobs_ref, near_ref, far_ref):
     def pair(i, carry):
-        near, far = [], []
-        for k, ref in enumerate(sources):
-            skip = int(k == len(sources) - 1)
-            coded = [level_codes(ref, 2 * i + odd, skip) for odd in range(2)]
-            for n, (first, second) in enumerate(zip(*coded)):
-                if k == 0:
-                    own_ref[i, n] = shorts(jnp.concatenate([first, second], 0))
-                last, start = joined_halves(first, second)
-                near.append(jnp.where(even, last, start))
-                far.append(jnp.where(even, start, last))
-            if len(near) % 2:
-                near.append(jnp.zeros((SUB, LANES), jnp.float32))
-                far.append(jnp.zeros((SUB, LANES), jnp.float32))
-        for tiles, ref in ((near, near_ref), (far, far_ref)):
-            for n in range(0, len(tiles), 2):
-                ref[i, n // 2] = shorts(jnp.concatenate(tiles[n : n + 2], 0))
+        groups = [
+            [level_codes(ref, 2 * i + odd, skip) for odd in range(2)]
+            for ref, skip in ((inc_ref, 0), (dobs_ref, 1))
+        ]
+        write_halves(i, groups, near_ref, far_ref)
         return carry
 
     lax.fori_loop(0, near_ref.shape[0], pair, 0)
 
 
-def half_tile(ref, i, n):
-    whole = floats(ref[i, n // 2])
-    return whole[SUB:] if n % 2 else whole[:SUB]
-
-
-def around_kernel(windows, nvar, levels, *refs):
-    pieces, (own_ref, near_ref, far_ref) = refs[:windows], refs[windows : windows + 3]
-    outs, total_ref = refs[windows + 3 : -1], refs[-1]
+def dual_half_kernel(windows, nvar, levels, *refs):
+    pieces, (coded_ref, near_ref, far_ref, total_ref) = refs[:windows], refs[windows:]
     me = lax.axis_index("window")
-    even = even_place()
     total = jnp.zeros((SUB, LANES), jnp.float32)
     for d in range(windows):
         split = pieces[d][pieces[d].shape[0] - 1].astype(jnp.float32)
@@ -190,13 +195,15 @@
         for lev in range(levels):
             one = total[lev : lev + 1, v : v + 1]
             total_ref[v * levels + lev] = jnp.broadcast_to(one, (SUB, LANES))
-    for i, out_ref in enumerate(outs):
-        for n in range(own_ref.shape[1]):
-            own = floats(own_ref[i, n])
-            near, far = half_tile(near_ref, i, n), half_tile(far_ref, i, n)
-            for odd in range(2):
-                halves = widened(own[odd * SUB : (odd + 1) * SUB], near, far, odd, even)
-                out_ref[odd, n] = shorts(jnp.concatenate(halves, 0))
+    for i in range(levels // 2):
+        whole = [floats(coded_ref[i, n]) for n in range(coded_ref.shape[1])]
+        groups = [[[tile[:SUB] for tile in whole], [tile[SUB:] for tile in whole]]]
+        write_halves(i, groups, near_ref, far_ref)
+
+
+def half_tile(ref, i, n):
+    whole = floats(ref[i, n // 2])
+    return whole[SUB:] if n % 2 else whole[:SUB]
 
 
 def decoded(ref, i, first, nvar, tiles):
@@ -230,8 +237,9 @@
 
 
 def assemble_kernel(windows, steps, nvar, levels, part, *refs):
-    pieces = refs[:windows]
-    own_ref, near_ref, far_ref, stack_ref = refs[windows + 1 :]
+    pieces, codes_ref = refs[:windows], refs[windows]
+    own_ref, near_ref, far_ref, out_ref, stack_ref = refs[windows + 4 :]
+    out_ref[...] = codes_ref[...]
     me = lax.axis_index("window")
     even = even_place()
     lane = lane_index()
@@ -301,9 +309,8 @@
     even = even_place()
     blocks = [slice(0, SUB), slice(SUB, 2 * SUB)]
     cuts = [slice(t * LANES, (t + 1) * LANES) for t in range(tiles)]
-    offset = -(-(nvar * tiles + 1) // 2) * 2
     for i in range(levels // 2):
-        fields = [decoded(ref, i, offset, nvar, tiles) for ref in (near_ref, far_ref)]
+        fields = [decoded(ref, i, 0, nvar, tiles) for ref in (near_ref, far_ref)]
         for odd in range(2):
             lev = 2 * i + odd
             for t in range(tiles):
@@ -315,26 +322,30 @@
 
 
 def prepare_adjoint_kernel(
-    steps, nvar, levels, tiles, count_ref, near_ref, far_ref, dobs_ref, *refs
+    steps, nvar, levels, tiles,
+    count_ref, near_ref, far_ref, dobs_ref, after_ref, anear_ref, afar_ref, order_ref,
+    last_ref, force_ref,
 ):
-    after_refs, (last_ref, force_ref) = refs[: levels // 2], refs[levels // 2 + 1 :]
     even = even_place()
     blocks = [slice(0, SUB), slice(SUB, 2 * SUB)]
     cuts = [slice(t * LANES, (t + 1) * LANES) for t in range(tiles)]
     seen = [jnp.where(j < count_ref[0], 1.0, 0.0) for j in range(steps)]
     offset = -(-(nvar * tiles + 1) // 2) * 2
     none = [[jnp.zeros((SUB, LANES), jnp.float32)] * tiles]
-    for i, after_ref in enumerate(after_refs):
-        forces = [
-            none + decoded(ref, i, 2 * offset, steps - 1, tiles) for ref in (near_ref, far_ref)
-        ]
+    for i in range(levels // 2):
+        forces = [none + decoded(ref, i, offset, steps - 1, tiles) for ref in (near_ref, far_ref)]
+        afters = [decoded(ref, i, 0, nvar, tiles) for ref in (anear_ref, afar_ref)]
+        scales = jnp.exp2(floats(after_ref[i, nvar * tiles])) * (1.0 / CODE_MAX)
         for odd in range(2):
             lev = 2 * i + odd
-            scales = jnp.exp2(floats(after_ref[odd, nvar * tiles])) * (-1.0 / CODE_MAX)
+            rows = blocks[odd]
             for t in range(tiles):
                 for v in range(nvar):
-                    value = floats(after_ref[odd, v * tiles + t])
-                    last_ref[lev, v, t] = value * scales[:, v : v + 1]
+                    near, far = (side[v][t] for side in afters)
+                    own = floats(after_ref[i, v * tiles + t])[rows] * scales[rows, v : v + 1]
+                    halves = widened(own, near, far, odd, even)
+                    for b in range(2):
+                        last_ref[lev, v, t, blocks[b], :] = -halves[b]
                 for j in range(steps):
                     near, far = (side[j][t] for side in forces)
                     halves = widened(dobs_ref[0, j, lev, :, cuts[t]], near, far, odd, even)
@@ -655,28 +666,26 @@
 
     payload = shape((pairs, nvar * tiles + 1, 2 * SUB, LANES), i16)
 
-    counts = [nvar, nvar, steps - 1]
-    half_tiles = sum(-(-(count * tiles + 1) // 2) for count in counts)
-    halves = shape((pairs, half_tiles, 2 * SUB, LANES), i16)
-    near, far, dual = pl.pallas_call(
-        half_code_kernel,
-        out_shape=[halves, halves, payload],
-        in_specs=[VMEM] * 3,
-        out_specs=[VMEM] * 3,
-        compiler_params=params(),
-    )(dual_model, increment, dual_obs)
+    def half_shape(*counts):
+        total = sum(-(-(count * tiles + 1) // 2) for count in counts)
+        return shape((pairs, total, 2 * SUB, LANES), i16)
+
+    near, far = pl.pallas_call(
+        field_half_kernel,
+        out_shape=[half_shape(nvar, steps - 1)] * 2,
+        in_specs=[VMEM] * 2,
+        out_specs=[VMEM] * 2,
+        compiler_params=params(),
+    )(increment, dual_obs)
     far, near = swapped(far, "space", 1), swapped(near, "space", 0)
-
+    dual = pl.pallas_call(
+        own_code_kernel,
+        out_shape=payload,
+        in_specs=[VMEM],
+        out_specs=VMEM,
+        compiler_params=params(),
+    )(dual_model)
     blocks_here = [arrived[d] for d in range(windows)]
-    *after, totals = pl.pallas_call(
-        lambda *refs: around_kernel(windows, nvar, levels, *refs),
-        out_shape=[shape((2,) + payload.shape[1:], i16)] * pairs
-        + [shape((nvar * levels, rows, LANES), f32)],
-        in_specs=[VMEM] * (windows + 3),
-        out_specs=[VMEM] * (pairs + 1),
-        compiler_params=params(),
-    )(*blocks_here, dual, near, far)
-    after = [moved(piece, "window", -1) for piece in after]
 
     obs, share, mix = pl.pallas_call(
         lambda *refs: prepare_factor_kernel(steps, nvar, levels, tiles, *refs),
@@ -690,19 +699,29 @@
         compiler_params=params(),
     )(obs_count, obs_var, coupling, dual_obs, innovation)
 
-    own, traj_near, traj_far = pl.pallas_call(
+    own, traj_near, traj_far, dual = pl.pallas_call(
         lambda *refs: assemble_kernel(windows, steps, nvar, levels, part, *refs),
         out_shape=[
             shape((steps, nvar * levels, rows, columns), bf16),
             shape((steps, nvar * pairs, rows, columns), bf16),
             shape((far_base(steps, nvar, levels)[1], rows, columns), bf16),
+            payload,
         ],
-        in_specs=[VMEM] * windows + [ANY],
+        in_specs=[VMEM] * (windows + 1) + [ANY] * 3,
+        out_specs=[VMEM] * 4,
+        scratch_shapes=[pltpu.VMEM((windows, block.shape[0] - 1, rows, LANES), bf16)],
+        compiler_params=params(),
+    )(*blocks_here, dual, mix, near, far)
+    traj_near, traj_far = swapped(traj_near, "space", 0), swapped(traj_far, "space", 1)
+    after = moved(dual, "window", -1)
+    after_near, after_far, totals = pl.pallas_call(
+        lambda *refs: dual_half_kernel(windows, nvar, levels, *refs),
+        out_shape=[half_shape(nvar)] * 2 + [shape((nvar * levels, rows, LANES), f32)],
+        in_specs=[VMEM] * (windows + 1),
         out_specs=[VMEM] * 3,
-        scratch_shapes=[pltpu.VMEM((windows, block.shape[0] - 1, rows, LANES), bf16)],
-        compiler_params=params(),
-    )(*blocks_here, mix)
-    traj_near, traj_far = swapped(traj_near, "space", 0), swapped(traj_far, "space", 1)
+        compiler_params=params(),
+    )(*blocks_here, after)
+    after_near, after_far = swapped(after_near, "space", 0), swapped(after_far, "space", 1)
 
     first = pl.pallas_call(
         lambda *refs: prepare_tangent_kernel(nvar, levels, tiles, *refs),
@@ -727,10 +746,10 @@
     last, force = pl.pallas_call(
         lambda *refs: prepare_adjoint_kernel(steps, nvar, levels, tiles, *refs),
         out_shape=[shape((levels, n, tiles, 2 * SUB, LANES), f32) for n in (nvar, steps)],
-        in_specs=[SMEM] + [VMEM] * (3 + pairs) + [ANY],
+        in_specs=[SMEM] + [VMEM] * 6 + [ANY],
         out_specs=[VMEM] * 2,
         compiler_params=params(),
-    )(obs_count, near, far, dual_obs, *after, ends)
+    )(obs_count, near, far, dual_obs, after, after_near, after_far, ends)
     state = shape((nvar, levels, rows, columns), f32)
     base_dual, base_inc, *payloads = pl.pallas_call(
         lambda *refs: adjoint_kernel(windows, spaces, steps, nvar, levels, tiles, *refs),

time: 48.2 us -> 50 us (1.037)
  waiting for transfers between devices: 17.1 us -> 20 us
  starting transfers between devices: 16.6 us -> 15.4 us
    ppermute x8 -> x7, waiting for transfers between devices: 17.1 us -> 20 us  [moved(): return lax.ppermute(block, axis, route)]
    ppermute x8 -> x7, starting transfers between devices: 15.1 us -> 12.6 us  [moved(): return lax.ppermute(block, axis, route)]
    ppermute x4 -> x6, starting transfers between devices: 1.49 us -> 2.72 us  [swapped(): return lax.ppermute(block, axis, swaps(axis, first))]
  transfers between devices with their start and end apart: 12 -> 13, of which waited for: 5 -> 4; matrix products, arithmetic and copies ran while one was open for 0% -> 0% of each run, Pallas kernels for 13% -> 11%
where the time goes in v9:
time: 50 us; the launch traced here: 49 us
  waiting for transfers between devices  20 us (40%)
  starting transfers between devices  15.4 us (31%)
  Pallas kernels  10.3 us (21%)
  local copies, waits for them, and re-layouts  1.81 us (4%)
  between operations  1.55 us (3%)
    ppermute x7, waiting for transfers between devices, moved(): return lax.ppermute(block, axis, route)  20 us
    ppermute x7, starting transfers between devices, moved(): return lax.ppermute(block, axis, route)  12.6 us
    pallas_call x1, Pallas kernels, body(): pl.pallas_call(lambda *refs: tangent_kernel(spaces, steps, nvar, levels,...  3.57 us
    pallas_call x1, Pallas kernels, body(): pl.pallas_call(lambda *refs: adjoint_kernel(windows, spaces, steps, nvar,...  2.89 us
    ppermute x6, starting transfers between devices, swapped(): return lax.ppermute(block, axis, swaps(axis, first))  2.72 us
    unnamed x18, local copies, waits for them, and re-layouts  1.13 us
    pallas_call x1, Pallas kernels, body(): pl.pallas_call(lambda *refs: final_kernel(windows, nvar, levels, tiles, *...  1.08 us
  transfers between devices with their start and end apart: 13, of which 4 were waited for; matrix products, arithmetic and copies ran while one was open for 0% of the time, Pallas kernels for 11%

profile of v9, /device:TPU:0, one launch (start us, length us, event | category | flops | bytes accessed | tf_op | source)
XLA Modules:
  0.0 49.0 jit_solution(10842572360264507907)
XLA Ops:
  0.6 0.7 %pad.4.refs_0_ = f32[8,128]{1,0:T(8,128)S(1)} pad(f32[4,5]{1,0:T(4,128)} %bitcast.3, f32[]{:T(128)} %constant.2.clone.1), padding=0_4x0_123 | pad | bytes 4180 | tf_op jit(solution)/shard_map/jit(_pad)/pad | solution.py:648
  1.3 1.1 %copy-done = bf16[4,4,5,4,8,96]{5,4,3,2,1,0:T(8,128)(2,1)S(1)} copy-done((bf16[4,4,5,4,8,96]{5,4,3,2,1,0:T(8,128)(2,1)S(1)}, bf16[4,4,5,4,8,96]{5,4,3,2,1,0:T(8,128)(2,1)}, u32[]{:S(2)}) %copy-start) | copy-done | bytes 491544
  2.5 0.1 shard_map.123
  2.6 3.1 %collective-permute-start = (bf16[61,8,128]{2,1,0:T(8,128)(2,1)S(1)}, bf16[61,8,128]{2,1,0:T(8,128)(2,1)S(1)}, u32[]{:S(2)}, u32[]{:S(2)}) collective-permute-start(bf16[61,8,128]{2,1,0:T(8,128)(2,1)S(1)} %shard_map.123), channel_id=1, source_target_pairs={{0,4},{4,8},{8,12},{12,0},{1,5},{5,9},{9,13},{13,1},{2,6},{6,10},{... | collective-permute-start | bytes 374792 | tf_op jit(solution)/shard_map/ppermute | solution.py:608
  5.7 0.1 shard_map.124
  5.8 2.7 %collective-permute-start.1 = (bf16[61,8,128]{2,1,0:T(8,128)(2,1)S(1)}, bf16[61,8,128]{2,1,0:T(8,128)(2,1)S(1)}, u32[]{:S(2)}, u32[]{:S(2)}) collective-permute-start(bf16[61,8,128]{2,1,0:T(8,128)(2,1)S(1)} %shard_map.124), channel_id=1, source_target_pairs={{0,8},{4,12},{8,0},{12,4},{1,9},{5,13},{9,1},{13,5},{2,10},{6,14},... | collective-permute-start | bytes 374792 | tf_op jit(solution)/shard_map/ppermute | solution.py:608
  8.4 0.1 shard_map.125
  8.5 1.4 %collective-permute-start.2 = (bf16[61,8,128]{2,1,0:T(8,128)(2,1)S(1)}, bf16[61,8,128]{2,1,0:T(8,128)(2,1)S(1)}, u32[]{:S(2)}, u32[]{:S(2)}) collective-permute-start(bf16[61,8,128]{2,1,0:T(8,128)(2,1)S(1)} %shard_map.125), channel_id=1, source_target_pairs={{0,12},{4,0},{8,4},{12,8},{1,13},{5,1},{9,5},{13,9},{2,14},{6,2},{... | collective-permute-start | bytes 374792 | tf_op jit(solution)/shard_map/ppermute | solution.py:608
  9.9 0.3 shard_map.127
  10.3 0.1 collective-permute-start.3
  10.4 0.7 %collective-permute-start.4 = (s16[2,13,16,128]{3,2,1,0:T(8,128)(2,1)S(1)}, s16[2,13,16,128]{3,2,1,0:T(8,128)(2,1)S(1)}, u32[]{:S(2)}, u32[]{:S(2)}) collective-permute-start(s16[2,13,16,128]{3,2,1,0:T(8,128)(2,1)S(1)} %get-tuple-element.29), channel_id=1, source_target_pairs={{1,2},{2,1},{5,6},{6,5},{9,10},{10,9},{13,14},{14,13},{17,18},{18,... | collective-permute-start | bytes 319496 | tf_op jit(solution)/shard_map/ppermute | solution.py:619
  11.1 0.1 shard_map.122.refs_0_
  11.8 0.3 shard_map.126.refs_4_
  12.1 0.7 %shard_map.121 = (f32[4,4,3,8,128]{4,3,2,1,0:T(8,128)S(1)}, f32[4,4,8,128]{3,2,1,0:T(8,128)S(1)}, f32[5,5,8,128]{3,2,1,0:T(8,128)S(1)}) custom-call(s32[1]{0:T(128)S(6)} %copy.13.refs_0_, f32[1,4,4]{2,1,0:T(4,128)S(1)} %copy-done.8, f32[5,5]{1,0:T(8,128)S(1)} %copy-done.7, f32[1,4,4,8,384]{4,3,2,1,0:T(8,128)S(1)} %copy-done.3, f32[1,4,4,8,384]{4,3,2,1,0:T(8,128)S(1)} %copy-done.6), custom_call_target="tpu_custom_call" | custom-call | tf_op jit(solution)/shard_map/pallas_call | solution.py:690
  12.9 3.6 %collective-permute-done.1.refs_2_ = bf16[61,8,128]{2,1,0:T(8,128)(2,1)S(1)} collective-permute-done((bf16[61,8,128]{2,1,0:T(8,128)(2,1)S(1)}, bf16[61,8,128]{2,1,0:T(8,128)(2,1)S(1)}, u32[]{:S(2)}, u32[]{:S(2)}) %collective-permute-start.1) | collective-permute-done | bytes 124960 | tf_op jit(solution)/shard_map/ppermute | solution.py:608
  16.5 0.5 shard_map.128
  17.0 0.4 collective-permute-start.6
  17.4 1.3 %collective-permute-start.5 = (s16[2,16,16,128]{3,2,1,0:T(8,128)(2,1)S(1)}, s16[2,16,16,128]{3,2,1,0:T(8,128)(2,1)S(1)}, u32[]{:S(2)}, u32[]{:S(2)}) collective-permute-start(s16[2,16,16,128]{3,2,1,0:T(8,128)(2,1)S(1)} %get-tuple-element.30), channel_id=1, source_target_pairs={{4,0},{8,4},{12,8},{5,1},{9,5},{13,9},{6,2},{10,6},{14,10},{7,3},{... | collective-permute-start | bytes 393224 | tf_op jit(solution)/shard_map/ppermute | solution.py:608
  18.7 0.7 %collective-permute-start.7 = (bf16[31,8,384]{2,1,0:T(8,128)(2,1)S(1)}, bf16[31,8,384]{2,1,0:T(8,128)(2,1)S(1)}, u32[]{:S(2)}, u32[]{:S(2)}) collective-permute-start(bf16[31,8,384]{2,1,0:T(8,128)(2,1)S(1)} %get-tuple-element.36), channel_id=1, source_target_pairs={{1,2},{2,1},{5,6},{6,5},{9,10},{10,9},{13,14},{14,13},{17,18},{18,... | collective-permute-start | bytes 571400 | tf_op jit(solution)/shard_map/ppermute | solution.py:619
  19.4 6.9 %collective-permute-done.5.refs_4_ = s16[2,16,16,128]{3,2,1,0:T(8,128)(2,1)S(1)} collective-permute-done((s16[2,16,16,128]{3,2,1,0:T(8,128)(2,1)S(1)}, s16[2,16,16,128]{3,2,1,0:T(8,128)(2,1)S(1)}, u32[]{:S(2)}, u32[]{:S(2)}) %collective-permute-start.5) | collective-permute-done | bytes 131104 | tf_op jit(solution)/shard_map/ppermute | solution.py:608
  26.2 0.2 shard_map.129
  26.5 0.1 collective-permute-start.8
  26.5 0.8 %collective-permute-start.9 = (s16[2,8,16,128]{3,2,1,0:T(8,128)(2,1)S(1)}, s16[2,8,16,128]{3,2,1,0:T(8,128)(2,1)S(1)}, u32[]{:S(2)}, u32[]{:S(2)}) collective-permute-start(s16[2,8,16,128]{3,2,1,0:T(8,128)(2,1)S(1)} %get-tuple-element.39), channel_id=1, source_target_pairs={{1,2},{2,1},{5,6},{6,5},{9,10},{10,9},{13,14},{14,13},{17,18},{18,... | collective-permute-start | bytes 196616 | tf_op jit(solution)/shard_map/ppermute | solution.py:619
  27.3 0.1 shard_map.130.refs_6_
  27.5 3.6 %shard_map.131 = (f32[1,4,4,8,384]{4,3,2,1,0:T(8,128)}, f32[4,5,3,8,128]{4,3,2,1,0:T(8,128)S(1)}, f32[4,4,5,3,16,128]{5,4,3,2,1,0:T(8,128)S(1)}) custom-call(f32[5,5,8,128]{3,2,1,0:T(8,128)S(1)} %get-tuple-element.27.refs_5_.refs_0_, f32[4,4,8,128]{3,2,1,0:T(8,128)S(1)} %get-tuple-element.32.refs_1_, f32[4,4,3,8,128]{4,3,2,1,0:T(8,128)S(1)} %get-tuple-element.33.refs_2_, ...), custom_call_target="tpu_custom_call" | custom-call | tf_op jit(solution)/shard_map/pallas_call | solution.py:733
  31.1 0.2 shard_map.132
  31.3 2.9 %shard_map.133 = (f32[5,4,8,384]{3,2,1,0:T(8,128)S(1)}, f32[5,4,8,384]{3,2,1,0:T(8,128)S(1)}, s16[2,16,16,128]{3,2,1,0:T(8,128)(2,1)S(1)}, s16[2,16,16,128]{3,2,...) custom-call(f32[5,5,8,128]{3,2,1,0:T(8,128)S(1)} %get-tuple-element.27.refs_5_.refs_0_, ...), custom_call_target="tpu_custom_call" | custom-call | tf_op jit(solution)/shard_map/pallas_call | solution.py:754
  34.2 1.8 %collective-permute-start.10 = (s16[2,16,16,128]{3,2,1,0:T(8,128)(2,1)S(1)}, s16[2,16,16,128]{3,2,1,0:T(8,128)(2,1)S(1)}, u32[]{:S(2)}, u32[]{:S(2)}) collective-permute-start(s16[2,16,16,128]{3,2,1,0:T(8,128)(2,1)S(1)} %get-tuple-element.43), channel_id=1, source_target_pairs={{0,4},{4,8},{8,12},{12,0},{1,5},{5,9},{9,13},{13,1},{2,6},{6,10},{... | collective-permute-start | bytes 393224 | tf_op jit(solution)/shard_map/ppermute | solution.py:608
  36.0 2.4 %collective-permute-start.12 = (s16[2,16,16,128]{3,2,1,0:T(8,128)(2,1)S(1)}, s16[2,16,16,128]{3,2,1,0:T(8,128)(2,1)S(1)}, u32[]{:S(2)}, u32[]{:S(2)}) collective-permute-start(s16[2,16,16,128]{3,2,1,0:T(8,128)(2,1)S(1)} %get-tuple-element.45), channel_id=1, source_target_pairs={{0,12},{4,0},{8,4},{12,8},{1,13},{5,1},{9,5},{13,9},{2,14},{6,2},{... | collective-permute-start | bytes 393224 | tf_op jit(solution)/shard_map/ppermute | solution.py:608
  38.4 2.7 %collective-permute-done.10.refs_0_ = s16[2,16,16,128]{3,2,1,0:T(8,128)(2,1)S(1)} collective-permute-done((s16[2,16,16,128]{3,2,1,0:T(8,128)(2,1)S(1)}, s16[2,16,16,128]{3,2,1,0:T(8,128)(2,1)S(1)}, u32[]{:S(2)}, u32[]{:S(2)}) %collective-permute-start.10) | collective-permute-done | bytes 131104 | tf_op jit(solution)/shard_map/ppermute | solution.py:608
  41.2 6.8 %collective-permute-done.11.refs_1_ = s16[2,16,16,128]{3,2,1,0:T(8,128)(2,1)S(1)} collective-permute-done((s16[2,16,16,128]{3,2,1,0:T(8,128)(2,1)S(1)}, s16[2,16,16,128]{3,2,1,0:T(8,128)(2,1)S(1)}, u32[]{:S(2)}, u32[]{:S(2)}) %collective-permute-start.11) | collective-permute-done | bytes 131104 | tf_op jit(solution)/shard_map/ppermute | solution.py:608
  48.0 1.1 %shard_map.134 = (f32[1,5,4,8,384]{4,3,2,1,0:T(8,128)}, f32[1,5,4,8,384]{4,3,2,1,0:T(8,128)}) custom-call(s16[2,16,16,128]{3,2,1,0:T(8,128)(2,1)S(1)} %collective-permute-done.10.refs_0_, s16[2,16,16,128]{3,2,1,0:T(8,128)(2,1)S(1)} %collective-permute-done.11.refs_1_, s16[2,16,16,128]{3,2,1,0:T(8,128)(2,1)S(1)} %collective-permute-done.12.refs_2_, ...), custom_call_target="tpu_custom_call" | custom-call | tf_op jit(solution)/shard_map/pallas_call | solution.py:769
  (27 shorter events, 0.1 us)
Async XLA Ops:
  1.3 1.1 %copy-start = (bf16[4,4,5,4,8,96]{5,4,3,2,1,0:T(8,128)(2,1)S(1)}, bf16[4,4,5,4,8,96]{5,4,3,2,1,0:T(8,128)(2,1)}, u32[]{:S(2)}) copy-start(bf16[4,4,5,4,8,96]{5,4,3,2,1,0:T(8,128)(2,1)} %refs_1_.9) | copy-start | bytes 1474564
  2.4 7.5 %copy-start.2 = (f32[1,5,4,8,384]{4,3,2,1,0:T(8,128)S(1)}, f32[1,5,4,8,384]{4,3,2,1,0:T(8,128)}, u32[]{:S(2)}) copy-start(f32[1,5,4,8,384]{4,3,2,1,0:T(8,128)} %refs_6_.1) | copy-start | bytes 737284
  2.4 7.5 %copy-start.3 = (f32[1,4,4,8,384]{4,3,2,1,0:T(8,128)S(1)}, f32[1,4,4,8,384]{4,3,2,1,0:T(8,128)}, u32[]{:S(2)}) copy-start(f32[1,4,4,8,384]{4,3,2,1,0:T(8,128)} %refs_3_.3) | copy-start | bytes 589828
  2.4 8.6 %copy-start.1 = (bf16[4,4,5,4,8,96]{5,4,3,2,1,0:T(8,128)(2,1)S(1)}, bf16[4,4,5,4,8,96]{5,4,3,2,1,0:T(8,128)(2,1)}, u32[]{:S(2)}) copy-start(bf16[4,4,5,4,8,96]{5,4,3,2,1,0:T(8,128)(2,1)} %refs_1_.9) | copy-start | bytes 1474564
  2.4 9.4 %copy-start.4 = (f32[1,5,4,8,384]{4,3,2,1,0:T(8,128)S(1)}, f32[1,5,4,8,384]{4,3,2,1,0:T(8,128)}, u32[]{:S(2)}) copy-start(f32[1,5,4,8,384]{4,3,2,1,0:T(8,128)} %refs_8_.1) | copy-start | bytes 737284
  2.4 9.7 %copy-start.6 = (f32[1,4,4,8,384]{4,3,2,1,0:T(8,128)S(1)}, f32[1,4,4,8,384]{4,3,2,1,0:T(8,128)}, u32[]{:S(2)}) copy-start(f32[1,4,4,8,384]{4,3,2,1,0:T(8,128)} %refs_4_.1) | copy-start | bytes 589828
  2.4 9.7 %copy-start.7 = (f32[5,5]{1,0:T(8,128)S(1)}, f32[5,5]{1,0:T(8,128)}, u32[]{:S(2)}) copy-start(f32[5,5]{1,0:T(8,128)} %refs_2_.2) | copy-start | bytes 304
  2.4 9.7 %copy-start.8 = (f32[1,4,4]{2,1,0:T(4,128)S(1)}, f32[1,4,4]{2,1,0:T(4,128)}, u32[]{:S(2)}) copy-start(f32[1,4,4]{2,1,0:T(4,128)} %refs_1_.5) | copy-start | bytes 196
  2.6 10.3 %collective-permute-start = (bf16[61,8,128]{2,1,0:T(8,128)(2,1)S(1)}, bf16[61,8,128]{2,1,0:T(8,128)(2,1)S(1)}, u32[]{:S(2)}, u32[]{:S(2)}) collective-permute-start(bf16[61,8,128]{2,1,0:T(8,128)(2,1)S(1)} %shard_map.123), channel_id=1, source_target_pairs={{0,4},{4,8},{8,12},{12,0},{1,5},{5,9},{9,13},{13,1},{2,6},{6,10},{... | collective-permute-start | bytes 374792 | tf_op jit(solution)/shard_map/ppermute | solution.py:608
  5.8 10.7 %collective-permute-start.1 = (bf16[61,8,128]{2,1,0:T(8,128)(2,1)S(1)}, bf16[61,8,128]{2,1,0:T(8,128)(2,1)S(1)}, u32[]{:S(2)}, u32[]{:S(2)}) collective-permute-start(bf16[61,8,128]{2,1,0:T(8,128)(2,1)S(1)} %shard_map.124), channel_id=1, source_target_pairs={{0,8},{4,12},{8,0},{12,4},{1,9},{5,13},{9,1},{13,5},{2,10},{6,14},... | collective-permute-start | bytes 374792 | tf_op jit(solution)/shard_map/ppermute | solution.py:608
  8.5 8.0 %collective-permute-start.2 = (bf16[61,8,128]{2,1,0:T(8,128)(2,1)S(1)}, bf16[61,8,128]{2,1,0:T(8,128)(2,1)S(1)}, u32[]{:S(2)}, u32[]{:S(2)}) collective-permute-start(bf16[61,8,128]{2,1,0:T(8,128)(2,1)S(1)} %shard_map.125), channel_id=1, source_target_pairs={{0,12},{4,0},{8,4},{12,8},{1,13},{5,1},{9,5},{13,9},{2,14},{6,2},{... | collective-permute-start | bytes 374792 | tf_op jit(solution)/shard_map/ppermute | solution.py:608
  10.3 2.5 %collective-permute-start.3 = (s16[2,13,16,128]{3,2,1,0:T(8,128)(2,1)S(1)}, s16[2,13,16,128]{3,2,1,0:T(8,128)(2,1)S(1)}, u32[]{:S(2)}, u32[]{:S(2)}) collective-permute-start(s16[2,13,16,128]{3,2,1,0:T(8,128)(2,1)S(1)} %get-tuple-element.28), channel_id=1, source_target_pairs={{0,1},{1,0},{2,3},{3,2},{4,5},{5,4},{6,7},{7,6},{8,9},{9,8},{10,11... | collective-permute-start | bytes 319496 | tf_op jit(solution)/shard_map/ppermute | solution.py:619
  10.4 2.5 %collective-permute-start.4 = (s16[2,13,16,128]{3,2,1,0:T(8,128)(2,1)S(1)}, s16[2,13,16,128]{3,2,1,0:T(8,128)(2,1)S(1)}, u32[]{:S(2)}, u32[]{:S(2)}) collective-permute-start(s16[2,13,16,128]{3,2,1,0:T(8,128)(2,1)S(1)} %get-tuple-element.29), channel_id=1, source_target_pairs={{1,2},{2,1},{5,6},{6,5},{9,10},{10,9},{13,14},{14,13},{17,18},{18,... | collective-permute-start | bytes 319496 | tf_op jit(solution)/shard_map/ppermute | solution.py:619
  17.0 10.5 %collective-permute-start.6 = (bf16[4,10,8,384]{3,2,1,0:T(8,128)(2,1)S(1)}, bf16[4,10,8,384]{3,2,1,0:T(8,128)(2,1)S(1)}, u32[]{:S(2)}, u32[]{:S(2)}) collective-permute-start(bf16[4,10,8,384]{3,2,1,0:T(8,128)(2,1)S(1)} %get-tuple-element.35), channel_id=1, source_target_pairs={{0,1},{1,0},{2,3},{3,2},{4,5},{5,4},{6,7},{7,6},{8,9},{9,8},{10,11... | collective-permute-start | bytes 737288 | tf_op jit(solution)/shard_map/ppermute | solution.py:619
  17.4 8.8 %collective-permute-start.5 = (s16[2,16,16,128]{3,2,1,0:T(8,128)(2,1)S(1)}, s16[2,16,16,128]{3,2,1,0:T(8,128)(2,1)S(1)}, u32[]{:S(2)}, u32[]{:S(2)}) collective-permute-start(s16[2,16,16,128]{3,2,1,0:T(8,128)(2,1)S(1)} %get-tuple-element.30), channel_id=1, source_target_pairs={{4,0},{8,4},{12,8},{5,1},{9,5},{13,9},{6,2},{10,6},{14,10},{7,3},{... | collective-permute-start | bytes 393224 | tf_op jit(solution)/shard_map/ppermute | solution.py:608
  18.7 8.8 %collective-permute-start.7 = (bf16[31,8,384]{2,1,0:T(8,128)(2,1)S(1)}, bf16[31,8,384]{2,1,0:T(8,128)(2,1)S(1)}, u32[]{:S(2)}, u32[]{:S(2)}) collective-permute-start(bf16[31,8,384]{2,1,0:T(8,128)(2,1)S(1)} %get-tuple-element.36), channel_id=1, source_target_pairs={{1,2},{2,1},{5,6},{6,5},{9,10},{10,9},{13,14},{14,13},{17,18},{18,... | collective-permute-start | bytes 571400 | tf_op jit(solution)/shard_map/ppermute | solution.py:619
  26.4 4.9 %copy-start.5 = (f32[1,5,4,8,384]{4,3,2,1,0:T(8,128)S(1)}, f32[1,5,4,8,384]{4,3,2,1,0:T(8,128)}, u32[]{:S(2)}) copy-start(f32[1,5,4,8,384]{4,3,2,1,0:T(8,128)} %refs_7_.1) | copy-start | bytes 737284
  26.5 4.6 %collective-permute-start.8 = (s16[2,8,16,128]{3,2,1,0:T(8,128)(2,1)S(1)}, s16[2,8,16,128]{3,2,1,0:T(8,128)(2,1)S(1)}, u32[]{:S(2)}, u32[]{:S(2)}) collective-permute-start(s16[2,8,16,128]{3,2,1,0:T(8,128)(2,1)S(1)} %get-tuple-element.38), channel_id=1, source_target_pairs={{0,1},{1,0},{2,3},{3,2},{4,5},{5,4},{6,7},{7,6},{8,9},{9,8},{10,11... | collective-permute-start | bytes 196616 | tf_op jit(solution)/shard_map/ppermute | solution.py:619
  26.5 4.5 %collective-permute-start.9 = (s16[2,8,16,128]{3,2,1,0:T(8,128)(2,1)S(1)}, s16[2,8,16,128]{3,2,1,0:T(8,128)(2,1)S(1)}, u32[]{:S(2)}, u32[]{:S(2)}) collective-permute-start(s16[2,8,16,128]{3,2,1,0:T(8,128)(2,1)S(1)} %get-tuple-element.39), channel_id=1, source_target_pairs={{1,2},{2,1},{5,6},{6,5},{9,10},{10,9},{13,14},{14,13},{17,18},{18,... | collective-permute-start | bytes 196616 | tf_op jit(solution)/shard_map/ppermute | solution.py:619
  34.2 7.0 %collective-permute-start.10 = (s16[2,16,16,128]{3,2,1,0:T(8,128)(2,1)S(1)}, s16[2,16,16,128]{3,2,1,0:T(8,128)(2,1)S(1)}, u32[]{:S(2)}, u32[]{:S(2)}) collective-permute-start(s16[2,16,16,128]{3,2,1,0:T(8,128)(2,1)S(1)} %get-tuple-element.43), channel_id=1, source_target_pairs={{0,4},{4,8},{8,12},{12,0},{1,5},{5,9},{9,13},{13,1},{2,6},{6,10},{... | collective-permute-start | bytes 393224 | tf_op jit(solution)/shard_map/ppermute | solution.py:608
  36.0 12.0 %collective-permute-start.11 = (s16[2,16,16,128]{3,2,1,0:T(8,128)(2,1)S(1)}, s16[2,16,16,128]{3,2,1,0:T(8,128)(2,1)S(1)}, u32[]{:S(2)}, u32[]{:S(2)}) collective-permute-start(s16[2,16,16,128]{3,2,1,0:T(8,128)(2,1)S(1)} %get-tuple-element.44), channel_id=1, source_target_pairs={{0,8},{4,12},{8,0},{12,4},{1,9},{5,13},{9,1},{13,5},{2,10},{6,14},... | collective-permute-start | bytes 393224 | tf_op jit(solution)/shard_map/ppermute | solution.py:608
  36.0 12.0 %collective-permute-start.12 = (s16[2,16,16,128]{3,2,1,0:T(8,128)(2,1)S(1)}, s16[2,16,16,128]{3,2,1,0:T(8,128)(2,1)S(1)}, u32[]{:S(2)}, u32[]{:S(2)}) collective-permute-start(s16[2,16,16,128]{3,2,1,0:T(8,128)(2,1)S(1)} %get-tuple-element.45), channel_id=1, source_target_pairs={{0,12},{4,0},{8,4},{12,8},{1,13},{5,1},{9,5},{13,9},{2,14},{6,2},{... | collective-permute-start | bytes 393224 | tf_op jit(solution)/shard_map/ppermute | solution.py:608

commit v10 on v8

--- a/solution.py
+++ b/solution.py
@@ -315,31 +315,27 @@
 
 
 def prepare_adjoint_kernel(
-    steps, nvar, levels, tiles, count_ref, near_ref, far_ref, dobs_ref, *refs
+    i, steps, nvar, tiles, count_ref, near_ref, far_ref, dobs_ref, after_ref, *refs
 ):
-    after_refs, (last_ref, force_ref) = refs[: levels // 2], refs[levels // 2 + 1 :]
+    _, last_ref, force_ref = refs
     even = even_place()
     blocks = [slice(0, SUB), slice(SUB, 2 * SUB)]
     cuts = [slice(t * LANES, (t + 1) * LANES) for t in range(tiles)]
     seen = [jnp.where(j < count_ref[0], 1.0, 0.0) for j in range(steps)]
     offset = -(-(nvar * tiles + 1) // 2) * 2
     none = [[jnp.zeros((SUB, LANES), jnp.float32)] * tiles]
-    for i, after_ref in enumerate(after_refs):
-        forces = [
-            none + decoded(ref, i, 2 * offset, steps - 1, tiles) for ref in (near_ref, far_ref)
-        ]
-        for odd in range(2):
-            lev = 2 * i + odd
-            scales = jnp.exp2(floats(after_ref[odd, nvar * tiles])) * (-1.0 / CODE_MAX)
-            for t in range(tiles):
-                for v in range(nvar):
-                    value = floats(after_ref[odd, v * tiles + t])
-                    last_ref[lev, v, t] = value * scales[:, v : v + 1]
-                for j in range(steps):
-                    near, far = (side[j][t] for side in forces)
-                    halves = widened(dobs_ref[0, j, lev, :, cuts[t]], near, far, odd, even)
-                    for b in range(2):
-                        force_ref[lev, j, t, blocks[b], :] = seen[j] * halves[b]
+    forces = [none + decoded(ref, i, 2 * offset, steps - 1, tiles) for ref in (near_ref, far_ref)]
+    for odd in range(2):
+        scales = jnp.exp2(floats(after_ref[odd, nvar * tiles])) * (-1.0 / CODE_MAX)
+        for t in range(tiles):
+            for v in range(nvar):
+                value = floats(after_ref[odd, v * tiles + t])
+                last_ref[odd, v, t] = value * scales[:, v : v + 1]
+            for j in range(steps):
+                near, far = (side[j][t] for side in forces)
+                halves = widened(dobs_ref[0, j, 2 * i + odd, :, cuts[t]], near, far, odd, even)
+                for b in range(2):
+                    force_ref[odd, j, t, blocks[b], :] = seen[j] * halves[b]
 
 
 def from_north(line, lane):
@@ -465,7 +461,7 @@
 
 
 def adjoint_kernel(
-    windows, spaces, steps, nvar, levels, tiles,
+    i, windows, spaces, steps, nvar, levels, tiles,
     mix_ref, total_ref, x_ref, last_ref, force_ref, ends_ref, inc_ref, rhs_ref, dual_ref,
     ndm_ref, ninc_ref, *rest,
 ):
@@ -474,107 +470,101 @@
     me = lax.axis_index("window")
     lane = lane_index()
     walled = walls(spaces)
-    pairs = levels // 2
     cuts = [slice(t * LANES, (t + 1) * LANES) for t in range(tiles)]
 
-    def pair(i, outer):
+    for odd in range(2):
+        lev = 2 * i + odd
+        for t in range(tiles):
+            for j in range(steps):
+                x0_ref[odd, j, t, SUB : 3 * SUB, :] = x_ref[lev, j, 0, t]
+            for v in range(nvar):
+                a_ref[odd, 0, v, t, SUB : 3 * SUB, :] = last_ref[odd, v, t]
+
+    def step(turn, carry):
+        now = lax.rem(turn, 2)
+        j = steps - 1 - turn
         for odd in range(2):
             lev = 2 * i + odd
+            for b in range(2):
+                part = slice(b * SUB, (b + 1) * SUB)
+                here, up, down = BLOCKS[b], UPS[b], DOWNS[b]
+                x = [[x_ref[lev, j, u, t, part, :] for t in range(tiles)] for u in range(nvar)]
+                ce = [diffusion + half_adv * x0_ref[odd, j, t, up, :] for t in range(tiles)]
+                cw = [diffusion - half_adv * x0_ref[odd, j, t, down, :] for t in range(tiles)]
+                ce, cw = walled(b, ce, cw)
+                cn = masked_first([diffusion + half_adv * value for value in x[1]], lane)
+                cs = masked_last([diffusion - half_adv * value for value in x[1]], lane)
+                a = [
+                    [a_ref[odd, now, u, t, here, :] for t in range(tiles)] for u in range(nvar)
+                ]
+                for u in range(nvar):
+                    north = from_north([cn[t] * a[u][t] for t in range(tiles)], lane)
+                    south = from_south([cs[t] * a[u][t] for t in range(tiles)], lane)
+                    for t in range(tiles):
+                        fresh = keep * a[u][t] + ce[t] * a_ref[odd, now, u, t, up, :]
+                        fresh = fresh + cw[t] * a_ref[odd, now, u, t, down, :]
+                        fresh = fresh + north[t] + south[t]
+                        pull = mix_ref[0, u] * a[0][t]
+                        for v in range(1, nvar):
+                            pull = pull + mix_ref[v, u] * a[v][t]
+                        fresh = fresh + x[u][t] * pull
+                        if u == 0:
+                            fresh = fresh + force_ref[odd, j, t, part, :]
+                        a_ref[odd, 1 - now, u, t, here, :] = fresh
+        return carry
+
+    lax.fori_loop(0, steps, step, 0)
+
+    end = steps % 2
+    coded = []
+    for odd in range(2):
+        lev = 2 * i + odd
+        back, ahead = [], []
+        for v in range(nvar):
+            share = total_ref[v * levels + lev]
+            tv, gv = [], []
             for t in range(tiles):
-                for j in range(steps):
-                    x0_ref[odd, j, t, SUB : 3 * SUB, :] = x_ref[lev, j, 0, t]
-                for v in range(nvar):
-                    a_ref[odd, 0, v, t, SUB : 3 * SUB, :] = last_ref[lev, v, t]
-
-        def step(turn, carry):
-            now = lax.rem(turn, 2)
-            j = steps - 1 - turn
-            for odd in range(2):
-                lev = 2 * i + odd
-                for b in range(2):
-                    part = slice(b * SUB, (b + 1) * SUB)
-                    here, up, down = BLOCKS[b], UPS[b], DOWNS[b]
-                    x = [[x_ref[lev, j, u, t, part, :] for t in range(tiles)] for u in range(nvar)]
-                    ce = [diffusion + half_adv * x0_ref[odd, j, t, up, :] for t in range(tiles)]
-                    cw = [diffusion - half_adv * x0_ref[odd, j, t, down, :] for t in range(tiles)]
-                    ce, cw = walled(b, ce, cw)
-                    cn = masked_first([diffusion + half_adv * value for value in x[1]], lane)
-                    cs = masked_last([diffusion - half_adv * value for value in x[1]], lane)
-                    a = [
-                        [a_ref[odd, now, u, t, here, :] for t in range(tiles)] for u in range(nvar)
-                    ]
-                    for u in range(nvar):
-                        north = from_north([cn[t] * a[u][t] for t in range(tiles)], lane)
-                        south = from_south([cs[t] * a[u][t] for t in range(tiles)], lane)
-                        for t in range(tiles):
-                            fresh = keep * a[u][t] + ce[t] * a_ref[odd, now, u, t, up, :]
-                            fresh = fresh + cw[t] * a_ref[odd, now, u, t, down, :]
-                            fresh = fresh + north[t] + south[t]
-                            pull = mix_ref[0, u] * a[0][t]
-                            for v in range(1, nvar):
-                                pull = pull + mix_ref[v, u] * a[v][t]
-                            fresh = fresh + x[u][t] * pull
-                            if u == 0:
-                                fresh = fresh + force_ref[lev, j, t, part, :]
-                            a_ref[odd, 1 - now, u, t, here, :] = fresh
-            return carry
-
-        lax.fori_loop(0, steps, step, 0)
-
-        end = steps % 2
-        coded = []
-        for odd in range(2):
-            lev = 2 * i + odd
-            back, ahead = [], []
-            for v in range(nvar):
-                share = total_ref[v * levels + lev]
-                tv, gv = [], []
-                for t in range(tiles):
-                    term = a_ref[odd, end, v, t, MINE, :] - last_ref[lev, v, t, HALF : HALF + SUB, :]
-                    given = rhs_ref[0, v, lev, :, cuts[t]] - inc_ref[0, v, lev, :, cuts[t]]
-                    given = given + share * term
-                    ndm_ref[v, lev, :, cuts[t]] = -(dual_ref[0, v, lev, :, cuts[t]] + term)
-                    ninc_ref[v, lev, :, cuts[t]] = given
-                    tv.append(term)
-                    gv.append(given + ends_ref[lev, v, t])
-                back.append(tv)
-                ahead.append(gv)
-            coded.append((row_codes(back), row_codes(ahead)))
-        for kind in range(2):
-            first, second = coded[0][kind], coded[1][kind]
-            for n, (a, b) in enumerate(zip(first[0] + [first[1]], second[0] + [second[1]])):
-                q_ref[kind, i, n] = shorts(jnp.concatenate([a, b], 0))
-        return outer
-
-    lax.fori_loop(0, pairs, pair, 0)
+                term = a_ref[odd, end, v, t, MINE, :] - last_ref[odd, v, t, HALF : HALF + SUB, :]
+                given = rhs_ref[0, v, lev, :, cuts[t]] - inc_ref[0, v, lev, :, cuts[t]]
+                given = given + share * term
+                ndm_ref[v, odd, :, cuts[t]] = -(dual_ref[0, v, lev, :, cuts[t]] + term)
+                ninc_ref[v, odd, :, cuts[t]] = given
+                tv.append(term)
+                gv.append(given + ends_ref[lev, v, t])
+            back.append(tv)
+            ahead.append(gv)
+        coded.append((row_codes(back), row_codes(ahead)))
+    for kind in range(2):
+        first, second = coded[0][kind], coded[1][kind]
+        for n, (a, b) in enumerate(zip(first[0] + [first[1]], second[0] + [second[1]])):
+            q_ref[kind, n] = shorts(jnp.concatenate([a, b], 0))
     for d in range(1, windows):
         payload_refs[d - 1][...] = q_ref[jnp.where(me + d >= windows, 0, 1)]
 
 
 def final_kernel(windows, nvar, levels, tiles, *refs):
-    pieces, refs = refs[:-5], refs[-5:]
-    total_ref, base_dual_ref, base_inc_ref, ndm_ref, ninc_ref = refs
+    pairs = levels // 2
+    cut = pairs * (windows - 1)
+    pieces, base_duals, base_incs = refs[:cut], refs[cut : cut + pairs], refs[cut + pairs : -3]
+    total_ref, ndm_ref, ninc_ref = refs[-3:]
     me = lax.axis_index("window")
-    pairs = levels // 2
     cuts = [slice(t * LANES, (t + 1) * LANES) for t in range(tiles)]
-    from_later = [d > me for d in range(1, windows)]
-
-    def pair(i, carry):
+
+    for i in range(pairs):
         tails = [None] * (nvar * tiles)
         heads = [None] * (nvar * tiles)
-
-        def add(sums, n, value):
-            sums[n] = value if sums[n] is None else sums[n] + value
-
-        for piece, later in zip(pieces, from_later):
-            scales = jnp.exp2(floats(piece[i, nvar * tiles])) * (1.0 / CODE_MAX)
+        for d in range(1, windows):
+            piece = pieces[i * (windows - 1) + d - 1]
+            later = d > me
+            scales = jnp.exp2(floats(piece[nvar * tiles])) * (1.0 / CODE_MAX)
             for v in range(nvar):
                 scale = scales[:, v : v + 1]
                 for t in range(tiles):
                     n = v * tiles + t
-                    value = floats(piece[i, n]) * scale
-                    add(tails, n, jnp.where(later, value, 0.0))
-                    add(heads, n, jnp.where(later, 0.0, value))
+                    value = floats(piece[n]) * scale
+                    tail, head = jnp.where(later, value, 0.0), jnp.where(later, 0.0, value)
+                    tails[n] = tail if d == 1 else tails[n] + tail
+                    heads[n] = head if d == 1 else heads[n] + head
         for v in range(nvar):
             for odd in range(2):
                 lev = 2 * i + odd
@@ -582,13 +572,10 @@
                 for t in range(tiles):
                     rows = slice(odd * SUB, (odd + 1) * SUB)
                     tail, head = tails[v * tiles + t][rows], heads[v * tiles + t][rows]
-                    ndm_ref[0, v, lev, :, cuts[t]] = base_dual_ref[v, lev, :, cuts[t]] - tail
+                    ndm_ref[0, v, lev, :, cuts[t]] = base_duals[i][v, odd, :, cuts[t]] - tail
                     ninc_ref[0, v, lev, :, cuts[t]] = (
-                        base_inc_ref[v, lev, :, cuts[t]] + head + share * tail
+                        base_incs[i][v, odd, :, cuts[t]] + head + share * tail
                     )
-        return carry
-
-    lax.fori_loop(0, pairs, pair, 0)
 
 
 def moved(block, axis, distance, around=False):
@@ -724,36 +711,45 @@
         compiler_params=params(),
     )(mix, share, obs, own, traj_near, traj_far, first)
 
-    last, force = pl.pallas_call(
-        lambda *refs: prepare_adjoint_kernel(steps, nvar, levels, tiles, *refs),
-        out_shape=[shape((levels, n, tiles, 2 * SUB, LANES), f32) for n in (nvar, steps)],
-        in_specs=[SMEM] + [VMEM] * (3 + pairs) + [ANY],
-        out_specs=[VMEM] * 2,
-        compiler_params=params(),
-    )(obs_count, near, far, dual_obs, *after, ends)
-    state = shape((nvar, levels, rows, columns), f32)
-    base_dual, base_inc, *payloads = pl.pallas_call(
-        lambda *refs: adjoint_kernel(windows, spaces, steps, nvar, levels, tiles, *refs),
-        out_shape=[state, state] + [payload] * (windows - 1),
-        in_specs=[VMEM] * 9,
-        out_specs=[VMEM] * (2 + windows - 1),
-        scratch_shapes=[
-            pltpu.VMEM((2, steps, tiles, 4 * SUB, LANES), f32),
-            pltpu.VMEM((2, 2, nvar, tiles, 4 * SUB, LANES), f32),
-            pltpu.VMEM((2,) + payload.shape, i16),
-        ],
-        compiler_params=params(),
-    )(mix, totals, wide_traj, last, force, ends, increment, model_rhs, dual_model)
-    sent = {d: moved(payloads[d - 1], "window", d, around=True) for d in order}
-    sent = [sent[d] for d in range(1, windows)]
+    state = shape((nvar, 2, rows, columns), f32)
+    coded = shape((nvar * tiles + 1, 2 * SUB, LANES), i16)
+    base_duals, base_incs, sent = [], [], []
+    before = ends
+    for i in range(pairs):
+        last, force = pl.pallas_call(
+            lambda *refs, i=i: prepare_adjoint_kernel(i, steps, nvar, tiles, *refs),
+            out_shape=[shape((2, n, tiles, 2 * SUB, LANES), f32) for n in (nvar, steps)],
+            in_specs=[SMEM] + [VMEM] * 4 + [ANY],
+            out_specs=[VMEM] * 2,
+            compiler_params=params(),
+        )(obs_count, near, far, dual_obs, after[i], before)
+        base_dual, base_inc, *payloads = pl.pallas_call(
+            lambda *refs, i=i: adjoint_kernel(
+                i, windows, spaces, steps, nvar, levels, tiles, *refs
+            ),
+            out_shape=[state, state] + [coded] * (windows - 1),
+            in_specs=[VMEM] * 9,
+            out_specs=[VMEM] * (2 + windows - 1),
+            scratch_shapes=[
+                pltpu.VMEM((2, steps, tiles, 4 * SUB, LANES), f32),
+                pltpu.VMEM((2, 2, nvar, tiles, 4 * SUB, LANES), f32),
+                pltpu.VMEM((2,) + coded.shape, i16),
+            ],
+            compiler_params=params(),
+        )(mix, totals, wide_traj, last, force, ends, increment, model_rhs, dual_model)
+        before = base_dual
+        base_duals.append(base_dual)
+        base_incs.append(base_inc)
+        moving = {d: moved(payloads[d - 1], "window", d, around=True) for d in order}
+        sent += [moving[d] for d in range(1, windows)]
 
     new_dual_model, new_increment = pl.pallas_call(
         lambda *refs: final_kernel(windows, nvar, levels, tiles, *refs),
         out_shape=[shape(dual_model.shape, f32), shape(increment.shape, f32)],
-        in_specs=[VMEM] * (len(sent) + 3),
+        in_specs=[VMEM] * (len(sent) + 2 * pairs + 1),
         out_specs=[VMEM] * 2,
         compiler_params=params(),
-    )(*sent, totals, base_dual, base_inc)
+    )(*sent, *base_duals, *base_incs, totals)
     return new_dual_model, new_dual_obs, new_increment
 
 

time: 48.2 us -> 47.4 us (0.983); the launches traced: 47.3 us -> 47.1 us
  waiting for transfers between devices: 17.1 us -> 11.2 us
  starting transfers between devices: 16.6 us -> 22.4 us
    ppermute x8 -> x11, waiting for transfers between devices: 17.1 us -> 11.2 us  [moved(): return lax.ppermute(block, axis, route)]
    ppermute x8 -> x11, starting transfers between devices: 15.1 us -> 20.9 us  [moved(): return lax.ppermute(block, axis, route)]
    pallas_call x2 -> x4, Pallas kernels: 3.06 us -> 3.13 us  [the longest x2 2.89 us: body(): pl.pallas_call(lambda *refs, i=i: adjoint_kernel(i, windows, spaces, step...]
  transfers between devices with their start and end apart: 12 -> 15, of which waited for: 5 -> 4; matrix products, arithmetic and copies ran while one was open for 0% -> 0% of each run, Pallas kernels for 13% -> 19%
where the time goes in v10:
time: 47.4 us; the launch traced here: 47.1 us
  starting transfers between devices  22.4 us (47%)
  waiting for transfers between devices  11.2 us (24%)
  Pallas kernels  10.2 us (22%)
  local copies, waits for them, and re-layouts  1.82 us (4%)
  between operations  1.55 us (3%)
    ppermute x11, starting transfers between devices, moved(): return lax.ppermute(block, axis, route)  20.9 us
    ppermute x11, waiting for transfers between devices, moved(): return lax.ppermute(block, axis, route)  11.2 us
    pallas_call x1, Pallas kernels, body(): pl.pallas_call(lambda *refs: tangent_kernel(spaces, steps, nvar, levels,...  3.58 us
    pallas_call x2, Pallas kernels, body(): pl.pallas_call(lambda *refs, i=i: adjoint_kernel(i, windows, spaces, step...  2.89 us
    ppermute x4, starting transfers between devices, swapped(): return lax.ppermute(block, axis, swaps(axis, first))  1.49 us
    unnamed x18, local copies, waits for them, and re-layouts  1.12 us
    pallas_call x1, Pallas kernels, body(): pl.pallas_call(lambda *refs: final_kernel(windows, nvar, levels, tiles, *...  1.02 us
  transfers between devices with their start and end apart: 15, of which 4 were waited for; matrix products, arithmetic and copies ran while one was open for 0% of the time, Pallas kernels for 19%

profile of v10, /device:TPU:0, one launch (start us, length us, event | category | flops | bytes accessed | tf_op | source)
XLA Modules:
  0.0 47.1 jit_solution(15303073810697891941)
XLA Ops:
  0.7 0.7 %pad.4.refs_0_ = f32[8,128]{1,0:T(8,128)S(1)} pad(f32[4,5]{1,0:T(4,128)} %bitcast.3, f32[]{:T(128)} %constant.2.clone.1), padding=0_4x0_123 | pad | bytes 4180 | tf_op jit(solution)/shard_map/jit(_pad)/pad | solution.py:624
  1.4 1.1 %copy-done = bf16[4,4,5,4,8,96]{5,4,3,2,1,0:T(8,128)(2,1)S(1)} copy-done((bf16[4,4,5,4,8,96]{5,4,3,2,1,0:T(8,128)(2,1)S(1)}, bf16[4,4,5,4,8,96]{5,4,3,2,1,0:T(8,128)(2,1)}, u32[]{:S(2)}) %copy-start) | copy-done | bytes 491544
  2.5 0.1 shard_map.123
  2.6 3.1 %collective-permute-start = (bf16[61,8,128]{2,1,0:T(8,128)(2,1)S(1)}, bf16[61,8,128]{2,1,0:T(8,128)(2,1)S(1)}, u32[]{:S(2)}, u32[]{:S(2)}) collective-permute-start(bf16[61,8,128]{2,1,0:T(8,128)(2,1)S(1)} %shard_map.123), channel_id=1, source_target_pairs={{0,4},{4,8},{8,12},{12,0},{1,5},{5,9},{9,13},{13,1},{2,6},{6,10},{... | collective-permute-start | bytes 374792 | tf_op jit(solution)/shard_map/ppermute | solution.py:584
  5.7 0.1 shard_map.124
  5.8 2.7 %collective-permute-start.1 = (bf16[61,8,128]{2,1,0:T(8,128)(2,1)S(1)}, bf16[61,8,128]{2,1,0:T(8,128)(2,1)S(1)}, u32[]{:S(2)}, u32[]{:S(2)}) collective-permute-start(bf16[61,8,128]{2,1,0:T(8,128)(2,1)S(1)} %shard_map.124), channel_id=1, source_target_pairs={{0,8},{4,12},{8,0},{12,4},{1,9},{5,13},{9,1},{13,5},{2,10},{6,14},... | collective-permute-start | bytes 374792 | tf_op jit(solution)/shard_map/ppermute | solution.py:584
  8.5 1.4 %collective-permute-start.2 = (bf16[61,8,128]{2,1,0:T(8,128)(2,1)S(1)}, bf16[61,8,128]{2,1,0:T(8,128)(2,1)S(1)}, u32[]{:S(2)}, u32[]{:S(2)}) collective-permute-start(bf16[61,8,128]{2,1,0:T(8,128)(2,1)S(1)} %shard_map.125), channel_id=1, source_target_pairs={{0,12},{4,0},{8,4},{12,8},{1,13},{5,1},{9,5},{13,9},{2,14},{6,2},{... | collective-permute-start | bytes 374792 | tf_op jit(solution)/shard_map/ppermute | solution.py:584
  10.0 0.5 shard_map.126
  10.5 0.7 %collective-permute-start.4 = (s16[2,21,16,128]{3,2,1,0:T(8,128)(2,1)S(1)}, s16[2,21,16,128]{3,2,1,0:T(8,128)(2,1)S(1)}, u32[]{:S(2)}, u32[]{:S(2)}) collective-permute-start(s16[2,21,16,128]{3,2,1,0:T(8,128)(2,1)S(1)} %get-tuple-element.37), channel_id=1, source_target_pairs={{1,2},{2,1},{5,6},{6,5},{9,10},{10,9},{13,14},{14,13},{17,18},{18,... | collective-permute-start | bytes 516104 | tf_op jit(solution)/shard_map/ppermute | solution.py:595
  11.2 0.1 shard_map.122.refs_0_
  12.0 0.7 %shard_map.121 = (f32[4,4,3,8,128]{4,3,2,1,0:T(8,128)S(1)}, f32[4,4,8,128]{3,2,1,0:T(8,128)S(1)}, f32[5,5,8,128]{3,2,1,0:T(8,128)S(1)}) custom-call(s32[1]{0:T(128)S(6)} %copy.13.refs_0_, f32[1,4,4]{2,1,0:T(4,128)S(1)} %copy-done.8, f32[5,5]{1,0:T(8,128)S(1)} %copy-done.7, f32[1,4,4,8,384]{4,3,2,1,0:T(8,128)S(1)} %copy-done.3, f32[1,4,4,8,384]{4,3,2,1,0:T(8,128)S(1)} %copy-done.6), custom_call_target="tpu_custom_call" | custom-call | tf_op jit(solution)/shard_map/pallas_call | solution.py:668
  12.7 3.8 %collective-permute-done.1.refs_2_ = bf16[61,8,128]{2,1,0:T(8,128)(2,1)S(1)} collective-permute-done((bf16[61,8,128]{2,1,0:T(8,128)(2,1)S(1)}, bf16[61,8,128]{2,1,0:T(8,128)(2,1)S(1)}, u32[]{:S(2)}, u32[]{:S(2)}) %collective-permute-start.1) | collective-permute-done | bytes 124960 | tf_op jit(solution)/shard_map/ppermute | solution.py:584
  16.5 0.5 shard_map.128
  17.1 0.7 %collective-permute-start.6 = (bf16[31,8,384]{2,1,0:T(8,128)(2,1)S(1)}, bf16[31,8,384]{2,1,0:T(8,128)(2,1)S(1)}, u32[]{:S(2)}, u32[]{:S(2)}) collective-permute-start(bf16[31,8,384]{2,1,0:T(8,128)(2,1)S(1)} %get-tuple-element.43), channel_id=1, source_target_pairs={{1,2},{2,1},{5,6},{6,5},{9,10},{10,9},{13,14},{14,13},{17,18},{18,... | collective-permute-start | bytes 571400 | tf_op jit(solution)/shard_map/ppermute | solution.py:595
  17.8 0.3 shard_map.127
  18.0 1.4 %collective-permute-start.7 = (s16[2,16,16,128]{3,2,1,0:T(8,128)(2,1)S(1)}, s16[2,16,16,128]{3,2,1,0:T(8,128)(2,1)S(1)}, u32[]{:S(2)}, u32[]{:S(2)}) collective-permute-start(s16[2,16,16,128]{3,2,1,0:T(8,128)(2,1)S(1)} %get-tuple-element.45), channel_id=1, source_target_pairs={{4,0},{8,4},{12,8},{5,1},{9,5},{13,9},{6,2},{10,6},{14,10},{7,3},{... | collective-permute-start | bytes 393224 | tf_op jit(solution)/shard_map/ppermute | solution.py:584
  19.5 1.3 %collective-permute-start.11 = (s16[2,16,16,128]{3,2,1,0:T(8,128)(2,1)S(1)}, s16[2,16,16,128]{3,2,1,0:T(8,128)(2,1)S(1)}, u32[]{:S(2)}, u32[]{:S(2)}) collective-permute-start(s16[2,16,16,128]{3,2,1,0:T(8,128)(2,1)S(1)} %get-tuple-element.52), channel_id=1, source_target_pairs={{4,0},{8,4},{12,8},{5,1},{9,5},{13,9},{6,2},{10,6},{14,10},{7,3},{... | collective-permute-start | bytes 393224 | tf_op jit(solution)/shard_map/ppermute | solution.py:584
  20.8 0.1 shard_map.129.refs_6_
  20.9 3.6 %shard_map.130 = (f32[1,4,4,8,384]{4,3,2,1,0:T(8,128)}, f32[4,5,3,8,128]{4,3,2,1,0:T(8,128)S(1)}, f32[4,4,5,3,16,128]{5,4,3,2,1,0:T(8,128)S(1)}) custom-call(f32[5,5,8,128]{3,2,1,0:T(8,128)S(1)} %get-tuple-element.34.refs_4_.refs_0_, f32[4,4,8,128]{3,2,1,0:T(8,128)S(1)} %get-tuple-element.39.refs_1_, f32[4,4,3,8,128]{4,3,2,1,0:T(8,128)S(1)} %get-tuple-element.40.refs_2_, ...), custom_call_target="tpu_custom_call" | custom-call | tf_op jit(solution)/shard_map/pallas_call | solution.py:701
  24.5 1.7 %collective-permute-done.7.refs_4_ = s16[2,16,16,128]{3,2,1,0:T(8,128)(2,1)S(1)} collective-permute-done((s16[2,16,16,128]{3,2,1,0:T(8,128)(2,1)S(1)}, s16[2,16,16,128]{3,2,1,0:T(8,128)(2,1)S(1)}, u32[]{:S(2)}, u32[]{:S(2)}) %collective-permute-start.7) | collective-permute-done | bytes 131104 | tf_op jit(solution)/shard_map/ppermute | solution.py:584
  26.2 0.1 shard_map.131
  26.3 1.4 %shard_map.132 = (f32[5,2,8,384]{3,2,1,0:T(8,128)S(1)}, f32[5,2,8,384]{3,2,1,0:T(8,128)S(1)}, s16[16,16,128]{2,1,0:T(8,128)(2,1)S(1)}, s16[16,16,128]{2,1,0:T(8,128)(2,1)S(1)}, s16[16,16,128]{2,1,0:T(8,128)(2,1)S(1)}) custom-call(f32[5,5,8,128]{3,2,1,0:T(8,128)S(1)} %get-tuple-element.34.refs_4_.refs_0_, ...), custom_call_target="tpu_custom_call" | custom-call | tf_op jit(solution)/shard_map/pallas_call | solution.py:726
  27.7 2.8 %collective-permute-start.8 = (s16[16,16,128]{2,1,0:T(8,128)(2,1)S(1)}, s16[16,16,128]{2,1,0:T(8,128)(2,1)S(1)}, u32[]{:S(2)}, u32[]{:S(2)}) collective-permute-start(s16[16,16,128]{2,1,0:T(8,128)(2,1)S(1)} %get-tuple-element.49), channel_id=1, source_target_pairs={{0,4},{4,8},{8,12},{12,0},{1,5},{5,9},{9,13},{13,1},{2,6},{6,10},{... | collective-permute-start | bytes 196616 | tf_op jit(solution)/shard_map/ppermute | solution.py:584
  30.6 3.5 %collective-permute-start.9 = (s16[16,16,128]{2,1,0:T(8,128)(2,1)S(1)}, s16[16,16,128]{2,1,0:T(8,128)(2,1)S(1)}, u32[]{:S(2)}, u32[]{:S(2)}) collective-permute-start(s16[16,16,128]{2,1,0:T(8,128)(2,1)S(1)} %get-tuple-element.50), channel_id=1, source_target_pairs={{0,8},{4,12},{8,0},{12,4},{1,9},{5,13},{9,1},{13,5},{2,10},{6,14},... | collective-permute-start | bytes 196616 | tf_op jit(solution)/shard_map/ppermute | solution.py:584
  34.0 0.9 %collective-permute-start.10 = (s16[16,16,128]{2,1,0:T(8,128)(2,1)S(1)}, s16[16,16,128]{2,1,0:T(8,128)(2,1)S(1)}, u32[]{:S(2)}, u32[]{:S(2)}) collective-permute-start(s16[16,16,128]{2,1,0:T(8,128)(2,1)S(1)} %get-tuple-element.51), channel_id=1, source_target_pairs={{0,12},{4,0},{8,4},{12,8},{1,13},{5,1},{9,5},{13,9},{2,14},{6,2},{... | collective-permute-start | bytes 196616 | tf_op jit(solution)/shard_map/ppermute | solution.py:584
  34.9 0.1 shard_map.133
  35.1 1.4 %shard_map.134 = (f32[5,2,8,384]{3,2,1,0:T(8,128)S(1)}, f32[5,2,8,384]{3,2,1,0:T(8,128)S(1)}, s16[16,16,128]{2,1,0:T(8,128)(2,1)S(1)}, s16[16,16,128]{2,1,0:T(8,128)(2,1)S(1)}, s16[16,16,128]{2,1,0:T(8,128)(2,1)S(1)}) custom-call(f32[5,5,8,128]{3,2,1,0:T(8,128)S(1)} %get-tuple-element.34.refs_4_.refs_0_, ...), custom_call_target="tpu_custom_call" | custom-call | tf_op jit(solution)/shard_map/pallas_call | solution.py:726
  36.5 1.2 %collective-permute-start.12 = (s16[16,16,128]{2,1,0:T(8,128)(2,1)S(1)}, s16[16,16,128]{2,1,0:T(8,128)(2,1)S(1)}, u32[]{:S(2)}, u32[]{:S(2)}) collective-permute-start(s16[16,16,128]{2,1,0:T(8,128)(2,1)S(1)} %get-tuple-element.56), channel_id=1, source_target_pairs={{0,4},{4,8},{8,12},{12,0},{1,5},{5,9},{9,13},{13,1},{2,6},{6,10},{... | collective-permute-start | bytes 196616 | tf_op jit(solution)/shard_map/ppermute | solution.py:584
  37.7 2.7 %collective-permute-start.14 = (s16[16,16,128]{2,1,0:T(8,128)(2,1)S(1)}, s16[16,16,128]{2,1,0:T(8,128)(2,1)S(1)}, u32[]{:S(2)}, u32[]{:S(2)}) collective-permute-start(s16[16,16,128]{2,1,0:T(8,128)(2,1)S(1)} %get-tuple-element.58), channel_id=1, source_target_pairs={{0,12},{4,0},{8,4},{12,8},{1,13},{5,1},{9,5},{13,9},{2,14},{6,2},{... | collective-permute-start | bytes 196616 | tf_op jit(solution)/shard_map/ppermute | solution.py:584
  40.4 2.3 %collective-permute-done.12.refs_3_ = s16[16,16,128]{2,1,0:T(8,128)(2,1)S(1)} collective-permute-done((s16[16,16,128]{2,1,0:T(8,128)(2,1)S(1)}, s16[16,16,128]{2,1,0:T(8,128)(2,1)S(1)}, u32[]{:S(2)}, u32[]{:S(2)}) %collective-permute-start.12) | collective-permute-done | bytes 65568 | tf_op jit(solution)/shard_map/ppermute | solution.py:584
  42.7 3.4 %collective-permute-done.13.refs_4_ = s16[16,16,128]{2,1,0:T(8,128)(2,1)S(1)} collective-permute-done((s16[16,16,128]{2,1,0:T(8,128)(2,1)S(1)}, s16[16,16,128]{2,1,0:T(8,128)(2,1)S(1)}, u32[]{:S(2)}, u32[]{:S(2)}) %collective-permute-start.13) | collective-permute-done | bytes 65568 | tf_op jit(solution)/shard_map/ppermute | solution.py:584
  46.1 1.0 %shard_map.135 = (f32[1,5,4,8,384]{4,3,2,1,0:T(8,128)}, f32[1,5,4,8,384]{4,3,2,1,0:T(8,128)}) custom-call(s16[16,16,128]{2,1,0:T(8,128)(2,1)S(1)} %collective-permute-done.8.refs_0_, s16[16,16,128]{2,1,0:T(8,128)(2,1)S(1)} %collective-permute-done.9.refs_1_, s16[16,16,128]{2,1,0:T(8,128)(2,1)S(1)} %collective-permute-done.10.refs_2_, ...), custom_call_target="tpu_custom_call" | custom-call | tf_op jit(solution)/shard_map/pallas_call | solution.py:746
  (32 shorter events, 0.3 us)
Async XLA Ops:
  0.6 11.3 %copy-start.8 = (f32[1,4,4]{2,1,0:T(4,128)S(1)}, f32[1,4,4]{2,1,0:T(4,128)}, u32[]{:S(2)}) copy-start(f32[1,4,4]{2,1,0:T(4,128)} %refs_1_.6) | copy-start | bytes 196
  0.6 11.3 %copy-start.7 = (f32[5,5]{1,0:T(8,128)S(1)}, f32[5,5]{1,0:T(8,128)}, u32[]{:S(2)}) copy-start(f32[5,5]{1,0:T(8,128)} %refs_2_.3) | copy-start | bytes 304
  1.3 1.1 %copy-start = (bf16[4,4,5,4,8,96]{5,4,3,2,1,0:T(8,128)(2,1)S(1)}, bf16[4,4,5,4,8,96]{5,4,3,2,1,0:T(8,128)(2,1)}, u32[]{:S(2)}) copy-start(bf16[4,4,5,4,8,96]{5,4,3,2,1,0:T(8,128)(2,1)} %refs_1_.10) | copy-start | bytes 1474564
  2.4 7.5 %copy-start.2 = (f32[1,5,4,8,384]{4,3,2,1,0:T(8,128)S(1)}, f32[1,5,4,8,384]{4,3,2,1,0:T(8,128)}, u32[]{:S(2)}) copy-start(f32[1,5,4,8,384]{4,3,2,1,0:T(8,128)} %refs_6_.3) | copy-start | bytes 737284
  2.4 7.5 %copy-start.3 = (f32[1,4,4,8,384]{4,3,2,1,0:T(8,128)S(1)}, f32[1,4,4,8,384]{4,3,2,1,0:T(8,128)}, u32[]{:S(2)}) copy-start(f32[1,4,4,8,384]{4,3,2,1,0:T(8,128)} %refs_3_.5) | copy-start | bytes 589828
  2.4 7.5 %copy-start.4 = (f32[1,5,4,8,384]{4,3,2,1,0:T(8,128)S(1)}, f32[1,5,4,8,384]{4,3,2,1,0:T(8,128)}, u32[]{:S(2)}) copy-start(f32[1,5,4,8,384]{4,3,2,1,0:T(8,128)} %refs_8_.3) | copy-start | bytes 737284
  2.4 8.7 %copy-start.1 = (bf16[4,4,5,4,8,96]{5,4,3,2,1,0:T(8,128)(2,1)S(1)}, bf16[4,4,5,4,8,96]{5,4,3,2,1,0:T(8,128)(2,1)}, u32[]{:S(2)}) copy-start(bf16[4,4,5,4,8,96]{5,4,3,2,1,0:T(8,128)(2,1)} %refs_1_.10) | copy-start | bytes 1474564
  2.4 9.5 %copy-start.6 = (f32[1,4,4,8,384]{4,3,2,1,0:T(8,128)S(1)}, f32[1,4,4,8,384]{4,3,2,1,0:T(8,128)}, u32[]{:S(2)}) copy-start(f32[1,4,4,8,384]{4,3,2,1,0:T(8,128)} %refs_4_.1) | copy-start | bytes 589828
  2.6 10.1 %collective-permute-start = (bf16[61,8,128]{2,1,0:T(8,128)(2,1)S(1)}, bf16[61,8,128]{2,1,0:T(8,128)(2,1)S(1)}, u32[]{:S(2)}, u32[]{:S(2)}) collective-permute-start(bf16[61,8,128]{2,1,0:T(8,128)(2,1)S(1)} %shard_map.123), channel_id=1, source_target_pairs={{0,4},{4,8},{8,12},{12,0},{1,5},{5,9},{9,13},{13,1},{2,6},{6,10},{... | collective-permute-start | bytes 374792 | tf_op jit(solution)/shard_map/ppermute | solution.py:584
  5.8 10.7 %collective-permute-start.1 = (bf16[61,8,128]{2,1,0:T(8,128)(2,1)S(1)}, bf16[61,8,128]{2,1,0:T(8,128)(2,1)S(1)}, u32[]{:S(2)}, u32[]{:S(2)}) collective-permute-start(bf16[61,8,128]{2,1,0:T(8,128)(2,1)S(1)} %shard_map.124), channel_id=1, source_target_pairs={{0,8},{4,12},{8,0},{12,4},{1,9},{5,13},{9,1},{13,5},{2,10},{6,14},... | collective-permute-start | bytes 374792 | tf_op jit(solution)/shard_map/ppermute | solution.py:584
  8.5 8.0 %collective-permute-start.2 = (bf16[61,8,128]{2,1,0:T(8,128)(2,1)S(1)}, bf16[61,8,128]{2,1,0:T(8,128)(2,1)S(1)}, u32[]{:S(2)}, u32[]{:S(2)}) collective-permute-start(bf16[61,8,128]{2,1,0:T(8,128)(2,1)S(1)} %shard_map.125), channel_id=1, source_target_pairs={{0,12},{4,0},{8,4},{12,8},{1,13},{5,1},{9,5},{13,9},{2,14},{6,2},{... | collective-permute-start | bytes 374792 | tf_op jit(solution)/shard_map/ppermute | solution.py:584
  10.4 7.3 %collective-permute-start.3 = (s16[2,21,16,128]{3,2,1,0:T(8,128)(2,1)S(1)}, s16[2,21,16,128]{3,2,1,0:T(8,128)(2,1)S(1)}, u32[]{:S(2)}, u32[]{:S(2)}) collective-permute-start(s16[2,21,16,128]{3,2,1,0:T(8,128)(2,1)S(1)} %get-tuple-element.36), channel_id=1, source_target_pairs={{0,1},{1,0},{2,3},{3,2},{4,5},{5,4},{6,7},{7,6},{8,9},{9,8},{10,11... | collective-permute-start | bytes 516104 | tf_op jit(solution)/shard_map/ppermute | solution.py:595
  10.5 7.2 %collective-permute-start.4 = (s16[2,21,16,128]{3,2,1,0:T(8,128)(2,1)S(1)}, s16[2,21,16,128]{3,2,1,0:T(8,128)(2,1)S(1)}, u32[]{:S(2)}, u32[]{:S(2)}) collective-permute-start(s16[2,21,16,128]{3,2,1,0:T(8,128)(2,1)S(1)} %get-tuple-element.37), channel_id=1, source_target_pairs={{1,2},{2,1},{5,6},{6,5},{9,10},{10,9},{13,14},{14,13},{17,18},{18,... | collective-permute-start | bytes 516104 | tf_op jit(solution)/shard_map/ppermute | solution.py:595
  17.0 3.9 %collective-permute-start.5 = (bf16[4,10,8,384]{3,2,1,0:T(8,128)(2,1)S(1)}, bf16[4,10,8,384]{3,2,1,0:T(8,128)(2,1)S(1)}, u32[]{:S(2)}, u32[]{:S(2)}) collective-permute-start(bf16[4,10,8,384]{3,2,1,0:T(8,128)(2,1)S(1)} %get-tuple-element.42), channel_id=1, source_target_pairs={{0,1},{1,0},{2,3},{3,2},{4,5},{5,4},{6,7},{7,6},{8,9},{9,8},{10,11... | collective-permute-start | bytes 737288 | tf_op jit(solution)/shard_map/ppermute | solution.py:595
  17.1 3.9 %collective-permute-start.6 = (bf16[31,8,384]{2,1,0:T(8,128)(2,1)S(1)}, bf16[31,8,384]{2,1,0:T(8,128)(2,1)S(1)}, u32[]{:S(2)}, u32[]{:S(2)}) collective-permute-start(bf16[31,8,384]{2,1,0:T(8,128)(2,1)S(1)} %get-tuple-element.43), channel_id=1, source_target_pairs={{1,2},{2,1},{5,6},{6,5},{9,10},{10,9},{13,14},{14,13},{17,18},{18,... | collective-permute-start | bytes 571400 | tf_op jit(solution)/shard_map/ppermute | solution.py:595
  18.0 8.3 %copy-start.5 = (f32[1,5,4,8,384]{4,3,2,1,0:T(8,128)S(1)}, f32[1,5,4,8,384]{4,3,2,1,0:T(8,128)}, u32[]{:S(2)}) copy-start(f32[1,5,4,8,384]{4,3,2,1,0:T(8,128)} %refs_7_.3) | copy-start | bytes 737284
  18.0 8.1 %collective-permute-start.7 = (s16[2,16,16,128]{3,2,1,0:T(8,128)(2,1)S(1)}, s16[2,16,16,128]{3,2,1,0:T(8,128)(2,1)S(1)}, u32[]{:S(2)}, u32[]{:S(2)}) collective-permute-start(s16[2,16,16,128]{3,2,1,0:T(8,128)(2,1)S(1)} %get-tuple-element.45), channel_id=1, source_target_pairs={{4,0},{8,4},{12,8},{5,1},{9,5},{13,9},{6,2},{10,6},{14,10},{7,3},{... | collective-permute-start | bytes 393224 | tf_op jit(solution)/shard_map/ppermute | solution.py:584
  19.5 15.5 %collective-permute-start.11 = (s16[2,16,16,128]{3,2,1,0:T(8,128)(2,1)S(1)}, s16[2,16,16,128]{3,2,1,0:T(8,128)(2,1)S(1)}, u32[]{:S(2)}, u32[]{:S(2)}) collective-permute-start(s16[2,16,16,128]{3,2,1,0:T(8,128)(2,1)S(1)} %get-tuple-element.52), channel_id=1, source_target_pairs={{4,0},{8,4},{12,8},{5,1},{9,5},{13,9},{6,2},{10,6},{14,10},{7,3},{... | collective-permute-start | bytes 393224 | tf_op jit(solution)/shard_map/ppermute | solution.py:584
  27.7 9.9 %collective-permute-start.8 = (s16[16,16,128]{2,1,0:T(8,128)(2,1)S(1)}, s16[16,16,128]{2,1,0:T(8,128)(2,1)S(1)}, u32[]{:S(2)}, u32[]{:S(2)}) collective-permute-start(s16[16,16,128]{2,1,0:T(8,128)(2,1)S(1)} %get-tuple-element.49), channel_id=1, source_target_pairs={{0,4},{4,8},{8,12},{12,0},{1,5},{5,9},{9,13},{13,1},{2,6},{6,10},{... | collective-permute-start | bytes 196616 | tf_op jit(solution)/shard_map/ppermute | solution.py:584
  30.6 9.8 %collective-permute-start.9 = (s16[16,16,128]{2,1,0:T(8,128)(2,1)S(1)}, s16[16,16,128]{2,1,0:T(8,128)(2,1)S(1)}, u32[]{:S(2)}, u32[]{:S(2)}) collective-permute-start(s16[16,16,128]{2,1,0:T(8,128)(2,1)S(1)} %get-tuple-element.50), channel_id=1, source_target_pairs={{0,8},{4,12},{8,0},{12,4},{1,9},{5,13},{9,1},{13,5},{2,10},{6,14},... | collective-permute-start | bytes 196616 | tf_op jit(solution)/shard_map/ppermute | solution.py:584
  34.0 6.4 %collective-permute-start.10 = (s16[16,16,128]{2,1,0:T(8,128)(2,1)S(1)}, s16[16,16,128]{2,1,0:T(8,128)(2,1)S(1)}, u32[]{:S(2)}, u32[]{:S(2)}) collective-permute-start(s16[16,16,128]{2,1,0:T(8,128)(2,1)S(1)} %get-tuple-element.51), channel_id=1, source_target_pairs={{0,12},{4,0},{8,4},{12,8},{1,13},{5,1},{9,5},{13,9},{2,14},{6,2},{... | collective-permute-start | bytes 196616 | tf_op jit(solution)/shard_map/ppermute | solution.py:584
  36.5 6.2 %collective-permute-start.12 = (s16[16,16,128]{2,1,0:T(8,128)(2,1)S(1)}, s16[16,16,128]{2,1,0:T(8,128)(2,1)S(1)}, u32[]{:S(2)}, u32[]{:S(2)}) collective-permute-start(s16[16,16,128]{2,1,0:T(8,128)(2,1)S(1)} %get-tuple-element.56), channel_id=1, source_target_pairs={{0,4},{4,8},{8,12},{12,0},{1,5},{5,9},{9,13},{13,1},{2,6},{6,10},{... | collective-permute-start | bytes 196616 | tf_op jit(solution)/shard_map/ppermute | solution.py:584
  37.7 8.4 %collective-permute-start.13 = (s16[16,16,128]{2,1,0:T(8,128)(2,1)S(1)}, s16[16,16,128]{2,1,0:T(8,128)(2,1)S(1)}, u32[]{:S(2)}, u32[]{:S(2)}) collective-permute-start(s16[16,16,128]{2,1,0:T(8,128)(2,1)S(1)} %get-tuple-element.57), channel_id=1, source_target_pairs={{0,8},{4,12},{8,0},{12,4},{1,9},{5,13},{9,1},{13,5},{2,10},{6,14},... | collective-permute-start | bytes 196616 | tf_op jit(solution)/shard_map/ppermute | solution.py:584
  37.7 8.4 %collective-permute-start.14 = (s16[16,16,128]{2,1,0:T(8,128)(2,1)S(1)}, s16[16,16,128]{2,1,0:T(8,128)(2,1)S(1)}, u32[]{:S(2)}, u32[]{:S(2)}) collective-permute-start(s16[16,16,128]{2,1,0:T(8,128)(2,1)S(1)} %get-tuple-element.58), channel_id=1, source_target_pairs={{0,12},{4,0},{8,4},{12,8},{1,13},{5,1},{9,5},{13,9},{2,14},{6,2},{... | collective-permute-start | bytes 196616 | tf_op jit(solution)/shard_map/ppermute | solution.py:584

commit v11 on v10

--- a/solution.py
+++ b/solution.py
@@ -104,8 +104,7 @@
     return value.astype(jnp.int32).astype(jnp.float32)
 
 
-def pack_kernel(distances, windows, steps, nvar, levels, part, var_ref, traj_ref, *outs):
-    me = lax.axis_index("window")
+def pack_kernel(steps, nvar, levels, part, var_ref, traj_ref, out_ref):
     lane = lane_index()
     variance = var_ref[...]
     high = variance.astype(jnp.bfloat16).astype(jnp.float32)
@@ -114,22 +113,18 @@
     split = high + pltpu.roll(middle, HALF, 0) + pltpu.roll(low, LANES // 2, 1)
     split = split.astype(jnp.bfloat16)
 
-    for n, d in enumerate(distances):
-        outs[n][outs[n].shape[0] - 1] = split
-        target = lax.rem(me + d, windows)
-
-        def variable(v, carry, n=n, target=target):
+    def window(w, carry):
+        out_ref[w, out_ref.shape[1] - 1] = split
+        for v in range(nvar):
             for lev in range(levels):
-                pieces = [
-                    tiled(traj_ref[target, j, v, lev].astype(jnp.float32)) for j in range(steps)
-                ]
+                pieces = [tiled(traj_ref[w, j, v, lev].astype(jnp.float32)) for j in range(steps)]
                 parts = [(j, pieces[j], 0, part, j * part) for j in range(steps)]
                 placed = place(parts, {}, lane)
                 for t, value in enumerate(placed):
-                    outs[n][(v * levels + lev) * len(placed) + t] = value.astype(jnp.bfloat16)
-            return carry
-
-        lax.fori_loop(0, nvar, variable, 0, unroll=len(distances) == 1)
+                    out_ref[w, (v * levels + lev) * len(placed) + t] = value.astype(jnp.bfloat16)
+        return carry
+
+    lax.fori_loop(0, out_ref.shape[0], window, 0)
 
 
 def even_place():
@@ -146,7 +141,7 @@
 
 
 def half_code_kernel(*refs):
-    sources, (near_ref, far_ref, own_ref) = refs[:-3], refs[-3:]
+    sources, (near_ref, far_ref, own_ref) = refs[:-4], refs[-3:]
     even = even_place()
 
     def pair(i, carry):
@@ -177,15 +172,15 @@
 
 
 def around_kernel(windows, nvar, levels, *refs):
-    pieces, (own_ref, near_ref, far_ref) = refs[:windows], refs[windows : windows + 3]
-    outs, total_ref = refs[windows + 3 : -1], refs[-1]
+    blocks_ref, own_ref, near_ref, far_ref = refs[:4]
+    outs, total_ref = refs[4:-1], refs[-1]
     me = lax.axis_index("window")
     even = even_place()
     total = jnp.zeros((SUB, LANES), jnp.float32)
-    for d in range(windows):
-        split = pieces[d][pieces[d].shape[0] - 1].astype(jnp.float32)
+    for w in range(windows):
+        split = blocks_ref[w, blocks_ref.shape[1] - 1].astype(jnp.float32)
         here = split + pltpu.roll(split, HALF, 0) + pltpu.roll(split, LANES // 2, 1)
-        total = total + jnp.where(lax.rem(me - d + windows, windows) <= me, here, 0.0)
+        total = total + jnp.where(w <= me, here, 0.0)
     for v in range(nvar):
         for lev in range(levels):
             one = total[lev : lev + 1, v : v + 1]
@@ -230,16 +225,10 @@
 
 
 def assemble_kernel(windows, steps, nvar, levels, part, *refs):
-    pieces = refs[:windows]
-    own_ref, near_ref, far_ref, stack_ref = refs[windows + 1 :]
-    me = lax.axis_index("window")
+    blocks_ref, _, own_ref, near_ref, far_ref = refs
     even = even_place()
     lane = lane_index()
-    count = stack_ref.shape[1]
-    packed_tiles = count // (nvar * levels)
-    for d in range(windows):
-        source = lax.rem(me - d + windows, windows)
-        stack_ref[source] = pieces[d][:count]
+    packed_tiles = blocks_ref.shape[1] // (nvar * levels)
 
     pairs = levels // 2
     base, _ = far_base(steps, nvar, levels)
@@ -250,7 +239,7 @@
             plane = v * levels + lev
             sources = [
                 [
-                    stack_ref[w, plane * packed_tiles + t].astype(jnp.float32)
+                    blocks_ref[w, plane * packed_tiles + t].astype(jnp.float32)
                     for t in range(packed_tiles)
                 ]
                 for w in range(windows)
@@ -623,22 +612,15 @@
     block = shape((nvar * levels * wide // LANES + 1, rows, LANES), bf16)
     variances = jnp.pad(error_var[0].T, ((0, SUB - levels), (0, LANES - nvar)))
 
-    def packed(distances):
-        return pl.pallas_call(
-            lambda *refs: pack_kernel(distances, windows, steps, nvar, levels, part, *refs),
-            out_shape=[block] * len(distances),
-            in_specs=[VMEM, VMEM],
-            out_specs=[VMEM] * len(distances),
-            compiler_params=params(),
-        )(variances, trajectory)
-
+    blocks = pl.pallas_call(
+        lambda *refs: pack_kernel(steps, nvar, levels, part, *refs),
+        out_shape=shape((windows,) + block.shape, bf16),
+        in_specs=[VMEM, VMEM],
+        out_specs=VMEM,
+        compiler_params=params(),
+    )(variances, trajectory)
+    packed, blocks = blocks, lax.all_to_all(blocks, "window", 0, 0, tiled=True)
     order = sorted(range(1, windows), key=lambda d: -d * (windows - d))
-    groups = [[d] for d in order] if windows <= 4 else [order]
-    blocks = {}
-    for group in groups:
-        blocks.update(zip(group, packed(group)))
-    arrived = {d: moved(blocks[d], "window", d, around=True) for d in order}
-    arrived[0] = packed([0])[0]
 
     payload = shape((pairs, nvar * tiles + 1, 2 * SUB, LANES), i16)
 
@@ -648,21 +630,20 @@
     near, far, dual = pl.pallas_call(
         half_code_kernel,
         out_shape=[halves, halves, payload],
-        in_specs=[VMEM] * 3,
+        in_specs=[VMEM] * 3 + [ANY],
         out_specs=[VMEM] * 3,
         compiler_params=params(),
-    )(dual_model, increment, dual_obs)
+    )(dual_model, increment, dual_obs, packed)
     far, near = swapped(far, "space", 1), swapped(near, "space", 0)
 
-    blocks_here = [arrived[d] for d in range(windows)]
     *after, totals = pl.pallas_call(
         lambda *refs: around_kernel(windows, nvar, levels, *refs),
         out_shape=[shape((2,) + payload.shape[1:], i16)] * pairs
         + [shape((nvar * levels, rows, LANES), f32)],
-        in_specs=[VMEM] * (windows + 3),
+        in_specs=[VMEM] * 4,
         out_specs=[VMEM] * (pairs + 1),
         compiler_params=params(),
-    )(*blocks_here, dual, near, far)
+    )(blocks, dual, near, far)
     after = [moved(piece, "window", -1) for piece in after]
 
     obs, share, mix = pl.pallas_call(
@@ -684,11 +665,10 @@
             shape((steps, nvar * pairs, rows, columns), bf16),
             shape((far_base(steps, nvar, levels)[1], rows, columns), bf16),
         ],
-        in_specs=[VMEM] * windows + [ANY],
+        in_specs=[VMEM, ANY],
         out_specs=[VMEM] * 3,
-        scratch_shapes=[pltpu.VMEM((windows, block.shape[0] - 1, rows, LANES), bf16)],
         compiler_params=params(),
-    )(*blocks_here, mix)
+    )(blocks, mix)
     traj_near, traj_far = swapped(traj_near, "space", 0), swapped(traj_far, "space", 1)
 
     first = pl.pallas_call(

time: 47.4 us -> 52.8 us (1.11)
  waiting for transfers between devices: 11.2 us -> 16.4 us
  Pallas kernels: 10.2 us -> 11 us
  starting transfers between devices: 22.4 us -> 21.6 us
    all_to_all x0 -> x1, waiting for transfers between devices: none -> 11.3 us  [body(): lax.all_to_all(blocks, 'window', 0, 0, tiled=True)]
    ppermute x11 -> x8, starting transfers between devices: 20.9 us -> 13.8 us  [moved(): return lax.ppermute(block, axis, route)]
    all_to_all x0 -> x1, starting transfers between devices: none -> 6.32 us  [body(): lax.all_to_all(blocks, 'window', 0, 0, tiled=True)]
    ppermute x11 -> x8, waiting for transfers between devices: 11.2 us -> 5.09 us  [moved(): return lax.ppermute(block, axis, route)]
    pallas_call x4 -> x1, Pallas kernels: 0.45 us -> 1.29 us  [body(): pl.pallas_call(lambda *refs: pack_kernel(steps, nvar, levels, part, *refs...]
    unnamed x18 -> x16, local copies, waits for them, and re-layouts: 1.12 us -> 1.12 us
  transfers between devices with their start and end apart: 15 -> 13, of which waited for: 4 -> 5; matrix products, arithmetic and copies ran while one was open for 0% -> 0% of each run, Pallas kernels for 19% -> 17%
where the time goes in v11:
time: 52.8 us; the launch traced here: 52.4 us
  starting transfers between devices  21.6 us (41%)
  waiting for transfers between devices  16.4 us (31%)
  Pallas kernels  11 us (21%)
  local copies, waits for them, and re-layouts  1.87 us (4%)
  between operations  1.51 us (3%)
    ppermute x8, starting transfers between devices, moved(): return lax.ppermute(block, axis, route)  13.8 us
    all_to_all x1, waiting for transfers between devices, body(): lax.all_to_all(blocks, 'window', 0, 0, tiled=True)  11.3 us
    all_to_all x1, starting transfers between devices, body(): lax.all_to_all(blocks, 'window', 0, 0, tiled=True)  6.32 us
    ppermute x8, waiting for transfers between devices, moved(): return lax.ppermute(block, axis, route)  5.09 us
    pallas_call x1, Pallas kernels, body(): pl.pallas_call(lambda *refs: tangent_kernel(spaces, steps, nvar, levels,...  3.6 us
    pallas_call x2, Pallas kernels, body(): pl.pallas_call(lambda *refs, i=i: adjoint_kernel(i, windows, spaces, step...  2.89 us
    ppermute x4, starting transfers between devices, swapped(): return lax.ppermute(block, axis, swaps(axis, first))  1.49 us
    pallas_call x1, Pallas kernels, body(): pl.pallas_call(lambda *refs: pack_kernel(steps, nvar, levels, part, *refs...  1.29 us
  transfers between devices with their start and end apart: 13, of which 5 were waited for; matrix products, arithmetic and copies ran while one was open for 0% of the time, Pallas kernels for 17%

profile of v11, /device:TPU:0, one launch (start us, length us, event | category | flops | bytes accessed | tf_op | source)
XLA Modules:
  0.0 52.4 jit_solution(6045795812233950861)
XLA Ops:
  0.7 0.8 %pad.4.refs_0_ = f32[8,128]{1,0:T(8,128)S(1)} pad(f32[4,5]{1,0:T(4,128)} %bitcast.3, f32[]{:T(128)} %constant.2.clone.1), padding=0_4x0_123 | pad | bytes 4180 | tf_op jit(solution)/shard_map/jit(_pad)/pad | solution.py:613
  1.4 1.1 %copy-done.4 = bf16[4,4,5,4,8,96]{5,4,3,2,1,0:T(8,128)(2,1)S(1)} copy-done((bf16[4,4,5,4,8,96]{5,4,3,2,1,0:T(8,128)(2,1)S(1)}, bf16[4,4,5,4,8,96]{5,4,3,2,1,0:T(8,128)(2,1)}, u32[]{:S(2)}) %copy-start.4) | copy-done | bytes 491544
  2.5 1.3 %shard_map.122.refs_3_ = bf16[4,61,8,128]{3,2,1,0:T(8,128)(2,1)} custom-call(f32[8,128]{1,0:T(8,128)S(1)} %pad.4.refs_0_, bf16[4,4,5,4,8,96]{5,4,3,2,1,0:T(8,128)(2,1)S(1)} %copy-done.4), custom_call_target="tpu_custom_call" | custom-call | tf_op jit(solution)/shard_map/pallas_call | solution.py:615
  3.8 6.3 %all-to-all-start = ((bf16[4,61,8,128]{3,2,1,0:T(8,128)(2,1)}), bf16[4,61,8,128]{3,2,1,0:T(8,128)(2,1)S(1)}, u32[]{:S(2)}, u32[]{:S(2)}) async-start(bf16[4,61,8,128]{3,2,1,0:T(8,128)(2,1)} %shard_map.122.refs_3_), calls=%async_computation | async-start | bytes 999424 | tf_op jit(solution)/shard_map/all_to_all | solution.py:622
  10.1 0.5 shard_map.123
  10.6 0.1 collective-permute-start
  10.7 0.7 %collective-permute-start.1 = (s16[2,21,16,128]{3,2,1,0:T(8,128)(2,1)S(1)}, s16[2,21,16,128]{3,2,1,0:T(8,128)(2,1)S(1)}, u32[]{:S(2)}, u32[]{:S(2)}) collective-permute-start(s16[2,21,16,128]{3,2,1,0:T(8,128)(2,1)S(1)} %get-tuple-element.37), channel_id=1, source_target_pairs={{1,2},{2,1},{5,6},{6,5},{9,10},{10,9},{13,14},{14,13},{17,18},{18,... | collective-permute-start | bytes 516104 | tf_op jit(solution)/shard_map/ppermute | solution.py:584
  12.0 0.7 %shard_map.121 = (f32[4,4,3,8,128]{4,3,2,1,0:T(8,128)S(1)}, f32[4,4,8,128]{3,2,1,0:T(8,128)S(1)}, f32[5,5,8,128]{3,2,1,0:T(8,128)S(1)}) custom-call(s32[1]{0:T(128)S(6)} %copy.13.refs_0_, f32[1,4,4]{2,1,0:T(4,128)S(1)} %copy-done.7, f32[5,5]{1,0:T(8,128)S(1)} %copy-done.6, f32[1,4,4,8,384]{4,3,2,1,0:T(8,128)S(1)} %copy-done.1, f32[1,4,4,8,384]{4,3,2,1,0:T(8,128)S(1)} %copy-done.5), custom_call_target="tpu_custom_call" | custom-call | tf_op jit(solution)/shard_map/pallas_call | solution.py:649
  12.7 11.3 %all-to-all-done.refs_0_ = bf16[4,61,8,128]{3,2,1,0:T(8,128)(2,1)S(1)} async-done(((bf16[4,61,8,128]{3,2,1,0:T(8,128)(2,1)}), bf16[4,61,8,128]{3,2,1,0:T(8,128)(2,1)S(1)}, u32[]{:S(2)}, u32[]{:S(2)}) %all-to-all-start) | async-done | bytes 499744 | tf_op jit(solution)/shard_map/all_to_all | solution.py:622
  24.1 0.4 shard_map.125
  24.5 0.1 collective-permute-start.2
  24.5 0.7 %collective-permute-start.3 = (bf16[31,8,384]{2,1,0:T(8,128)(2,1)S(1)}, bf16[31,8,384]{2,1,0:T(8,128)(2,1)S(1)}, u32[]{:S(2)}, u32[]{:S(2)}) collective-permute-start(bf16[31,8,384]{2,1,0:T(8,128)(2,1)S(1)} %get-tuple-element.43), channel_id=1, source_target_pairs={{1,2},{2,1},{5,6},{6,5},{9,10},{10,9},{13,14},{14,13},{17,18},{18,... | collective-permute-start | bytes 571400 | tf_op jit(solution)/shard_map/ppermute | solution.py:584
  25.2 0.3 shard_map.124
  25.5 1.4 %collective-permute-start.4 = (s16[2,16,16,128]{3,2,1,0:T(8,128)(2,1)S(1)}, s16[2,16,16,128]{3,2,1,0:T(8,128)(2,1)S(1)}, u32[]{:S(2)}, u32[]{:S(2)}) collective-permute-start(s16[2,16,16,128]{3,2,1,0:T(8,128)(2,1)S(1)} %get-tuple-element.45), channel_id=1, source_target_pairs={{4,0},{8,4},{12,8},{5,1},{9,5},{13,9},{6,2},{10,6},{14,10},{7,3},{... | collective-permute-start | bytes 393224 | tf_op jit(solution)/shard_map/ppermute | solution.py:573
  27.0 1.3 %collective-permute-start.8 = (s16[2,16,16,128]{3,2,1,0:T(8,128)(2,1)S(1)}, s16[2,16,16,128]{3,2,1,0:T(8,128)(2,1)S(1)}, u32[]{:S(2)}, u32[]{:S(2)}) collective-permute-start(s16[2,16,16,128]{3,2,1,0:T(8,128)(2,1)S(1)} %get-tuple-element.52), channel_id=1, source_target_pairs={{4,0},{8,4},{12,8},{5,1},{9,5},{13,9},{6,2},{10,6},{14,10},{7,3},{... | collective-permute-start | bytes 393224 | tf_op jit(solution)/shard_map/ppermute | solution.py:573
  28.3 0.1 shard_map.126.refs_6_
  28.4 3.6 %shard_map.127 = (f32[1,4,4,8,384]{4,3,2,1,0:T(8,128)}, f32[4,5,3,8,128]{4,3,2,1,0:T(8,128)S(1)}, f32[4,4,5,3,16,128]{5,4,3,2,1,0:T(8,128)S(1)}) custom-call(f32[5,5,8,128]{3,2,1,0:T(8,128)S(1)} %get-tuple-element.34.refs_1_.refs_0_, f32[4,4,8,128]{3,2,1,0:T(8,128)S(1)} %get-tuple-element.39.refs_1_, f32[4,4,3,8,128]{4,3,2,1,0:T(8,128)S(1)} %get-tuple-element.40.refs_2_, ...), custom_call_target="tpu_custom_call" | custom-call | tf_op jit(solution)/shard_map/pallas_call | solution.py:681
  32.0 0.5 collective-permute-done.4.refs_4_
  32.5 0.1 shard_map.128
  32.7 1.4 %shard_map.129 = (f32[5,2,8,384]{3,2,1,0:T(8,128)S(1)}, f32[5,2,8,384]{3,2,1,0:T(8,128)S(1)}, s16[16,16,128]{2,1,0:T(8,128)(2,1)S(1)}, s16[16,16,128]{2,1,0:T(8,128)(2,1)S(1)}, s16[16,16,128]{2,1,0:T(8,128)(2,1)S(1)}) custom-call(f32[5,5,8,128]{3,2,1,0:T(8,128)S(1)} %get-tuple-element.34.refs_1_.refs_0_, ...), custom_call_target="tpu_custom_call" | custom-call | tf_op jit(solution)/shard_map/pallas_call | solution.py:706
  34.1 2.8 %collective-permute-start.5 = (s16[16,16,128]{2,1,0:T(8,128)(2,1)S(1)}, s16[16,16,128]{2,1,0:T(8,128)(2,1)S(1)}, u32[]{:S(2)}, u32[]{:S(2)}) collective-permute-start(s16[16,16,128]{2,1,0:T(8,128)(2,1)S(1)} %get-tuple-element.49), channel_id=1, source_target_pairs={{0,4},{4,8},{8,12},{12,0},{1,5},{5,9},{9,13},{13,1},{2,6},{6,10},{... | collective-permute-start | bytes 196616 | tf_op jit(solution)/shard_map/ppermute | solution.py:573
  36.9 1.5 %collective-permute-start.6 = (s16[16,16,128]{2,1,0:T(8,128)(2,1)S(1)}, s16[16,16,128]{2,1,0:T(8,128)(2,1)S(1)}, u32[]{:S(2)}, u32[]{:S(2)}) collective-permute-start(s16[16,16,128]{2,1,0:T(8,128)(2,1)S(1)} %get-tuple-element.50), channel_id=1, source_target_pairs={{0,8},{4,12},{8,0},{12,4},{1,9},{5,13},{9,1},{13,5},{2,10},{6,14},... | collective-permute-start | bytes 196616 | tf_op jit(solution)/shard_map/ppermute | solution.py:573
  38.5 2.8 %collective-permute-start.7 = (s16[16,16,128]{2,1,0:T(8,128)(2,1)S(1)}, s16[16,16,128]{2,1,0:T(8,128)(2,1)S(1)}, u32[]{:S(2)}, u32[]{:S(2)}) collective-permute-start(s16[16,16,128]{2,1,0:T(8,128)(2,1)S(1)} %get-tuple-element.51), channel_id=1, source_target_pairs={{0,12},{4,0},{8,4},{12,8},{1,13},{5,1},{9,5},{13,9},{2,14},{6,2},{... | collective-permute-start | bytes 196616 | tf_op jit(solution)/shard_map/ppermute | solution.py:573
  41.3 0.1 shard_map.130
  41.4 1.4 %shard_map.131 = (f32[5,2,8,384]{3,2,1,0:T(8,128)S(1)}, f32[5,2,8,384]{3,2,1,0:T(8,128)S(1)}, s16[16,16,128]{2,1,0:T(8,128)(2,1)S(1)}, s16[16,16,128]{2,1,0:T(8,128)(2,1)S(1)}, s16[16,16,128]{2,1,0:T(8,128)(2,1)S(1)}) custom-call(f32[5,5,8,128]{3,2,1,0:T(8,128)S(1)} %get-tuple-element.34.refs_1_.refs_0_, ...), custom_call_target="tpu_custom_call" | custom-call | tf_op jit(solution)/shard_map/pallas_call | solution.py:706
  42.9 0.1 collective-permute-start.9
  43.0 0.6 %collective-permute-start.10 = (s16[16,16,128]{2,1,0:T(8,128)(2,1)S(1)}, s16[16,16,128]{2,1,0:T(8,128)(2,1)S(1)}, u32[]{:S(2)}, u32[]{:S(2)}) collective-permute-start(s16[16,16,128]{2,1,0:T(8,128)(2,1)S(1)} %get-tuple-element.57), channel_id=1, source_target_pairs={{0,8},{4,12},{8,0},{12,4},{1,9},{5,13},{9,1},{13,5},{2,10},{6,14},... | collective-permute-start | bytes 196616 | tf_op jit(solution)/shard_map/ppermute | solution.py:573
  43.5 3.3 %collective-permute-start.11 = (s16[16,16,128]{2,1,0:T(8,128)(2,1)S(1)}, s16[16,16,128]{2,1,0:T(8,128)(2,1)S(1)}, u32[]{:S(2)}, u32[]{:S(2)}) collective-permute-start(s16[16,16,128]{2,1,0:T(8,128)(2,1)S(1)} %get-tuple-element.58), channel_id=1, source_target_pairs={{0,12},{4,0},{8,4},{12,8},{1,13},{5,1},{9,5},{13,9},{2,14},{6,2},{... | collective-permute-start | bytes 196616 | tf_op jit(solution)/shard_map/ppermute | solution.py:573
  46.8 2.7 %collective-permute-done.9.refs_3_ = s16[16,16,128]{2,1,0:T(8,128)(2,1)S(1)} collective-permute-done((s16[16,16,128]{2,1,0:T(8,128)(2,1)S(1)}, s16[16,16,128]{2,1,0:T(8,128)(2,1)S(1)}, u32[]{:S(2)}, u32[]{:S(2)}) %collective-permute-start.9) | collective-permute-done | bytes 65568 | tf_op jit(solution)/shard_map/ppermute | solution.py:573
  49.5 1.6 %collective-permute-done.10.refs_4_ = s16[16,16,128]{2,1,0:T(8,128)(2,1)S(1)} collective-permute-done((s16[16,16,128]{2,1,0:T(8,128)(2,1)S(1)}, s16[16,16,128]{2,1,0:T(8,128)(2,1)S(1)}, u32[]{:S(2)}, u32[]{:S(2)}) %collective-permute-start.10) | collective-permute-done | bytes 65568 | tf_op jit(solution)/shard_map/ppermute | solution.py:573
  51.1 0.3 collective-permute-done.11.refs_5_
  51.4 1.0 %shard_map.132 = (f32[1,5,4,8,384]{4,3,2,1,0:T(8,128)}, f32[1,5,4,8,384]{4,3,2,1,0:T(8,128)}) custom-call(s16[16,16,128]{2,1,0:T(8,128)(2,1)S(1)} %collective-permute-done.5.refs_0_, s16[16,16,128]{2,1,0:T(8,128)(2,1)S(1)} %collective-permute-done.6.refs_1_, s16[16,16,128]{2,1,0:T(8,128)(2,1)S(1)} %collective-permute-done.7.refs_2_, ...), custom_call_target="tpu_custom_call" | custom-call | tf_op jit(solution)/shard_map/pallas_call | solution.py:726
  (23 shorter events, 0.1 us)
Async XLA Ops:
  0.6 9.5 %copy-start.1 = (f32[1,4,4,8,384]{4,3,2,1,0:T(8,128)S(1)}, f32[1,4,4,8,384]{4,3,2,1,0:T(8,128)}, u32[]{:S(2)}) copy-start(f32[1,4,4,8,384]{4,3,2,1,0:T(8,128)} %refs_3_.5) | copy-start | bytes 589828
  0.6 9.5 %copy-start = (f32[1,5,4,8,384]{4,3,2,1,0:T(8,128)S(1)}, f32[1,5,4,8,384]{4,3,2,1,0:T(8,128)}, u32[]{:S(2)}) copy-start(f32[1,5,4,8,384]{4,3,2,1,0:T(8,128)} %refs_6_.3) | copy-start | bytes 737284
  0.7 9.5 %copy-start.2 = (f32[1,5,4,8,384]{4,3,2,1,0:T(8,128)S(1)}, f32[1,5,4,8,384]{4,3,2,1,0:T(8,128)}, u32[]{:S(2)}) copy-start(f32[1,5,4,8,384]{4,3,2,1,0:T(8,128)} %refs_8_.3) | copy-start | bytes 737284
  1.4 1.1 %copy-start.4 = (bf16[4,4,5,4,8,96]{5,4,3,2,1,0:T(8,128)(2,1)S(1)}, bf16[4,4,5,4,8,96]{5,4,3,2,1,0:T(8,128)(2,1)}, u32[]{:S(2)}) copy-start(bf16[4,4,5,4,8,96]{5,4,3,2,1,0:T(8,128)(2,1)} %refs_1_.4) | copy-start | bytes 1474564
  2.5 9.5 %copy-start.5 = (f32[1,4,4,8,384]{4,3,2,1,0:T(8,128)S(1)}, f32[1,4,4,8,384]{4,3,2,1,0:T(8,128)}, u32[]{:S(2)}) copy-start(f32[1,4,4,8,384]{4,3,2,1,0:T(8,128)} %refs_4_.1) | copy-start | bytes 589828
  2.5 9.5 %copy-start.6 = (f32[5,5]{1,0:T(8,128)S(1)}, f32[5,5]{1,0:T(8,128)}, u32[]{:S(2)}) copy-start(f32[5,5]{1,0:T(8,128)} %refs_2_.3) | copy-start | bytes 304
  2.5 9.5 %copy-start.7 = (f32[1,4,4]{2,1,0:T(4,128)S(1)}, f32[1,4,4]{2,1,0:T(4,128)}, u32[]{:S(2)}) copy-start(f32[1,4,4]{2,1,0:T(4,128)} %refs_1_.3) | copy-start | bytes 196
  3.8 20.3 %all-to-all-start = ((bf16[4,61,8,128]{3,2,1,0:T(8,128)(2,1)}), bf16[4,61,8,128]{3,2,1,0:T(8,128)(2,1)S(1)}, u32[]{:S(2)}, u32[]{:S(2)}) async-start(bf16[4,61,8,128]{3,2,1,0:T(8,128)(2,1)} %shard_map.122.refs_3_), calls=%async_computation | async-start | bytes 999424 | tf_op jit(solution)/shard_map/all_to_all | solution.py:622
  10.6 14.6 %collective-permute-start = (s16[2,21,16,128]{3,2,1,0:T(8,128)(2,1)S(1)}, s16[2,21,16,128]{3,2,1,0:T(8,128)(2,1)S(1)}, u32[]{:S(2)}, u32[]{:S(2)}) collective-permute-start(s16[2,21,16,128]{3,2,1,0:T(8,128)(2,1)S(1)} %get-tuple-element.36), channel_id=1, source_target_pairs={{0,1},{1,0},{2,3},{3,2},{4,5},{5,4},{6,7},{7,6},{8,9},{9,8},{10,11... | collective-permute-start | bytes 516104 | tf_op jit(solution)/shard_map/ppermute | solution.py:584
  10.7 14.6 %collective-permute-start.1 = (s16[2,21,16,128]{3,2,1,0:T(8,128)(2,1)S(1)}, s16[2,21,16,128]{3,2,1,0:T(8,128)(2,1)S(1)}, u32[]{:S(2)}, u32[]{:S(2)}) collective-permute-start(s16[2,21,16,128]{3,2,1,0:T(8,128)(2,1)S(1)} %get-tuple-element.37), channel_id=1, source_target_pairs={{1,2},{2,1},{5,6},{6,5},{9,10},{10,9},{13,14},{14,13},{17,18},{18,... | collective-permute-start | bytes 516104 | tf_op jit(solution)/shard_map/ppermute | solution.py:584
  24.5 3.9 %collective-permute-start.2 = (bf16[4,10,8,384]{3,2,1,0:T(8,128)(2,1)S(1)}, bf16[4,10,8,384]{3,2,1,0:T(8,128)(2,1)S(1)}, u32[]{:S(2)}, u32[]{:S(2)}) collective-permute-start(bf16[4,10,8,384]{3,2,1,0:T(8,128)(2,1)S(1)} %get-tuple-element.42), channel_id=1, source_target_pairs={{0,1},{1,0},{2,3},{3,2},{4,5},{5,4},{6,7},{7,6},{8,9},{9,8},{10,11... | collective-permute-start | bytes 737288 | tf_op jit(solution)/shard_map/ppermute | solution.py:584
  24.5 3.9 %collective-permute-start.3 = (bf16[31,8,384]{2,1,0:T(8,128)(2,1)S(1)}, bf16[31,8,384]{2,1,0:T(8,128)(2,1)S(1)}, u32[]{:S(2)}, u32[]{:S(2)}) collective-permute-start(bf16[31,8,384]{2,1,0:T(8,128)(2,1)S(1)} %get-tuple-element.43), channel_id=1, source_target_pairs={{1,2},{2,1},{5,6},{6,5},{9,10},{10,9},{13,14},{14,13},{17,18},{18,... | collective-permute-start | bytes 571400 | tf_op jit(solution)/shard_map/ppermute | solution.py:584
  25.5 7.1 %copy-start.3 = (f32[1,5,4,8,384]{4,3,2,1,0:T(8,128)S(1)}, f32[1,5,4,8,384]{4,3,2,1,0:T(8,128)}, u32[]{:S(2)}) copy-start(f32[1,5,4,8,384]{4,3,2,1,0:T(8,128)} %refs_7_.3) | copy-start | bytes 737284
  25.5 7.0 %collective-permute-start.4 = (s16[2,16,16,128]{3,2,1,0:T(8,128)(2,1)S(1)}, s16[2,16,16,128]{3,2,1,0:T(8,128)(2,1)S(1)}, u32[]{:S(2)}, u32[]{:S(2)}) collective-permute-start(s16[2,16,16,128]{3,2,1,0:T(8,128)(2,1)S(1)} %get-tuple-element.45), channel_id=1, source_target_pairs={{4,0},{8,4},{12,8},{5,1},{9,5},{13,9},{6,2},{10,6},{14,10},{7,3},{... | collective-permute-start | bytes 393224 | tf_op jit(solution)/shard_map/ppermute | solution.py:573
  27.0 14.4 %collective-permute-start.8 = (s16[2,16,16,128]{3,2,1,0:T(8,128)(2,1)S(1)}, s16[2,16,16,128]{3,2,1,0:T(8,128)(2,1)S(1)}, u32[]{:S(2)}, u32[]{:S(2)}) collective-permute-start(s16[2,16,16,128]{3,2,1,0:T(8,128)(2,1)S(1)} %get-tuple-element.52), channel_id=1, source_target_pairs={{4,0},{8,4},{12,8},{5,1},{9,5},{13,9},{6,2},{10,6},{14,10},{7,3},{... | collective-permute-start | bytes 393224 | tf_op jit(solution)/shard_map/ppermute | solution.py:573
  34.1 9.4 %collective-permute-start.5 = (s16[16,16,128]{2,1,0:T(8,128)(2,1)S(1)}, s16[16,16,128]{2,1,0:T(8,128)(2,1)S(1)}, u32[]{:S(2)}, u32[]{:S(2)}) collective-permute-start(s16[16,16,128]{2,1,0:T(8,128)(2,1)S(1)} %get-tuple-element.49), channel_id=1, source_target_pairs={{0,4},{4,8},{8,12},{12,0},{1,5},{5,9},{9,13},{13,1},{2,6},{6,10},{... | collective-permute-start | bytes 196616 | tf_op jit(solution)/shard_map/ppermute | solution.py:573
  36.9 9.8 %collective-permute-start.6 = (s16[16,16,128]{2,1,0:T(8,128)(2,1)S(1)}, s16[16,16,128]{2,1,0:T(8,128)(2,1)S(1)}, u32[]{:S(2)}, u32[]{:S(2)}) collective-permute-start(s16[16,16,128]{2,1,0:T(8,128)(2,1)S(1)} %get-tuple-element.50), channel_id=1, source_target_pairs={{0,8},{4,12},{8,0},{12,4},{1,9},{5,13},{9,1},{13,5},{2,10},{6,14},... | collective-permute-start | bytes 196616 | tf_op jit(solution)/shard_map/ppermute | solution.py:573
  38.5 8.3 %collective-permute-start.7 = (s16[16,16,128]{2,1,0:T(8,128)(2,1)S(1)}, s16[16,16,128]{2,1,0:T(8,128)(2,1)S(1)}, u32[]{:S(2)}, u32[]{:S(2)}) collective-permute-start(s16[16,16,128]{2,1,0:T(8,128)(2,1)S(1)} %get-tuple-element.51), channel_id=1, source_target_pairs={{0,12},{4,0},{8,4},{12,8},{1,13},{5,1},{9,5},{13,9},{2,14},{6,2},{... | collective-permute-start | bytes 196616 | tf_op jit(solution)/shard_map/ppermute | solution.py:573
  42.9 6.6 %collective-permute-start.9 = (s16[16,16,128]{2,1,0:T(8,128)(2,1)S(1)}, s16[16,16,128]{2,1,0:T(8,128)(2,1)S(1)}, u32[]{:S(2)}, u32[]{:S(2)}) collective-permute-start(s16[16,16,128]{2,1,0:T(8,128)(2,1)S(1)} %get-tuple-element.56), channel_id=1, source_target_pairs={{0,4},{4,8},{8,12},{12,0},{1,5},{5,9},{9,13},{13,1},{2,6},{6,10},{... | collective-permute-start | bytes 196616 | tf_op jit(solution)/shard_map/ppermute | solution.py:573
  43.0 8.1 %collective-permute-start.10 = (s16[16,16,128]{2,1,0:T(8,128)(2,1)S(1)}, s16[16,16,128]{2,1,0:T(8,128)(2,1)S(1)}, u32[]{:S(2)}, u32[]{:S(2)}) collective-permute-start(s16[16,16,128]{2,1,0:T(8,128)(2,1)S(1)} %get-tuple-element.57), channel_id=1, source_target_pairs={{0,8},{4,12},{8,0},{12,4},{1,9},{5,13},{9,1},{13,5},{2,10},{6,14},... | collective-permute-start | bytes 196616 | tf_op jit(solution)/shard_map/ppermute | solution.py:573
  43.5 7.8 %collective-permute-start.11 = (s16[16,16,128]{2,1,0:T(8,128)(2,1)S(1)}, s16[16,16,128]{2,1,0:T(8,128)(2,1)S(1)}, u32[]{:S(2)}, u32[]{:S(2)}) collective-permute-start(s16[16,16,128]{2,1,0:T(8,128)(2,1)S(1)} %get-tuple-element.58), channel_id=1, source_target_pairs={{0,12},{4,0},{8,4},{12,8},{1,13},{5,1},{9,5},{13,9},{2,14},{6,2},{... | collective-permute-start | bytes 196616 | tf_op jit(solution)/shard_map/ppermute | solution.py:573

commit v12 on v10

--- a/solution.py
+++ b/solution.py
@@ -104,7 +104,11 @@
     return value.astype(jnp.int32).astype(jnp.float32)
 
 
-def pack_kernel(distances, windows, steps, nvar, levels, part, var_ref, traj_ref, *outs):
+def distances(windows):
+    return sorted(range(1, windows), key=lambda d: -d * (windows - d))
+
+
+def pack_kernel(ways, windows, steps, nvar, levels, part, var_ref, traj_ref, *outs):
     me = lax.axis_index("window")
     lane = lane_index()
     variance = var_ref[...]
@@ -114,7 +118,7 @@
     split = high + pltpu.roll(middle, HALF, 0) + pltpu.roll(low, LANES // 2, 1)
     split = split.astype(jnp.bfloat16)
 
-    for n, d in enumerate(distances):
+    for n, d in enumerate(ways):
         outs[n][outs[n].shape[0] - 1] = split
         target = lax.rem(me + d, windows)
 
@@ -129,7 +133,7 @@
                     outs[n][(v * levels + lev) * len(placed) + t] = value.astype(jnp.bfloat16)
             return carry
 
-        lax.fori_loop(0, nvar, variable, 0, unroll=len(distances) == 1)
+        lax.fori_loop(0, nvar, variable, 0, unroll=len(ways) == 1)
 
 
 def even_place():
@@ -538,8 +542,8 @@
         first, second = coded[0][kind], coded[1][kind]
         for n, (a, b) in enumerate(zip(first[0] + [first[1]], second[0] + [second[1]])):
             q_ref[kind, n] = shorts(jnp.concatenate([a, b], 0))
-    for d in range(1, windows):
-        payload_refs[d - 1][...] = q_ref[jnp.where(me + d >= windows, 0, 1)]
+    for ref, d in zip(payload_refs, distances(windows)):
+        ref[...] = q_ref[jnp.where(me + d >= windows, 0, 1)]
 
 
 def final_kernel(windows, nvar, levels, tiles, *refs):
@@ -553,18 +557,18 @@
     for i in range(pairs):
         tails = [None] * (nvar * tiles)
         heads = [None] * (nvar * tiles)
-        for d in range(1, windows):
-            piece = pieces[i * (windows - 1) + d - 1]
+        for n, d in enumerate(distances(windows)):
+            piece = pieces[i * (windows - 1) + n]
             later = d > me
             scales = jnp.exp2(floats(piece[nvar * tiles])) * (1.0 / CODE_MAX)
             for v in range(nvar):
                 scale = scales[:, v : v + 1]
                 for t in range(tiles):
-                    n = v * tiles + t
-                    value = floats(piece[n]) * scale
+                    k = v * tiles + t
+                    value = floats(piece[k]) * scale
                     tail, head = jnp.where(later, value, 0.0), jnp.where(later, 0.0, value)
-                    tails[n] = tail if d == 1 else tails[n] + tail
-                    heads[n] = head if d == 1 else heads[n] + head
+                    tails[k] = tails[k] + tail if n else tail
+                    heads[k] = heads[k] + head if n else head
         for v in range(nvar):
             for odd in range(2):
                 lev = 2 * i + odd
@@ -623,16 +627,16 @@
     block = shape((nvar * levels * wide // LANES + 1, rows, LANES), bf16)
     variances = jnp.pad(error_var[0].T, ((0, SUB - levels), (0, LANES - nvar)))
 
-    def packed(distances):
+    def packed(ways):
         return pl.pallas_call(
-            lambda *refs: pack_kernel(distances, windows, steps, nvar, levels, part, *refs),
-            out_shape=[block] * len(distances),
+            lambda *refs: pack_kernel(ways, windows, steps, nvar, levels, part, *refs),
+            out_shape=[block] * len(ways),
             in_specs=[VMEM, VMEM],
-            out_specs=[VMEM] * len(distances),
+            out_specs=[VMEM] * len(ways),
             compiler_params=params(),
         )(variances, trajectory)
 
-    order = sorted(range(1, windows), key=lambda d: -d * (windows - d))
+    order = distances(windows)
     groups = [[d] for d in order] if windows <= 4 else [order]
     blocks = {}
     for group in groups:
@@ -740,8 +744,9 @@
         before = base_dual
         base_duals.append(base_dual)
         base_incs.append(base_inc)
-        moving = {d: moved(payloads[d - 1], "window", d, around=True) for d in order}
-        sent += [moving[d] for d in range(1, windows)]
+        sent += [
+            moved(piece, "window", d, around=True) for piece, d in zip(payloads, order)
+        ]
 
     new_dual_model, new_increment = pl.pallas_call(
         lambda *refs: final_kernel(windows, nvar, levels, tiles, *refs),

time: 47.4 us -> 47.6 us (level)
  starting transfers between devices: 22.4 us -> 23.4 us
  waiting for transfers between devices: 11.2 us -> 10.4 us
    ppermute x11, starting transfers between devices: 20.9 us -> 21.9 us  [moved(): return lax.ppermute(block, axis, route)]
    ppermute x11, waiting for transfers between devices: 11.2 us -> 10.4 us  [moved(): return lax.ppermute(block, axis, route)]
where the time goes in v12:
time: 47.6 us; the launch traced here: 47.3 us
  starting transfers between devices  23.4 us (49%)
  waiting for transfers between devices  10.4 us (22%)
  Pallas kernels  10.2 us (21%)
  local copies, waits for them, and re-layouts  1.82 us (4%)
  between operations  1.56 us (3%)
    ppermute x11, starting transfers between devices, moved(): return lax.ppermute(block, axis, route)  21.9 us
    ppermute x11, waiting for transfers between devices, moved(): return lax.ppermute(block, axis, route)  10.4 us
    pallas_call x1, Pallas kernels, body(): pl.pallas_call(lambda *refs: tangent_kernel(spaces, steps, nvar, levels,...  3.58 us
    pallas_call x2, Pallas kernels, body(): pl.pallas_call(lambda *refs, i=i: adjoint_kernel(i, windows, spaces, step...  2.89 us
    ppermute x4, starting transfers between devices, swapped(): return lax.ppermute(block, axis, swaps(axis, first))  1.49 us
    unnamed x18, local copies, waits for them, and re-layouts  1.12 us
    pallas_call x1, Pallas kernels, body(): pl.pallas_call(lambda *refs: final_kernel(windows, nvar, levels, tiles, *...  1.02 us
  transfers between devices with their start and end apart: 15, of which 4 were waited for; matrix products, arithmetic and copies ran while one was open for 0% of the time, Pallas kernels for 19%

profile of v12, /device:TPU:0, one launch (start us, length us, event | category | flops | bytes accessed | tf_op | source)
XLA Modules:
  0.0 47.3 jit_solution(13009031220239507174)
XLA Ops:
  0.7 0.7 %pad.4.refs_0_ = f32[8,128]{1,0:T(8,128)S(1)} pad(f32[4,5]{1,0:T(4,128)} %bitcast.3, f32[]{:T(128)} %constant.2.clone.1), padding=0_4x0_123 | pad | bytes 4180 | tf_op jit(solution)/shard_map/jit(_pad)/pad | solution.py:628
  1.4 1.1 %copy-done = bf16[4,4,5,4,8,96]{5,4,3,2,1,0:T(8,128)(2,1)S(1)} copy-done((bf16[4,4,5,4,8,96]{5,4,3,2,1,0:T(8,128)(2,1)S(1)}, bf16[4,4,5,4,8,96]{5,4,3,2,1,0:T(8,128)(2,1)}, u32[]{:S(2)}) %copy-start) | copy-done | bytes 491544
  2.5 0.1 shard_map.123
  2.6 3.1 %collective-permute-start = (bf16[61,8,128]{2,1,0:T(8,128)(2,1)S(1)}, bf16[61,8,128]{2,1,0:T(8,128)(2,1)S(1)}, u32[]{:S(2)}, u32[]{:S(2)}) collective-permute-start(bf16[61,8,128]{2,1,0:T(8,128)(2,1)S(1)} %shard_map.123), channel_id=1, source_target_pairs={{0,4},{4,8},{8,12},{12,0},{1,5},{5,9},{9,13},{13,1},{2,6},{6,10},{... | collective-permute-start | bytes 374792 | tf_op jit(solution)/shard_map/ppermute | solution.py:588
  5.8 2.7 %collective-permute-start.1 = (bf16[61,8,128]{2,1,0:T(8,128)(2,1)S(1)}, bf16[61,8,128]{2,1,0:T(8,128)(2,1)S(1)}, u32[]{:S(2)}, u32[]{:S(2)}) collective-permute-start(bf16[61,8,128]{2,1,0:T(8,128)(2,1)S(1)} %shard_map.124), channel_id=1, source_target_pairs={{0,8},{4,12},{8,0},{12,4},{1,9},{5,13},{9,1},{13,5},{2,10},{6,14},... | collective-permute-start | bytes 374792 | tf_op jit(solution)/shard_map/ppermute | solution.py:588
  8.4 0.1 shard_map.125
  8.5 1.4 %collective-permute-start.2 = (bf16[61,8,128]{2,1,0:T(8,128)(2,1)S(1)}, bf16[61,8,128]{2,1,0:T(8,128)(2,1)S(1)}, u32[]{:S(2)}, u32[]{:S(2)}) collective-permute-start(bf16[61,8,128]{2,1,0:T(8,128)(2,1)S(1)} %shard_map.125), channel_id=1, source_target_pairs={{0,12},{4,0},{8,4},{12,8},{1,13},{5,1},{9,5},{13,9},{2,14},{6,2},{... | collective-permute-start | bytes 374792 | tf_op jit(solution)/shard_map/ppermute | solution.py:588
  10.0 0.5 shard_map.126
  10.5 0.7 %collective-permute-start.4 = (s16[2,21,16,128]{3,2,1,0:T(8,128)(2,1)S(1)}, s16[2,21,16,128]{3,2,1,0:T(8,128)(2,1)S(1)}, u32[]{:S(2)}, u32[]{:S(2)}) collective-permute-start(s16[2,21,16,128]{3,2,1,0:T(8,128)(2,1)S(1)} %get-tuple-element.37), channel_id=1, source_target_pairs={{1,2},{2,1},{5,6},{6,5},{9,10},{10,9},{13,14},{14,13},{17,18},{18,... | collective-permute-start | bytes 516104 | tf_op jit(solution)/shard_map/ppermute | solution.py:599
  11.2 0.1 shard_map.122.refs_0_
  12.0 0.7 %shard_map.121 = (f32[4,4,3,8,128]{4,3,2,1,0:T(8,128)S(1)}, f32[4,4,8,128]{3,2,1,0:T(8,128)S(1)}, f32[5,5,8,128]{3,2,1,0:T(8,128)S(1)}) custom-call(s32[1]{0:T(128)S(6)} %copy.13.refs_0_, f32[1,4,4]{2,1,0:T(4,128)S(1)} %copy-done.8, f32[5,5]{1,0:T(8,128)S(1)} %copy-done.7, f32[1,4,4,8,384]{4,3,2,1,0:T(8,128)S(1)} %copy-done.3, f32[1,4,4,8,384]{4,3,2,1,0:T(8,128)S(1)} %copy-done.6), custom_call_target="tpu_custom_call" | custom-call | tf_op jit(solution)/shard_map/pallas_call | solution.py:672
  12.7 3.8 %collective-permute-done.1.refs_2_ = bf16[61,8,128]{2,1,0:T(8,128)(2,1)S(1)} collective-permute-done((bf16[61,8,128]{2,1,0:T(8,128)(2,1)S(1)}, bf16[61,8,128]{2,1,0:T(8,128)(2,1)S(1)}, u32[]{:S(2)}, u32[]{:S(2)}) %collective-permute-start.1) | collective-permute-done | bytes 124960 | tf_op jit(solution)/shard_map/ppermute | solution.py:588
  16.5 0.5 shard_map.128
  17.1 0.7 %collective-permute-start.6 = (bf16[31,8,384]{2,1,0:T(8,128)(2,1)S(1)}, bf16[31,8,384]{2,1,0:T(8,128)(2,1)S(1)}, u32[]{:S(2)}, u32[]{:S(2)}) collective-permute-start(bf16[31,8,384]{2,1,0:T(8,128)(2,1)S(1)} %get-tuple-element.43), channel_id=1, source_target_pairs={{1,2},{2,1},{5,6},{6,5},{9,10},{10,9},{13,14},{14,13},{17,18},{18,... | collective-permute-start | bytes 571400 | tf_op jit(solution)/shard_map/ppermute | solution.py:599
  17.8 0.3 shard_map.127
  18.0 1.4 %collective-permute-start.7 = (s16[2,16,16,128]{3,2,1,0:T(8,128)(2,1)S(1)}, s16[2,16,16,128]{3,2,1,0:T(8,128)(2,1)S(1)}, u32[]{:S(2)}, u32[]{:S(2)}) collective-permute-start(s16[2,16,16,128]{3,2,1,0:T(8,128)(2,1)S(1)} %get-tuple-element.45), channel_id=1, source_target_pairs={{4,0},{8,4},{12,8},{5,1},{9,5},{13,9},{6,2},{10,6},{14,10},{7,3},{... | collective-permute-start | bytes 393224 | tf_op jit(solution)/shard_map/ppermute | solution.py:588
  19.5 1.3 %collective-permute-start.11 = (s16[2,16,16,128]{3,2,1,0:T(8,128)(2,1)S(1)}, s16[2,16,16,128]{3,2,1,0:T(8,128)(2,1)S(1)}, u32[]{:S(2)}, u32[]{:S(2)}) collective-permute-start(s16[2,16,16,128]{3,2,1,0:T(8,128)(2,1)S(1)} %get-tuple-element.52), channel_id=1, source_target_pairs={{4,0},{8,4},{12,8},{5,1},{9,5},{13,9},{6,2},{10,6},{14,10},{7,3},{... | collective-permute-start | bytes 393224 | tf_op jit(solution)/shard_map/ppermute | solution.py:588
  20.8 0.1 shard_map.129.refs_6_
  20.9 3.6 %shard_map.130 = (f32[1,4,4,8,384]{4,3,2,1,0:T(8,128)}, f32[4,5,3,8,128]{4,3,2,1,0:T(8,128)S(1)}, f32[4,4,5,3,16,128]{5,4,3,2,1,0:T(8,128)S(1)}) custom-call(f32[5,5,8,128]{3,2,1,0:T(8,128)S(1)} %get-tuple-element.34.refs_4_.refs_0_, f32[4,4,8,128]{3,2,1,0:T(8,128)S(1)} %get-tuple-element.39.refs_1_, f32[4,4,3,8,128]{4,3,2,1,0:T(8,128)S(1)} %get-tuple-element.40.refs_2_, ...), custom_call_target="tpu_custom_call" | custom-call | tf_op jit(solution)/shard_map/pallas_call | solution.py:705
  24.5 1.7 %collective-permute-done.7.refs_4_ = s16[2,16,16,128]{3,2,1,0:T(8,128)(2,1)S(1)} collective-permute-done((s16[2,16,16,128]{3,2,1,0:T(8,128)(2,1)S(1)}, s16[2,16,16,128]{3,2,1,0:T(8,128)(2,1)S(1)}, u32[]{:S(2)}, u32[]{:S(2)}) %collective-permute-start.7) | collective-permute-done | bytes 131104 | tf_op jit(solution)/shard_map/ppermute | solution.py:588
  26.2 0.1 shard_map.131
  26.3 1.4 %shard_map.132 = (f32[5,2,8,384]{3,2,1,0:T(8,128)S(1)}, f32[5,2,8,384]{3,2,1,0:T(8,128)S(1)}, s16[16,16,128]{2,1,0:T(8,128)(2,1)S(1)}, s16[16,16,128]{2,1,0:T(8,128)(2,1)S(1)}, s16[16,16,128]{2,1,0:T(8,128)(2,1)S(1)}) custom-call(f32[5,5,8,128]{3,2,1,0:T(8,128)S(1)} %get-tuple-element.34.refs_4_.refs_0_, ...), custom_call_target="tpu_custom_call" | custom-call | tf_op jit(solution)/shard_map/pallas_call | solution.py:730
  27.7 4.3 %collective-permute-start.8 = (s16[16,16,128]{2,1,0:T(8,128)(2,1)S(1)}, s16[16,16,128]{2,1,0:T(8,128)(2,1)S(1)}, u32[]{:S(2)}, u32[]{:S(2)}) collective-permute-start(s16[16,16,128]{2,1,0:T(8,128)(2,1)S(1)} %get-tuple-element.49), channel_id=1, source_target_pairs={{0,8},{4,12},{8,0},{12,4},{1,9},{5,13},{9,1},{13,5},{2,10},{6,14},... | collective-permute-start | bytes 196616 | tf_op jit(solution)/shard_map/ppermute | solution.py:588
  32.0 2.0 %collective-permute-start.9 = (s16[16,16,128]{2,1,0:T(8,128)(2,1)S(1)}, s16[16,16,128]{2,1,0:T(8,128)(2,1)S(1)}, u32[]{:S(2)}, u32[]{:S(2)}) collective-permute-start(s16[16,16,128]{2,1,0:T(8,128)(2,1)S(1)} %get-tuple-element.50), channel_id=1, source_target_pairs={{0,4},{4,8},{8,12},{12,0},{1,5},{5,9},{9,13},{13,1},{2,6},{6,10},{... | collective-permute-start | bytes 196616 | tf_op jit(solution)/shard_map/ppermute | solution.py:588
  34.0 1.8 %collective-permute-start.10 = (s16[16,16,128]{2,1,0:T(8,128)(2,1)S(1)}, s16[16,16,128]{2,1,0:T(8,128)(2,1)S(1)}, u32[]{:S(2)}, u32[]{:S(2)}) collective-permute-start(s16[16,16,128]{2,1,0:T(8,128)(2,1)S(1)} %get-tuple-element.51), channel_id=1, source_target_pairs={{0,12},{4,0},{8,4},{12,8},{1,13},{5,1},{9,5},{13,9},{2,14},{6,2},{... | collective-permute-start | bytes 196616 | tf_op jit(solution)/shard_map/ppermute | solution.py:588
  35.8 0.1 shard_map.133
  36.0 1.4 %shard_map.134 = (f32[5,2,8,384]{3,2,1,0:T(8,128)S(1)}, f32[5,2,8,384]{3,2,1,0:T(8,128)S(1)}, s16[16,16,128]{2,1,0:T(8,128)(2,1)S(1)}, s16[16,16,128]{2,1,0:T(8,128)(2,1)S(1)}, s16[16,16,128]{2,1,0:T(8,128)(2,1)S(1)}) custom-call(f32[5,5,8,128]{3,2,1,0:T(8,128)S(1)} %get-tuple-element.34.refs_4_.refs_0_, ...), custom_call_target="tpu_custom_call" | custom-call | tf_op jit(solution)/shard_map/pallas_call | solution.py:730
  37.5 0.6 %collective-permute-start.13 = (s16[16,16,128]{2,1,0:T(8,128)(2,1)S(1)}, s16[16,16,128]{2,1,0:T(8,128)(2,1)S(1)}, u32[]{:S(2)}, u32[]{:S(2)}) collective-permute-start(s16[16,16,128]{2,1,0:T(8,128)(2,1)S(1)} %get-tuple-element.57), channel_id=1, source_target_pairs={{0,4},{4,8},{8,12},{12,0},{1,5},{5,9},{9,13},{13,1},{2,6},{6,10},{... | collective-permute-start | bytes 196616 | tf_op jit(solution)/shard_map/ppermute | solution.py:588
  38.1 3.3 %collective-permute-start.14 = (s16[16,16,128]{2,1,0:T(8,128)(2,1)S(1)}, s16[16,16,128]{2,1,0:T(8,128)(2,1)S(1)}, u32[]{:S(2)}, u32[]{:S(2)}) collective-permute-start(s16[16,16,128]{2,1,0:T(8,128)(2,1)S(1)} %get-tuple-element.58), channel_id=1, source_target_pairs={{0,12},{4,0},{8,4},{12,8},{1,13},{5,1},{9,5},{13,9},{2,14},{6,2},{... | collective-permute-start | bytes 196616 | tf_op jit(solution)/shard_map/ppermute | solution.py:588
  41.4 4.4 %collective-permute-done.12.refs_3_ = s16[16,16,128]{2,1,0:T(8,128)(2,1)S(1)} collective-permute-done((s16[16,16,128]{2,1,0:T(8,128)(2,1)S(1)}, s16[16,16,128]{2,1,0:T(8,128)(2,1)S(1)}, u32[]{:S(2)}, u32[]{:S(2)}) %collective-permute-start.12) | collective-permute-done | bytes 65568 | tf_op jit(solution)/shard_map/ppermute | solution.py:588
  45.8 0.5 %collective-permute-done.14.refs_5_ = s16[16,16,128]{2,1,0:T(8,128)(2,1)S(1)} collective-permute-done((s16[16,16,128]{2,1,0:T(8,128)(2,1)S(1)}, s16[16,16,128]{2,1,0:T(8,128)(2,1)S(1)}, u32[]{:S(2)}, u32[]{:S(2)}) %collective-permute-start.14) | collective-permute-done | bytes 65568 | tf_op jit(solution)/shard_map/ppermute | solution.py:588
  46.3 1.0 %shard_map.135 = (f32[1,5,4,8,384]{4,3,2,1,0:T(8,128)}, f32[1,5,4,8,384]{4,3,2,1,0:T(8,128)}) custom-call(s16[16,16,128]{2,1,0:T(8,128)(2,1)S(1)} %collective-permute-done.8.refs_0_, s16[16,16,128]{2,1,0:T(8,128)(2,1)S(1)} %collective-permute-done.9.refs_1_, s16[16,16,128]{2,1,0:T(8,128)(2,1)S(1)} %collective-permute-done.10.refs_2_, ...), custom_call_target="tpu_custom_call" | custom-call | tf_op jit(solution)/shard_map/pallas_call | solution.py:751
  (32 shorter events, 0.4 us)
Async XLA Ops:
  0.6 11.3 %copy-start.8 = (f32[1,4,4]{2,1,0:T(4,128)S(1)}, f32[1,4,4]{2,1,0:T(4,128)}, u32[]{:S(2)}) copy-start(f32[1,4,4]{2,1,0:T(4,128)} %refs_1_.6) | copy-start | bytes 196
  0.6 11.3 %copy-start.7 = (f32[5,5]{1,0:T(8,128)S(1)}, f32[5,5]{1,0:T(8,128)}, u32[]{:S(2)}) copy-start(f32[5,5]{1,0:T(8,128)} %refs_2_.3) | copy-start | bytes 304
  1.3 1.1 %copy-start = (bf16[4,4,5,4,8,96]{5,4,3,2,1,0:T(8,128)(2,1)S(1)}, bf16[4,4,5,4,8,96]{5,4,3,2,1,0:T(8,128)(2,1)}, u32[]{:S(2)}) copy-start(bf16[4,4,5,4,8,96]{5,4,3,2,1,0:T(8,128)(2,1)} %refs_1_.10) | copy-start | bytes 1474564
  2.4 7.5 %copy-start.2 = (f32[1,5,4,8,384]{4,3,2,1,0:T(8,128)S(1)}, f32[1,5,4,8,384]{4,3,2,1,0:T(8,128)}, u32[]{:S(2)}) copy-start(f32[1,5,4,8,384]{4,3,2,1,0:T(8,128)} %refs_6_.3) | copy-start | bytes 737284
  2.4 7.5 %copy-start.3 = (f32[1,4,4,8,384]{4,3,2,1,0:T(8,128)S(1)}, f32[1,4,4,8,384]{4,3,2,1,0:T(8,128)}, u32[]{:S(2)}) copy-start(f32[1,4,4,8,384]{4,3,2,1,0:T(8,128)} %refs_3_.5) | copy-start | bytes 589828
  2.4 7.5 %copy-start.4 = (f32[1,5,4,8,384]{4,3,2,1,0:T(8,128)S(1)}, f32[1,5,4,8,384]{4,3,2,1,0:T(8,128)}, u32[]{:S(2)}) copy-start(f32[1,5,4,8,384]{4,3,2,1,0:T(8,128)} %refs_8_.3) | copy-start | bytes 737284
  2.4 8.7 %copy-start.1 = (bf16[4,4,5,4,8,96]{5,4,3,2,1,0:T(8,128)(2,1)S(1)}, bf16[4,4,5,4,8,96]{5,4,3,2,1,0:T(8,128)(2,1)}, u32[]{:S(2)}) copy-start(bf16[4,4,5,4,8,96]{5,4,3,2,1,0:T(8,128)(2,1)} %refs_1_.10) | copy-start | bytes 1474564
  2.4 9.5 %copy-start.6 = (f32[1,4,4,8,384]{4,3,2,1,0:T(8,128)S(1)}, f32[1,4,4,8,384]{4,3,2,1,0:T(8,128)}, u32[]{:S(2)}) copy-start(f32[1,4,4,8,384]{4,3,2,1,0:T(8,128)} %refs_4_.1) | copy-start | bytes 589828
  2.6 10.1 %collective-permute-start = (bf16[61,8,128]{2,1,0:T(8,128)(2,1)S(1)}, bf16[61,8,128]{2,1,0:T(8,128)(2,1)S(1)}, u32[]{:S(2)}, u32[]{:S(2)}) collective-permute-start(bf16[61,8,128]{2,1,0:T(8,128)(2,1)S(1)} %shard_map.123), channel_id=1, source_target_pairs={{0,4},{4,8},{8,12},{12,0},{1,5},{5,9},{9,13},{13,1},{2,6},{6,10},{... | collective-permute-start | bytes 374792 | tf_op jit(solution)/shard_map/ppermute | solution.py:588
  5.8 10.7 %collective-permute-start.1 = (bf16[61,8,128]{2,1,0:T(8,128)(2,1)S(1)}, bf16[61,8,128]{2,1,0:T(8,128)(2,1)S(1)}, u32[]{:S(2)}, u32[]{:S(2)}) collective-permute-start(bf16[61,8,128]{2,1,0:T(8,128)(2,1)S(1)} %shard_map.124), channel_id=1, source_target_pairs={{0,8},{4,12},{8,0},{12,4},{1,9},{5,13},{9,1},{13,5},{2,10},{6,14},... | collective-permute-start | bytes 374792 | tf_op jit(solution)/shard_map/ppermute | solution.py:588
  8.5 8.0 %collective-permute-start.2 = (bf16[61,8,128]{2,1,0:T(8,128)(2,1)S(1)}, bf16[61,8,128]{2,1,0:T(8,128)(2,1)S(1)}, u32[]{:S(2)}, u32[]{:S(2)}) collective-permute-start(bf16[61,8,128]{2,1,0:T(8,128)(2,1)S(1)} %shard_map.125), channel_id=1, source_target_pairs={{0,12},{4,0},{8,4},{12,8},{1,13},{5,1},{9,5},{13,9},{2,14},{6,2},{... | collective-permute-start | bytes 374792 | tf_op jit(solution)/shard_map/ppermute | solution.py:588
  10.4 7.3 %collective-permute-start.3 = (s16[2,21,16,128]{3,2,1,0:T(8,128)(2,1)S(1)}, s16[2,21,16,128]{3,2,1,0:T(8,128)(2,1)S(1)}, u32[]{:S(2)}, u32[]{:S(2)}) collective-permute-start(s16[2,21,16,128]{3,2,1,0:T(8,128)(2,1)S(1)} %get-tuple-element.36), channel_id=1, source_target_pairs={{0,1},{1,0},{2,3},{3,2},{4,5},{5,4},{6,7},{7,6},{8,9},{9,8},{10,11... | collective-permute-start | bytes 516104 | tf_op jit(solution)/shard_map/ppermute | solution.py:599
  10.5 7.2 %collective-permute-start.4 = (s16[2,21,16,128]{3,2,1,0:T(8,128)(2,1)S(1)}, s16[2,21,16,128]{3,2,1,0:T(8,128)(2,1)S(1)}, u32[]{:S(2)}, u32[]{:S(2)}) collective-permute-start(s16[2,21,16,128]{3,2,1,0:T(8,128)(2,1)S(1)} %get-tuple-element.37), channel_id=1, source_target_pairs={{1,2},{2,1},{5,6},{6,5},{9,10},{10,9},{13,14},{14,13},{17,18},{18,... | collective-permute-start | bytes 516104 | tf_op jit(solution)/shard_map/ppermute | solution.py:599
  17.0 3.9 %collective-permute-start.5 = (bf16[4,10,8,384]{3,2,1,0:T(8,128)(2,1)S(1)}, bf16[4,10,8,384]{3,2,1,0:T(8,128)(2,1)S(1)}, u32[]{:S(2)}, u32[]{:S(2)}) collective-permute-start(bf16[4,10,8,384]{3,2,1,0:T(8,128)(2,1)S(1)} %get-tuple-element.42), channel_id=1, source_target_pairs={{0,1},{1,0},{2,3},{3,2},{4,5},{5,4},{6,7},{7,6},{8,9},{9,8},{10,11... | collective-permute-start | bytes 737288 | tf_op jit(solution)/shard_map/ppermute | solution.py:599
  17.1 3.9 %collective-permute-start.6 = (bf16[31,8,384]{2,1,0:T(8,128)(2,1)S(1)}, bf16[31,8,384]{2,1,0:T(8,128)(2,1)S(1)}, u32[]{:S(2)}, u32[]{:S(2)}) collective-permute-start(bf16[31,8,384]{2,1,0:T(8,128)(2,1)S(1)} %get-tuple-element.43), channel_id=1, source_target_pairs={{1,2},{2,1},{5,6},{6,5},{9,10},{10,9},{13,14},{14,13},{17,18},{18,... | collective-permute-start | bytes 571400 | tf_op jit(solution)/shard_map/ppermute | solution.py:599
  18.0 8.3 %copy-start.5 = (f32[1,5,4,8,384]{4,3,2,1,0:T(8,128)S(1)}, f32[1,5,4,8,384]{4,3,2,1,0:T(8,128)}, u32[]{:S(2)}) copy-start(f32[1,5,4,8,384]{4,3,2,1,0:T(8,128)} %refs_7_.3) | copy-start | bytes 737284
  18.0 8.1 %collective-permute-start.7 = (s16[2,16,16,128]{3,2,1,0:T(8,128)(2,1)S(1)}, s16[2,16,16,128]{3,2,1,0:T(8,128)(2,1)S(1)}, u32[]{:S(2)}, u32[]{:S(2)}) collective-permute-start(s16[2,16,16,128]{3,2,1,0:T(8,128)(2,1)S(1)} %get-tuple-element.45), channel_id=1, source_target_pairs={{4,0},{8,4},{12,8},{5,1},{9,5},{13,9},{6,2},{10,6},{14,10},{7,3},{... | collective-permute-start | bytes 393224 | tf_op jit(solution)/shard_map/ppermute | solution.py:588
  19.5 16.4 %collective-permute-start.11 = (s16[2,16,16,128]{3,2,1,0:T(8,128)(2,1)S(1)}, s16[2,16,16,128]{3,2,1,0:T(8,128)(2,1)S(1)}, u32[]{:S(2)}, u32[]{:S(2)}) collective-permute-start(s16[2,16,16,128]{3,2,1,0:T(8,128)(2,1)S(1)} %get-tuple-element.52), channel_id=1, source_target_pairs={{4,0},{8,4},{12,8},{5,1},{9,5},{13,9},{6,2},{10,6},{14,10},{7,3},{... | collective-permute-start | bytes 393224 | tf_op jit(solution)/shard_map/ppermute | solution.py:588
  27.7 10.3 %collective-permute-start.8 = (s16[16,16,128]{2,1,0:T(8,128)(2,1)S(1)}, s16[16,16,128]{2,1,0:T(8,128)(2,1)S(1)}, u32[]{:S(2)}, u32[]{:S(2)}) collective-permute-start(s16[16,16,128]{2,1,0:T(8,128)(2,1)S(1)} %get-tuple-element.49), channel_id=1, source_target_pairs={{0,8},{4,12},{8,0},{12,4},{1,9},{5,13},{9,1},{13,5},{2,10},{6,14},... | collective-permute-start | bytes 196616 | tf_op jit(solution)/shard_map/ppermute | solution.py:588
  32.0 9.4 %collective-permute-start.9 = (s16[16,16,128]{2,1,0:T(8,128)(2,1)S(1)}, s16[16,16,128]{2,1,0:T(8,128)(2,1)S(1)}, u32[]{:S(2)}, u32[]{:S(2)}) collective-permute-start(s16[16,16,128]{2,1,0:T(8,128)(2,1)S(1)} %get-tuple-element.50), channel_id=1, source_target_pairs={{0,4},{4,8},{8,12},{12,0},{1,5},{5,9},{9,13},{13,1},{2,6},{6,10},{... | collective-permute-start | bytes 196616 | tf_op jit(solution)/shard_map/ppermute | solution.py:588
  34.0 7.4 %collective-permute-start.10 = (s16[16,16,128]{2,1,0:T(8,128)(2,1)S(1)}, s16[16,16,128]{2,1,0:T(8,128)(2,1)S(1)}, u32[]{:S(2)}, u32[]{:S(2)}) collective-permute-start(s16[16,16,128]{2,1,0:T(8,128)(2,1)S(1)} %get-tuple-element.51), channel_id=1, source_target_pairs={{0,12},{4,0},{8,4},{12,8},{1,13},{5,1},{9,5},{13,9},{2,14},{6,2},{... | collective-permute-start | bytes 196616 | tf_op jit(solution)/shard_map/ppermute | solution.py:588
  37.4 8.4 %collective-permute-start.12 = (s16[16,16,128]{2,1,0:T(8,128)(2,1)S(1)}, s16[16,16,128]{2,1,0:T(8,128)(2,1)S(1)}, u32[]{:S(2)}, u32[]{:S(2)}) collective-permute-start(s16[16,16,128]{2,1,0:T(8,128)(2,1)S(1)} %get-tuple-element.56), channel_id=1, source_target_pairs={{0,8},{4,12},{8,0},{12,4},{1,9},{5,13},{9,1},{13,5},{2,10},{6,14},... | collective-permute-start | bytes 196616 | tf_op jit(solution)/shard_map/ppermute | solution.py:588
  37.5 8.3 %collective-permute-start.13 = (s16[16,16,128]{2,1,0:T(8,128)(2,1)S(1)}, s16[16,16,128]{2,1,0:T(8,128)(2,1)S(1)}, u32[]{:S(2)}, u32[]{:S(2)}) collective-permute-start(s16[16,16,128]{2,1,0:T(8,128)(2,1)S(1)} %get-tuple-element.57), channel_id=1, source_target_pairs={{0,4},{4,8},{8,12},{12,0},{1,5},{5,9},{9,13},{13,1},{2,6},{6,10},{... | collective-permute-start | bytes 196616 | tf_op jit(solution)/shard_map/ppermute | solution.py:588
  38.1 8.2 %collective-permute-start.14 = (s16[16,16,128]{2,1,0:T(8,128)(2,1)S(1)}, s16[16,16,128]{2,1,0:T(8,128)(2,1)S(1)}, u32[]{:S(2)}, u32[]{:S(2)}) collective-permute-start(s16[16,16,128]{2,1,0:T(8,128)(2,1)S(1)} %get-tuple-element.58), channel_id=1, source_target_pairs={{0,12},{4,0},{8,4},{12,8},{1,13},{5,1},{9,5},{13,9},{2,14},{6,2},{... | collective-permute-start | bytes 196616 | tf_op jit(solution)/shard_map/ppermute | solution.py:588

commit v13 on v12

--- a/solution.py
+++ b/solution.py
@@ -8,7 +8,7 @@
 LANES = 128
 SUB = 8
 HALF = SUB // 2
-CODE_MAX = 32766.0
+CODE_MAX = 32000.0
 ROUNDER = 12582912.0
 
 diffusion = 0.2
@@ -423,8 +423,8 @@
                 for t in range(tiles):
                     s_ref[odd, 0, v, t, SUB : 3 * SUB, :] = first_ref[2 * i + odd, v, t]
 
-        def step(j, carry):
-            now = lax.rem(j, 2)
+        for j in range(steps):
+            now = j % 2
             for odd in range(2):
                 lev = 2 * i + odd
                 for t in range(tiles):
@@ -452,9 +452,6 @@
                             for u in range(nvar):
                                 fresh = fresh + mix_ref[v, u] * xs[u][t]
                             s_ref[odd, 1 - now, v, t, here, :] = fresh
-            return carry
-
-        lax.fori_loop(0, steps, step, 0)
         for odd in range(2):
             for v in range(nvar):
                 for t in range(tiles):
@@ -484,8 +481,8 @@
             for v in range(nvar):
                 a_ref[odd, 0, v, t, SUB : 3 * SUB, :] = last_ref[odd, v, t]
 
-    def step(turn, carry):
-        now = lax.rem(turn, 2)
+    for turn in range(steps):
+        now = turn % 2
         j = steps - 1 - turn
         for odd in range(2):
             lev = 2 * i + odd
@@ -515,10 +512,6 @@
                         if u == 0:
                             fresh = fresh + force_ref[odd, j, t, part, :]
                         a_ref[odd, 1 - now, u, t, here, :] = fresh
-        return carry
-
-    lax.fori_loop(0, steps, step, 0)
-
     end = steps % 2
     coded = []
     for odd in range(2):

time: 47.6 us -> 46.3 us (0.973)
  Pallas kernels: 10.2 us -> 8.86 us
  starting transfers between devices: 23.4 us -> 22.6 us
  waiting for transfers between devices: 10.4 us -> 11.1 us
    ppermute x11, starting transfers between devices: 21.9 us -> 21.1 us  [moved(): return lax.ppermute(block, axis, route)]
    pallas_call x1, Pallas kernels: 3.58 us -> 2.82 us  [body(): pl.pallas_call(lambda *refs: tangent_kernel(spaces, steps, nvar, levels,...]
    ppermute x11, waiting for transfers between devices: 10.4 us -> 11.1 us  [moved(): return lax.ppermute(block, axis, route)]
    pallas_call x2, Pallas kernels: 2.89 us -> 2.32 us  [body(): pl.pallas_call(lambda *refs, i=i: adjoint_kernel(i, windows, spaces, step...]
  transfers between devices with their start and end apart: 15 -> 15, of which waited for: 4 -> 4; matrix products, arithmetic and copies ran while one was open for 0% -> 0% of each run, Pallas kernels for 19% -> 17%
where the time goes in v13:
time: 46.3 us; the launch traced here: 46 us
  starting transfers between devices  22.6 us (49%)
  waiting for transfers between devices  11.1 us (24%)
  Pallas kernels  8.86 us (19%)
  local copies, waits for them, and re-layouts  1.82 us (4%)
  between operations  1.55 us (3%)
    ppermute x11, starting transfers between devices, moved(): return lax.ppermute(block, axis, route)  21.1 us
    ppermute x11, waiting for transfers between devices, moved(): return lax.ppermute(block, axis, route)  11.1 us
    pallas_call x1, Pallas kernels, body(): pl.pallas_call(lambda *refs: tangent_kernel(spaces, steps, nvar, levels,...  2.82 us
    pallas_call x2, Pallas kernels, body(): pl.pallas_call(lambda *refs, i=i: adjoint_kernel(i, windows, spaces, step...  2.32 us
    ppermute x4, starting transfers between devices, swapped(): return lax.ppermute(block, axis, swaps(axis, first))  1.49 us
    unnamed x18, local copies, waits for them, and re-layouts  1.12 us
    pallas_call x1, Pallas kernels, body(): pl.pallas_call(lambda *refs: final_kernel(windows, nvar, levels, tiles, *...  1.02 us
  transfers between devices with their start and end apart: 15, of which 4 were waited for; matrix products, arithmetic and copies ran while one was open for 0% of the time, Pallas kernels for 17%

profile of v13, /device:TPU:0, one launch (start us, length us, event | category | flops | bytes accessed | tf_op | source)
XLA Modules:
  0.0 46.0 jit_solution(16332486644487955355)
XLA Ops:
  0.7 0.7 %pad.4.refs_0_ = f32[8,128]{1,0:T(8,128)S(1)} pad(f32[4,5]{1,0:T(4,128)} %bitcast.3, f32[]{:T(128)} %constant.2.clone.1), padding=0_4x0_123 | pad | bytes 4180 | tf_op jit(solution)/shard_map/jit(_pad)/pad | solution.py:621
  1.4 1.1 %copy-done = bf16[4,4,5,4,8,96]{5,4,3,2,1,0:T(8,128)(2,1)S(1)} copy-done((bf16[4,4,5,4,8,96]{5,4,3,2,1,0:T(8,128)(2,1)S(1)}, bf16[4,4,5,4,8,96]{5,4,3,2,1,0:T(8,128)(2,1)}, u32[]{:S(2)}) %copy-start) | copy-done | bytes 491544
  2.5 0.1 shard_map.123
  2.6 3.1 %collective-permute-start = (bf16[61,8,128]{2,1,0:T(8,128)(2,1)S(1)}, bf16[61,8,128]{2,1,0:T(8,128)(2,1)S(1)}, u32[]{:S(2)}, u32[]{:S(2)}) collective-permute-start(bf16[61,8,128]{2,1,0:T(8,128)(2,1)S(1)} %shard_map.123), channel_id=1, source_target_pairs={{0,4},{4,8},{8,12},{12,0},{1,5},{5,9},{9,13},{13,1},{2,6},{6,10},{... | collective-permute-start | bytes 374792 | tf_op jit(solution)/shard_map/ppermute | solution.py:581
  5.8 2.7 %collective-permute-start.1 = (bf16[61,8,128]{2,1,0:T(8,128)(2,1)S(1)}, bf16[61,8,128]{2,1,0:T(8,128)(2,1)S(1)}, u32[]{:S(2)}, u32[]{:S(2)}) collective-permute-start(bf16[61,8,128]{2,1,0:T(8,128)(2,1)S(1)} %shard_map.124), channel_id=1, source_target_pairs={{0,8},{4,12},{8,0},{12,4},{1,9},{5,13},{9,1},{13,5},{2,10},{6,14},... | collective-permute-start | bytes 374792 | tf_op jit(solution)/shard_map/ppermute | solution.py:581
  8.4 0.1 shard_map.125
  8.5 1.4 %collective-permute-start.2 = (bf16[61,8,128]{2,1,0:T(8,128)(2,1)S(1)}, bf16[61,8,128]{2,1,0:T(8,128)(2,1)S(1)}, u32[]{:S(2)}, u32[]{:S(2)}) collective-permute-start(bf16[61,8,128]{2,1,0:T(8,128)(2,1)S(1)} %shard_map.125), channel_id=1, source_target_pairs={{0,12},{4,0},{8,4},{12,8},{1,13},{5,1},{9,5},{13,9},{2,14},{6,2},{... | collective-permute-start | bytes 374792 | tf_op jit(solution)/shard_map/ppermute | solution.py:581
  10.0 0.5 %shard_map.126 = (s16[2,21,16,128]{3,2,1,0:T(8,128)(2,1)S(1)}, s16[2,21,16,128]{3,2,1,0:T(8,128)(2,1)S(1)}, s16[2,16,16,128]{3,2,1,0:T(8,128)(2,1)S(1)}) custom-call(f32[1,5,4,8,384]{4,3,2,1,0:T(8,128)S(1)} %copy-done.4, f32[1,5,4,8,384]{4,3,2,1,0:T(8,128)S(1)} %copy-done.2, f32[1,4,4,8,384]{4,3,2,1,0:T(8,128)S(1)} %copy-done.3), custom_call_target="tpu_custom_call" | custom-call | tf_op jit(solution)/shard_map/pallas_call | solution.py:645
  10.5 0.7 %collective-permute-start.4 = (s16[2,21,16,128]{3,2,1,0:T(8,128)(2,1)S(1)}, s16[2,21,16,128]{3,2,1,0:T(8,128)(2,1)S(1)}, u32[]{:S(2)}, u32[]{:S(2)}) collective-permute-start(s16[2,21,16,128]{3,2,1,0:T(8,128)(2,1)S(1)} %get-tuple-element.37), channel_id=1, source_target_pairs={{1,2},{2,1},{5,6},{6,5},{9,10},{10,9},{13,14},{14,13},{17,18},{18,... | collective-permute-start | bytes 516104 | tf_op jit(solution)/shard_map/ppermute | solution.py:592
  11.2 0.1 shard_map.122.refs_0_
  12.0 0.7 %shard_map.121 = (f32[4,4,3,8,128]{4,3,2,1,0:T(8,128)S(1)}, f32[4,4,8,128]{3,2,1,0:T(8,128)S(1)}, f32[5,5,8,128]{3,2,1,0:T(8,128)S(1)}) custom-call(s32[1]{0:T(128)S(6)} %copy.13.refs_0_, f32[1,4,4]{2,1,0:T(4,128)S(1)} %copy-done.8, f32[5,5]{1,0:T(8,128)S(1)} %copy-done.7, f32[1,4,4,8,384]{4,3,2,1,0:T(8,128)S(1)} %copy-done.3, f32[1,4,4,8,384]{4,3,2,1,0:T(8,128)S(1)} %copy-done.6), custom_call_target="tpu_custom_call" | custom-call | tf_op jit(solution)/shard_map/pallas_call | solution.py:665
  12.7 3.8 %collective-permute-done.1.refs_2_ = bf16[61,8,128]{2,1,0:T(8,128)(2,1)S(1)} collective-permute-done((bf16[61,8,128]{2,1,0:T(8,128)(2,1)S(1)}, bf16[61,8,128]{2,1,0:T(8,128)(2,1)S(1)}, u32[]{:S(2)}, u32[]{:S(2)}) %collective-permute-start.1) | collective-permute-done | bytes 124960 | tf_op jit(solution)/shard_map/ppermute | solution.py:581
  16.5 0.5 shard_map.128
  17.1 0.7 %collective-permute-start.6 = (bf16[31,8,384]{2,1,0:T(8,128)(2,1)S(1)}, bf16[31,8,384]{2,1,0:T(8,128)(2,1)S(1)}, u32[]{:S(2)}, u32[]{:S(2)}) collective-permute-start(bf16[31,8,384]{2,1,0:T(8,128)(2,1)S(1)} %get-tuple-element.43), channel_id=1, source_target_pairs={{1,2},{2,1},{5,6},{6,5},{9,10},{10,9},{13,14},{14,13},{17,18},{18,... | collective-permute-start | bytes 571400 | tf_op jit(solution)/shard_map/ppermute | solution.py:592
  17.8 0.3 shard_map.127
  18.0 1.4 %collective-permute-start.7 = (s16[2,16,16,128]{3,2,1,0:T(8,128)(2,1)S(1)}, s16[2,16,16,128]{3,2,1,0:T(8,128)(2,1)S(1)}, u32[]{:S(2)}, u32[]{:S(2)}) collective-permute-start(s16[2,16,16,128]{3,2,1,0:T(8,128)(2,1)S(1)} %get-tuple-element.45), channel_id=1, source_target_pairs={{4,0},{8,4},{12,8},{5,1},{9,5},{13,9},{6,2},{10,6},{14,10},{7,3},{... | collective-permute-start | bytes 393224 | tf_op jit(solution)/shard_map/ppermute | solution.py:581
  19.5 1.3 %collective-permute-start.11 = (s16[2,16,16,128]{3,2,1,0:T(8,128)(2,1)S(1)}, s16[2,16,16,128]{3,2,1,0:T(8,128)(2,1)S(1)}, u32[]{:S(2)}, u32[]{:S(2)}) collective-permute-start(s16[2,16,16,128]{3,2,1,0:T(8,128)(2,1)S(1)} %get-tuple-element.52), channel_id=1, source_target_pairs={{4,0},{8,4},{12,8},{5,1},{9,5},{13,9},{6,2},{10,6},{14,10},{7,3},{... | collective-permute-start | bytes 393224 | tf_op jit(solution)/shard_map/ppermute | solution.py:581
  20.8 0.1 shard_map.129.refs_6_
  20.9 2.8 %shard_map.130 = (f32[1,4,4,8,384]{4,3,2,1,0:T(8,128)}, f32[4,5,3,8,128]{4,3,2,1,0:T(8,128)S(1)}, f32[4,4,5,3,16,128]{5,4,3,2,1,0:T(8,128)S(1)}) custom-call(f32[5,5,8,128]{3,2,1,0:T(8,128)S(1)} %get-tuple-element.34.refs_4_.refs_0_, f32[4,4,8,128]{3,2,1,0:T(8,128)S(1)} %get-tuple-element.39.refs_1_, f32[4,4,3,8,128]{4,3,2,1,0:T(8,128)S(1)} %get-tuple-element.40.refs_2_, ...), custom_call_target="tpu_custom_call" | custom-call | tf_op jit(solution)/shard_map/pallas_call | solution.py:698
  23.8 2.4 %collective-permute-done.7.refs_4_ = s16[2,16,16,128]{3,2,1,0:T(8,128)(2,1)S(1)} collective-permute-done((s16[2,16,16,128]{3,2,1,0:T(8,128)(2,1)S(1)}, s16[2,16,16,128]{3,2,1,0:T(8,128)(2,1)S(1)}, u32[]{:S(2)}, u32[]{:S(2)}) %collective-permute-start.7) | collective-permute-done | bytes 131104 | tf_op jit(solution)/shard_map/ppermute | solution.py:581
  26.2 0.1 shard_map.131
  26.3 1.2 %shard_map.132 = (f32[5,2,8,384]{3,2,1,0:T(8,128)S(1)}, f32[5,2,8,384]{3,2,1,0:T(8,128)S(1)}, s16[16,16,128]{2,1,0:T(8,128)(2,1)S(1)}, s16[16,16,128]{2,1,0:T(8,128)(2,1)S(1)}, s16[16,16,128]{2,1,0:T(8,128)(2,1)S(1)}) custom-call(f32[5,5,8,128]{3,2,1,0:T(8,128)S(1)} %get-tuple-element.34.refs_4_.refs_0_, ...), custom_call_target="tpu_custom_call" | custom-call | tf_op jit(solution)/shard_map/pallas_call | solution.py:723
  27.5 3.5 %collective-permute-start.8 = (s16[16,16,128]{2,1,0:T(8,128)(2,1)S(1)}, s16[16,16,128]{2,1,0:T(8,128)(2,1)S(1)}, u32[]{:S(2)}, u32[]{:S(2)}) collective-permute-start(s16[16,16,128]{2,1,0:T(8,128)(2,1)S(1)} %get-tuple-element.49), channel_id=1, source_target_pairs={{0,8},{4,12},{8,0},{12,4},{1,9},{5,13},{9,1},{13,5},{2,10},{6,14},... | collective-permute-start | bytes 196616 | tf_op jit(solution)/shard_map/ppermute | solution.py:581
  31.0 2.0 %collective-permute-start.9 = (s16[16,16,128]{2,1,0:T(8,128)(2,1)S(1)}, s16[16,16,128]{2,1,0:T(8,128)(2,1)S(1)}, u32[]{:S(2)}, u32[]{:S(2)}) collective-permute-start(s16[16,16,128]{2,1,0:T(8,128)(2,1)S(1)} %get-tuple-element.50), channel_id=1, source_target_pairs={{0,4},{4,8},{8,12},{12,0},{1,5},{5,9},{9,13},{13,1},{2,6},{6,10},{... | collective-permute-start | bytes 196616 | tf_op jit(solution)/shard_map/ppermute | solution.py:581
  33.0 1.8 %collective-permute-start.10 = (s16[16,16,128]{2,1,0:T(8,128)(2,1)S(1)}, s16[16,16,128]{2,1,0:T(8,128)(2,1)S(1)}, u32[]{:S(2)}, u32[]{:S(2)}) collective-permute-start(s16[16,16,128]{2,1,0:T(8,128)(2,1)S(1)} %get-tuple-element.51), channel_id=1, source_target_pairs={{0,12},{4,0},{8,4},{12,8},{1,13},{5,1},{9,5},{13,9},{2,14},{6,2},{... | collective-permute-start | bytes 196616 | tf_op jit(solution)/shard_map/ppermute | solution.py:581
  34.8 0.1 shard_map.133
  34.9 1.2 %shard_map.134 = (f32[5,2,8,384]{3,2,1,0:T(8,128)S(1)}, f32[5,2,8,384]{3,2,1,0:T(8,128)S(1)}, s16[16,16,128]{2,1,0:T(8,128)(2,1)S(1)}, s16[16,16,128]{2,1,0:T(8,128)(2,1)S(1)}, s16[16,16,128]{2,1,0:T(8,128)(2,1)S(1)}) custom-call(f32[5,5,8,128]{3,2,1,0:T(8,128)S(1)} %get-tuple-element.34.refs_4_.refs_0_, ...), custom_call_target="tpu_custom_call" | custom-call | tf_op jit(solution)/shard_map/pallas_call | solution.py:723
  36.2 0.6 %collective-permute-start.13 = (s16[16,16,128]{2,1,0:T(8,128)(2,1)S(1)}, s16[16,16,128]{2,1,0:T(8,128)(2,1)S(1)}, u32[]{:S(2)}, u32[]{:S(2)}) collective-permute-start(s16[16,16,128]{2,1,0:T(8,128)(2,1)S(1)} %get-tuple-element.57), channel_id=1, source_target_pairs={{0,4},{4,8},{8,12},{12,0},{1,5},{5,9},{9,13},{13,1},{2,6},{6,10},{... | collective-permute-start | bytes 196616 | tf_op jit(solution)/shard_map/ppermute | solution.py:581
  36.7 3.3 %collective-permute-start.14 = (s16[16,16,128]{2,1,0:T(8,128)(2,1)S(1)}, s16[16,16,128]{2,1,0:T(8,128)(2,1)S(1)}, u32[]{:S(2)}, u32[]{:S(2)}) collective-permute-start(s16[16,16,128]{2,1,0:T(8,128)(2,1)S(1)} %get-tuple-element.58), channel_id=1, source_target_pairs={{0,12},{4,0},{8,4},{12,8},{1,13},{5,1},{9,5},{13,9},{2,14},{6,2},{... | collective-permute-start | bytes 196616 | tf_op jit(solution)/shard_map/ppermute | solution.py:581
  40.1 4.4 %collective-permute-done.12.refs_3_ = s16[16,16,128]{2,1,0:T(8,128)(2,1)S(1)} collective-permute-done((s16[16,16,128]{2,1,0:T(8,128)(2,1)S(1)}, s16[16,16,128]{2,1,0:T(8,128)(2,1)S(1)}, u32[]{:S(2)}, u32[]{:S(2)}) %collective-permute-start.12) | collective-permute-done | bytes 65568 | tf_op jit(solution)/shard_map/ppermute | solution.py:581
  44.5 0.5 %collective-permute-done.14.refs_5_ = s16[16,16,128]{2,1,0:T(8,128)(2,1)S(1)} collective-permute-done((s16[16,16,128]{2,1,0:T(8,128)(2,1)S(1)}, s16[16,16,128]{2,1,0:T(8,128)(2,1)S(1)}, u32[]{:S(2)}, u32[]{:S(2)}) %collective-permute-start.14) | collective-permute-done | bytes 65568 | tf_op jit(solution)/shard_map/ppermute | solution.py:581
  45.0 1.0 %shard_map.135 = (f32[1,5,4,8,384]{4,3,2,1,0:T(8,128)}, f32[1,5,4,8,384]{4,3,2,1,0:T(8,128)}) custom-call(s16[16,16,128]{2,1,0:T(8,128)(2,1)S(1)} %collective-permute-done.8.refs_0_, s16[16,16,128]{2,1,0:T(8,128)(2,1)S(1)} %collective-permute-done.9.refs_1_, s16[16,16,128]{2,1,0:T(8,128)(2,1)S(1)} %collective-permute-done.10.refs_2_, ...), custom_call_target="tpu_custom_call" | custom-call | tf_op jit(solution)/shard_map/pallas_call | solution.py:744
  (32 shorter events, 0.4 us)
Async XLA Ops:
  0.6 11.3 %copy-start.8 = (f32[1,4,4]{2,1,0:T(4,128)S(1)}, f32[1,4,4]{2,1,0:T(4,128)}, u32[]{:S(2)}) copy-start(f32[1,4,4]{2,1,0:T(4,128)} %refs_1_.6) | copy-start | bytes 196
  0.6 11.3 %copy-start.7 = (f32[5,5]{1,0:T(8,128)S(1)}, f32[5,5]{1,0:T(8,128)}, u32[]{:S(2)}) copy-start(f32[5,5]{1,0:T(8,128)} %refs_2_.3) | copy-start | bytes 304
  1.3 1.1 %copy-start = (bf16[4,4,5,4,8,96]{5,4,3,2,1,0:T(8,128)(2,1)S(1)}, bf16[4,4,5,4,8,96]{5,4,3,2,1,0:T(8,128)(2,1)}, u32[]{:S(2)}) copy-start(bf16[4,4,5,4,8,96]{5,4,3,2,1,0:T(8,128)(2,1)} %refs_1_.10) | copy-start | bytes 1474564
  2.4 7.5 %copy-start.2 = (f32[1,5,4,8,384]{4,3,2,1,0:T(8,128)S(1)}, f32[1,5,4,8,384]{4,3,2,1,0:T(8,128)}, u32[]{:S(2)}) copy-start(f32[1,5,4,8,384]{4,3,2,1,0:T(8,128)} %refs_6_.3) | copy-start | bytes 737284
  2.4 7.5 %copy-start.3 = (f32[1,4,4,8,384]{4,3,2,1,0:T(8,128)S(1)}, f32[1,4,4,8,384]{4,3,2,1,0:T(8,128)}, u32[]{:S(2)}) copy-start(f32[1,4,4,8,384]{4,3,2,1,0:T(8,128)} %refs_3_.5) | copy-start | bytes 589828
  2.4 7.5 %copy-start.4 = (f32[1,5,4,8,384]{4,3,2,1,0:T(8,128)S(1)}, f32[1,5,4,8,384]{4,3,2,1,0:T(8,128)}, u32[]{:S(2)}) copy-start(f32[1,5,4,8,384]{4,3,2,1,0:T(8,128)} %refs_8_.3) | copy-start | bytes 737284
  2.4 8.7 %copy-start.1 = (bf16[4,4,5,4,8,96]{5,4,3,2,1,0:T(8,128)(2,1)S(1)}, bf16[4,4,5,4,8,96]{5,4,3,2,1,0:T(8,128)(2,1)}, u32[]{:S(2)}) copy-start(bf16[4,4,5,4,8,96]{5,4,3,2,1,0:T(8,128)(2,1)} %refs_1_.10) | copy-start | bytes 1474564
  2.4 9.5 %copy-start.6 = (f32[1,4,4,8,384]{4,3,2,1,0:T(8,128)S(1)}, f32[1,4,4,8,384]{4,3,2,1,0:T(8,128)}, u32[]{:S(2)}) copy-start(f32[1,4,4,8,384]{4,3,2,1,0:T(8,128)} %refs_4_.1) | copy-start | bytes 589828
  2.6 10.1 %collective-permute-start = (bf16[61,8,128]{2,1,0:T(8,128)(2,1)S(1)}, bf16[61,8,128]{2,1,0:T(8,128)(2,1)S(1)}, u32[]{:S(2)}, u32[]{:S(2)}) collective-permute-start(bf16[61,8,128]{2,1,0:T(8,128)(2,1)S(1)} %shard_map.123), channel_id=1, source_target_pairs={{0,4},{4,8},{8,12},{12,0},{1,5},{5,9},{9,13},{13,1},{2,6},{6,10},{... | collective-permute-start | bytes 374792 | tf_op jit(solution)/shard_map/ppermute | solution.py:581
  5.8 10.7 %collective-permute-start.1 = (bf16[61,8,128]{2,1,0:T(8,128)(2,1)S(1)}, bf16[61,8,128]{2,1,0:T(8,128)(2,1)S(1)}, u32[]{:S(2)}, u32[]{:S(2)}) collective-permute-start(bf16[61,8,128]{2,1,0:T(8,128)(2,1)S(1)} %shard_map.124), channel_id=1, source_target_pairs={{0,8},{4,12},{8,0},{12,4},{1,9},{5,13},{9,1},{13,5},{2,10},{6,14},... | collective-permute-start | bytes 374792 | tf_op jit(solution)/shard_map/ppermute | solution.py:581
  8.5 8.0 %collective-permute-start.2 = (bf16[61,8,128]{2,1,0:T(8,128)(2,1)S(1)}, bf16[61,8,128]{2,1,0:T(8,128)(2,1)S(1)}, u32[]{:S(2)}, u32[]{:S(2)}) collective-permute-start(bf16[61,8,128]{2,1,0:T(8,128)(2,1)S(1)} %shard_map.125), channel_id=1, source_target_pairs={{0,12},{4,0},{8,4},{12,8},{1,13},{5,1},{9,5},{13,9},{2,14},{6,2},{... | collective-permute-start | bytes 374792 | tf_op jit(solution)/shard_map/ppermute | solution.py:581
  10.4 7.3 %collective-permute-start.3 = (s16[2,21,16,128]{3,2,1,0:T(8,128)(2,1)S(1)}, s16[2,21,16,128]{3,2,1,0:T(8,128)(2,1)S(1)}, u32[]{:S(2)}, u32[]{:S(2)}) collective-permute-start(s16[2,21,16,128]{3,2,1,0:T(8,128)(2,1)S(1)} %get-tuple-element.36), channel_id=1, source_target_pairs={{0,1},{1,0},{2,3},{3,2},{4,5},{5,4},{6,7},{7,6},{8,9},{9,8},{10,11... | collective-permute-start | bytes 516104 | tf_op jit(solution)/shard_map/ppermute | solution.py:592
  10.5 7.2 %collective-permute-start.4 = (s16[2,21,16,128]{3,2,1,0:T(8,128)(2,1)S(1)}, s16[2,21,16,128]{3,2,1,0:T(8,128)(2,1)S(1)}, u32[]{:S(2)}, u32[]{:S(2)}) collective-permute-start(s16[2,21,16,128]{3,2,1,0:T(8,128)(2,1)S(1)} %get-tuple-element.37), channel_id=1, source_target_pairs={{1,2},{2,1},{5,6},{6,5},{9,10},{10,9},{13,14},{14,13},{17,18},{18,... | collective-permute-start | bytes 516104 | tf_op jit(solution)/shard_map/ppermute | solution.py:592
  17.0 3.9 %collective-permute-start.5 = (bf16[4,10,8,384]{3,2,1,0:T(8,128)(2,1)S(1)}, bf16[4,10,8,384]{3,2,1,0:T(8,128)(2,1)S(1)}, u32[]{:S(2)}, u32[]{:S(2)}) collective-permute-start(bf16[4,10,8,384]{3,2,1,0:T(8,128)(2,1)S(1)} %get-tuple-element.42), channel_id=1, source_target_pairs={{0,1},{1,0},{2,3},{3,2},{4,5},{5,4},{6,7},{7,6},{8,9},{9,8},{10,11... | collective-permute-start | bytes 737288 | tf_op jit(solution)/shard_map/ppermute | solution.py:592
  17.1 3.9 %collective-permute-start.6 = (bf16[31,8,384]{2,1,0:T(8,128)(2,1)S(1)}, bf16[31,8,384]{2,1,0:T(8,128)(2,1)S(1)}, u32[]{:S(2)}, u32[]{:S(2)}) collective-permute-start(bf16[31,8,384]{2,1,0:T(8,128)(2,1)S(1)} %get-tuple-element.43), channel_id=1, source_target_pairs={{1,2},{2,1},{5,6},{6,5},{9,10},{10,9},{13,14},{14,13},{17,18},{18,... | collective-permute-start | bytes 571400 | tf_op jit(solution)/shard_map/ppermute | solution.py:592
  18.0 8.3 %copy-start.5 = (f32[1,5,4,8,384]{4,3,2,1,0:T(8,128)S(1)}, f32[1,5,4,8,384]{4,3,2,1,0:T(8,128)}, u32[]{:S(2)}) copy-start(f32[1,5,4,8,384]{4,3,2,1,0:T(8,128)} %refs_7_.3) | copy-start | bytes 737284
  18.0 8.1 %collective-permute-start.7 = (s16[2,16,16,128]{3,2,1,0:T(8,128)(2,1)S(1)}, s16[2,16,16,128]{3,2,1,0:T(8,128)(2,1)S(1)}, u32[]{:S(2)}, u32[]{:S(2)}) collective-permute-start(s16[2,16,16,128]{3,2,1,0:T(8,128)(2,1)S(1)} %get-tuple-element.45), channel_id=1, source_target_pairs={{4,0},{8,4},{12,8},{5,1},{9,5},{13,9},{6,2},{10,6},{14,10},{7,3},{... | collective-permute-start | bytes 393224 | tf_op jit(solution)/shard_map/ppermute | solution.py:581
  19.5 15.3 %collective-permute-start.11 = (s16[2,16,16,128]{3,2,1,0:T(8,128)(2,1)S(1)}, s16[2,16,16,128]{3,2,1,0:T(8,128)(2,1)S(1)}, u32[]{:S(2)}, u32[]{:S(2)}) collective-permute-start(s16[2,16,16,128]{3,2,1,0:T(8,128)(2,1)S(1)} %get-tuple-element.52), channel_id=1, source_target_pairs={{4,0},{8,4},{12,8},{5,1},{9,5},{13,9},{6,2},{10,6},{14,10},{7,3},{... | collective-permute-start | bytes 393224 | tf_op jit(solution)/shard_map/ppermute | solution.py:581
  27.5 9.3 %collective-permute-start.8 = (s16[16,16,128]{2,1,0:T(8,128)(2,1)S(1)}, s16[16,16,128]{2,1,0:T(8,128)(2,1)S(1)}, u32[]{:S(2)}, u32[]{:S(2)}) collective-permute-start(s16[16,16,128]{2,1,0:T(8,128)(2,1)S(1)} %get-tuple-element.49), channel_id=1, source_target_pairs={{0,8},{4,12},{8,0},{12,4},{1,9},{5,13},{9,1},{13,5},{2,10},{6,14},... | collective-permute-start | bytes 196616 | tf_op jit(solution)/shard_map/ppermute | solution.py:581
  31.0 9.1 %collective-permute-start.9 = (s16[16,16,128]{2,1,0:T(8,128)(2,1)S(1)}, s16[16,16,128]{2,1,0:T(8,128)(2,1)S(1)}, u32[]{:S(2)}, u32[]{:S(2)}) collective-permute-start(s16[16,16,128]{2,1,0:T(8,128)(2,1)S(1)} %get-tuple-element.50), channel_id=1, source_target_pairs={{0,4},{4,8},{8,12},{12,0},{1,5},{5,9},{9,13},{13,1},{2,6},{6,10},{... | collective-permute-start | bytes 196616 | tf_op jit(solution)/shard_map/ppermute | solution.py:581
  33.0 7.1 %collective-permute-start.10 = (s16[16,16,128]{2,1,0:T(8,128)(2,1)S(1)}, s16[16,16,128]{2,1,0:T(8,128)(2,1)S(1)}, u32[]{:S(2)}, u32[]{:S(2)}) collective-permute-start(s16[16,16,128]{2,1,0:T(8,128)(2,1)S(1)} %get-tuple-element.51), channel_id=1, source_target_pairs={{0,12},{4,0},{8,4},{12,8},{1,13},{5,1},{9,5},{13,9},{2,14},{6,2},{... | collective-permute-start | bytes 196616 | tf_op jit(solution)/shard_map/ppermute | solution.py:581
  36.1 8.4 %collective-permute-start.12 = (s16[16,16,128]{2,1,0:T(8,128)(2,1)S(1)}, s16[16,16,128]{2,1,0:T(8,128)(2,1)S(1)}, u32[]{:S(2)}, u32[]{:S(2)}) collective-permute-start(s16[16,16,128]{2,1,0:T(8,128)(2,1)S(1)} %get-tuple-element.56), channel_id=1, source_target_pairs={{0,8},{4,12},{8,0},{12,4},{1,9},{5,13},{9,1},{13,5},{2,10},{6,14},... | collective-permute-start | bytes 196616 | tf_op jit(solution)/shard_map/ppermute | solution.py:581
  36.2 8.3 %collective-permute-start.13 = (s16[16,16,128]{2,1,0:T(8,128)(2,1)S(1)}, s16[16,16,128]{2,1,0:T(8,128)(2,1)S(1)}, u32[]{:S(2)}, u32[]{:S(2)}) collective-permute-start(s16[16,16,128]{2,1,0:T(8,128)(2,1)S(1)} %get-tuple-element.57), channel_id=1, source_target_pairs={{0,4},{4,8},{8,12},{12,0},{1,5},{5,9},{9,13},{13,1},{2,6},{6,10},{... | collective-permute-start | bytes 196616 | tf_op jit(solution)/shard_map/ppermute | solution.py:581
  36.7 8.2 %collective-permute-start.14 = (s16[16,16,128]{2,1,0:T(8,128)(2,1)S(1)}, s16[16,16,128]{2,1,0:T(8,128)(2,1)S(1)}, u32[]{:S(2)}, u32[]{:S(2)}) collective-permute-start(s16[16,16,128]{2,1,0:T(8,128)(2,1)S(1)} %get-tuple-element.58), channel_id=1, source_target_pairs={{0,12},{4,0},{8,4},{12,8},{1,13},{5,1},{9,5},{13,9},{2,14},{6,2},{... | collective-permute-start | bytes 196616 | tf_op jit(solution)/shard_map/ppermute | solution.py:581

commit v14 on v13

--- a/solution.py
+++ b/solution.py
@@ -104,8 +104,8 @@
     return value.astype(jnp.int32).astype(jnp.float32)
 
 
-def distances(windows):
-    return sorted(range(1, windows), key=lambda d: -d * (windows - d))
+def partners(windows):
+    return list(range(windows - 1, 0, -1))
 
 
 def pack_kernel(ways, windows, steps, nvar, levels, part, var_ref, traj_ref, *outs):
@@ -120,7 +120,7 @@
 
     for n, d in enumerate(ways):
         outs[n][outs[n].shape[0] - 1] = split
-        target = lax.rem(me + d, windows)
+        target = me ^ d
 
         def variable(v, carry, n=n, target=target):
             for lev in range(levels):
@@ -189,7 +189,7 @@
     for d in range(windows):
         split = pieces[d][pieces[d].shape[0] - 1].astype(jnp.float32)
         here = split + pltpu.roll(split, HALF, 0) + pltpu.roll(split, LANES // 2, 1)
-        total = total + jnp.where(lax.rem(me - d + windows, windows) <= me, here, 0.0)
+        total = total + jnp.where((me ^ d) <= me, here, 0.0)
     for v in range(nvar):
         for lev in range(levels):
             one = total[lev : lev + 1, v : v + 1]
@@ -242,8 +242,7 @@
     count = stack_ref.shape[1]
     packed_tiles = count // (nvar * levels)
     for d in range(windows):
-        source = lax.rem(me - d + windows, windows)
-        stack_ref[source] = pieces[d][:count]
+        stack_ref[me ^ d] = pieces[d][:count]
 
     pairs = levels // 2
     base, _ = far_base(steps, nvar, levels)
@@ -535,8 +534,8 @@
         first, second = coded[0][kind], coded[1][kind]
         for n, (a, b) in enumerate(zip(first[0] + [first[1]], second[0] + [second[1]])):
             q_ref[kind, n] = shorts(jnp.concatenate([a, b], 0))
-    for ref, d in zip(payload_refs, distances(windows)):
-        ref[...] = q_ref[jnp.where(me + d >= windows, 0, 1)]
+    for ref, d in zip(payload_refs, partners(windows)):
+        ref[...] = q_ref[jnp.where((me ^ d) < me, 0, 1)]
 
 
 def final_kernel(windows, nvar, levels, tiles, *refs):
@@ -550,9 +549,9 @@
     for i in range(pairs):
         tails = [None] * (nvar * tiles)
         heads = [None] * (nvar * tiles)
-        for n, d in enumerate(distances(windows)):
+        for n, d in enumerate(partners(windows)):
             piece = pieces[i * (windows - 1) + n]
-            later = d > me
+            later = (me ^ d) > me
             scales = jnp.exp2(floats(piece[nvar * tiles])) * (1.0 / CODE_MAX)
             for v in range(nvar):
                 scale = scales[:, v : v + 1]
@@ -575,10 +574,13 @@
                     )
 
 
-def moved(block, axis, distance, around=False):
-    count = lax.axis_size(axis)
-    route = [(i, (i + distance) % count) for i in range(count) if around or 0 <= i + distance < count]
-    return lax.ppermute(block, axis, route)
+def moved(block, axis, distance):
+    devices = range(lax.axis_size(axis))
+    return lax.ppermute(block, axis, [(i, i + distance) for i in devices if i + distance in devices])
+
+
+def exchanged(block, axis, mask):
+    return lax.ppermute(block, axis, [(i, i ^ mask) for i in range(lax.axis_size(axis))])
 
 
 def swaps(axis, first):
@@ -610,6 +612,7 @@
     tiles = columns // LANES
     assert trajectory.shape[0] == windows and windows > 1 and rows == SUB and steps == HALF
     assert columns == tiles * LANES == windows * part and levels % 4 == 0
+    assert windows & (windows - 1) == 0
     pairs = levels // 2
     wide = -(-steps * part // LANES) * LANES
     bf16, f32, i16 = jnp.bfloat16, jnp.float32, jnp.int16
@@ -629,12 +632,12 @@
             compiler_params=params(),
         )(variances, trajectory)
 
-    order = distances(windows)
+    order = partners(windows)
     groups = [[d] for d in order] if windows <= 4 else [order]
     blocks = {}
     for group in groups:
         blocks.update(zip(group, packed(group)))
-    arrived = {d: moved(blocks[d], "window", d, around=True) for d in order}
+    arrived = {d: exchanged(blocks[d], "window", d) for d in order}
     arrived[0] = packed([0])[0]
 
     payload = shape((pairs, nvar * tiles + 1, 2 * SUB, LANES), i16)
@@ -738,7 +741,7 @@
         base_duals.append(base_dual)
         base_incs.append(base_inc)
         sent += [
-            moved(piece, "window", d, around=True) for piece, d in zip(payloads, order)
+            exchanged(piece, "window", d) for piece, d in zip(payloads, order)
         ]
 
     new_dual_model, new_increment = pl.pallas_call(

time: 46.3 us -> 46 us (level)
  starting transfers between devices: 22.6 us -> 20 us
  waiting for transfers between devices: 11.1 us -> 13.5 us
    ppermute x11, starting transfers between devices: 21.1 us -> 18.5 us  [the longest x9 15.8 us: exchanged(): lax.ppermute(block, axis, [(i, i ^ mask) for i in range(lax.axis_size(axi...]
    ppermute x11, waiting for transfers between devices: 11.1 us -> 13.5 us  [the longest x9 12.2 us: exchanged(): lax.ppermute(block, axis, [(i, i ^ mask) for i in range(lax.axis_size(axi...]
where the time goes in v14:
time: 46 us; the launch traced here: 45.7 us
  starting transfers between devices  20 us (43%)
  waiting for transfers between devices  13.5 us (29%)
  Pallas kernels  8.81 us (19%)
  local copies, waits for them, and re-layouts  1.82 us (4%)
  between operations  1.57 us (3%)
    ppermute x9, starting transfers between devices, exchanged(): lax.ppermute(block, axis, [(i, i ^ mask) for i in range(lax.axis_size(axi...  15.8 us
    ppermute x9, waiting for transfers between devices, exchanged(): lax.ppermute(block, axis, [(i, i ^ mask) for i in range(lax.axis_size(axi...  12.2 us
    pallas_call x1, Pallas kernels, body(): pl.pallas_call(lambda *refs: tangent_kernel(spaces, steps, nvar, levels,...  2.82 us
    ppermute x2, starting transfers between devices, moved(): lax.ppermute(block, axis, [(i, i + distance) for i in devices if i + dist...  2.72 us
    pallas_call x2, Pallas kernels, body(): pl.pallas_call(lambda *refs, i=i: adjoint_kernel(i, windows, spaces, step...  2.32 us
    ppermute x4, starting transfers between devices, swapped(): return lax.ppermute(block, axis, swaps(axis, first))  1.49 us
    ppermute x2, waiting for transfers between devices, moved(): lax.ppermute(block, axis, [(i, i + distance) for i in devices if i + dist...  1.28 us
    unnamed x18, local copies, waits for them, and re-layouts  1.12 us
  transfers between devices with their start and end apart: 15, of which 4 were waited for; matrix products, arithmetic and copies ran while one was open for 0% of the time, Pallas kernels for 17%

profile of v14, /device:TPU:0, one launch (start us, length us, event | category | flops | bytes accessed | tf_op | source)
XLA Modules:
  0.0 45.7 jit_solution(8488705413164399477)
XLA Ops:
  0.7 0.7 %pad.4.refs_0_ = f32[8,128]{1,0:T(8,128)S(1)} pad(f32[4,5]{1,0:T(4,128)} %bitcast.3, f32[]{:T(128)} %constant.2.clone.1), padding=0_4x0_123 | pad | bytes 4180 | tf_op jit(solution)/shard_map/jit(_pad)/pad | solution.py:624
  1.4 1.1 %copy-done = bf16[4,4,5,4,8,96]{5,4,3,2,1,0:T(8,128)(2,1)S(1)} copy-done((bf16[4,4,5,4,8,96]{5,4,3,2,1,0:T(8,128)(2,1)S(1)}, bf16[4,4,5,4,8,96]{5,4,3,2,1,0:T(8,128)(2,1)}, u32[]{:S(2)}) %copy-start) | copy-done | bytes 491544
  2.5 0.1 shard_map.123
  2.6 3.1 %collective-permute-start = (bf16[61,8,128]{2,1,0:T(8,128)(2,1)S(1)}, bf16[61,8,128]{2,1,0:T(8,128)(2,1)S(1)}, u32[]{:S(2)}, u32[]{:S(2)}) collective-permute-start(bf16[61,8,128]{2,1,0:T(8,128)(2,1)S(1)} %shard_map.123), channel_id=1, source_target_pairs={{0,4},{4,0},{8,12},{12,8},{1,5},{5,1},{9,13},{13,9},{2,6},{6,2},{1... | collective-permute-start | bytes 374792 | tf_op jit(solution)/shard_map/ppermute | solution.py:583
  5.7 0.1 shard_map.124
  5.8 2.7 %collective-permute-start.1 = (bf16[61,8,128]{2,1,0:T(8,128)(2,1)S(1)}, bf16[61,8,128]{2,1,0:T(8,128)(2,1)S(1)}, u32[]{:S(2)}, u32[]{:S(2)}) collective-permute-start(bf16[61,8,128]{2,1,0:T(8,128)(2,1)S(1)} %shard_map.124), channel_id=1, source_target_pairs={{0,8},{4,12},{8,0},{12,4},{1,9},{5,13},{9,1},{13,5},{2,10},{6,14},... | collective-permute-start | bytes 374792 | tf_op jit(solution)/shard_map/ppermute | solution.py:583
  8.4 0.1 shard_map.125
  8.6 0.1 collective-permute-start.2
  8.7 0.5 %shard_map.126 = (s16[2,21,16,128]{3,2,1,0:T(8,128)(2,1)S(1)}, s16[2,21,16,128]{3,2,1,0:T(8,128)(2,1)S(1)}, s16[2,16,16,128]{3,2,1,0:T(8,128)(2,1)S(1)}) custom-call(f32[1,5,4,8,384]{4,3,2,1,0:T(8,128)S(1)} %copy-done.4, f32[1,5,4,8,384]{4,3,2,1,0:T(8,128)S(1)} %copy-done.2, f32[1,4,4,8,384]{4,3,2,1,0:T(8,128)S(1)} %copy-done.3), custom_call_target="tpu_custom_call" | custom-call | tf_op jit(solution)/shard_map/pallas_call | solution.py:648
  9.2 0.7 %collective-permute-start.4 = (s16[2,21,16,128]{3,2,1,0:T(8,128)(2,1)S(1)}, s16[2,21,16,128]{3,2,1,0:T(8,128)(2,1)S(1)}, u32[]{:S(2)}, u32[]{:S(2)}) collective-permute-start(s16[2,21,16,128]{3,2,1,0:T(8,128)(2,1)S(1)} %get-tuple-element.37), channel_id=1, source_target_pairs={{1,2},{2,1},{5,6},{6,5},{9,10},{10,9},{13,14},{14,13},{17,18},{18,... | collective-permute-start | bytes 516104 | tf_op jit(solution)/shard_map/ppermute | solution.py:594
  9.9 0.1 shard_map.122.refs_0_
  10.7 0.7 %shard_map.121 = (f32[4,4,3,8,128]{4,3,2,1,0:T(8,128)S(1)}, f32[4,4,8,128]{3,2,1,0:T(8,128)S(1)}, f32[5,5,8,128]{3,2,1,0:T(8,128)S(1)}) custom-call(s32[1]{0:T(128)S(6)} %copy.13.refs_0_, f32[1,4,4]{2,1,0:T(4,128)S(1)} %copy-done.8, f32[5,5]{1,0:T(8,128)S(1)} %copy-done.7, f32[1,4,4,8,384]{4,3,2,1,0:T(8,128)S(1)} %copy-done.3, f32[1,4,4,8,384]{4,3,2,1,0:T(8,128)S(1)} %copy-done.6), custom_call_target="tpu_custom_call" | custom-call | tf_op jit(solution)/shard_map/pallas_call | solution.py:668
  11.4 6.9 %collective-permute-done.1.refs_2_ = bf16[61,8,128]{2,1,0:T(8,128)(2,1)S(1)} collective-permute-done((bf16[61,8,128]{2,1,0:T(8,128)(2,1)S(1)}, bf16[61,8,128]{2,1,0:T(8,128)(2,1)S(1)}, u32[]{:S(2)}, u32[]{:S(2)}) %collective-permute-start.1) | collective-permute-done | bytes 124960 | tf_op jit(solution)/shard_map/ppermute | solution.py:583
  18.3 0.4 shard_map.128
  18.8 0.7 %collective-permute-start.6 = (bf16[31,8,384]{2,1,0:T(8,128)(2,1)S(1)}, bf16[31,8,384]{2,1,0:T(8,128)(2,1)S(1)}, u32[]{:S(2)}, u32[]{:S(2)}) collective-permute-start(bf16[31,8,384]{2,1,0:T(8,128)(2,1)S(1)} %get-tuple-element.43), channel_id=1, source_target_pairs={{1,2},{2,1},{5,6},{6,5},{9,10},{10,9},{13,14},{14,13},{17,18},{18,... | collective-permute-start | bytes 571400 | tf_op jit(solution)/shard_map/ppermute | solution.py:594
  19.5 0.3 shard_map.127
  19.8 1.4 %collective-permute-start.7 = (s16[2,16,16,128]{3,2,1,0:T(8,128)(2,1)S(1)}, s16[2,16,16,128]{3,2,1,0:T(8,128)(2,1)S(1)}, u32[]{:S(2)}, u32[]{:S(2)}) collective-permute-start(s16[2,16,16,128]{3,2,1,0:T(8,128)(2,1)S(1)} %get-tuple-element.45), channel_id=1, source_target_pairs={{4,0},{8,4},{12,8},{5,1},{9,5},{13,9},{6,2},{10,6},{14,10},{7,3},{... | collective-permute-start | bytes 393224 | tf_op jit(solution)/shard_map/ppermute | solution.py:579
  21.2 1.3 %collective-permute-start.11 = (s16[2,16,16,128]{3,2,1,0:T(8,128)(2,1)S(1)}, s16[2,16,16,128]{3,2,1,0:T(8,128)(2,1)S(1)}, u32[]{:S(2)}, u32[]{:S(2)}) collective-permute-start(s16[2,16,16,128]{3,2,1,0:T(8,128)(2,1)S(1)} %get-tuple-element.52), channel_id=1, source_target_pairs={{4,0},{8,4},{12,8},{5,1},{9,5},{13,9},{6,2},{10,6},{14,10},{7,3},{... | collective-permute-start | bytes 393224 | tf_op jit(solution)/shard_map/ppermute | solution.py:579
  22.5 0.1 shard_map.129.refs_6_
  22.7 2.8 %shard_map.130 = (f32[1,4,4,8,384]{4,3,2,1,0:T(8,128)}, f32[4,5,3,8,128]{4,3,2,1,0:T(8,128)S(1)}, f32[4,4,5,3,16,128]{5,4,3,2,1,0:T(8,128)S(1)}) custom-call(f32[5,5,8,128]{3,2,1,0:T(8,128)S(1)} %get-tuple-element.34.refs_4_.refs_0_, f32[4,4,8,128]{3,2,1,0:T(8,128)S(1)} %get-tuple-element.39.refs_1_, f32[4,4,3,8,128]{4,3,2,1,0:T(8,128)S(1)} %get-tuple-element.40.refs_2_, ...), custom_call_target="tpu_custom_call" | custom-call | tf_op jit(solution)/shard_map/pallas_call | solution.py:701
  25.5 1.3 %collective-permute-done.7.refs_4_ = s16[2,16,16,128]{3,2,1,0:T(8,128)(2,1)S(1)} collective-permute-done((s16[2,16,16,128]{3,2,1,0:T(8,128)(2,1)S(1)}, s16[2,16,16,128]{3,2,1,0:T(8,128)(2,1)S(1)}, u32[]{:S(2)}, u32[]{:S(2)}) %collective-permute-start.7) | collective-permute-done | bytes 131104 | tf_op jit(solution)/shard_map/ppermute | solution.py:579
  26.8 0.1 shard_map.131
  26.9 1.2 %shard_map.132 = (f32[5,2,8,384]{3,2,1,0:T(8,128)S(1)}, f32[5,2,8,384]{3,2,1,0:T(8,128)S(1)}, s16[16,16,128]{2,1,0:T(8,128)(2,1)S(1)}, s16[16,16,128]{2,1,0:T(8,128)(2,1)S(1)}, s16[16,16,128]{2,1,0:T(8,128)(2,1)S(1)}) custom-call(f32[5,5,8,128]{3,2,1,0:T(8,128)S(1)} %get-tuple-element.34.refs_4_.refs_0_, ...), custom_call_target="tpu_custom_call" | custom-call | tf_op jit(solution)/shard_map/pallas_call | solution.py:726
  28.1 4.9 %collective-permute-start.8 = (s16[16,16,128]{2,1,0:T(8,128)(2,1)S(1)}, s16[16,16,128]{2,1,0:T(8,128)(2,1)S(1)}, u32[]{:S(2)}, u32[]{:S(2)}) collective-permute-start(s16[16,16,128]{2,1,0:T(8,128)(2,1)S(1)} %get-tuple-element.49), channel_id=1, source_target_pairs={{0,12},{4,8},{8,4},{12,0},{1,13},{5,9},{9,5},{13,1},{2,14},{6,10},... | collective-permute-start | bytes 196616 | tf_op jit(solution)/shard_map/ppermute | solution.py:583
  32.9 0.6 %collective-permute-start.10 = (s16[16,16,128]{2,1,0:T(8,128)(2,1)S(1)}, s16[16,16,128]{2,1,0:T(8,128)(2,1)S(1)}, u32[]{:S(2)}, u32[]{:S(2)}) collective-permute-start(s16[16,16,128]{2,1,0:T(8,128)(2,1)S(1)} %get-tuple-element.51), channel_id=1, source_target_pairs={{0,4},{4,0},{8,12},{12,8},{1,5},{5,1},{9,13},{13,9},{2,6},{6,2},{1... | collective-permute-start | bytes 196616 | tf_op jit(solution)/shard_map/ppermute | solution.py:583
  33.6 0.1 shard_map.133
  33.7 1.2 %shard_map.134 = (f32[5,2,8,384]{3,2,1,0:T(8,128)S(1)}, f32[5,2,8,384]{3,2,1,0:T(8,128)S(1)}, s16[16,16,128]{2,1,0:T(8,128)(2,1)S(1)}, s16[16,16,128]{2,1,0:T(8,128)(2,1)S(1)}, s16[16,16,128]{2,1,0:T(8,128)(2,1)S(1)}) custom-call(f32[5,5,8,128]{3,2,1,0:T(8,128)S(1)} %get-tuple-element.34.refs_4_.refs_0_, ...), custom_call_target="tpu_custom_call" | custom-call | tf_op jit(solution)/shard_map/pallas_call | solution.py:726
  34.9 3.8 %collective-permute-start.12 = (s16[16,16,128]{2,1,0:T(8,128)(2,1)S(1)}, s16[16,16,128]{2,1,0:T(8,128)(2,1)S(1)}, u32[]{:S(2)}, u32[]{:S(2)}) collective-permute-start(s16[16,16,128]{2,1,0:T(8,128)(2,1)S(1)} %get-tuple-element.56), channel_id=1, source_target_pairs={{0,12},{4,8},{8,4},{12,0},{1,13},{5,9},{9,5},{13,1},{2,14},{6,10},... | collective-permute-start | bytes 196616 | tf_op jit(solution)/shard_map/ppermute | solution.py:583
  38.7 0.6 %collective-permute-start.14 = (s16[16,16,128]{2,1,0:T(8,128)(2,1)S(1)}, s16[16,16,128]{2,1,0:T(8,128)(2,1)S(1)}, u32[]{:S(2)}, u32[]{:S(2)}) collective-permute-start(s16[16,16,128]{2,1,0:T(8,128)(2,1)S(1)} %get-tuple-element.58), channel_id=1, source_target_pairs={{0,4},{4,0},{8,12},{12,8},{1,5},{5,1},{9,13},{13,9},{2,6},{6,2},{1... | collective-permute-start | bytes 196616 | tf_op jit(solution)/shard_map/ppermute | solution.py:583
  39.3 1.8 %collective-permute-done.12.refs_3_ = s16[16,16,128]{2,1,0:T(8,128)(2,1)S(1)} collective-permute-done((s16[16,16,128]{2,1,0:T(8,128)(2,1)S(1)}, s16[16,16,128]{2,1,0:T(8,128)(2,1)S(1)}, u32[]{:S(2)}, u32[]{:S(2)}) %collective-permute-start.12) | collective-permute-done | bytes 65568 | tf_op jit(solution)/shard_map/ppermute | solution.py:583
  41.1 3.6 %collective-permute-done.13.refs_4_ = s16[16,16,128]{2,1,0:T(8,128)(2,1)S(1)} collective-permute-done((s16[16,16,128]{2,1,0:T(8,128)(2,1)S(1)}, s16[16,16,128]{2,1,0:T(8,128)(2,1)S(1)}, u32[]{:S(2)}, u32[]{:S(2)}) %collective-permute-start.13) | collective-permute-done | bytes 65568 | tf_op jit(solution)/shard_map/ppermute | solution.py:583
  44.7 1.0 %shard_map.135 = (f32[1,5,4,8,384]{4,3,2,1,0:T(8,128)}, f32[1,5,4,8,384]{4,3,2,1,0:T(8,128)}) custom-call(s16[16,16,128]{2,1,0:T(8,128)(2,1)S(1)} %collective-permute-done.8.refs_0_, s16[16,16,128]{2,1,0:T(8,128)(2,1)S(1)} %collective-permute-done.9.refs_1_, s16[16,16,128]{2,1,0:T(8,128)(2,1)S(1)} %collective-permute-done.10.refs_2_, ...), custom_call_target="tpu_custom_call" | custom-call | tf_op jit(solution)/shard_map/pallas_call | solution.py:747
  (32 shorter events, 0.2 us)
Async XLA Ops:
  0.6 10.1 %copy-start.8 = (f32[1,4,4]{2,1,0:T(4,128)S(1)}, f32[1,4,4]{2,1,0:T(4,128)}, u32[]{:S(2)}) copy-start(f32[1,4,4]{2,1,0:T(4,128)} %refs_1_.6) | copy-start | bytes 196
  0.6 10.1 %copy-start.7 = (f32[5,5]{1,0:T(8,128)S(1)}, f32[5,5]{1,0:T(8,128)}, u32[]{:S(2)}) copy-start(f32[5,5]{1,0:T(8,128)} %refs_2_.3) | copy-start | bytes 304
  1.3 1.1 %copy-start = (bf16[4,4,5,4,8,96]{5,4,3,2,1,0:T(8,128)(2,1)S(1)}, bf16[4,4,5,4,8,96]{5,4,3,2,1,0:T(8,128)(2,1)}, u32[]{:S(2)}) copy-start(bf16[4,4,5,4,8,96]{5,4,3,2,1,0:T(8,128)(2,1)} %refs_1_.10) | copy-start | bytes 1474564
  2.4 6.2 %copy-start.2 = (f32[1,5,4,8,384]{4,3,2,1,0:T(8,128)S(1)}, f32[1,5,4,8,384]{4,3,2,1,0:T(8,128)}, u32[]{:S(2)}) copy-start(f32[1,5,4,8,384]{4,3,2,1,0:T(8,128)} %refs_6_.3) | copy-start | bytes 737284
  2.4 6.2 %copy-start.3 = (f32[1,4,4,8,384]{4,3,2,1,0:T(8,128)S(1)}, f32[1,4,4,8,384]{4,3,2,1,0:T(8,128)}, u32[]{:S(2)}) copy-start(f32[1,4,4,8,384]{4,3,2,1,0:T(8,128)} %refs_3_.5) | copy-start | bytes 589828
  2.4 6.2 %copy-start.4 = (f32[1,5,4,8,384]{4,3,2,1,0:T(8,128)S(1)}, f32[1,5,4,8,384]{4,3,2,1,0:T(8,128)}, u32[]{:S(2)}) copy-start(f32[1,5,4,8,384]{4,3,2,1,0:T(8,128)} %refs_8_.3) | copy-start | bytes 737284
  2.4 7.5 %copy-start.1 = (bf16[4,4,5,4,8,96]{5,4,3,2,1,0:T(8,128)(2,1)S(1)}, bf16[4,4,5,4,8,96]{5,4,3,2,1,0:T(8,128)(2,1)}, u32[]{:S(2)}) copy-start(bf16[4,4,5,4,8,96]{5,4,3,2,1,0:T(8,128)(2,1)} %refs_1_.10) | copy-start | bytes 1474564
  2.4 8.3 %copy-start.6 = (f32[1,4,4,8,384]{4,3,2,1,0:T(8,128)S(1)}, f32[1,4,4,8,384]{4,3,2,1,0:T(8,128)}, u32[]{:S(2)}) copy-start(f32[1,4,4,8,384]{4,3,2,1,0:T(8,128)} %refs_4_.1) | copy-start | bytes 589828
  2.6 8.8 %collective-permute-start = (bf16[61,8,128]{2,1,0:T(8,128)(2,1)S(1)}, bf16[61,8,128]{2,1,0:T(8,128)(2,1)S(1)}, u32[]{:S(2)}, u32[]{:S(2)}) collective-permute-start(bf16[61,8,128]{2,1,0:T(8,128)(2,1)S(1)} %shard_map.123), channel_id=1, source_target_pairs={{0,4},{4,0},{8,12},{12,8},{1,5},{5,1},{9,13},{13,9},{2,6},{6,2},{1... | collective-permute-start | bytes 374792 | tf_op jit(solution)/shard_map/ppermute | solution.py:583
  5.8 12.5 %collective-permute-start.1 = (bf16[61,8,128]{2,1,0:T(8,128)(2,1)S(1)}, bf16[61,8,128]{2,1,0:T(8,128)(2,1)S(1)}, u32[]{:S(2)}, u32[]{:S(2)}) collective-permute-start(bf16[61,8,128]{2,1,0:T(8,128)(2,1)S(1)} %shard_map.124), channel_id=1, source_target_pairs={{0,8},{4,12},{8,0},{12,4},{1,9},{5,13},{9,1},{13,5},{2,10},{6,14},... | collective-permute-start | bytes 374792 | tf_op jit(solution)/shard_map/ppermute | solution.py:583
  8.6 9.7 %collective-permute-start.2 = (bf16[61,8,128]{2,1,0:T(8,128)(2,1)S(1)}, bf16[61,8,128]{2,1,0:T(8,128)(2,1)S(1)}, u32[]{:S(2)}, u32[]{:S(2)}) collective-permute-start(bf16[61,8,128]{2,1,0:T(8,128)(2,1)S(1)} %shard_map.125), channel_id=1, source_target_pairs={{0,12},{4,8},{8,4},{12,0},{1,13},{5,9},{9,5},{13,1},{2,14},{6,10},... | collective-permute-start | bytes 374792 | tf_op jit(solution)/shard_map/ppermute | solution.py:583
  9.1 10.3 %collective-permute-start.3 = (s16[2,21,16,128]{3,2,1,0:T(8,128)(2,1)S(1)}, s16[2,21,16,128]{3,2,1,0:T(8,128)(2,1)S(1)}, u32[]{:S(2)}, u32[]{:S(2)}) collective-permute-start(s16[2,21,16,128]{3,2,1,0:T(8,128)(2,1)S(1)} %get-tuple-element.36), channel_id=1, source_target_pairs={{0,1},{1,0},{2,3},{3,2},{4,5},{5,4},{6,7},{7,6},{8,9},{9,8},{10,11... | collective-permute-start | bytes 516104 | tf_op jit(solution)/shard_map/ppermute | solution.py:594
  9.2 10.3 %collective-permute-start.4 = (s16[2,21,16,128]{3,2,1,0:T(8,128)(2,1)S(1)}, s16[2,21,16,128]{3,2,1,0:T(8,128)(2,1)S(1)}, u32[]{:S(2)}, u32[]{:S(2)}) collective-permute-start(s16[2,21,16,128]{3,2,1,0:T(8,128)(2,1)S(1)} %get-tuple-element.37), channel_id=1, source_target_pairs={{1,2},{2,1},{5,6},{6,5},{9,10},{10,9},{13,14},{14,13},{17,18},{18,... | collective-permute-start | bytes 516104 | tf_op jit(solution)/shard_map/ppermute | solution.py:594
  18.7 3.9 %collective-permute-start.5 = (bf16[4,10,8,384]{3,2,1,0:T(8,128)(2,1)S(1)}, bf16[4,10,8,384]{3,2,1,0:T(8,128)(2,1)S(1)}, u32[]{:S(2)}, u32[]{:S(2)}) collective-permute-start(bf16[4,10,8,384]{3,2,1,0:T(8,128)(2,1)S(1)} %get-tuple-element.42), channel_id=1, source_target_pairs={{0,1},{1,0},{2,3},{3,2},{4,5},{5,4},{6,7},{7,6},{8,9},{9,8},{10,11... | collective-permute-start | bytes 737288 | tf_op jit(solution)/shard_map/ppermute | solution.py:594
  18.8 3.9 %collective-permute-start.6 = (bf16[31,8,384]{2,1,0:T(8,128)(2,1)S(1)}, bf16[31,8,384]{2,1,0:T(8,128)(2,1)S(1)}, u32[]{:S(2)}, u32[]{:S(2)}) collective-permute-start(bf16[31,8,384]{2,1,0:T(8,128)(2,1)S(1)} %get-tuple-element.43), channel_id=1, source_target_pairs={{1,2},{2,1},{5,6},{6,5},{9,10},{10,9},{13,14},{14,13},{17,18},{18,... | collective-permute-start | bytes 571400 | tf_op jit(solution)/shard_map/ppermute | solution.py:594
  19.8 7.1 %copy-start.5 = (f32[1,5,4,8,384]{4,3,2,1,0:T(8,128)S(1)}, f32[1,5,4,8,384]{4,3,2,1,0:T(8,128)}, u32[]{:S(2)}) copy-start(f32[1,5,4,8,384]{4,3,2,1,0:T(8,128)} %refs_7_.3) | copy-start | bytes 737284
  19.8 7.0 %collective-permute-start.7 = (s16[2,16,16,128]{3,2,1,0:T(8,128)(2,1)S(1)}, s16[2,16,16,128]{3,2,1,0:T(8,128)(2,1)S(1)}, u32[]{:S(2)}, u32[]{:S(2)}) collective-permute-start(s16[2,16,16,128]{3,2,1,0:T(8,128)(2,1)S(1)} %get-tuple-element.45), channel_id=1, source_target_pairs={{4,0},{8,4},{12,8},{5,1},{9,5},{13,9},{6,2},{10,6},{14,10},{7,3},{... | collective-permute-start | bytes 393224 | tf_op jit(solution)/shard_map/ppermute | solution.py:579
  21.2 12.4 %collective-permute-start.11 = (s16[2,16,16,128]{3,2,1,0:T(8,128)(2,1)S(1)}, s16[2,16,16,128]{3,2,1,0:T(8,128)(2,1)S(1)}, u32[]{:S(2)}, u32[]{:S(2)}) collective-permute-start(s16[2,16,16,128]{3,2,1,0:T(8,128)(2,1)S(1)} %get-tuple-element.52), channel_id=1, source_target_pairs={{4,0},{8,4},{12,8},{5,1},{9,5},{13,9},{6,2},{10,6},{14,10},{7,3},{... | collective-permute-start | bytes 393224 | tf_op jit(solution)/shard_map/ppermute | solution.py:579
  28.1 10.6 %collective-permute-start.8 = (s16[16,16,128]{2,1,0:T(8,128)(2,1)S(1)}, s16[16,16,128]{2,1,0:T(8,128)(2,1)S(1)}, u32[]{:S(2)}, u32[]{:S(2)}) collective-permute-start(s16[16,16,128]{2,1,0:T(8,128)(2,1)S(1)} %get-tuple-element.49), channel_id=1, source_target_pairs={{0,12},{4,8},{8,4},{12,0},{1,13},{5,9},{9,5},{13,1},{2,14},{6,10},... | collective-permute-start | bytes 196616 | tf_op jit(solution)/shard_map/ppermute | solution.py:583
  32.9 6.4 %collective-permute-start.9 = (s16[16,16,128]{2,1,0:T(8,128)(2,1)S(1)}, s16[16,16,128]{2,1,0:T(8,128)(2,1)S(1)}, u32[]{:S(2)}, u32[]{:S(2)}) collective-permute-start(s16[16,16,128]{2,1,0:T(8,128)(2,1)S(1)} %get-tuple-element.50), channel_id=1, source_target_pairs={{0,8},{4,12},{8,0},{12,4},{1,9},{5,13},{9,1},{13,5},{2,10},{6,14},... | collective-permute-start | bytes 196616 | tf_op jit(solution)/shard_map/ppermute | solution.py:583
  32.9 6.4 %collective-permute-start.10 = (s16[16,16,128]{2,1,0:T(8,128)(2,1)S(1)}, s16[16,16,128]{2,1,0:T(8,128)(2,1)S(1)}, u32[]{:S(2)}, u32[]{:S(2)}) collective-permute-start(s16[16,16,128]{2,1,0:T(8,128)(2,1)S(1)} %get-tuple-element.51), channel_id=1, source_target_pairs={{0,4},{4,0},{8,12},{12,8},{1,5},{5,1},{9,13},{13,9},{2,6},{6,2},{1... | collective-permute-start | bytes 196616 | tf_op jit(solution)/shard_map/ppermute | solution.py:583
  34.9 6.2 %collective-permute-start.12 = (s16[16,16,128]{2,1,0:T(8,128)(2,1)S(1)}, s16[16,16,128]{2,1,0:T(8,128)(2,1)S(1)}, u32[]{:S(2)}, u32[]{:S(2)}) collective-permute-start(s16[16,16,128]{2,1,0:T(8,128)(2,1)S(1)} %get-tuple-element.56), channel_id=1, source_target_pairs={{0,12},{4,8},{8,4},{12,0},{1,13},{5,9},{9,5},{13,1},{2,14},{6,10},... | collective-permute-start | bytes 196616 | tf_op jit(solution)/shard_map/ppermute | solution.py:583
  38.7 6.0 %collective-permute-start.13 = (s16[16,16,128]{2,1,0:T(8,128)(2,1)S(1)}, s16[16,16,128]{2,1,0:T(8,128)(2,1)S(1)}, u32[]{:S(2)}, u32[]{:S(2)}) collective-permute-start(s16[16,16,128]{2,1,0:T(8,128)(2,1)S(1)} %get-tuple-element.57), channel_id=1, source_target_pairs={{0,8},{4,12},{8,0},{12,4},{1,9},{5,13},{9,1},{13,5},{2,10},{6,14},... | collective-permute-start | bytes 196616 | tf_op jit(solution)/shard_map/ppermute | solution.py:583
  38.7 6.0 %collective-permute-start.14 = (s16[16,16,128]{2,1,0:T(8,128)(2,1)S(1)}, s16[16,16,128]{2,1,0:T(8,128)(2,1)S(1)}, u32[]{:S(2)}, u32[]{:S(2)}) collective-permute-start(s16[16,16,128]{2,1,0:T(8,128)(2,1)S(1)} %get-tuple-element.58), channel_id=1, source_target_pairs={{0,4},{4,0},{8,12},{12,8},{1,5},{5,1},{9,13},{13,9},{2,6},{6,2},{1... | collective-permute-start | bytes 196616 | tf_op jit(solution)/shard_map/ppermute | solution.py:583

commit v15 on v14

--- a/solution.py
+++ b/solution.py
@@ -215,7 +215,7 @@
     return 0 < j < steps - 1 and not (v == 0 and j + 1 > HALF // 2)
 
 
-def far_base(steps, nvar, levels):
+def edge_base(steps, nvar, levels):
     base, total = {}, 0
     for j in range(steps):
         for v in range(nvar):
@@ -244,8 +244,7 @@
     for d in range(windows):
         stack_ref[me ^ d] = pieces[d][:count]
 
-    pairs = levels // 2
-    base, _ = far_base(steps, nvar, levels)
+    base, _ = edge_base(steps, nvar, levels)
 
     def variable(v):
         built = {}
@@ -264,18 +263,20 @@
                 built[j, lev] = place(parts, rolled, lane)
                 own_ref[j, plane] = jnp.concatenate(built[j, lev], 1).astype(jnp.bfloat16)
         for j in range(steps):
-            for i in range(pairs):
-                halves = [joined_halves(a, b) for a, b in zip(built[j, 2 * i], built[j, 2 * i + 1])]
-                last, start = (jnp.concatenate([h[k] for h in halves], 1) for k in range(2))
-                near_ref[j, v * pairs + i] = jnp.where(even, last, start).astype(jnp.bfloat16)
-                if not is_quarter(j, v, steps):
-                    far_ref[base[j, v] + i] = jnp.where(even, start, last).astype(jnp.bfloat16)
             if is_quarter(j, v, steps):
-                for q in range(levels // 4):
-                    four = zip(*[built[j, 4 * q + n] for n in range(4)])
-                    ends = [joined_quarters(tiles) for tiles in four]
-                    last, start = (jnp.concatenate([e[k] for e in ends], 1) for k in range(2))
-                    far_ref[base[j, v] + q] = jnp.where(even, start, last).astype(jnp.bfloat16)
+                groups = [
+                    [joined_quarters(four) for four in zip(*[built[j, 4 * q + n] for n in range(4)])]
+                    for q in range(levels // 4)
+                ]
+            else:
+                groups = [
+                    [joined_halves(a, b) for a, b in zip(built[j, 2 * i], built[j, 2 * i + 1])]
+                    for i in range(levels // 2)
+                ]
+            for n, group in enumerate(groups):
+                last, start = (jnp.concatenate([e[k] for e in group], 1) for k in range(2))
+                near_ref[base[j, v] + n] = jnp.where(even, last, start).astype(jnp.bfloat16)
+                far_ref[base[j, v] + n] = jnp.where(even, start, last).astype(jnp.bfloat16)
 
     for v in range(nvar):
         variable(v)
@@ -380,7 +381,7 @@
 
 def tangent_kernel(
     spaces, steps, nvar, levels, tiles,
-    mix_ref, share_ref, obs_ref, own_ref, near_ref, far_ref, first_ref,
+    mix_ref, share_ref, obs_ref, own_ref, far_ref, near_ref, first_ref,
     ndo_ref, ends_ref, x_ref, s_ref,
 ):
     lane, row = lane_index(), row_index()
@@ -389,30 +390,27 @@
     walled = walls(spaces)
     pairs = levels // 2
     cuts = [slice(t * LANES, (t + 1) * LANES) for t in range(tiles)]
-    base, _ = far_base(steps, nvar, levels)
+    base, _ = edge_base(steps, nvar, levels)
 
     for lev in range(levels):
-        i, odd = lev // 2, lev % 2
+        odd = lev % 2
         for j in range(steps):
             for v in range(nvar):
                 for t in range(tiles):
                     own = own_ref[j, v * levels + lev, :, cuts[t]].astype(jnp.float32)
-                    near = near_ref[j, v * pairs + i, :, cuts[t]].astype(jnp.float32)
                     quarter = is_quarter(j, v, steps)
-                    far = far_ref[base[j, v] + lev // (4 if quarter else 2), :, cuts[t]]
-                    far = far.astype(jnp.float32)
+                    tile = base[j, v] + lev // (4 if quarter else 2)
+                    near = near_ref[tile, :, cuts[t]].astype(jnp.float32)
+                    far = far_ref[tile, :, cuts[t]].astype(jnp.float32)
+                    low, high = jnp.where(even, far, near), jnp.where(even, near, far)
                     if quarter:
                         slot = 2 * (lev % 4)
-                        low_far = pltpu.roll(far, (HALF - 2 - slot) % SUB, 0)
-                        high_far = pltpu.roll(far, (HALF - slot) % SUB, 0)
+                        low = pltpu.roll(low, (HALF - 2 - slot) % SUB, 0)
+                        high = pltpu.roll(high, (HALF - slot) % SUB, 0)
                     else:
-                        low_far = pltpu.roll(far, HALF, 0) if odd else far
-                        high_far = far if odd else pltpu.roll(far, HALF, 0)
-                    low_near = pltpu.roll(near, HALF, 0) if odd else near
-                    high_near = near if odd else pltpu.roll(near, HALF, 0)
+                        low = pltpu.roll(low, HALF, 0) if odd else low
+                        high = high if odd else pltpu.roll(high, HALF, 0)
                     turned = pltpu.roll(own, HALF, 0)
-                    low = jnp.where(even, low_far, low_near)
-                    high = jnp.where(even, high_near, high_far)
                     x_ref[lev, j, v, t, :SUB, :] = jnp.where(top, low, turned)
                     x_ref[lev, j, v, t, SUB:, :] = jnp.where(top, turned, high)
 
@@ -681,15 +679,15 @@
         lambda *refs: assemble_kernel(windows, steps, nvar, levels, part, *refs),
         out_shape=[
             shape((steps, nvar * levels, rows, columns), bf16),
-            shape((steps, nvar * pairs, rows, columns), bf16),
-            shape((far_base(steps, nvar, levels)[1], rows, columns), bf16),
+            shape((edge_base(steps, nvar, levels)[1], rows, columns), bf16),
+            shape((edge_base(steps, nvar, levels)[1], rows, columns), bf16),
         ],
         in_specs=[VMEM] * windows + [ANY],
         out_specs=[VMEM] * 3,
         scratch_shapes=[pltpu.VMEM((windows, block.shape[0] - 1, rows, LANES), bf16)],
         compiler_params=params(),
     )(*blocks_here, mix)
-    traj_near, traj_far = swapped(traj_near, "space", 0), swapped(traj_far, "space", 1)
+    traj_far, traj_near = swapped(traj_far, "space", 1), swapped(traj_near, "space", 0)
 
     first = pl.pallas_call(
         lambda *refs: prepare_tangent_kernel(nvar, levels, tiles, *refs),
@@ -709,7 +707,7 @@
         out_specs=[VMEM] * 3,
         scratch_shapes=[pltpu.VMEM((2, 2, nvar, tiles, 4 * SUB, LANES), f32)],
         compiler_params=params(),
-    )(mix, share, obs, own, traj_near, traj_far, first)
+    )(mix, share, obs, own, traj_far, traj_near, first)
 
     state = shape((nvar, 2, rows, columns), f32)
     coded = shape((nvar * tiles + 1, 2 * SUB, LANES), i16)

time: 46 us -> 48.3 us (1.050)
  starting transfers between devices: 20 us -> 21.8 us
  waiting for transfers between devices: 13.5 us -> 14.2 us
    ppermute x4, starting transfers between devices: 1.49 us -> 4.32 us  [swapped(): return lax.ppermute(block, axis, swaps(axis, first))]
    ppermute x2, waiting for transfers between devices: 1.28 us -> 2.69 us  [moved(): lax.ppermute(block, axis, [(i, i + distance) for i in devices if i + dist...]
    ppermute x9, starting transfers between devices: 15.8 us -> 14.7 us  [exchanged(): lax.ppermute(block, axis, [(i, i ^ mask) for i in range(lax.axis_size(axi...]
    ppermute x9, waiting for transfers between devices: 12.2 us -> 11.5 us  [exchanged(): lax.ppermute(block, axis, [(i, i ^ mask) for i in range(lax.axis_size(axi...]
  transfers between devices with their start and end apart: 15 -> 15, of which waited for: 4 -> 4; matrix products, arithmetic and copies ran while one was open for 0% -> 0% of each run, Pallas kernels for 17% -> 16%
where the time goes in v15:
time: 48.3 us; the launch traced here: 48 us
  starting transfers between devices  21.8 us (45%)
  waiting for transfers between devices  14.2 us (29%)
  Pallas kernels  8.76 us (18%)
  local copies, waits for them, and re-layouts  1.82 us (4%)
  between operations  1.55 us (3%)
    ppermute x9, starting transfers between devices, exchanged(): lax.ppermute(block, axis, [(i, i ^ mask) for i in range(lax.axis_size(axi...  14.7 us
    ppermute x9, waiting for transfers between devices, exchanged(): lax.ppermute(block, axis, [(i, i ^ mask) for i in range(lax.axis_size(axi...  11.5 us
    ppermute x4, starting transfers between devices, swapped(): return lax.ppermute(block, axis, swaps(axis, first))  4.32 us
    pallas_call x1, Pallas kernels, body(): pl.pallas_call(lambda *refs: tangent_kernel(spaces, steps, nvar, levels,...  2.78 us
    ppermute x2, starting transfers between devices, moved(): lax.ppermute(block, axis, [(i, i + distance) for i in devices if i + dist...  2.72 us
    ppermute x2, waiting for transfers between devices, moved(): lax.ppermute(block, axis, [(i, i + distance) for i in devices if i + dist...  2.69 us
    pallas_call x2, Pallas kernels, body(): pl.pallas_call(lambda *refs, i=i: adjoint_kernel(i, windows, spaces, step...  2.33 us
    unnamed x18, local copies, waits for them, and re-layouts  1.12 us
  transfers between devices with their start and end apart: 15, of which 4 were waited for; matrix products, arithmetic and copies ran while one was open for 0% of the time, Pallas kernels for 16%

profile of v15, /device:TPU:0, one launch (start us, length us, event | category | flops | bytes accessed | tf_op | source)
XLA Modules:
  0.0 48.0 jit_solution(9924381192884140073)
XLA Ops:
  0.7 0.7 %pad.4.refs_0_ = f32[8,128]{1,0:T(8,128)S(1)} pad(f32[4,5]{1,0:T(4,128)} %bitcast.3, f32[]{:T(128)} %constant.2.clone.1), padding=0_4x0_123 | pad | bytes 4180 | tf_op jit(solution)/shard_map/jit(_pad)/pad | solution.py:622
  1.4 1.1 %copy-done = bf16[4,4,5,4,8,96]{5,4,3,2,1,0:T(8,128)(2,1)S(1)} copy-done((bf16[4,4,5,4,8,96]{5,4,3,2,1,0:T(8,128)(2,1)S(1)}, bf16[4,4,5,4,8,96]{5,4,3,2,1,0:T(8,128)(2,1)}, u32[]{:S(2)}) %copy-start) | copy-done | bytes 491544
  2.5 0.1 shard_map.123
  2.6 3.1 %collective-permute-start = (bf16[61,8,128]{2,1,0:T(8,128)(2,1)S(1)}, bf16[61,8,128]{2,1,0:T(8,128)(2,1)S(1)}, u32[]{:S(2)}, u32[]{:S(2)}) collective-permute-start(bf16[61,8,128]{2,1,0:T(8,128)(2,1)S(1)} %shard_map.123), channel_id=1, source_target_pairs={{0,4},{4,0},{8,12},{12,8},{1,5},{5,1},{9,13},{13,9},{2,6},{6,2},{1... | collective-permute-start | bytes 374792 | tf_op jit(solution)/shard_map/ppermute | solution.py:581
  5.7 0.1 shard_map.124
  5.8 2.7 %collective-permute-start.1 = (bf16[61,8,128]{2,1,0:T(8,128)(2,1)S(1)}, bf16[61,8,128]{2,1,0:T(8,128)(2,1)S(1)}, u32[]{:S(2)}, u32[]{:S(2)}) collective-permute-start(bf16[61,8,128]{2,1,0:T(8,128)(2,1)S(1)} %shard_map.124), channel_id=1, source_target_pairs={{0,8},{4,12},{8,0},{12,4},{1,9},{5,13},{9,1},{13,5},{2,10},{6,14},... | collective-permute-start | bytes 374792 | tf_op jit(solution)/shard_map/ppermute | solution.py:581
  8.4 0.1 shard_map.125
  8.7 0.5 shard_map.126
  9.2 0.7 %collective-permute-start.4 = (s16[2,21,16,128]{3,2,1,0:T(8,128)(2,1)S(1)}, s16[2,21,16,128]{3,2,1,0:T(8,128)(2,1)S(1)}, u32[]{:S(2)}, u32[]{:S(2)}) collective-permute-start(s16[2,21,16,128]{3,2,1,0:T(8,128)(2,1)S(1)} %get-tuple-element.37), channel_id=1, source_target_pairs={{1,2},{2,1},{5,6},{6,5},{9,10},{10,9},{13,14},{14,13},{17,18},{18,... | collective-permute-start | bytes 516104 | tf_op jit(solution)/shard_map/ppermute | solution.py:592
  9.9 0.1 shard_map.122.refs_0_
  10.7 0.7 %shard_map.121 = (f32[4,4,3,8,128]{4,3,2,1,0:T(8,128)S(1)}, f32[4,4,8,128]{3,2,1,0:T(8,128)S(1)}, f32[5,5,8,128]{3,2,1,0:T(8,128)S(1)}) custom-call(s32[1]{0:T(128)S(6)} %copy.13.refs_0_, f32[1,4,4]{2,1,0:T(4,128)S(1)} %copy-done.8, f32[5,5]{1,0:T(8,128)S(1)} %copy-done.7, f32[1,4,4,8,384]{4,3,2,1,0:T(8,128)S(1)} %copy-done.3, f32[1,4,4,8,384]{4,3,2,1,0:T(8,128)S(1)} %copy-done.6), custom_call_target="tpu_custom_call" | custom-call | tf_op jit(solution)/shard_map/pallas_call | solution.py:666
  11.4 6.9 %collective-permute-done.1.refs_2_ = bf16[61,8,128]{2,1,0:T(8,128)(2,1)S(1)} collective-permute-done((bf16[61,8,128]{2,1,0:T(8,128)(2,1)S(1)}, bf16[61,8,128]{2,1,0:T(8,128)(2,1)S(1)}, u32[]{:S(2)}, u32[]{:S(2)}) %collective-permute-start.1) | collective-permute-done | bytes 124960 | tf_op jit(solution)/shard_map/ppermute | solution.py:581
  18.3 0.4 shard_map.128
  18.7 0.7 %collective-permute-start.5 = (bf16[31,8,384]{2,1,0:T(8,128)(2,1)S(1)}, bf16[31,8,384]{2,1,0:T(8,128)(2,1)S(1)}, u32[]{:S(2)}, u32[]{:S(2)}) collective-permute-start(bf16[31,8,384]{2,1,0:T(8,128)(2,1)S(1)} %get-tuple-element.42), channel_id=1, source_target_pairs={{1,2},{2,1},{5,6},{6,5},{9,10},{10,9},{13,14},{14,13},{17,18},{18,... | collective-permute-start | bytes 571400 | tf_op jit(solution)/shard_map/ppermute | solution.py:592
  19.4 2.9 %collective-permute-start.6 = (bf16[31,8,384]{2,1,0:T(8,128)(2,1)S(1)}, bf16[31,8,384]{2,1,0:T(8,128)(2,1)S(1)}, u32[]{:S(2)}, u32[]{:S(2)}) collective-permute-start(bf16[31,8,384]{2,1,0:T(8,128)(2,1)S(1)} %get-tuple-element.43), channel_id=1, source_target_pairs={{0,1},{1,0},{2,3},{3,2},{4,5},{5,4},{6,7},{7,6},{8,9},{9,8},{10,11... | collective-permute-start | bytes 571400 | tf_op jit(solution)/shard_map/ppermute | solution.py:592
  22.3 0.3 shard_map.127
  22.5 1.4 %collective-permute-start.7 = (s16[2,16,16,128]{3,2,1,0:T(8,128)(2,1)S(1)}, s16[2,16,16,128]{3,2,1,0:T(8,128)(2,1)S(1)}, u32[]{:S(2)}, u32[]{:S(2)}) collective-permute-start(s16[2,16,16,128]{3,2,1,0:T(8,128)(2,1)S(1)} %get-tuple-element.45), channel_id=1, source_target_pairs={{4,0},{8,4},{12,8},{5,1},{9,5},{13,9},{6,2},{10,6},{14,10},{7,3},{... | collective-permute-start | bytes 393224 | tf_op jit(solution)/shard_map/ppermute | solution.py:577
  24.0 1.3 %collective-permute-start.11 = (s16[2,16,16,128]{3,2,1,0:T(8,128)(2,1)S(1)}, s16[2,16,16,128]{3,2,1,0:T(8,128)(2,1)S(1)}, u32[]{:S(2)}, u32[]{:S(2)}) collective-permute-start(s16[2,16,16,128]{3,2,1,0:T(8,128)(2,1)S(1)} %get-tuple-element.52), channel_id=1, source_target_pairs={{4,0},{8,4},{12,8},{5,1},{9,5},{13,9},{6,2},{10,6},{14,10},{7,3},{... | collective-permute-start | bytes 393224 | tf_op jit(solution)/shard_map/ppermute | solution.py:577
  25.3 0.1 shard_map.129.refs_6_
  25.4 2.8 %shard_map.130 = (f32[1,4,4,8,384]{4,3,2,1,0:T(8,128)}, f32[4,5,3,8,128]{4,3,2,1,0:T(8,128)S(1)}, f32[4,4,5,3,16,128]{5,4,3,2,1,0:T(8,128)S(1)}) custom-call(f32[5,5,8,128]{3,2,1,0:T(8,128)S(1)} %get-tuple-element.34.refs_4_.refs_0_, f32[4,4,8,128]{3,2,1,0:T(8,128)S(1)} %get-tuple-element.39.refs_1_, f32[4,4,3,8,128]{4,3,2,1,0:T(8,128)S(1)} %get-tuple-element.40.refs_2_, ...), custom_call_target="tpu_custom_call" | custom-call | tf_op jit(solution)/shard_map/pallas_call | solution.py:699
  28.2 2.7 %collective-permute-done.7.refs_4_ = s16[2,16,16,128]{3,2,1,0:T(8,128)(2,1)S(1)} collective-permute-done((s16[2,16,16,128]{3,2,1,0:T(8,128)(2,1)S(1)}, s16[2,16,16,128]{3,2,1,0:T(8,128)(2,1)S(1)}, u32[]{:S(2)}, u32[]{:S(2)}) %collective-permute-start.7) | collective-permute-done | bytes 131104 | tf_op jit(solution)/shard_map/ppermute | solution.py:577
  30.9 0.1 shard_map.131
  31.0 1.2 %shard_map.132 = (f32[5,2,8,384]{3,2,1,0:T(8,128)S(1)}, f32[5,2,8,384]{3,2,1,0:T(8,128)S(1)}, s16[16,16,128]{2,1,0:T(8,128)(2,1)S(1)}, s16[16,16,128]{2,1,0:T(8,128)(2,1)S(1)}, s16[16,16,128]{2,1,0:T(8,128)(2,1)S(1)}) custom-call(f32[5,5,8,128]{3,2,1,0:T(8,128)S(1)} %get-tuple-element.34.refs_4_.refs_0_, ...), custom_call_target="tpu_custom_call" | custom-call | tf_op jit(solution)/shard_map/pallas_call | solution.py:724
  32.2 3.5 %collective-permute-start.8 = (s16[16,16,128]{2,1,0:T(8,128)(2,1)S(1)}, s16[16,16,128]{2,1,0:T(8,128)(2,1)S(1)}, u32[]{:S(2)}, u32[]{:S(2)}) collective-permute-start(s16[16,16,128]{2,1,0:T(8,128)(2,1)S(1)} %get-tuple-element.49), channel_id=1, source_target_pairs={{0,12},{4,8},{8,4},{12,0},{1,13},{5,9},{9,5},{13,1},{2,14},{6,10},... | collective-permute-start | bytes 196616 | tf_op jit(solution)/shard_map/ppermute | solution.py:581
  35.7 1.0 %collective-permute-start.10 = (s16[16,16,128]{2,1,0:T(8,128)(2,1)S(1)}, s16[16,16,128]{2,1,0:T(8,128)(2,1)S(1)}, u32[]{:S(2)}, u32[]{:S(2)}) collective-permute-start(s16[16,16,128]{2,1,0:T(8,128)(2,1)S(1)} %get-tuple-element.51), channel_id=1, source_target_pairs={{0,4},{4,0},{8,12},{12,8},{1,5},{5,1},{9,13},{13,9},{2,6},{6,2},{1... | collective-permute-start | bytes 196616 | tf_op jit(solution)/shard_map/ppermute | solution.py:581
  36.7 0.1 shard_map.133
  36.8 1.2 %shard_map.134 = (f32[5,2,8,384]{3,2,1,0:T(8,128)S(1)}, f32[5,2,8,384]{3,2,1,0:T(8,128)S(1)}, s16[16,16,128]{2,1,0:T(8,128)(2,1)S(1)}, s16[16,16,128]{2,1,0:T(8,128)(2,1)S(1)}, s16[16,16,128]{2,1,0:T(8,128)(2,1)S(1)}) custom-call(f32[5,5,8,128]{3,2,1,0:T(8,128)S(1)} %get-tuple-element.34.refs_4_.refs_0_, ...), custom_call_target="tpu_custom_call" | custom-call | tf_op jit(solution)/shard_map/pallas_call | solution.py:724
  38.0 3.5 %collective-permute-start.12 = (s16[16,16,128]{2,1,0:T(8,128)(2,1)S(1)}, s16[16,16,128]{2,1,0:T(8,128)(2,1)S(1)}, u32[]{:S(2)}, u32[]{:S(2)}) collective-permute-start(s16[16,16,128]{2,1,0:T(8,128)(2,1)S(1)} %get-tuple-element.56), channel_id=1, source_target_pairs={{0,12},{4,8},{8,4},{12,0},{1,13},{5,9},{9,5},{13,1},{2,14},{6,10},... | collective-permute-start | bytes 196616 | tf_op jit(solution)/shard_map/ppermute | solution.py:581
  41.4 1.0 %collective-permute-start.14 = (s16[16,16,128]{2,1,0:T(8,128)(2,1)S(1)}, s16[16,16,128]{2,1,0:T(8,128)(2,1)S(1)}, u32[]{:S(2)}, u32[]{:S(2)}) collective-permute-start(s16[16,16,128]{2,1,0:T(8,128)(2,1)S(1)} %get-tuple-element.58), channel_id=1, source_target_pairs={{0,4},{4,0},{8,12},{12,8},{1,5},{5,1},{9,13},{13,9},{2,6},{6,2},{1... | collective-permute-start | bytes 196616 | tf_op jit(solution)/shard_map/ppermute | solution.py:581
  42.4 1.7 %collective-permute-done.9.refs_1_ = s16[16,16,128]{2,1,0:T(8,128)(2,1)S(1)} collective-permute-done((s16[16,16,128]{2,1,0:T(8,128)(2,1)S(1)}, s16[16,16,128]{2,1,0:T(8,128)(2,1)S(1)}, u32[]{:S(2)}, u32[]{:S(2)}) %collective-permute-start.9) | collective-permute-done | bytes 65568 | tf_op jit(solution)/shard_map/ppermute | solution.py:581
  44.1 2.9 %collective-permute-done.13.refs_4_ = s16[16,16,128]{2,1,0:T(8,128)(2,1)S(1)} collective-permute-done((s16[16,16,128]{2,1,0:T(8,128)(2,1)S(1)}, s16[16,16,128]{2,1,0:T(8,128)(2,1)S(1)}, u32[]{:S(2)}, u32[]{:S(2)}) %collective-permute-start.13) | collective-permute-done | bytes 65568 | tf_op jit(solution)/shard_map/ppermute | solution.py:581
  47.0 1.0 %shard_map.135 = (f32[1,5,4,8,384]{4,3,2,1,0:T(8,128)}, f32[1,5,4,8,384]{4,3,2,1,0:T(8,128)}) custom-call(s16[16,16,128]{2,1,0:T(8,128)(2,1)S(1)} %collective-permute-done.8.refs_0_, s16[16,16,128]{2,1,0:T(8,128)(2,1)S(1)} %collective-permute-done.9.refs_1_, s16[16,16,128]{2,1,0:T(8,128)(2,1)S(1)} %collective-permute-done.10.refs_2_, ...), custom_call_target="tpu_custom_call" | custom-call | tf_op jit(solution)/shard_map/pallas_call | solution.py:745
  (32 shorter events, 0.2 us)
Async XLA Ops:
  0.6 10.1 %copy-start.8 = (f32[1,4,4]{2,1,0:T(4,128)S(1)}, f32[1,4,4]{2,1,0:T(4,128)}, u32[]{:S(2)}) copy-start(f32[1,4,4]{2,1,0:T(4,128)} %refs_1_.6) | copy-start | bytes 196
  0.6 10.1 %copy-start.7 = (f32[5,5]{1,0:T(8,128)S(1)}, f32[5,5]{1,0:T(8,128)}, u32[]{:S(2)}) copy-start(f32[5,5]{1,0:T(8,128)} %refs_2_.3) | copy-start | bytes 304
  1.3 1.1 %copy-start = (bf16[4,4,5,4,8,96]{5,4,3,2,1,0:T(8,128)(2,1)S(1)}, bf16[4,4,5,4,8,96]{5,4,3,2,1,0:T(8,128)(2,1)}, u32[]{:S(2)}) copy-start(bf16[4,4,5,4,8,96]{5,4,3,2,1,0:T(8,128)(2,1)} %refs_1_.10) | copy-start | bytes 1474564
  2.4 6.2 %copy-start.2 = (f32[1,5,4,8,384]{4,3,2,1,0:T(8,128)S(1)}, f32[1,5,4,8,384]{4,3,2,1,0:T(8,128)}, u32[]{:S(2)}) copy-start(f32[1,5,4,8,384]{4,3,2,1,0:T(8,128)} %refs_6_.3) | copy-start | bytes 737284
  2.4 6.2 %copy-start.3 = (f32[1,4,4,8,384]{4,3,2,1,0:T(8,128)S(1)}, f32[1,4,4,8,384]{4,3,2,1,0:T(8,128)}, u32[]{:S(2)}) copy-start(f32[1,4,4,8,384]{4,3,2,1,0:T(8,128)} %refs_3_.5) | copy-start | bytes 589828
  2.4 6.2 %copy-start.4 = (f32[1,5,4,8,384]{4,3,2,1,0:T(8,128)S(1)}, f32[1,5,4,8,384]{4,3,2,1,0:T(8,128)}, u32[]{:S(2)}) copy-start(f32[1,5,4,8,384]{4,3,2,1,0:T(8,128)} %refs_8_.3) | copy-start | bytes 737284
  2.4 7.5 %copy-start.1 = (bf16[4,4,5,4,8,96]{5,4,3,2,1,0:T(8,128)(2,1)S(1)}, bf16[4,4,5,4,8,96]{5,4,3,2,1,0:T(8,128)(2,1)}, u32[]{:S(2)}) copy-start(bf16[4,4,5,4,8,96]{5,4,3,2,1,0:T(8,128)(2,1)} %refs_1_.10) | copy-start | bytes 1474564
  2.4 8.3 %copy-start.6 = (f32[1,4,4,8,384]{4,3,2,1,0:T(8,128)S(1)}, f32[1,4,4,8,384]{4,3,2,1,0:T(8,128)}, u32[]{:S(2)}) copy-start(f32[1,4,4,8,384]{4,3,2,1,0:T(8,128)} %refs_4_.1) | copy-start | bytes 589828
  2.6 8.8 %collective-permute-start = (bf16[61,8,128]{2,1,0:T(8,128)(2,1)S(1)}, bf16[61,8,128]{2,1,0:T(8,128)(2,1)S(1)}, u32[]{:S(2)}, u32[]{:S(2)}) collective-permute-start(bf16[61,8,128]{2,1,0:T(8,128)(2,1)S(1)} %shard_map.123), channel_id=1, source_target_pairs={{0,4},{4,0},{8,12},{12,8},{1,5},{5,1},{9,13},{13,9},{2,6},{6,2},{1... | collective-permute-start | bytes 374792 | tf_op jit(solution)/shard_map/ppermute | solution.py:581
  5.8 12.5 %collective-permute-start.1 = (bf16[61,8,128]{2,1,0:T(8,128)(2,1)S(1)}, bf16[61,8,128]{2,1,0:T(8,128)(2,1)S(1)}, u32[]{:S(2)}, u32[]{:S(2)}) collective-permute-start(bf16[61,8,128]{2,1,0:T(8,128)(2,1)S(1)} %shard_map.124), channel_id=1, source_target_pairs={{0,8},{4,12},{8,0},{12,4},{1,9},{5,13},{9,1},{13,5},{2,10},{6,14},... | collective-permute-start | bytes 374792 | tf_op jit(solution)/shard_map/ppermute | solution.py:581
  8.6 9.7 %collective-permute-start.2 = (bf16[61,8,128]{2,1,0:T(8,128)(2,1)S(1)}, bf16[61,8,128]{2,1,0:T(8,128)(2,1)S(1)}, u32[]{:S(2)}, u32[]{:S(2)}) collective-permute-start(bf16[61,8,128]{2,1,0:T(8,128)(2,1)S(1)} %shard_map.125), channel_id=1, source_target_pairs={{0,12},{4,8},{8,4},{12,0},{1,13},{5,9},{9,5},{13,1},{2,14},{6,10},... | collective-permute-start | bytes 374792 | tf_op jit(solution)/shard_map/ppermute | solution.py:581
  9.1 13.1 %collective-permute-start.3 = (s16[2,21,16,128]{3,2,1,0:T(8,128)(2,1)S(1)}, s16[2,21,16,128]{3,2,1,0:T(8,128)(2,1)S(1)}, u32[]{:S(2)}, u32[]{:S(2)}) collective-permute-start(s16[2,21,16,128]{3,2,1,0:T(8,128)(2,1)S(1)} %get-tuple-element.36), channel_id=1, source_target_pairs={{0,1},{1,0},{2,3},{3,2},{4,5},{5,4},{6,7},{7,6},{8,9},{9,8},{10,11... | collective-permute-start | bytes 516104 | tf_op jit(solution)/shard_map/ppermute | solution.py:592
  9.2 13.0 %collective-permute-start.4 = (s16[2,21,16,128]{3,2,1,0:T(8,128)(2,1)S(1)}, s16[2,21,16,128]{3,2,1,0:T(8,128)(2,1)S(1)}, u32[]{:S(2)}, u32[]{:S(2)}) collective-permute-start(s16[2,21,16,128]{3,2,1,0:T(8,128)(2,1)S(1)} %get-tuple-element.37), channel_id=1, source_target_pairs={{1,2},{2,1},{5,6},{6,5},{9,10},{10,9},{13,14},{14,13},{17,18},{18,... | collective-permute-start | bytes 516104 | tf_op jit(solution)/shard_map/ppermute | solution.py:592
  18.7 6.8 %collective-permute-start.5 = (bf16[31,8,384]{2,1,0:T(8,128)(2,1)S(1)}, bf16[31,8,384]{2,1,0:T(8,128)(2,1)S(1)}, u32[]{:S(2)}, u32[]{:S(2)}) collective-permute-start(bf16[31,8,384]{2,1,0:T(8,128)(2,1)S(1)} %get-tuple-element.42), channel_id=1, source_target_pairs={{1,2},{2,1},{5,6},{6,5},{9,10},{10,9},{13,14},{14,13},{17,18},{18,... | collective-permute-start | bytes 571400 | tf_op jit(solution)/shard_map/ppermute | solution.py:592
  19.4 6.1 %collective-permute-start.6 = (bf16[31,8,384]{2,1,0:T(8,128)(2,1)S(1)}, bf16[31,8,384]{2,1,0:T(8,128)(2,1)S(1)}, u32[]{:S(2)}, u32[]{:S(2)}) collective-permute-start(bf16[31,8,384]{2,1,0:T(8,128)(2,1)S(1)} %get-tuple-element.43), channel_id=1, source_target_pairs={{0,1},{1,0},{2,3},{3,2},{4,5},{5,4},{6,7},{7,6},{8,9},{9,8},{10,11... | collective-permute-start | bytes 571400 | tf_op jit(solution)/shard_map/ppermute | solution.py:592
  22.5 8.5 %copy-start.5 = (f32[1,5,4,8,384]{4,3,2,1,0:T(8,128)S(1)}, f32[1,5,4,8,384]{4,3,2,1,0:T(8,128)}, u32[]{:S(2)}) copy-start(f32[1,5,4,8,384]{4,3,2,1,0:T(8,128)} %refs_7_.3) | copy-start | bytes 737284
  22.5 8.4 %collective-permute-start.7 = (s16[2,16,16,128]{3,2,1,0:T(8,128)(2,1)S(1)}, s16[2,16,16,128]{3,2,1,0:T(8,128)(2,1)S(1)}, u32[]{:S(2)}, u32[]{:S(2)}) collective-permute-start(s16[2,16,16,128]{3,2,1,0:T(8,128)(2,1)S(1)} %get-tuple-element.45), channel_id=1, source_target_pairs={{4,0},{8,4},{12,8},{5,1},{9,5},{13,9},{6,2},{10,6},{14,10},{7,3},{... | collective-permute-start | bytes 393224 | tf_op jit(solution)/shard_map/ppermute | solution.py:577
  24.0 12.7 %collective-permute-start.11 = (s16[2,16,16,128]{3,2,1,0:T(8,128)(2,1)S(1)}, s16[2,16,16,128]{3,2,1,0:T(8,128)(2,1)S(1)}, u32[]{:S(2)}, u32[]{:S(2)}) collective-permute-start(s16[2,16,16,128]{3,2,1,0:T(8,128)(2,1)S(1)} %get-tuple-element.52), channel_id=1, source_target_pairs={{4,0},{8,4},{12,8},{5,1},{9,5},{13,9},{6,2},{10,6},{14,10},{7,3},{... | collective-permute-start | bytes 393224 | tf_op jit(solution)/shard_map/ppermute | solution.py:577
  32.2 9.2 %collective-permute-start.8 = (s16[16,16,128]{2,1,0:T(8,128)(2,1)S(1)}, s16[16,16,128]{2,1,0:T(8,128)(2,1)S(1)}, u32[]{:S(2)}, u32[]{:S(2)}) collective-permute-start(s16[16,16,128]{2,1,0:T(8,128)(2,1)S(1)} %get-tuple-element.49), channel_id=1, source_target_pairs={{0,12},{4,8},{8,4},{12,0},{1,13},{5,9},{9,5},{13,1},{2,14},{6,10},... | collective-permute-start | bytes 196616 | tf_op jit(solution)/shard_map/ppermute | solution.py:581
  35.7 8.4 %collective-permute-start.9 = (s16[16,16,128]{2,1,0:T(8,128)(2,1)S(1)}, s16[16,16,128]{2,1,0:T(8,128)(2,1)S(1)}, u32[]{:S(2)}, u32[]{:S(2)}) collective-permute-start(s16[16,16,128]{2,1,0:T(8,128)(2,1)S(1)} %get-tuple-element.50), channel_id=1, source_target_pairs={{0,8},{4,12},{8,0},{12,4},{1,9},{5,13},{9,1},{13,5},{2,10},{6,14},... | collective-permute-start | bytes 196616 | tf_op jit(solution)/shard_map/ppermute | solution.py:581
  35.7 8.4 %collective-permute-start.10 = (s16[16,16,128]{2,1,0:T(8,128)(2,1)S(1)}, s16[16,16,128]{2,1,0:T(8,128)(2,1)S(1)}, u32[]{:S(2)}, u32[]{:S(2)}) collective-permute-start(s16[16,16,128]{2,1,0:T(8,128)(2,1)S(1)} %get-tuple-element.51), channel_id=1, source_target_pairs={{0,4},{4,0},{8,12},{12,8},{1,5},{5,1},{9,13},{13,9},{2,6},{6,2},{1... | collective-permute-start | bytes 196616 | tf_op jit(solution)/shard_map/ppermute | solution.py:581
  38.0 6.2 %collective-permute-start.12 = (s16[16,16,128]{2,1,0:T(8,128)(2,1)S(1)}, s16[16,16,128]{2,1,0:T(8,128)(2,1)S(1)}, u32[]{:S(2)}, u32[]{:S(2)}) collective-permute-start(s16[16,16,128]{2,1,0:T(8,128)(2,1)S(1)} %get-tuple-element.56), channel_id=1, source_target_pairs={{0,12},{4,8},{8,4},{12,0},{1,13},{5,9},{9,5},{13,1},{2,14},{6,10},... | collective-permute-start | bytes 196616 | tf_op jit(solution)/shard_map/ppermute | solution.py:581
  41.4 5.6 %collective-permute-start.13 = (s16[16,16,128]{2,1,0:T(8,128)(2,1)S(1)}, s16[16,16,128]{2,1,0:T(8,128)(2,1)S(1)}, u32[]{:S(2)}, u32[]{:S(2)}) collective-permute-start(s16[16,16,128]{2,1,0:T(8,128)(2,1)S(1)} %get-tuple-element.57), channel_id=1, source_target_pairs={{0,8},{4,12},{8,0},{12,4},{1,9},{5,13},{9,1},{13,5},{2,10},{6,14},... | collective-permute-start | bytes 196616 | tf_op jit(solution)/shard_map/ppermute | solution.py:581
  41.4 5.6 %collective-permute-start.14 = (s16[16,16,128]{2,1,0:T(8,128)(2,1)S(1)}, s16[16,16,128]{2,1,0:T(8,128)(2,1)S(1)}, u32[]{:S(2)}, u32[]{:S(2)}) collective-permute-start(s16[16,16,128]{2,1,0:T(8,128)(2,1)S(1)} %get-tuple-element.58), channel_id=1, source_target_pairs={{0,4},{4,0},{8,12},{12,8},{1,5},{5,1},{9,13},{13,9},{2,6},{6,2},{1... | collective-permute-start | bytes 196616 | tf_op jit(solution)/shard_map/ppermute | solution.py:581

commit v16 on v15

--- a/solution.py
+++ b/solution.py
@@ -120,7 +120,7 @@
 
     for n, d in enumerate(ways):
         outs[n][outs[n].shape[0] - 1] = split
-        target = me ^ d
+        target = lax.rem(me + d, windows)
 
         def variable(v, carry, n=n, target=target):
             for lev in range(levels):
@@ -189,7 +189,7 @@
     for d in range(windows):
         split = pieces[d][pieces[d].shape[0] - 1].astype(jnp.float32)
         here = split + pltpu.roll(split, HALF, 0) + pltpu.roll(split, LANES // 2, 1)
-        total = total + jnp.where((me ^ d) <= me, here, 0.0)
+        total = total + jnp.where(lax.rem(me - d + windows, windows) <= me, here, 0.0)
     for v in range(nvar):
         for lev in range(levels):
             one = total[lev : lev + 1, v : v + 1]
@@ -242,7 +242,7 @@
     count = stack_ref.shape[1]
     packed_tiles = count // (nvar * levels)
     for d in range(windows):
-        stack_ref[me ^ d] = pieces[d][:count]
+        stack_ref[lax.rem(me - d + windows, windows)] = pieces[d][:count]
 
     base, _ = edge_base(steps, nvar, levels)
 
@@ -381,7 +381,7 @@
 
 def tangent_kernel(
     spaces, steps, nvar, levels, tiles,
-    mix_ref, share_ref, obs_ref, own_ref, far_ref, near_ref, first_ref,
+    mix_ref, share_ref, obs_ref, own_ref, near_ref, far_ref, first_ref,
     ndo_ref, ends_ref, x_ref, s_ref,
 ):
     lane, row = lane_index(), row_index()
@@ -577,6 +577,11 @@
     return lax.ppermute(block, axis, [(i, i + distance) for i in devices if i + distance in devices])
 
 
+def rotated(block, axis, distance):
+    count = lax.axis_size(axis)
+    return lax.ppermute(block, axis, [(i, (i + distance) % count) for i in range(count)])
+
+
 def exchanged(block, axis, mask):
     return lax.ppermute(block, axis, [(i, i ^ mask) for i in range(lax.axis_size(axis))])
 
@@ -630,12 +635,12 @@
             compiler_params=params(),
         )(variances, trajectory)
 
-    order = partners(windows)
+    order = list(range(1, windows))
     groups = [[d] for d in order] if windows <= 4 else [order]
     blocks = {}
     for group in groups:
         blocks.update(zip(group, packed(group)))
-    arrived = {d: exchanged(blocks[d], "window", d) for d in order}
+    arrived = {d: rotated(blocks[d], "window", d) for d in order}
     arrived[0] = packed([0])[0]
 
     payload = shape((pairs, nvar * tiles + 1, 2 * SUB, LANES), i16)
@@ -707,7 +712,7 @@
         out_specs=[VMEM] * 3,
         scratch_shapes=[pltpu.VMEM((2, 2, nvar, tiles, 4 * SUB, LANES), f32)],
         compiler_params=params(),
-    )(mix, share, obs, own, traj_far, traj_near, first)
+    )(mix, share, obs, own, traj_near, traj_far, first)
 
     state = shape((nvar, 2, rows, columns), f32)
     coded = shape((nvar * tiles + 1, 2 * SUB, LANES), i16)
@@ -739,7 +744,8 @@
         base_duals.append(base_dual)
         base_incs.append(base_inc)
         sent += [
-            exchanged(piece, "window", d) for piece, d in zip(payloads, order)
+            exchanged(piece, "window", mask)
+            for piece, mask in zip(payloads, partners(windows))
         ]
 
     new_dual_model, new_increment = pl.pallas_call(

time: 48.3 us -> 45.7 us (0.946)
  waiting for transfers between devices: 14.2 us -> 11.9 us
  starting transfers between devices: 21.8 us -> 21.3 us
    ppermute x0 -> x3, starting transfers between devices: none -> 7.13 us  [rotated(): lax.ppermute(block, axis, [(i, (i + distance) % count) for i in range(cou...]
    ppermute x9 -> x6, waiting for transfers between devices: 11.5 us -> 5.64 us  [exchanged(): lax.ppermute(block, axis, [(i, i ^ mask) for i in range(lax.axis_size(axi...]
    ppermute x9 -> x6, starting transfers between devices: 14.7 us -> 10 us  [exchanged(): lax.ppermute(block, axis, [(i, i ^ mask) for i in range(lax.axis_size(axi...]
    ppermute x0 -> x3, waiting for transfers between devices: none -> 3.81 us  [rotated(): lax.ppermute(block, axis, [(i, (i + distance) % count) for i in range(cou...]
    ppermute x4, starting transfers between devices: 4.32 us -> 1.49 us  [swapped(): return lax.ppermute(block, axis, swaps(axis, first))]
  transfers between devices with their start and end apart: 15 -> 15, of which waited for: 4 -> 5; matrix products, arithmetic and copies ran while one was open for 0% -> 0% of each run, Pallas kernels for 16% -> 17%
where the time goes in v16:
time: 45.7 us; the launch traced here: 45.4 us
  starting transfers between devices  21.3 us (47%)
  waiting for transfers between devices  11.9 us (26%)
  Pallas kernels  8.79 us (19%)
  local copies, waits for them, and re-layouts  1.82 us (4%)
  between operations  1.54 us (3%)
    ppermute x6, starting transfers between devices, exchanged(): lax.ppermute(block, axis, [(i, i ^ mask) for i in range(lax.axis_size(axi...  10 us
    ppermute x3, starting transfers between devices, rotated(): lax.ppermute(block, axis, [(i, (i + distance) % count) for i in range(cou...  7.13 us
    ppermute x6, waiting for transfers between devices, exchanged(): lax.ppermute(block, axis, [(i, i ^ mask) for i in range(lax.axis_size(axi...  5.64 us
    ppermute x3, waiting for transfers between devices, rotated(): lax.ppermute(block, axis, [(i, (i + distance) % count) for i in range(cou...  3.81 us
    pallas_call x1, Pallas kernels, body(): pl.pallas_call(lambda *refs: tangent_kernel(spaces, steps, nvar, levels,...  2.78 us
    ppermute x2, starting transfers between devices, moved(): lax.ppermute(block, axis, [(i, i + distance) for i in devices if i + dist...  2.72 us
    ppermute x2, waiting for transfers between devices, moved(): lax.ppermute(block, axis, [(i, i + distance) for i in devices if i + dist...  2.45 us
    pallas_call x2, Pallas kernels, body(): pl.pallas_call(lambda *refs, i=i: adjoint_kernel(i, windows, spaces, step...  2.33 us
  transfers between devices with their start and end apart: 15, of which 5 were waited for; matrix products, arithmetic and copies ran while one was open for 0% of the time, Pallas kernels for 17%

profile of v16, /device:TPU:0, one launch (start us, length us, event | category | flops | bytes accessed | tf_op | source)
XLA Modules:
  0.0 45.4 jit_solution(13493069522975250218)
XLA Ops:
  0.7 0.7 %pad.4.refs_0_ = f32[8,128]{1,0:T(8,128)S(1)} pad(f32[4,5]{1,0:T(4,128)} %bitcast.3, f32[]{:T(128)} %constant.2.clone.1), padding=0_4x0_123 | pad | bytes 4180 | tf_op jit(solution)/shard_map/jit(_pad)/pad | solution.py:627
  1.4 1.1 %copy-done = bf16[4,4,5,4,8,96]{5,4,3,2,1,0:T(8,128)(2,1)S(1)} copy-done((bf16[4,4,5,4,8,96]{5,4,3,2,1,0:T(8,128)(2,1)S(1)}, bf16[4,4,5,4,8,96]{5,4,3,2,1,0:T(8,128)(2,1)}, u32[]{:S(2)}) %copy-start) | copy-done | bytes 491544
  2.5 0.1 shard_map.123
  2.6 3.1 %collective-permute-start = (bf16[61,8,128]{2,1,0:T(8,128)(2,1)S(1)}, bf16[61,8,128]{2,1,0:T(8,128)(2,1)S(1)}, u32[]{:S(2)}, u32[]{:S(2)}) collective-permute-start(bf16[61,8,128]{2,1,0:T(8,128)(2,1)S(1)} %shard_map.123), channel_id=1, source_target_pairs={{0,4},{4,8},{8,12},{12,0},{1,5},{5,9},{9,13},{13,1},{2,6},{6,10},{... | collective-permute-start | bytes 374792 | tf_op jit(solution)/shard_map/ppermute | solution.py:582
  5.7 0.1 shard_map.124
  5.8 2.7 %collective-permute-start.1 = (bf16[61,8,128]{2,1,0:T(8,128)(2,1)S(1)}, bf16[61,8,128]{2,1,0:T(8,128)(2,1)S(1)}, u32[]{:S(2)}, u32[]{:S(2)}) collective-permute-start(bf16[61,8,128]{2,1,0:T(8,128)(2,1)S(1)} %shard_map.124), channel_id=1, source_target_pairs={{0,8},{4,12},{8,0},{12,4},{1,9},{5,13},{9,1},{13,5},{2,10},{6,14},... | collective-permute-start | bytes 374792 | tf_op jit(solution)/shard_map/ppermute | solution.py:582
  8.5 1.4 %collective-permute-start.2 = (bf16[61,8,128]{2,1,0:T(8,128)(2,1)S(1)}, bf16[61,8,128]{2,1,0:T(8,128)(2,1)S(1)}, u32[]{:S(2)}, u32[]{:S(2)}) collective-permute-start(bf16[61,8,128]{2,1,0:T(8,128)(2,1)S(1)} %shard_map.125), channel_id=1, source_target_pairs={{0,12},{4,0},{8,4},{12,8},{1,13},{5,1},{9,5},{13,9},{2,14},{6,2},{... | collective-permute-start | bytes 374792 | tf_op jit(solution)/shard_map/ppermute | solution.py:582
  10.0 0.5 %shard_map.126 = (s16[2,21,16,128]{3,2,1,0:T(8,128)(2,1)S(1)}, s16[2,21,16,128]{3,2,1,0:T(8,128)(2,1)S(1)}, s16[2,16,16,128]{3,2,1,0:T(8,128)(2,1)S(1)}) custom-call(f32[1,5,4,8,384]{4,3,2,1,0:T(8,128)S(1)} %copy-done.4, f32[1,5,4,8,384]{4,3,2,1,0:T(8,128)S(1)} %copy-done.2, f32[1,4,4,8,384]{4,3,2,1,0:T(8,128)S(1)} %copy-done.3), custom_call_target="tpu_custom_call" | custom-call | tf_op jit(solution)/shard_map/pallas_call | solution.py:651
  10.5 0.7 %collective-permute-start.4 = (s16[2,21,16,128]{3,2,1,0:T(8,128)(2,1)S(1)}, s16[2,21,16,128]{3,2,1,0:T(8,128)(2,1)S(1)}, u32[]{:S(2)}, u32[]{:S(2)}) collective-permute-start(s16[2,21,16,128]{3,2,1,0:T(8,128)(2,1)S(1)} %get-tuple-element.37), channel_id=1, source_target_pairs={{1,2},{2,1},{5,6},{6,5},{9,10},{10,9},{13,14},{14,13},{17,18},{18,... | collective-permute-start | bytes 516104 | tf_op jit(solution)/shard_map/ppermute | solution.py:597
  11.2 0.1 shard_map.122.refs_0_
  12.0 0.7 %shard_map.121 = (f32[4,4,3,8,128]{4,3,2,1,0:T(8,128)S(1)}, f32[4,4,8,128]{3,2,1,0:T(8,128)S(1)}, f32[5,5,8,128]{3,2,1,0:T(8,128)S(1)}) custom-call(s32[1]{0:T(128)S(6)} %copy.13.refs_0_, f32[1,4,4]{2,1,0:T(4,128)S(1)} %copy-done.8, f32[5,5]{1,0:T(8,128)S(1)} %copy-done.7, f32[1,4,4,8,384]{4,3,2,1,0:T(8,128)S(1)} %copy-done.3, f32[1,4,4,8,384]{4,3,2,1,0:T(8,128)S(1)} %copy-done.6), custom_call_target="tpu_custom_call" | custom-call | tf_op jit(solution)/shard_map/pallas_call | solution.py:671
  12.7 3.8 %collective-permute-done.1.refs_2_ = bf16[61,8,128]{2,1,0:T(8,128)(2,1)S(1)} collective-permute-done((bf16[61,8,128]{2,1,0:T(8,128)(2,1)S(1)}, bf16[61,8,128]{2,1,0:T(8,128)(2,1)S(1)}, u32[]{:S(2)}, u32[]{:S(2)}) %collective-permute-start.1) | collective-permute-done | bytes 124960 | tf_op jit(solution)/shard_map/ppermute | solution.py:582
  16.5 0.4 shard_map.128
  17.0 0.7 %collective-permute-start.6 = (bf16[31,8,384]{2,1,0:T(8,128)(2,1)S(1)}, bf16[31,8,384]{2,1,0:T(8,128)(2,1)S(1)}, u32[]{:S(2)}, u32[]{:S(2)}) collective-permute-start(bf16[31,8,384]{2,1,0:T(8,128)(2,1)S(1)} %get-tuple-element.43), channel_id=1, source_target_pairs={{1,2},{2,1},{5,6},{6,5},{9,10},{10,9},{13,14},{14,13},{17,18},{18,... | collective-permute-start | bytes 571400 | tf_op jit(solution)/shard_map/ppermute | solution.py:597
  17.7 0.3 shard_map.127
  18.0 1.4 %collective-permute-start.7 = (s16[2,16,16,128]{3,2,1,0:T(8,128)(2,1)S(1)}, s16[2,16,16,128]{3,2,1,0:T(8,128)(2,1)S(1)}, u32[]{:S(2)}, u32[]{:S(2)}) collective-permute-start(s16[2,16,16,128]{3,2,1,0:T(8,128)(2,1)S(1)} %get-tuple-element.45), channel_id=1, source_target_pairs={{4,0},{8,4},{12,8},{5,1},{9,5},{13,9},{6,2},{10,6},{14,10},{7,3},{... | collective-permute-start | bytes 393224 | tf_op jit(solution)/shard_map/ppermute | solution.py:577
  19.4 1.3 %collective-permute-start.11 = (s16[2,16,16,128]{3,2,1,0:T(8,128)(2,1)S(1)}, s16[2,16,16,128]{3,2,1,0:T(8,128)(2,1)S(1)}, u32[]{:S(2)}, u32[]{:S(2)}) collective-permute-start(s16[2,16,16,128]{3,2,1,0:T(8,128)(2,1)S(1)} %get-tuple-element.52), channel_id=1, source_target_pairs={{4,0},{8,4},{12,8},{5,1},{9,5},{13,9},{6,2},{10,6},{14,10},{7,3},{... | collective-permute-start | bytes 393224 | tf_op jit(solution)/shard_map/ppermute | solution.py:577
  20.7 0.1 shard_map.129.refs_6_
  20.9 2.8 %shard_map.130 = (f32[1,4,4,8,384]{4,3,2,1,0:T(8,128)}, f32[4,5,3,8,128]{4,3,2,1,0:T(8,128)S(1)}, f32[4,4,5,3,16,128]{5,4,3,2,1,0:T(8,128)S(1)}) custom-call(f32[5,5,8,128]{3,2,1,0:T(8,128)S(1)} %get-tuple-element.34.refs_4_.refs_0_, f32[4,4,8,128]{3,2,1,0:T(8,128)S(1)} %get-tuple-element.39.refs_1_, f32[4,4,3,8,128]{4,3,2,1,0:T(8,128)S(1)} %get-tuple-element.40.refs_2_, ...), custom_call_target="tpu_custom_call" | custom-call | tf_op jit(solution)/shard_map/pallas_call | solution.py:704
  23.7 2.4 %collective-permute-done.7.refs_4_ = s16[2,16,16,128]{3,2,1,0:T(8,128)(2,1)S(1)} collective-permute-done((s16[2,16,16,128]{3,2,1,0:T(8,128)(2,1)S(1)}, s16[2,16,16,128]{3,2,1,0:T(8,128)(2,1)S(1)}, u32[]{:S(2)}, u32[]{:S(2)}) %collective-permute-start.7) | collective-permute-done | bytes 131104 | tf_op jit(solution)/shard_map/ppermute | solution.py:577
  26.1 0.1 shard_map.131
  26.3 1.2 %shard_map.132 = (f32[5,2,8,384]{3,2,1,0:T(8,128)S(1)}, f32[5,2,8,384]{3,2,1,0:T(8,128)S(1)}, s16[16,16,128]{2,1,0:T(8,128)(2,1)S(1)}, s16[16,16,128]{2,1,0:T(8,128)(2,1)S(1)}, s16[16,16,128]{2,1,0:T(8,128)(2,1)S(1)}) custom-call(f32[5,5,8,128]{3,2,1,0:T(8,128)S(1)} %get-tuple-element.34.refs_4_.refs_0_, ...), custom_call_target="tpu_custom_call" | custom-call | tf_op jit(solution)/shard_map/pallas_call | solution.py:729
  27.4 4.9 %collective-permute-start.8 = (s16[16,16,128]{2,1,0:T(8,128)(2,1)S(1)}, s16[16,16,128]{2,1,0:T(8,128)(2,1)S(1)}, u32[]{:S(2)}, u32[]{:S(2)}) collective-permute-start(s16[16,16,128]{2,1,0:T(8,128)(2,1)S(1)} %get-tuple-element.49), channel_id=1, source_target_pairs={{0,12},{4,8},{8,4},{12,0},{1,13},{5,9},{9,5},{13,1},{2,14},{6,10},... | collective-permute-start | bytes 196616 | tf_op jit(solution)/shard_map/ppermute | solution.py:586
  32.3 0.6 %collective-permute-start.10 = (s16[16,16,128]{2,1,0:T(8,128)(2,1)S(1)}, s16[16,16,128]{2,1,0:T(8,128)(2,1)S(1)}, u32[]{:S(2)}, u32[]{:S(2)}) collective-permute-start(s16[16,16,128]{2,1,0:T(8,128)(2,1)S(1)} %get-tuple-element.51), channel_id=1, source_target_pairs={{0,4},{4,0},{8,12},{12,8},{1,5},{5,1},{9,13},{13,9},{2,6},{6,2},{1... | collective-permute-start | bytes 196616 | tf_op jit(solution)/shard_map/ppermute | solution.py:586
  33.0 0.1 shard_map.133
  33.1 1.2 %shard_map.134 = (f32[5,2,8,384]{3,2,1,0:T(8,128)S(1)}, f32[5,2,8,384]{3,2,1,0:T(8,128)S(1)}, s16[16,16,128]{2,1,0:T(8,128)(2,1)S(1)}, s16[16,16,128]{2,1,0:T(8,128)(2,1)S(1)}, s16[16,16,128]{2,1,0:T(8,128)(2,1)S(1)}) custom-call(f32[5,5,8,128]{3,2,1,0:T(8,128)S(1)} %get-tuple-element.34.refs_4_.refs_0_, ...), custom_call_target="tpu_custom_call" | custom-call | tf_op jit(solution)/shard_map/pallas_call | solution.py:729
  34.3 3.8 %collective-permute-start.12 = (s16[16,16,128]{2,1,0:T(8,128)(2,1)S(1)}, s16[16,16,128]{2,1,0:T(8,128)(2,1)S(1)}, u32[]{:S(2)}, u32[]{:S(2)}) collective-permute-start(s16[16,16,128]{2,1,0:T(8,128)(2,1)S(1)} %get-tuple-element.56), channel_id=1, source_target_pairs={{0,12},{4,8},{8,4},{12,0},{1,13},{5,9},{9,5},{13,1},{2,14},{6,10},... | collective-permute-start | bytes 196616 | tf_op jit(solution)/shard_map/ppermute | solution.py:586
  38.1 0.6 %collective-permute-start.14 = (s16[16,16,128]{2,1,0:T(8,128)(2,1)S(1)}, s16[16,16,128]{2,1,0:T(8,128)(2,1)S(1)}, u32[]{:S(2)}, u32[]{:S(2)}) collective-permute-start(s16[16,16,128]{2,1,0:T(8,128)(2,1)S(1)} %get-tuple-element.58), channel_id=1, source_target_pairs={{0,4},{4,0},{8,12},{12,8},{1,5},{5,1},{9,13},{13,9},{2,6},{6,2},{1... | collective-permute-start | bytes 196616 | tf_op jit(solution)/shard_map/ppermute | solution.py:586
  38.7 0.3 collective-permute-done.9.refs_1_
  39.1 1.4 %collective-permute-done.12.refs_3_ = s16[16,16,128]{2,1,0:T(8,128)(2,1)S(1)} collective-permute-done((s16[16,16,128]{2,1,0:T(8,128)(2,1)S(1)}, s16[16,16,128]{2,1,0:T(8,128)(2,1)S(1)}, u32[]{:S(2)}, u32[]{:S(2)}) %collective-permute-start.12) | collective-permute-done | bytes 65568 | tf_op jit(solution)/shard_map/ppermute | solution.py:586
  40.5 3.9 %collective-permute-done.13.refs_4_ = s16[16,16,128]{2,1,0:T(8,128)(2,1)S(1)} collective-permute-done((s16[16,16,128]{2,1,0:T(8,128)(2,1)S(1)}, s16[16,16,128]{2,1,0:T(8,128)(2,1)S(1)}, u32[]{:S(2)}, u32[]{:S(2)}) %collective-permute-start.13) | collective-permute-done | bytes 65568 | tf_op jit(solution)/shard_map/ppermute | solution.py:586
  44.4 1.0 %shard_map.135 = (f32[1,5,4,8,384]{4,3,2,1,0:T(8,128)}, f32[1,5,4,8,384]{4,3,2,1,0:T(8,128)}) custom-call(s16[16,16,128]{2,1,0:T(8,128)(2,1)S(1)} %collective-permute-done.8.refs_0_, s16[16,16,128]{2,1,0:T(8,128)(2,1)S(1)} %collective-permute-done.9.refs_1_, s16[16,16,128]{2,1,0:T(8,128)(2,1)S(1)} %collective-permute-done.10.refs_2_, ...), custom_call_target="tpu_custom_call" | custom-call | tf_op jit(solution)/shard_map/pallas_call | solution.py:751
  (32 shorter events, 0.3 us)
Async XLA Ops:
  0.6 11.3 %copy-start.8 = (f32[1,4,4]{2,1,0:T(4,128)S(1)}, f32[1,4,4]{2,1,0:T(4,128)}, u32[]{:S(2)}) copy-start(f32[1,4,4]{2,1,0:T(4,128)} %refs_1_.6) | copy-start | bytes 196
  0.6 11.3 %copy-start.7 = (f32[5,5]{1,0:T(8,128)S(1)}, f32[5,5]{1,0:T(8,128)}, u32[]{:S(2)}) copy-start(f32[5,5]{1,0:T(8,128)} %refs_2_.3) | copy-start | bytes 304
  1.3 1.1 %copy-start = (bf16[4,4,5,4,8,96]{5,4,3,2,1,0:T(8,128)(2,1)S(1)}, bf16[4,4,5,4,8,96]{5,4,3,2,1,0:T(8,128)(2,1)}, u32[]{:S(2)}) copy-start(bf16[4,4,5,4,8,96]{5,4,3,2,1,0:T(8,128)(2,1)} %refs_1_.10) | copy-start | bytes 1474564
  2.4 7.5 %copy-start.2 = (f32[1,5,4,8,384]{4,3,2,1,0:T(8,128)S(1)}, f32[1,5,4,8,384]{4,3,2,1,0:T(8,128)}, u32[]{:S(2)}) copy-start(f32[1,5,4,8,384]{4,3,2,1,0:T(8,128)} %refs_6_.3) | copy-start | bytes 737284
  2.4 7.5 %copy-start.3 = (f32[1,4,4,8,384]{4,3,2,1,0:T(8,128)S(1)}, f32[1,4,4,8,384]{4,3,2,1,0:T(8,128)}, u32[]{:S(2)}) copy-start(f32[1,4,4,8,384]{4,3,2,1,0:T(8,128)} %refs_3_.5) | copy-start | bytes 589828
  2.4 7.5 %copy-start.4 = (f32[1,5,4,8,384]{4,3,2,1,0:T(8,128)S(1)}, f32[1,5,4,8,384]{4,3,2,1,0:T(8,128)}, u32[]{:S(2)}) copy-start(f32[1,5,4,8,384]{4,3,2,1,0:T(8,128)} %refs_8_.3) | copy-start | bytes 737284
  2.4 8.7 %copy-start.1 = (bf16[4,4,5,4,8,96]{5,4,3,2,1,0:T(8,128)(2,1)S(1)}, bf16[4,4,5,4,8,96]{5,4,3,2,1,0:T(8,128)(2,1)}, u32[]{:S(2)}) copy-start(bf16[4,4,5,4,8,96]{5,4,3,2,1,0:T(8,128)(2,1)} %refs_1_.10) | copy-start | bytes 1474564
  2.4 9.5 %copy-start.6 = (f32[1,4,4,8,384]{4,3,2,1,0:T(8,128)S(1)}, f32[1,4,4,8,384]{4,3,2,1,0:T(8,128)}, u32[]{:S(2)}) copy-start(f32[1,4,4,8,384]{4,3,2,1,0:T(8,128)} %refs_4_.1) | copy-start | bytes 589828
  2.6 10.1 %collective-permute-start = (bf16[61,8,128]{2,1,0:T(8,128)(2,1)S(1)}, bf16[61,8,128]{2,1,0:T(8,128)(2,1)S(1)}, u32[]{:S(2)}, u32[]{:S(2)}) collective-permute-start(bf16[61,8,128]{2,1,0:T(8,128)(2,1)S(1)} %shard_map.123), channel_id=1, source_target_pairs={{0,4},{4,8},{8,12},{12,0},{1,5},{5,9},{9,13},{13,1},{2,6},{6,10},{... | collective-permute-start | bytes 374792 | tf_op jit(solution)/shard_map/ppermute | solution.py:582
  5.8 10.7 %collective-permute-start.1 = (bf16[61,8,128]{2,1,0:T(8,128)(2,1)S(1)}, bf16[61,8,128]{2,1,0:T(8,128)(2,1)S(1)}, u32[]{:S(2)}, u32[]{:S(2)}) collective-permute-start(bf16[61,8,128]{2,1,0:T(8,128)(2,1)S(1)} %shard_map.124), channel_id=1, source_target_pairs={{0,8},{4,12},{8,0},{12,4},{1,9},{5,13},{9,1},{13,5},{2,10},{6,14},... | collective-permute-start | bytes 374792 | tf_op jit(solution)/shard_map/ppermute | solution.py:582
  8.5 8.0 %collective-permute-start.2 = (bf16[61,8,128]{2,1,0:T(8,128)(2,1)S(1)}, bf16[61,8,128]{2,1,0:T(8,128)(2,1)S(1)}, u32[]{:S(2)}, u32[]{:S(2)}) collective-permute-start(bf16[61,8,128]{2,1,0:T(8,128)(2,1)S(1)} %shard_map.125), channel_id=1, source_target_pairs={{0,12},{4,0},{8,4},{12,8},{1,13},{5,1},{9,5},{13,9},{2,14},{6,2},{... | collective-permute-start | bytes 374792 | tf_op jit(solution)/shard_map/ppermute | solution.py:582
  10.4 7.3 %collective-permute-start.3 = (s16[2,21,16,128]{3,2,1,0:T(8,128)(2,1)S(1)}, s16[2,21,16,128]{3,2,1,0:T(8,128)(2,1)S(1)}, u32[]{:S(2)}, u32[]{:S(2)}) collective-permute-start(s16[2,21,16,128]{3,2,1,0:T(8,128)(2,1)S(1)} %get-tuple-element.36), channel_id=1, source_target_pairs={{0,1},{1,0},{2,3},{3,2},{4,5},{5,4},{6,7},{7,6},{8,9},{9,8},{10,11... | collective-permute-start | bytes 516104 | tf_op jit(solution)/shard_map/ppermute | solution.py:597
  10.5 7.2 %collective-permute-start.4 = (s16[2,21,16,128]{3,2,1,0:T(8,128)(2,1)S(1)}, s16[2,21,16,128]{3,2,1,0:T(8,128)(2,1)S(1)}, u32[]{:S(2)}, u32[]{:S(2)}) collective-permute-start(s16[2,21,16,128]{3,2,1,0:T(8,128)(2,1)S(1)} %get-tuple-element.37), channel_id=1, source_target_pairs={{1,2},{2,1},{5,6},{6,5},{9,10},{10,9},{13,14},{14,13},{17,18},{18,... | collective-permute-start | bytes 516104 | tf_op jit(solution)/shard_map/ppermute | solution.py:597
  16.9 3.9 %collective-permute-start.5 = (bf16[31,8,384]{2,1,0:T(8,128)(2,1)S(1)}, bf16[31,8,384]{2,1,0:T(8,128)(2,1)S(1)}, u32[]{:S(2)}, u32[]{:S(2)}) collective-permute-start(bf16[31,8,384]{2,1,0:T(8,128)(2,1)S(1)} %get-tuple-element.42), channel_id=1, source_target_pairs={{0,1},{1,0},{2,3},{3,2},{4,5},{5,4},{6,7},{7,6},{8,9},{9,8},{10,11... | collective-permute-start | bytes 571400 | tf_op jit(solution)/shard_map/ppermute | solution.py:597
  17.0 3.9 %collective-permute-start.6 = (bf16[31,8,384]{2,1,0:T(8,128)(2,1)S(1)}, bf16[31,8,384]{2,1,0:T(8,128)(2,1)S(1)}, u32[]{:S(2)}, u32[]{:S(2)}) collective-permute-start(bf16[31,8,384]{2,1,0:T(8,128)(2,1)S(1)} %get-tuple-element.43), channel_id=1, source_target_pairs={{1,2},{2,1},{5,6},{6,5},{9,10},{10,9},{13,14},{14,13},{17,18},{18,... | collective-permute-start | bytes 571400 | tf_op jit(solution)/shard_map/ppermute | solution.py:597
  18.0 8.3 %copy-start.5 = (f32[1,5,4,8,384]{4,3,2,1,0:T(8,128)S(1)}, f32[1,5,4,8,384]{4,3,2,1,0:T(8,128)}, u32[]{:S(2)}) copy-start(f32[1,5,4,8,384]{4,3,2,1,0:T(8,128)} %refs_7_.3) | copy-start | bytes 737284
  18.0 8.1 %collective-permute-start.7 = (s16[2,16,16,128]{3,2,1,0:T(8,128)(2,1)S(1)}, s16[2,16,16,128]{3,2,1,0:T(8,128)(2,1)S(1)}, u32[]{:S(2)}, u32[]{:S(2)}) collective-permute-start(s16[2,16,16,128]{3,2,1,0:T(8,128)(2,1)S(1)} %get-tuple-element.45), channel_id=1, source_target_pairs={{4,0},{8,4},{12,8},{5,1},{9,5},{13,9},{6,2},{10,6},{14,10},{7,3},{... | collective-permute-start | bytes 393224 | tf_op jit(solution)/shard_map/ppermute | solution.py:577
  19.4 13.6 %collective-permute-start.11 = (s16[2,16,16,128]{3,2,1,0:T(8,128)(2,1)S(1)}, s16[2,16,16,128]{3,2,1,0:T(8,128)(2,1)S(1)}, u32[]{:S(2)}, u32[]{:S(2)}) collective-permute-start(s16[2,16,16,128]{3,2,1,0:T(8,128)(2,1)S(1)} %get-tuple-element.52), channel_id=1, source_target_pairs={{4,0},{8,4},{12,8},{5,1},{9,5},{13,9},{6,2},{10,6},{14,10},{7,3},{... | collective-permute-start | bytes 393224 | tf_op jit(solution)/shard_map/ppermute | solution.py:577
  27.4 10.7 %collective-permute-start.8 = (s16[16,16,128]{2,1,0:T(8,128)(2,1)S(1)}, s16[16,16,128]{2,1,0:T(8,128)(2,1)S(1)}, u32[]{:S(2)}, u32[]{:S(2)}) collective-permute-start(s16[16,16,128]{2,1,0:T(8,128)(2,1)S(1)} %get-tuple-element.49), channel_id=1, source_target_pairs={{0,12},{4,8},{8,4},{12,0},{1,13},{5,9},{9,5},{13,1},{2,14},{6,10},... | collective-permute-start | bytes 196616 | tf_op jit(solution)/shard_map/ppermute | solution.py:586
  32.3 6.7 %collective-permute-start.9 = (s16[16,16,128]{2,1,0:T(8,128)(2,1)S(1)}, s16[16,16,128]{2,1,0:T(8,128)(2,1)S(1)}, u32[]{:S(2)}, u32[]{:S(2)}) collective-permute-start(s16[16,16,128]{2,1,0:T(8,128)(2,1)S(1)} %get-tuple-element.50), channel_id=1, source_target_pairs={{0,8},{4,12},{8,0},{12,4},{1,9},{5,13},{9,1},{13,5},{2,10},{6,14},... | collective-permute-start | bytes 196616 | tf_op jit(solution)/shard_map/ppermute | solution.py:586
  32.3 6.7 %collective-permute-start.10 = (s16[16,16,128]{2,1,0:T(8,128)(2,1)S(1)}, s16[16,16,128]{2,1,0:T(8,128)(2,1)S(1)}, u32[]{:S(2)}, u32[]{:S(2)}) collective-permute-start(s16[16,16,128]{2,1,0:T(8,128)(2,1)S(1)} %get-tuple-element.51), channel_id=1, source_target_pairs={{0,4},{4,0},{8,12},{12,8},{1,5},{5,1},{9,13},{13,9},{2,6},{6,2},{1... | collective-permute-start | bytes 196616 | tf_op jit(solution)/shard_map/ppermute | solution.py:586
  34.3 6.2 %collective-permute-start.12 = (s16[16,16,128]{2,1,0:T(8,128)(2,1)S(1)}, s16[16,16,128]{2,1,0:T(8,128)(2,1)S(1)}, u32[]{:S(2)}, u32[]{:S(2)}) collective-permute-start(s16[16,16,128]{2,1,0:T(8,128)(2,1)S(1)} %get-tuple-element.56), channel_id=1, source_target_pairs={{0,12},{4,8},{8,4},{12,0},{1,13},{5,9},{9,5},{13,1},{2,14},{6,10},... | collective-permute-start | bytes 196616 | tf_op jit(solution)/shard_map/ppermute | solution.py:586
  38.1 6.3 %collective-permute-start.13 = (s16[16,16,128]{2,1,0:T(8,128)(2,1)S(1)}, s16[16,16,128]{2,1,0:T(8,128)(2,1)S(1)}, u32[]{:S(2)}, u32[]{:S(2)}) collective-permute-start(s16[16,16,128]{2,1,0:T(8,128)(2,1)S(1)} %get-tuple-element.57), channel_id=1, source_target_pairs={{0,8},{4,12},{8,0},{12,4},{1,9},{5,13},{9,1},{13,5},{2,10},{6,14},... | collective-permute-start | bytes 196616 | tf_op jit(solution)/shard_map/ppermute | solution.py:586
  38.1 6.3 %collective-permute-start.14 = (s16[16,16,128]{2,1,0:T(8,128)(2,1)S(1)}, s16[16,16,128]{2,1,0:T(8,128)(2,1)S(1)}, u32[]{:S(2)}, u32[]{:S(2)}) collective-permute-start(s16[16,16,128]{2,1,0:T(8,128)(2,1)S(1)} %get-tuple-element.58), channel_id=1, source_target_pairs={{0,4},{4,0},{8,12},{12,8},{1,5},{5,1},{9,13},{13,9},{2,6},{6,2},{1... | collective-permute-start | bytes 196616 | tf_op jit(solution)/shard_map/ppermute | solution.py:586

commit v17 on v16

--- a/solution.py
+++ b/solution.py
@@ -105,7 +105,7 @@
 
 
 def partners(windows):
-    return list(range(windows - 1, 0, -1))
+    return list(range(1, windows))
 
 
 def pack_kernel(ways, windows, steps, nvar, levels, part, var_ref, traj_ref, *outs):

time: 45.7 us -> 46.8 us (1.024)
  waiting for transfers between devices: 11.9 us -> 13.1 us
    ppermute x6, waiting for transfers between devices: 5.64 us -> 6.8 us  [exchanged(): lax.ppermute(block, axis, [(i, i ^ mask) for i in range(lax.axis_size(axi...]
  transfers between devices with their start and end apart: 15 -> 15, of which waited for: 5 -> 6; matrix products, arithmetic and copies ran while one was open for 0% -> 0% of each run, Pallas kernels for 17% -> 16%
where the time goes in v17:
time: 46.8 us; the launch traced here: 46.5 us
  starting transfers between devices  21.3 us (46%)
  waiting for transfers between devices  13.1 us (28%)
  Pallas kernels  8.79 us (19%)
  local copies, waits for them, and re-layouts  1.82 us (4%)
  between operations  1.54 us (3%)
    ppermute x6, starting transfers between devices, exchanged(): lax.ppermute(block, axis, [(i, i ^ mask) for i in range(lax.axis_size(axi...  9.94 us
    ppermute x3, starting transfers between devices, rotated(): lax.ppermute(block, axis, [(i, (i + distance) % count) for i in range(cou...  7.13 us
    ppermute x6, waiting for transfers between devices, exchanged(): lax.ppermute(block, axis, [(i, i ^ mask) for i in range(lax.axis_size(axi...  6.8 us
    ppermute x3, waiting for transfers between devices, rotated(): lax.ppermute(block, axis, [(i, (i + distance) % count) for i in range(cou...  3.81 us
    pallas_call x1, Pallas kernels, body(): pl.pallas_call(lambda *refs: tangent_kernel(spaces, steps, nvar, levels,...  2.78 us
    ppermute x2, starting transfers between devices, moved(): lax.ppermute(block, axis, [(i, i + distance) for i in devices if i + dist...  2.72 us
    ppermute x2, waiting for transfers between devices, moved(): lax.ppermute(block, axis, [(i, i + distance) for i in devices if i + dist...  2.45 us
    pallas_call x2, Pallas kernels, body(): pl.pallas_call(lambda *refs, i=i: adjoint_kernel(i, windows, spaces, step...  2.33 us
  transfers between devices with their start and end apart: 15, of which 6 were waited for; matrix products, arithmetic and copies ran while one was open for 0% of the time, Pallas kernels for 16%

profile of v17, /device:TPU:0, one launch (start us, length us, event | category | flops | bytes accessed | tf_op | source)
XLA Modules:
  0.0 46.5 jit_solution(8619899593333257335)
XLA Ops:
  0.7 0.7 %pad.4.refs_0_ = f32[8,128]{1,0:T(8,128)S(1)} pad(f32[4,5]{1,0:T(4,128)} %bitcast.3, f32[]{:T(128)} %constant.2.clone.1), padding=0_4x0_123 | pad | bytes 4180 | tf_op jit(solution)/shard_map/jit(_pad)/pad | solution.py:627
  1.4 1.1 %copy-done = bf16[4,4,5,4,8,96]{5,4,3,2,1,0:T(8,128)(2,1)S(1)} copy-done((bf16[4,4,5,4,8,96]{5,4,3,2,1,0:T(8,128)(2,1)S(1)}, bf16[4,4,5,4,8,96]{5,4,3,2,1,0:T(8,128)(2,1)}, u32[]{:S(2)}) %copy-start) | copy-done | bytes 491544
  2.5 0.1 shard_map.123
  2.6 3.1 %collective-permute-start = (bf16[61,8,128]{2,1,0:T(8,128)(2,1)S(1)}, bf16[61,8,128]{2,1,0:T(8,128)(2,1)S(1)}, u32[]{:S(2)}, u32[]{:S(2)}) collective-permute-start(bf16[61,8,128]{2,1,0:T(8,128)(2,1)S(1)} %shard_map.123), channel_id=1, source_target_pairs={{0,4},{4,8},{8,12},{12,0},{1,5},{5,9},{9,13},{13,1},{2,6},{6,10},{... | collective-permute-start | bytes 374792 | tf_op jit(solution)/shard_map/ppermute | solution.py:582
  5.8 2.7 %collective-permute-start.1 = (bf16[61,8,128]{2,1,0:T(8,128)(2,1)S(1)}, bf16[61,8,128]{2,1,0:T(8,128)(2,1)S(1)}, u32[]{:S(2)}, u32[]{:S(2)}) collective-permute-start(bf16[61,8,128]{2,1,0:T(8,128)(2,1)S(1)} %shard_map.124), channel_id=1, source_target_pairs={{0,8},{4,12},{8,0},{12,4},{1,9},{5,13},{9,1},{13,5},{2,10},{6,14},... | collective-permute-start | bytes 374792 | tf_op jit(solution)/shard_map/ppermute | solution.py:582
  8.5 1.4 %collective-permute-start.2 = (bf16[61,8,128]{2,1,0:T(8,128)(2,1)S(1)}, bf16[61,8,128]{2,1,0:T(8,128)(2,1)S(1)}, u32[]{:S(2)}, u32[]{:S(2)}) collective-permute-start(bf16[61,8,128]{2,1,0:T(8,128)(2,1)S(1)} %shard_map.125), channel_id=1, source_target_pairs={{0,12},{4,0},{8,4},{12,8},{1,13},{5,1},{9,5},{13,9},{2,14},{6,2},{... | collective-permute-start | bytes 374792 | tf_op jit(solution)/shard_map/ppermute | solution.py:582
  10.0 0.5 %shard_map.126 = (s16[2,21,16,128]{3,2,1,0:T(8,128)(2,1)S(1)}, s16[2,21,16,128]{3,2,1,0:T(8,128)(2,1)S(1)}, s16[2,16,16,128]{3,2,1,0:T(8,128)(2,1)S(1)}) custom-call(f32[1,5,4,8,384]{4,3,2,1,0:T(8,128)S(1)} %copy-done.4, f32[1,5,4,8,384]{4,3,2,1,0:T(8,128)S(1)} %copy-done.2, f32[1,4,4,8,384]{4,3,2,1,0:T(8,128)S(1)} %copy-done.3), custom_call_target="tpu_custom_call" | custom-call | tf_op jit(solution)/shard_map/pallas_call | solution.py:651
  10.5 0.7 %collective-permute-start.4 = (s16[2,21,16,128]{3,2,1,0:T(8,128)(2,1)S(1)}, s16[2,21,16,128]{3,2,1,0:T(8,128)(2,1)S(1)}, u32[]{:S(2)}, u32[]{:S(2)}) collective-permute-start(s16[2,21,16,128]{3,2,1,0:T(8,128)(2,1)S(1)} %get-tuple-element.37), channel_id=1, source_target_pairs={{1,2},{2,1},{5,6},{6,5},{9,10},{10,9},{13,14},{14,13},{17,18},{18,... | collective-permute-start | bytes 516104 | tf_op jit(solution)/shard_map/ppermute | solution.py:597
  11.2 0.1 shard_map.122.refs_0_
  12.0 0.7 %shard_map.121 = (f32[4,4,3,8,128]{4,3,2,1,0:T(8,128)S(1)}, f32[4,4,8,128]{3,2,1,0:T(8,128)S(1)}, f32[5,5,8,128]{3,2,1,0:T(8,128)S(1)}) custom-call(s32[1]{0:T(128)S(6)} %copy.13.refs_0_, f32[1,4,4]{2,1,0:T(4,128)S(1)} %copy-done.8, f32[5,5]{1,0:T(8,128)S(1)} %copy-done.7, f32[1,4,4,8,384]{4,3,2,1,0:T(8,128)S(1)} %copy-done.3, f32[1,4,4,8,384]{4,3,2,1,0:T(8,128)S(1)} %copy-done.6), custom_call_target="tpu_custom_call" | custom-call | tf_op jit(solution)/shard_map/pallas_call | solution.py:671
  12.7 3.8 %collective-permute-done.1.refs_2_ = bf16[61,8,128]{2,1,0:T(8,128)(2,1)S(1)} collective-permute-done((bf16[61,8,128]{2,1,0:T(8,128)(2,1)S(1)}, bf16[61,8,128]{2,1,0:T(8,128)(2,1)S(1)}, u32[]{:S(2)}, u32[]{:S(2)}) %collective-permute-start.1) | collective-permute-done | bytes 124960 | tf_op jit(solution)/shard_map/ppermute | solution.py:582
  16.5 0.4 shard_map.128
  17.0 0.7 %collective-permute-start.6 = (bf16[31,8,384]{2,1,0:T(8,128)(2,1)S(1)}, bf16[31,8,384]{2,1,0:T(8,128)(2,1)S(1)}, u32[]{:S(2)}, u32[]{:S(2)}) collective-permute-start(bf16[31,8,384]{2,1,0:T(8,128)(2,1)S(1)} %get-tuple-element.43), channel_id=1, source_target_pairs={{1,2},{2,1},{5,6},{6,5},{9,10},{10,9},{13,14},{14,13},{17,18},{18,... | collective-permute-start | bytes 571400 | tf_op jit(solution)/shard_map/ppermute | solution.py:597
  17.7 0.3 shard_map.127
  18.0 1.4 %collective-permute-start.7 = (s16[2,16,16,128]{3,2,1,0:T(8,128)(2,1)S(1)}, s16[2,16,16,128]{3,2,1,0:T(8,128)(2,1)S(1)}, u32[]{:S(2)}, u32[]{:S(2)}) collective-permute-start(s16[2,16,16,128]{3,2,1,0:T(8,128)(2,1)S(1)} %get-tuple-element.45), channel_id=1, source_target_pairs={{4,0},{8,4},{12,8},{5,1},{9,5},{13,9},{6,2},{10,6},{14,10},{7,3},{... | collective-permute-start | bytes 393224 | tf_op jit(solution)/shard_map/ppermute | solution.py:577
  19.4 1.3 %collective-permute-start.11 = (s16[2,16,16,128]{3,2,1,0:T(8,128)(2,1)S(1)}, s16[2,16,16,128]{3,2,1,0:T(8,128)(2,1)S(1)}, u32[]{:S(2)}, u32[]{:S(2)}) collective-permute-start(s16[2,16,16,128]{3,2,1,0:T(8,128)(2,1)S(1)} %get-tuple-element.52), channel_id=1, source_target_pairs={{4,0},{8,4},{12,8},{5,1},{9,5},{13,9},{6,2},{10,6},{14,10},{7,3},{... | collective-permute-start | bytes 393224 | tf_op jit(solution)/shard_map/ppermute | solution.py:577
  20.7 0.1 shard_map.129.refs_6_
  20.9 2.8 %shard_map.130 = (f32[1,4,4,8,384]{4,3,2,1,0:T(8,128)}, f32[4,5,3,8,128]{4,3,2,1,0:T(8,128)S(1)}, f32[4,4,5,3,16,128]{5,4,3,2,1,0:T(8,128)S(1)}) custom-call(f32[5,5,8,128]{3,2,1,0:T(8,128)S(1)} %get-tuple-element.34.refs_4_.refs_0_, f32[4,4,8,128]{3,2,1,0:T(8,128)S(1)} %get-tuple-element.39.refs_1_, f32[4,4,3,8,128]{4,3,2,1,0:T(8,128)S(1)} %get-tuple-element.40.refs_2_, ...), custom_call_target="tpu_custom_call" | custom-call | tf_op jit(solution)/shard_map/pallas_call | solution.py:704
  23.7 2.4 %collective-permute-done.7.refs_4_ = s16[2,16,16,128]{3,2,1,0:T(8,128)(2,1)S(1)} collective-permute-done((s16[2,16,16,128]{3,2,1,0:T(8,128)(2,1)S(1)}, s16[2,16,16,128]{3,2,1,0:T(8,128)(2,1)S(1)}, u32[]{:S(2)}, u32[]{:S(2)}) %collective-permute-start.7) | collective-permute-done | bytes 131104 | tf_op jit(solution)/shard_map/ppermute | solution.py:577
  26.1 0.1 shard_map.131
  26.3 1.2 %shard_map.132 = (f32[5,2,8,384]{3,2,1,0:T(8,128)S(1)}, f32[5,2,8,384]{3,2,1,0:T(8,128)S(1)}, s16[16,16,128]{2,1,0:T(8,128)(2,1)S(1)}, s16[16,16,128]{2,1,0:T(8,128)(2,1)S(1)}, s16[16,16,128]{2,1,0:T(8,128)(2,1)S(1)}) custom-call(f32[5,5,8,128]{3,2,1,0:T(8,128)S(1)} %get-tuple-element.34.refs_4_.refs_0_, ...), custom_call_target="tpu_custom_call" | custom-call | tf_op jit(solution)/shard_map/pallas_call | solution.py:729
  27.4 2.1 %collective-permute-start.8 = (s16[16,16,128]{2,1,0:T(8,128)(2,1)S(1)}, s16[16,16,128]{2,1,0:T(8,128)(2,1)S(1)}, u32[]{:S(2)}, u32[]{:S(2)}) collective-permute-start(s16[16,16,128]{2,1,0:T(8,128)(2,1)S(1)} %get-tuple-element.49), channel_id=1, source_target_pairs={{0,4},{4,0},{8,12},{12,8},{1,5},{5,1},{9,13},{13,9},{2,6},{6,2},{1... | collective-permute-start | bytes 196616 | tf_op jit(solution)/shard_map/ppermute | solution.py:586
  29.5 3.4 %collective-permute-start.9 = (s16[16,16,128]{2,1,0:T(8,128)(2,1)S(1)}, s16[16,16,128]{2,1,0:T(8,128)(2,1)S(1)}, u32[]{:S(2)}, u32[]{:S(2)}) collective-permute-start(s16[16,16,128]{2,1,0:T(8,128)(2,1)S(1)} %get-tuple-element.50), channel_id=1, source_target_pairs={{0,8},{4,12},{8,0},{12,4},{1,9},{5,13},{9,1},{13,5},{2,10},{6,14},... | collective-permute-start | bytes 196616 | tf_op jit(solution)/shard_map/ppermute | solution.py:586
  32.9 0.1 shard_map.133
  33.0 1.2 %shard_map.134 = (f32[5,2,8,384]{3,2,1,0:T(8,128)S(1)}, f32[5,2,8,384]{3,2,1,0:T(8,128)S(1)}, s16[16,16,128]{2,1,0:T(8,128)(2,1)S(1)}, s16[16,16,128]{2,1,0:T(8,128)(2,1)S(1)}, s16[16,16,128]{2,1,0:T(8,128)(2,1)S(1)}) custom-call(f32[5,5,8,128]{3,2,1,0:T(8,128)S(1)} %get-tuple-element.34.refs_4_.refs_0_, ...), custom_call_target="tpu_custom_call" | custom-call | tf_op jit(solution)/shard_map/pallas_call | solution.py:729
  34.2 0.6 %collective-permute-start.12 = (s16[16,16,128]{2,1,0:T(8,128)(2,1)S(1)}, s16[16,16,128]{2,1,0:T(8,128)(2,1)S(1)}, u32[]{:S(2)}, u32[]{:S(2)}) collective-permute-start(s16[16,16,128]{2,1,0:T(8,128)(2,1)S(1)} %get-tuple-element.56), channel_id=1, source_target_pairs={{0,4},{4,0},{8,12},{12,8},{1,5},{5,1},{9,13},{13,9},{2,6},{6,2},{1... | collective-permute-start | bytes 196616 | tf_op jit(solution)/shard_map/ppermute | solution.py:586
  34.8 3.8 %collective-permute-start.13 = (s16[16,16,128]{2,1,0:T(8,128)(2,1)S(1)}, s16[16,16,128]{2,1,0:T(8,128)(2,1)S(1)}, u32[]{:S(2)}, u32[]{:S(2)}) collective-permute-start(s16[16,16,128]{2,1,0:T(8,128)(2,1)S(1)} %get-tuple-element.57), channel_id=1, source_target_pairs={{0,8},{4,12},{8,0},{12,4},{1,9},{5,13},{9,1},{13,5},{2,10},{6,14},... | collective-permute-start | bytes 196616 | tf_op jit(solution)/shard_map/ppermute | solution.py:586
  38.7 0.5 collective-permute-done.10.refs_2_
  39.1 1.9 %collective-permute-done.12.refs_3_ = s16[16,16,128]{2,1,0:T(8,128)(2,1)S(1)} collective-permute-done((s16[16,16,128]{2,1,0:T(8,128)(2,1)S(1)}, s16[16,16,128]{2,1,0:T(8,128)(2,1)S(1)}, u32[]{:S(2)}, u32[]{:S(2)}) %collective-permute-start.12) | collective-permute-done | bytes 65568 | tf_op jit(solution)/shard_map/ppermute | solution.py:586
  41.0 1.6 %collective-permute-done.13.refs_4_ = s16[16,16,128]{2,1,0:T(8,128)(2,1)S(1)} collective-permute-done((s16[16,16,128]{2,1,0:T(8,128)(2,1)S(1)}, s16[16,16,128]{2,1,0:T(8,128)(2,1)S(1)}, u32[]{:S(2)}, u32[]{:S(2)}) %collective-permute-start.13) | collective-permute-done | bytes 65568 | tf_op jit(solution)/shard_map/ppermute | solution.py:586
  42.7 2.8 %collective-permute-done.14.refs_5_ = s16[16,16,128]{2,1,0:T(8,128)(2,1)S(1)} collective-permute-done((s16[16,16,128]{2,1,0:T(8,128)(2,1)S(1)}, s16[16,16,128]{2,1,0:T(8,128)(2,1)S(1)}, u32[]{:S(2)}, u32[]{:S(2)}) %collective-permute-start.14) | collective-permute-done | bytes 65568 | tf_op jit(solution)/shard_map/ppermute | solution.py:586
  45.5 1.0 %shard_map.135 = (f32[1,5,4,8,384]{4,3,2,1,0:T(8,128)}, f32[1,5,4,8,384]{4,3,2,1,0:T(8,128)}) custom-call(s16[16,16,128]{2,1,0:T(8,128)(2,1)S(1)} %collective-permute-done.8.refs_0_, s16[16,16,128]{2,1,0:T(8,128)(2,1)S(1)} %collective-permute-done.9.refs_1_, s16[16,16,128]{2,1,0:T(8,128)(2,1)S(1)} %collective-permute-done.10.refs_2_, ...), custom_call_target="tpu_custom_call" | custom-call | tf_op jit(solution)/shard_map/pallas_call | solution.py:751
  (32 shorter events, 0.4 us)
Async XLA Ops:
  0.6 11.3 %copy-start.8 = (f32[1,4,4]{2,1,0:T(4,128)S(1)}, f32[1,4,4]{2,1,0:T(4,128)}, u32[]{:S(2)}) copy-start(f32[1,4,4]{2,1,0:T(4,128)} %refs_1_.6) | copy-start | bytes 196
  0.6 11.3 %copy-start.7 = (f32[5,5]{1,0:T(8,128)S(1)}, f32[5,5]{1,0:T(8,128)}, u32[]{:S(2)}) copy-start(f32[5,5]{1,0:T(8,128)} %refs_2_.3) | copy-start | bytes 304
  1.3 1.1 %copy-start = (bf16[4,4,5,4,8,96]{5,4,3,2,1,0:T(8,128)(2,1)S(1)}, bf16[4,4,5,4,8,96]{5,4,3,2,1,0:T(8,128)(2,1)}, u32[]{:S(2)}) copy-start(bf16[4,4,5,4,8,96]{5,4,3,2,1,0:T(8,128)(2,1)} %refs_1_.10) | copy-start | bytes 1474564
  2.4 7.5 %copy-start.2 = (f32[1,5,4,8,384]{4,3,2,1,0:T(8,128)S(1)}, f32[1,5,4,8,384]{4,3,2,1,0:T(8,128)}, u32[]{:S(2)}) copy-start(f32[1,5,4,8,384]{4,3,2,1,0:T(8,128)} %refs_6_.3) | copy-start | bytes 737284
  2.4 7.5 %copy-start.3 = (f32[1,4,4,8,384]{4,3,2,1,0:T(8,128)S(1)}, f32[1,4,4,8,384]{4,3,2,1,0:T(8,128)}, u32[]{:S(2)}) copy-start(f32[1,4,4,8,384]{4,3,2,1,0:T(8,128)} %refs_3_.5) | copy-start | bytes 589828
  2.4 7.5 %copy-start.4 = (f32[1,5,4,8,384]{4,3,2,1,0:T(8,128)S(1)}, f32[1,5,4,8,384]{4,3,2,1,0:T(8,128)}, u32[]{:S(2)}) copy-start(f32[1,5,4,8,384]{4,3,2,1,0:T(8,128)} %refs_8_.3) | copy-start | bytes 737284
  2.4 8.7 %copy-start.1 = (bf16[4,4,5,4,8,96]{5,4,3,2,1,0:T(8,128)(2,1)S(1)}, bf16[4,4,5,4,8,96]{5,4,3,2,1,0:T(8,128)(2,1)}, u32[]{:S(2)}) copy-start(bf16[4,4,5,4,8,96]{5,4,3,2,1,0:T(8,128)(2,1)} %refs_1_.10) | copy-start | bytes 1474564
  2.4 9.5 %copy-start.6 = (f32[1,4,4,8,384]{4,3,2,1,0:T(8,128)S(1)}, f32[1,4,4,8,384]{4,3,2,1,0:T(8,128)}, u32[]{:S(2)}) copy-start(f32[1,4,4,8,384]{4,3,2,1,0:T(8,128)} %refs_4_.1) | copy-start | bytes 589828
  2.6 10.1 %collective-permute-start = (bf16[61,8,128]{2,1,0:T(8,128)(2,1)S(1)}, bf16[61,8,128]{2,1,0:T(8,128)(2,1)S(1)}, u32[]{:S(2)}, u32[]{:S(2)}) collective-permute-start(bf16[61,8,128]{2,1,0:T(8,128)(2,1)S(1)} %shard_map.123), channel_id=1, source_target_pairs={{0,4},{4,8},{8,12},{12,0},{1,5},{5,9},{9,13},{13,1},{2,6},{6,10},{... | collective-permute-start | bytes 374792 | tf_op jit(solution)/shard_map/ppermute | solution.py:582
  5.8 10.7 %collective-permute-start.1 = (bf16[61,8,128]{2,1,0:T(8,128)(2,1)S(1)}, bf16[61,8,128]{2,1,0:T(8,128)(2,1)S(1)}, u32[]{:S(2)}, u32[]{:S(2)}) collective-permute-start(bf16[61,8,128]{2,1,0:T(8,128)(2,1)S(1)} %shard_map.124), channel_id=1, source_target_pairs={{0,8},{4,12},{8,0},{12,4},{1,9},{5,13},{9,1},{13,5},{2,10},{6,14},... | collective-permute-start | bytes 374792 | tf_op jit(solution)/shard_map/ppermute | solution.py:582
  8.5 8.0 %collective-permute-start.2 = (bf16[61,8,128]{2,1,0:T(8,128)(2,1)S(1)}, bf16[61,8,128]{2,1,0:T(8,128)(2,1)S(1)}, u32[]{:S(2)}, u32[]{:S(2)}) collective-permute-start(bf16[61,8,128]{2,1,0:T(8,128)(2,1)S(1)} %shard_map.125), channel_id=1, source_target_pairs={{0,12},{4,0},{8,4},{12,8},{1,13},{5,1},{9,5},{13,9},{2,14},{6,2},{... | collective-permute-start | bytes 374792 | tf_op jit(solution)/shard_map/ppermute | solution.py:582
  10.4 7.3 %collective-permute-start.3 = (s16[2,21,16,128]{3,2,1,0:T(8,128)(2,1)S(1)}, s16[2,21,16,128]{3,2,1,0:T(8,128)(2,1)S(1)}, u32[]{:S(2)}, u32[]{:S(2)}) collective-permute-start(s16[2,21,16,128]{3,2,1,0:T(8,128)(2,1)S(1)} %get-tuple-element.36), channel_id=1, source_target_pairs={{0,1},{1,0},{2,3},{3,2},{4,5},{5,4},{6,7},{7,6},{8,9},{9,8},{10,11... | collective-permute-start | bytes 516104 | tf_op jit(solution)/shard_map/ppermute | solution.py:597
  10.5 7.2 %collective-permute-start.4 = (s16[2,21,16,128]{3,2,1,0:T(8,128)(2,1)S(1)}, s16[2,21,16,128]{3,2,1,0:T(8,128)(2,1)S(1)}, u32[]{:S(2)}, u32[]{:S(2)}) collective-permute-start(s16[2,21,16,128]{3,2,1,0:T(8,128)(2,1)S(1)} %get-tuple-element.37), channel_id=1, source_target_pairs={{1,2},{2,1},{5,6},{6,5},{9,10},{10,9},{13,14},{14,13},{17,18},{18,... | collective-permute-start | bytes 516104 | tf_op jit(solution)/shard_map/ppermute | solution.py:597
  16.9 3.9 %collective-permute-start.5 = (bf16[31,8,384]{2,1,0:T(8,128)(2,1)S(1)}, bf16[31,8,384]{2,1,0:T(8,128)(2,1)S(1)}, u32[]{:S(2)}, u32[]{:S(2)}) collective-permute-start(bf16[31,8,384]{2,1,0:T(8,128)(2,1)S(1)} %get-tuple-element.42), channel_id=1, source_target_pairs={{0,1},{1,0},{2,3},{3,2},{4,5},{5,4},{6,7},{7,6},{8,9},{9,8},{10,11... | collective-permute-start | bytes 571400 | tf_op jit(solution)/shard_map/ppermute | solution.py:597
  17.0 3.9 %collective-permute-start.6 = (bf16[31,8,384]{2,1,0:T(8,128)(2,1)S(1)}, bf16[31,8,384]{2,1,0:T(8,128)(2,1)S(1)}, u32[]{:S(2)}, u32[]{:S(2)}) collective-permute-start(bf16[31,8,384]{2,1,0:T(8,128)(2,1)S(1)} %get-tuple-element.43), channel_id=1, source_target_pairs={{1,2},{2,1},{5,6},{6,5},{9,10},{10,9},{13,14},{14,13},{17,18},{18,... | collective-permute-start | bytes 571400 | tf_op jit(solution)/shard_map/ppermute | solution.py:597
  18.0 8.3 %copy-start.5 = (f32[1,5,4,8,384]{4,3,2,1,0:T(8,128)S(1)}, f32[1,5,4,8,384]{4,3,2,1,0:T(8,128)}, u32[]{:S(2)}) copy-start(f32[1,5,4,8,384]{4,3,2,1,0:T(8,128)} %refs_7_.3) | copy-start | bytes 737284
  18.0 8.1 %collective-permute-start.7 = (s16[2,16,16,128]{3,2,1,0:T(8,128)(2,1)S(1)}, s16[2,16,16,128]{3,2,1,0:T(8,128)(2,1)S(1)}, u32[]{:S(2)}, u32[]{:S(2)}) collective-permute-start(s16[2,16,16,128]{3,2,1,0:T(8,128)(2,1)S(1)} %get-tuple-element.45), channel_id=1, source_target_pairs={{4,0},{8,4},{12,8},{5,1},{9,5},{13,9},{6,2},{10,6},{14,10},{7,3},{... | collective-permute-start | bytes 393224 | tf_op jit(solution)/shard_map/ppermute | solution.py:577
  19.4 13.5 %collective-permute-start.11 = (s16[2,16,16,128]{3,2,1,0:T(8,128)(2,1)S(1)}, s16[2,16,16,128]{3,2,1,0:T(8,128)(2,1)S(1)}, u32[]{:S(2)}, u32[]{:S(2)}) collective-permute-start(s16[2,16,16,128]{3,2,1,0:T(8,128)(2,1)S(1)} %get-tuple-element.52), channel_id=1, source_target_pairs={{4,0},{8,4},{12,8},{5,1},{9,5},{13,9},{6,2},{10,6},{14,10},{7,3},{... | collective-permute-start | bytes 393224 | tf_op jit(solution)/shard_map/ppermute | solution.py:577
  27.4 11.2 %collective-permute-start.8 = (s16[16,16,128]{2,1,0:T(8,128)(2,1)S(1)}, s16[16,16,128]{2,1,0:T(8,128)(2,1)S(1)}, u32[]{:S(2)}, u32[]{:S(2)}) collective-permute-start(s16[16,16,128]{2,1,0:T(8,128)(2,1)S(1)} %get-tuple-element.49), channel_id=1, source_target_pairs={{0,4},{4,0},{8,12},{12,8},{1,5},{5,1},{9,13},{13,9},{2,6},{6,2},{1... | collective-permute-start | bytes 196616 | tf_op jit(solution)/shard_map/ppermute | solution.py:586
  29.5 9.2 %collective-permute-start.9 = (s16[16,16,128]{2,1,0:T(8,128)(2,1)S(1)}, s16[16,16,128]{2,1,0:T(8,128)(2,1)S(1)}, u32[]{:S(2)}, u32[]{:S(2)}) collective-permute-start(s16[16,16,128]{2,1,0:T(8,128)(2,1)S(1)} %get-tuple-element.50), channel_id=1, source_target_pairs={{0,8},{4,12},{8,0},{12,4},{1,9},{5,13},{9,1},{13,5},{2,10},{6,14},... | collective-permute-start | bytes 196616 | tf_op jit(solution)/shard_map/ppermute | solution.py:586
  32.9 6.2 %collective-permute-start.10 = (s16[16,16,128]{2,1,0:T(8,128)(2,1)S(1)}, s16[16,16,128]{2,1,0:T(8,128)(2,1)S(1)}, u32[]{:S(2)}, u32[]{:S(2)}) collective-permute-start(s16[16,16,128]{2,1,0:T(8,128)(2,1)S(1)} %get-tuple-element.51), channel_id=1, source_target_pairs={{0,12},{4,8},{8,4},{12,0},{1,13},{5,9},{9,5},{13,1},{2,14},{6,10},... | collective-permute-start | bytes 196616 | tf_op jit(solution)/shard_map/ppermute | solution.py:586
  34.2 6.8 %collective-permute-start.12 = (s16[16,16,128]{2,1,0:T(8,128)(2,1)S(1)}, s16[16,16,128]{2,1,0:T(8,128)(2,1)S(1)}, u32[]{:S(2)}, u32[]{:S(2)}) collective-permute-start(s16[16,16,128]{2,1,0:T(8,128)(2,1)S(1)} %get-tuple-element.56), channel_id=1, source_target_pairs={{0,4},{4,0},{8,12},{12,8},{1,5},{5,1},{9,13},{13,9},{2,6},{6,2},{1... | collective-permute-start | bytes 196616 | tf_op jit(solution)/shard_map/ppermute | solution.py:586
  34.8 7.8 %collective-permute-start.13 = (s16[16,16,128]{2,1,0:T(8,128)(2,1)S(1)}, s16[16,16,128]{2,1,0:T(8,128)(2,1)S(1)}, u32[]{:S(2)}, u32[]{:S(2)}) collective-permute-start(s16[16,16,128]{2,1,0:T(8,128)(2,1)S(1)} %get-tuple-element.57), channel_id=1, source_target_pairs={{0,8},{4,12},{8,0},{12,4},{1,9},{5,13},{9,1},{13,5},{2,10},{6,14},... | collective-permute-start | bytes 196616 | tf_op jit(solution)/shard_map/ppermute | solution.py:586
  38.7 6.8 %collective-permute-start.14 = (s16[16,16,128]{2,1,0:T(8,128)(2,1)S(1)}, s16[16,16,128]{2,1,0:T(8,128)(2,1)S(1)}, u32[]{:S(2)}, u32[]{:S(2)}) collective-permute-start(s16[16,16,128]{2,1,0:T(8,128)(2,1)S(1)} %get-tuple-element.58), channel_id=1, source_target_pairs={{0,12},{4,8},{8,4},{12,0},{1,13},{5,9},{9,5},{13,1},{2,14},{6,10},... | collective-permute-start | bytes 196616 | tf_op jit(solution)/shard_map/ppermute | solution.py:586

commit v18 on v16

--- a/solution.py
+++ b/solution.py
@@ -180,11 +180,20 @@
     return whole[SUB:] if n % 2 else whole[:SUB]
 
 
-def around_kernel(windows, nvar, levels, *refs):
-    pieces, (own_ref, near_ref, far_ref) = refs[:windows], refs[windows : windows + 3]
-    outs, total_ref = refs[windows + 3 : -1], refs[-1]
+def around_kernel(i, own_ref, near_ref, far_ref, *refs):
+    out_ref = refs[-1]
+    even = even_place()
+    for n in range(own_ref.shape[1]):
+        own = floats(own_ref[i, n])
+        near, far = half_tile(near_ref, i, n), half_tile(far_ref, i, n)
+        for odd in range(2):
+            halves = widened(own[odd * SUB : (odd + 1) * SUB], near, far, odd, even)
+            out_ref[odd, n] = shorts(jnp.concatenate(halves, 0))
+
+
+def total_kernel(windows, nvar, levels, *refs):
+    pieces, total_ref = refs[:windows], refs[-1]
     me = lax.axis_index("window")
-    even = even_place()
     total = jnp.zeros((SUB, LANES), jnp.float32)
     for d in range(windows):
         split = pieces[d][pieces[d].shape[0] - 1].astype(jnp.float32)
@@ -194,13 +203,6 @@
         for lev in range(levels):
             one = total[lev : lev + 1, v : v + 1]
             total_ref[v * levels + lev] = jnp.broadcast_to(one, (SUB, LANES))
-    for i, out_ref in enumerate(outs):
-        for n in range(own_ref.shape[1]):
-            own = floats(own_ref[i, n])
-            near, far = half_tile(near_ref, i, n), half_tile(far_ref, i, n)
-            for odd in range(2):
-                halves = widened(own[odd * SUB : (odd + 1) * SUB], near, far, odd, even)
-                out_ref[odd, n] = shorts(jnp.concatenate(halves, 0))
 
 
 def decoded(ref, i, first, nvar, tiles):
@@ -658,16 +660,24 @@
     far, near = swapped(far, "space", 1), swapped(near, "space", 0)
 
     blocks_here = [arrived[d] for d in range(windows)]
-    *after, totals = pl.pallas_call(
-        lambda *refs: around_kernel(windows, nvar, levels, *refs),
-        out_shape=[shape((2,) + payload.shape[1:], i16)] * pairs
-        + [shape((nvar * levels, rows, LANES), f32)],
-        in_specs=[VMEM] * (windows + 3),
-        out_specs=[VMEM] * (pairs + 1),
+
+    def shifted(i, before):
+        codes = pl.pallas_call(
+            lambda *refs: around_kernel(i, *refs),
+            out_shape=shape((2,) + payload.shape[1:], i16),
+            in_specs=[VMEM] * 3 + [ANY],
+            out_specs=VMEM,
+            compiler_params=params(),
+        )(dual, near, far, before)
+        return moved(codes, "window", -1)
+
+    totals = pl.pallas_call(
+        lambda *refs: total_kernel(windows, nvar, levels, *refs),
+        out_shape=shape((nvar * levels, rows, LANES), f32),
+        in_specs=[VMEM] * windows,
+        out_specs=VMEM,
         compiler_params=params(),
-    )(*blocks_here, dual, near, far)
-    after = [moved(piece, "window", -1) for piece in after]
-
+    )(*blocks_here)
     obs, share, mix = pl.pallas_call(
         lambda *refs: prepare_factor_kernel(steps, nvar, levels, tiles, *refs),
         out_shape=[
@@ -714,6 +724,7 @@
         compiler_params=params(),
     )(mix, share, obs, own, traj_near, traj_far, first)
 
+    after = [shifted(i, ends if i else own) for i in range(pairs)]
     state = shape((nvar, 2, rows, columns), f32)
     coded = shape((nvar * tiles + 1, 2 * SUB, LANES), i16)
     base_duals, base_incs, sent = [], [], []

time: 45.7 us -> 46.9 us (1.026)
  waiting for transfers between devices: 11.9 us -> 12.5 us
    ppermute x6, waiting for transfers between devices: 5.64 us -> 6.54 us  [exchanged(): lax.ppermute(block, axis, [(i, i ^ mask) for i in range(lax.axis_size(axi...]
where the time goes in v18:
time: 46.9 us; the launch traced here: 46.3 us
  starting transfers between devices  21.5 us (46%)
  waiting for transfers between devices  12.5 us (27%)
  Pallas kernels  8.89 us (19%)
  local copies, waits for them, and re-layouts  1.82 us (4%)
  between operations  1.55 us (3%)
    ppermute x6, starting transfers between devices, exchanged(): lax.ppermute(block, axis, [(i, i ^ mask) for i in range(lax.axis_size(axi...  10.3 us
    ppermute x3, starting transfers between devices, rotated(): lax.ppermute(block, axis, [(i, (i + distance) % count) for i in range(cou...  7.13 us
    ppermute x6, waiting for transfers between devices, exchanged(): lax.ppermute(block, axis, [(i, i ^ mask) for i in range(lax.axis_size(axi...  6.54 us
    ppermute x3, waiting for transfers between devices, rotated(): lax.ppermute(block, axis, [(i, (i + distance) % count) for i in range(cou...  3.81 us
    pallas_call x1, Pallas kernels, body(): pl.pallas_call(lambda *refs: tangent_kernel(spaces, steps, nvar, levels,...  2.8 us
    ppermute x2, starting transfers between devices, moved(): lax.ppermute(block, axis, [(i, i + distance) for i in devices if i + dist...  2.58 us
    pallas_call x2, Pallas kernels, body(): pl.pallas_call(lambda *refs, i=i: adjoint_kernel(i, windows, spaces, step...  2.33 us
    ppermute x2, waiting for transfers between devices, moved(): lax.ppermute(block, axis, [(i, i + distance) for i in devices if i + dist...  2.14 us
  transfers between devices with their start and end apart: 15, of which 5 were waited for; matrix products, arithmetic and copies ran while one was open for 0% of the time, Pallas kernels for 17%

profile of v18, /device:TPU:0, one launch (start us, length us, event | category | flops | bytes accessed | tf_op | source)
XLA Modules:
  0.0 46.3 jit_solution(9064528370558880359)
XLA Ops:
  0.7 0.7 %pad.4.refs_0_ = f32[8,128]{1,0:T(8,128)S(1)} pad(f32[4,5]{1,0:T(4,128)} %bitcast.3, f32[]{:T(128)} %constant.2.clone.1), padding=0_4x0_123 | pad | bytes 4180 | tf_op jit(solution)/shard_map/jit(_pad)/pad | solution.py:629
  1.4 1.1 %copy-done = bf16[4,4,5,4,8,96]{5,4,3,2,1,0:T(8,128)(2,1)S(1)} copy-done((bf16[4,4,5,4,8,96]{5,4,3,2,1,0:T(8,128)(2,1)S(1)}, bf16[4,4,5,4,8,96]{5,4,3,2,1,0:T(8,128)(2,1)}, u32[]{:S(2)}) %copy-start) | copy-done | bytes 491544
  2.5 0.1 shard_map.123
  2.6 3.1 %collective-permute-start = (bf16[61,8,128]{2,1,0:T(8,128)(2,1)S(1)}, bf16[61,8,128]{2,1,0:T(8,128)(2,1)S(1)}, u32[]{:S(2)}, u32[]{:S(2)}) collective-permute-start(bf16[61,8,128]{2,1,0:T(8,128)(2,1)S(1)} %shard_map.123), channel_id=1, source_target_pairs={{0,4},{4,8},{8,12},{12,0},{1,5},{5,9},{9,13},{13,1},{2,6},{6,10},{... | collective-permute-start | bytes 374792 | tf_op jit(solution)/shard_map/ppermute | solution.py:584
  5.8 2.7 %collective-permute-start.1 = (bf16[61,8,128]{2,1,0:T(8,128)(2,1)S(1)}, bf16[61,8,128]{2,1,0:T(8,128)(2,1)S(1)}, u32[]{:S(2)}, u32[]{:S(2)}) collective-permute-start(bf16[61,8,128]{2,1,0:T(8,128)(2,1)S(1)} %shard_map.124), channel_id=1, source_target_pairs={{0,8},{4,12},{8,0},{12,4},{1,9},{5,13},{9,1},{13,5},{2,10},{6,14},... | collective-permute-start | bytes 374792 | tf_op jit(solution)/shard_map/ppermute | solution.py:584
  8.4 0.1 shard_map.125
  8.5 1.4 %collective-permute-start.2 = (bf16[61,8,128]{2,1,0:T(8,128)(2,1)S(1)}, bf16[61,8,128]{2,1,0:T(8,128)(2,1)S(1)}, u32[]{:S(2)}, u32[]{:S(2)}) collective-permute-start(bf16[61,8,128]{2,1,0:T(8,128)(2,1)S(1)} %shard_map.125), channel_id=1, source_target_pairs={{0,12},{4,0},{8,4},{12,8},{1,13},{5,1},{9,5},{13,9},{2,14},{6,2},{... | collective-permute-start | bytes 374792 | tf_op jit(solution)/shard_map/ppermute | solution.py:584
  10.0 0.5 %shard_map.128 = (s16[2,21,16,128]{3,2,1,0:T(8,128)(2,1)S(1)}, s16[2,21,16,128]{3,2,1,0:T(8,128)(2,1)S(1)}, s16[2,16,16,128]{3,2,1,0:T(8,128)(2,1)S(1)}) custom-call(f32[1,5,4,8,384]{4,3,2,1,0:T(8,128)S(1)} %copy-done.4, f32[1,5,4,8,384]{4,3,2,1,0:T(8,128)S(1)} %copy-done.2, f32[1,4,4,8,384]{4,3,2,1,0:T(8,128)S(1)} %copy-done.3), custom_call_target="tpu_custom_call" | custom-call | tf_op jit(solution)/shard_map/pallas_call | solution.py:653
  10.5 0.7 %collective-permute-start.6 = (s16[2,21,16,128]{3,2,1,0:T(8,128)(2,1)S(1)}, s16[2,21,16,128]{3,2,1,0:T(8,128)(2,1)S(1)}, u32[]{:S(2)}, u32[]{:S(2)}) collective-permute-start(s16[2,21,16,128]{3,2,1,0:T(8,128)(2,1)S(1)} %get-tuple-element.38), channel_id=1, source_target_pairs={{1,2},{2,1},{5,6},{6,5},{9,10},{10,9},{13,14},{14,13},{17,18},{18,... | collective-permute-start | bytes 516104 | tf_op jit(solution)/shard_map/ppermute | solution.py:599
  11.2 0.1 shard_map.122.refs_0_
  12.0 0.7 %shard_map.121 = (f32[4,4,3,8,128]{4,3,2,1,0:T(8,128)S(1)}, f32[4,4,8,128]{3,2,1,0:T(8,128)S(1)}, f32[5,5,8,128]{3,2,1,0:T(8,128)S(1)}) custom-call(s32[1]{0:T(128)S(6)} %copy.13.refs_0_, f32[1,4,4]{2,1,0:T(4,128)S(1)} %copy-done.8, f32[5,5]{1,0:T(8,128)S(1)} %copy-done.7, f32[1,4,4,8,384]{4,3,2,1,0:T(8,128)S(1)} %copy-done.3, f32[1,4,4,8,384]{4,3,2,1,0:T(8,128)S(1)} %copy-done.6), custom_call_target="tpu_custom_call" | custom-call | tf_op jit(solution)/shard_map/pallas_call | solution.py:681
  12.7 3.8 %collective-permute-done.1.refs_2_ = bf16[61,8,128]{2,1,0:T(8,128)(2,1)S(1)} collective-permute-done((bf16[61,8,128]{2,1,0:T(8,128)(2,1)S(1)}, bf16[61,8,128]{2,1,0:T(8,128)(2,1)S(1)}, u32[]{:S(2)}, u32[]{:S(2)}) %collective-permute-start.1) | collective-permute-done | bytes 124960 | tf_op jit(solution)/shard_map/ppermute | solution.py:584
  16.5 0.4 shard_map.127
  17.0 0.7 %collective-permute-start.4 = (bf16[31,8,384]{2,1,0:T(8,128)(2,1)S(1)}, bf16[31,8,384]{2,1,0:T(8,128)(2,1)S(1)}, u32[]{:S(2)}, u32[]{:S(2)}) collective-permute-start(bf16[31,8,384]{2,1,0:T(8,128)(2,1)S(1)} %get-tuple-element.36), channel_id=1, source_target_pairs={{1,2},{2,1},{5,6},{6,5},{9,10},{10,9},{13,14},{14,13},{17,18},{18,... | collective-permute-start | bytes 571400 | tf_op jit(solution)/shard_map/ppermute | solution.py:599
  17.8 1.3 %collective-permute-start.7 = (s16[2,16,16,128]{3,2,1,0:T(8,128)(2,1)S(1)}, s16[2,16,16,128]{3,2,1,0:T(8,128)(2,1)S(1)}, u32[]{:S(2)}, u32[]{:S(2)}) collective-permute-start(s16[2,16,16,128]{3,2,1,0:T(8,128)(2,1)S(1)} %shard_map.131), channel_id=1, source_target_pairs={{4,0},{8,4},{12,8},{5,1},{9,5},{13,9},{6,2},{10,6},{14,10},{7,3},{... | collective-permute-start | bytes 393224 | tf_op jit(solution)/shard_map/ppermute | solution.py:579
  19.1 0.1 shard_map.129.refs_6_
  19.3 2.8 %shard_map.130 = (f32[1,4,4,8,384]{4,3,2,1,0:T(8,128)}, f32[4,5,3,8,128]{4,3,2,1,0:T(8,128)S(1)}, f32[4,4,5,3,16,128]{5,4,3,2,1,0:T(8,128)S(1)}) custom-call(f32[5,5,8,128]{3,2,1,0:T(8,128)S(1)} %get-tuple-element.31.refs_4_.refs_0_, f32[4,4,8,128]{3,2,1,0:T(8,128)S(1)} %get-tuple-element.32.refs_1_, f32[4,4,3,8,128]{4,3,2,1,0:T(8,128)S(1)} %get-tuple-element.33.refs_2_, ...), custom_call_target="tpu_custom_call" | custom-call | tf_op jit(solution)/shard_map/pallas_call | solution.py:714
  22.2 1.3 %collective-permute-start.11 = (s16[2,16,16,128]{3,2,1,0:T(8,128)(2,1)S(1)}, s16[2,16,16,128]{3,2,1,0:T(8,128)(2,1)S(1)}, u32[]{:S(2)}, u32[]{:S(2)}) collective-permute-start(s16[2,16,16,128]{3,2,1,0:T(8,128)(2,1)S(1)} %shard_map.134), channel_id=1, source_target_pairs={{4,0},{8,4},{12,8},{5,1},{9,5},{13,9},{6,2},{10,6},{14,10},{7,3},{... | collective-permute-start | bytes 393224 | tf_op jit(solution)/shard_map/ppermute | solution.py:579
  23.5 0.2 shard_map.126.refs_1_.refs_10_
  23.7 2.1 %collective-permute-done.7.refs_4_ = s16[2,16,16,128]{3,2,1,0:T(8,128)(2,1)S(1)} collective-permute-done((s16[2,16,16,128]{3,2,1,0:T(8,128)(2,1)S(1)}, s16[2,16,16,128]{3,2,1,0:T(8,128)(2,1)S(1)}, u32[]{:S(2)}, u32[]{:S(2)}) %collective-permute-start.7) | collective-permute-done | bytes 131104 | tf_op jit(solution)/shard_map/ppermute | solution.py:579
  25.8 0.1 shard_map.132
  25.9 1.2 %shard_map.133 = (f32[5,2,8,384]{3,2,1,0:T(8,128)S(1)}, f32[5,2,8,384]{3,2,1,0:T(8,128)S(1)}, s16[16,16,128]{2,1,0:T(8,128)(2,1)S(1)}, s16[16,16,128]{2,1,0:T(8,128)(2,1)S(1)}, s16[16,16,128]{2,1,0:T(8,128)(2,1)S(1)}) custom-call(f32[5,5,8,128]{3,2,1,0:T(8,128)S(1)} %get-tuple-element.31.refs_4_.refs_0_, f32[20,8,128]{2,1,0:T(8,128)S(1)} %shard_map.126.refs_1_.refs_10_, ...), custom_call_target="tpu_custom_call" | custom-call | tf_op jit(solution)/shard_map/pallas_call | solution.py:740
  27.1 5.2 %collective-permute-start.8 = (s16[16,16,128]{2,1,0:T(8,128)(2,1)S(1)}, s16[16,16,128]{2,1,0:T(8,128)(2,1)S(1)}, u32[]{:S(2)}, u32[]{:S(2)}) collective-permute-start(s16[16,16,128]{2,1,0:T(8,128)(2,1)S(1)} %get-tuple-element.44), channel_id=1, source_target_pairs={{0,12},{4,8},{8,4},{12,0},{1,13},{5,9},{9,5},{13,1},{2,14},{6,10},... | collective-permute-start | bytes 196616 | tf_op jit(solution)/shard_map/ppermute | solution.py:588
  32.3 0.6 %collective-permute-start.10 = (s16[16,16,128]{2,1,0:T(8,128)(2,1)S(1)}, s16[16,16,128]{2,1,0:T(8,128)(2,1)S(1)}, u32[]{:S(2)}, u32[]{:S(2)}) collective-permute-start(s16[16,16,128]{2,1,0:T(8,128)(2,1)S(1)} %get-tuple-element.46), channel_id=1, source_target_pairs={{0,4},{4,0},{8,12},{12,8},{1,5},{5,1},{9,13},{13,9},{2,6},{6,2},{1... | collective-permute-start | bytes 196616 | tf_op jit(solution)/shard_map/ppermute | solution.py:588
  33.0 0.1 shard_map.135
  33.1 1.2 %shard_map.136 = (f32[5,2,8,384]{3,2,1,0:T(8,128)S(1)}, f32[5,2,8,384]{3,2,1,0:T(8,128)S(1)}, s16[16,16,128]{2,1,0:T(8,128)(2,1)S(1)}, s16[16,16,128]{2,1,0:T(8,128)(2,1)S(1)}, s16[16,16,128]{2,1,0:T(8,128)(2,1)S(1)}) custom-call(f32[5,5,8,128]{3,2,1,0:T(8,128)S(1)} %get-tuple-element.31.refs_4_.refs_0_, f32[20,8,128]{2,1,0:T(8,128)S(1)} %shard_map.126.refs_1_.refs_10_, ...), custom_call_target="tpu_custom_call" | custom-call | tf_op jit(solution)/shard_map/pallas_call | solution.py:740
  34.3 3.8 %collective-permute-start.12 = (s16[16,16,128]{2,1,0:T(8,128)(2,1)S(1)}, s16[16,16,128]{2,1,0:T(8,128)(2,1)S(1)}, u32[]{:S(2)}, u32[]{:S(2)}) collective-permute-start(s16[16,16,128]{2,1,0:T(8,128)(2,1)S(1)} %get-tuple-element.50), channel_id=1, source_target_pairs={{0,12},{4,8},{8,4},{12,0},{1,13},{5,9},{9,5},{13,1},{2,14},{6,10},... | collective-permute-start | bytes 196616 | tf_op jit(solution)/shard_map/ppermute | solution.py:588
  38.1 0.6 %collective-permute-start.14 = (s16[16,16,128]{2,1,0:T(8,128)(2,1)S(1)}, s16[16,16,128]{2,1,0:T(8,128)(2,1)S(1)}, u32[]{:S(2)}, u32[]{:S(2)}) collective-permute-start(s16[16,16,128]{2,1,0:T(8,128)(2,1)S(1)} %get-tuple-element.52), channel_id=1, source_target_pairs={{0,4},{4,0},{8,12},{12,8},{1,5},{5,1},{9,13},{13,9},{2,6},{6,2},{1... | collective-permute-start | bytes 196616 | tf_op jit(solution)/shard_map/ppermute | solution.py:588
  38.7 0.6 %collective-permute-done.9.refs_1_ = s16[16,16,128]{2,1,0:T(8,128)(2,1)S(1)} collective-permute-done((s16[16,16,128]{2,1,0:T(8,128)(2,1)S(1)}, s16[16,16,128]{2,1,0:T(8,128)(2,1)S(1)}, u32[]{:S(2)}, u32[]{:S(2)}) %collective-permute-start.9) | collective-permute-done | bytes 65568 | tf_op jit(solution)/shard_map/ppermute | solution.py:588
  39.4 1.7 %collective-permute-done.12.refs_3_ = s16[16,16,128]{2,1,0:T(8,128)(2,1)S(1)} collective-permute-done((s16[16,16,128]{2,1,0:T(8,128)(2,1)S(1)}, s16[16,16,128]{2,1,0:T(8,128)(2,1)S(1)}, u32[]{:S(2)}, u32[]{:S(2)}) %collective-permute-start.12) | collective-permute-done | bytes 65568 | tf_op jit(solution)/shard_map/ppermute | solution.py:588
  41.1 4.2 %collective-permute-done.13.refs_4_ = s16[16,16,128]{2,1,0:T(8,128)(2,1)S(1)} collective-permute-done((s16[16,16,128]{2,1,0:T(8,128)(2,1)S(1)}, s16[16,16,128]{2,1,0:T(8,128)(2,1)S(1)}, u32[]{:S(2)}, u32[]{:S(2)}) %collective-permute-start.13) | collective-permute-done | bytes 65568 | tf_op jit(solution)/shard_map/ppermute | solution.py:588
  45.3 1.0 %shard_map.137 = (f32[1,5,4,8,384]{4,3,2,1,0:T(8,128)}, f32[1,5,4,8,384]{4,3,2,1,0:T(8,128)}) custom-call(s16[16,16,128]{2,1,0:T(8,128)(2,1)S(1)} %collective-permute-done.8.refs_0_, s16[16,16,128]{2,1,0:T(8,128)(2,1)S(1)} %collective-permute-done.9.refs_1_, s16[16,16,128]{2,1,0:T(8,128)(2,1)S(1)} %collective-permute-done.10.refs_2_, ...), custom_call_target="tpu_custom_call" | custom-call | tf_op jit(solution)/shard_map/pallas_call | solution.py:762
  (34 shorter events, 0.5 us)
Async XLA Ops:
  0.6 11.3 %copy-start.8 = (f32[1,4,4]{2,1,0:T(4,128)S(1)}, f32[1,4,4]{2,1,0:T(4,128)}, u32[]{:S(2)}) copy-start(f32[1,4,4]{2,1,0:T(4,128)} %refs_1_.6) | copy-start | bytes 196
  0.6 11.3 %copy-start.7 = (f32[5,5]{1,0:T(8,128)S(1)}, f32[5,5]{1,0:T(8,128)}, u32[]{:S(2)}) copy-start(f32[5,5]{1,0:T(8,128)} %refs_2_.3) | copy-start | bytes 304
  1.3 1.1 %copy-start = (bf16[4,4,5,4,8,96]{5,4,3,2,1,0:T(8,128)(2,1)S(1)}, bf16[4,4,5,4,8,96]{5,4,3,2,1,0:T(8,128)(2,1)}, u32[]{:S(2)}) copy-start(bf16[4,4,5,4,8,96]{5,4,3,2,1,0:T(8,128)(2,1)} %refs_1_.10) | copy-start | bytes 1474564
  2.4 7.5 %copy-start.2 = (f32[1,5,4,8,384]{4,3,2,1,0:T(8,128)S(1)}, f32[1,5,4,8,384]{4,3,2,1,0:T(8,128)}, u32[]{:S(2)}) copy-start(f32[1,5,4,8,384]{4,3,2,1,0:T(8,128)} %refs_6_.3) | copy-start | bytes 737284
  2.4 7.5 %copy-start.3 = (f32[1,4,4,8,384]{4,3,2,1,0:T(8,128)S(1)}, f32[1,4,4,8,384]{4,3,2,1,0:T(8,128)}, u32[]{:S(2)}) copy-start(f32[1,4,4,8,384]{4,3,2,1,0:T(8,128)} %refs_3_.5) | copy-start | bytes 589828
  2.4 7.5 %copy-start.4 = (f32[1,5,4,8,384]{4,3,2,1,0:T(8,128)S(1)}, f32[1,5,4,8,384]{4,3,2,1,0:T(8,128)}, u32[]{:S(2)}) copy-start(f32[1,5,4,8,384]{4,3,2,1,0:T(8,128)} %refs_8_.3) | copy-start | bytes 737284
  2.4 8.7 %copy-start.1 = (bf16[4,4,5,4,8,96]{5,4,3,2,1,0:T(8,128)(2,1)S(1)}, bf16[4,4,5,4,8,96]{5,4,3,2,1,0:T(8,128)(2,1)}, u32[]{:S(2)}) copy-start(bf16[4,4,5,4,8,96]{5,4,3,2,1,0:T(8,128)(2,1)} %refs_1_.10) | copy-start | bytes 1474564
  2.4 9.5 %copy-start.6 = (f32[1,4,4,8,384]{4,3,2,1,0:T(8,128)S(1)}, f32[1,4,4,8,384]{4,3,2,1,0:T(8,128)}, u32[]{:S(2)}) copy-start(f32[1,4,4,8,384]{4,3,2,1,0:T(8,128)} %refs_4_.1) | copy-start | bytes 589828
  2.6 10.1 %collective-permute-start = (bf16[61,8,128]{2,1,0:T(8,128)(2,1)S(1)}, bf16[61,8,128]{2,1,0:T(8,128)(2,1)S(1)}, u32[]{:S(2)}, u32[]{:S(2)}) collective-permute-start(bf16[61,8,128]{2,1,0:T(8,128)(2,1)S(1)} %shard_map.123), channel_id=1, source_target_pairs={{0,4},{4,8},{8,12},{12,0},{1,5},{5,9},{9,13},{13,1},{2,6},{6,10},{... | collective-permute-start | bytes 374792 | tf_op jit(solution)/shard_map/ppermute | solution.py:584
  5.8 10.7 %collective-permute-start.1 = (bf16[61,8,128]{2,1,0:T(8,128)(2,1)S(1)}, bf16[61,8,128]{2,1,0:T(8,128)(2,1)S(1)}, u32[]{:S(2)}, u32[]{:S(2)}) collective-permute-start(bf16[61,8,128]{2,1,0:T(8,128)(2,1)S(1)} %shard_map.124), channel_id=1, source_target_pairs={{0,8},{4,12},{8,0},{12,4},{1,9},{5,13},{9,1},{13,5},{2,10},{6,14},... | collective-permute-start | bytes 374792 | tf_op jit(solution)/shard_map/ppermute | solution.py:584
  8.5 8.0 %collective-permute-start.2 = (bf16[61,8,128]{2,1,0:T(8,128)(2,1)S(1)}, bf16[61,8,128]{2,1,0:T(8,128)(2,1)S(1)}, u32[]{:S(2)}, u32[]{:S(2)}) collective-permute-start(bf16[61,8,128]{2,1,0:T(8,128)(2,1)S(1)} %shard_map.125), channel_id=1, source_target_pairs={{0,12},{4,0},{8,4},{12,8},{1,13},{5,1},{9,5},{13,9},{2,14},{6,2},{... | collective-permute-start | bytes 374792 | tf_op jit(solution)/shard_map/ppermute | solution.py:584
  10.4 7.3 %collective-permute-start.5 = (s16[2,21,16,128]{3,2,1,0:T(8,128)(2,1)S(1)}, s16[2,21,16,128]{3,2,1,0:T(8,128)(2,1)S(1)}, u32[]{:S(2)}, u32[]{:S(2)}) collective-permute-start(s16[2,21,16,128]{3,2,1,0:T(8,128)(2,1)S(1)} %get-tuple-element.37), channel_id=1, source_target_pairs={{0,1},{1,0},{2,3},{3,2},{4,5},{5,4},{6,7},{7,6},{8,9},{9,8},{10,11... | collective-permute-start | bytes 516104 | tf_op jit(solution)/shard_map/ppermute | solution.py:599
  10.5 7.2 %collective-permute-start.6 = (s16[2,21,16,128]{3,2,1,0:T(8,128)(2,1)S(1)}, s16[2,21,16,128]{3,2,1,0:T(8,128)(2,1)S(1)}, u32[]{:S(2)}, u32[]{:S(2)}) collective-permute-start(s16[2,21,16,128]{3,2,1,0:T(8,128)(2,1)S(1)} %get-tuple-element.38), channel_id=1, source_target_pairs={{1,2},{2,1},{5,6},{6,5},{9,10},{10,9},{13,14},{14,13},{17,18},{18,... | collective-permute-start | bytes 516104 | tf_op jit(solution)/shard_map/ppermute | solution.py:599
  16.9 2.3 %collective-permute-start.3 = (bf16[31,8,384]{2,1,0:T(8,128)(2,1)S(1)}, bf16[31,8,384]{2,1,0:T(8,128)(2,1)S(1)}, u32[]{:S(2)}, u32[]{:S(2)}) collective-permute-start(bf16[31,8,384]{2,1,0:T(8,128)(2,1)S(1)} %get-tuple-element.35), channel_id=1, source_target_pairs={{0,1},{1,0},{2,3},{3,2},{4,5},{5,4},{6,7},{7,6},{8,9},{9,8},{10,11... | collective-permute-start | bytes 571400 | tf_op jit(solution)/shard_map/ppermute | solution.py:599
  17.0 2.2 %collective-permute-start.4 = (bf16[31,8,384]{2,1,0:T(8,128)(2,1)S(1)}, bf16[31,8,384]{2,1,0:T(8,128)(2,1)S(1)}, u32[]{:S(2)}, u32[]{:S(2)}) collective-permute-start(bf16[31,8,384]{2,1,0:T(8,128)(2,1)S(1)} %get-tuple-element.36), channel_id=1, source_target_pairs={{1,2},{2,1},{5,6},{6,5},{9,10},{10,9},{13,14},{14,13},{17,18},{18,... | collective-permute-start | bytes 571400 | tf_op jit(solution)/shard_map/ppermute | solution.py:599
  17.8 8.0 %collective-permute-start.7 = (s16[2,16,16,128]{3,2,1,0:T(8,128)(2,1)S(1)}, s16[2,16,16,128]{3,2,1,0:T(8,128)(2,1)S(1)}, u32[]{:S(2)}, u32[]{:S(2)}) collective-permute-start(s16[2,16,16,128]{3,2,1,0:T(8,128)(2,1)S(1)} %shard_map.131), channel_id=1, source_target_pairs={{4,0},{8,4},{12,8},{5,1},{9,5},{13,9},{6,2},{10,6},{14,10},{7,3},{... | collective-permute-start | bytes 393224 | tf_op jit(solution)/shard_map/ppermute | solution.py:579
  19.3 6.7 %copy-start.5 = (f32[1,5,4,8,384]{4,3,2,1,0:T(8,128)S(1)}, f32[1,5,4,8,384]{4,3,2,1,0:T(8,128)}, u32[]{:S(2)}) copy-start(f32[1,5,4,8,384]{4,3,2,1,0:T(8,128)} %refs_7_.3) | copy-start | bytes 737284
  22.2 10.8 %collective-permute-start.11 = (s16[2,16,16,128]{3,2,1,0:T(8,128)(2,1)S(1)}, s16[2,16,16,128]{3,2,1,0:T(8,128)(2,1)S(1)}, u32[]{:S(2)}, u32[]{:S(2)}) collective-permute-start(s16[2,16,16,128]{3,2,1,0:T(8,128)(2,1)S(1)} %shard_map.134), channel_id=1, source_target_pairs={{4,0},{8,4},{12,8},{5,1},{9,5},{13,9},{6,2},{10,6},{14,10},{7,3},{... | collective-permute-start | bytes 393224 | tf_op jit(solution)/shard_map/ppermute | solution.py:579
  27.1 11.0 %collective-permute-start.8 = (s16[16,16,128]{2,1,0:T(8,128)(2,1)S(1)}, s16[16,16,128]{2,1,0:T(8,128)(2,1)S(1)}, u32[]{:S(2)}, u32[]{:S(2)}) collective-permute-start(s16[16,16,128]{2,1,0:T(8,128)(2,1)S(1)} %get-tuple-element.44), channel_id=1, source_target_pairs={{0,12},{4,8},{8,4},{12,0},{1,13},{5,9},{9,5},{13,1},{2,14},{6,10},... | collective-permute-start | bytes 196616 | tf_op jit(solution)/shard_map/ppermute | solution.py:588
  32.3 7.0 %collective-permute-start.9 = (s16[16,16,128]{2,1,0:T(8,128)(2,1)S(1)}, s16[16,16,128]{2,1,0:T(8,128)(2,1)S(1)}, u32[]{:S(2)}, u32[]{:S(2)}) collective-permute-start(s16[16,16,128]{2,1,0:T(8,128)(2,1)S(1)} %get-tuple-element.45), channel_id=1, source_target_pairs={{0,8},{4,12},{8,0},{12,4},{1,9},{5,13},{9,1},{13,5},{2,10},{6,14},... | collective-permute-start | bytes 196616 | tf_op jit(solution)/shard_map/ppermute | solution.py:588
  32.3 7.0 %collective-permute-start.10 = (s16[16,16,128]{2,1,0:T(8,128)(2,1)S(1)}, s16[16,16,128]{2,1,0:T(8,128)(2,1)S(1)}, u32[]{:S(2)}, u32[]{:S(2)}) collective-permute-start(s16[16,16,128]{2,1,0:T(8,128)(2,1)S(1)} %get-tuple-element.46), channel_id=1, source_target_pairs={{0,4},{4,0},{8,12},{12,8},{1,5},{5,1},{9,13},{13,9},{2,6},{6,2},{1... | collective-permute-start | bytes 196616 | tf_op jit(solution)/shard_map/ppermute | solution.py:588
  34.3 6.8 %collective-permute-start.12 = (s16[16,16,128]{2,1,0:T(8,128)(2,1)S(1)}, s16[16,16,128]{2,1,0:T(8,128)(2,1)S(1)}, u32[]{:S(2)}, u32[]{:S(2)}) collective-permute-start(s16[16,16,128]{2,1,0:T(8,128)(2,1)S(1)} %get-tuple-element.50), channel_id=1, source_target_pairs={{0,12},{4,8},{8,4},{12,0},{1,13},{5,9},{9,5},{13,1},{2,14},{6,10},... | collective-permute-start | bytes 196616 | tf_op jit(solution)/shard_map/ppermute | solution.py:588
  38.1 7.2 %collective-permute-start.13 = (s16[16,16,128]{2,1,0:T(8,128)(2,1)S(1)}, s16[16,16,128]{2,1,0:T(8,128)(2,1)S(1)}, u32[]{:S(2)}, u32[]{:S(2)}) collective-permute-start(s16[16,16,128]{2,1,0:T(8,128)(2,1)S(1)} %get-tuple-element.51), channel_id=1, source_target_pairs={{0,8},{4,12},{8,0},{12,4},{1,9},{5,13},{9,1},{13,5},{2,10},{6,14},... | collective-permute-start | bytes 196616 | tf_op jit(solution)/shard_map/ppermute | solution.py:588
  38.1 7.2 %collective-permute-start.14 = (s16[16,16,128]{2,1,0:T(8,128)(2,1)S(1)}, s16[16,16,128]{2,1,0:T(8,128)(2,1)S(1)}, u32[]{:S(2)}, u32[]{:S(2)}) collective-permute-start(s16[16,16,128]{2,1,0:T(8,128)(2,1)S(1)} %get-tuple-element.52), channel_id=1, source_target_pairs={{0,4},{4,0},{8,12},{12,8},{1,5},{5,1},{9,13},{13,9},{2,6},{6,2},{1... | collective-permute-start | bytes 196616 | tf_op jit(solution)/shard_map/ppermute | solution.py:588

commit v19 on v16

--- a/solution.py
+++ b/solution.py
@@ -194,13 +194,16 @@
         for lev in range(levels):
             one = total[lev : lev + 1, v : v + 1]
             total_ref[v * levels + lev] = jnp.broadcast_to(one, (SUB, LANES))
-    for i, out_ref in enumerate(outs):
-        for n in range(own_ref.shape[1]):
-            own = floats(own_ref[i, n])
-            near, far = half_tile(near_ref, i, n), half_tile(far_ref, i, n)
-            for odd in range(2):
-                halves = widened(own[odd * SUB : (odd + 1) * SUB], near, far, odd, even)
-                out_ref[odd, n] = shorts(jnp.concatenate(halves, 0))
+    lev = 0
+    for out_ref in outs:
+        for k in range(out_ref.shape[0]):
+            i, odd = lev // 2, lev % 2
+            for n in range(own_ref.shape[1]):
+                own = floats(own_ref[i, n])[odd * SUB : (odd + 1) * SUB]
+                near, far = half_tile(near_ref, i, n), half_tile(far_ref, i, n)
+                halves = widened(own, near, far, odd, even)
+                out_ref[k, n] = shorts(jnp.concatenate(halves, 0))
+            lev += 1
 
 
 def decoded(ref, i, first, nvar, tiles):
@@ -319,9 +322,9 @@
 
 
 def prepare_adjoint_kernel(
-    i, steps, nvar, tiles, count_ref, near_ref, far_ref, dobs_ref, after_ref, *refs
+    i, steps, nvar, tiles, count_ref, near_ref, far_ref, dobs_ref, *refs
 ):
-    _, last_ref, force_ref = refs
+    after_refs, (_, last_ref, force_ref) = refs[:-3], refs[-3:]
     even = even_place()
     blocks = [slice(0, SUB), slice(SUB, 2 * SUB)]
     cuts = [slice(t * LANES, (t + 1) * LANES) for t in range(tiles)]
@@ -330,10 +333,11 @@
     none = [[jnp.zeros((SUB, LANES), jnp.float32)] * tiles]
     forces = [none + decoded(ref, i, 2 * offset, steps - 1, tiles) for ref in (near_ref, far_ref)]
     for odd in range(2):
-        scales = jnp.exp2(floats(after_ref[odd, nvar * tiles])) * (-1.0 / CODE_MAX)
+        after_ref, k = (after_refs[odd], 0) if len(after_refs) == 2 else (after_refs[0], odd)
+        scales = jnp.exp2(floats(after_ref[k, nvar * tiles])) * (-1.0 / CODE_MAX)
         for t in range(tiles):
             for v in range(nvar):
-                value = floats(after_ref[odd, v * tiles + t])
+                value = floats(after_ref[k, v * tiles + t])
                 last_ref[odd, v, t] = value * scales[:, v : v + 1]
             for j in range(steps):
                 near, far = (side[j][t] for side in forces)
@@ -658,15 +662,17 @@
     far, near = swapped(far, "space", 1), swapped(near, "space", 0)
 
     blocks_here = [arrived[d] for d in range(windows)]
+    flows = [1, 1] + [2] * (pairs - 1)
     *after, totals = pl.pallas_call(
         lambda *refs: around_kernel(windows, nvar, levels, *refs),
-        out_shape=[shape((2,) + payload.shape[1:], i16)] * pairs
+        out_shape=[shape((count,) + payload.shape[1:], i16) for count in flows]
         + [shape((nvar * levels, rows, LANES), f32)],
         in_specs=[VMEM] * (windows + 3),
-        out_specs=[VMEM] * (pairs + 1),
+        out_specs=[VMEM] * (len(flows) + 1),
         compiler_params=params(),
     )(*blocks_here, dual, near, far)
     after = [moved(piece, "window", -1) for piece in after]
+    after = [after[:2]] + [[piece] for piece in after[2:]]
 
     obs, share, mix = pl.pallas_call(
         lambda *refs: prepare_factor_kernel(steps, nvar, levels, tiles, *refs),
@@ -722,10 +728,10 @@
         last, force = pl.pallas_call(
             lambda *refs, i=i: prepare_adjoint_kernel(i, steps, nvar, tiles, *refs),
             out_shape=[shape((2, n, tiles, 2 * SUB, LANES), f32) for n in (nvar, steps)],
-            in_specs=[SMEM] + [VMEM] * 4 + [ANY],
+            in_specs=[SMEM] + [VMEM] * (3 + len(after[i])) + [ANY],
             out_specs=[VMEM] * 2,
             compiler_params=params(),
-        )(obs_count, near, far, dual_obs, after[i], before)
+        )(obs_count, near, far, dual_obs, *after[i], before)
         base_dual, base_inc, *payloads = pl.pallas_call(
             lambda *refs, i=i: adjoint_kernel(
                 i, windows, spaces, steps, nvar, levels, tiles, *refs

time: 45.7 us -> 47.3 us (1.035)
  starting transfers between devices: 21.3 us -> 22.9 us
    ppermute x2 -> x3, starting transfers between devices: 2.72 us -> 4.01 us  [moved(): lax.ppermute(block, axis, [(i, i + distance) for i in devices if i + dist...]
    ppermute x2 -> x3, waiting for transfers between devices: 2.45 us -> 2.83 us  [moved(): lax.ppermute(block, axis, [(i, i + distance) for i in devices if i + dist...]
  transfers between devices with their start and end apart: 15 -> 16, of which waited for: 5 -> 5; matrix products, arithmetic and copies ran while one was open for 0% -> 0% of each run, Pallas kernels for 17% -> 16%
where the time goes in v19:
time: 47.3 us; the launch traced here: 47 us
  starting transfers between devices  22.9 us (48%)
  waiting for transfers between devices  12 us (25%)
  Pallas kernels  8.79 us (19%)
  local copies, waits for them, and re-layouts  1.82 us (4%)
  between operations  1.55 us (3%)
    ppermute x6, starting transfers between devices, exchanged(): lax.ppermute(block, axis, [(i, i ^ mask) for i in range(lax.axis_size(axi...  10.3 us
    ppermute x3, starting transfers between devices, rotated(): lax.ppermute(block, axis, [(i, (i + distance) % count) for i in range(cou...  7.13 us
    ppermute x6, waiting for transfers between devices, exchanged(): lax.ppermute(block, axis, [(i, i ^ mask) for i in range(lax.axis_size(axi...  5.31 us
    ppermute x3, starting transfers between devices, moved(): lax.ppermute(block, axis, [(i, i + distance) for i in devices if i + dist...  4.01 us
    ppermute x3, waiting for transfers between devices, rotated(): lax.ppermute(block, axis, [(i, (i + distance) % count) for i in range(cou...  3.81 us
    ppermute x3, waiting for transfers between devices, moved(): lax.ppermute(block, axis, [(i, i + distance) for i in devices if i + dist...  2.83 us
    pallas_call x1, Pallas kernels, body(): pl.pallas_call(lambda *refs: tangent_kernel(spaces, steps, nvar, levels,...  2.78 us
    pallas_call x2, Pallas kernels, body(): pl.pallas_call(lambda *refs, i=i: adjoint_kernel(i, windows, spaces, step...  2.33 us
  transfers between devices with their start and end apart: 16, of which 5 were waited for; matrix products, arithmetic and copies ran while one was open for 0% of the time, Pallas kernels for 16%

profile of v19, /device:TPU:0, one launch (start us, length us, event | category | flops | bytes accessed | tf_op | source)
XLA Modules:
  0.0 47.0 jit_solution(16543807851294316286)
XLA Ops:
  0.7 0.7 %pad.4.refs_0_ = f32[8,128]{1,0:T(8,128)S(1)} pad(f32[4,5]{1,0:T(4,128)} %bitcast.3, f32[]{:T(128)} %constant.2.clone.1), padding=0_4x0_123 | pad | bytes 4180 | tf_op jit(solution)/shard_map/jit(_pad)/pad | solution.py:631
  1.4 1.1 %copy-done = bf16[4,4,5,4,8,96]{5,4,3,2,1,0:T(8,128)(2,1)S(1)} copy-done((bf16[4,4,5,4,8,96]{5,4,3,2,1,0:T(8,128)(2,1)S(1)}, bf16[4,4,5,4,8,96]{5,4,3,2,1,0:T(8,128)(2,1)}, u32[]{:S(2)}) %copy-start) | copy-done | bytes 491544
  2.5 0.1 shard_map.123
  2.6 3.1 %collective-permute-start = (bf16[61,8,128]{2,1,0:T(8,128)(2,1)S(1)}, bf16[61,8,128]{2,1,0:T(8,128)(2,1)S(1)}, u32[]{:S(2)}, u32[]{:S(2)}) collective-permute-start(bf16[61,8,128]{2,1,0:T(8,128)(2,1)S(1)} %shard_map.123), channel_id=1, source_target_pairs={{0,4},{4,8},{8,12},{12,0},{1,5},{5,9},{9,13},{13,1},{2,6},{6,10},{... | collective-permute-start | bytes 374792 | tf_op jit(solution)/shard_map/ppermute | solution.py:586
  5.8 2.7 %collective-permute-start.1 = (bf16[61,8,128]{2,1,0:T(8,128)(2,1)S(1)}, bf16[61,8,128]{2,1,0:T(8,128)(2,1)S(1)}, u32[]{:S(2)}, u32[]{:S(2)}) collective-permute-start(bf16[61,8,128]{2,1,0:T(8,128)(2,1)S(1)} %shard_map.124), channel_id=1, source_target_pairs={{0,8},{4,12},{8,0},{12,4},{1,9},{5,13},{9,1},{13,5},{2,10},{6,14},... | collective-permute-start | bytes 374792 | tf_op jit(solution)/shard_map/ppermute | solution.py:586
  8.5 1.4 %collective-permute-start.2 = (bf16[61,8,128]{2,1,0:T(8,128)(2,1)S(1)}, bf16[61,8,128]{2,1,0:T(8,128)(2,1)S(1)}, u32[]{:S(2)}, u32[]{:S(2)}) collective-permute-start(bf16[61,8,128]{2,1,0:T(8,128)(2,1)S(1)} %shard_map.125), channel_id=1, source_target_pairs={{0,12},{4,0},{8,4},{12,8},{1,13},{5,1},{9,5},{13,9},{2,14},{6,2},{... | collective-permute-start | bytes 374792 | tf_op jit(solution)/shard_map/ppermute | solution.py:586
  10.0 0.5 shard_map.126
  10.5 0.7 %collective-permute-start.4 = (s16[2,21,16,128]{3,2,1,0:T(8,128)(2,1)S(1)}, s16[2,21,16,128]{3,2,1,0:T(8,128)(2,1)S(1)}, u32[]{:S(2)}, u32[]{:S(2)}) collective-permute-start(s16[2,21,16,128]{3,2,1,0:T(8,128)(2,1)S(1)} %get-tuple-element.38), channel_id=1, source_target_pairs={{1,2},{2,1},{5,6},{6,5},{9,10},{10,9},{13,14},{14,13},{17,18},{18,... | collective-permute-start | bytes 516104 | tf_op jit(solution)/shard_map/ppermute | solution.py:601
  11.2 0.1 shard_map.122.refs_0_
  12.0 0.7 %shard_map.121 = (f32[4,4,3,8,128]{4,3,2,1,0:T(8,128)S(1)}, f32[4,4,8,128]{3,2,1,0:T(8,128)S(1)}, f32[5,5,8,128]{3,2,1,0:T(8,128)S(1)}) custom-call(s32[1]{0:T(128)S(6)} %copy.13.refs_0_, f32[1,4,4]{2,1,0:T(4,128)S(1)} %copy-done.8, f32[5,5]{1,0:T(8,128)S(1)} %copy-done.7, f32[1,4,4,8,384]{4,3,2,1,0:T(8,128)S(1)} %copy-done.3, f32[1,4,4,8,384]{4,3,2,1,0:T(8,128)S(1)} %copy-done.6), custom_call_target="tpu_custom_call" | custom-call | tf_op jit(solution)/shard_map/pallas_call | solution.py:677
  12.7 3.8 %collective-permute-done.1.refs_2_ = bf16[61,8,128]{2,1,0:T(8,128)(2,1)S(1)} collective-permute-done((bf16[61,8,128]{2,1,0:T(8,128)(2,1)S(1)}, bf16[61,8,128]{2,1,0:T(8,128)(2,1)S(1)}, u32[]{:S(2)}, u32[]{:S(2)}) %collective-permute-start.1) | collective-permute-done | bytes 124960 | tf_op jit(solution)/shard_map/ppermute | solution.py:586
  16.5 0.4 shard_map.128
  17.0 0.7 %collective-permute-start.6 = (bf16[31,8,384]{2,1,0:T(8,128)(2,1)S(1)}, bf16[31,8,384]{2,1,0:T(8,128)(2,1)S(1)}, u32[]{:S(2)}, u32[]{:S(2)}) collective-permute-start(bf16[31,8,384]{2,1,0:T(8,128)(2,1)S(1)} %get-tuple-element.44), channel_id=1, source_target_pairs={{1,2},{2,1},{5,6},{6,5},{9,10},{10,9},{13,14},{14,13},{17,18},{18,... | collective-permute-start | bytes 571400 | tf_op jit(solution)/shard_map/ppermute | solution.py:601
  17.7 0.3 shard_map.127
  18.0 1.4 %collective-permute-start.7 = (s16[1,16,16,128]{3,2,1,0:T(8,128)(2,1)S(1)}, s16[1,16,16,128]{3,2,1,0:T(8,128)(2,1)S(1)}, u32[]{:S(2)}, u32[]{:S(2)}) collective-permute-start(s16[1,16,16,128]{3,2,1,0:T(8,128)(2,1)S(1)} %get-tuple-element.46), channel_id=1, source_target_pairs={{4,0},{8,4},{12,8},{5,1},{9,5},{13,9},{6,2},{10,6},{14,10},{7,3},{... | collective-permute-start | bytes 196616 | tf_op jit(solution)/shard_map/ppermute | solution.py:581
  19.4 1.3 %collective-permute-start.8 = (s16[1,16,16,128]{3,2,1,0:T(8,128)(2,1)S(1)}, s16[1,16,16,128]{3,2,1,0:T(8,128)(2,1)S(1)}, u32[]{:S(2)}, u32[]{:S(2)}) collective-permute-start(s16[1,16,16,128]{3,2,1,0:T(8,128)(2,1)S(1)} %get-tuple-element.47), channel_id=1, source_target_pairs={{4,0},{8,4},{12,8},{5,1},{9,5},{13,9},{6,2},{10,6},{14,10},{7,3},{... | collective-permute-start | bytes 196616 | tf_op jit(solution)/shard_map/ppermute | solution.py:581
  20.7 1.3 %collective-permute-start.12 = (s16[2,16,16,128]{3,2,1,0:T(8,128)(2,1)S(1)}, s16[2,16,16,128]{3,2,1,0:T(8,128)(2,1)S(1)}, u32[]{:S(2)}, u32[]{:S(2)}) collective-permute-start(s16[2,16,16,128]{3,2,1,0:T(8,128)(2,1)S(1)} %get-tuple-element.54), channel_id=1, source_target_pairs={{4,0},{8,4},{12,8},{5,1},{9,5},{13,9},{6,2},{10,6},{14,10},{7,3},{... | collective-permute-start | bytes 393224 | tf_op jit(solution)/shard_map/ppermute | solution.py:581
  22.0 0.1 shard_map.129.refs_6_
  22.2 2.8 %shard_map.130 = (f32[1,4,4,8,384]{4,3,2,1,0:T(8,128)}, f32[4,5,3,8,128]{4,3,2,1,0:T(8,128)S(1)}, f32[4,4,5,3,16,128]{5,4,3,2,1,0:T(8,128)S(1)}) custom-call(f32[5,5,8,128]{3,2,1,0:T(8,128)S(1)} %get-tuple-element.35.refs_4_.refs_0_, f32[4,4,8,128]{3,2,1,0:T(8,128)S(1)} %get-tuple-element.40.refs_1_, f32[4,4,3,8,128]{4,3,2,1,0:T(8,128)S(1)} %get-tuple-element.41.refs_2_, ...), custom_call_target="tpu_custom_call" | custom-call | tf_op jit(solution)/shard_map/pallas_call | solution.py:710
  25.0 0.4 collective-permute-done.7.refs_4_
  25.4 2.4 %collective-permute-done.8.refs_5_ = s16[1,16,16,128]{3,2,1,0:T(8,128)(2,1)S(1)} collective-permute-done((s16[1,16,16,128]{3,2,1,0:T(8,128)(2,1)S(1)}, s16[1,16,16,128]{3,2,1,0:T(8,128)(2,1)S(1)}, u32[]{:S(2)}, u32[]{:S(2)}) %collective-permute-start.8) | collective-permute-done | bytes 65568 | tf_op jit(solution)/shard_map/ppermute | solution.py:581
  27.8 0.1 shard_map.131
  27.9 1.2 %shard_map.132 = (f32[5,2,8,384]{3,2,1,0:T(8,128)S(1)}, f32[5,2,8,384]{3,2,1,0:T(8,128)S(1)}, s16[16,16,128]{2,1,0:T(8,128)(2,1)S(1)}, s16[16,16,128]{2,1,0:T(8,128)(2,1)S(1)}, s16[16,16,128]{2,1,0:T(8,128)(2,1)S(1)}) custom-call(f32[5,5,8,128]{3,2,1,0:T(8,128)S(1)} %get-tuple-element.35.refs_4_.refs_0_, ...), custom_call_target="tpu_custom_call" | custom-call | tf_op jit(solution)/shard_map/pallas_call | solution.py:735
  29.1 5.2 %collective-permute-start.9 = (s16[16,16,128]{2,1,0:T(8,128)(2,1)S(1)}, s16[16,16,128]{2,1,0:T(8,128)(2,1)S(1)}, u32[]{:S(2)}, u32[]{:S(2)}) collective-permute-start(s16[16,16,128]{2,1,0:T(8,128)(2,1)S(1)} %get-tuple-element.51), channel_id=1, source_target_pairs={{0,12},{4,8},{8,4},{12,0},{1,13},{5,9},{9,5},{13,1},{2,14},{6,10},... | collective-permute-start | bytes 196616 | tf_op jit(solution)/shard_map/ppermute | solution.py:590
  34.3 0.6 %collective-permute-start.11 = (s16[16,16,128]{2,1,0:T(8,128)(2,1)S(1)}, s16[16,16,128]{2,1,0:T(8,128)(2,1)S(1)}, u32[]{:S(2)}, u32[]{:S(2)}) collective-permute-start(s16[16,16,128]{2,1,0:T(8,128)(2,1)S(1)} %get-tuple-element.53), channel_id=1, source_target_pairs={{0,4},{4,0},{8,12},{12,8},{1,5},{5,1},{9,13},{13,9},{2,6},{6,2},{1... | collective-permute-start | bytes 196616 | tf_op jit(solution)/shard_map/ppermute | solution.py:590
  34.9 0.1 shard_map.133
  35.0 1.2 %shard_map.134 = (f32[5,2,8,384]{3,2,1,0:T(8,128)S(1)}, f32[5,2,8,384]{3,2,1,0:T(8,128)S(1)}, s16[16,16,128]{2,1,0:T(8,128)(2,1)S(1)}, s16[16,16,128]{2,1,0:T(8,128)(2,1)S(1)}, s16[16,16,128]{2,1,0:T(8,128)(2,1)S(1)}) custom-call(f32[5,5,8,128]{3,2,1,0:T(8,128)S(1)} %get-tuple-element.35.refs_4_.refs_0_, ...), custom_call_target="tpu_custom_call" | custom-call | tf_op jit(solution)/shard_map/pallas_call | solution.py:735
  36.2 3.8 %collective-permute-start.13 = (s16[16,16,128]{2,1,0:T(8,128)(2,1)S(1)}, s16[16,16,128]{2,1,0:T(8,128)(2,1)S(1)}, u32[]{:S(2)}, u32[]{:S(2)}) collective-permute-start(s16[16,16,128]{2,1,0:T(8,128)(2,1)S(1)} %get-tuple-element.58), channel_id=1, source_target_pairs={{0,12},{4,8},{8,4},{12,0},{1,13},{5,9},{9,5},{13,1},{2,14},{6,10},... | collective-permute-start | bytes 196616 | tf_op jit(solution)/shard_map/ppermute | solution.py:590
  40.0 0.6 %collective-permute-start.15 = (s16[16,16,128]{2,1,0:T(8,128)(2,1)S(1)}, s16[16,16,128]{2,1,0:T(8,128)(2,1)S(1)}, u32[]{:S(2)}, u32[]{:S(2)}) collective-permute-start(s16[16,16,128]{2,1,0:T(8,128)(2,1)S(1)} %get-tuple-element.60), channel_id=1, source_target_pairs={{0,4},{4,0},{8,12},{12,8},{1,5},{5,1},{9,13},{13,9},{2,6},{6,2},{1... | collective-permute-start | bytes 196616 | tf_op jit(solution)/shard_map/ppermute | solution.py:590
  40.7 1.8 %collective-permute-done.13.refs_3_ = s16[16,16,128]{2,1,0:T(8,128)(2,1)S(1)} collective-permute-done((s16[16,16,128]{2,1,0:T(8,128)(2,1)S(1)}, s16[16,16,128]{2,1,0:T(8,128)(2,1)S(1)}, u32[]{:S(2)}, u32[]{:S(2)}) %collective-permute-start.13) | collective-permute-done | bytes 65568 | tf_op jit(solution)/shard_map/ppermute | solution.py:590
  42.5 3.5 %collective-permute-done.14.refs_4_ = s16[16,16,128]{2,1,0:T(8,128)(2,1)S(1)} collective-permute-done((s16[16,16,128]{2,1,0:T(8,128)(2,1)S(1)}, s16[16,16,128]{2,1,0:T(8,128)(2,1)S(1)}, u32[]{:S(2)}, u32[]{:S(2)}) %collective-permute-start.14) | collective-permute-done | bytes 65568 | tf_op jit(solution)/shard_map/ppermute | solution.py:590
  46.0 1.0 %shard_map.135 = (f32[1,5,4,8,384]{4,3,2,1,0:T(8,128)}, f32[1,5,4,8,384]{4,3,2,1,0:T(8,128)}) custom-call(s16[16,16,128]{2,1,0:T(8,128)(2,1)S(1)} %collective-permute-done.9.refs_0_, s16[16,16,128]{2,1,0:T(8,128)(2,1)S(1)} %collective-permute-done.10.refs_1_, s16[16,16,128]{2,1,0:T(8,128)(2,1)S(1)} %collective-permute-done.11.refs_2_, ...), custom_call_target="tpu_custom_call" | custom-call | tf_op jit(solution)/shard_map/pallas_call | solution.py:757
  (34 shorter events, 0.4 us)
Async XLA Ops:
  0.6 11.3 %copy-start.8 = (f32[1,4,4]{2,1,0:T(4,128)S(1)}, f32[1,4,4]{2,1,0:T(4,128)}, u32[]{:S(2)}) copy-start(f32[1,4,4]{2,1,0:T(4,128)} %refs_1_.6) | copy-start | bytes 196
  0.6 11.3 %copy-start.7 = (f32[5,5]{1,0:T(8,128)S(1)}, f32[5,5]{1,0:T(8,128)}, u32[]{:S(2)}) copy-start(f32[5,5]{1,0:T(8,128)} %refs_2_.3) | copy-start | bytes 304
  1.3 1.1 %copy-start = (bf16[4,4,5,4,8,96]{5,4,3,2,1,0:T(8,128)(2,1)S(1)}, bf16[4,4,5,4,8,96]{5,4,3,2,1,0:T(8,128)(2,1)}, u32[]{:S(2)}) copy-start(bf16[4,4,5,4,8,96]{5,4,3,2,1,0:T(8,128)(2,1)} %refs_1_.10) | copy-start | bytes 1474564
  2.4 7.5 %copy-start.2 = (f32[1,5,4,8,384]{4,3,2,1,0:T(8,128)S(1)}, f32[1,5,4,8,384]{4,3,2,1,0:T(8,128)}, u32[]{:S(2)}) copy-start(f32[1,5,4,8,384]{4,3,2,1,0:T(8,128)} %refs_6_.3) | copy-start | bytes 737284
  2.4 7.5 %copy-start.3 = (f32[1,4,4,8,384]{4,3,2,1,0:T(8,128)S(1)}, f32[1,4,4,8,384]{4,3,2,1,0:T(8,128)}, u32[]{:S(2)}) copy-start(f32[1,4,4,8,384]{4,3,2,1,0:T(8,128)} %refs_3_.5) | copy-start | bytes 589828
  2.4 7.5 %copy-start.4 = (f32[1,5,4,8,384]{4,3,2,1,0:T(8,128)S(1)}, f32[1,5,4,8,384]{4,3,2,1,0:T(8,128)}, u32[]{:S(2)}) copy-start(f32[1,5,4,8,384]{4,3,2,1,0:T(8,128)} %refs_8_.3) | copy-start | bytes 737284
  2.4 8.7 %copy-start.1 = (bf16[4,4,5,4,8,96]{5,4,3,2,1,0:T(8,128)(2,1)S(1)}, bf16[4,4,5,4,8,96]{5,4,3,2,1,0:T(8,128)(2,1)}, u32[]{:S(2)}) copy-start(bf16[4,4,5,4,8,96]{5,4,3,2,1,0:T(8,128)(2,1)} %refs_1_.10) | copy-start | bytes 1474564
  2.4 9.5 %copy-start.6 = (f32[1,4,4,8,384]{4,3,2,1,0:T(8,128)S(1)}, f32[1,4,4,8,384]{4,3,2,1,0:T(8,128)}, u32[]{:S(2)}) copy-start(f32[1,4,4,8,384]{4,3,2,1,0:T(8,128)} %refs_4_.1) | copy-start | bytes 589828
  2.6 10.1 %collective-permute-start = (bf16[61,8,128]{2,1,0:T(8,128)(2,1)S(1)}, bf16[61,8,128]{2,1,0:T(8,128)(2,1)S(1)}, u32[]{:S(2)}, u32[]{:S(2)}) collective-permute-start(bf16[61,8,128]{2,1,0:T(8,128)(2,1)S(1)} %shard_map.123), channel_id=1, source_target_pairs={{0,4},{4,8},{8,12},{12,0},{1,5},{5,9},{9,13},{13,1},{2,6},{6,10},{... | collective-permute-start | bytes 374792 | tf_op jit(solution)/shard_map/ppermute | solution.py:586
  5.8 10.7 %collective-permute-start.1 = (bf16[61,8,128]{2,1,0:T(8,128)(2,1)S(1)}, bf16[61,8,128]{2,1,0:T(8,128)(2,1)S(1)}, u32[]{:S(2)}, u32[]{:S(2)}) collective-permute-start(bf16[61,8,128]{2,1,0:T(8,128)(2,1)S(1)} %shard_map.124), channel_id=1, source_target_pairs={{0,8},{4,12},{8,0},{12,4},{1,9},{5,13},{9,1},{13,5},{2,10},{6,14},... | collective-permute-start | bytes 374792 | tf_op jit(solution)/shard_map/ppermute | solution.py:586
  8.5 8.0 %collective-permute-start.2 = (bf16[61,8,128]{2,1,0:T(8,128)(2,1)S(1)}, bf16[61,8,128]{2,1,0:T(8,128)(2,1)S(1)}, u32[]{:S(2)}, u32[]{:S(2)}) collective-permute-start(bf16[61,8,128]{2,1,0:T(8,128)(2,1)S(1)} %shard_map.125), channel_id=1, source_target_pairs={{0,12},{4,0},{8,4},{12,8},{1,13},{5,1},{9,5},{13,9},{2,14},{6,2},{... | collective-permute-start | bytes 374792 | tf_op jit(solution)/shard_map/ppermute | solution.py:586
  10.4 7.3 %collective-permute-start.3 = (s16[2,21,16,128]{3,2,1,0:T(8,128)(2,1)S(1)}, s16[2,21,16,128]{3,2,1,0:T(8,128)(2,1)S(1)}, u32[]{:S(2)}, u32[]{:S(2)}) collective-permute-start(s16[2,21,16,128]{3,2,1,0:T(8,128)(2,1)S(1)} %get-tuple-element.37), channel_id=1, source_target_pairs={{0,1},{1,0},{2,3},{3,2},{4,5},{5,4},{6,7},{7,6},{8,9},{9,8},{10,11... | collective-permute-start | bytes 516104 | tf_op jit(solution)/shard_map/ppermute | solution.py:601
  10.5 7.2 %collective-permute-start.4 = (s16[2,21,16,128]{3,2,1,0:T(8,128)(2,1)S(1)}, s16[2,21,16,128]{3,2,1,0:T(8,128)(2,1)S(1)}, u32[]{:S(2)}, u32[]{:S(2)}) collective-permute-start(s16[2,21,16,128]{3,2,1,0:T(8,128)(2,1)S(1)} %get-tuple-element.38), channel_id=1, source_target_pairs={{1,2},{2,1},{5,6},{6,5},{9,10},{10,9},{13,14},{14,13},{17,18},{18,... | collective-permute-start | bytes 516104 | tf_op jit(solution)/shard_map/ppermute | solution.py:601
  16.9 5.2 %collective-permute-start.5 = (bf16[31,8,384]{2,1,0:T(8,128)(2,1)S(1)}, bf16[31,8,384]{2,1,0:T(8,128)(2,1)S(1)}, u32[]{:S(2)}, u32[]{:S(2)}) collective-permute-start(bf16[31,8,384]{2,1,0:T(8,128)(2,1)S(1)} %get-tuple-element.43), channel_id=1, source_target_pairs={{0,1},{1,0},{2,3},{3,2},{4,5},{5,4},{6,7},{7,6},{8,9},{9,8},{10,11... | collective-permute-start | bytes 571400 | tf_op jit(solution)/shard_map/ppermute | solution.py:601
  17.0 5.2 %collective-permute-start.6 = (bf16[31,8,384]{2,1,0:T(8,128)(2,1)S(1)}, bf16[31,8,384]{2,1,0:T(8,128)(2,1)S(1)}, u32[]{:S(2)}, u32[]{:S(2)}) collective-permute-start(bf16[31,8,384]{2,1,0:T(8,128)(2,1)S(1)} %get-tuple-element.44), channel_id=1, source_target_pairs={{1,2},{2,1},{5,6},{6,5},{9,10},{10,9},{13,14},{14,13},{17,18},{18,... | collective-permute-start | bytes 571400 | tf_op jit(solution)/shard_map/ppermute | solution.py:601
  18.0 9.9 %copy-start.5 = (f32[1,5,4,8,384]{4,3,2,1,0:T(8,128)S(1)}, f32[1,5,4,8,384]{4,3,2,1,0:T(8,128)}, u32[]{:S(2)}) copy-start(f32[1,5,4,8,384]{4,3,2,1,0:T(8,128)} %refs_7_.3) | copy-start | bytes 737284
  18.0 7.4 %collective-permute-start.7 = (s16[1,16,16,128]{3,2,1,0:T(8,128)(2,1)S(1)}, s16[1,16,16,128]{3,2,1,0:T(8,128)(2,1)S(1)}, u32[]{:S(2)}, u32[]{:S(2)}) collective-permute-start(s16[1,16,16,128]{3,2,1,0:T(8,128)(2,1)S(1)} %get-tuple-element.46), channel_id=1, source_target_pairs={{4,0},{8,4},{12,8},{5,1},{9,5},{13,9},{6,2},{10,6},{14,10},{7,3},{... | collective-permute-start | bytes 196616 | tf_op jit(solution)/shard_map/ppermute | solution.py:581
  19.4 8.4 %collective-permute-start.8 = (s16[1,16,16,128]{3,2,1,0:T(8,128)(2,1)S(1)}, s16[1,16,16,128]{3,2,1,0:T(8,128)(2,1)S(1)}, u32[]{:S(2)}, u32[]{:S(2)}) collective-permute-start(s16[1,16,16,128]{3,2,1,0:T(8,128)(2,1)S(1)} %get-tuple-element.47), channel_id=1, source_target_pairs={{4,0},{8,4},{12,8},{5,1},{9,5},{13,9},{6,2},{10,6},{14,10},{7,3},{... | collective-permute-start | bytes 196616 | tf_op jit(solution)/shard_map/ppermute | solution.py:581
  20.7 14.2 %collective-permute-start.12 = (s16[2,16,16,128]{3,2,1,0:T(8,128)(2,1)S(1)}, s16[2,16,16,128]{3,2,1,0:T(8,128)(2,1)S(1)}, u32[]{:S(2)}, u32[]{:S(2)}) collective-permute-start(s16[2,16,16,128]{3,2,1,0:T(8,128)(2,1)S(1)} %get-tuple-element.54), channel_id=1, source_target_pairs={{4,0},{8,4},{12,8},{5,1},{9,5},{13,9},{6,2},{10,6},{14,10},{7,3},{... | collective-permute-start | bytes 393224 | tf_op jit(solution)/shard_map/ppermute | solution.py:581
  29.1 10.9 %collective-permute-start.9 = (s16[16,16,128]{2,1,0:T(8,128)(2,1)S(1)}, s16[16,16,128]{2,1,0:T(8,128)(2,1)S(1)}, u32[]{:S(2)}, u32[]{:S(2)}) collective-permute-start(s16[16,16,128]{2,1,0:T(8,128)(2,1)S(1)} %get-tuple-element.51), channel_id=1, source_target_pairs={{0,12},{4,8},{8,4},{12,0},{1,13},{5,9},{9,5},{13,1},{2,14},{6,10},... | collective-permute-start | bytes 196616 | tf_op jit(solution)/shard_map/ppermute | solution.py:590
  34.3 6.4 %collective-permute-start.10 = (s16[16,16,128]{2,1,0:T(8,128)(2,1)S(1)}, s16[16,16,128]{2,1,0:T(8,128)(2,1)S(1)}, u32[]{:S(2)}, u32[]{:S(2)}) collective-permute-start(s16[16,16,128]{2,1,0:T(8,128)(2,1)S(1)} %get-tuple-element.52), channel_id=1, source_target_pairs={{0,8},{4,12},{8,0},{12,4},{1,9},{5,13},{9,1},{13,5},{2,10},{6,14},... | collective-permute-start | bytes 196616 | tf_op jit(solution)/shard_map/ppermute | solution.py:590
  34.3 6.4 %collective-permute-start.11 = (s16[16,16,128]{2,1,0:T(8,128)(2,1)S(1)}, s16[16,16,128]{2,1,0:T(8,128)(2,1)S(1)}, u32[]{:S(2)}, u32[]{:S(2)}) collective-permute-start(s16[16,16,128]{2,1,0:T(8,128)(2,1)S(1)} %get-tuple-element.53), channel_id=1, source_target_pairs={{0,4},{4,0},{8,12},{12,8},{1,5},{5,1},{9,13},{13,9},{2,6},{6,2},{1... | collective-permute-start | bytes 196616 | tf_op jit(solution)/shard_map/ppermute | solution.py:590
  36.2 6.2 %collective-permute-start.13 = (s16[16,16,128]{2,1,0:T(8,128)(2,1)S(1)}, s16[16,16,128]{2,1,0:T(8,128)(2,1)S(1)}, u32[]{:S(2)}, u32[]{:S(2)}) collective-permute-start(s16[16,16,128]{2,1,0:T(8,128)(2,1)S(1)} %get-tuple-element.58), channel_id=1, source_target_pairs={{0,12},{4,8},{8,4},{12,0},{1,13},{5,9},{9,5},{13,1},{2,14},{6,10},... | collective-permute-start | bytes 196616 | tf_op jit(solution)/shard_map/ppermute | solution.py:590
  40.0 6.0 %collective-permute-start.14 = (s16[16,16,128]{2,1,0:T(8,128)(2,1)S(1)}, s16[16,16,128]{2,1,0:T(8,128)(2,1)S(1)}, u32[]{:S(2)}, u32[]{:S(2)}) collective-permute-start(s16[16,16,128]{2,1,0:T(8,128)(2,1)S(1)} %get-tuple-element.59), channel_id=1, source_target_pairs={{0,8},{4,12},{8,0},{12,4},{1,9},{5,13},{9,1},{13,5},{2,10},{6,14},... | collective-permute-start | bytes 196616 | tf_op jit(solution)/shard_map/ppermute | solution.py:590
  40.0 6.0 %collective-permute-start.15 = (s16[16,16,128]{2,1,0:T(8,128)(2,1)S(1)}, s16[16,16,128]{2,1,0:T(8,128)(2,1)S(1)}, u32[]{:S(2)}, u32[]{:S(2)}) collective-permute-start(s16[16,16,128]{2,1,0:T(8,128)(2,1)S(1)} %get-tuple-element.60), channel_id=1, source_target_pairs={{0,4},{4,0},{8,12},{12,8},{1,5},{5,1},{9,13},{13,9},{2,6},{6,2},{1... | collective-permute-start | bytes 196616 | tf_op jit(solution)/shard_map/ppermute | solution.py:590

commit v20 on v16

--- a/solution.py
+++ b/solution.py
@@ -536,40 +536,61 @@
         ref[...] = q_ref[jnp.where((me ^ d) < me, 0, 1)]
 
 
-def final_kernel(windows, nvar, levels, tiles, *refs):
-    pairs = levels // 2
-    cut = pairs * (windows - 1)
-    pieces, base_duals, base_incs = refs[:cut], refs[cut : cut + pairs], refs[cut + pairs : -3]
-    total_ref, ndm_ref, ninc_ref = refs[-3:]
+def add_pair(i, windows, nvar, levels, tiles, pieces, base_dual_ref, base_inc_ref, total_ref, write):
     me = lax.axis_index("window")
     cuts = [slice(t * LANES, (t + 1) * LANES) for t in range(tiles)]
-
-    for i in range(pairs):
-        tails = [None] * (nvar * tiles)
-        heads = [None] * (nvar * tiles)
-        for n, d in enumerate(partners(windows)):
-            piece = pieces[i * (windows - 1) + n]
-            later = (me ^ d) > me
-            scales = jnp.exp2(floats(piece[nvar * tiles])) * (1.0 / CODE_MAX)
-            for v in range(nvar):
-                scale = scales[:, v : v + 1]
-                for t in range(tiles):
-                    k = v * tiles + t
-                    value = floats(piece[k]) * scale
-                    tail, head = jnp.where(later, value, 0.0), jnp.where(later, 0.0, value)
-                    tails[k] = tails[k] + tail if n else tail
-                    heads[k] = heads[k] + head if n else head
+    tails = [None] * (nvar * tiles)
+    heads = [None] * (nvar * tiles)
+    for n, d in enumerate(partners(windows)):
+        piece = pieces[n]
+        later = (me ^ d) > me
+        scales = jnp.exp2(floats(piece[nvar * tiles])) * (1.0 / CODE_MAX)
         for v in range(nvar):
-            for odd in range(2):
-                lev = 2 * i + odd
-                share = total_ref[v * levels + lev]
-                for t in range(tiles):
-                    rows = slice(odd * SUB, (odd + 1) * SUB)
-                    tail, head = tails[v * tiles + t][rows], heads[v * tiles + t][rows]
-                    ndm_ref[0, v, lev, :, cuts[t]] = base_duals[i][v, odd, :, cuts[t]] - tail
-                    ninc_ref[0, v, lev, :, cuts[t]] = (
-                        base_incs[i][v, odd, :, cuts[t]] + head + share * tail
-                    )
+            scale = scales[:, v : v + 1]
+            for t in range(tiles):
+                k = v * tiles + t
+                value = floats(piece[k]) * scale
+                tail, head = jnp.where(later, value, 0.0), jnp.where(later, 0.0, value)
+                tails[k] = tails[k] + tail if n else tail
+                heads[k] = heads[k] + head if n else head
+    for v in range(nvar):
+        for odd in range(2):
+            share = total_ref[v * levels + 2 * i + odd]
+            for t in range(tiles):
+                rows = slice(odd * SUB, (odd + 1) * SUB)
+                tail, head = tails[v * tiles + t][rows], heads[v * tiles + t][rows]
+                dual = base_dual_ref[v, odd, :, cuts[t]] - tail
+                write(v, odd, cuts[t], dual, base_inc_ref[v, odd, :, cuts[t]] + head + share * tail)
+
+
+def early_kernel(i, windows, nvar, levels, tiles, *refs):
+    pieces, (base_dual_ref, base_inc_ref, total_ref, dual_ref, inc_ref) = refs[:-5], refs[-5:]
+
+    def write(v, odd, cut, dual, inc):
+        dual_ref[v, odd, :, cut] = dual
+        inc_ref[v, odd, :, cut] = inc
+
+    add_pair(
+        i, windows, nvar, levels, tiles, pieces, base_dual_ref, base_inc_ref, total_ref, write
+    )
+
+
+def final_kernel(windows, nvar, levels, tiles, *refs):
+    last = levels // 2 - 1
+    pieces, done = refs[: windows - 1], refs[windows - 1 : windows - 1 + 2 * last]
+    base_dual_ref, base_inc_ref, total_ref, ndm_ref, ninc_ref = refs[-5:]
+    for i in range(last):
+        for odd in range(2):
+            ndm_ref[0, :, 2 * i + odd] = done[2 * i][:, odd]
+            ninc_ref[0, :, 2 * i + odd] = done[2 * i + 1][:, odd]
+
+    def write(v, odd, cut, dual, inc):
+        ndm_ref[0, v, 2 * last + odd, :, cut] = dual
+        ninc_ref[0, v, 2 * last + odd, :, cut] = inc
+
+    add_pair(
+        last, windows, nvar, levels, tiles, pieces, base_dual_ref, base_inc_ref, total_ref, write
+    )
 
 
 def moved(block, axis, distance):
@@ -716,7 +737,7 @@
 
     state = shape((nvar, 2, rows, columns), f32)
     coded = shape((nvar * tiles + 1, 2 * SUB, LANES), i16)
-    base_duals, base_incs, sent = [], [], []
+    done = []
     before = ends
     for i in range(pairs):
         last, force = pl.pallas_call(
@@ -741,20 +762,26 @@
             compiler_params=params(),
         )(mix, totals, wide_traj, last, force, ends, increment, model_rhs, dual_model)
         before = base_dual
-        base_duals.append(base_dual)
-        base_incs.append(base_inc)
-        sent += [
+        sent = [
             exchanged(piece, "window", mask)
             for piece, mask in zip(payloads, partners(windows))
         ]
+        if i < pairs - 1:
+            done += pl.pallas_call(
+                lambda *refs, i=i: early_kernel(i, windows, nvar, levels, tiles, *refs),
+                out_shape=[state, state],
+                in_specs=[VMEM] * (windows + 2),
+                out_specs=[VMEM] * 2,
+                compiler_params=params(),
+            )(*sent, base_dual, base_inc, totals)
 
     new_dual_model, new_increment = pl.pallas_call(
         lambda *refs: final_kernel(windows, nvar, levels, tiles, *refs),
         out_shape=[shape(dual_model.shape, f32), shape(increment.shape, f32)],
-        in_specs=[VMEM] * (len(sent) + 2 * pairs + 1),
+        in_specs=[VMEM] * (windows + 2 + len(done)),
         out_specs=[VMEM] * 2,
         compiler_params=params(),
-    )(*sent, *base_duals, *base_incs, totals)
+    )(*sent, *done, base_dual, base_inc, totals)
     return new_dual_model, new_dual_obs, new_increment
 
 

time: 45.7 us -> 45.6 us (level)
  no operation moved by 1% of the time
where the time goes in v20:
time: 45.6 us; the launch traced here: 45.3 us
  starting transfers between devices  21.3 us (47%)
  waiting for transfers between devices  11.8 us (26%)
  Pallas kernels  8.84 us (19%)
  local copies, waits for them, and re-layouts  1.82 us (4%)
  between operations  1.55 us (3%)
    ppermute x6, starting transfers between devices, exchanged(): lax.ppermute(block, axis, [(i, i ^ mask) for i in range(lax.axis_size(axi...  10 us
    ppermute x3, starting transfers between devices, rotated(): lax.ppermute(block, axis, [(i, (i + distance) % count) for i in range(cou...  7.13 us
    ppermute x6, waiting for transfers between devices, exchanged(): lax.ppermute(block, axis, [(i, i ^ mask) for i in range(lax.axis_size(axi...  5.49 us
    ppermute x3, waiting for transfers between devices, rotated(): lax.ppermute(block, axis, [(i, (i + distance) % count) for i in range(cou...  3.81 us
    pallas_call x1, Pallas kernels, body(): pl.pallas_call(lambda *refs: tangent_kernel(spaces, steps, nvar, levels,...  2.77 us
    ppermute x2, starting transfers between devices, moved(): lax.ppermute(block, axis, [(i, i + distance) for i in devices if i + dist...  2.72 us
    ppermute x2, waiting for transfers between devices, moved(): lax.ppermute(block, axis, [(i, i + distance) for i in devices if i + dist...  2.45 us
    pallas_call x2, Pallas kernels, body(): pl.pallas_call(lambda *refs, i=i: adjoint_kernel(i, windows, spaces, step...  2.33 us
  transfers between devices with their start and end apart: 15, of which 5 were waited for; matrix products, arithmetic and copies ran while one was open for 0% of the time, Pallas kernels for 17%

profile of v20, /device:TPU:0, one launch (start us, length us, event | category | flops | bytes accessed | tf_op | source)
XLA Modules:
  0.0 45.3 jit_solution(6337925442905200003)
XLA Ops:
  0.7 0.7 %pad.4.refs_0_ = f32[8,128]{1,0:T(8,128)S(1)} pad(f32[4,5]{1,0:T(4,128)} %bitcast.3, f32[]{:T(128)} %constant.2.clone.1), padding=0_4x0_123 | pad | bytes 4180 | tf_op jit(solution)/shard_map/jit(_pad)/pad | solution.py:648
  1.4 1.1 %copy-done = bf16[4,4,5,4,8,96]{5,4,3,2,1,0:T(8,128)(2,1)S(1)} copy-done((bf16[4,4,5,4,8,96]{5,4,3,2,1,0:T(8,128)(2,1)S(1)}, bf16[4,4,5,4,8,96]{5,4,3,2,1,0:T(8,128)(2,1)}, u32[]{:S(2)}) %copy-start) | copy-done | bytes 491544
  2.5 0.1 shard_map.123
  2.6 3.1 %collective-permute-start = (bf16[61,8,128]{2,1,0:T(8,128)(2,1)S(1)}, bf16[61,8,128]{2,1,0:T(8,128)(2,1)S(1)}, u32[]{:S(2)}, u32[]{:S(2)}) collective-permute-start(bf16[61,8,128]{2,1,0:T(8,128)(2,1)S(1)} %shard_map.123), channel_id=1, source_target_pairs={{0,4},{4,8},{8,12},{12,0},{1,5},{5,9},{9,13},{13,1},{2,6},{6,10},{... | collective-permute-start | bytes 374792 | tf_op jit(solution)/shard_map/ppermute | solution.py:603
  5.8 2.7 %collective-permute-start.1 = (bf16[61,8,128]{2,1,0:T(8,128)(2,1)S(1)}, bf16[61,8,128]{2,1,0:T(8,128)(2,1)S(1)}, u32[]{:S(2)}, u32[]{:S(2)}) collective-permute-start(bf16[61,8,128]{2,1,0:T(8,128)(2,1)S(1)} %shard_map.124), channel_id=1, source_target_pairs={{0,8},{4,12},{8,0},{12,4},{1,9},{5,13},{9,1},{13,5},{2,10},{6,14},... | collective-permute-start | bytes 374792 | tf_op jit(solution)/shard_map/ppermute | solution.py:603
  8.5 1.4 %collective-permute-start.2 = (bf16[61,8,128]{2,1,0:T(8,128)(2,1)S(1)}, bf16[61,8,128]{2,1,0:T(8,128)(2,1)S(1)}, u32[]{:S(2)}, u32[]{:S(2)}) collective-permute-start(bf16[61,8,128]{2,1,0:T(8,128)(2,1)S(1)} %shard_map.125), channel_id=1, source_target_pairs={{0,12},{4,0},{8,4},{12,8},{1,13},{5,1},{9,5},{13,9},{2,14},{6,2},{... | collective-permute-start | bytes 374792 | tf_op jit(solution)/shard_map/ppermute | solution.py:603
  10.0 0.5 %shard_map.126 = (s16[2,21,16,128]{3,2,1,0:T(8,128)(2,1)S(1)}, s16[2,21,16,128]{3,2,1,0:T(8,128)(2,1)S(1)}, s16[2,16,16,128]{3,2,1,0:T(8,128)(2,1)S(1)}) custom-call(f32[1,5,4,8,384]{4,3,2,1,0:T(8,128)S(1)} %copy-done.4, f32[1,5,4,8,384]{4,3,2,1,0:T(8,128)S(1)} %copy-done.2, f32[1,4,4,8,384]{4,3,2,1,0:T(8,128)S(1)} %copy-done.3), custom_call_target="tpu_custom_call" | custom-call | tf_op jit(solution)/shard_map/pallas_call | solution.py:672
  10.5 0.7 %collective-permute-start.4 = (s16[2,21,16,128]{3,2,1,0:T(8,128)(2,1)S(1)}, s16[2,21,16,128]{3,2,1,0:T(8,128)(2,1)S(1)}, u32[]{:S(2)}, u32[]{:S(2)}) collective-permute-start(s16[2,21,16,128]{3,2,1,0:T(8,128)(2,1)S(1)} %get-tuple-element.39), channel_id=1, source_target_pairs={{1,2},{2,1},{5,6},{6,5},{9,10},{10,9},{13,14},{14,13},{17,18},{18,... | collective-permute-start | bytes 516104 | tf_op jit(solution)/shard_map/ppermute | solution.py:618
  11.2 0.1 shard_map.122.refs_0_
  12.0 0.7 %shard_map.121 = (f32[4,4,3,8,128]{4,3,2,1,0:T(8,128)S(1)}, f32[4,4,8,128]{3,2,1,0:T(8,128)S(1)}, f32[5,5,8,128]{3,2,1,0:T(8,128)S(1)}) custom-call(s32[1]{0:T(128)S(6)} %copy.13.refs_0_, f32[1,4,4]{2,1,0:T(4,128)S(1)} %copy-done.8, f32[5,5]{1,0:T(8,128)S(1)} %copy-done.7, f32[1,4,4,8,384]{4,3,2,1,0:T(8,128)S(1)} %copy-done.3, f32[1,4,4,8,384]{4,3,2,1,0:T(8,128)S(1)} %copy-done.6), custom_call_target="tpu_custom_call" | custom-call | tf_op jit(solution)/shard_map/pallas_call | solution.py:692
  12.7 3.8 %collective-permute-done.1.refs_2_ = bf16[61,8,128]{2,1,0:T(8,128)(2,1)S(1)} collective-permute-done((bf16[61,8,128]{2,1,0:T(8,128)(2,1)S(1)}, bf16[61,8,128]{2,1,0:T(8,128)(2,1)S(1)}, u32[]{:S(2)}, u32[]{:S(2)}) %collective-permute-start.1) | collective-permute-done | bytes 124960 | tf_op jit(solution)/shard_map/ppermute | solution.py:603
  16.5 0.4 shard_map.128
  17.0 0.7 %collective-permute-start.6 = (bf16[31,8,384]{2,1,0:T(8,128)(2,1)S(1)}, bf16[31,8,384]{2,1,0:T(8,128)(2,1)S(1)}, u32[]{:S(2)}, u32[]{:S(2)}) collective-permute-start(bf16[31,8,384]{2,1,0:T(8,128)(2,1)S(1)} %get-tuple-element.45), channel_id=1, source_target_pairs={{1,2},{2,1},{5,6},{6,5},{9,10},{10,9},{13,14},{14,13},{17,18},{18,... | collective-permute-start | bytes 571400 | tf_op jit(solution)/shard_map/ppermute | solution.py:618
  17.7 0.3 shard_map.127
  18.0 1.4 %collective-permute-start.8 = (s16[2,16,16,128]{3,2,1,0:T(8,128)(2,1)S(1)}, s16[2,16,16,128]{3,2,1,0:T(8,128)(2,1)S(1)}, u32[]{:S(2)}, u32[]{:S(2)}) collective-permute-start(s16[2,16,16,128]{3,2,1,0:T(8,128)(2,1)S(1)} %get-tuple-element.48), channel_id=1, source_target_pairs={{4,0},{8,4},{12,8},{5,1},{9,5},{13,9},{6,2},{10,6},{14,10},{7,3},{... | collective-permute-start | bytes 393224 | tf_op jit(solution)/shard_map/ppermute | solution.py:598
  19.4 1.3 %collective-permute-start.7 = (s16[2,16,16,128]{3,2,1,0:T(8,128)(2,1)S(1)}, s16[2,16,16,128]{3,2,1,0:T(8,128)(2,1)S(1)}, u32[]{:S(2)}, u32[]{:S(2)}) collective-permute-start(s16[2,16,16,128]{3,2,1,0:T(8,128)(2,1)S(1)} %get-tuple-element.47), channel_id=1, source_target_pairs={{4,0},{8,4},{12,8},{5,1},{9,5},{13,9},{6,2},{10,6},{14,10},{7,3},{... | collective-permute-start | bytes 393224 | tf_op jit(solution)/shard_map/ppermute | solution.py:598
  20.7 0.1 shard_map.129.refs_6_
  20.9 2.8 %shard_map.130 = (f32[1,4,4,8,384]{4,3,2,1,0:T(8,128)}, f32[4,5,3,8,128]{4,3,2,1,0:T(8,128)S(1)}, f32[4,4,5,3,16,128]{5,4,3,2,1,0:T(8,128)S(1)}) custom-call(f32[5,5,8,128]{3,2,1,0:T(8,128)S(1)} %get-tuple-element.36.refs_4_.refs_0_, f32[4,4,8,128]{3,2,1,0:T(8,128)S(1)} %get-tuple-element.41.refs_1_, f32[4,4,3,8,128]{4,3,2,1,0:T(8,128)S(1)} %get-tuple-element.42.refs_2_, ...), custom_call_target="tpu_custom_call" | custom-call | tf_op jit(solution)/shard_map/pallas_call | solution.py:725
  23.7 2.5 %collective-permute-done.8.refs_4_ = s16[2,16,16,128]{3,2,1,0:T(8,128)(2,1)S(1)} collective-permute-done((s16[2,16,16,128]{3,2,1,0:T(8,128)(2,1)S(1)}, s16[2,16,16,128]{3,2,1,0:T(8,128)(2,1)S(1)}, u32[]{:S(2)}, u32[]{:S(2)}) %collective-permute-start.8) | collective-permute-done | bytes 131104 | tf_op jit(solution)/shard_map/ppermute | solution.py:598
  26.1 0.1 shard_map.131
  26.3 1.2 %shard_map.132 = (f32[5,2,8,384]{3,2,1,0:T(8,128)S(1)}, f32[5,2,8,384]{3,2,1,0:T(8,128)S(1)}, s16[16,16,128]{2,1,0:T(8,128)(2,1)S(1)}, s16[16,16,128]{2,1,0:T(8,128)(2,1)S(1)}, s16[16,16,128]{2,1,0:T(8,128)(2,1)S(1)}) custom-call(f32[5,5,8,128]{3,2,1,0:T(8,128)S(1)} %get-tuple-element.36.refs_4_.refs_0_, ...), custom_call_target="tpu_custom_call" | custom-call | tf_op jit(solution)/shard_map/pallas_call | solution.py:750
  27.4 4.9 %collective-permute-start.12 = (s16[16,16,128]{2,1,0:T(8,128)(2,1)S(1)}, s16[16,16,128]{2,1,0:T(8,128)(2,1)S(1)}, u32[]{:S(2)}, u32[]{:S(2)}) collective-permute-start(s16[16,16,128]{2,1,0:T(8,128)(2,1)S(1)} %get-tuple-element.58), channel_id=1, source_target_pairs={{0,12},{4,8},{8,4},{12,0},{1,13},{5,9},{9,5},{13,1},{2,14},{6,10},... | collective-permute-start | bytes 196616 | tf_op jit(solution)/shard_map/ppermute | solution.py:607
  32.3 0.6 %collective-permute-start.14 = (s16[16,16,128]{2,1,0:T(8,128)(2,1)S(1)}, s16[16,16,128]{2,1,0:T(8,128)(2,1)S(1)}, u32[]{:S(2)}, u32[]{:S(2)}) collective-permute-start(s16[16,16,128]{2,1,0:T(8,128)(2,1)S(1)} %get-tuple-element.60), channel_id=1, source_target_pairs={{0,4},{4,0},{8,12},{12,8},{1,5},{5,1},{9,13},{13,9},{2,6},{6,2},{1... | collective-permute-start | bytes 196616 | tf_op jit(solution)/shard_map/ppermute | solution.py:607
  33.0 0.1 shard_map.133
  33.1 1.2 %shard_map.134 = (f32[5,2,8,384]{3,2,1,0:T(8,128)S(1)}, f32[5,2,8,384]{3,2,1,0:T(8,128)S(1)}, s16[16,16,128]{2,1,0:T(8,128)(2,1)S(1)}, s16[16,16,128]{2,1,0:T(8,128)(2,1)S(1)}, s16[16,16,128]{2,1,0:T(8,128)(2,1)S(1)}) custom-call(f32[5,5,8,128]{3,2,1,0:T(8,128)S(1)} %get-tuple-element.36.refs_4_.refs_0_, ...), custom_call_target="tpu_custom_call" | custom-call | tf_op jit(solution)/shard_map/pallas_call | solution.py:750
  34.3 3.8 %collective-permute-start.9 = (s16[16,16,128]{2,1,0:T(8,128)(2,1)S(1)}, s16[16,16,128]{2,1,0:T(8,128)(2,1)S(1)}, u32[]{:S(2)}, u32[]{:S(2)}) collective-permute-start(s16[16,16,128]{2,1,0:T(8,128)(2,1)S(1)} %get-tuple-element.55), channel_id=1, source_target_pairs={{0,12},{4,8},{8,4},{12,0},{1,13},{5,9},{9,5},{13,1},{2,14},{6,10},... | collective-permute-start | bytes 196616 | tf_op jit(solution)/shard_map/ppermute | solution.py:607
  38.1 0.6 %collective-permute-start.11 = (s16[16,16,128]{2,1,0:T(8,128)(2,1)S(1)}, s16[16,16,128]{2,1,0:T(8,128)(2,1)S(1)}, u32[]{:S(2)}, u32[]{:S(2)}) collective-permute-start(s16[16,16,128]{2,1,0:T(8,128)(2,1)S(1)} %get-tuple-element.57), channel_id=1, source_target_pairs={{0,4},{4,0},{8,12},{12,8},{1,5},{5,1},{9,13},{13,9},{2,6},{6,2},{1... | collective-permute-start | bytes 196616 | tf_op jit(solution)/shard_map/ppermute | solution.py:607
  38.7 0.3 collective-permute-done.13.refs_1_
  39.1 0.2 shard_map.135
  39.3 1.3 %collective-permute-done.9.refs_0_ = s16[16,16,128]{2,1,0:T(8,128)(2,1)S(1)} collective-permute-done((s16[16,16,128]{2,1,0:T(8,128)(2,1)S(1)}, s16[16,16,128]{2,1,0:T(8,128)(2,1)S(1)}, u32[]{:S(2)}, u32[]{:S(2)}) %collective-permute-start.9) | collective-permute-done | bytes 65568 | tf_op jit(solution)/shard_map/ppermute | solution.py:607
  40.5 3.9 %collective-permute-done.10.refs_1_ = s16[16,16,128]{2,1,0:T(8,128)(2,1)S(1)} collective-permute-done((s16[16,16,128]{2,1,0:T(8,128)(2,1)S(1)}, s16[16,16,128]{2,1,0:T(8,128)(2,1)S(1)}, u32[]{:S(2)}, u32[]{:S(2)}) %collective-permute-start.10) | collective-permute-done | bytes 65568 | tf_op jit(solution)/shard_map/ppermute | solution.py:607
  44.4 0.9 %shard_map.136 = (f32[1,5,4,8,384]{4,3,2,1,0:T(8,128)}, f32[1,5,4,8,384]{4,3,2,1,0:T(8,128)}) custom-call(s16[16,16,128]{2,1,0:T(8,128)(2,1)S(1)} %collective-permute-done.9.refs_0_, s16[16,16,128]{2,1,0:T(8,128)(2,1)S(1)} %collective-permute-done.10.refs_1_, s16[16,16,128]{2,1,0:T(8,128)(2,1)S(1)} %collective-permute-done.11.refs_2_, ...), custom_call_target="tpu_custom_call" | custom-call | tf_op jit(solution)/shard_map/pallas_call | solution.py:778
  (33 shorter events, 0.4 us)
Async XLA Ops:
  0.6 11.3 %copy-start.8 = (f32[1,4,4]{2,1,0:T(4,128)S(1)}, f32[1,4,4]{2,1,0:T(4,128)}, u32[]{:S(2)}) copy-start(f32[1,4,4]{2,1,0:T(4,128)} %refs_1_.6) | copy-start | bytes 196
  0.6 11.3 %copy-start.7 = (f32[5,5]{1,0:T(8,128)S(1)}, f32[5,5]{1,0:T(8,128)}, u32[]{:S(2)}) copy-start(f32[5,5]{1,0:T(8,128)} %refs_2_.3) | copy-start | bytes 304
  1.3 1.1 %copy-start = (bf16[4,4,5,4,8,96]{5,4,3,2,1,0:T(8,128)(2,1)S(1)}, bf16[4,4,5,4,8,96]{5,4,3,2,1,0:T(8,128)(2,1)}, u32[]{:S(2)}) copy-start(bf16[4,4,5,4,8,96]{5,4,3,2,1,0:T(8,128)(2,1)} %refs_1_.10) | copy-start | bytes 1474564
  2.4 7.5 %copy-start.2 = (f32[1,5,4,8,384]{4,3,2,1,0:T(8,128)S(1)}, f32[1,5,4,8,384]{4,3,2,1,0:T(8,128)}, u32[]{:S(2)}) copy-start(f32[1,5,4,8,384]{4,3,2,1,0:T(8,128)} %refs_6_.3) | copy-start | bytes 737284
  2.4 7.5 %copy-start.3 = (f32[1,4,4,8,384]{4,3,2,1,0:T(8,128)S(1)}, f32[1,4,4,8,384]{4,3,2,1,0:T(8,128)}, u32[]{:S(2)}) copy-start(f32[1,4,4,8,384]{4,3,2,1,0:T(8,128)} %refs_3_.5) | copy-start | bytes 589828
  2.4 7.5 %copy-start.4 = (f32[1,5,4,8,384]{4,3,2,1,0:T(8,128)S(1)}, f32[1,5,4,8,384]{4,3,2,1,0:T(8,128)}, u32[]{:S(2)}) copy-start(f32[1,5,4,8,384]{4,3,2,1,0:T(8,128)} %refs_8_.3) | copy-start | bytes 737284
  2.4 8.7 %copy-start.1 = (bf16[4,4,5,4,8,96]{5,4,3,2,1,0:T(8,128)(2,1)S(1)}, bf16[4,4,5,4,8,96]{5,4,3,2,1,0:T(8,128)(2,1)}, u32[]{:S(2)}) copy-start(bf16[4,4,5,4,8,96]{5,4,3,2,1,0:T(8,128)(2,1)} %refs_1_.10) | copy-start | bytes 1474564
  2.4 9.5 %copy-start.6 = (f32[1,4,4,8,384]{4,3,2,1,0:T(8,128)S(1)}, f32[1,4,4,8,384]{4,3,2,1,0:T(8,128)}, u32[]{:S(2)}) copy-start(f32[1,4,4,8,384]{4,3,2,1,0:T(8,128)} %refs_4_.1) | copy-start | bytes 589828
  2.6 10.1 %collective-permute-start = (bf16[61,8,128]{2,1,0:T(8,128)(2,1)S(1)}, bf16[61,8,128]{2,1,0:T(8,128)(2,1)S(1)}, u32[]{:S(2)}, u32[]{:S(2)}) collective-permute-start(bf16[61,8,128]{2,1,0:T(8,128)(2,1)S(1)} %shard_map.123), channel_id=1, source_target_pairs={{0,4},{4,8},{8,12},{12,0},{1,5},{5,9},{9,13},{13,1},{2,6},{6,10},{... | collective-permute-start | bytes 374792 | tf_op jit(solution)/shard_map/ppermute | solution.py:603
  5.8 10.7 %collective-permute-start.1 = (bf16[61,8,128]{2,1,0:T(8,128)(2,1)S(1)}, bf16[61,8,128]{2,1,0:T(8,128)(2,1)S(1)}, u32[]{:S(2)}, u32[]{:S(2)}) collective-permute-start(bf16[61,8,128]{2,1,0:T(8,128)(2,1)S(1)} %shard_map.124), channel_id=1, source_target_pairs={{0,8},{4,12},{8,0},{12,4},{1,9},{5,13},{9,1},{13,5},{2,10},{6,14},... | collective-permute-start | bytes 374792 | tf_op jit(solution)/shard_map/ppermute | solution.py:603
  8.5 8.0 %collective-permute-start.2 = (bf16[61,8,128]{2,1,0:T(8,128)(2,1)S(1)}, bf16[61,8,128]{2,1,0:T(8,128)(2,1)S(1)}, u32[]{:S(2)}, u32[]{:S(2)}) collective-permute-start(bf16[61,8,128]{2,1,0:T(8,128)(2,1)S(1)} %shard_map.125), channel_id=1, source_target_pairs={{0,12},{4,0},{8,4},{12,8},{1,13},{5,1},{9,5},{13,9},{2,14},{6,2},{... | collective-permute-start | bytes 374792 | tf_op jit(solution)/shard_map/ppermute | solution.py:603
  10.4 7.3 %collective-permute-start.3 = (s16[2,21,16,128]{3,2,1,0:T(8,128)(2,1)S(1)}, s16[2,21,16,128]{3,2,1,0:T(8,128)(2,1)S(1)}, u32[]{:S(2)}, u32[]{:S(2)}) collective-permute-start(s16[2,21,16,128]{3,2,1,0:T(8,128)(2,1)S(1)} %get-tuple-element.38), channel_id=1, source_target_pairs={{0,1},{1,0},{2,3},{3,2},{4,5},{5,4},{6,7},{7,6},{8,9},{9,8},{10,11... | collective-permute-start | bytes 516104 | tf_op jit(solution)/shard_map/ppermute | solution.py:618
  10.5 7.2 %collective-permute-start.4 = (s16[2,21,16,128]{3,2,1,0:T(8,128)(2,1)S(1)}, s16[2,21,16,128]{3,2,1,0:T(8,128)(2,1)S(1)}, u32[]{:S(2)}, u32[]{:S(2)}) collective-permute-start(s16[2,21,16,128]{3,2,1,0:T(8,128)(2,1)S(1)} %get-tuple-element.39), channel_id=1, source_target_pairs={{1,2},{2,1},{5,6},{6,5},{9,10},{10,9},{13,14},{14,13},{17,18},{18,... | collective-permute-start | bytes 516104 | tf_op jit(solution)/shard_map/ppermute | solution.py:618
  16.9 3.9 %collective-permute-start.5 = (bf16[31,8,384]{2,1,0:T(8,128)(2,1)S(1)}, bf16[31,8,384]{2,1,0:T(8,128)(2,1)S(1)}, u32[]{:S(2)}, u32[]{:S(2)}) collective-permute-start(bf16[31,8,384]{2,1,0:T(8,128)(2,1)S(1)} %get-tuple-element.44), channel_id=1, source_target_pairs={{0,1},{1,0},{2,3},{3,2},{4,5},{5,4},{6,7},{7,6},{8,9},{9,8},{10,11... | collective-permute-start | bytes 571400 | tf_op jit(solution)/shard_map/ppermute | solution.py:618
  17.0 3.9 %collective-permute-start.6 = (bf16[31,8,384]{2,1,0:T(8,128)(2,1)S(1)}, bf16[31,8,384]{2,1,0:T(8,128)(2,1)S(1)}, u32[]{:S(2)}, u32[]{:S(2)}) collective-permute-start(bf16[31,8,384]{2,1,0:T(8,128)(2,1)S(1)} %get-tuple-element.45), channel_id=1, source_target_pairs={{1,2},{2,1},{5,6},{6,5},{9,10},{10,9},{13,14},{14,13},{17,18},{18,... | collective-permute-start | bytes 571400 | tf_op jit(solution)/shard_map/ppermute | solution.py:618
  18.0 8.3 %copy-start.5 = (f32[1,5,4,8,384]{4,3,2,1,0:T(8,128)S(1)}, f32[1,5,4,8,384]{4,3,2,1,0:T(8,128)}, u32[]{:S(2)}) copy-start(f32[1,5,4,8,384]{4,3,2,1,0:T(8,128)} %refs_7_.3) | copy-start | bytes 737284
  18.0 8.1 %collective-permute-start.8 = (s16[2,16,16,128]{3,2,1,0:T(8,128)(2,1)S(1)}, s16[2,16,16,128]{3,2,1,0:T(8,128)(2,1)S(1)}, u32[]{:S(2)}, u32[]{:S(2)}) collective-permute-start(s16[2,16,16,128]{3,2,1,0:T(8,128)(2,1)S(1)} %get-tuple-element.48), channel_id=1, source_target_pairs={{4,0},{8,4},{12,8},{5,1},{9,5},{13,9},{6,2},{10,6},{14,10},{7,3},{... | collective-permute-start | bytes 393224 | tf_op jit(solution)/shard_map/ppermute | solution.py:598
  19.4 13.6 %collective-permute-start.7 = (s16[2,16,16,128]{3,2,1,0:T(8,128)(2,1)S(1)}, s16[2,16,16,128]{3,2,1,0:T(8,128)(2,1)S(1)}, u32[]{:S(2)}, u32[]{:S(2)}) collective-permute-start(s16[2,16,16,128]{3,2,1,0:T(8,128)(2,1)S(1)} %get-tuple-element.47), channel_id=1, source_target_pairs={{4,0},{8,4},{12,8},{5,1},{9,5},{13,9},{6,2},{10,6},{14,10},{7,3},{... | collective-permute-start | bytes 393224 | tf_op jit(solution)/shard_map/ppermute | solution.py:598
  27.4 10.7 %collective-permute-start.12 = (s16[16,16,128]{2,1,0:T(8,128)(2,1)S(1)}, s16[16,16,128]{2,1,0:T(8,128)(2,1)S(1)}, u32[]{:S(2)}, u32[]{:S(2)}) collective-permute-start(s16[16,16,128]{2,1,0:T(8,128)(2,1)S(1)} %get-tuple-element.58), channel_id=1, source_target_pairs={{0,12},{4,8},{8,4},{12,0},{1,13},{5,9},{9,5},{13,1},{2,14},{6,10},... | collective-permute-start | bytes 196616 | tf_op jit(solution)/shard_map/ppermute | solution.py:607
  32.3 6.8 %collective-permute-start.13 = (s16[16,16,128]{2,1,0:T(8,128)(2,1)S(1)}, s16[16,16,128]{2,1,0:T(8,128)(2,1)S(1)}, u32[]{:S(2)}, u32[]{:S(2)}) collective-permute-start(s16[16,16,128]{2,1,0:T(8,128)(2,1)S(1)} %get-tuple-element.59), channel_id=1, source_target_pairs={{0,8},{4,12},{8,0},{12,4},{1,9},{5,13},{9,1},{13,5},{2,10},{6,14},... | collective-permute-start | bytes 196616 | tf_op jit(solution)/shard_map/ppermute | solution.py:607
  32.3 6.8 %collective-permute-start.14 = (s16[16,16,128]{2,1,0:T(8,128)(2,1)S(1)}, s16[16,16,128]{2,1,0:T(8,128)(2,1)S(1)}, u32[]{:S(2)}, u32[]{:S(2)}) collective-permute-start(s16[16,16,128]{2,1,0:T(8,128)(2,1)S(1)} %get-tuple-element.60), channel_id=1, source_target_pairs={{0,4},{4,0},{8,12},{12,8},{1,5},{5,1},{9,13},{13,9},{2,6},{6,2},{1... | collective-permute-start | bytes 196616 | tf_op jit(solution)/shard_map/ppermute | solution.py:607
  34.3 6.2 %collective-permute-start.9 = (s16[16,16,128]{2,1,0:T(8,128)(2,1)S(1)}, s16[16,16,128]{2,1,0:T(8,128)(2,1)S(1)}, u32[]{:S(2)}, u32[]{:S(2)}) collective-permute-start(s16[16,16,128]{2,1,0:T(8,128)(2,1)S(1)} %get-tuple-element.55), channel_id=1, source_target_pairs={{0,12},{4,8},{8,4},{12,0},{1,13},{5,9},{9,5},{13,1},{2,14},{6,10},... | collective-permute-start | bytes 196616 | tf_op jit(solution)/shard_map/ppermute | solution.py:607
  38.1 6.3 %collective-permute-start.10 = (s16[16,16,128]{2,1,0:T(8,128)(2,1)S(1)}, s16[16,16,128]{2,1,0:T(8,128)(2,1)S(1)}, u32[]{:S(2)}, u32[]{:S(2)}) collective-permute-start(s16[16,16,128]{2,1,0:T(8,128)(2,1)S(1)} %get-tuple-element.56), channel_id=1, source_target_pairs={{0,8},{4,12},{8,0},{12,4},{1,9},{5,13},{9,1},{13,5},{2,10},{6,14},... | collective-permute-start | bytes 196616 | tf_op jit(solution)/shard_map/ppermute | solution.py:607
  38.1 6.3 %collective-permute-start.11 = (s16[16,16,128]{2,1,0:T(8,128)(2,1)S(1)}, s16[16,16,128]{2,1,0:T(8,128)(2,1)S(1)}, u32[]{:S(2)}, u32[]{:S(2)}) collective-permute-start(s16[16,16,128]{2,1,0:T(8,128)(2,1)S(1)} %get-tuple-element.57), channel_id=1, source_target_pairs={{0,4},{4,0},{8,12},{12,8},{1,5},{5,1},{9,13},{13,9},{2,6},{6,2},{1... | collective-permute-start | bytes 196616 | tf_op jit(solution)/shard_map/ppermute | solution.py:607
